TPU v7x, 32 devices: a whole 2x2x4 slice. The times are simulated.
32 devices in a mesh: groups: 2 (over x), node: 8 (over z, y), local: 2 (over core).
Axes of the slice: x: 2, y: 2, z: 4, core: 2. Of those that a mesh axis runs over, the one named last changes fastest.
Arguments:
- tokens: bfloat16 [4096, 3584], P(('groups', 'node', 'local')), parts along dimension 0, may hold values from -6 to 6
- routes: int32 [4096, 2], P(('groups', 'node', 'local')), parts along dimension 0, may hold values from 0 to 7, all different within a row; in each aligned block of 128 rows (0 to 127, 128 to 255, ...) at most 80 rows name the same one
- route_scale: float32 [4096, 2], P(('groups', 'node', 'local')), parts along dimension 0, may hold values from 0.3 to 1.5
- w_gate: bfloat16 [8, 3584, 1024], P('node', None, 'local'), may hold values from -0.09375 to 0.09375
- w_up: bfloat16 [8, 3584, 1024], P('node', None, 'local'), may hold values from -0.09375 to 0.09375
- w_down: bfloat16 [8, 1024, 3584], P('node', 'local'), may hold values from -0.1875 to 0.1875
Outputs:
- mixed: bfloat16 [4096, 3584], P(('groups', 'node', 'local')), parts along dimension 0
There are 2 independent parts, one for each index of `groups`. A program takes and returns all parts, laid end to end along the dimension named above; an argument that names none is the same for every part. Nothing has to cross between parts.
Inputs may be any that keep to these rules, and one draw needn't show every extreme that they name: `routes`: the 2 experts of a token differ. Within the rows of one device (aligned blocks of 128 tokens) no expert is named by more than 80 tokens, a bound that some block reaches.
All inputs are finite; a program needn't handle non-finite values.
Results may differ from a plain program's by a relative error of at most 0.006.
Values may be sent and summed in bfloat16 or wider, within the bound.
No kernel may reach another device: no remote copies, remote signals or barrier semaphores. Data moves between devices by JAX's collectives and lax.ppermute only.
A program may use at most 128 MiB of HBM per device.

v0:
```python
import jax
import jax.numpy as jnp
from jax import lax
from jax.sharding import PartitionSpec as P


def on_device(tokens, routes, route_scale, w_gate, w_up, w_down):
    count = tokens.shape[0]
    width = tokens.shape[1]
    experts = lax.axis_size("node")
    halves = lax.axis_size("local")
    cap_rows = 5 * count // experts
    pairs = routes.reshape(-1)
    onehot = (pairs[:, None] == jnp.arange(experts, dtype=jnp.int32)[None, :]).astype(jnp.int32)
    rank = jnp.sum((jnp.cumsum(onehot, axis=0) - onehot) * onehot, axis=1)
    dest = pairs * cap_rows + rank
    source = (
        jnp.full((experts * cap_rows,), 2 * count, jnp.int32)
        .at[dest]
        .set(jnp.arange(2 * count, dtype=jnp.int32))
    )
    padded = jnp.concatenate([tokens, jnp.zeros((1, width), tokens.dtype)], axis=0)
    outgoing = padded[source // 2].reshape(experts, cap_rows, width)
    copies = jnp.broadcast_to(outgoing[:, None], (experts, halves, cap_rows, width))
    copies = copies.reshape(experts * halves, cap_rows, width)
    arrived = lax.all_to_all(copies, ("node", "local"), split_axis=0, concat_axis=0, tiled=True)
    arrived = arrived.reshape(experts, halves, cap_rows, width)
    block_rows = arrived.reshape(-1, width)
    gate = jnp.dot(block_rows, w_gate[0], preferred_element_type=jnp.float32)
    up = jnp.dot(block_rows, w_up[0], preferred_element_type=jnp.float32)
    hidden = (jax.nn.silu(gate) * up).astype(jnp.bfloat16)
    partial_value = jnp.dot(hidden, w_down[0], preferred_element_type=jnp.float32)
    partial_value = partial_value.reshape(experts, halves, cap_rows, width)
    summed = lax.psum_scatter(partial_value, "local", scatter_dimension=1, tiled=True).astype(
        jnp.bfloat16
    )
    returned = lax.all_to_all(summed, "node", split_axis=0, concat_axis=0, tiled=True)
    returned = returned.reshape(experts * cap_rows, width)
    picked = returned[dest].astype(jnp.float32).reshape(count, 2, width)
    mixed = jnp.sum(picked * route_scale[:, :, None], axis=1)
    return mixed.astype(jnp.bfloat16)


def solution(mesh):
    placed = (
        P(("groups", "node", "local"), None),
        P(("groups", "node", "local"), None),
        P(("groups", "node", "local"), None),
        P("node", None, "local"),
        P("node", None, "local"),
        P("node", "local", None),
    )
    return jax.shard_map(
        on_device,
        mesh=mesh,
        in_specs=placed,
        out_specs=P(("groups", "node", "local"), None),
        check_vma=False,
    )
```

profile of v0, /device:TPU:0, one launch (start us, length us, event | category | flops | bytes accessed | tf_op | source)
XLA Modules:
  0.0 432.3 jit_solution(17683019763289177869)
XLA Ops:
  0.0 0.8 copy.13
  0.8 0.1 eq.29
  0.9 0.1 eq.25
  1.1 0.7 broadcast_multiply_fusion
  1.8 0.6 reduce-window.6
  2.3 0.2 slice_reduce_fusion
  2.6 0.1 copy.12
  2.7 0.1 mul.36
  2.8 0.1 fusion.13
  3.0 1.4 scatter_custom_fusion
  4.4 1.2 concatenate.3
  5.6 5.2 %gather_fusion = bf16[640,3584]{1,0:T(8,128)(2,1)} fusion(bf16[129,3584]{1,0:T(8,128)(2,1)S(1)} %concatenate.3, s32[1024]{0:T(1024)S(1)} %pad_clamp_fusion.1), kind=kCustom, calls=%fused_computation | custom fusion | bytes 9177600 | tf_op jit(solution)/shard_map/gather | solution.py:23
  10.8 6.7 %broadcast_in_dim.21 = bf16[8,2,80,3584]{3,2,1,0:T(8,128)(2,1)} broadcast(bf16[8,80,3584]{2,1,0:T(8,128)(2,1)} %bitcast.39), dimensions={0,2,3} | broadcast | bytes 13762560 | tf_op jit(solution)/shard_map/broadcast_in_dim | solution.py:24
  17.5 0.0 copy-start.3
  17.5 7.6 %all-to-all-start = ((bf16[16,80,3584]{2,1,0:T(8,128)(2,1)}), bf16[16,80,3584]{2,1,0:T(8,128)(2,1)}, u32[]{:S(2)}, u32[]{:S(2)}) async-start(bf16[16,80,3584]{2,1,0:T(8,128)(2,1)} %bitcast.38), calls=%async_computation | async-start | bytes 18350080 | tf_op jit(solution)/shard_map/all_to_all | solution.py:26
  25.1 0.0 copy-done.3
  25.1 0.6 dynamic-slice
  25.7 163.8 %all-to-all-done = bf16[16,80,3584]{2,1,0:T(8,128)(2,1)} async-done(((bf16[16,80,3584]{2,1,0:T(8,128)(2,1)}), bf16[16,80,3584]{2,1,0:T(8,128)(2,1)}, u32[]{:S(2)}, u32[]{:S(2)}) %all-to-all-start) | async-done | bytes 9175072 | tf_op jit(solution)/shard_map/all_to_all | solution.py:26
  189.5 0.0 copy-start.1
  189.5 8.6 %fusion.4 = f32[1280,512]{1,0:T(8,128)S(1)} fusion(bf16[1280,3584]{1,0:T(8,128)(2,1)} %bitcast.6, bf16[1,3584,512]{2,1,0:T(8,128)(2,1)} %param.9), kind=kOutput, calls=%fused_computation.8 | convolution fusion | flops 4697620480 | bytes 15466496 | tf_op jit(solution)/shard_map/dot_general | solution.py:29
  198.2 0.0 copy-done.1
  198.2 0.0 copy-start.2
  198.2 9.0 %fusion.9 = bf16[1280,512]{1,0:T(8,128)(2,1)S(1)} fusion(bf16[1280,3584]{1,0:T(8,128)(2,1)} %bitcast.6, bf16[1,3584,512]{2,1,0:T(8,128)(2,1)S(1)} %copy-done.1, f32[1280,512]{1,0:T(8,128)S(1)} %fusion.4), kind=kOutput, calls=%fused_computation.12 | convolution fusion | flops 4701552640 | bytes 16777216 | tf_op jit(solution)/shard_map/dot_general | solution.py:30
  207.2 0.0 copy-done.2
  207.2 8.9 %fusion = f32[8,2,80,3584]{3,2,1,0:T(8,128)} fusion(bf16[8,2,80,512]{3,2,1,0:T(8,128)(2,1)S(1)} %bitcast.43, bf16[1,512,3584]{2,1,0:T(8,128)(2,1)S(1)} %copy-done.2), kind=kOutput, calls=%fused_computation.4 | convolution fusion | flops 4697620480 | bytes 23330816 | tf_op jit(solution)/shard_map/dot_general | solution.py:32
  216.1 50.6 %all-reduce.3 = bf16[8,2,80,3584]{3,2,1,0:T(8,128)(2,1)} all-reduce(f32[8,2,80,3584]{3,2,1,0:T(8,128)} %fusion), channel_id=2, replica_groups=mesh['groups'=2,'node'=8,'local'=2] {'local'}, use_global_device_ids=true, to_apply=%region_4.5.clone | all-reduce | flops 4587520 | bytes 27525120
  266.7 5.3 %dynamic-slice_convert_fusion = bf16[8,1,80,3584]{3,2,1,0:T(8,128)(2,1)} fusion(bf16[8,2,80,3584]{3,2,1,0:T(8,128)(2,1)} %all-reduce.3, u32[]{:T(128)} %bitcast.19), kind=kLoop, calls=%fused_computation.3 | loop fusion | bytes 9175044 | tf_op jit(solution)/shard_map/convert_element_type | solution.py:34
  272.0 0.0 copy-start
  272.0 39.2 %all-to-all-start.1 = ((bf16[8,1,80,3584]{3,2,1,0:T(8,128)(2,1)}), bf16[8,1,80,3584]{3,2,1,0:T(8,128)(2,1)}, u32[]{:S(2)}, u32[]{:S(2)}) async-start(bf16[8,1,80,3584]{3,2,1,0:T(8,128)(2,1)} %dynamic-slice_convert_fusion), calls=%async_computation.1 | async-start | bytes 9175040 | tf_op jit(solution)/shard_map/all_to_all | solution.py:37
  311.2 0.0 copy-done
  311.2 0.1 copy.15
  311.4 102.8 %all-to-all-done.1 = bf16[8,1,80,3584]{3,2,1,0:T(8,128)(2,1)} async-done(((bf16[8,1,80,3584]{3,2,1,0:T(8,128)(2,1)}), bf16[8,1,80,3584]{3,2,1,0:T(8,128)(2,1)}, u32[]{:S(2)}, u32[]{:S(2)}) %all-to-all-start.1) | async-done | bytes 4587552 | tf_op jit(solution)/shard_map/all_to_all | solution.py:37
  414.2 6.4 %gather_fusion.1 = bf16[256,3584]{1,0:T(8,128)(2,1)S(1)} fusion(bf16[640,3584]{1,0:T(8,128)(2,1)} %bitcast.13, s32[1024]{0:T(1024)S(1)} %pad_clamp_fusion), kind=kCustom, calls=%fused_computation.1 | custom fusion | bytes 3671040 | tf_op jit(solution)/shard_map/gather | solution.py:39
  420.6 3.5 reshape.63
  424.1 8.2 %multiply_reduce_fusion = bf16[128,3584]{1,0:T(8,128)(2,1)} fusion(f32[128,2,3584]{2,1,0:T(2,128)} %reshape.63, f32[128,2]{1,0:T(8,128)S(1)} %copy.15), kind=kLoop, calls=%fused_computation.10 | loop fusion | flops 1376256 | bytes 4588544 | tf_op jit(solution)/shard_map/reduce_sum | solution.py:40
  (8 shorter events, 0.1 us)
Async XLA Ops:
  17.5 7.6 %copy-start.3 = (u32[32]{0:T(128)S(1)}, u32[32]{0:T(128)}, u32[]{:S(2)}) copy-start(u32[32]{0:T(128)} %constant.43) | copy-start | bytes 388
  17.5 172.0 %all-to-all-start = ((bf16[16,80,3584]{2,1,0:T(8,128)(2,1)}), bf16[16,80,3584]{2,1,0:T(8,128)(2,1)}, u32[]{:S(2)}, u32[]{:S(2)}) async-start(bf16[16,80,3584]{2,1,0:T(8,128)(2,1)} %bitcast.38), calls=%async_computation | async-start | bytes 18350080 | tf_op jit(solution)/shard_map/all_to_all | solution.py:26
  189.5 8.7 %copy-start.1 = (bf16[1,3584,512]{2,1,0:T(8,128)(2,1)S(1)}, bf16[1,3584,512]{2,1,0:T(8,128)(2,1)}, u32[]{:S(2)}) copy-start(bf16[1,3584,512]{2,1,0:T(8,128)(2,1)} %param.10) | copy-start | bytes 11010052
  198.2 9.0 %copy-start.2 = (bf16[1,512,3584]{2,1,0:T(8,128)(2,1)S(1)}, bf16[1,512,3584]{2,1,0:T(8,128)(2,1)}, u32[]{:S(2)}) copy-start(bf16[1,512,3584]{2,1,0:T(8,128)(2,1)} %param.11) | copy-start | bytes 11010052
  272.0 39.2 %copy-start = (f32[128,2]{0,1:T(2,128)S(1)}, f32[128,2]{0,1:T(2,128)}, u32[]{:S(2)}) copy-start(f32[128,2]{0,1:T(2,128)} %param.8) | copy-start | bytes 3076
  272.0 142.2 %all-to-all-start.1 = ((bf16[8,1,80,3584]{3,2,1,0:T(8,128)(2,1)}), bf16[8,1,80,3584]{3,2,1,0:T(8,128)(2,1)}, u32[]{:S(2)}, u32[]{:S(2)}) async-start(bf16[8,1,80,3584]{3,2,1,0:T(8,128)(2,1)} %dynamic-slice_convert_fusion), calls=%async_computation.1 | async-start | bytes 9175040 | tf_op jit(solution)/shard_map/all_to_all | solution.py:37
where the time goes:
time: 433 us; the launch traced here: 432 us
  waiting for transfers between devices  267 us (62%)
  blocking collectives  50.6 us (12%)
  starting transfers between devices  46.8 us (11%)
  local copies, waits for them, and re-layouts  32 us (7%)
  matrix products  26.5 us (6%)
  other arithmetic  9.63 us (2%)
    all_to_all x1, waiting for transfers between devices, on_device(): lax.all_to_all(copies, ('node', 'local'), split_axis=0, concat_axis=0, ti...  164 us
    all_to_all x1, waiting for transfers between devices, on_device(): lax.all_to_all(summed, 'node', split_axis=0, concat_axis=0, tiled=True)  103 us
    unnamed x1, blocking collectives  50.6 us
    all_to_all x1, starting transfers between devices, on_device(): lax.all_to_all(summed, 'node', split_axis=0, concat_axis=0, tiled=True)  39.2 us
    dot_general x1, matrix products, on_device(): up = jnp.dot(block_rows, w_up[0], preferred_element_type=jnp.float32)  9.03 us
    dot_general x1, matrix products, on_device(): jnp.dot(hidden, w_down[0], preferred_element_type=jnp.float32)  8.88 us
  transfers between devices with their start and end apart: 2, of which 2 were waited for; matrix products, arithmetic and copies ran while one was open for 0% of the time, Pallas kernels for 0%

commit v1 on v0

v1 whole, which is shorter than its diff:
```python
import jax
import jax.numpy as jnp
from jax import lax
from jax.sharding import PartitionSpec as P


def on_device(tokens, routes, route_scale, w_gate, w_up, w_down):
    count, width = tokens.shape
    experts = lax.axis_size("node")
    me = lax.axis_index("node")
    swap = [(0, 1), (1, 0)]
    own = (w_gate[0], w_up[0], w_down[0])
    other = tuple(lax.ppermute(w, "local", swap) for w in own)
    every = lax.all_gather(tokens, "node", axis=0, tiled=True)
    mine = jnp.arange(experts, dtype=jnp.int32)
    weight = jnp.sum(
        jnp.where(routes[None, :, :] == mine[:, None, None], route_scale[None, :, :], 0.0), axis=2
    )
    weight = lax.all_gather(weight, "node", axis=0, tiled=False)
    weight = lax.dynamic_index_in_dim(weight, me, axis=1, keepdims=False).reshape(-1)
    scaled = []
    for rows, factor in zip(jnp.split(every, experts // 8), jnp.split(weight, experts // 8)):
        total = 0.0
        for gate_w, up_w, down_w in (own, other):
            gate = jnp.dot(rows, gate_w, preferred_element_type=jnp.float32)
            up = jnp.dot(rows, up_w, preferred_element_type=jnp.float32)
            hidden = (jax.nn.silu(gate) * up).astype(jnp.bfloat16)
            total = total + jnp.dot(hidden, down_w, preferred_element_type=jnp.float32)
        scaled.append((total * factor[:, None]).astype(jnp.bfloat16))
    scaled = jnp.concatenate(scaled, axis=0)
    return lax.psum_scatter(scaled, "node", scatter_dimension=0, tiled=True)


def solution(mesh):
    placed = (
        P(("groups", "node", "local"), None),
        P(("groups", "node", "local"), None),
        P(("groups", "node", "local"), None),
        P("node", None, "local"),
        P("node", None, "local"),
        P("node", "local", None),
    )
    return jax.shard_map(
        on_device,
        mesh=mesh,
        in_specs=placed,
        out_specs=P(("groups", "node", "local"), None),
        check_vma=False,
    )
```

time: 433 us -> 310 us (0.72)
  waiting for transfers between devices: 267 us -> 215 us
  starting transfers between devices: 46.8 us -> 1.07 us
  local copies, waits for them, and re-layouts: 32 us -> 0.01 us
  matrix products: 26.5 us -> 47.5 us
  blocking collectives: 50.6 us -> 32.2 us
  between operations: 0.13 us -> 13.4 us
  other arithmetic: 9.63 us -> 0.7 us
    all_to_all x2 -> x0, waiting for transfers between devices: 267 us -> none  [the longest x1 164 us: on_device(): lax.all_to_all(copies, ('node', 'local'), split_axis=0, concat_axis=0, ti...]
    reduce_scatter x0 -> x1, waiting for transfers between devices: none -> 131 us  [on_device(): return lax.psum_scatter(scaled, 'node', scatter_dimension=0, tiled=True)]
    all_gather x0 -> x1, waiting for transfers between devices: none -> 83.2 us  [on_device(): every = lax.all_gather(tokens, 'node', axis=0, tiled=True)]
    unnamed x1 -> x0, blocking collectives: 50.6 us -> none
    all_to_all x2 -> x0, starting transfers between devices: 46.8 us -> none  [the longest x1 39.2 us: on_device(): lax.all_to_all(summed, 'node', split_axis=0, concat_axis=0, tiled=True)]
    all_gather x0 -> x1, blocking collectives: none -> 32.2 us  [on_device(): weight = lax.all_gather(weight, 'node', axis=0, tiled=False)]
    dot_general x3 -> x4, matrix products: 26.5 us -> 47.5 us  [the longest x2 31.9 us: on_device(): total = total + jnp.dot(hidden, down_w, preferred_element_type=jnp.float32)]
    gather x2 -> x0, local copies, waits for them, and re-layouts: 11.6 us -> none  [the longest x1 6.42 us: on_device(): picked = returned[dest].astype(jnp.float32).reshape(count, 2, width)]
  transfers between devices with their start and end apart: 2 -> 5, of which waited for: 2 -> 2; matrix products, arithmetic and copies ran while one was open for 0% -> 10% of each run, Pallas kernels for 0% -> 0%
where the time goes in v1:
time: 310 us
  waiting for transfers between devices  215 us (69%)
  matrix products  47.5 us (15%)
  blocking collectives  32.2 us (10%)
  between operations  13.4 us (4%)
    reduce_scatter x1, waiting for transfers between devices, on_device(): return lax.psum_scatter(scaled, 'node', scatter_dimension=0, tiled=True)  131 us
    all_gather x1, waiting for transfers between devices, on_device(): every = lax.all_gather(tokens, 'node', axis=0, tiled=True)  83.2 us
    all_gather x1, blocking collectives, on_device(): weight = lax.all_gather(weight, 'node', axis=0, tiled=False)  32.2 us
    dot_general x2, matrix products, on_device(): total = total + jnp.dot(hidden, down_w, preferred_element_type=jnp.float32)  31.9 us
    dot_general x2, matrix products, on_device(): gate = jnp.dot(rows, gate_w, preferred_element_type=jnp.float32)  15.6 us
  transfers between devices with their start and end apart: 5, of which 2 were waited for; matrix products, arithmetic and copies ran while one was open for 10% of the time, Pallas kernels for 0%

profile of v1, /device:TPU:0, one launch (start us, length us, event | category | flops | bytes accessed | tf_op | source)
XLA Modules:
  0.0 309.9 jit_solution(4772907442263888816)
XLA Ops:
  6.5 0.0 all-gather.3.cloned.1.call-start
  6.5 0.7 all-gather.3.cloned.1.call-update
  7.3 0.0 reduce-scatter.2.cloned.1.call-start
  7.3 0.5 collective-permute-start
  7.8 0.1 collective-permute-start.2
  7.9 0.4 collective-permute-start.1
  8.3 0.7 select_reduce_fusion
  9.0 32.2 %all-gather = f32[64,128]{1,0:T(8,128)S(1)} all-gather(f32[8,128]{1,0:T(8,128)S(1)} %select_reduce_fusion), channel_id=2, replica_groups=mesh['groups'=2,'node'=8,'local'=2] {'node'}, dimensions={0}, use_global_device_ids=true | all-gather | bytes 36864 | tf_op jit(solution)/shard_map/all_gather | solution.py:19
  41.3 83.2 %all-gather.3.cloned.1.call-done = bf16[1024,3584]{1,0:T(8,128)(2,1)} async-done(((bf16[128,3584]{1,0:T(8,128)(2,1)}), bf16[1024,3584]{1,0:T(8,128)(2,1)}) %all-gather.3.cloned.1.call-update) | async-done | bytes 7340048 | tf_op jit(solution)/shard_map/all_gather | solution.py:14
  124.5 0.0 copy-start
  124.5 9.6 %fusion.5 = f32[1024,512]{1,0:T(8,128)} fusion(bf16[1024,3584]{1,0:T(8,128)(2,1)} %all-gather.3.cloned.1.call-done, bf16[1,3584,512]{2,1,0:T(8,128)(2,1)} %param.9), kind=kOutput, calls=%fused_computation.10 | convolution fusion | flops 3758096384 | bytes 13107200 | tf_op jit(solution)/shard_map/dot_general | solution.py:25
  134.0 0.0 collective-permute-done
  134.0 0.0 copy-done
  134.1 6.0 %fusion.11 = f32[1024,512]{1,0:T(8,128)S(1)} fusion(bf16[1024,3584]{1,0:T(8,128)(2,1)S(1)} %copy-done, bf16[3584,512]{1,0:T(8,128)(2,1)} %collective-permute-done), kind=kOutput, calls=%fused_computation.15 | convolution fusion | flops 3758096384 | bytes 13107200 | tf_op jit(solution)/shard_map/dot_general | solution.py:25
  140.0 15.6 %fusion.1 = f32[1024,3584]{1,0:T(8,128)} fusion(f32[1024,512]{1,0:T(8,128)} %fusion.5, bf16[1024,3584]{1,0:T(8,128)(2,1)} %all-gather.3.cloned.1.call-done, bf16[1,512,3584]{2,1,0:T(8,128)(2,1)} %param.11, bf16[1,3584,512]{2,1,0:T(8,128)(2,1)} %param.10), kind=kOutput, calls=%fused_computation.4 | convolution fusion | flops 7519338496 | bytes 31457280 | tf_op jit(solution)/shard_map/dot_general | solution.py:28
  155.7 0.0 collective-permute-done.2
  155.7 0.0 collective-permute-done.1
  155.7 16.3 %multiply_convert_fusion = bf16[1024,3584]{1,0:T(8,128)(2,1)} fusion(f32[1024,3584]{1,0:T(8,128)} %fusion.1, bf16[512,3584]{1,0:T(8,128)(2,1)} %collective-permute-done.2, f32[1024]{0:T(1024)S(1)} %bitcast.20, f32[1024,512]{1,0:T(8,128)S(1)} %fusion.11, bf16[1024,3584]{1,0:T(8,128)(2,1)} %all-gather.3.cloned.1.call-done, ...), kind=kOutput, calls=%fused_computation | convolution fusion | flops 7530348544 | bytes 38801408 | tf_op jit(solution)/shard_map/dot_general | solution.py:28
  172.0 0.0 reduce-scatter.2.cloned.1.call-update
  172.0 131.0 %reduce-scatter.2.cloned.1.call-done = bf16[128,3584]{1,0:T(8,128)(2,1)} async-done(((bf16[1024,3584]{1,0:T(8,128)(2,1)}), bf16[128,3584]{1,0:T(8,128)(2,1)}) %reduce-scatter.2.cloned.1.call-update) | async-done | bytes 917520 | tf_op jit(solution)/shard_map/reduce_scatter | solution.py:31
  (1 shorter events, 0.0 us)
Async XLA Ops:
  6.5 117.9 %all-gather.3.cloned.1.call-start = ((), (), s32[]{:S(2)}) async-start(), calls=%async_computation.1 | async-start | bytes 8257536 | tf_op jit(solution)/shard_map/all_gather | solution.py:14
  7.3 295.8 %reduce-scatter.2.cloned.1.call-start = ((), (), s32[]{:S(2)}) async-start(), calls=%async_computation.2 | async-start | bytes 8257536 | tf_op jit(solution)/shard_map/reduce_scatter | solution.py:31
  7.3 126.7 %collective-permute-start = (bf16[3584,512]{1,0:T(8,128)(2,1)}, bf16[3584,512]{1,0:T(8,128)(2,1)}, u32[]{:S(2)}, u32[]{:S(2)}) collective-permute-start(bf16[3584,512]{1,0:T(8,128)(2,1)} %bitcast.21), channel_id=1, source_target_pairs={{0,1},{1,0},{2,3},{3,2},{4,5},{5,4},{6,7},{7,6},{8,9},{9,8},{10,11... | collective-permute-start | bytes 11010056 | tf_op jit(solution)/shard_map/ppermute | solution.py:13
  7.8 147.9 %collective-permute-start.2 = (bf16[512,3584]{1,0:T(8,128)(2,1)}, bf16[512,3584]{1,0:T(8,128)(2,1)}, u32[]{:S(2)}, u32[]{:S(2)}) collective-permute-start(bf16[512,3584]{1,0:T(8,128)(2,1)} %bitcast.22), channel_id=1, source_target_pairs={{0,1},{1,0},{2,3},{3,2},{4,5},{5,4},{6,7},{7,6},{8,9},{9,8},{10,11... | collective-permute-start | bytes 11010056 | tf_op jit(solution)/shard_map/ppermute | solution.py:13
  7.9 147.8 %collective-permute-start.1 = (bf16[3584,512]{1,0:T(8,128)(2,1)}, bf16[3584,512]{1,0:T(8,128)(2,1)}, u32[]{:S(2)}, u32[]{:S(2)}) collective-permute-start(bf16[3584,512]{1,0:T(8,128)(2,1)} %bitcast.23), channel_id=1, source_target_pairs={{0,1},{1,0},{2,3},{3,2},{4,5},{5,4},{6,7},{7,6},{8,9},{9,8},{10,11... | collective-permute-start | bytes 11010056 | tf_op jit(solution)/shard_map/ppermute | solution.py:13
  124.5 9.6 %copy-start = (bf16[1024,3584]{1,0:T(8,128)(2,1)S(1)}, bf16[1024,3584]{1,0:T(8,128)(2,1)}, u32[]{:S(2)}) copy-start(bf16[1024,3584]{1,0:T(8,128)(2,1)} %all-gather.3.cloned.1.call-done) | copy-start | bytes 22020100
Sparse Core Ops, SparseCore 0:
  9.5 114.8 all-gather.2
  172.1 130.8 reduce-scatter.1

commit v2 on v1

v2 whole, which is shorter than its diff:
```python
import jax
import jax.numpy as jnp
import numpy as np
from jax import lax
from jax.sharding import PartitionSpec as P


def arrivals(places):
    plan = []
    for place in range(places):
        spare, row = [], []
        for step in range(1, places):
            here = [way for way in (1, -1) if 0 <= place - way * step < places]
            if len(here) == 2 and place % 2 == 0:
                here.reverse()
            spare += [(way, step) for way in here[1:]]
            row.append((here[0], step) if here else spare.pop(0))
        plan.append(row)
    return plan


def parts_of(value):
    high = lax.reduce_precision(value, 8, 7)
    rest = value - high
    middle = lax.reduce_precision(rest, 8, 7)
    return [part.astype(jnp.bfloat16) for part in (high, middle, rest - middle)]


def on_device(tokens, routes, route_scale, w_gate, w_up, w_down):
    count, width = tokens.shape
    experts = lax.axis_size("node")
    places = experts // 2
    node = lax.axis_index("node")
    place, side = node // 2, node % 2
    cap = -(-(5 * count // experts) // 16) * 16

    swap = [(0, 1), (1, 0)]
    own = (w_gate[0], w_up[0], w_down[0])
    halves = (own, tuple(lax.ppermute(w, "local", swap) for w in own))

    def along(block, pairs):
        moves = [(2 * a + y, 2 * b + y) for a, b in pairs for y in range(2)]
        return lax.ppermute(block, "node", moves)

    def across(block):
        return lax.ppermute(block, "node", [(n, n ^ 1) for n in range(experts)])

    weight = jnp.sum(
        jnp.where(routes[:, :, None] == jnp.arange(experts, dtype=jnp.int32), route_scale[:, :, None], 0.0),
        axis=1,
    )
    marks = parts_of(weight)
    room = -(3 * experts) % 128
    block = jnp.concatenate([tokens, *marks, jnp.zeros((count, room), jnp.bfloat16)], axis=1)

    earlier = jnp.asarray(np.tri(count, k=-1), jnp.bfloat16)

    def picker(high):
        named = high != 0
        rank = jnp.dot(earlier, named.astype(jnp.bfloat16), preferred_element_type=jnp.float32)
        slot = jnp.arange(cap, dtype=jnp.float32)[:, None]
        return ((rank[None, :] == slot) & named[None, :]).astype(jnp.bfloat16)

    def column(rows, expert):
        return lax.dynamic_index_in_dim(rows, width + expert, axis=1, keepdims=False)

    def choose(candidates):
        picks, rows = [], []
        for expert in (node, node ^ 1):
            pick, row = 0, 0.0
            for cand, counts in candidates:
                one = picker(jnp.where(counts, column(cand, expert), 0))
                pick = pick + one
                row = row + jnp.dot(one, cand, preferred_element_type=jnp.float32)
            picks.append(pick)
            rows.append(row.astype(jnp.bfloat16))
        return jnp.concatenate(picks, axis=0), rows

    def expert_of(rows):
        data = rows[:, :width]
        scale = sum(
            lax.dynamic_index_in_dim(rows, width + k * experts + node, axis=1).astype(jnp.float32)
            for k in range(3)
        )
        total = 0.0
        for gate_w, up_w, down_w in halves:
            gate = jnp.dot(data, gate_w, preferred_element_type=jnp.float32)
            up = jnp.dot(data, up_w, preferred_element_type=jnp.float32)
            hidden = (jax.nn.silu(gate) * up).astype(jnp.bfloat16)
            total = total + jnp.dot(hidden, down_w, preferred_element_type=jnp.float32)
        return (total * scale).astype(jnp.bfloat16)

    def work(candidates):
        picks, (mine, theirs) = choose(candidates)
        rows = jnp.concatenate([mine, across(theirs)], axis=0)
        out = expert_of(rows)
        back = jnp.concatenate([out[:cap], across(out[cap:])], axis=0)
        return lax.dot_general(
            picks, back, (((0,), (0,)), ((), ())), preferred_element_type=jnp.float32
        ).astype(jnp.bfloat16)

    plan = arrivals(places)
    held = {}
    for step in range(1, places):
        for way in (1, -1):
            pairs = [
                (a, a + way)
                for a in range(places)
                if 0 <= a + way < places and 0 <= a - way * (step - 1) < places
            ]
            held[way, step] = along(held.get((way, step - 1), block), pairs)

    total = work([(block, True)]).astype(jnp.float32)
    for slot in range(places - 1):
        candidates = []
        for key in sorted({row[slot] for row in plan}):
            mine = np.array([row[slot] == key for row in plan])
            candidates.append((held[key], jnp.asarray(mine)[place]))
        done = work(candidates)
        home = [(a, a - row[slot][0] * row[slot][1]) for a, row in enumerate(plan)]
        while home:
            now = list({b: (a, b) for a, b in home}.values())
            home = [pair for pair in home if pair not in now]
            total = total + along(done, now).astype(jnp.float32)
    return total.astype(jnp.bfloat16)


def solution(mesh):
    placed = (
        P(("groups", "node", "local"), None),
        P(("groups", "node", "local"), None),
        P(("groups", "node", "local"), None),
        P("node", None, "local"),
        P("node", None, "local"),
        P("node", "local", None),
    )
    return jax.shard_map(
        on_device,
        mesh=mesh,
        in_specs=placed,
        out_specs=P(("groups", "node", "local"), None),
        check_vma=False,
    )
```

time: 310 us -> 281 us (0.906)
  waiting for transfers between devices: 215 us -> 105 us
  matrix products: 47.5 us -> 105 us
  starting transfers between devices: 1.07 us -> 37.5 us
  blocking collectives: 32.2 us -> 0 us
  other arithmetic: 0.7 us -> 16.5 us
  local copies, waits for them, and re-layouts: 0.01 us -> 14.3 us
  between operations: 13.4 us -> 0.73 us
    reduce_scatter x1 -> x0, waiting for transfers between devices: 131 us -> none  [on_device(): return lax.psum_scatter(scaled, 'node', scatter_dimension=0, tiled=True)]
    ppermute x3 -> x20, waiting for transfers between devices: 0.01 us -> 105 us  [the longest x9 73.8 us: along(): return lax.ppermute(block, 'node', moves)]
    all_gather x1 -> x0, waiting for transfers between devices: 83.2 us -> none  [on_device(): every = lax.all_gather(tokens, 'node', axis=0, tiled=True)]
    dot_general x4 -> x56, matrix products: 47.5 us -> 105 us  [the longest x8 49.3 us: expert_of(): total = total + jnp.dot(hidden, down_w, preferred_element_type=jnp.float32)]
    ppermute x3 -> x20, starting transfers between devices: 1.03 us -> 37.5 us  [the longest x9 27.9 us: along(): return lax.ppermute(block, 'node', moves)]
    all_gather x1 -> x0, blocking collectives: 32.2 us -> none  [on_device(): weight = lax.all_gather(weight, 'node', axis=0, tiled=False)]
    ne x0 -> x7, other arithmetic: none -> 10.3 us  [picker(): named = high != 0]
    slice x0 -> x4, local copies, waits for them, and re-layouts: none -> 5.8 us  [work(): back = jnp.concatenate([out[:cap], across(out[cap:])], axis=0)]
  transfers between devices with their start and end apart: 5 -> 20, of which waited for: 2 -> 9; matrix products, arithmetic and copies ran while one was open for 10% -> 43% of each run, Pallas kernels for 0% -> 0%
where the time goes in v2:
time: 281 us; the launch traced here: 279 us
  matrix products  105 us (37%)
  waiting for transfers between devices  105 us (37%)
  starting transfers between devices  37.5 us (13%)
  other arithmetic  16.5 us (6%)
  local copies, waits for them, and re-layouts  14.3 us (5%)
    ppermute x9, waiting for transfers between devices, along(): return lax.ppermute(block, 'node', moves)  73.8 us
    dot_general x8, matrix products, expert_of(): total = total + jnp.dot(hidden, down_w, preferred_element_type=jnp.float32)  49.3 us
    ppermute x8, waiting for transfers between devices, across(): return lax.ppermute(block, 'node', [(n, n ^ 1) for n in range(experts)])  31.6 us
    ppermute x9, starting transfers between devices, along(): return lax.ppermute(block, 'node', moves)  27.9 us
    dot_general x18, matrix products, choose(): row = row + jnp.dot(one, cand, preferred_element_type=jnp.float32)  26.2 us
    dot_general x8, matrix products, expert_of(): gate = jnp.dot(data, gate_w, preferred_element_type=jnp.float32)  20.5 us
    ne x7, other arithmetic, picker(): named = high != 0  10.3 us
    ppermute x8, starting transfers between devices, across(): return lax.ppermute(block, 'node', [(n, n ^ 1) for n in range(experts)])  9.03 us
  transfers between devices with their start and end apart: 20, of which 9 were waited for; matrix products, arithmetic and copies ran while one was open for 43% of the time, Pallas kernels for 0%

profile of v2, /device:TPU:0, one launch (start us, length us, event | category | flops | bytes accessed | tf_op | source)
XLA Modules:
  0.0 279.4 jit_solution(8357667038547495661)
XLA Ops:
  1.1 1.3 concatenate.42
  2.9 1.1 convolution_convert_fusion.4
  4.0 3.0 %collective-permute-start = (bf16[80,3712]{1,0:T(8,128)(2,1)}, bf16[80,3712]{1,0:T(8,128)(2,1)S(1)}, u32[]{:S(2)}, u32[]{:S(2)}) collective-permute-start(bf16[80,3712]{1,0:T(8,128)(2,1)} %convolution_convert_fusion.4), channel_id=1, source_target_pairs={{0,2},{2,0},{4,6},{6,4},{8,10},{10,8},{12,14},{14,12},{1,3},{3,1},... | collective-permute-start | bytes 1781768 | tf_op jit(solution)/shard_map/ppermute | solution.py:46
  7.0 4.4 %collective-permute-start.6 = (bf16[128,3712]{1,0:T(8,128)(2,1)S(1)}, bf16[128,3712]{1,0:T(8,128)(2,1)}, u32[]{:S(2)}, u32[]{:S(2)}) collective-permute-start(bf16[128,3712]{1,0:T(8,128)(2,1)S(1)} %concatenate.42), channel_id=1, source_target_pairs={{0,4},{2,6},{4,8},{6,10},{8,12},{10,14},{1,5},{3,7},{5,9},{7,11},{... | collective-permute-start | bytes 2850824 | tf_op jit(solution)/shard_map/ppermute | solution.py:43
  11.4 1.3 collective-permute-start.5
  18.5 2.1 collective-permute-done
  22.6 1.7 add_reduce_fusion.3
  24.2 1.5 fusion.231
  25.7 6.2 %fusion.37 = f32[160,3584]{1,0:T(8,128)} fusion(f32[160,512]{1,0:T(8,128)} %fusion.231, bf16[1,512,3584]{2,1,0:T(8,128)(2,1)} %param.20, bf16[160,3584]{1,0:T(8,128)(2,1)S(1)} %fusion.24, bf16[1,3584,512]{2,1,0:T(8,128)(2,1)} %param.19), kind=kOutput, calls=%fused_computation.113 | convolution fusion | flops 1174896640 | bytes 11108352 | tf_op jit(solution)/shard_map/dot_general | solution.py:90
  31.9 2.3 compare_reduce_fusion.12
  34.4 1.1 collective-permute-done.5
  35.5 1.3 compare_reduce_fusion.13
  37.7 1.5 fusion.86
  40.3 1.3 collective-permute-start.10
  41.6 1.5 fusion.79
  43.1 2.5 fusion.111
  45.7 1.4 fusion.104
  47.1 2.5 fusion.125
  49.7 1.4 fusion.118
  51.4 3.0 %collective-permute-done.7 = bf16[80,3712]{1,0:T(8,128)(2,1)S(1)} collective-permute-done((bf16[80,3712]{1,0:T(8,128)(2,1)S(1)}, bf16[80,3712]{1,0:T(8,128)(2,1)S(1)}, u32[]{:S(2)}, u32[]{:S(2)}) %collective-permute-start.7) | collective-permute-done | bytes 593952 | tf_op jit(solution)/shard_map/ppermute | solution.py:46
  54.4 1.6 collective-permute-start.11
  56.8 1.5 fusion.229
  58.3 6.1 %fusion.38 = f32[160,3584]{1,0:T(8,128)} fusion(f32[160,512]{1,0:T(8,128)} %fusion.229, bf16[1,512,3584]{2,1,0:T(8,128)(2,1)} %param.20, bf16[160,3584]{1,0:T(8,128)(2,1)S(1)} %fusion.23, bf16[1,3584,512]{2,1,0:T(8,128)(2,1)} %param.19), kind=kOutput, calls=%fused_computation.114 | convolution fusion | flops 1174896640 | bytes 11108352 | tf_op jit(solution)/shard_map/dot_general | solution.py:90
  64.4 1.6 compare_reduce_fusion.8
  66.1 1.7 compare_reduce_fusion.9
  68.2 1.5 fusion.100
  69.7 1.5 fusion.18
  71.2 1.8 collective-permute-start.12
  73.1 1.3 collective-permute-start.15
  74.4 1.5 fusion.93
  75.9 1.7 fusion.17
  77.5 8.9 %collective-permute-done.12 = bf16[80,3712]{1,0:T(8,128)(2,1)S(1)} collective-permute-done((bf16[80,3712]{1,0:T(8,128)(2,1)S(1)}, bf16[80,3712]{1,0:T(8,128)(2,1)S(1)}, u32[]{:S(2)}, u32[]{:S(2)}) %collective-permute-start.12) | collective-permute-done | bytes 593952 | tf_op jit(solution)/shard_map/ppermute | solution.py:46
  86.4 1.6 collective-permute-start.16
  88.9 1.5 fusion.227
  90.4 6.1 %fusion.39 = f32[160,3584]{1,0:T(8,128)} fusion(f32[160,512]{1,0:T(8,128)} %fusion.227, bf16[1,512,3584]{2,1,0:T(8,128)(2,1)} %param.20, bf16[160,3584]{1,0:T(8,128)(2,1)S(1)} %fusion.22, bf16[1,3584,512]{2,1,0:T(8,128)(2,1)} %param.19), kind=kOutput, calls=%fused_computation.115 | convolution fusion | flops 1174896640 | bytes 11108352 | tf_op jit(solution)/shard_map/dot_general | solution.py:90
  96.5 13.5 %collective-permute-done.15 = bf16[128,3712]{1,0:T(8,128)(2,1)} collective-permute-done((bf16[128,3712]{1,0:T(8,128)(2,1)}, bf16[128,3712]{1,0:T(8,128)(2,1)}, u32[]{:S(2)}, u32[]{:S(2)}) %collective-permute-start.15) | collective-permute-done | bytes 950304 | tf_op jit(solution)/shard_map/ppermute | solution.py:43
  110.0 1.7 compare_reduce_fusion.2
  111.7 1.6 compare_reduce_fusion
  113.5 2.3 fusion.13
  115.9 1.7 fusion.20
  119.2 1.6 fusion.14
  120.8 1.7 fusion.19
  122.4 8.4 %collective-permute-done.17 = bf16[80,3712]{1,0:T(8,128)(2,1)S(1)} collective-permute-done((bf16[80,3712]{1,0:T(8,128)(2,1)S(1)}, bf16[80,3712]{1,0:T(8,128)(2,1)S(1)}, u32[]{:S(2)}, u32[]{:S(2)}) %collective-permute-start.17) | collective-permute-done | bytes 593952 | tf_op jit(solution)/shard_map/ppermute | solution.py:46
  132.2 1.5 fusion.225
  133.7 6.4 %fusion.40 = f32[160,3584]{1,0:T(8,128)} fusion(f32[160,512]{1,0:T(8,128)} %fusion.225, bf16[1,512,3584]{2,1,0:T(8,128)(2,1)} %param.20, bf16[160,3584]{1,0:T(8,128)(2,1)} %copy-done.4, bf16[1,3584,512]{2,1,0:T(8,128)(2,1)} %param.19), kind=kOutput, calls=%fused_computation.116 | convolution fusion | flops 1174896640 | bytes 11108352 | tf_op jit(solution)/shard_map/dot_general | solution.py:90
  140.1 3.9 %fusion.258 = f32[160,512]{1,0:T(8,128)} fusion(bf16[160,3584]{1,0:T(8,128)(2,1)} %copy-done.4, bf16[3584,512]{1,0:T(8,128)(2,1)} %collective-permute-done.1), kind=kOutput, calls=%fused_computation.342 | convolution fusion | flops 587202560 | bytes 5144576 | tf_op jit(solution)/shard_map/dot_general | solution.py:87
  144.0 6.7 %fusion.4 = bf16[160,3584]{1,0:T(8,128)(2,1)} fusion(f32[160,3584]{1,0:T(8,128)} %fusion.40, bf16[512,3584]{1,0:T(8,128)(2,1)} %collective-permute-done.3, f32[160]{0:T(256)S(1)} %add_reduce_fusion, f32[160,512]{1,0:T(8,128)} %fusion.258, bf16[160,3584]{1,0:T(8,128)(2,1)} %copy-done.4, bf16[3584,512]{1,0:T(8,128)(2,1)} %collective-permute-done.2), kind=kOutput, calls=%fused_computation.8 | convolution fusion | flops 1176616960 | bytes 12255872 | tf_op jit(solution)/shard_map/dot_general | solution.py:90
  150.7 2.3 fusion.246
  153.6 3.5 %fusion.257 = f32[160,512]{1,0:T(8,128)} fusion(bf16[160,3584]{1,0:T(8,128)(2,1)S(1)} %fusion.22, bf16[3584,512]{1,0:T(8,128)(2,1)} %collective-permute-done.1), kind=kOutput, calls=%fused_computation.341 | convolution fusion | flops 587202560 | bytes 5144576 | tf_op jit(solution)/shard_map/dot_general | solution.py:87
  157.1 6.4 %fusion.5 = bf16[160,3584]{1,0:T(8,128)(2,1)} fusion(f32[160,3584]{1,0:T(8,128)} %fusion.39, bf16[512,3584]{1,0:T(8,128)(2,1)} %collective-permute-done.3, f32[160]{0:T(256)S(1)} %copy-done.39, f32[160,512]{1,0:T(8,128)} %fusion.257, bf16[160,3584]{1,0:T(8,128)(2,1)S(1)} %fusion.22, bf16[3584,512]{1,0:T(8,128)(2,1)} %collective-permute-done.2), kind=kOutput, calls=%fused_computation.9 | convolution fusion | flops 1176616960 | bytes 12255872 | tf_op jit(solution)/shard_map/dot_general | solution.py:90
  163.5 2.3 fusion.245
  165.8 1.5 collective-permute-start.13
  167.3 3.5 %fusion.256 = f32[160,512]{1,0:T(8,128)} fusion(bf16[160,3584]{1,0:T(8,128)(2,1)S(1)} %fusion.23, bf16[3584,512]{1,0:T(8,128)(2,1)} %collective-permute-done.1), kind=kOutput, calls=%fused_computation.340 | convolution fusion | flops 587202560 | bytes 5144576 | tf_op jit(solution)/shard_map/dot_general | solution.py:87
  170.8 5.4 %fusion.6 = bf16[160,3584]{1,0:T(8,128)(2,1)S(1)} fusion(f32[160,3584]{1,0:T(8,128)} %fusion.38, bf16[512,3584]{1,0:T(8,128)(2,1)} %collective-permute-done.3, f32[160]{0:T(256)S(1)} %copy-done.38, f32[160,512]{1,0:T(8,128)} %fusion.256, bf16[160,3584]{1,0:T(8,128)(2,1)S(1)} %fusion.23, bf16[3584,512]{1,0:T(8,128)(2,1)} %collective-permute-done.2), kind=kOutput, calls=%fused_computation.10 | convolution fusion | flops 1176616960 | bytes 12255872 | tf_op jit(solution)/shard_map/dot_general | solution.py:90
  177.8 3.7 %fusion.255 = f32[160,512]{1,0:T(8,128)} fusion(bf16[160,3584]{1,0:T(8,128)(2,1)S(1)} %fusion.24, bf16[3584,512]{1,0:T(8,128)(2,1)} %collective-permute-done.1), kind=kOutput, calls=%fused_computation.339 | convolution fusion | flops 587202560 | bytes 5144576 | tf_op jit(solution)/shard_map/dot_general | solution.py:87
  181.5 6.0 %fusion.7 = bf16[160,3584]{1,0:T(8,128)(2,1)} fusion(f32[160,3584]{1,0:T(8,128)S(1)} %copy-done.6, bf16[512,3584]{1,0:T(8,128)(2,1)} %collective-permute-done.3, f32[160]{0:T(256)S(1)} %copy-done.37, f32[160,512]{1,0:T(8,128)} %fusion.255, bf16[160,3584]{1,0:T(8,128)(2,1)S(1)} %fusion.24, bf16[3584,512]{1,0:T(8,128)(2,1)} %collective-permute-done.2), kind=kOutput, calls=%fused_computation.11 | convolution fusion | flops 1176616960 | bytes 12255872 | tf_op jit(solution)/shard_map/dot_general | solution.py:90
  187.5 1.7 convolution_convert_fusion
  189.3 15.7 %collective-permute-start.19 = (bf16[128,3584]{1,0:T(8,128)(2,1)S(1)}, bf16[128,3584]{1,0:T(8,128)(2,1)S(1)}, u32[]{:S(2)}, u32[]{:S(2)}) collective-permute-start(bf16[128,3584]{1,0:T(8,128)(2,1)S(1)} %convolution_convert_fusion), channel_id=1, source_target_pairs={{0,12},{2,14},{4,8},{6,10},{8,4},{10,6},{12,0},{14,2},{1,13},{3,15... | collective-permute-start | bytes 2752520 | tf_op jit(solution)/shard_map/ppermute | solution.py:43
  205.0 1.5 convolution_convert_fusion.1
  206.6 1.6 convolution_convert_fusion.2
  209.4 9.2 %collective-permute-done.4 = bf16[80,3584]{1,0:T(8,128)(2,1)S(1)} collective-permute-done((bf16[80,3584]{1,0:T(8,128)(2,1)S(1)}, bf16[80,3584]{1,0:T(8,128)(2,1)S(1)}, u32[]{:S(2)}, u32[]{:S(2)}) %collective-permute-start.4) | collective-permute-done | bytes 573472 | tf_op jit(solution)/shard_map/ppermute | solution.py:46
  218.6 7.7 %collective-permute-done.19 = bf16[128,3584]{1,0:T(8,128)(2,1)S(1)} collective-permute-done((bf16[128,3584]{1,0:T(8,128)(2,1)S(1)}, bf16[128,3584]{1,0:T(8,128)(2,1)S(1)}, u32[]{:S(2)}, u32[]{:S(2)}) %collective-permute-start.19) | collective-permute-done | bytes 917536 | tf_op jit(solution)/shard_map/ppermute | solution.py:43
  226.3 51.5 %collective-permute-done.14 = bf16[128,3584]{1,0:T(8,128)(2,1)S(1)} collective-permute-done((bf16[128,3584]{1,0:T(8,128)(2,1)S(1)}, bf16[128,3584]{1,0:T(8,128)(2,1)S(1)}, u32[]{:S(2)}, u32[]{:S(2)}) %collective-permute-start.14) | collective-permute-done | bytes 917536 | tf_op jit(solution)/shard_map/ppermute | solution.py:43
  277.8 1.6 fusion.12
  (166 shorter events, 20.5 us)
Async XLA Ops:
  0.0 2.7 copy-start.5
  2.4 10.9 %copy-start.47 = (pred[4]{0:T(512)(128)(4,1)S(1)}, pred[4]{0:T(512)(128)(4,1)}, u32[]{:S(2)}) copy-start(pred[4]{0:T(512)(128)(4,1)} %constant.138.clone) | copy-start | bytes 16
  2.4 11.5 %copy-start.46 = (pred[4]{0:T(512)(128)(4,1)S(1)}, pred[4]{0:T(512)(128)(4,1)}, u32[]{:S(2)}) copy-start(pred[4]{0:T(512)(128)(4,1)} %constant.143.clone) | copy-start | bytes 16
  2.4 12.1 %copy-start.45 = (pred[4]{0:T(512)(128)(4,1)S(1)}, pred[4]{0:T(512)(128)(4,1)}, u32[]{:S(2)}) copy-start(pred[4]{0:T(512)(128)(4,1)} %constant.137.clone) | copy-start | bytes 16
  2.4 12.6 %copy-start.44 = (pred[4]{0:T(512)(128)(4,1)S(1)}, pred[4]{0:T(512)(128)(4,1)}, u32[]{:S(2)}) copy-start(pred[4]{0:T(512)(128)(4,1)} %constant.141.clone) | copy-start | bytes 16
  2.5 13.2 %copy-start.43 = (pred[4]{0:T(512)(128)(4,1)S(1)}, pred[4]{0:T(512)(128)(4,1)}, u32[]{:S(2)}) copy-start(pred[4]{0:T(512)(128)(4,1)} %constant.142.clone) | copy-start | bytes 16
  2.5 13.8 %copy-start.42 = (pred[4]{0:T(512)(128)(4,1)S(1)}, pred[4]{0:T(512)(128)(4,1)}, u32[]{:S(2)}) copy-start(pred[4]{0:T(512)(128)(4,1)} %constant.144.clone) | copy-start | bytes 16
  2.5 14.3 %copy-start.41 = (pred[4]{0:T(512)(128)(4,1)S(1)}, pred[4]{0:T(512)(128)(4,1)}, u32[]{:S(2)}) copy-start(pred[4]{0:T(512)(128)(4,1)} %constant.140.clone) | copy-start | bytes 16
  2.5 14.9 %copy-start.40 = (pred[4]{0:T(512)(128)(4,1)S(1)}, pred[4]{0:T(512)(128)(4,1)}, u32[]{:S(2)}) copy-start(pred[4]{0:T(512)(128)(4,1)} %constant.139.clone) | copy-start | bytes 16
  2.7 15.8 %copy-start.13 = (pred[128]{0:T(512)(128)(4,1)}, pred[128]{0:T(512)(128)(4,1)S(1)}, u32[]{:S(2)}) copy-start(pred[128]{0:T(512)(128)(4,1)S(1)} %get-tuple-element.5) | copy-start | bytes 388
  2.7 15.8 %copy-start.15 = (pred[128]{0:T(512)(128)(4,1)}, pred[128]{0:T(512)(128)(4,1)S(1)}, u32[]{:S(2)}) copy-start(pred[128]{0:T(512)(128)(4,1)S(1)} %get-tuple-element.6) | copy-start | bytes 388
  2.9 15.7 %copy-start.25 = (f32[128]{0:T(128)}, f32[128]{0:T(128)S(1)}, u32[]{:S(2)}) copy-start(f32[128]{0:T(128)S(1)} %convolution_bitcast_fusion.16) | copy-start | bytes 1540
  4.0 16.6 %collective-permute-start = (bf16[80,3712]{1,0:T(8,128)(2,1)}, bf16[80,3712]{1,0:T(8,128)(2,1)S(1)}, u32[]{:S(2)}, u32[]{:S(2)}) collective-permute-start(bf16[80,3712]{1,0:T(8,128)(2,1)} %convolution_convert_fusion.4), channel_id=1, source_target_pairs={{0,2},{2,0},{4,6},{6,4},{8,10},{10,8},{12,14},{14,12},{1,3},{3,1},... | collective-permute-start | bytes 1781768 | tf_op jit(solution)/shard_map/ppermute | solution.py:46
  7.0 24.9 %collective-permute-start.6 = (bf16[128,3712]{1,0:T(8,128)(2,1)S(1)}, bf16[128,3712]{1,0:T(8,128)(2,1)}, u32[]{:S(2)}, u32[]{:S(2)}) collective-permute-start(bf16[128,3712]{1,0:T(8,128)(2,1)S(1)} %concatenate.42), channel_id=1, source_target_pairs={{0,4},{2,6},{4,8},{6,10},{8,12},{10,14},{1,5},{3,7},{5,9},{7,11},{... | collective-permute-start | bytes 2850824 | tf_op jit(solution)/shard_map/ppermute | solution.py:43
  11.4 24.1 %collective-permute-start.5 = (bf16[128,3712]{1,0:T(8,128)(2,1)S(1)}, bf16[128,3712]{1,0:T(8,128)(2,1)S(1)}, u32[]{:S(2)}, u32[]{:S(2)}) collective-permute-start(bf16[128,3712]{1,0:T(8,128)(2,1)S(1)} %concatenate.42), channel_id=1, source_target_pairs={{4,0},{6,2},{8,4},{10,6},{12,8},{14,10},{5,1},{7,3},{9,5},{11,7},{... | collective-permute-start | bytes 2850824 | tf_op jit(solution)/shard_map/ppermute | solution.py:43
  12.7 131.3 %collective-permute-start.3 = (bf16[512,3584]{1,0:T(8,128)(2,1)}, bf16[512,3584]{1,0:T(8,128)(2,1)}, u32[]{:S(2)}, u32[]{:S(2)}) collective-permute-start(bf16[512,3584]{1,0:T(8,128)(2,1)} %bitcast.206), channel_id=1, source_target_pairs={{0,1},{1,0},{2,3},{3,2},{4,5},{5,4},{6,7},{7,6},{8,9},{9,8},{10,11... | collective-permute-start | bytes 11010056 | tf_op jit(solution)/shard_map/ppermute | solution.py:39
  12.8 127.3 %collective-permute-start.1 = (bf16[3584,512]{1,0:T(8,128)(2,1)}, bf16[3584,512]{1,0:T(8,128)(2,1)}, u32[]{:S(2)}, u32[]{:S(2)}) collective-permute-start(bf16[3584,512]{1,0:T(8,128)(2,1)} %bitcast.205), channel_id=1, source_target_pairs={{0,1},{1,0},{2,3},{3,2},{4,5},{5,4},{6,7},{7,6},{8,9},{9,8},{10,11... | collective-permute-start | bytes 11010056 | tf_op jit(solution)/shard_map/ppermute | solution.py:39
  18.1 4.4 %copy-start.27 = (f32[128]{0:T(128)}, f32[128]{0:T(128)S(1)}, u32[]{:S(2)}) copy-start(f32[128]{0:T(128)S(1)} %convolution_bitcast_fusion.17) | copy-start | bytes 1540
  18.1 6.1 %copy-start = (bf16[1,3584,512]{2,1,0:T(8,128)(2,1)S(1)}, bf16[1,3584,512]{2,1,0:T(8,128)(2,1)}, u32[]{:S(2)}) copy-start(bf16[1,3584,512]{2,1,0:T(8,128)(2,1)} %param.18) | copy-start | bytes 11010052
  21.4 122.6 %collective-permute-start.2 = (bf16[3584,512]{1,0:T(8,128)(2,1)}, bf16[3584,512]{1,0:T(8,128)(2,1)}, u32[]{:S(2)}, u32[]{:S(2)}) collective-permute-start(bf16[3584,512]{1,0:T(8,128)(2,1)} %bitcast.207), channel_id=1, source_target_pairs={{0,1},{1,0},{2,3},{3,2},{4,5},{5,4},{6,7},{7,6},{8,9},{9,8},{10,11... | collective-permute-start | bytes 11010056 | tf_op jit(solution)/shard_map/ppermute | solution.py:39
  34.2 8.9 %copy-start.17 = (pred[128]{0:T(512)(128)(4,1)}, pred[128]{0:T(512)(128)(4,1)S(1)}, u32[]{:S(2)}) copy-start(pred[128]{0:T(512)(128)(4,1)S(1)} %get-tuple-element.12) | copy-start | bytes 388
  34.2 12.8 %copy-start.19 = (pred[128]{0:T(512)(128)(4,1)}, pred[128]{0:T(512)(128)(4,1)S(1)}, u32[]{:S(2)}) copy-start(pred[128]{0:T(512)(128)(4,1)S(1)} %get-tuple-element.13) | copy-start | bytes 388
  34.4 8.8 %copy-start.29 = (f32[128]{0:T(128)}, f32[128]{0:T(128)S(1)}, u32[]{:S(2)}) copy-start(f32[128]{0:T(128)S(1)} %convolution_bitcast_fusion.5) | copy-start | bytes 1540
  36.9 8.8 %copy-start.21 = (pred[128]{0:T(512)(128)(4,1)}, pred[128]{0:T(512)(128)(4,1)S(1)}, u32[]{:S(2)}) copy-start(pred[128]{0:T(512)(128)(4,1)S(1)} %get-tuple-element.8) | copy-start | bytes 388
  36.9 12.8 %copy-start.23 = (pred[128]{0:T(512)(128)(4,1)}, pred[128]{0:T(512)(128)(4,1)S(1)}, u32[]{:S(2)}) copy-start(pred[128]{0:T(512)(128)(4,1)S(1)} %get-tuple-element.9) | copy-start | bytes 388
  37.0 8.7 %copy-start.31 = (f32[128]{0:T(128)}, f32[128]{0:T(128)S(1)}, u32[]{:S(2)}) copy-start(f32[128]{0:T(128)S(1)} %convolution_bitcast_fusion.7) | copy-start | bytes 1540
  37.1 9.9 %copy-start.33 = (f32[128]{0:T(128)}, f32[128]{0:T(128)S(1)}, u32[]{:S(2)}) copy-start(f32[128]{0:T(128)S(1)} %convolution_bitcast_fusion.1) | copy-start | bytes 1540
  39.6 14.8 %collective-permute-start.7 = (bf16[80,3712]{1,0:T(8,128)(2,1)S(1)}, bf16[80,3712]{1,0:T(8,128)(2,1)S(1)}, u32[]{:S(2)}, u32[]{:S(2)}) collective-permute-start(bf16[80,3712]{1,0:T(8,128)(2,1)S(1)} %fusion.16), channel_id=1, source_target_pairs={{0,2},{2,0},{4,6},{6,4},{8,10},{10,8},{12,14},{14,12},{1,3},{3,1},... | collective-permute-start | bytes 1781768 | tf_op jit(solution)/shard_map/ppermute | solution.py:46
  40.3 25.8 %collective-permute-start.10 = (bf16[128,3712]{1,0:T(8,128)(2,1)S(1)}, bf16[128,3712]{1,0:T(8,128)(2,1)}, u32[]{:S(2)}, u32[]{:S(2)}) collective-permute-start(bf16[128,3712]{1,0:T(8,128)(2,1)S(1)} %collective-permute-done.5), channel_id=1, source_target_pairs={{4,0},{6,2},{8,4},{10,6},{5,1},{7,3},{9,5},{11,7},{20,16},{22,18},... | collective-permute-start | bytes 2850824 | tf_op jit(solution)/shard_map/ppermute | solution.py:43
  49.7 1.7 copy-start.35
  51.1 5.7 %copy-start.1 = (bf16[1,3584,512]{2,1,0:T(8,128)(2,1)S(1)}, bf16[1,3584,512]{2,1,0:T(8,128)(2,1)}, u32[]{:S(2)}) copy-start(bf16[1,3584,512]{2,1,0:T(8,128)(2,1)} %param.18) | copy-start | bytes 11010052
  54.4 10.0 %collective-permute-start.11 = (bf16[128,3712]{1,0:T(8,128)(2,1)}, bf16[128,3712]{1,0:T(8,128)(2,1)}, u32[]{:S(2)}, u32[]{:S(2)}) collective-permute-start(bf16[128,3712]{1,0:T(8,128)(2,1)} %collective-permute-done.6), channel_id=1, source_target_pairs={{4,8},{6,10},{8,12},{10,14},{5,9},{7,11},{9,13},{11,15},{20,24},{2... | collective-permute-start | bytes 2850824 | tf_op jit(solution)/shard_map/ppermute | solution.py:43
  71.2 15.2 %collective-permute-start.12 = (bf16[80,3712]{1,0:T(8,128)(2,1)S(1)}, bf16[80,3712]{1,0:T(8,128)(2,1)S(1)}, u32[]{:S(2)}, u32[]{:S(2)}) collective-permute-start(bf16[80,3712]{1,0:T(8,128)(2,1)S(1)} %fusion.18), channel_id=1, source_target_pairs={{0,2},{2,0},{4,6},{6,4},{8,10},{10,8},{12,14},{14,12},{1,3},{3,1},... | collective-permute-start | bytes 1781768 | tf_op jit(solution)/shard_map/ppermute | solution.py:46
  73.1 36.9 %collective-permute-start.15 = (bf16[128,3712]{1,0:T(8,128)(2,1)}, bf16[128,3712]{1,0:T(8,128)(2,1)}, u32[]{:S(2)}, u32[]{:S(2)}) collective-permute-start(bf16[128,3712]{1,0:T(8,128)(2,1)} %collective-permute-done.10), channel_id=1, source_target_pairs={{4,0},{6,2},{5,1},{7,3},{20,16},{22,18},{21,17},{23,19}} | collective-permute-start | bytes 2850824 | tf_op jit(solution)/shard_map/ppermute | solution.py:43
  75.9 13.0 %copy-start.2 = (bf16[1,3584,512]{2,1,0:T(8,128)(2,1)S(1)}, bf16[1,3584,512]{2,1,0:T(8,128)(2,1)}, u32[]{:S(2)}) copy-start(bf16[1,3584,512]{2,1,0:T(8,128)(2,1)} %param.18) | copy-start | bytes 11010052
  86.4 25.2 %collective-permute-start.16 = (bf16[128,3712]{1,0:T(8,128)(2,1)}, bf16[128,3712]{1,0:T(8,128)(2,1)}, u32[]{:S(2)}, u32[]{:S(2)}) collective-permute-start(bf16[128,3712]{1,0:T(8,128)(2,1)} %collective-permute-done.11), channel_id=1, source_target_pairs={{8,12},{10,14},{9,13},{11,15},{24,28},{26,30},{25,29},{27,31}} | collective-permute-start | bytes 2850824 | tf_op jit(solution)/shard_map/ppermute | solution.py:43
  115.8 2.6 copy-start.18
  115.8 2.6 copy-start.20
  115.8 2.6 copy-start.22
  115.8 2.6 copy-start.24
  115.8 2.6 copy-start.30
  115.8 2.6 copy-start.32
  115.9 2.6 copy-start.34
  115.9 2.6 copy-start.36
  115.9 3.3 %copy-start.7 = (f32[80,3712]{1,0:T(8,128)S(1)}, f32[80,3712]{1,0:T(8,128)}, u32[]{:S(2)}) copy-start(f32[80,3712]{1,0:T(8,128)} %fusion.111) | copy-start | bytes 3563524
  115.9 3.3 %copy-start.8 = (f32[80,3712]{1,0:T(8,128)S(1)}, f32[80,3712]{1,0:T(8,128)}, u32[]{:S(2)}) copy-start(f32[80,3712]{1,0:T(8,128)} %fusion.104) | copy-start | bytes 3563524
  117.5 13.3 %collective-permute-start.17 = (bf16[80,3712]{1,0:T(8,128)(2,1)S(1)}, bf16[80,3712]{1,0:T(8,128)(2,1)S(1)}, u32[]{:S(2)}, u32[]{:S(2)}) collective-permute-start(bf16[80,3712]{1,0:T(8,128)(2,1)S(1)} %fusion.20), channel_id=1, source_target_pairs={{0,2},{2,0},{4,6},{6,4},{8,10},{10,8},{12,14},{14,12},{1,3},{3,1},... | collective-permute-start | bytes 1781768 | tf_op jit(solution)/shard_map/ppermute | solution.py:46
  120.7 11.4 %copy-start.3 = (bf16[1,3584,512]{2,1,0:T(8,128)(2,1)S(1)}, bf16[1,3584,512]{2,1,0:T(8,128)(2,1)}, u32[]{:S(2)}) copy-start(bf16[1,3584,512]{2,1,0:T(8,128)(2,1)} %param.18) | copy-start | bytes 11010052
  153.0 4.0 %copy-start.39 = (f32[160]{0:T(256)S(1)}, f32[160]{0:T(256)}, u32[]{:S(2)}) copy-start(f32[160]{0:T(256)} %add_reduce_fusion.1) | copy-start | bytes 1924
  153.0 34.5 %collective-permute-start.18 = (bf16[80,3584]{1,0:T(8,128)(2,1)}, bf16[80,3584]{1,0:T(8,128)(2,1)}, u32[]{:S(2)}, u32[]{:S(2)}) collective-permute-start(bf16[80,3584]{1,0:T(8,128)(2,1)} %get-tuple-element.30), channel_id=1, source_target_pairs={{0,2},{2,0},{4,6},{6,4},{8,10},{10,8},{12,14},{14,12},{1,3},{3,1},... | collective-permute-start | bytes 1720328 | tf_op jit(solution)/shard_map/ppermute | solution.py:46
  165.8 5.0 %copy-start.38 = (f32[160]{0:T(256)S(1)}, f32[160]{0:T(256)}, u32[]{:S(2)}) copy-start(f32[160]{0:T(256)} %add_reduce_fusion.2) | copy-start | bytes 1924
  165.8 39.2 %collective-permute-start.13 = (bf16[80,3584]{1,0:T(8,128)(2,1)}, bf16[80,3584]{1,0:T(8,128)(2,1)}, u32[]{:S(2)}, u32[]{:S(2)}) collective-permute-start(bf16[80,3584]{1,0:T(8,128)(2,1)} %get-tuple-element.28), channel_id=1, source_target_pairs={{0,2},{2,0},{4,6},{6,4},{8,10},{10,8},{12,14},{14,12},{1,3},{3,1},... | collective-permute-start | bytes 1720328 | tf_op jit(solution)/shard_map/ppermute | solution.py:46
  177.3 4.2 %copy-start.37 = (f32[160]{0:T(256)S(1)}, f32[160]{0:T(256)}, u32[]{:S(2)}) copy-start(f32[160]{0:T(256)} %add_reduce_fusion.3) | copy-start | bytes 1924
  177.3 29.2 %collective-permute-start.8 = (bf16[80,3584]{1,0:T(8,128)(2,1)}, bf16[80,3584]{1,0:T(8,128)(2,1)}, u32[]{:S(2)}, u32[]{:S(2)}) collective-permute-start(bf16[80,3584]{1,0:T(8,128)(2,1)} %get-tuple-element.26), channel_id=1, source_target_pairs={{0,2},{2,0},{4,6},{6,4},{8,10},{10,8},{12,14},{14,12},{1,3},{3,1},... | collective-permute-start | bytes 1720328 | tf_op jit(solution)/shard_map/ppermute | solution.py:46
  177.8 3.7 %copy-start.6 = (f32[160,3584]{1,0:T(8,128)S(1)}, f32[160,3584]{1,0:T(8,128)}, u32[]{:S(2)}) copy-start(f32[160,3584]{1,0:T(8,128)} %fusion.37) | copy-start | bytes 6881284
  187.5 17.5 %copy-start.12 = (bf16[80,3584]{1,0:T(8,128)(2,1)S(1)}, bf16[80,3584]{1,0:T(8,128)(2,1)}, u32[]{:S(2)}) copy-start(bf16[80,3584]{1,0:T(8,128)(2,1)} %get-tuple-element.27) | copy-start | bytes 1720324
  189.3 17.3 %copy-start.11 = (bf16[80,3584]{1,0:T(8,128)(2,1)S(1)}, bf16[80,3584]{1,0:T(8,128)(2,1)}, u32[]{:S(2)}) copy-start(bf16[80,3584]{1,0:T(8,128)(2,1)} %get-tuple-element.25) | copy-start | bytes 1720324
  189.3 37.1 %collective-permute-start.19 = (bf16[128,3584]{1,0:T(8,128)(2,1)S(1)}, bf16[128,3584]{1,0:T(8,128)(2,1)S(1)}, u32[]{:S(2)}, u32[]{:S(2)}) collective-permute-start(bf16[128,3584]{1,0:T(8,128)(2,1)S(1)} %convolution_convert_fusion), channel_id=1, source_target_pairs={{0,12},{2,14},{4,8},{6,10},{8,4},{10,6},{12,0},{14,2},{1,13},{3,15... | collective-permute-start | bytes 2752520 | tf_op jit(solution)/shard_map/ppermute | solution.py:43
  206.5 2.3 copy-start.9
  206.5 71.3 %collective-permute-start.14 = (bf16[128,3584]{1,0:T(8,128)(2,1)S(1)}, bf16[128,3584]{1,0:T(8,128)(2,1)S(1)}, u32[]{:S(2)}, u32[]{:S(2)}) collective-permute-start(bf16[128,3584]{1,0:T(8,128)(2,1)S(1)} %convolution_convert_fusion.1), channel_id=1, source_target_pairs={{0,8},{2,10},{4,12},{6,14},{8,0},{10,2},{12,4},{14,6},{1,9},{3,11}... | collective-permute-start | bytes 2752520 | tf_op jit(solution)/shard_map/ppermute | solution.py:43
  208.1 1.2 copy-start.14
  208.1 1.2 copy-start.16
  208.2 69.6 %collective-permute-start.9 = (bf16[128,3584]{1,0:T(8,128)(2,1)S(1)}, bf16[128,3584]{1,0:T(8,128)(2,1)S(1)}, u32[]{:S(2)}, u32[]{:S(2)}) collective-permute-start(bf16[128,3584]{1,0:T(8,128)(2,1)S(1)} %convolution_convert_fusion.2), channel_id=1, source_target_pairs={{0,4},{2,6},{4,0},{6,2},{8,12},{10,14},{12,8},{14,10},{1,5},{3,7},... | collective-permute-start | bytes 2752520 | tf_op jit(solution)/shard_map/ppermute | solution.py:43
  208.9 9.8 %collective-permute-start.4 = (bf16[80,3584]{1,0:T(8,128)(2,1)S(1)}, bf16[80,3584]{1,0:T(8,128)(2,1)S(1)}, u32[]{:S(2)}, u32[]{:S(2)}) collective-permute-start(bf16[80,3584]{1,0:T(8,128)(2,1)S(1)} %get-tuple-element.24), channel_id=1, source_target_pairs={{0,2},{2,0},{4,6},{6,4},{8,10},{10,8},{12,14},{14,12},{1,3},{3,1},... | collective-permute-start | bytes 1720328 | tf_op jit(solution)/shard_map/ppermute | solution.py:46
  (4 other events, 4.3 us)

commit v3 on v1

v3 whole, which is shorter than its diff:
```python
import functools

import jax
import jax.numpy as jnp
from jax import lax
from jax.experimental import pallas as pl
from jax.experimental.pallas import tpu as pltpu
from jax.sharding import PartitionSpec as P

ANYWHERE = pl.BlockSpec(memory_space=pl.ANY)
IN_VMEM = pl.BlockSpec(memory_space=pltpu.VMEM)
MIB = 1024 * 1024


def arrivals(places):
    plan = []
    for place in range(places):
        left = [(-1, step) for step in range(1, places - place)]
        right = [(1, step) for step in range(1, place + 1)]
        plan.append(left + right if place < places // 2 else right + left)
    return plan


def call(kernel, outs, ins, after=(), scratch=(), specs=None, vmem=24):
    body = kernel
    if after:
        first, last = len(ins), len(ins) + len(after)

        def body(*refs):
            kernel(*refs[:first], *refs[last:])

    specs = list(specs or [IN_VMEM] * len(ins)) + [ANYWHERE] * len(after)
    return pl.pallas_call(
        body,
        out_shape=outs,
        in_specs=specs,
        out_specs=[IN_VMEM] * len(outs),
        scratch_shapes=scratch,
        compiler_params=pltpu.CompilerParams(vmem_limit_bytes=vmem * MIB),
        cost_estimate=pl.CostEstimate(flops=0, bytes_accessed=0, transcendentals=0),
    )(*ins, *after)


def mark_kernel(experts, tokens, routes, scale, block):
    count, width = tokens.shape
    lane = lax.broadcasted_iota(jnp.int32, (count, block.shape[1] - width), 1)
    expert, part = lax.rem(lane, experts), lax.div(lane, experts)
    weight = jnp.zeros(lane.shape, jnp.float32)
    for r in range(routes.shape[1]):
        weight += jnp.where(routes[:, r : r + 1] == expert, scale[:, r : r + 1], 0.0)
    high = weight.astype(jnp.bfloat16).astype(jnp.float32)
    middle = (weight - high).astype(jnp.bfloat16).astype(jnp.float32)
    low = weight - high - middle
    marks = jnp.where(part == 0, high, jnp.where(part == 1, middle, jnp.where(part == 2, low, 0.0)))
    block[:, :width] = tokens[...]
    block[:, width:] = marks.astype(jnp.bfloat16)


def pick_kernel(users, *refs):
    blocks, (own_map, other_map, own_rows, other_rows, held, sem) = refs[: len(users)], refs[len(users) :]
    node = lax.axis_index("node")
    for block, places in zip(blocks, users):
        here = functools.reduce(jnp.logical_or, [lax.div(node, 2) == place for place in places])

        @pl.when(here)
        def _():
            copy = pltpu.make_async_copy(block, held, sem)
            copy.start()
            copy.wait()

    count, cap = own_map.shape
    marks = held[:, held.shape[1] - 128 :].astype(jnp.float32)
    lane = lax.broadcasted_iota(jnp.int32, marks.shape, 1)
    earlier = lax.broadcasted_iota(jnp.int32, (count, count), 0) > lax.broadcasted_iota(jnp.int32, (count, count), 1)
    named = jnp.where(marks != 0, 1.0, 0.0)
    rank = jnp.dot(
        jnp.where(earlier, 1.0, 0.0).astype(jnp.bfloat16), named.astype(jnp.bfloat16), preferred_element_type=jnp.float32
    )
    place = jnp.where(named > 0, rank, -1.0)
    slot = lax.broadcasted_iota(jnp.int32, (count, cap), 1)
    for expert, one_hot, rows in ((node, own_map, own_rows), (node ^ 1, other_map, other_rows)):
        mine = jnp.sum(jnp.where(lane == expert, place, 0.0), axis=1, keepdims=True).astype(jnp.int32)
        chosen = jnp.where(mine == slot, 1.0, 0.0).astype(jnp.bfloat16)
        one_hot[...] = chosen
        rows[...] = lax.dot_general(
            chosen, held[...], (((0,), (0,)), ((), ())), preferred_element_type=jnp.float32
        ).astype(jnp.bfloat16)


def expert_kernel(experts, own, other, *refs):
    weights, (own_out, other_out, rows, total, gates, ups, downs, sems) = refs[:6], refs[6:]
    cap, width = own_out.shape
    tiles, _, size = gates.shape
    copies = []
    for tile in range(tiles):
        gate, up, down = weights[:3] if tile < tiles // 2 else weights[3:]
        part = pl.ds(tile % (tiles // 2) * size, size)
        copies.append(
            [
                pltpu.make_async_copy(gate.at[:, part], gates.at[tile], sems.at[tile, 0]),
                pltpu.make_async_copy(up.at[:, part], ups.at[tile], sems.at[tile, 1]),
                pltpu.make_async_copy(down.at[part, :], downs.at[tile], sems.at[tile, 2]),
            ]
        )
        for copy in copies[-1]:
            copy.start()
    rows[:cap] = own[:, :width]
    rows[cap:] = other[:, :width]
    node = lax.axis_index("node")
    for tile in range(tiles):
        copies[tile][0].wait()
        gate = jnp.dot(rows[...], gates[tile], preferred_element_type=jnp.float32)
        copies[tile][1].wait()
        up = jnp.dot(rows[...], ups[tile], preferred_element_type=jnp.float32)
        hidden = (gate / (1.0 + jnp.exp(-gate)) * up).astype(jnp.bfloat16)
        copies[tile][2].wait()
        out = jnp.dot(hidden, downs[tile], preferred_element_type=jnp.float32)
        if tile == 0:
            total[...] = out
        elif tile < tiles - 1:
            total[...] += out
        else:
            out += total[...]
            for first, marks, result in ((0, own, own_out), (cap, other, other_out)):
                marks = marks[:, width:].astype(jnp.float32)
                lane = lax.broadcasted_iota(jnp.int32, marks.shape, 1)
                mine = (lax.rem(lane, experts) == node) & (lane < 3 * experts)
                scale = jnp.sum(jnp.where(mine, marks, 0.0), axis=1, keepdims=True)
                result[...] = (out[first : first + cap] * scale).astype(jnp.bfloat16)


def spread_kernel(own_map, other_map, own_out, other_out, *refs):
    result = refs[-1]
    total = jnp.dot(own_map[...], own_out[...], preferred_element_type=jnp.float32)
    total += jnp.dot(other_map[...], other_out[...], preferred_element_type=jnp.float32)
    for extra in refs[:-1]:
        total += extra[...].astype(jnp.float32)
    result[...] = total.astype(jnp.bfloat16)


def on_device(tokens, routes, route_scale, w_gate, w_up, w_down):
    count, width = tokens.shape
    experts = lax.axis_size("node")
    places = experts // 2
    hidden = w_gate.shape[2]
    size = min(hidden, 256)
    cap = -(-(5 * count // experts) // 16) * 16
    wide = width + -(-3 * experts // 128) * 128
    bf16 = functools.partial(jax.ShapeDtypeStruct, dtype=jnp.bfloat16)

    own = (w_gate[0], w_up[0], w_down[0])
    weights = own + tuple(lax.ppermute(w, "local", [(0, 1), (1, 0)]) for w in own)

    def along(block, pairs):
        moves = [(2 * a + y, 2 * b + y) for a, b in pairs for y in range(2)]
        return lax.ppermute(block, "node", moves)

    def across(block):
        return lax.ppermute(block, "node", [(n, n ^ 1) for n in range(experts)])

    def pick(blocks, users, after=()):
        return call(
            functools.partial(pick_kernel, users),
            [bf16((count, cap)), bf16((count, cap)), bf16((cap, wide)), bf16((cap, wide))],
            blocks,
            after,
            [pltpu.VMEM((count, wide), jnp.bfloat16), pltpu.SemaphoreType.DMA],
            [ANYWHERE] * len(blocks),
        )

    def expert(own_rows, other_rows, after=()):
        tiles = 2 * hidden // size
        return call(
            functools.partial(expert_kernel, experts),
            [bf16((cap, width)), bf16((cap, width))],
            [own_rows, other_rows, *weights],
            after,
            [
                pltpu.VMEM((2 * cap, width), jnp.bfloat16),
                pltpu.VMEM((2 * cap, width), jnp.float32),
                pltpu.VMEM((tiles, width, size), jnp.bfloat16),
                pltpu.VMEM((tiles, width, size), jnp.bfloat16),
                pltpu.VMEM((tiles, size, width), jnp.bfloat16),
                pltpu.SemaphoreType.DMA((tiles, 3)),
            ],
            [IN_VMEM] * 2 + [ANYWHERE] * 6,
            56,
        )

    def spread(maps, own_out, other_out, extras=(), after=()):
        return call(spread_kernel, [bf16((count, width))], [*maps, own_out, other_out, *extras], after)[0]

    (block,) = call(
        functools.partial(mark_kernel, experts), [bf16((count, wide))], [tokens, routes, route_scale]
    )
    plan = arrivals(places)
    held = {}
    for step in range(1, places):
        for way in (1, -1):
            pairs = [
                (a, a + way)
                for a in range(places)
                if 0 <= a + way < places and 0 <= a - way * (step - 1) < places
            ]
            held[way, step] = along(held.get((way, step - 1), block), pairs)

    last = []

    def ordered(function, *args):
        out = function(*args, after=tuple(last))
        last[:] = [out[0] if isinstance(out, (list, tuple)) else out]
        return out

    picks, outs, returned = {}, {}, []

    def do_pick(slot):
        if slot == 0:
            blocks, users = [block], [range(places)]
        else:
            keys = sorted({row[slot - 1] for row in plan})
            blocks = [held[key] for key in keys]
            users = [[place for place, row in enumerate(plan) if row[slot - 1] == key] for key in keys]
        *maps, own_rows, other_rows = ordered(pick, blocks, users)
        picks[slot] = maps, own_rows, across(other_rows)

    def do_expert(slot):
        own_out, other_out = ordered(expert, picks[slot][1], picks[slot][2])
        outs[slot] = own_out, across(other_out)

    def do_spread(slot):
        done = ordered(spread, picks[slot][0], *outs[slot])
        home = [(a, a - row[slot - 1][0] * row[slot - 1][1]) for a, row in enumerate(plan)]
        rounds = []
        while home:
            now = list({b: (a, b) for a, b in home}.values())
            home = [pair for pair in home if pair not in now]
            rounds.append(along(done, now))
        returned.append(rounds)

    do_pick(0)
    do_pick(1)
    do_expert(0)
    for slot in range(1, places):
        do_expert(slot)
        if slot + 1 < places:
            do_pick(slot + 1)
            do_spread(slot)
    first = ordered(spread, picks[0][0], *outs[0], returned[0])
    do_spread(places - 1)
    total = first.astype(jnp.float32)
    for block in sum(returned[1:], []):
        total = total + block.astype(jnp.float32)
    return total.astype(jnp.bfloat16)


def solution(mesh):
    placed = (
        P(("groups", "node", "local"), None),
        P(("groups", "node", "local"), None),
        P(("groups", "node", "local"), None),
        P("node", None, "local"),
        P("node", None, "local"),
        P("node", "local", None),
    )
    return jax.shard_map(
        on_device,
        mesh=mesh,
        in_specs=placed,
        out_specs=P(("groups", "node", "local"), None),
        check_vma=False,
    )
```

time: 310 us -> 250 us (0.81)
  waiting for transfers between devices: 215 us -> 149 us
  Pallas kernels: 0 us -> 52.9 us
  matrix products: 47.5 us -> 0 us
  starting transfers between devices: 1.07 us -> 34.7 us
  blocking collectives: 32.2 us -> 0 us
  between operations: 13.4 us -> 0.38 us
  local copies, waits for them, and re-layouts: 0.01 us -> 11.7 us
    ppermute x3 -> x22, waiting for transfers between devices: 0.01 us -> 149 us  [the longest x11 88.4 us: along(): return lax.ppermute(block, 'node', moves)]
    reduce_scatter x1 -> x0, waiting for transfers between devices: 131 us -> none  [on_device(): return lax.psum_scatter(scaled, 'node', scatter_dimension=0, tiled=True)]
    all_gather x1 -> x0, waiting for transfers between devices: 83.2 us -> none  [on_device(): every = lax.all_gather(tokens, 'node', axis=0, tiled=True)]
    pallas_call x0 -> x13, Pallas kernels: none -> 52.9 us  [call(): pl.pallas_call(body, out_shape=outs, in_specs=specs, out_specs=[IN_VMEM]...]
    dot_general x4 -> x0, matrix products: 47.5 us -> none  [the longest x2 31.9 us: on_device(): total = total + jnp.dot(hidden, down_w, preferred_element_type=jnp.float32)]
    ppermute x3 -> x22, starting transfers between devices: 1.03 us -> 34.7 us  [the longest x11 23.2 us: along(): return lax.ppermute(block, 'node', moves)]
    all_gather x1 -> x0, blocking collectives: 32.2 us -> none  [on_device(): weight = lax.all_gather(weight, 'node', axis=0, tiled=False)]
    unnamed x2 -> x50, local copies, waits for them, and re-layouts: 0.01 us -> 11.7 us
  transfers between devices with their start and end apart: 5 -> 22, of which waited for: 2 -> 9; matrix products, arithmetic and copies ran while one was open for 10% -> 1% of each run, Pallas kernels for 0% -> 21%
where the time goes in v3:
time: 250 us
  waiting for transfers between devices  149 us (60%)
  Pallas kernels  52.9 us (21%)
  starting transfers between devices  34.7 us (14%)
  local copies, waits for them, and re-layouts  11.7 us (5%)
    ppermute x11, waiting for transfers between devices, along(): return lax.ppermute(block, 'node', moves)  88.4 us
    ppermute x8, waiting for transfers between devices, across(): return lax.ppermute(block, 'node', [(n, n ^ 1) for n in range(experts)])  60.3 us
    pallas_call x13, Pallas kernels, call(): pl.pallas_call(body, out_shape=outs, in_specs=specs, out_specs=[IN_VMEM]...  52.9 us
    ppermute x11, starting transfers between devices, along(): return lax.ppermute(block, 'node', moves)  23.2 us
    unnamed x50, local copies, waits for them, and re-layouts  11.7 us
    ppermute x8, starting transfers between devices, across(): return lax.ppermute(block, 'node', [(n, n ^ 1) for n in range(experts)])  10.6 us
  transfers between devices with their start and end apart: 22, of which 9 were waited for; matrix products, arithmetic and copies ran while one was open for 1% of the time, Pallas kernels for 21%

profile of v3, /device:TPU:0, one launch (start us, length us, event | category | flops | bytes accessed | tf_op | source)
XLA Modules:
  0.0 249.8 jit_solution(9998523801806482218)
XLA Ops:
  0.0 0.5 collective-permute-start.1
  0.5 0.1 collective-permute-start.2
  0.5 0.5 collective-permute-start.3
  1.0 0.8 copy.7.routes
  1.7 0.8 copy.8.scale
  2.5 1.2 copy-done.10
  3.7 0.1 shard_map.64.refs_0_
  3.9 1.0 shard_map.65
  4.9 2.6 %collective-permute-start = (bf16[80,3712]{1,0:T(8,128)(2,1)S(1)}, bf16[80,3712]{1,0:T(8,128)(2,1)S(1)}, u32[]{:S(2)}, u32[]{:S(2)}) collective-permute-start(bf16[80,3712]{1,0:T(8,128)(2,1)S(1)} %get-tuple-element.32), channel_id=1, source_target_pairs={{0,2},{2,0},{4,6},{6,4},{8,10},{10,8},{12,14},{14,12},{1,3},{3,1},... | collective-permute-start | bytes 1781768 | tf_op jit(solution)/shard_map/ppermute | solution.py:159
  7.5 3.5 %collective-permute-start.5 = (bf16[128,3712]{1,0:T(8,128)(2,1)S(1)}, bf16[128,3712]{1,0:T(8,128)(2,1)S(1)}, u32[]{:S(2)}, u32[]{:S(2)}) collective-permute-start(bf16[128,3712]{1,0:T(8,128)(2,1)S(1)} %shard_map.64.refs_0_), channel_id=1, source_target_pairs={{0,4},{2,6},{4,8},{6,10},{8,12},{10,14},{1,5},{3,7},{5,9},{7,11},{... | collective-permute-start | bytes 2850824 | tf_op jit(solution)/shard_map/ppermute | solution.py:156
  11.0 10.6 %collective-permute-done.refs_1_ = bf16[80,3712]{1,0:T(8,128)(2,1)S(1)} collective-permute-done((bf16[80,3712]{1,0:T(8,128)(2,1)S(1)}, bf16[80,3712]{1,0:T(8,128)(2,1)S(1)}, u32[]{:S(2)}, u32[]{:S(2)}) %collective-permute-start) | collective-permute-done | bytes 593952 | tf_op jit(solution)/shard_map/ppermute | solution.py:159
  21.6 1.3 collective-permute-start.4
  22.9 8.8 %collective-permute-done.5.refs_1_.refs_2_ = bf16[128,3712]{1,0:T(8,128)(2,1)S(1)} collective-permute-done((bf16[128,3712]{1,0:T(8,128)(2,1)S(1)}, bf16[128,3712]{1,0:T(8,128)(2,1)S(1)}, u32[]{:S(2)}, u32[]{:S(2)}) %collective-permute-start.5) | collective-permute-done | bytes 950304 | tf_op jit(solution)/shard_map/ppermute | solution.py:156
  31.7 0.7 collective-permute-start.10
  32.4 14.0 %collective-permute-done.4.refs_0_ = bf16[128,3712]{1,0:T(8,128)(2,1)S(1)} collective-permute-done((bf16[128,3712]{1,0:T(8,128)(2,1)S(1)}, bf16[128,3712]{1,0:T(8,128)(2,1)S(1)}, u32[]{:S(2)}, u32[]{:S(2)}) %collective-permute-start.4) | collective-permute-done | bytes 950304 | tf_op jit(solution)/shard_map/ppermute | solution.py:156
  46.4 1.3 collective-permute-start.9
  47.6 1.0 shard_map.66
  48.7 0.0 copy-start.11
  48.7 0.8 copy-done.11
  49.5 0.6 copy-done.15
  50.1 0.0 collective-permute-done.10.refs_1_
  50.1 1.5 collective-permute-start.7
  51.7 18.6 %collective-permute-done.9.refs_0_ = bf16[128,3712]{1,0:T(8,128)(2,1)S(1)} collective-permute-done((bf16[128,3712]{1,0:T(8,128)(2,1)S(1)}, bf16[128,3712]{1,0:T(8,128)(2,1)S(1)}, u32[]{:S(2)}, u32[]{:S(2)}) %collective-permute-start.9) | collective-permute-done | bytes 950304 | tf_op jit(solution)/shard_map/ppermute | solution.py:156
  70.3 1.3 collective-permute-start.13
  71.6 0.9 collective-permute-start.14
  72.5 0.0 collective-permute-done.2.refs_6_
  72.5 0.0 collective-permute-done.3.refs_7_
  72.5 11.5 %shard_map.67 = (bf16[80,3584]{1,0:T(8,128)(2,1)}, bf16[80,3584]{1,0:T(8,128)(2,1)}) custom-call(bf16[80,3712]{1,0:T(8,128)(2,1)} %copy-done.12, bf16[80,3712]{1,0:T(8,128)(2,1)} %copy-done.18, bf16[3584,512]{1,0:T(8,128)(2,1)} %bitcast.4, bf16[3584,512]{1,0:T(8,128)(2,1)} %bitcast.9, bf16[512,3584]{1,0:T(8,128)(2,1)} %bitcast.14, ...), custom_call_target="tpu_custom_call" | custom-call | tf_op jit(solution)/shard_map/pallas_call | solution.py:33
  84.0 0.8 copy-done.17
  84.8 11.4 %shard_map.68 = (bf16[80,3584]{1,0:T(8,128)(2,1)}, bf16[80,3584]{1,0:T(8,128)(2,1)}) custom-call(bf16[80,3712]{1,0:T(8,128)(2,1)} %copy-done.11, bf16[80,3712]{1,0:T(8,128)(2,1)} %copy-done.17, bf16[3584,512]{1,0:T(8,128)(2,1)} %bitcast.5, bf16[3584,512]{1,0:T(8,128)(2,1)} %bitcast.10, bf16[512,3584]{1,0:T(8,128)(2,1)} %bitcast.15, ...), custom_call_target="tpu_custom_call" | custom-call | tf_op jit(solution)/shard_map/pallas_call | solution.py:33
  96.3 1.1 copy-done.8
  97.3 1.2 shard_map.69
  98.6 1.4 collective-permute-start.15
  99.9 0.7 collective-permute-start.8
  100.7 23.7 %collective-permute-done.8.refs_3_ = bf16[80,3584]{1,0:T(8,128)(2,1)S(1)} collective-permute-done((bf16[80,3584]{1,0:T(8,128)(2,1)S(1)}, bf16[80,3584]{1,0:T(8,128)(2,1)S(1)}, u32[]{:S(2)}, u32[]{:S(2)}) %collective-permute-start.8) | collective-permute-done | bytes 573472 | tf_op jit(solution)/shard_map/ppermute | solution.py:159
  124.4 0.6 shard_map.70.refs_8_
  125.0 0.0 copy-start
  125.0 0.9 copy-done
  126.0 0.8 copy-done.20
  126.8 11.4 %shard_map.71 = (bf16[80,3584]{1,0:T(8,128)(2,1)}, bf16[80,3584]{1,0:T(8,128)(2,1)}) custom-call(bf16[80,3712]{1,0:T(8,128)(2,1)} %copy-done.14, bf16[80,3712]{1,0:T(8,128)(2,1)} %copy-done.20, bf16[3584,512]{1,0:T(8,128)(2,1)} %bitcast.6, bf16[3584,512]{1,0:T(8,128)(2,1)} %bitcast.11, bf16[512,3584]{1,0:T(8,128)(2,1)} %bitcast.16, ...), custom_call_target="tpu_custom_call" | custom-call | tf_op jit(solution)/shard_map/pallas_call | solution.py:33
  138.3 1.1 copy-done.5
  139.3 1.0 shard_map.72
  140.4 1.1 collective-permute-start.16
  141.5 1.0 collective-permute-start.17
  142.5 0.7 collective-permute-start.11
  143.2 5.2 %collective-permute-start.12 = (bf16[128,3584]{1,0:T(8,128)(2,1)S(1)}, bf16[128,3584]{1,0:T(8,128)(2,1)S(1)}, u32[]{:S(2)}, u32[]{:S(2)}) collective-permute-start(bf16[128,3584]{1,0:T(8,128)(2,1)S(1)} %copy-done.1), channel_id=1, source_target_pairs={{0,4},{2,6},{4,8},{6,10},{1,5},{3,7},{5,9},{7,11},{16,20},{18,22},... | collective-permute-start | bytes 2752520 | tf_op jit(solution)/shard_map/ppermute | solution.py:156
  148.5 1.1 collective-permute-start.6
  149.6 19.5 %collective-permute-done.17.refs_3_ = bf16[80,3584]{1,0:T(8,128)(2,1)S(1)} collective-permute-done((bf16[80,3584]{1,0:T(8,128)(2,1)S(1)}, bf16[80,3584]{1,0:T(8,128)(2,1)S(1)}, u32[]{:S(2)}, u32[]{:S(2)}) %collective-permute-start.17) | collective-permute-done | bytes 573472 | tf_op jit(solution)/shard_map/ppermute | solution.py:159
  169.1 0.6 shard_map.73.refs_8_
  169.7 0.0 copy-start.2
  169.7 0.9 copy-done.2
  170.7 0.8 copy-done.19
  171.5 11.6 %shard_map.74 = (bf16[80,3584]{1,0:T(8,128)(2,1)}, bf16[80,3584]{1,0:T(8,128)(2,1)}) custom-call(bf16[80,3712]{1,0:T(8,128)(2,1)} %copy-done.13, bf16[80,3712]{1,0:T(8,128)(2,1)} %copy-done.19, bf16[3584,512]{1,0:T(8,128)(2,1)} %bitcast.7, bf16[3584,512]{1,0:T(8,128)(2,1)} %bitcast.12, bf16[512,3584]{1,0:T(8,128)(2,1)} %bitcast.17, ...), custom_call_target="tpu_custom_call" | custom-call | tf_op jit(solution)/shard_map/pallas_call | solution.py:33
  183.1 1.1 collective-permute-start.19
  184.2 0.6 collective-permute-start.18
  184.9 1.1 copy-done.7
  185.9 0.7 shard_map.75.refs_4_
  186.6 6.4 %collective-permute-done.19.refs_3_ = bf16[80,3584]{1,0:T(8,128)(2,1)S(1)} collective-permute-done((bf16[80,3584]{1,0:T(8,128)(2,1)}, bf16[80,3584]{1,0:T(8,128)(2,1)S(1)}, u32[]{:S(2)}, u32[]{:S(2)}) %collective-permute-start.19) | collective-permute-done | bytes 573472 | tf_op jit(solution)/shard_map/ppermute | solution.py:159
  193.1 0.6 shard_map.76
  193.7 1.3 collective-permute-start.20
  195.0 6.3 %collective-permute-start.21 = (bf16[128,3584]{1,0:T(8,128)(2,1)S(1)}, bf16[128,3584]{1,0:T(8,128)(2,1)S(1)}, u32[]{:S(2)}, u32[]{:S(2)}) collective-permute-start(bf16[128,3584]{1,0:T(8,128)(2,1)S(1)} %shard_map.76), channel_id=1, source_target_pairs={{0,12},{2,14},{4,0},{6,2},{1,13},{3,15},{5,1},{7,3},{16,28},{18,30... | collective-permute-start | bytes 2752520 | tf_op jit(solution)/shard_map/ppermute | solution.py:156
  201.3 37.2 %collective-permute-done.18 = bf16[128,3584]{1,0:T(8,128)(2,1)S(1)} collective-permute-done((bf16[128,3584]{1,0:T(8,128)(2,1)S(1)}, bf16[128,3584]{1,0:T(8,128)(2,1)S(1)}, u32[]{:S(2)}, u32[]{:S(2)}) %collective-permute-start.18) | collective-permute-done | bytes 917536 | tf_op jit(solution)/shard_map/ppermute | solution.py:156
  238.5 9.9 %collective-permute-done.21 = bf16[128,3584]{1,0:T(8,128)(2,1)S(1)} collective-permute-done((bf16[128,3584]{1,0:T(8,128)(2,1)S(1)}, bf16[128,3584]{1,0:T(8,128)(2,1)S(1)}, u32[]{:S(2)}, u32[]{:S(2)}) %collective-permute-start.21) | collective-permute-done | bytes 917536 | tf_op jit(solution)/shard_map/ppermute | solution.py:156
  248.4 1.4 add_convert_fusion
  (44 shorter events, 0.1 us)
Async XLA Ops:
  0.0 71.6 %collective-permute-start.1 = (bf16[3584,512]{1,0:T(8,128)(2,1)}, bf16[3584,512]{1,0:T(8,128)(2,1)}, u32[]{:S(2)}, u32[]{:S(2)}) collective-permute-start(bf16[3584,512]{1,0:T(8,128)(2,1)} %bitcast.3), channel_id=1, source_target_pairs={{0,1},{1,0},{2,3},{3,2},{4,5},{5,4},{6,7},{7,6},{8,9},{9,8},{10,11... | collective-permute-start | bytes 11010056 | tf_op jit(solution)/shard_map/ppermute | solution.py:152
  0.5 72.0 %collective-permute-start.2 = (bf16[3584,512]{1,0:T(8,128)(2,1)}, bf16[3584,512]{1,0:T(8,128)(2,1)}, u32[]{:S(2)}, u32[]{:S(2)}) collective-permute-start(bf16[3584,512]{1,0:T(8,128)(2,1)} %bitcast.8), channel_id=1, source_target_pairs={{0,1},{1,0},{2,3},{3,2},{4,5},{5,4},{6,7},{7,6},{8,9},{9,8},{10,11... | collective-permute-start | bytes 11010056 | tf_op jit(solution)/shard_map/ppermute | solution.py:152
  0.5 72.0 %collective-permute-start.3 = (bf16[512,3584]{1,0:T(8,128)(2,1)}, bf16[512,3584]{1,0:T(8,128)(2,1)}, u32[]{:S(2)}, u32[]{:S(2)}) collective-permute-start(bf16[512,3584]{1,0:T(8,128)(2,1)} %bitcast.13), channel_id=1, source_target_pairs={{0,1},{1,0},{2,3},{3,2},{4,5},{5,4},{6,7},{7,6},{8,9},{9,8},{10,11... | collective-permute-start | bytes 11010056 | tf_op jit(solution)/shard_map/ppermute | solution.py:152
  2.5 1.2 copy-start.10
  4.9 66.7 %copy-start.12 = (bf16[80,3712]{1,0:T(8,128)(2,1)}, bf16[80,3712]{1,0:T(8,128)(2,1)S(1)}, u32[]{:S(2)}) copy-start(bf16[80,3712]{1,0:T(8,128)(2,1)S(1)} %get-tuple-element.31.refs_0_) | copy-start | bytes 1781764
  4.9 16.7 %collective-permute-start = (bf16[80,3712]{1,0:T(8,128)(2,1)S(1)}, bf16[80,3712]{1,0:T(8,128)(2,1)S(1)}, u32[]{:S(2)}, u32[]{:S(2)}) collective-permute-start(bf16[80,3712]{1,0:T(8,128)(2,1)S(1)} %get-tuple-element.32), channel_id=1, source_target_pairs={{0,2},{2,0},{4,6},{6,4},{8,10},{10,8},{12,14},{14,12},{1,3},{3,1},... | collective-permute-start | bytes 1781768 | tf_op jit(solution)/shard_map/ppermute | solution.py:159
  7.5 24.2 %collective-permute-start.5 = (bf16[128,3712]{1,0:T(8,128)(2,1)S(1)}, bf16[128,3712]{1,0:T(8,128)(2,1)S(1)}, u32[]{:S(2)}, u32[]{:S(2)}) collective-permute-start(bf16[128,3712]{1,0:T(8,128)(2,1)S(1)} %shard_map.64.refs_0_), channel_id=1, source_target_pairs={{0,4},{2,6},{4,8},{6,10},{8,12},{10,14},{1,5},{3,7},{5,9},{7,11},{... | collective-permute-start | bytes 2850824 | tf_op jit(solution)/shard_map/ppermute | solution.py:156
  21.6 50.9 %copy-start.18 = (bf16[80,3712]{1,0:T(8,128)(2,1)}, bf16[80,3712]{1,0:T(8,128)(2,1)S(1)}, u32[]{:S(2)}) copy-start(bf16[80,3712]{1,0:T(8,128)(2,1)S(1)} %collective-permute-done.refs_1_) | copy-start | bytes 1781764
  21.6 24.8 %collective-permute-start.4 = (bf16[128,3712]{1,0:T(8,128)(2,1)S(1)}, bf16[128,3712]{1,0:T(8,128)(2,1)S(1)}, u32[]{:S(2)}, u32[]{:S(2)}) collective-permute-start(bf16[128,3712]{1,0:T(8,128)(2,1)S(1)} %shard_map.64.refs_0_), channel_id=1, source_target_pairs={{4,0},{6,2},{8,4},{10,6},{12,8},{14,10},{5,1},{7,3},{9,5},{11,7},{... | collective-permute-start | bytes 2850824 | tf_op jit(solution)/shard_map/ppermute | solution.py:156
  31.7 18.5 %collective-permute-start.10 = (bf16[128,3712]{1,0:T(8,128)(2,1)S(1)}, bf16[128,3712]{1,0:T(8,128)(2,1)S(1)}, u32[]{:S(2)}, u32[]{:S(2)}) collective-permute-start(bf16[128,3712]{1,0:T(8,128)(2,1)S(1)} %collective-permute-done.5.refs_1_.refs_2_), channel_id=1, source_target_pairs={{4,8},{6,10},{8,12},{10,14},{5,9},{7,11},{9,13},{11,15},{20,24},{2... | collective-permute-start | bytes 2850824 | tf_op jit(solution)/shard_map/ppermute | solution.py:156
  46.4 23.9 %collective-permute-start.9 = (bf16[128,3712]{1,0:T(8,128)(2,1)S(1)}, bf16[128,3712]{1,0:T(8,128)(2,1)S(1)}, u32[]{:S(2)}, u32[]{:S(2)}) collective-permute-start(bf16[128,3712]{1,0:T(8,128)(2,1)S(1)} %collective-permute-done.4.refs_0_), channel_id=1, source_target_pairs={{4,0},{6,2},{8,4},{10,6},{5,1},{7,3},{9,5},{11,7},{20,16},{22,18},... | collective-permute-start | bytes 2850824 | tf_op jit(solution)/shard_map/ppermute | solution.py:156
  48.7 0.8 copy-start.11
  49.5 0.6 copy-start.15
  50.1 33.9 %collective-permute-start.7 = (bf16[80,3712]{1,0:T(8,128)(2,1)S(1)}, bf16[80,3712]{1,0:T(8,128)(2,1)S(1)}, u32[]{:S(2)}, u32[]{:S(2)}) collective-permute-start(bf16[80,3712]{1,0:T(8,128)(2,1)S(1)} %get-tuple-element.38), channel_id=1, source_target_pairs={{0,2},{2,0},{4,6},{6,4},{8,10},{10,8},{12,14},{14,12},{1,3},{3,1},... | collective-permute-start | bytes 1781768 | tf_op jit(solution)/shard_map/ppermute | solution.py:159
  70.3 68.0 %collective-permute-start.13 = (bf16[128,3712]{1,0:T(8,128)(2,1)S(1)}, bf16[128,3712]{1,0:T(8,128)(2,1)S(1)}, u32[]{:S(2)}, u32[]{:S(2)}) collective-permute-start(bf16[128,3712]{1,0:T(8,128)(2,1)S(1)} %collective-permute-done.9.refs_0_), channel_id=1, source_target_pairs={{4,0},{6,2},{5,1},{7,3},{20,16},{22,18},{21,17},{23,19}} | collective-permute-start | bytes 2850824 | tf_op jit(solution)/shard_map/ppermute | solution.py:156
  71.6 66.7 %collective-permute-start.14 = (bf16[128,3712]{1,0:T(8,128)(2,1)S(1)}, bf16[128,3712]{1,0:T(8,128)(2,1)S(1)}, u32[]{:S(2)}, u32[]{:S(2)}) collective-permute-start(bf16[128,3712]{1,0:T(8,128)(2,1)S(1)} %collective-permute-done.10.refs_1_), channel_id=1, source_target_pairs={{8,12},{10,14},{9,13},{11,15},{24,28},{26,30},{25,29},{27,31}} | collective-permute-start | bytes 2850824 | tf_op jit(solution)/shard_map/ppermute | solution.py:156
  84.0 0.8 copy-start.17
  96.3 1.1 copy-start.8
  97.3 2.6 %copy-start.23 = (bf16[80,3584]{1,0:T(8,128)(2,1)S(1)}, bf16[80,3584]{1,0:T(8,128)(2,1)}, u32[]{:S(2)}) copy-start(bf16[80,3584]{1,0:T(8,128)(2,1)} %get-tuple-element.40) | copy-start | bytes 1720324
  97.3 27.1 %copy-start.9 = (bf16[80,3584]{1,0:T(8,128)(2,1)S(1)}, bf16[80,3584]{1,0:T(8,128)(2,1)}, u32[]{:S(2)}) copy-start(bf16[80,3584]{1,0:T(8,128)(2,1)} %get-tuple-element.39.refs_2_) | copy-start | bytes 1720324
  97.3 27.1 %copy-start.16 = (bf16[128,80]{1,0:T(8,128)(2,1)S(1)}, bf16[128,80]{1,0:T(8,128)(2,1)}, u32[]{:S(2)}) copy-start(bf16[128,80]{1,0:T(8,128)(2,1)} %copy-done.15) | copy-start | bytes 61444
  98.6 26.5 %copy-start.14 = (bf16[80,3712]{1,0:T(8,128)(2,1)}, bf16[80,3712]{1,0:T(8,128)(2,1)S(1)}, u32[]{:S(2)}) copy-start(bf16[80,3712]{1,0:T(8,128)(2,1)S(1)} %get-tuple-element.42.refs_0_) | copy-start | bytes 1781764
  98.6 27.4 %collective-permute-start.15 = (bf16[80,3712]{1,0:T(8,128)(2,1)S(1)}, bf16[80,3712]{1,0:T(8,128)(2,1)S(1)}, u32[]{:S(2)}, u32[]{:S(2)}) collective-permute-start(bf16[80,3712]{1,0:T(8,128)(2,1)S(1)} %get-tuple-element.43), channel_id=1, source_target_pairs={{0,2},{2,0},{4,6},{6,4},{8,10},{10,8},{12,14},{14,12},{1,3},{3,1},... | collective-permute-start | bytes 1781768 | tf_op jit(solution)/shard_map/ppermute | solution.py:159
  99.9 24.4 %collective-permute-start.8 = (bf16[80,3584]{1,0:T(8,128)(2,1)S(1)}, bf16[80,3584]{1,0:T(8,128)(2,1)S(1)}, u32[]{:S(2)}, u32[]{:S(2)}) collective-permute-start(bf16[80,3584]{1,0:T(8,128)(2,1)S(1)} %copy-done.23), channel_id=1, source_target_pairs={{0,2},{2,0},{4,6},{6,4},{8,10},{10,8},{12,14},{14,12},{1,3},{3,1},... | collective-permute-start | bytes 1720328 | tf_op jit(solution)/shard_map/ppermute | solution.py:159
  125.0 0.9 copy-start
  126.0 0.8 copy-start.20
  138.3 1.1 copy-start.5
  139.3 2.2 copy-start.22
  139.3 3.2 %copy-start.1 = (bf16[128,3584]{1,0:T(8,128)(2,1)S(1)}, bf16[128,3584]{1,0:T(8,128)(2,1)}, u32[]{:S(2)}) copy-start(bf16[128,3584]{1,0:T(8,128)(2,1)} %copy-done) | copy-start | bytes 2752516
  139.3 9.1 %copy-start.21 = (bf16[80,3584]{1,0:T(8,128)(2,1)S(1)}, bf16[80,3584]{1,0:T(8,128)(2,1)}, u32[]{:S(2)}) copy-start(bf16[80,3584]{1,0:T(8,128)(2,1)} %get-tuple-element.35) | copy-start | bytes 1720324
  139.3 29.8 %copy-start.6 = (bf16[80,3584]{1,0:T(8,128)(2,1)S(1)}, bf16[80,3584]{1,0:T(8,128)(2,1)}, u32[]{:S(2)}) copy-start(bf16[80,3584]{1,0:T(8,128)(2,1)} %get-tuple-element.44.refs_4_.refs_2_) | copy-start | bytes 1720324
  140.4 30.3 %copy-start.13 = (bf16[80,3712]{1,0:T(8,128)(2,1)}, bf16[80,3712]{1,0:T(8,128)(2,1)S(1)}, u32[]{:S(2)}) copy-start(bf16[80,3712]{1,0:T(8,128)(2,1)S(1)} %get-tuple-element.45.refs_0_) | copy-start | bytes 1781764
  140.4 30.3 %collective-permute-start.16 = (bf16[80,3712]{1,0:T(8,128)(2,1)S(1)}, bf16[80,3712]{1,0:T(8,128)(2,1)S(1)}, u32[]{:S(2)}, u32[]{:S(2)}) collective-permute-start(bf16[80,3712]{1,0:T(8,128)(2,1)S(1)} %get-tuple-element.46), channel_id=1, source_target_pairs={{0,2},{2,0},{4,6},{6,4},{8,10},{10,8},{12,14},{14,12},{1,3},{3,1},... | collective-permute-start | bytes 1781768 | tf_op jit(solution)/shard_map/ppermute | solution.py:159
  141.5 27.6 %collective-permute-start.17 = (bf16[80,3584]{1,0:T(8,128)(2,1)S(1)}, bf16[80,3584]{1,0:T(8,128)(2,1)S(1)}, u32[]{:S(2)}, u32[]{:S(2)}) collective-permute-start(bf16[80,3584]{1,0:T(8,128)(2,1)S(1)} %copy-done.22), channel_id=1, source_target_pairs={{0,2},{2,0},{4,6},{6,4},{8,10},{10,8},{12,14},{14,12},{1,3},{3,1},... | collective-permute-start | bytes 1720328 | tf_op jit(solution)/shard_map/ppermute | solution.py:159
  142.5 42.3 %collective-permute-start.11 = (bf16[128,3584]{1,0:T(8,128)(2,1)S(1)}, bf16[128,3584]{1,0:T(8,128)(2,1)S(1)}, u32[]{:S(2)}, u32[]{:S(2)}) collective-permute-start(bf16[128,3584]{1,0:T(8,128)(2,1)S(1)} %copy-done.1), channel_id=1, source_target_pairs={{8,4},{10,6},{12,8},{14,10},{9,5},{11,7},{13,9},{15,11},{24,20},{2... | collective-permute-start | bytes 2752520 | tf_op jit(solution)/shard_map/ppermute | solution.py:156
  143.2 41.6 %collective-permute-start.12 = (bf16[128,3584]{1,0:T(8,128)(2,1)S(1)}, bf16[128,3584]{1,0:T(8,128)(2,1)S(1)}, u32[]{:S(2)}, u32[]{:S(2)}) collective-permute-start(bf16[128,3584]{1,0:T(8,128)(2,1)S(1)} %copy-done.1), channel_id=1, source_target_pairs={{0,4},{2,6},{4,8},{6,10},{1,5},{3,7},{5,9},{7,11},{16,20},{18,22},... | collective-permute-start | bytes 2752520 | tf_op jit(solution)/shard_map/ppermute | solution.py:156
  148.5 36.4 %collective-permute-start.6 = (bf16[80,3584]{1,0:T(8,128)(2,1)S(1)}, bf16[80,3584]{1,0:T(8,128)(2,1)S(1)}, u32[]{:S(2)}, u32[]{:S(2)}) collective-permute-start(bf16[80,3584]{1,0:T(8,128)(2,1)S(1)} %copy-done.21), channel_id=1, source_target_pairs={{0,2},{2,0},{4,6},{6,4},{8,10},{10,8},{12,14},{14,12},{1,3},{3,1},... | collective-permute-start | bytes 1720328 | tf_op jit(solution)/shard_map/ppermute | solution.py:159
  169.7 0.9 copy-start.2
  170.7 0.8 copy-start.19
  171.5 12.7 %copy-start.3 = (bf16[128,3584]{1,0:T(8,128)(2,1)S(1)}, bf16[128,3584]{1,0:T(8,128)(2,1)}, u32[]{:S(2)}) copy-start(bf16[128,3584]{1,0:T(8,128)(2,1)} %copy-done.2) | copy-start | bytes 2752516
  171.5 13.3 %copy-start.4 = (bf16[80,3584]{1,0:T(8,128)(2,1)S(1)}, bf16[80,3584]{1,0:T(8,128)(2,1)}, u32[]{:S(2)}) copy-start(bf16[80,3584]{1,0:T(8,128)(2,1)} %get-tuple-element.34.refs_8_.refs_2_) | copy-start | bytes 1720324
  183.1 10.0 %collective-permute-start.19 = (bf16[80,3584]{1,0:T(8,128)(2,1)}, bf16[80,3584]{1,0:T(8,128)(2,1)S(1)}, u32[]{:S(2)}, u32[]{:S(2)}) collective-permute-start(bf16[80,3584]{1,0:T(8,128)(2,1)} %get-tuple-element.52), channel_id=1, source_target_pairs={{0,2},{2,0},{4,6},{6,4},{8,10},{10,8},{12,14},{14,12},{1,3},{3,1},... | collective-permute-start | bytes 1720328 | tf_op jit(solution)/shard_map/ppermute | solution.py:159
  184.2 54.3 %collective-permute-start.18 = (bf16[128,3584]{1,0:T(8,128)(2,1)S(1)}, bf16[128,3584]{1,0:T(8,128)(2,1)S(1)}, u32[]{:S(2)}, u32[]{:S(2)}) collective-permute-start(bf16[128,3584]{1,0:T(8,128)(2,1)S(1)} %copy-done.3), channel_id=1, source_target_pairs={{0,8},{2,10},{4,12},{6,14},{8,0},{10,2},{12,4},{14,6},{1,9},{3,11}... | collective-permute-start | bytes 2752520 | tf_op jit(solution)/shard_map/ppermute | solution.py:156
  184.8 1.1 copy-start.7
  193.7 44.9 %collective-permute-start.20 = (bf16[128,3584]{1,0:T(8,128)(2,1)S(1)}, bf16[128,3584]{1,0:T(8,128)(2,1)S(1)}, u32[]{:S(2)}, u32[]{:S(2)}) collective-permute-start(bf16[128,3584]{1,0:T(8,128)(2,1)S(1)} %shard_map.76), channel_id=1, source_target_pairs={{8,12},{10,14},{12,0},{14,2},{9,13},{11,15},{13,1},{15,3},{24,28},... | collective-permute-start | bytes 2752520 | tf_op jit(solution)/shard_map/ppermute | solution.py:156
  195.0 53.4 %collective-permute-start.21 = (bf16[128,3584]{1,0:T(8,128)(2,1)S(1)}, bf16[128,3584]{1,0:T(8,128)(2,1)S(1)}, u32[]{:S(2)}, u32[]{:S(2)}) collective-permute-start(bf16[128,3584]{1,0:T(8,128)(2,1)S(1)} %shard_map.76), channel_id=1, source_target_pairs={{0,12},{2,14},{4,0},{6,2},{1,13},{3,15},{5,1},{7,3},{16,28},{18,30... | collective-permute-start | bytes 2752520 | tf_op jit(solution)/shard_map/ppermute | solution.py:156

commit v4 on v3

--- a/solution.py
+++ b/solution.py
@@ -8,6 +8,7 @@
 from jax.sharding import PartitionSpec as P
 
 ANYWHERE = pl.BlockSpec(memory_space=pl.ANY)
+IN_HBM = pl.BlockSpec(memory_space=pltpu.HBM)
 IN_VMEM = pl.BlockSpec(memory_space=pltpu.VMEM)
 MIB = 1024 * 1024
 
@@ -41,11 +42,23 @@
     )(*ins, *after)
 
 
+def tied(arrays, after):
+    return pl.pallas_call(
+        lambda *refs: None,
+        out_shape=[jax.ShapeDtypeStruct(a.shape, a.dtype) for a in arrays],
+        in_specs=[ANYWHERE] * (len(arrays) + len(after)),
+        out_specs=[ANYWHERE] * len(arrays),
+        input_output_aliases={k: k for k in range(len(arrays))},
+        cost_estimate=pl.CostEstimate(flops=0, bytes_accessed=0, transcendentals=0),
+    )(*arrays, *after)
+
+
 def mark_kernel(experts, tokens, routes, scale, block):
     count, width = tokens.shape
     lane = lax.broadcasted_iota(jnp.int32, (count, block.shape[1] - width), 1)
     expert, part = lax.rem(lane, experts), lax.div(lane, experts)
     weight = jnp.zeros(lane.shape, jnp.float32)
+    routes, scale = routes[...].T, scale[...].T
     for r in range(routes.shape[1]):
         weight += jnp.where(routes[:, r : r + 1] == expert, scale[:, r : r + 1], 0.0)
     high = weight.astype(jnp.bfloat16).astype(jnp.float32)
@@ -87,33 +100,41 @@
         ).astype(jnp.bfloat16)
 
 
-def expert_kernel(experts, own, other, *refs):
-    weights, (own_out, other_out, rows, total, gates, ups, downs, sems) = refs[:6], refs[6:]
+def expert_kernel(experts, own, other, gate_w, up_w, down_w, own_out, other_out, *scratch):
+    rows, total, gates, ups, downs, sems = scratch
     cap, width = own_out.shape
     tiles, _, size = gates.shape
+    each = tiles // gate_w.shape[0]
     copies = []
     for tile in range(tiles):
-        gate, up, down = weights[:3] if tile < tiles // 2 else weights[3:]
-        part = pl.ds(tile % (tiles // 2) * size, size)
+        half, part = tile // each, pl.ds(tile % each * size, size)
         copies.append(
             [
-                pltpu.make_async_copy(gate.at[:, part], gates.at[tile], sems.at[tile, 0]),
-                pltpu.make_async_copy(up.at[:, part], ups.at[tile], sems.at[tile, 1]),
-                pltpu.make_async_copy(down.at[part, :], downs.at[tile], sems.at[tile, 2]),
+                pltpu.make_async_copy(gate_w.at[half, :, part], gates.at[tile], sems.at[tile, 0]),
+                pltpu.make_async_copy(up_w.at[half, :, part], ups.at[tile], sems.at[tile, 1]),
+                pltpu.make_async_copy(down_w.at[half, part, :], downs.at[tile], sems.at[tile, 2]),
             ]
         )
-        for copy in copies[-1]:
-            copy.start()
+    ahead = [copy for tile in copies for copy in tile]
+    for copy in ahead[:4]:
+        copy.start()
+    waiting = list(ahead[4:])
+
+    def arrived(copy):
+        copy.wait()
+        if waiting:
+            waiting.pop(0).start()
+
     rows[:cap] = own[:, :width]
     rows[cap:] = other[:, :width]
     node = lax.axis_index("node")
     for tile in range(tiles):
-        copies[tile][0].wait()
+        arrived(copies[tile][0])
         gate = jnp.dot(rows[...], gates[tile], preferred_element_type=jnp.float32)
-        copies[tile][1].wait()
+        arrived(copies[tile][1])
         up = jnp.dot(rows[...], ups[tile], preferred_element_type=jnp.float32)
         hidden = (gate / (1.0 + jnp.exp(-gate)) * up).astype(jnp.bfloat16)
-        copies[tile][2].wait()
+        arrived(copies[tile][2])
         out = jnp.dot(hidden, downs[tile], preferred_element_type=jnp.float32)
         if tile == 0:
             total[...] = out
@@ -149,7 +170,7 @@
     bf16 = functools.partial(jax.ShapeDtypeStruct, dtype=jnp.bfloat16)
 
     own = (w_gate[0], w_up[0], w_down[0])
-    weights = own + tuple(lax.ppermute(w, "local", [(0, 1), (1, 0)]) for w in own)
+    weights = tuple(lax.all_gather(w, "local") for w in own)
 
     def along(block, pairs):
         moves = [(2 * a + y, 2 * b + y) for a, b in pairs for y in range(2)]
@@ -183,19 +204,29 @@
                 pltpu.VMEM((tiles, size, width), jnp.bfloat16),
                 pltpu.SemaphoreType.DMA((tiles, 3)),
             ],
-            [IN_VMEM] * 2 + [ANYWHERE] * 6,
-            56,
+            [IN_VMEM] * 2 + [IN_HBM] * 3,
+            36,
         )
 
     def spread(maps, own_out, other_out, extras=(), after=()):
         return call(spread_kernel, [bf16((count, width))], [*maps, own_out, other_out, *extras], after)[0]
 
     (block,) = call(
-        functools.partial(mark_kernel, experts), [bf16((count, wide))], [tokens, routes, route_scale]
+        functools.partial(mark_kernel, experts), [bf16((count, wide))], [tokens, routes.T, route_scale.T]
     )
     plan = arrivals(places)
     held = {}
-    for step in range(1, places):
+
+    last = []
+
+    def ordered(function, *args, after=()):
+        out = function(*args, after=(*last, *after))
+        last[:] = [out[0] if isinstance(out, (list, tuple)) else out]
+        return out
+
+    picks, outs, returned = {}, {}, []
+
+    def relay(step):
         for way in (1, -1):
             pairs = [
                 (a, a + way)
@@ -204,31 +235,22 @@
             ]
             held[way, step] = along(held.get((way, step - 1), block), pairs)
 
-    last = []
-
-    def ordered(function, *args):
-        out = function(*args, after=tuple(last))
-        last[:] = [out[0] if isinstance(out, (list, tuple)) else out]
-        return out
-
-    picks, outs, returned = {}, {}, []
-
-    def do_pick(slot):
+    def do_pick(slot, after=()):
         if slot == 0:
             blocks, users = [block], [range(places)]
         else:
             keys = sorted({row[slot - 1] for row in plan})
             blocks = [held[key] for key in keys]
             users = [[place for place, row in enumerate(plan) if row[slot - 1] == key] for key in keys]
-        *maps, own_rows, other_rows = ordered(pick, blocks, users)
+        *maps, own_rows, other_rows = ordered(pick, blocks, users, after=after)
         picks[slot] = maps, own_rows, across(other_rows)
 
-    def do_expert(slot):
-        own_out, other_out = ordered(expert, picks[slot][1], picks[slot][2])
+    def do_expert(slot, after=()):
+        own_out, other_out = ordered(expert, picks[slot][1], picks[slot][2], after=after)
         outs[slot] = own_out, across(other_out)
 
-    def do_spread(slot):
-        done = ordered(spread, picks[slot][0], *outs[slot])
+    def do_spread(slot, after=()):
+        done = ordered(spread, picks[slot][0], *outs[slot], after=after)
         home = [(a, a - row[slot - 1][0] * row[slot - 1][1]) for a, row in enumerate(plan)]
         rounds = []
         while home:
@@ -237,18 +259,26 @@
             rounds.append(along(done, now))
         returned.append(rounds)
 
+    relay(1)
     do_pick(0)
+    held[1, 1], held[-1, 1] = tied([held[1, 1], held[-1, 1]], [picks[0][2]])
+    for step in range(2, places):
+        relay(step)
     do_pick(1)
     do_expert(0)
-    for slot in range(1, places):
-        do_expert(slot)
+    do_expert(1)
+    do_pick(2, after=[outs[0][1]])
+    total = ordered(spread, picks[0][0], *outs[0])
+    do_spread(1)
+    for slot in range(2, places):
+        do_expert(slot, after=returned[slot - 3] if slot > 2 else ())
         if slot + 1 < places:
             do_pick(slot + 1)
-            do_spread(slot)
-    first = ordered(spread, picks[0][0], *outs[0], returned[0])
+        if slot > 2:
+            do_spread(slot - 1)
     do_spread(places - 1)
-    total = first.astype(jnp.float32)
-    for block in sum(returned[1:], []):
+    total = total.astype(jnp.float32)
+    for block in sum(returned, []):
         total = total + block.astype(jnp.float32)
     return total.astype(jnp.bfloat16)
 

time: 250 us -> 257 us (1.028)
  between operations: 0.38 us -> 13.4 us
  waiting for transfers between devices: 149 us -> 139 us
  Pallas kernels: 52.9 us -> 45.5 us
  local copies, waits for them, and re-layouts: 11.7 us -> 17.2 us
  starting transfers between devices: 34.7 us -> 39.8 us
    ppermute x11, waiting for transfers between devices: 88.4 us -> 61.3 us  [along(): return lax.ppermute(block, 'node', moves)]
    all_gather x0 -> x3, waiting for transfers between devices: none -> 23.3 us  [on_device(): weights = tuple((lax.all_gather(w, 'local') for w in own))]
    ppermute x8, waiting for transfers between devices: 60.3 us -> 52.1 us  [across(): return lax.ppermute(block, 'node', [(n, n ^ 1) for n in range(experts)])]
    pallas_call x13, Pallas kernels: 52.9 us -> 45.5 us  [call(): pl.pallas_call(body, out_shape=outs, in_specs=specs, out_specs=[IN_VMEM]...]
    ppermute x11, starting transfers between devices: 23.2 us -> 30.5 us  [along(): return lax.ppermute(block, 'node', moves)]
    unnamed x50 -> x38, local copies, waits for them, and re-layouts: 11.7 us -> 17.2 us
  transfers between devices with their start and end apart: 22 -> 22, of which waited for: 9 -> 13; matrix products, arithmetic and copies ran while one was open for 1% -> 0% of each run, Pallas kernels for 21% -> 18%
where the time goes in v4:
time: 257 us; the launch traced here: 256 us
  waiting for transfers between devices  139 us (54%)
  Pallas kernels  45.5 us (18%)
  starting transfers between devices  39.8 us (15%)
  local copies, waits for them, and re-layouts  17.2 us (7%)
  between operations  13.4 us (5%)
    ppermute x11, waiting for transfers between devices, along(): return lax.ppermute(block, 'node', moves)  61.3 us
    ppermute x8, waiting for transfers between devices, across(): return lax.ppermute(block, 'node', [(n, n ^ 1) for n in range(experts)])  52.1 us
    pallas_call x13, Pallas kernels, call(): pl.pallas_call(body, out_shape=outs, in_specs=specs, out_specs=[IN_VMEM]...  45.5 us
    ppermute x11, starting transfers between devices, along(): return lax.ppermute(block, 'node', moves)  30.5 us
    all_gather x3, waiting for transfers between devices, on_device(): weights = tuple((lax.all_gather(w, 'local') for w in own))  23.3 us
    unnamed x38, local copies, waits for them, and re-layouts  17.2 us
    ppermute x8, starting transfers between devices, across(): return lax.ppermute(block, 'node', [(n, n ^ 1) for n in range(experts)])  9.3 us
  transfers between devices with their start and end apart: 22, of which 13 were waited for; matrix products, arithmetic and copies ran while one was open for 0% of the time, Pallas kernels for 18%

profile of v4, /device:TPU:0, one launch (start us, length us, event | category | flops | bytes accessed | tf_op | source)
XLA Modules:
  0.0 256.4 jit_solution(2282534700667114151)
XLA Ops:
  6.5 0.7 all-gather.4.cloned.1.call-update
  7.3 0.0 all-gather.6.cloned.1.call-start
  7.3 0.7 all-gather.6.cloned.1.call-update
  8.0 0.0 all-gather.8.cloned.1.call-start
  8.1 0.7 all-gather.8.cloned.1.call-update
  8.8 0.4 copy-done.12
  9.2 0.3 shard_map.64.refs_0_
  9.5 5.0 %collective-permute-start.1 = (bf16[128,3712]{1,0:T(8,128)(2,1)S(1)}, bf16[128,3712]{1,0:T(8,128)(2,1)S(1)}, u32[]{:S(2)}, u32[]{:S(2)}) collective-permute-start(bf16[128,3712]{1,0:T(8,128)(2,1)S(1)} %shard_map.64.refs_0_), channel_id=1, source_target_pairs={{0,4},{2,6},{4,8},{6,10},{8,12},{10,14},{1,5},{3,7},{5,9},{7,11},{... | collective-permute-start | bytes 2850824 | tf_op jit(solution)/shard_map/ppermute | solution.py:177
  14.5 1.3 collective-permute-start.2
  15.8 1.0 shard_map.65
  16.9 0.8 copy-done.15
  17.7 1.5 collective-permute-start
  19.2 13.4 %collective-permute-done.refs_2_.refs_1_ = bf16[80,3712]{1,0:T(8,128)(2,1)S(1)} collective-permute-done((bf16[80,3712]{1,0:T(8,128)(2,1)S(1)}, bf16[80,3712]{1,0:T(8,128)(2,1)S(1)}, u32[]{:S(2)}, u32[]{:S(2)}) %collective-permute-start) | collective-permute-done | bytes 593952 | tf_op jit(solution)/shard_map/ppermute | solution.py:180
  32.6 2.2 collective-permute-done.1.refs_0_
  34.7 4.2 %collective-permute-done.2.refs_1_ = bf16[128,3712]{1,0:T(8,128)(2,1)S(1)} collective-permute-done((bf16[128,3712]{1,0:T(8,128)(2,1)S(1)}, bf16[128,3712]{1,0:T(8,128)(2,1)S(1)}, u32[]{:S(2)}, u32[]{:S(2)}) %collective-permute-start.2) | collective-permute-done | bytes 950304 | tf_op jit(solution)/shard_map/ppermute | solution.py:177
  38.9 1.0 copy-done.7
  39.9 1.3 collective-permute-start.4
  41.2 0.7 collective-permute-start.5
  41.9 1.4 copy-done.5
  43.3 1.5 copy-done.8
  44.7 1.8 shard_map.67
  46.6 0.8 copy-done.13
  47.4 1.4 collective-permute-start.6
  48.7 2.3 all-gather.6.cloned.1.call-done.refs_3_
  51.0 21.1 %all-gather.8.cloned.1.call-done.refs_4_ = bf16[2,512,3584]{2,1,0:T(8,128)(2,1)} async-done(((bf16[1,512,3584]{2,1,0:T(8,128)(2,1)}), bf16[2,512,3584]{2,1,0:T(8,128)(2,1)}) %all-gather.8.cloned.1.call-update) | async-done | bytes 7340048 | tf_op jit(solution)/shard_map/all_gather | solution.py:173
  72.1 3.1 %copy-done = bf16[2,3584,512]{2,1,0:T(8,128)(2,1)S(1)} copy-done((bf16[2,3584,512]{2,1,0:T(8,128)(2,1)S(1)}, bf16[2,3584,512]{2,1,0:T(8,128)(2,1)}, u32[]{:S(2)}) %copy-start) | copy-done | bytes 7340056
  75.1 3.1 %copy-done.2 = bf16[2,3584,512]{2,1,0:T(8,128)(2,1)S(1)} copy-done((bf16[2,3584,512]{2,1,0:T(8,128)(2,1)S(1)}, bf16[2,3584,512]{2,1,0:T(8,128)(2,1)}, u32[]{:S(2)}) %copy-start.2) | copy-done | bytes 7340056
  78.2 1.1 copy-done.16
  79.3 9.6 %shard_map.68 = (bf16[80,3584]{1,0:T(8,128)(2,1)S(1)}, bf16[80,3584]{1,0:T(8,128)(2,1)}) custom-call(bf16[80,3712]{1,0:T(8,128)(2,1)S(1)} %copy-done.16, bf16[80,3712]{1,0:T(8,128)(2,1)S(1)} %copy-done.11, bf16[2,3584,512]{2,1,0:T(8,128)(2,1)S(1)} %copy-done, bf16[2,3584,512]{2,1,0:T(8,128)(2,1)S(1)} %copy-done.2, ...), custom_call_target="tpu_custom_call" | custom-call | tf_op jit(solution)/shard_map/pallas_call | solution.py:34
  88.8 1.8 collective-permute-start.3
  90.6 0.0 collective-permute-done.4.refs_0_
  90.6 1.3 collective-permute-start.12
  91.9 0.0 collective-permute-done.5.refs_1_
  91.9 1.6 collective-permute-start.13
  93.6 3.1 %copy-done.3 = bf16[2,3584,512]{2,1,0:T(8,128)(2,1)S(1)} copy-done((bf16[2,3584,512]{2,1,0:T(8,128)(2,1)S(1)}, bf16[2,3584,512]{2,1,0:T(8,128)(2,1)}, u32[]{:S(2)}) %copy-start.3) | copy-done | bytes 7340056
  96.7 1.1 copy-done.14
  97.7 9.8 %shard_map.69 = (bf16[80,3584]{1,0:T(8,128)(2,1)S(1)}, bf16[80,3584]{1,0:T(8,128)(2,1)S(1)}) custom-call(bf16[80,3712]{1,0:T(8,128)(2,1)S(1)} %copy-done.14, bf16[80,3712]{1,0:T(8,128)(2,1)} %collective-permute-done.6.refs_1_, bf16[2,3584,512]{2,1,0:T(8,128)(2,1)S(1)} %copy-done.1, bf16[2,3584,512]{2,1,0:T(8,128)(2,1)S(1)} %copy-done.3, ...), custom_call_target="tpu_custom_call" | custom-call | tf_op jit(solution)/shard_map/pallas_call | solution.py:34
  107.5 0.4 collective-permute-start.7
  107.9 1.0 shard_map.70
  108.9 1.8 collective-permute-start.10
  110.7 0.6 shard_map.71.refs_4_
  111.3 12.1 %collective-permute-done.7.refs_3_ = bf16[80,3584]{1,0:T(8,128)(2,1)S(1)} collective-permute-done((bf16[80,3584]{1,0:T(8,128)(2,1)S(1)}, bf16[80,3584]{1,0:T(8,128)(2,1)S(1)}, u32[]{:S(2)}, u32[]{:S(2)}) %collective-permute-start.7) | collective-permute-done | bytes 573472 | tf_op jit(solution)/shard_map/ppermute | solution.py:180
  123.4 0.6 shard_map.72.refs_5_
  124.1 0.7 collective-permute-start.8
  124.8 6.4 %collective-permute-start.9 = (bf16[128,3584]{1,0:T(8,128)(2,1)S(1)}, bf16[128,3584]{1,0:T(8,128)(2,1)S(1)}, u32[]{:S(2)}, u32[]{:S(2)}) collective-permute-start(bf16[128,3584]{1,0:T(8,128)(2,1)S(1)} %shard_map.72.refs_5_), channel_id=1, source_target_pairs={{0,4},{2,6},{4,8},{6,10},{1,5},{3,7},{5,9},{7,11},{16,20},{18,22},... | collective-permute-start | bytes 2752520 | tf_op jit(solution)/shard_map/ppermute | solution.py:177
  131.2 4.1 %collective-permute-done.10.refs_1_ = bf16[80,3712]{1,0:T(8,128)(2,1)S(1)} collective-permute-done((bf16[80,3712]{1,0:T(8,128)(2,1)S(1)}, bf16[80,3712]{1,0:T(8,128)(2,1)S(1)}, u32[]{:S(2)}, u32[]{:S(2)}) %collective-permute-start.10) | collective-permute-done | bytes 593952 | tf_op jit(solution)/shard_map/ppermute | solution.py:180
  135.2 8.8 %shard_map.73 = (bf16[80,3584]{1,0:T(8,128)(2,1)S(1)}, bf16[80,3584]{1,0:T(8,128)(2,1)S(1)}) custom-call(bf16[80,3712]{1,0:T(8,128)(2,1)S(1)} %get-tuple-element.47.refs_0_, bf16[80,3712]{1,0:T(8,128)(2,1)S(1)} %collective-permute-done.10.refs_1_, bf16[2,3584,512]{2,1,0:T(8,128)(2,1)S(1)} %copy-done.1, bf16[2,3584,512]{2,1,0:T(8,128)(2,1)S(1)} %copy-done.3, ...), custom_call_target="tpu_custom_call" | custom-call | tf_op jit(solution)/shard_map/pallas_call | solution.py:34
  144.0 2.0 shard_map.74
  146.0 0.4 collective-permute-start.14
  146.4 1.7 collective-permute-start.11
  148.1 0.1 collective-permute-done.9.refs_7_
  148.2 14.2 %collective-permute-done.14.refs_1_ = bf16[80,3712]{1,0:T(8,128)(2,1)S(1)} collective-permute-done((bf16[80,3712]{1,0:T(8,128)(2,1)S(1)}, bf16[80,3712]{1,0:T(8,128)(2,1)S(1)}, u32[]{:S(2)}, u32[]{:S(2)}) %collective-permute-start.14) | collective-permute-done | bytes 593952 | tf_op jit(solution)/shard_map/ppermute | solution.py:180
  162.4 8.8 %shard_map.75 = (bf16[80,3584]{1,0:T(8,128)(2,1)S(1)}, bf16[80,3584]{1,0:T(8,128)(2,1)S(1)}) custom-call(bf16[80,3712]{1,0:T(8,128)(2,1)S(1)} %get-tuple-element.51.refs_0_, bf16[80,3712]{1,0:T(8,128)(2,1)S(1)} %collective-permute-done.14.refs_1_, bf16[2,3584,512]{2,1,0:T(8,128)(2,1)S(1)} %copy-done.1, ...), custom_call_target="tpu_custom_call" | custom-call | tf_op jit(solution)/shard_map/pallas_call | solution.py:34
  171.3 0.4 collective-permute-start.16
  171.6 3.1 %collective-permute-done.11.refs_3_ = bf16[80,3584]{1,0:T(8,128)(2,1)S(1)} collective-permute-done((bf16[80,3584]{1,0:T(8,128)(2,1)S(1)}, bf16[80,3584]{1,0:T(8,128)(2,1)S(1)}, u32[]{:S(2)}, u32[]{:S(2)}) %collective-permute-start.11) | collective-permute-done | bytes 573472 | tf_op jit(solution)/shard_map/ppermute | solution.py:180
  174.7 0.6 shard_map.76.refs_4_
  175.3 4.6 %collective-permute-start.15 = (bf16[128,3584]{1,0:T(8,128)(2,1)S(1)}, bf16[128,3584]{1,0:T(8,128)(2,1)S(1)}, u32[]{:S(2)}, u32[]{:S(2)}) collective-permute-start(bf16[128,3584]{1,0:T(8,128)(2,1)S(1)} %shard_map.76.refs_4_), channel_id=1, source_target_pairs={{0,8},{2,10},{4,12},{6,14},{8,0},{10,2},{12,4},{14,6},{1,9},{3,11}... | collective-permute-start | bytes 2752520 | tf_op jit(solution)/shard_map/ppermute | solution.py:177
  179.9 5.3 %collective-permute-done.16.refs_3_ = bf16[80,3584]{1,0:T(8,128)(2,1)S(1)} collective-permute-done((bf16[80,3584]{1,0:T(8,128)(2,1)S(1)}, bf16[80,3584]{1,0:T(8,128)(2,1)S(1)}, u32[]{:S(2)}, u32[]{:S(2)}) %collective-permute-start.16) | collective-permute-done | bytes 573472 | tf_op jit(solution)/shard_map/ppermute | solution.py:180
  185.2 0.6 shard_map.77
  185.8 1.3 collective-permute-start.17
  187.1 6.3 %collective-permute-start.18 = (bf16[128,3584]{1,0:T(8,128)(2,1)S(1)}, bf16[128,3584]{1,0:T(8,128)(2,1)S(1)}, u32[]{:S(2)}, u32[]{:S(2)}) collective-permute-start(bf16[128,3584]{1,0:T(8,128)(2,1)S(1)} %shard_map.77), channel_id=1, source_target_pairs={{0,12},{2,14},{4,0},{6,2},{1,13},{3,15},{5,1},{7,3},{16,28},{18,30... | collective-permute-start | bytes 2752520 | tf_op jit(solution)/shard_map/ppermute | solution.py:177
  193.4 42.1 %collective-permute-done.15 = bf16[128,3584]{1,0:T(8,128)(2,1)S(1)} collective-permute-done((bf16[128,3584]{1,0:T(8,128)(2,1)S(1)}, bf16[128,3584]{1,0:T(8,128)(2,1)S(1)}, u32[]{:S(2)}, u32[]{:S(2)}) %collective-permute-start.15) | collective-permute-done | bytes 917536 | tf_op jit(solution)/shard_map/ppermute | solution.py:177
  235.6 12.7 %collective-permute-done.18 = bf16[128,3584]{1,0:T(8,128)(2,1)S(1)} collective-permute-done((bf16[128,3584]{1,0:T(8,128)(2,1)S(1)}, bf16[128,3584]{1,0:T(8,128)(2,1)S(1)}, u32[]{:S(2)}, u32[]{:S(2)}) %collective-permute-start.18) | collective-permute-done | bytes 917536 | tf_op jit(solution)/shard_map/ppermute | solution.py:177
  248.3 1.6 add_convert_fusion
  (36 shorter events, 0.1 us)
Async XLA Ops:
  6.5 42.2 %all-gather.4.cloned.1.call-start = ((), (), s32[]{:S(2)}) async-start(), calls=%async_computation | async-start | bytes 11010048 | tf_op jit(solution)/shard_map/all_gather | solution.py:173
  7.3 43.7 %all-gather.6.cloned.1.call-start = ((), (), s32[]{:S(2)}) async-start(), calls=%async_computation.1 | async-start | bytes 11010048 | tf_op jit(solution)/shard_map/all_gather | solution.py:173
  8.0 1.2 copy-start.12
  8.0 1.2 copy-start.17
  8.0 1.2 copy-start.18
  8.0 64.0 %all-gather.8.cloned.1.call-start = ((), (), s32[]{:S(2)}) async-start(), calls=%async_computation.2 | async-start | bytes 11010048 | tf_op jit(solution)/shard_map/all_gather | solution.py:173
  9.5 25.2 %collective-permute-start.1 = (bf16[128,3712]{1,0:T(8,128)(2,1)S(1)}, bf16[128,3712]{1,0:T(8,128)(2,1)S(1)}, u32[]{:S(2)}, u32[]{:S(2)}) collective-permute-start(bf16[128,3712]{1,0:T(8,128)(2,1)S(1)} %shard_map.64.refs_0_), channel_id=1, source_target_pairs={{0,4},{2,6},{4,8},{6,10},{8,12},{10,14},{1,5},{3,7},{5,9},{7,11},{... | collective-permute-start | bytes 2850824 | tf_op jit(solution)/shard_map/ppermute | solution.py:177
  14.5 24.4 %collective-permute-start.2 = (bf16[128,3712]{1,0:T(8,128)(2,1)S(1)}, bf16[128,3712]{1,0:T(8,128)(2,1)S(1)}, u32[]{:S(2)}, u32[]{:S(2)}) collective-permute-start(bf16[128,3712]{1,0:T(8,128)(2,1)S(1)} %shard_map.64.refs_0_), channel_id=1, source_target_pairs={{4,0},{6,2},{8,4},{10,6},{12,8},{14,10},{5,1},{7,3},{9,5},{11,7},{... | collective-permute-start | bytes 2850824 | tf_op jit(solution)/shard_map/ppermute | solution.py:177
  16.8 0.8 copy-start.15
  17.7 14.9 %collective-permute-start = (bf16[80,3712]{1,0:T(8,128)(2,1)S(1)}, bf16[80,3712]{1,0:T(8,128)(2,1)S(1)}, u32[]{:S(2)}, u32[]{:S(2)}) collective-permute-start(bf16[80,3712]{1,0:T(8,128)(2,1)S(1)} %get-tuple-element.34), channel_id=1, source_target_pairs={{0,2},{2,0},{4,6},{6,4},{8,10},{10,8},{12,14},{14,12},{1,3},{3,1},... | collective-permute-start | bytes 1781768 | tf_op jit(solution)/shard_map/ppermute | solution.py:180
  32.6 6.4 %copy-start.10 = (bf16[80,3712]{1,0:T(8,128)(2,1)}, bf16[80,3712]{1,0:T(8,128)(2,1)S(1)}, u32[]{:S(2)}) copy-start(bf16[80,3712]{1,0:T(8,128)(2,1)S(1)} %collective-permute-done.refs_2_.refs_1_) | copy-start | bytes 1781764
  34.7 4.2 %copy-start.4 = (bf16[128,3712]{1,0:T(8,128)(2,1)}, bf16[128,3712]{1,0:T(8,128)(2,1)S(1)}, u32[]{:S(2)}) copy-start(bf16[128,3712]{1,0:T(8,128)(2,1)S(1)} %collective-permute-done.1.refs_0_) | copy-start | bytes 2850820
  38.9 1.0 copy-start.7
  39.9 50.7 %collective-permute-start.4 = (bf16[128,3712]{1,0:T(8,128)(2,1)}, bf16[128,3712]{1,0:T(8,128)(2,1)S(1)}, u32[]{:S(2)}, u32[]{:S(2)}) collective-permute-start(bf16[128,3712]{1,0:T(8,128)(2,1)} %get-tuple-element.35.refs_0_), channel_id=1, source_target_pairs={{4,0},{6,2},{8,4},{10,6},{5,1},{7,3},{9,5},{11,7},{20,16},{22,18},... | collective-permute-start | bytes 2850824 | tf_op jit(solution)/shard_map/ppermute | solution.py:177
  41.2 50.8 %collective-permute-start.5 = (bf16[128,3712]{1,0:T(8,128)(2,1)}, bf16[128,3712]{1,0:T(8,128)(2,1)S(1)}, u32[]{:S(2)}, u32[]{:S(2)}) collective-permute-start(bf16[128,3712]{1,0:T(8,128)(2,1)} %get-tuple-element.36.refs_1_.refs_2_), channel_id=1, source_target_pairs={{4,8},{6,10},{8,12},{10,14},{5,9},{7,11},{9,13},{11,15},{20,24},{2... | collective-permute-start | bytes 2850824 | tf_op jit(solution)/shard_map/ppermute | solution.py:177
  41.9 1.4 copy-start.5
  43.3 1.5 copy-start.8
  44.7 27.3 %copy-start.11 = (bf16[80,3712]{1,0:T(8,128)(2,1)S(1)}, bf16[80,3712]{1,0:T(8,128)(2,1)}, u32[]{:S(2)}) copy-start(bf16[80,3712]{1,0:T(8,128)(2,1)} %copy-done.10) | copy-start | bytes 1781764
  46.6 0.8 copy-start.13
  47.4 46.2 %collective-permute-start.6 = (bf16[80,3712]{1,0:T(8,128)(2,1)}, bf16[80,3712]{1,0:T(8,128)(2,1)}, u32[]{:S(2)}, u32[]{:S(2)}) collective-permute-start(bf16[80,3712]{1,0:T(8,128)(2,1)} %get-tuple-element.41), channel_id=1, source_target_pairs={{0,2},{2,0},{4,6},{6,4},{8,10},{10,8},{12,14},{14,12},{1,3},{3,1},... | collective-permute-start | bytes 1781768 | tf_op jit(solution)/shard_map/ppermute | solution.py:180
  72.0 3.1 %copy-start = (bf16[2,3584,512]{2,1,0:T(8,128)(2,1)S(1)}, bf16[2,3584,512]{2,1,0:T(8,128)(2,1)}, u32[]{:S(2)}) copy-start(bf16[2,3584,512]{2,1,0:T(8,128)(2,1)} %all-gather.4.cloned.1.call-done.refs_2_) | copy-start | bytes 22020100
  75.1 3.1 %copy-start.2 = (bf16[2,3584,512]{2,1,0:T(8,128)(2,1)S(1)}, bf16[2,3584,512]{2,1,0:T(8,128)(2,1)}, u32[]{:S(2)}) copy-start(bf16[2,3584,512]{2,1,0:T(8,128)(2,1)} %all-gather.6.cloned.1.call-done.refs_3_) | copy-start | bytes 22020100
  78.2 1.1 copy-start.16
  79.3 14.3 %copy-start.1 = (bf16[2,3584,512]{2,1,0:T(8,128)(2,1)S(1)}, bf16[2,3584,512]{2,1,0:T(8,128)(2,1)}, u32[]{:S(2)}) copy-start(bf16[2,3584,512]{2,1,0:T(8,128)(2,1)} %all-gather.4.cloned.1.call-done.refs_2_) | copy-start | bytes 22020100
  88.8 19.1 %collective-permute-start.3 = (bf16[80,3584]{1,0:T(8,128)(2,1)}, bf16[80,3584]{1,0:T(8,128)(2,1)S(1)}, u32[]{:S(2)}, u32[]{:S(2)}) collective-permute-start(bf16[80,3584]{1,0:T(8,128)(2,1)} %get-tuple-element.39), channel_id=1, source_target_pairs={{0,2},{2,0},{4,6},{6,4},{8,10},{10,8},{12,14},{14,12},{1,3},{3,1},... | collective-permute-start | bytes 1720328 | tf_op jit(solution)/shard_map/ppermute | solution.py:180
  90.6 53.4 %collective-permute-start.12 = (bf16[128,3712]{1,0:T(8,128)(2,1)S(1)}, bf16[128,3712]{1,0:T(8,128)(2,1)}, u32[]{:S(2)}, u32[]{:S(2)}) collective-permute-start(bf16[128,3712]{1,0:T(8,128)(2,1)S(1)} %collective-permute-done.4.refs_0_), channel_id=1, source_target_pairs={{4,0},{6,2},{5,1},{7,3},{20,16},{22,18},{21,17},{23,19}} | collective-permute-start | bytes 2850824 | tf_op jit(solution)/shard_map/ppermute | solution.py:177
  91.9 52.1 %collective-permute-start.13 = (bf16[128,3712]{1,0:T(8,128)(2,1)S(1)}, bf16[128,3712]{1,0:T(8,128)(2,1)}, u32[]{:S(2)}, u32[]{:S(2)}) collective-permute-start(bf16[128,3712]{1,0:T(8,128)(2,1)S(1)} %collective-permute-done.5.refs_1_), channel_id=1, source_target_pairs={{8,12},{10,14},{9,13},{11,15},{24,28},{26,30},{25,29},{27,31}} | collective-permute-start | bytes 2850824 | tf_op jit(solution)/shard_map/ppermute | solution.py:177
  93.6 3.1 %copy-start.3 = (bf16[2,3584,512]{2,1,0:T(8,128)(2,1)S(1)}, bf16[2,3584,512]{2,1,0:T(8,128)(2,1)}, u32[]{:S(2)}) copy-start(bf16[2,3584,512]{2,1,0:T(8,128)(2,1)} %all-gather.6.cloned.1.call-done.refs_3_) | copy-start | bytes 22020100
  96.7 1.1 copy-start.14
  107.5 15.9 %collective-permute-start.7 = (bf16[80,3584]{1,0:T(8,128)(2,1)S(1)}, bf16[80,3584]{1,0:T(8,128)(2,1)S(1)}, u32[]{:S(2)}, u32[]{:S(2)}) collective-permute-start(bf16[80,3584]{1,0:T(8,128)(2,1)S(1)} %get-tuple-element.45), channel_id=1, source_target_pairs={{0,2},{2,0},{4,6},{6,4},{8,10},{10,8},{12,14},{14,12},{1,3},{3,1},... | collective-permute-start | bytes 1720328 | tf_op jit(solution)/shard_map/ppermute | solution.py:180
  108.9 26.3 %collective-permute-start.10 = (bf16[80,3712]{1,0:T(8,128)(2,1)S(1)}, bf16[80,3712]{1,0:T(8,128)(2,1)S(1)}, u32[]{:S(2)}, u32[]{:S(2)}) collective-permute-start(bf16[80,3712]{1,0:T(8,128)(2,1)S(1)} %get-tuple-element.48), channel_id=1, source_target_pairs={{0,2},{2,0},{4,6},{6,4},{8,10},{10,8},{12,14},{14,12},{1,3},{3,1},... | collective-permute-start | bytes 1781768 | tf_op jit(solution)/shard_map/ppermute | solution.py:180
  124.1 24.0 %collective-permute-start.8 = (bf16[128,3584]{1,0:T(8,128)(2,1)S(1)}, bf16[128,3584]{1,0:T(8,128)(2,1)S(1)}, u32[]{:S(2)}, u32[]{:S(2)}) collective-permute-start(bf16[128,3584]{1,0:T(8,128)(2,1)S(1)} %shard_map.72.refs_5_), channel_id=1, source_target_pairs={{8,4},{10,6},{12,8},{14,10},{9,5},{11,7},{13,9},{15,11},{24,20},{2... | collective-permute-start | bytes 2752520 | tf_op jit(solution)/shard_map/ppermute | solution.py:177
  124.8 23.4 %collective-permute-start.9 = (bf16[128,3584]{1,0:T(8,128)(2,1)S(1)}, bf16[128,3584]{1,0:T(8,128)(2,1)S(1)}, u32[]{:S(2)}, u32[]{:S(2)}) collective-permute-start(bf16[128,3584]{1,0:T(8,128)(2,1)S(1)} %shard_map.72.refs_5_), channel_id=1, source_target_pairs={{0,4},{2,6},{4,8},{6,10},{1,5},{3,7},{5,9},{7,11},{16,20},{18,22},... | collective-permute-start | bytes 2752520 | tf_op jit(solution)/shard_map/ppermute | solution.py:177
  135.2 8.8 %copy-start.6 = (bf16[128,3712]{1,0:T(8,128)(2,1)S(1)}, bf16[128,3712]{1,0:T(8,128)(2,1)}, u32[]{:S(2)}) copy-start(bf16[128,3712]{1,0:T(8,128)(2,1)} %get-tuple-element.36.refs_1_.refs_2_) | copy-start | bytes 2850820
  135.2 8.8 %copy-start.9 = (bf16[128,3712]{1,0:T(8,128)(2,1)S(1)}, bf16[128,3712]{1,0:T(8,128)(2,1)}, u32[]{:S(2)}) copy-start(bf16[128,3712]{1,0:T(8,128)(2,1)} %get-tuple-element.35.refs_0_) | copy-start | bytes 2850820
  146.0 16.4 %collective-permute-start.14 = (bf16[80,3712]{1,0:T(8,128)(2,1)S(1)}, bf16[80,3712]{1,0:T(8,128)(2,1)S(1)}, u32[]{:S(2)}, u32[]{:S(2)}) collective-permute-start(bf16[80,3712]{1,0:T(8,128)(2,1)S(1)} %get-tuple-element.52), channel_id=1, source_target_pairs={{0,2},{2,0},{4,6},{6,4},{8,10},{10,8},{12,14},{14,12},{1,3},{3,1},... | collective-permute-start | bytes 1781768 | tf_op jit(solution)/shard_map/ppermute | solution.py:180
  146.4 28.3 %collective-permute-start.11 = (bf16[80,3584]{1,0:T(8,128)(2,1)S(1)}, bf16[80,3584]{1,0:T(8,128)(2,1)S(1)}, u32[]{:S(2)}, u32[]{:S(2)}) collective-permute-start(bf16[80,3584]{1,0:T(8,128)(2,1)S(1)} %get-tuple-element.50), channel_id=1, source_target_pairs={{0,2},{2,0},{4,6},{6,4},{8,10},{10,8},{12,14},{14,12},{1,3},{3,1},... | collective-permute-start | bytes 1720328 | tf_op jit(solution)/shard_map/ppermute | solution.py:180
  171.3 13.9 %collective-permute-start.16 = (bf16[80,3584]{1,0:T(8,128)(2,1)S(1)}, bf16[80,3584]{1,0:T(8,128)(2,1)S(1)}, u32[]{:S(2)}, u32[]{:S(2)}) collective-permute-start(bf16[80,3584]{1,0:T(8,128)(2,1)S(1)} %get-tuple-element.56), channel_id=1, source_target_pairs={{0,2},{2,0},{4,6},{6,4},{8,10},{10,8},{12,14},{14,12},{1,3},{3,1},... | collective-permute-start | bytes 1720328 | tf_op jit(solution)/shard_map/ppermute | solution.py:180
  175.3 60.2 %collective-permute-start.15 = (bf16[128,3584]{1,0:T(8,128)(2,1)S(1)}, bf16[128,3584]{1,0:T(8,128)(2,1)S(1)}, u32[]{:S(2)}, u32[]{:S(2)}) collective-permute-start(bf16[128,3584]{1,0:T(8,128)(2,1)S(1)} %shard_map.76.refs_4_), channel_id=1, source_target_pairs={{0,8},{2,10},{4,12},{6,14},{8,0},{10,2},{12,4},{14,6},{1,9},{3,11}... | collective-permute-start | bytes 2752520 | tf_op jit(solution)/shard_map/ppermute | solution.py:177
  185.8 49.8 %collective-permute-start.17 = (bf16[128,3584]{1,0:T(8,128)(2,1)S(1)}, bf16[128,3584]{1,0:T(8,128)(2,1)S(1)}, u32[]{:S(2)}, u32[]{:S(2)}) collective-permute-start(bf16[128,3584]{1,0:T(8,128)(2,1)S(1)} %shard_map.77), channel_id=1, source_target_pairs={{8,12},{10,14},{12,0},{14,2},{9,13},{11,15},{13,1},{15,3},{24,28},... | collective-permute-start | bytes 2752520 | tf_op jit(solution)/shard_map/ppermute | solution.py:177
  187.1 61.2 %collective-permute-start.18 = (bf16[128,3584]{1,0:T(8,128)(2,1)S(1)}, bf16[128,3584]{1,0:T(8,128)(2,1)S(1)}, u32[]{:S(2)}, u32[]{:S(2)}) collective-permute-start(bf16[128,3584]{1,0:T(8,128)(2,1)S(1)} %shard_map.77), channel_id=1, source_target_pairs={{0,12},{2,14},{4,0},{6,2},{1,13},{3,15},{5,1},{7,3},{16,28},{18,30... | collective-permute-start | bytes 2752520 | tf_op jit(solution)/shard_map/ppermute | solution.py:177
Sparse Core Ops, SparseCore 0:
  8.9 20.9 all-gather.3
  31.5 19.4 all-gather.5
  52.5 19.4 all-gather.7

commit v5 on v4

--- a/solution.py
+++ b/solution.py
@@ -22,7 +22,7 @@
     return plan
 
 
-def call(kernel, outs, ins, after=(), scratch=(), specs=None, vmem=24):
+def call(kernel, outs, ins, after=(), scratch=(), specs=None, vmem=24, out_specs=None):
     body = kernel
     if after:
         first, last = len(ins), len(ins) + len(after)
@@ -35,7 +35,7 @@
         body,
         out_shape=outs,
         in_specs=specs,
-        out_specs=[IN_VMEM] * len(outs),
+        out_specs=out_specs or [IN_VMEM] * len(outs),
         scratch_shapes=scratch,
         compiler_params=pltpu.CompilerParams(vmem_limit_bytes=vmem * MIB),
         cost_estimate=pl.CostEstimate(flops=0, bytes_accessed=0, transcendentals=0),
@@ -53,7 +53,14 @@
     )(*arrays, *after)
 
 
-def mark_kernel(experts, tokens, routes, scale, block):
+def first_kernel(experts, tokens, routes, scale, gate_w, up_w, block, *refs):
+    picked, (stack, sems) = refs[:4], refs[4:]
+    copies = [
+        pltpu.make_async_copy(gate_w, stack.at[0], sems.at[0]),
+        pltpu.make_async_copy(up_w, stack.at[1], sems.at[1]),
+    ]
+    for copy in copies:
+        copy.start()
     count, width = tokens.shape
     lane = lax.broadcasted_iota(jnp.int32, (count, block.shape[1] - width), 1)
     expert, part = lax.rem(lane, experts), lax.div(lane, experts)
@@ -67,20 +74,13 @@
     marks = jnp.where(part == 0, high, jnp.where(part == 1, middle, jnp.where(part == 2, low, 0.0)))
     block[:, :width] = tokens[...]
     block[:, width:] = marks.astype(jnp.bfloat16)
-
-
-def pick_kernel(users, *refs):
-    blocks, (own_map, other_map, own_rows, other_rows, held, sem) = refs[: len(users)], refs[len(users) :]
+    choose(block, *picked)
+    for copy in copies:
+        copy.wait()
+
+
+def choose(held, own_map, other_map, own_rows, other_rows):
     node = lax.axis_index("node")
-    for block, places in zip(blocks, users):
-        here = functools.reduce(jnp.logical_or, [lax.div(node, 2) == place for place in places])
-
-        @pl.when(here)
-        def _():
-            copy = pltpu.make_async_copy(block, held, sem)
-            copy.start()
-            copy.wait()
-
     count, cap = own_map.shape
     marks = held[:, held.shape[1] - 128 :].astype(jnp.float32)
     lane = lax.broadcasted_iota(jnp.int32, marks.shape, 1)
@@ -100,54 +100,67 @@
         ).astype(jnp.bfloat16)
 
 
-def expert_kernel(experts, own, other, gate_w, up_w, down_w, own_out, other_out, *scratch):
-    rows, total, gates, ups, downs, sems = scratch
+def pick_kernel(users, *refs):
+    blocks, (held, sem) = refs[: len(users)], refs[len(users) + 4 :]
+    node = lax.axis_index("node")
+    for block, places in zip(blocks, users):
+        here = functools.reduce(jnp.logical_or, [lax.div(node, 2) == place for place in places])
+
+        @pl.when(here)
+        def _():
+            copy = pltpu.make_async_copy(block, held, sem)
+            copy.start()
+            copy.wait()
+
+    choose(held, *refs[len(users) : len(users) + 4])
+
+
+def expert_kernel(experts, own, other, *refs):
+    own_w, other_w, own_down, other_down, own_out, other_out, rows, hidden, gates, ups, downs, sems = refs
     cap, width = own_out.shape
     tiles, _, size = gates.shape
-    each = tiles // gate_w.shape[0]
-    copies = []
+    each = tiles // 2
+    queue = []
     for tile in range(tiles):
-        half, part = tile // each, pl.ds(tile % each * size, size)
-        copies.append(
-            [
-                pltpu.make_async_copy(gate_w.at[half, :, part], gates.at[tile], sems.at[tile, 0]),
-                pltpu.make_async_copy(up_w.at[half, :, part], ups.at[tile], sems.at[tile, 1]),
-                pltpu.make_async_copy(down_w.at[half, part, :], downs.at[tile], sems.at[tile, 2]),
-            ]
-        )
-    ahead = [copy for tile in copies for copy in tile]
-    for copy in ahead[:4]:
+        stack, part = (own_w, other_w)[tile // each], pl.ds(tile % each * size, size)
+        queue.append(pltpu.make_async_copy(stack.at[0, :, part], gates.at[tile], sems.at[tile, 0]))
+        queue.append(pltpu.make_async_copy(stack.at[1, :, part], ups.at[tile], sems.at[tile, 1]))
+    for half, down in enumerate((own_down, other_down)):
+        queue.append(pltpu.make_async_copy(down, downs.at[half], sems.at[half, 2]))
+    ahead = iter(queue[4:])
+    for copy in queue[:4]:
         copy.start()
-    waiting = list(ahead[4:])
 
     def arrived(copy):
         copy.wait()
-        if waiting:
-            waiting.pop(0).start()
+        for following in ahead:
+            following.start()
+            break
 
     rows[:cap] = own[:, :width]
     rows[cap:] = other[:, :width]
+    for tile in range(tiles):
+        arrived(queue[2 * tile])
+        gate = jnp.dot(rows[...], gates[tile], preferred_element_type=jnp.float32)
+        arrived(queue[2 * tile + 1])
+        up = jnp.dot(rows[...], ups[tile], preferred_element_type=jnp.float32)
+        hidden[:, tile * size : (tile + 1) * size] = (gate / (1.0 + jnp.exp(-gate)) * up).astype(jnp.bfloat16)
+    arrived(queue[-2])
+    arrived(queue[-1])
     node = lax.axis_index("node")
-    for tile in range(tiles):
-        arrived(copies[tile][0])
-        gate = jnp.dot(rows[...], gates[tile], preferred_element_type=jnp.float32)
-        arrived(copies[tile][1])
-        up = jnp.dot(rows[...], ups[tile], preferred_element_type=jnp.float32)
-        hidden = (gate / (1.0 + jnp.exp(-gate)) * up).astype(jnp.bfloat16)
-        arrived(copies[tile][2])
-        out = jnp.dot(hidden, downs[tile], preferred_element_type=jnp.float32)
-        if tile == 0:
-            total[...] = out
-        elif tile < tiles - 1:
-            total[...] += out
-        else:
-            out += total[...]
-            for first, marks, result in ((0, own, own_out), (cap, other, other_out)):
-                marks = marks[:, width:].astype(jnp.float32)
-                lane = lax.broadcasted_iota(jnp.int32, marks.shape, 1)
-                mine = (lax.rem(lane, experts) == node) & (lane < 3 * experts)
-                scale = jnp.sum(jnp.where(mine, marks, 0.0), axis=1, keepdims=True)
-                result[...] = (out[first : first + cap] * scale).astype(jnp.bfloat16)
+    scales = []
+    for marked in (own, other):
+        marks = marked[:, width:].astype(jnp.float32)
+        lane = lax.broadcasted_iota(jnp.int32, marks.shape, 1)
+        mine = (lax.rem(lane, experts) == node) & (lane < 3 * experts)
+        scales.append(jnp.sum(jnp.where(mine, marks, 0.0), axis=1, keepdims=True))
+    step = 512 if width % 512 == 0 else width
+    for start in range(0, width, step):
+        cut = slice(start, start + step)
+        out = jnp.dot(hidden[:, : each * size], downs[0, :, cut], preferred_element_type=jnp.float32)
+        out += jnp.dot(hidden[:, each * size :], downs[1, :, cut], preferred_element_type=jnp.float32)
+        own_out[:, cut] = (out[:cap] * scales[0]).astype(jnp.bfloat16)
+        other_out[:, cut] = (out[cap:] * scales[1]).astype(jnp.bfloat16)
 
 
 def spread_kernel(own_map, other_map, own_out, other_out, *refs):
@@ -167,10 +180,27 @@
     size = min(hidden, 256)
     cap = -(-(5 * count // experts) // 16) * 16
     wide = width + -(-3 * experts // 128) * 128
+    in_hbm = functools.partial(pltpu.with_memory_space_constraint, memory_space=pltpu.HBM)
     bf16 = functools.partial(jax.ShapeDtypeStruct, dtype=jnp.bfloat16)
 
-    own = (w_gate[0], w_up[0], w_down[0])
-    weights = tuple(lax.all_gather(w, "local") for w in own)
+    block, *picked, stack = call(
+        functools.partial(first_kernel, experts),
+        [
+            bf16((count, wide)),
+            bf16((count, cap)),
+            bf16((count, cap)),
+            bf16((cap, wide)),
+            bf16((cap, wide)),
+            pltpu.HBM((2, width, hidden), jnp.bfloat16),
+        ],
+        [tokens, routes.T, route_scale.T, in_hbm(w_gate[0]), in_hbm(w_up[0])],
+        (),
+        [pltpu.SemaphoreType.DMA((2,))],
+        [IN_VMEM] * 3 + [ANYWHERE] * 2,
+        out_specs=[IN_VMEM] * 5 + [IN_HBM],
+    )
+    swap = functools.partial(lax.ppermute, axis_name="local", perm=[(0, 1), (1, 0)])
+    weights = [in_hbm(stack), swap(stack), in_hbm(w_down[0]), swap(w_down[0])]
 
     def along(block, pairs):
         moves = [(2 * a + y, 2 * b + y) for a, b in pairs for y in range(2)]
@@ -198,22 +228,19 @@
             after,
             [
                 pltpu.VMEM((2 * cap, width), jnp.bfloat16),
-                pltpu.VMEM((2 * cap, width), jnp.float32),
+                pltpu.VMEM((2 * cap, 2 * hidden), jnp.bfloat16),
                 pltpu.VMEM((tiles, width, size), jnp.bfloat16),
                 pltpu.VMEM((tiles, width, size), jnp.bfloat16),
-                pltpu.VMEM((tiles, size, width), jnp.bfloat16),
+                pltpu.VMEM((2, hidden, width), jnp.bfloat16),
                 pltpu.SemaphoreType.DMA((tiles, 3)),
             ],
-            [IN_VMEM] * 2 + [IN_HBM] * 3,
+            [IN_VMEM] * 2 + [ANYWHERE] * 4,
             36,
         )
 
     def spread(maps, own_out, other_out, extras=(), after=()):
         return call(spread_kernel, [bf16((count, width))], [*maps, own_out, other_out, *extras], after)[0]
 
-    (block,) = call(
-        functools.partial(mark_kernel, experts), [bf16((count, wide))], [tokens, routes.T, route_scale.T]
-    )
     plan = arrivals(places)
     held = {}
 
@@ -236,12 +263,9 @@
             held[way, step] = along(held.get((way, step - 1), block), pairs)
 
     def do_pick(slot, after=()):
-        if slot == 0:
-            blocks, users = [block], [range(places)]
-        else:
-            keys = sorted({row[slot - 1] for row in plan})
-            blocks = [held[key] for key in keys]
-            users = [[place for place, row in enumerate(plan) if row[slot - 1] == key] for key in keys]
+        keys = sorted({row[slot - 1] for row in plan})
+        blocks = [held[key] for key in keys]
+        users = [[place for place, row in enumerate(plan) if row[slot - 1] == key] for key in keys]
         *maps, own_rows, other_rows = ordered(pick, blocks, users, after=after)
         picks[slot] = maps, own_rows, across(other_rows)
 
@@ -260,7 +284,7 @@
         returned.append(rounds)
 
     relay(1)
-    do_pick(0)
+    picks[0] = picked[:2], picked[2], across(picked[3])
     held[1, 1], held[-1, 1] = tied([held[1, 1], held[-1, 1]], [picks[0][2]])
     for step in range(2, places):
         relay(step)

time: 257 us -> 429 us (1.67)
  Pallas kernels: 45.5 us -> 267 us
  waiting for transfers between devices: 139 us -> 115 us
  between operations: 13.4 us -> 0.25 us
  local copies, waits for them, and re-layouts: 17.2 us -> 5.88 us
    pallas_call x13 -> x12, Pallas kernels: 45.5 us -> 267 us  [call(): pl.pallas_call(body, out_shape=outs, in_specs=specs, out_specs=out_specs...]
    all_gather x3 -> x0, waiting for transfers between devices: 23.3 us -> none  [on_device(): weights = tuple((lax.all_gather(w, 'local') for w in own))]
    unnamed x38 -> x22, local copies, waits for them, and re-layouts: 17.2 us -> 5.88 us
    ppermute x11, waiting for transfers between devices: 61.3 us -> 67.9 us  [along(): return lax.ppermute(block, 'node', moves)]
    ppermute x8, waiting for transfers between devices: 52.1 us -> 47.5 us  [across(): return lax.ppermute(block, 'node', [(n, n ^ 1) for n in range(experts)])]
  transfers between devices with their start and end apart: 22 -> 21, of which waited for: 13 -> 11; matrix products, arithmetic and copies ran while one was open for 0% -> 0% of each run, Pallas kernels for 18% -> 10%
where the time goes in v5:
time: 429 us; the launch traced here: 428 us
  Pallas kernels  267 us (62%)
  waiting for transfers between devices  115 us (27%)
  starting transfers between devices  38.7 us (9%)
  local copies, waits for them, and re-layouts  5.88 us (1%)
    pallas_call x12, Pallas kernels, call(): pl.pallas_call(body, out_shape=outs, in_specs=specs, out_specs=out_specs...  267 us
    ppermute x11, waiting for transfers between devices, along(): return lax.ppermute(block, 'node', moves)  67.9 us
    ppermute x8, waiting for transfers between devices, across(): return lax.ppermute(block, 'node', [(n, n ^ 1) for n in range(experts)])  47.5 us
    ppermute x11, starting transfers between devices, along(): return lax.ppermute(block, 'node', moves)  28.5 us
    ppermute x8, starting transfers between devices, across(): return lax.ppermute(block, 'node', [(n, n ^ 1) for n in range(experts)])  9.58 us
  transfers between devices with their start and end apart: 21, of which 11 were waited for; matrix products, arithmetic and copies ran while one was open for 0% of the time, Pallas kernels for 10%

profile of v5, /device:TPU:0, one launch (start us, length us, event | category | flops | bytes accessed | tf_op | source)
XLA Modules:
  0.0 428.5 jit_solution(15625998361782017355)
XLA Ops:
  0.0 1.2 copy-done.8
  1.2 0.7 copy-done.9
  1.9 0.7 copy-done.10
  2.5 223.5 %shard_map.64 = (bf16[128,3712]{1,0:T(8,128)(2,1)S(1)}, bf16[128,80]{1,0:T(8,128)(2,1)S(1)}, bf16[128,80]{1,0:T(8,128)(2,1)S(1)}, bf16[80,3712]{1,0:T(8,128)(2,1...) custom-call(bf16[128,3584]{1,0:T(8,128)(2,1)S(1)} %copy-done.8, s32[2,128]{1,0:T(2,128)S(1)} %bitcast.5, ...), custom_call_target="tpu_custom_call" | custom-call | tf_op jit(solution)/shard_map/pallas_call | solution.py:34
  226.0 0.5 collective-permute-start.1
  226.5 0.1 collective-permute-start.2
  226.6 5.0 %collective-permute-start.3 = (bf16[128,3712]{1,0:T(8,128)(2,1)S(1)}, bf16[128,3712]{1,0:T(8,128)(2,1)S(1)}, u32[]{:S(2)}, u32[]{:S(2)}) collective-permute-start(bf16[128,3712]{1,0:T(8,128)(2,1)S(1)} %get-tuple-element.38), channel_id=1, source_target_pairs={{0,4},{2,6},{4,8},{6,10},{8,12},{10,14},{1,5},{3,7},{5,9},{7,11},{... | collective-permute-start | bytes 2850824 | tf_op jit(solution)/shard_map/ppermute | solution.py:207
  231.6 1.3 collective-permute-start.4
  232.9 1.6 collective-permute-start
  234.5 13.6 %collective-permute-done.refs_2_.refs_1_ = bf16[80,3712]{1,0:T(8,128)(2,1)S(1)} collective-permute-done((bf16[80,3712]{1,0:T(8,128)(2,1)S(1)}, bf16[80,3712]{1,0:T(8,128)(2,1)S(1)}, u32[]{:S(2)}, u32[]{:S(2)}) %collective-permute-start) | collective-permute-done | bytes 593952 | tf_op jit(solution)/shard_map/ppermute | solution.py:210
  248.1 4.0 collective-permute-done.3.refs_0_
  252.1 4.2 collective-permute-done.4.refs_1_
  256.2 0.0 copy-done.6
  256.2 0.0 copy-done
  256.2 0.9 copy-done.3
  257.2 1.3 collective-permute-start.6
  258.5 0.7 collective-permute-start.7
  259.2 1.2 copy-done.1
  260.4 1.2 copy-done.4
  261.6 1.0 shard_map.66
  262.6 1.6 collective-permute-start.8
  264.2 0.0 collective-permute-done.2.refs_5_
  264.2 0.0 collective-permute-done.1.refs_3_
  264.2 0.0 copy-done.7
  264.2 9.2 %shard_map.67 = (bf16[80,3584]{1,0:T(8,128)(2,1)S(1)}, bf16[80,3584]{1,0:T(8,128)(2,1)S(1)}) custom-call(bf16[80,3712]{1,0:T(8,128)(2,1)S(1)} %get-tuple-element.35.refs_0_, bf16[80,3712]{1,0:T(8,128)(2,1)S(1)} %copy-done.7, bf16[2,3584,512]{2,1,0:T(8,128)(2,1)} %get-tuple-element.37.refs_2_, bf16[2,3584,512]{2,1,0:T(8,128)(2,1)} %collective-permute-done.1.refs_3_, ...), custom_call_target="tpu_custom_call" | custom-call | tf_op jit(solution)/shard_map/pallas_call | solution.py:34
  273.4 0.6 collective-permute-start.5
  274.0 7.1 %collective-permute-done.6.refs_0_ = bf16[128,3712]{1,0:T(8,128)(2,1)S(1)} collective-permute-done((bf16[128,3712]{1,0:T(8,128)(2,1)}, bf16[128,3712]{1,0:T(8,128)(2,1)S(1)}, u32[]{:S(2)}, u32[]{:S(2)}) %collective-permute-start.6) | collective-permute-done | bytes 950304 | tf_op jit(solution)/shard_map/ppermute | solution.py:207
  281.2 1.3 collective-permute-start.14
  282.4 0.0 collective-permute-done.7.refs_1_
  282.5 0.7 collective-permute-start.15
  283.2 0.0 collective-permute-done.8.refs_1_
  283.2 9.2 %shard_map.68 = (bf16[80,3584]{1,0:T(8,128)(2,1)S(1)}, bf16[80,3584]{1,0:T(8,128)(2,1)S(1)}) custom-call(bf16[80,3712]{1,0:T(8,128)(2,1)S(1)} %get-tuple-element.44.refs_0_, bf16[80,3712]{1,0:T(8,128)(2,1)S(1)} %collective-permute-done.8.refs_1_, bf16[2,3584,512]{2,1,0:T(8,128)(2,1)} %get-tuple-element.37.refs_2_, ...), custom_call_target="tpu_custom_call" | custom-call | tf_op jit(solution)/shard_map/pallas_call | solution.py:34
  292.4 1.6 collective-permute-start.9
  294.0 0.0 collective-permute-done.5.refs_3_
  294.0 1.2 shard_map.69
  295.2 0.6 collective-permute-start.12
  295.8 0.6 shard_map.70.refs_4_
  296.4 12.0 %collective-permute-done.9.refs_3_ = bf16[80,3584]{1,0:T(8,128)(2,1)S(1)} collective-permute-done((bf16[80,3584]{1,0:T(8,128)(2,1)S(1)}, bf16[80,3584]{1,0:T(8,128)(2,1)S(1)}, u32[]{:S(2)}, u32[]{:S(2)}) %collective-permute-start.9) | collective-permute-done | bytes 573472 | tf_op jit(solution)/shard_map/ppermute | solution.py:210
  308.4 0.6 shard_map.71.refs_6_
  309.0 0.7 collective-permute-start.10
  309.7 5.2 %collective-permute-start.11 = (bf16[128,3584]{1,0:T(8,128)(2,1)S(1)}, bf16[128,3584]{1,0:T(8,128)(2,1)S(1)}, u32[]{:S(2)}, u32[]{:S(2)}) collective-permute-start(bf16[128,3584]{1,0:T(8,128)(2,1)S(1)} %shard_map.71.refs_6_), channel_id=1, source_target_pairs={{0,4},{2,6},{4,8},{6,10},{1,5},{3,7},{5,9},{7,11},{16,20},{18,22},... | collective-permute-start | bytes 2752520 | tf_op jit(solution)/shard_map/ppermute | solution.py:207
  315.0 3.1 collective-permute-done.12.refs_1_
  318.1 9.6 %shard_map.72 = (bf16[80,3584]{1,0:T(8,128)(2,1)S(1)}, bf16[80,3584]{1,0:T(8,128)(2,1)S(1)}) custom-call(bf16[80,3712]{1,0:T(8,128)(2,1)S(1)} %get-tuple-element.51.refs_0_, bf16[80,3712]{1,0:T(8,128)(2,1)S(1)} %collective-permute-done.12.refs_1_, bf16[2,3584,512]{2,1,0:T(8,128)(2,1)} %get-tuple-element.37.refs_2_, ...), custom_call_target="tpu_custom_call" | custom-call | tf_op jit(solution)/shard_map/pallas_call | solution.py:34
  327.7 0.0 collective-permute-done.14.refs_1_
  327.7 0.0 collective-permute-done.15.refs_3_
  327.7 1.3 shard_map.73
  329.0 1.6 collective-permute-start.16
  330.6 0.5 collective-permute-start.13
  331.1 0.0 collective-permute-done.10.refs_7_
  331.1 0.0 collective-permute-done.11.refs_8_
  331.1 14.3 %collective-permute-done.16.refs_1_ = bf16[80,3712]{1,0:T(8,128)(2,1)S(1)} collective-permute-done((bf16[80,3712]{1,0:T(8,128)(2,1)S(1)}, bf16[80,3712]{1,0:T(8,128)(2,1)S(1)}, u32[]{:S(2)}, u32[]{:S(2)}) %collective-permute-start.16) | collective-permute-done | bytes 593952 | tf_op jit(solution)/shard_map/ppermute | solution.py:210
  345.4 9.2 %shard_map.74 = (bf16[80,3584]{1,0:T(8,128)(2,1)S(1)}, bf16[80,3584]{1,0:T(8,128)(2,1)S(1)}) custom-call(bf16[80,3712]{1,0:T(8,128)(2,1)S(1)} %get-tuple-element.55.refs_0_, bf16[80,3712]{1,0:T(8,128)(2,1)S(1)} %collective-permute-done.16.refs_1_, bf16[2,3584,512]{2,1,0:T(8,128)(2,1)} %get-tuple-element.37.refs_2_, ...), custom_call_target="tpu_custom_call" | custom-call | tf_op jit(solution)/shard_map/pallas_call | solution.py:34
  354.7 1.6 collective-permute-start.18
  356.3 1.5 collective-permute-done.13.refs_3_
  357.7 0.6 shard_map.75.refs_4_
  358.3 4.7 %collective-permute-start.17 = (bf16[128,3584]{1,0:T(8,128)(2,1)S(1)}, bf16[128,3584]{1,0:T(8,128)(2,1)S(1)}, u32[]{:S(2)}, u32[]{:S(2)}) collective-permute-start(bf16[128,3584]{1,0:T(8,128)(2,1)S(1)} %shard_map.75.refs_4_), channel_id=1, source_target_pairs={{0,8},{2,10},{4,12},{6,14},{8,0},{10,2},{12,4},{14,6},{1,9},{3,11}... | collective-permute-start | bytes 2752520 | tf_op jit(solution)/shard_map/ppermute | solution.py:207
  363.0 3.0 collective-permute-done.18.refs_3_
  366.1 0.6 shard_map.76
  366.7 1.3 collective-permute-start.19
  368.0 6.3 %collective-permute-start.20 = (bf16[128,3584]{1,0:T(8,128)(2,1)S(1)}, bf16[128,3584]{1,0:T(8,128)(2,1)S(1)}, u32[]{:S(2)}, u32[]{:S(2)}) collective-permute-start(bf16[128,3584]{1,0:T(8,128)(2,1)S(1)} %shard_map.76), channel_id=1, source_target_pairs={{0,12},{2,14},{4,0},{6,2},{1,13},{3,15},{5,1},{7,3},{16,28},{18,30... | collective-permute-start | bytes 2752520 | tf_op jit(solution)/shard_map/ppermute | solution.py:207
  374.3 40.2 %collective-permute-done.17 = bf16[128,3584]{1,0:T(8,128)(2,1)S(1)} collective-permute-done((bf16[128,3584]{1,0:T(8,128)(2,1)S(1)}, bf16[128,3584]{1,0:T(8,128)(2,1)S(1)}, u32[]{:S(2)}, u32[]{:S(2)}) %collective-permute-start.17) | collective-permute-done | bytes 917536 | tf_op jit(solution)/shard_map/ppermute | solution.py:207
  414.5 0.0 collective-permute-done.19
  414.5 12.4 %collective-permute-done.20 = bf16[128,3584]{1,0:T(8,128)(2,1)S(1)} collective-permute-done((bf16[128,3584]{1,0:T(8,128)(2,1)S(1)}, bf16[128,3584]{1,0:T(8,128)(2,1)S(1)}, u32[]{:S(2)}, u32[]{:S(2)}) %collective-permute-start.20) | collective-permute-done | bytes 917536 | tf_op jit(solution)/shard_map/ppermute | solution.py:207
  426.9 1.6 add_convert_fusion
  (14 shorter events, 0.0 us)
Async XLA Ops:
  0.0 1.2 copy-start.8
  1.2 0.7 copy-start.9
  1.9 0.7 copy-start.10
  226.0 38.2 %collective-permute-start.1 = (bf16[2,3584,512]{2,1,0:T(8,128)(2,1)}, bf16[2,3584,512]{2,1,0:T(8,128)(2,1)}, u32[]{:S(2)}, u32[]{:S(2)}) collective-permute-start(bf16[2,3584,512]{2,1,0:T(8,128)(2,1)} %get-tuple-element.37.refs_2_), channel_id=1, source_target_pairs={{0,1},{1,0},{2,3},{3,2},{4,5},{5,4},{6,7},{7,6},{8,9},{9,8},{10,11... | collective-permute-start | bytes 22020104 | tf_op jit(solution)/shard_map/ppermute | solution.py:203
  226.5 37.7 %collective-permute-start.2 = (bf16[512,3584]{1,0:T(8,128)(2,1)}, bf16[512,3584]{1,0:T(8,128)(2,1)}, u32[]{:S(2)}, u32[]{:S(2)}) collective-permute-start(bf16[512,3584]{1,0:T(8,128)(2,1)} %bitcast.4.refs_4_), channel_id=1, source_target_pairs={{0,1},{1,0},{2,3},{3,2},{4,5},{5,4},{6,7},{7,6},{8,9},{9,8},{10,11... | collective-permute-start | bytes 11010056 | tf_op jit(solution)/shard_map/ppermute | solution.py:203
  226.6 25.4 %collective-permute-start.3 = (bf16[128,3712]{1,0:T(8,128)(2,1)S(1)}, bf16[128,3712]{1,0:T(8,128)(2,1)S(1)}, u32[]{:S(2)}, u32[]{:S(2)}) collective-permute-start(bf16[128,3712]{1,0:T(8,128)(2,1)S(1)} %get-tuple-element.38), channel_id=1, source_target_pairs={{0,4},{2,6},{4,8},{6,10},{8,12},{10,14},{1,5},{3,7},{5,9},{7,11},{... | collective-permute-start | bytes 2850824 | tf_op jit(solution)/shard_map/ppermute | solution.py:207
  231.6 24.7 %collective-permute-start.4 = (bf16[128,3712]{1,0:T(8,128)(2,1)S(1)}, bf16[128,3712]{1,0:T(8,128)(2,1)S(1)}, u32[]{:S(2)}, u32[]{:S(2)}) collective-permute-start(bf16[128,3712]{1,0:T(8,128)(2,1)S(1)} %get-tuple-element.38), channel_id=1, source_target_pairs={{4,0},{6,2},{8,4},{10,6},{12,8},{14,10},{5,1},{7,3},{9,5},{11,7},{... | collective-permute-start | bytes 2850824 | tf_op jit(solution)/shard_map/ppermute | solution.py:207
  232.9 15.2 %collective-permute-start = (bf16[80,3712]{1,0:T(8,128)(2,1)S(1)}, bf16[80,3712]{1,0:T(8,128)(2,1)S(1)}, u32[]{:S(2)}, u32[]{:S(2)}) collective-permute-start(bf16[80,3712]{1,0:T(8,128)(2,1)S(1)} %get-tuple-element.36), channel_id=1, source_target_pairs={{0,2},{2,0},{4,6},{6,4},{8,10},{10,8},{12,14},{14,12},{1,3},{3,1},... | collective-permute-start | bytes 1781768 | tf_op jit(solution)/shard_map/ppermute | solution.py:210
  248.1 8.2 %copy-start.6 = (bf16[80,3712]{1,0:T(8,128)(2,1)}, bf16[80,3712]{1,0:T(8,128)(2,1)S(1)}, u32[]{:S(2)}) copy-start(bf16[80,3712]{1,0:T(8,128)(2,1)S(1)} %collective-permute-done.refs_2_.refs_1_) | copy-start | bytes 1781764
  252.1 4.2 copy-start
  256.2 1.0 copy-start.3
  257.2 24.0 %collective-permute-start.6 = (bf16[128,3712]{1,0:T(8,128)(2,1)}, bf16[128,3712]{1,0:T(8,128)(2,1)S(1)}, u32[]{:S(2)}, u32[]{:S(2)}) collective-permute-start(bf16[128,3712]{1,0:T(8,128)(2,1)} %get-tuple-element.39.refs_0_), channel_id=1, source_target_pairs={{4,0},{6,2},{8,4},{10,6},{5,1},{7,3},{9,5},{11,7},{20,16},{22,18},... | collective-permute-start | bytes 2850824 | tf_op jit(solution)/shard_map/ppermute | solution.py:207
  258.5 24.0 %collective-permute-start.7 = (bf16[128,3712]{1,0:T(8,128)(2,1)}, bf16[128,3712]{1,0:T(8,128)(2,1)S(1)}, u32[]{:S(2)}, u32[]{:S(2)}) collective-permute-start(bf16[128,3712]{1,0:T(8,128)(2,1)} %get-tuple-element.40.refs_1_.refs_2_), channel_id=1, source_target_pairs={{4,8},{6,10},{8,12},{10,14},{5,9},{7,11},{9,13},{11,15},{20,24},{2... | collective-permute-start | bytes 2850824 | tf_op jit(solution)/shard_map/ppermute | solution.py:207
  259.2 1.2 copy-start.1
  260.4 1.2 copy-start.4
  261.6 2.6 copy-start.7
  262.6 20.6 %collective-permute-start.8 = (bf16[80,3712]{1,0:T(8,128)(2,1)S(1)}, bf16[80,3712]{1,0:T(8,128)(2,1)S(1)}, u32[]{:S(2)}, u32[]{:S(2)}) collective-permute-start(bf16[80,3712]{1,0:T(8,128)(2,1)S(1)} %get-tuple-element.45), channel_id=1, source_target_pairs={{0,2},{2,0},{4,6},{6,4},{8,10},{10,8},{12,14},{14,12},{1,3},{3,1},... | collective-permute-start | bytes 1781768 | tf_op jit(solution)/shard_map/ppermute | solution.py:210
  273.4 20.6 %collective-permute-start.5 = (bf16[80,3584]{1,0:T(8,128)(2,1)S(1)}, bf16[80,3584]{1,0:T(8,128)(2,1)S(1)}, u32[]{:S(2)}, u32[]{:S(2)}) collective-permute-start(bf16[80,3584]{1,0:T(8,128)(2,1)S(1)} %get-tuple-element.43), channel_id=1, source_target_pairs={{0,2},{2,0},{4,6},{6,4},{8,10},{10,8},{12,14},{14,12},{1,3},{3,1},... | collective-permute-start | bytes 1720328 | tf_op jit(solution)/shard_map/ppermute | solution.py:210
  281.2 46.5 %collective-permute-start.14 = (bf16[128,3712]{1,0:T(8,128)(2,1)S(1)}, bf16[128,3712]{1,0:T(8,128)(2,1)S(1)}, u32[]{:S(2)}, u32[]{:S(2)}) collective-permute-start(bf16[128,3712]{1,0:T(8,128)(2,1)S(1)} %collective-permute-done.6.refs_0_), channel_id=1, source_target_pairs={{4,0},{6,2},{5,1},{7,3},{20,16},{22,18},{21,17},{23,19}} | collective-permute-start | bytes 2850824 | tf_op jit(solution)/shard_map/ppermute | solution.py:207
  282.5 45.3 %collective-permute-start.15 = (bf16[128,3712]{1,0:T(8,128)(2,1)S(1)}, bf16[128,3712]{1,0:T(8,128)(2,1)S(1)}, u32[]{:S(2)}, u32[]{:S(2)}) collective-permute-start(bf16[128,3712]{1,0:T(8,128)(2,1)S(1)} %collective-permute-done.7.refs_1_), channel_id=1, source_target_pairs={{8,12},{10,14},{9,13},{11,15},{24,28},{26,30},{25,29},{27,31}} | collective-permute-start | bytes 2850824 | tf_op jit(solution)/shard_map/ppermute | solution.py:207
  292.4 16.0 %collective-permute-start.9 = (bf16[80,3584]{1,0:T(8,128)(2,1)S(1)}, bf16[80,3584]{1,0:T(8,128)(2,1)S(1)}, u32[]{:S(2)}, u32[]{:S(2)}) collective-permute-start(bf16[80,3584]{1,0:T(8,128)(2,1)S(1)} %get-tuple-element.49), channel_id=1, source_target_pairs={{0,2},{2,0},{4,6},{6,4},{8,10},{10,8},{12,14},{14,12},{1,3},{3,1},... | collective-permute-start | bytes 1720328 | tf_op jit(solution)/shard_map/ppermute | solution.py:210
  295.2 22.9 %collective-permute-start.12 = (bf16[80,3712]{1,0:T(8,128)(2,1)S(1)}, bf16[80,3712]{1,0:T(8,128)(2,1)S(1)}, u32[]{:S(2)}, u32[]{:S(2)}) collective-permute-start(bf16[80,3712]{1,0:T(8,128)(2,1)S(1)} %get-tuple-element.52), channel_id=1, source_target_pairs={{0,2},{2,0},{4,6},{6,4},{8,10},{10,8},{12,14},{14,12},{1,3},{3,1},... | collective-permute-start | bytes 1781768 | tf_op jit(solution)/shard_map/ppermute | solution.py:210
  309.0 22.1 %collective-permute-start.10 = (bf16[128,3584]{1,0:T(8,128)(2,1)S(1)}, bf16[128,3584]{1,0:T(8,128)(2,1)S(1)}, u32[]{:S(2)}, u32[]{:S(2)}) collective-permute-start(bf16[128,3584]{1,0:T(8,128)(2,1)S(1)} %shard_map.71.refs_6_), channel_id=1, source_target_pairs={{8,4},{10,6},{12,8},{14,10},{9,5},{11,7},{13,9},{15,11},{24,20},{2... | collective-permute-start | bytes 2752520 | tf_op jit(solution)/shard_map/ppermute | solution.py:207
  309.7 21.4 %collective-permute-start.11 = (bf16[128,3584]{1,0:T(8,128)(2,1)S(1)}, bf16[128,3584]{1,0:T(8,128)(2,1)S(1)}, u32[]{:S(2)}, u32[]{:S(2)}) collective-permute-start(bf16[128,3584]{1,0:T(8,128)(2,1)S(1)} %shard_map.71.refs_6_), channel_id=1, source_target_pairs={{0,4},{2,6},{4,8},{6,10},{1,5},{3,7},{5,9},{7,11},{16,20},{18,22},... | collective-permute-start | bytes 2752520 | tf_op jit(solution)/shard_map/ppermute | solution.py:207
  318.1 9.6 %copy-start.2 = (bf16[128,3712]{1,0:T(8,128)(2,1)S(1)}, bf16[128,3712]{1,0:T(8,128)(2,1)}, u32[]{:S(2)}) copy-start(bf16[128,3712]{1,0:T(8,128)(2,1)} %get-tuple-element.40.refs_1_.refs_2_) | copy-start | bytes 2850820
  318.1 9.6 %copy-start.5 = (bf16[128,3712]{1,0:T(8,128)(2,1)S(1)}, bf16[128,3712]{1,0:T(8,128)(2,1)}, u32[]{:S(2)}) copy-start(bf16[128,3712]{1,0:T(8,128)(2,1)} %get-tuple-element.39.refs_0_) | copy-start | bytes 2850820
  329.0 16.4 %collective-permute-start.16 = (bf16[80,3712]{1,0:T(8,128)(2,1)S(1)}, bf16[80,3712]{1,0:T(8,128)(2,1)S(1)}, u32[]{:S(2)}, u32[]{:S(2)}) collective-permute-start(bf16[80,3712]{1,0:T(8,128)(2,1)S(1)} %get-tuple-element.56), channel_id=1, source_target_pairs={{0,2},{2,0},{4,6},{6,4},{8,10},{10,8},{12,14},{14,12},{1,3},{3,1},... | collective-permute-start | bytes 1781768 | tf_op jit(solution)/shard_map/ppermute | solution.py:210
  330.6 27.1 %collective-permute-start.13 = (bf16[80,3584]{1,0:T(8,128)(2,1)S(1)}, bf16[80,3584]{1,0:T(8,128)(2,1)S(1)}, u32[]{:S(2)}, u32[]{:S(2)}) collective-permute-start(bf16[80,3584]{1,0:T(8,128)(2,1)S(1)} %get-tuple-element.54), channel_id=1, source_target_pairs={{0,2},{2,0},{4,6},{6,4},{8,10},{10,8},{12,14},{14,12},{1,3},{3,1},... | collective-permute-start | bytes 1720328 | tf_op jit(solution)/shard_map/ppermute | solution.py:210
  354.7 11.4 %collective-permute-start.18 = (bf16[80,3584]{1,0:T(8,128)(2,1)S(1)}, bf16[80,3584]{1,0:T(8,128)(2,1)S(1)}, u32[]{:S(2)}, u32[]{:S(2)}) collective-permute-start(bf16[80,3584]{1,0:T(8,128)(2,1)S(1)} %get-tuple-element.60), channel_id=1, source_target_pairs={{0,2},{2,0},{4,6},{6,4},{8,10},{10,8},{12,14},{14,12},{1,3},{3,1},... | collective-permute-start | bytes 1720328 | tf_op jit(solution)/shard_map/ppermute | solution.py:210
  358.3 56.1 %collective-permute-start.17 = (bf16[128,3584]{1,0:T(8,128)(2,1)S(1)}, bf16[128,3584]{1,0:T(8,128)(2,1)S(1)}, u32[]{:S(2)}, u32[]{:S(2)}) collective-permute-start(bf16[128,3584]{1,0:T(8,128)(2,1)S(1)} %shard_map.75.refs_4_), channel_id=1, source_target_pairs={{0,8},{2,10},{4,12},{6,14},{8,0},{10,2},{12,4},{14,6},{1,9},{3,11}... | collective-permute-start | bytes 2752520 | tf_op jit(solution)/shard_map/ppermute | solution.py:207
  366.7 47.8 %collective-permute-start.19 = (bf16[128,3584]{1,0:T(8,128)(2,1)S(1)}, bf16[128,3584]{1,0:T(8,128)(2,1)S(1)}, u32[]{:S(2)}, u32[]{:S(2)}) collective-permute-start(bf16[128,3584]{1,0:T(8,128)(2,1)S(1)} %shard_map.76), channel_id=1, source_target_pairs={{8,12},{10,14},{12,0},{14,2},{9,13},{11,15},{13,1},{15,3},{24,28},... | collective-permute-start | bytes 2752520 | tf_op jit(solution)/shard_map/ppermute | solution.py:207
  368.0 58.9 %collective-permute-start.20 = (bf16[128,3584]{1,0:T(8,128)(2,1)S(1)}, bf16[128,3584]{1,0:T(8,128)(2,1)S(1)}, u32[]{:S(2)}, u32[]{:S(2)}) collective-permute-start(bf16[128,3584]{1,0:T(8,128)(2,1)S(1)} %shard_map.76), channel_id=1, source_target_pairs={{0,12},{2,14},{4,0},{6,2},{1,13},{3,15},{5,1},{7,3},{16,28},{18,30... | collective-permute-start | bytes 2752520 | tf_op jit(solution)/shard_map/ppermute | solution.py:207

commit v6 on v5

--- a/solution.py
+++ b/solution.py
@@ -8,7 +8,6 @@
 from jax.sharding import PartitionSpec as P
 
 ANYWHERE = pl.BlockSpec(memory_space=pl.ANY)
-IN_HBM = pl.BlockSpec(memory_space=pltpu.HBM)
 IN_VMEM = pl.BlockSpec(memory_space=pltpu.VMEM)
 MIB = 1024 * 1024
 
@@ -22,7 +21,7 @@
     return plan
 
 
-def call(kernel, outs, ins, after=(), scratch=(), specs=None, vmem=24, out_specs=None):
+def call(kernel, outs, ins, after=(), scratch=(), specs=None, vmem=16, out_specs=None):
     body = kernel
     if after:
         first, last = len(ins), len(ins) + len(after)
@@ -42,6 +41,10 @@
     )(*ins, *after)
 
 
+def in_vmem(array):
+    return pltpu.with_memory_space_constraint(array, pltpu.VMEM)
+
+
 def tied(arrays, after):
     return pl.pallas_call(
         lambda *refs: None,
@@ -50,7 +53,7 @@
         out_specs=[ANYWHERE] * len(arrays),
         input_output_aliases={k: k for k in range(len(arrays))},
         cost_estimate=pl.CostEstimate(flops=0, bytes_accessed=0, transcendentals=0),
-    )(*arrays, *after)
+    )(*[in_vmem(a) for a in arrays], *after)
 
 
 def first_kernel(experts, tokens, routes, scale, gate_w, up_w, block, *refs):
@@ -191,13 +194,13 @@
             bf16((count, cap)),
             bf16((cap, wide)),
             bf16((cap, wide)),
-            pltpu.HBM((2, width, hidden), jnp.bfloat16),
+            bf16((2, width, hidden)),
         ],
         [tokens, routes.T, route_scale.T, in_hbm(w_gate[0]), in_hbm(w_up[0])],
         (),
         [pltpu.SemaphoreType.DMA((2,))],
         [IN_VMEM] * 3 + [ANYWHERE] * 2,
-        out_specs=[IN_VMEM] * 5 + [IN_HBM],
+        out_specs=[IN_VMEM] * 6,
     )
     swap = functools.partial(lax.ppermute, axis_name="local", perm=[(0, 1), (1, 0)])
     weights = [in_hbm(stack), swap(stack), in_hbm(w_down[0]), swap(w_down[0])]
@@ -235,7 +238,7 @@
                 pltpu.SemaphoreType.DMA((tiles, 3)),
             ],
             [IN_VMEM] * 2 + [ANYWHERE] * 4,
-            36,
+            32,
         )
 
     def spread(maps, own_out, other_out, extras=(), after=()):
@@ -261,6 +264,9 @@
                 if 0 <= a + way < places and 0 <= a - way * (step - 1) < places
             ]
             held[way, step] = along(held.get((way, step - 1), block), pairs)
+
+    def hold(step, until):
+        held[1, step], held[-1, step] = tied([held[1, step], held[-1, step]], until)
 
     def do_pick(slot, after=()):
         keys = sorted({row[slot - 1] for row in plan})
@@ -285,22 +291,23 @@
 
     relay(1)
     picks[0] = picked[:2], picked[2], across(picked[3])
-    held[1, 1], held[-1, 1] = tied([held[1, 1], held[-1, 1]], [picks[0][2]])
-    for step in range(2, places):
-        relay(step)
+    hold(1, [picks[0][2]])
+    relay(2)
     do_pick(1)
     do_expert(0)
-    do_expert(1)
-    do_pick(2, after=[outs[0][1]])
-    total = ordered(spread, picks[0][0], *outs[0])
-    do_spread(1)
-    for slot in range(2, places):
-        do_expert(slot, after=returned[slot - 3] if slot > 2 else ())
-        if slot + 1 < places:
-            do_pick(slot + 1)
-        if slot > 2:
-            do_spread(slot - 1)
-    do_spread(places - 1)
+    hold(2, [picks[1][2], outs[0][0]])
+    for step in range(3, places):
+        relay(step)
+    do_pick(2)
+    do_expert(1, after=[outs[0][1]])
+    total = ordered(spread, picks[0][0], *outs[0], after=[picks[2][2]])
+    do_expert(2)
+    for slot in range(3, places):
+        do_pick(slot)
+        do_spread(slot - 2)
+        do_expert(slot)
+        do_spread(slot - 1)
+    do_spread(places - 1, after=returned[0])
     total = total.astype(jnp.float32)
     for block in sum(returned, []):
         total = total + block.astype(jnp.float32)

time: 429 us -> 205 us (0.48)
  Pallas kernels: 267 us -> 49.4 us
  waiting for transfers between devices: 115 us -> 105 us
  local copies, waits for them, and re-layouts: 5.88 us -> 11.2 us
    pallas_call x12, Pallas kernels: 267 us -> 49.4 us  [call(): pl.pallas_call(body, out_shape=outs, in_specs=specs, out_specs=out_specs...]
    unnamed x22 -> x40, local copies, waits for them, and re-layouts: 5.88 us -> 11.2 us
    ppermute x8, waiting for transfers between devices: 47.5 us -> 42.5 us  [across(): return lax.ppermute(block, 'node', [(n, n ^ 1) for n in range(experts)])]
    ppermute x11, waiting for transfers between devices: 67.9 us -> 62.9 us  [along(): return lax.ppermute(block, 'node', moves)]
  transfers between devices with their start and end apart: 21 -> 21, of which waited for: 11 -> 12; matrix products, arithmetic and copies ran while one was open for 0% -> 0% of each run, Pallas kernels for 10% -> 21%
where the time goes in v6:
time: 205 us
  waiting for transfers between devices  105 us (51%)
  Pallas kernels  49.4 us (24%)
  starting transfers between devices  36.9 us (18%)
  local copies, waits for them, and re-layouts  11.2 us (5%)
    ppermute x11, waiting for transfers between devices, along(): return lax.ppermute(block, 'node', moves)  62.9 us
    pallas_call x12, Pallas kernels, call(): pl.pallas_call(body, out_shape=outs, in_specs=specs, out_specs=out_specs...  49.4 us
    ppermute x8, waiting for transfers between devices, across(): return lax.ppermute(block, 'node', [(n, n ^ 1) for n in range(experts)])  42.5 us
    ppermute x11, starting transfers between devices, along(): return lax.ppermute(block, 'node', moves)  25.8 us
    unnamed x40, local copies, waits for them, and re-layouts  11.2 us
    ppermute x8, starting transfers between devices, across(): return lax.ppermute(block, 'node', [(n, n ^ 1) for n in range(experts)])  10.6 us
  transfers between devices with their start and end apart: 21, of which 12 were waited for; matrix products, arithmetic and copies ran while one was open for 0% of the time, Pallas kernels for 21%

profile of v6, /device:TPU:0, one launch (start us, length us, event | category | flops | bytes accessed | tf_op | source)
XLA Modules:
  0.0 204.8 jit_solution(2508245733335445090)
XLA Ops:
  0.0 1.2 copy-done.12
  1.2 0.7 copy-done.17
  1.9 0.7 copy-done.18
  2.5 6.7 %shard_map.64 = (bf16[128,3712]{1,0:T(8,128)(2,1)S(1)}, bf16[128,80]{1,0:T(8,128)(2,1)S(1)}, bf16[128,80]{1,0:T(8,128)(2,1)S(1)}, bf16[80,3712]{1,0:T(8,128)(2,1...) custom-call(bf16[128,3584]{1,0:T(8,128)(2,1)S(1)} %copy-done.12, s32[2,128]{1,0:T(2,128)S(1)} %bitcast.5, ...), custom_call_target="tpu_custom_call" | custom-call | tf_op jit(solution)/shard_map/pallas_call | solution.py:33
  9.3 0.8 copy-done.15
  10.1 0.5 collective-permute-start.1
  10.6 0.1 collective-permute-start.2
  10.6 5.0 %collective-permute-start.3 = (bf16[128,3712]{1,0:T(8,128)(2,1)S(1)}, bf16[128,3712]{1,0:T(8,128)(2,1)S(1)}, u32[]{:S(2)}, u32[]{:S(2)}) collective-permute-start(bf16[128,3712]{1,0:T(8,128)(2,1)S(1)} %get-tuple-element.40), channel_id=1, source_target_pairs={{0,4},{2,6},{4,8},{6,10},{8,12},{10,14},{1,5},{3,7},{5,9},{7,11},{... | collective-permute-start | bytes 2850824 | tf_op jit(solution)/shard_map/ppermute | solution.py:210
  15.6 1.3 collective-permute-start.4
  16.9 1.6 collective-permute-start
  18.5 13.5 %collective-permute-done.refs_2_.refs_1_ = bf16[80,3712]{1,0:T(8,128)(2,1)S(1)} collective-permute-done((bf16[80,3712]{1,0:T(8,128)(2,1)S(1)}, bf16[80,3712]{1,0:T(8,128)(2,1)S(1)}, u32[]{:S(2)}, u32[]{:S(2)}) %collective-permute-start) | collective-permute-done | bytes 593952 | tf_op jit(solution)/shard_map/ppermute | solution.py:213
  32.0 4.0 %collective-permute-done.3.refs_0_ = bf16[128,3712]{1,0:T(8,128)(2,1)S(1)} collective-permute-done((bf16[128,3712]{1,0:T(8,128)(2,1)S(1)}, bf16[128,3712]{1,0:T(8,128)(2,1)S(1)}, u32[]{:S(2)}, u32[]{:S(2)}) %collective-permute-start.3) | collective-permute-done | bytes 950304 | tf_op jit(solution)/shard_map/ppermute | solution.py:210
  36.0 4.2 %collective-permute-done.4.refs_1_ = bf16[128,3712]{1,0:T(8,128)(2,1)S(1)} collective-permute-done((bf16[128,3712]{1,0:T(8,128)(2,1)S(1)}, bf16[128,3712]{1,0:T(8,128)(2,1)S(1)}, u32[]{:S(2)}, u32[]{:S(2)}) %collective-permute-start.4) | collective-permute-done | bytes 950304 | tf_op jit(solution)/shard_map/ppermute | solution.py:210
  40.2 0.9 collective-permute-start.7
  41.0 1.3 collective-permute-start.8
  42.3 1.0 shard_map.66
  43.4 0.8 copy-done.13
  44.2 1.5 collective-permute-start.6
  45.7 0.0 collective-permute-done.2.refs_5_
  45.7 0.0 collective-permute-done.1.refs_3_
  45.8 1.1 copy-done.16
  46.8 9.2 %shard_map.67 = (bf16[80,3584]{1,0:T(8,128)(2,1)S(1)}, bf16[80,3584]{1,0:T(8,128)(2,1)S(1)}) custom-call(bf16[80,3712]{1,0:T(8,128)(2,1)S(1)} %copy-done.16, bf16[80,3712]{1,0:T(8,128)(2,1)S(1)} %copy-done.11, bf16[2,3584,512]{2,1,0:T(8,128)(2,1)} %get-tuple-element.39.refs_2_, bf16[2,3584,512]{2,1,0:T(8,128)(2,1)} %collective-permute-done.1.refs_3_, ...), custom_call_target="tpu_custom_call" | custom-call | tf_op jit(solution)/shard_map/pallas_call | solution.py:33
  56.1 0.8 copy-done.2
  56.9 0.8 copy-done.19
  57.7 0.7 collective-permute-done.6.refs_2_.refs_1_
  58.4 0.0 collective-permute-done.7.refs_0_
  58.4 1.0 copy-done.4
  59.4 7.7 %collective-permute-done.8.refs_1_ = bf16[128,3712]{1,0:T(8,128)(2,1)S(1)} collective-permute-done((bf16[128,3712]{1,0:T(8,128)(2,1)S(1)}, bf16[128,3712]{1,0:T(8,128)(2,1)S(1)}, u32[]{:S(2)}, u32[]{:S(2)}) %collective-permute-start.8) | collective-permute-done | bytes 950304 | tf_op jit(solution)/shard_map/ppermute | solution.py:210
  67.1 0.9 copy-done.6
  68.0 1.2 copy-done.5
  69.2 1.2 copy-done.7
  70.4 1.4 collective-permute-start.11
  71.8 0.7 collective-permute-start.12
  72.5 1.6 collective-permute-start.5
  74.1 1.2 shard_map.69
  75.3 0.6 collective-permute-start.9
  75.9 12.8 %collective-permute-done.5.refs_7_.refs_3_ = bf16[80,3584]{1,0:T(8,128)(2,1)S(1)} collective-permute-done((bf16[80,3584]{1,0:T(8,128)(2,1)}, bf16[80,3584]{1,0:T(8,128)(2,1)S(1)}, u32[]{:S(2)}, u32[]{:S(2)}) %collective-permute-start.5) | collective-permute-done | bytes 573472 | tf_op jit(solution)/shard_map/ppermute | solution.py:213
  88.7 9.2 %shard_map.70 = (bf16[80,3584]{1,0:T(8,128)(2,1)S(1)}, bf16[80,3584]{1,0:T(8,128)(2,1)S(1)}) custom-call(bf16[80,3712]{1,0:T(8,128)(2,1)S(1)} %copy-done.14, bf16[80,3712]{1,0:T(8,128)(2,1)S(1)} %copy-done.9, bf16[2,3584,512]{2,1,0:T(8,128)(2,1)} %get-tuple-element.39.refs_2_, bf16[2,3584,512]{2,1,0:T(8,128)(2,1)} %collective-permute-done.1.refs_3_, ...), custom_call_target="tpu_custom_call" | custom-call | tf_op jit(solution)/shard_map/pallas_call | solution.py:33
  98.0 1.6 collective-permute-start.10
  99.5 1.9 collective-permute-done.9.refs_5_.refs_1_
  101.5 0.6 shard_map.71.refs_6_
  102.1 9.3 %shard_map.72 = (bf16[80,3584]{1,0:T(8,128)(2,1)S(1)}, bf16[80,3584]{1,0:T(8,128)(2,1)S(1)}) custom-call(bf16[80,3712]{1,0:T(8,128)(2,1)S(1)} %get-tuple-element.55.refs_0_, bf16[80,3712]{1,0:T(8,128)(2,1)S(1)} %collective-permute-done.9.refs_5_.refs_1_, bf16[2,3584,512]{2,1,0:T(8,128)(2,1)} %get-tuple-element.39.refs_2_, ...), custom_call_target="tpu_custom_call" | custom-call | tf_op jit(solution)/shard_map/pallas_call | solution.py:33
  111.4 0.0 collective-permute-done.12.refs_3_
  111.4 1.0 shard_map.73
  112.5 1.6 collective-permute-start.16
  114.1 0.6 shard_map.74.refs_6_
  114.7 0.7 collective-permute-start.13
  115.4 5.5 %collective-permute-start.14 = (bf16[128,3584]{1,0:T(8,128)(2,1)S(1)}, bf16[128,3584]{1,0:T(8,128)(2,1)S(1)}, u32[]{:S(2)}, u32[]{:S(2)}) collective-permute-start(bf16[128,3584]{1,0:T(8,128)(2,1)S(1)} %shard_map.74.refs_6_), channel_id=1, source_target_pairs={{0,4},{2,6},{4,8},{6,10},{1,5},{3,7},{5,9},{7,11},{16,20},{18,22},... | collective-permute-start | bytes 2752520 | tf_op jit(solution)/shard_map/ppermute | solution.py:210
  120.9 0.6 collective-permute-start.15
  121.4 7.5 %collective-permute-done.16.refs_1_ = bf16[80,3712]{1,0:T(8,128)(2,1)S(1)} collective-permute-done((bf16[80,3712]{1,0:T(8,128)(2,1)S(1)}, bf16[80,3712]{1,0:T(8,128)(2,1)S(1)}, u32[]{:S(2)}, u32[]{:S(2)}) %collective-permute-start.16) | collective-permute-done | bytes 593952 | tf_op jit(solution)/shard_map/ppermute | solution.py:213
  128.9 9.2 %shard_map.75 = (bf16[80,3584]{1,0:T(8,128)(2,1)S(1)}, bf16[80,3584]{1,0:T(8,128)(2,1)S(1)}) custom-call(bf16[80,3712]{1,0:T(8,128)(2,1)S(1)} %get-tuple-element.60.refs_0_, bf16[80,3712]{1,0:T(8,128)(2,1)S(1)} %collective-permute-done.16.refs_1_, bf16[2,3584,512]{2,1,0:T(8,128)(2,1)} %get-tuple-element.39.refs_2_, ...), custom_call_target="tpu_custom_call" | custom-call | tf_op jit(solution)/shard_map/pallas_call | solution.py:33
  138.1 1.6 collective-permute-start.18
  139.7 1.5 collective-permute-done.15.refs_3_
  141.2 0.6 shard_map.76.refs_4_
  141.8 1.5 collective-permute-start.17
  143.3 0.0 collective-permute-done.13.refs_5_
  143.3 0.0 collective-permute-done.14.refs_6_
  143.3 4.6 %collective-permute-done.18.refs_3_ = bf16[80,3584]{1,0:T(8,128)(2,1)S(1)} collective-permute-done((bf16[80,3584]{1,0:T(8,128)(2,1)S(1)}, bf16[80,3584]{1,0:T(8,128)(2,1)S(1)}, u32[]{:S(2)}, u32[]{:S(2)}) %collective-permute-start.18) | collective-permute-done | bytes 573472 | tf_op jit(solution)/shard_map/ppermute | solution.py:213
  147.9 0.6 shard_map.77
  148.5 1.3 collective-permute-start.19
  149.8 6.3 %collective-permute-start.20 = (bf16[128,3584]{1,0:T(8,128)(2,1)S(1)}, bf16[128,3584]{1,0:T(8,128)(2,1)S(1)}, u32[]{:S(2)}, u32[]{:S(2)}) collective-permute-start(bf16[128,3584]{1,0:T(8,128)(2,1)S(1)} %shard_map.77), channel_id=1, source_target_pairs={{0,12},{2,14},{4,0},{6,2},{1,13},{3,15},{5,1},{7,3},{16,28},{18,30... | collective-permute-start | bytes 2752520 | tf_op jit(solution)/shard_map/ppermute | solution.py:210
  156.2 37.2 %collective-permute-done.17 = bf16[128,3584]{1,0:T(8,128)(2,1)S(1)} collective-permute-done((bf16[128,3584]{1,0:T(8,128)(2,1)S(1)}, bf16[128,3584]{1,0:T(8,128)(2,1)S(1)}, u32[]{:S(2)}, u32[]{:S(2)}) %collective-permute-start.17) | collective-permute-done | bytes 917536 | tf_op jit(solution)/shard_map/ppermute | solution.py:210
  193.4 9.8 %collective-permute-done.20 = bf16[128,3584]{1,0:T(8,128)(2,1)S(1)} collective-permute-done((bf16[128,3584]{1,0:T(8,128)(2,1)S(1)}, bf16[128,3584]{1,0:T(8,128)(2,1)S(1)}, u32[]{:S(2)}, u32[]{:S(2)}) %collective-permute-start.20) | collective-permute-done | bytes 917536 | tf_op jit(solution)/shard_map/ppermute | solution.py:210
  203.2 1.6 add_convert_fusion
  (33 shorter events, 0.1 us)
Async XLA Ops:
  0.0 1.2 copy-start.12
  1.2 0.7 copy-start.17
  1.9 0.7 copy-start.18
  9.3 0.8 copy-start.15
  10.1 35.6 %collective-permute-start.1 = (bf16[2,3584,512]{2,1,0:T(8,128)(2,1)}, bf16[2,3584,512]{2,1,0:T(8,128)(2,1)}, u32[]{:S(2)}, u32[]{:S(2)}) collective-permute-start(bf16[2,3584,512]{2,1,0:T(8,128)(2,1)} %get-tuple-element.39.refs_2_), channel_id=1, source_target_pairs={{0,1},{1,0},{2,3},{3,2},{4,5},{5,4},{6,7},{7,6},{8,9},{9,8},{10,11... | collective-permute-start | bytes 22020104 | tf_op jit(solution)/shard_map/ppermute | solution.py:206
  10.6 35.2 %collective-permute-start.2 = (bf16[512,3584]{1,0:T(8,128)(2,1)}, bf16[512,3584]{1,0:T(8,128)(2,1)}, u32[]{:S(2)}, u32[]{:S(2)}) collective-permute-start(bf16[512,3584]{1,0:T(8,128)(2,1)} %bitcast.4.refs_4_), channel_id=1, source_target_pairs={{0,1},{1,0},{2,3},{3,2},{4,5},{5,4},{6,7},{7,6},{8,9},{9,8},{10,11... | collective-permute-start | bytes 11010056 | tf_op jit(solution)/shard_map/ppermute | solution.py:206
  10.6 25.4 %collective-permute-start.3 = (bf16[128,3712]{1,0:T(8,128)(2,1)S(1)}, bf16[128,3712]{1,0:T(8,128)(2,1)S(1)}, u32[]{:S(2)}, u32[]{:S(2)}) collective-permute-start(bf16[128,3712]{1,0:T(8,128)(2,1)S(1)} %get-tuple-element.40), channel_id=1, source_target_pairs={{0,4},{2,6},{4,8},{6,10},{8,12},{10,14},{1,5},{3,7},{5,9},{7,11},{... | collective-permute-start | bytes 2850824 | tf_op jit(solution)/shard_map/ppermute | solution.py:210
  15.6 24.6 %collective-permute-start.4 = (bf16[128,3712]{1,0:T(8,128)(2,1)S(1)}, bf16[128,3712]{1,0:T(8,128)(2,1)S(1)}, u32[]{:S(2)}, u32[]{:S(2)}) collective-permute-start(bf16[128,3712]{1,0:T(8,128)(2,1)S(1)} %get-tuple-element.40), channel_id=1, source_target_pairs={{4,0},{6,2},{8,4},{10,6},{12,8},{14,10},{5,1},{7,3},{9,5},{11,7},{... | collective-permute-start | bytes 2850824 | tf_op jit(solution)/shard_map/ppermute | solution.py:210
  16.9 15.1 %collective-permute-start = (bf16[80,3712]{1,0:T(8,128)(2,1)S(1)}, bf16[80,3712]{1,0:T(8,128)(2,1)S(1)}, u32[]{:S(2)}, u32[]{:S(2)}) collective-permute-start(bf16[80,3712]{1,0:T(8,128)(2,1)S(1)} %get-tuple-element.38), channel_id=1, source_target_pairs={{0,2},{2,0},{4,6},{6,4},{8,10},{10,8},{12,14},{14,12},{1,3},{3,1},... | collective-permute-start | bytes 1781768 | tf_op jit(solution)/shard_map/ppermute | solution.py:213
  32.0 8.2 %copy-start.10 = (bf16[80,3712]{1,0:T(8,128)(2,1)}, bf16[80,3712]{1,0:T(8,128)(2,1)S(1)}, u32[]{:S(2)}) copy-start(bf16[80,3712]{1,0:T(8,128)(2,1)S(1)} %collective-permute-done.refs_2_.refs_1_) | copy-start | bytes 1781764
  40.2 15.9 %copy-start = (bf16[128,3712]{1,0:T(8,128)(2,1)}, bf16[128,3712]{1,0:T(8,128)(2,1)S(1)}, u32[]{:S(2)}) copy-start(bf16[128,3712]{1,0:T(8,128)(2,1)S(1)} %get-tuple-element.41.refs_0_) | copy-start | bytes 2850820
  40.2 5.6 %copy-start.11 = (bf16[80,3712]{1,0:T(8,128)(2,1)S(1)}, bf16[80,3712]{1,0:T(8,128)(2,1)}, u32[]{:S(2)}) copy-start(bf16[80,3712]{1,0:T(8,128)(2,1)} %copy-done.10) | copy-start | bytes 1781764
  40.2 18.2 %collective-permute-start.7 = (bf16[128,3712]{1,0:T(8,128)(2,1)S(1)}, bf16[128,3712]{1,0:T(8,128)(2,1)S(1)}, u32[]{:S(2)}, u32[]{:S(2)}) collective-permute-start(bf16[128,3712]{1,0:T(8,128)(2,1)S(1)} %get-tuple-element.42.refs_1_.refs_2_), channel_id=1, source_target_pairs={{4,8},{6,10},{8,12},{10,14},{5,9},{7,11},{9,13},{11,15},{20,24},{2... | collective-permute-start | bytes 2850824 | tf_op jit(solution)/shard_map/ppermute | solution.py:210
  41.0 26.0 %collective-permute-start.8 = (bf16[128,3712]{1,0:T(8,128)(2,1)S(1)}, bf16[128,3712]{1,0:T(8,128)(2,1)S(1)}, u32[]{:S(2)}, u32[]{:S(2)}) collective-permute-start(bf16[128,3712]{1,0:T(8,128)(2,1)S(1)} %get-tuple-element.41.refs_0_), channel_id=1, source_target_pairs={{4,0},{6,2},{8,4},{10,6},{5,1},{7,3},{9,5},{11,7},{20,16},{22,18},... | collective-permute-start | bytes 2850824 | tf_op jit(solution)/shard_map/ppermute | solution.py:210
  43.4 0.8 copy-start.13
  44.2 14.2 %collective-permute-start.6 = (bf16[80,3712]{1,0:T(8,128)(2,1)S(1)}, bf16[80,3712]{1,0:T(8,128)(2,1)S(1)}, u32[]{:S(2)}, u32[]{:S(2)}) collective-permute-start(bf16[80,3712]{1,0:T(8,128)(2,1)S(1)} %get-tuple-element.47), channel_id=1, source_target_pairs={{0,2},{2,0},{4,6},{6,4},{8,10},{10,8},{12,14},{14,12},{1,3},{3,1},... | collective-permute-start | bytes 1781768 | tf_op jit(solution)/shard_map/ppermute | solution.py:213
  45.8 1.1 copy-start.16
  56.1 0.8 copy-start.2
  56.9 0.8 copy-start.19
  58.4 8.7 %copy-start.8 = (bf16[80,3712]{1,0:T(8,128)(2,1)}, bf16[80,3712]{1,0:T(8,128)(2,1)S(1)}, u32[]{:S(2)}) copy-start(bf16[80,3712]{1,0:T(8,128)(2,1)S(1)} %collective-permute-done.6.refs_2_.refs_1_) | copy-start | bytes 1781764
  58.4 15.7 %copy-start.3 = (bf16[80,3584]{1,0:T(8,128)(2,1)S(1)}, bf16[80,3584]{1,0:T(8,128)(2,1)}, u32[]{:S(2)}) copy-start(bf16[80,3584]{1,0:T(8,128)(2,1)} %copy-done.2) | copy-start | bytes 1720324
  58.4 1.0 copy-start.4
  67.1 0.9 copy-start.6
  68.0 1.2 copy-start.5
  69.2 1.2 copy-start.7
  70.4 18.3 %copy-start.9 = (bf16[80,3712]{1,0:T(8,128)(2,1)S(1)}, bf16[80,3712]{1,0:T(8,128)(2,1)}, u32[]{:S(2)}) copy-start(bf16[80,3712]{1,0:T(8,128)(2,1)} %copy-done.8) | copy-start | bytes 1781764
  70.4 18.3 %copy-start.14 = (bf16[80,3712]{1,0:T(8,128)(2,1)S(1)}, bf16[80,3712]{1,0:T(8,128)(2,1)}, u32[]{:S(2)}) copy-start(bf16[80,3712]{1,0:T(8,128)(2,1)} %copy-done.13) | copy-start | bytes 1781764
  70.4 41.0 %collective-permute-start.11 = (bf16[128,3712]{1,0:T(8,128)(2,1)S(1)}, bf16[128,3712]{1,0:T(8,128)(2,1)S(1)}, u32[]{:S(2)}, u32[]{:S(2)}) collective-permute-start(bf16[128,3712]{1,0:T(8,128)(2,1)S(1)} %get-tuple-element.48.refs_0_), channel_id=1, source_target_pairs={{4,0},{6,2},{5,1},{7,3},{20,16},{22,18},{21,17},{23,19}} | collective-permute-start | bytes 2850824 | tf_op jit(solution)/shard_map/ppermute | solution.py:210
  71.8 39.6 %collective-permute-start.12 = (bf16[128,3712]{1,0:T(8,128)(2,1)S(1)}, bf16[128,3712]{1,0:T(8,128)(2,1)S(1)}, u32[]{:S(2)}, u32[]{:S(2)}) collective-permute-start(bf16[128,3712]{1,0:T(8,128)(2,1)S(1)} %get-tuple-element.49.refs_1_), channel_id=1, source_target_pairs={{8,12},{10,14},{9,13},{11,15},{24,28},{26,30},{25,29},{27,31}} | collective-permute-start | bytes 2850824 | tf_op jit(solution)/shard_map/ppermute | solution.py:210
  72.5 16.2 %collective-permute-start.5 = (bf16[80,3584]{1,0:T(8,128)(2,1)}, bf16[80,3584]{1,0:T(8,128)(2,1)S(1)}, u32[]{:S(2)}, u32[]{:S(2)}) collective-permute-start(bf16[80,3584]{1,0:T(8,128)(2,1)} %copy-done.19), channel_id=1, source_target_pairs={{0,2},{2,0},{4,6},{6,4},{8,10},{10,8},{12,14},{14,12},{1,3},{3,1},... | collective-permute-start | bytes 1720328 | tf_op jit(solution)/shard_map/ppermute | solution.py:213
  75.3 26.1 %collective-permute-start.9 = (bf16[80,3712]{1,0:T(8,128)(2,1)S(1)}, bf16[80,3712]{1,0:T(8,128)(2,1)S(1)}, u32[]{:S(2)}, u32[]{:S(2)}) collective-permute-start(bf16[80,3712]{1,0:T(8,128)(2,1)S(1)} %get-tuple-element.52), channel_id=1, source_target_pairs={{0,2},{2,0},{4,6},{6,4},{8,10},{10,8},{12,14},{14,12},{1,3},{3,1},... | collective-permute-start | bytes 1781768 | tf_op jit(solution)/shard_map/ppermute | solution.py:213
  98.0 16.1 %collective-permute-start.10 = (bf16[80,3584]{1,0:T(8,128)(2,1)S(1)}, bf16[80,3584]{1,0:T(8,128)(2,1)S(1)}, u32[]{:S(2)}, u32[]{:S(2)}) collective-permute-start(bf16[80,3584]{1,0:T(8,128)(2,1)S(1)} %get-tuple-element.54), channel_id=1, source_target_pairs={{0,2},{2,0},{4,6},{6,4},{8,10},{10,8},{12,14},{14,12},{1,3},{3,1},... | collective-permute-start | bytes 1720328 | tf_op jit(solution)/shard_map/ppermute | solution.py:213
  102.1 9.3 %copy-start.1 = (bf16[128,3712]{1,0:T(8,128)(2,1)S(1)}, bf16[128,3712]{1,0:T(8,128)(2,1)}, u32[]{:S(2)}) copy-start(bf16[128,3712]{1,0:T(8,128)(2,1)} %copy-done) | copy-start | bytes 2850820
  112.5 16.4 %collective-permute-start.16 = (bf16[80,3712]{1,0:T(8,128)(2,1)S(1)}, bf16[80,3712]{1,0:T(8,128)(2,1)S(1)}, u32[]{:S(2)}, u32[]{:S(2)}) collective-permute-start(bf16[80,3712]{1,0:T(8,128)(2,1)S(1)} %get-tuple-element.61), channel_id=1, source_target_pairs={{0,2},{2,0},{4,6},{6,4},{8,10},{10,8},{12,14},{14,12},{1,3},{3,1},... | collective-permute-start | bytes 1781768 | tf_op jit(solution)/shard_map/ppermute | solution.py:213
  114.7 28.6 %collective-permute-start.13 = (bf16[128,3584]{1,0:T(8,128)(2,1)S(1)}, bf16[128,3584]{1,0:T(8,128)(2,1)S(1)}, u32[]{:S(2)}, u32[]{:S(2)}) collective-permute-start(bf16[128,3584]{1,0:T(8,128)(2,1)S(1)} %shard_map.74.refs_6_), channel_id=1, source_target_pairs={{8,4},{10,6},{12,8},{14,10},{9,5},{11,7},{13,9},{15,11},{24,20},{2... | collective-permute-start | bytes 2752520 | tf_op jit(solution)/shard_map/ppermute | solution.py:210
  115.4 27.9 %collective-permute-start.14 = (bf16[128,3584]{1,0:T(8,128)(2,1)S(1)}, bf16[128,3584]{1,0:T(8,128)(2,1)S(1)}, u32[]{:S(2)}, u32[]{:S(2)}) collective-permute-start(bf16[128,3584]{1,0:T(8,128)(2,1)S(1)} %shard_map.74.refs_6_), channel_id=1, source_target_pairs={{0,4},{2,6},{4,8},{6,10},{1,5},{3,7},{5,9},{7,11},{16,20},{18,22},... | collective-permute-start | bytes 2752520 | tf_op jit(solution)/shard_map/ppermute | solution.py:210
  120.9 20.3 %collective-permute-start.15 = (bf16[80,3584]{1,0:T(8,128)(2,1)S(1)}, bf16[80,3584]{1,0:T(8,128)(2,1)S(1)}, u32[]{:S(2)}, u32[]{:S(2)}) collective-permute-start(bf16[80,3584]{1,0:T(8,128)(2,1)S(1)} %get-tuple-element.59), channel_id=1, source_target_pairs={{0,2},{2,0},{4,6},{6,4},{8,10},{10,8},{12,14},{14,12},{1,3},{3,1},... | collective-permute-start | bytes 1720328 | tf_op jit(solution)/shard_map/ppermute | solution.py:213
  138.1 9.8 %collective-permute-start.18 = (bf16[80,3584]{1,0:T(8,128)(2,1)S(1)}, bf16[80,3584]{1,0:T(8,128)(2,1)S(1)}, u32[]{:S(2)}, u32[]{:S(2)}) collective-permute-start(bf16[80,3584]{1,0:T(8,128)(2,1)S(1)} %get-tuple-element.64), channel_id=1, source_target_pairs={{0,2},{2,0},{4,6},{6,4},{8,10},{10,8},{12,14},{14,12},{1,3},{3,1},... | collective-permute-start | bytes 1720328 | tf_op jit(solution)/shard_map/ppermute | solution.py:213
  141.8 51.6 %collective-permute-start.17 = (bf16[128,3584]{1,0:T(8,128)(2,1)S(1)}, bf16[128,3584]{1,0:T(8,128)(2,1)S(1)}, u32[]{:S(2)}, u32[]{:S(2)}) collective-permute-start(bf16[128,3584]{1,0:T(8,128)(2,1)S(1)} %shard_map.76.refs_4_), channel_id=1, source_target_pairs={{0,8},{2,10},{4,12},{6,14},{8,0},{10,2},{12,4},{14,6},{1,9},{3,11}... | collective-permute-start | bytes 2752520 | tf_op jit(solution)/shard_map/ppermute | solution.py:210
  148.5 44.9 %collective-permute-start.19 = (bf16[128,3584]{1,0:T(8,128)(2,1)S(1)}, bf16[128,3584]{1,0:T(8,128)(2,1)S(1)}, u32[]{:S(2)}, u32[]{:S(2)}) collective-permute-start(bf16[128,3584]{1,0:T(8,128)(2,1)S(1)} %shard_map.77), channel_id=1, source_target_pairs={{8,12},{10,14},{12,0},{14,2},{9,13},{11,15},{13,1},{15,3},{24,28},... | collective-permute-start | bytes 2752520 | tf_op jit(solution)/shard_map/ppermute | solution.py:210
  149.8 53.3 %collective-permute-start.20 = (bf16[128,3584]{1,0:T(8,128)(2,1)S(1)}, bf16[128,3584]{1,0:T(8,128)(2,1)S(1)}, u32[]{:S(2)}, u32[]{:S(2)}) collective-permute-start(bf16[128,3584]{1,0:T(8,128)(2,1)S(1)} %shard_map.77), channel_id=1, source_target_pairs={{0,12},{2,14},{4,0},{6,2},{1,13},{3,15},{5,1},{7,3},{16,28},{18,30... | collective-permute-start | bytes 2752520 | tf_op jit(solution)/shard_map/ppermute | solution.py:210

commit v7 on v6

--- a/solution.py
+++ b/solution.py
@@ -56,14 +56,7 @@
     )(*[in_vmem(a) for a in arrays], *after)
 
 
-def first_kernel(experts, tokens, routes, scale, gate_w, up_w, block, *refs):
-    picked, (stack, sems) = refs[:4], refs[4:]
-    copies = [
-        pltpu.make_async_copy(gate_w, stack.at[0], sems.at[0]),
-        pltpu.make_async_copy(up_w, stack.at[1], sems.at[1]),
-    ]
-    for copy in copies:
-        copy.start()
+def first_kernel(experts, tokens, routes, scale, block, *picked):
     count, width = tokens.shape
     lane = lax.broadcasted_iota(jnp.int32, (count, block.shape[1] - width), 1)
     expert, part = lax.rem(lane, experts), lax.div(lane, experts)
@@ -78,8 +71,26 @@
     block[:, :width] = tokens[...]
     block[:, width:] = marks.astype(jnp.bfloat16)
     choose(block, *picked)
-    for copy in copies:
+
+
+def copy_kernel(source, result, held, sems):
+    pieces = sems.shape[1]
+    rows = source.shape[0] // pieces
+    cuts = [pl.ds(k * rows, rows) for k in range(pieces)]
+    fetch = [pltpu.make_async_copy(source.at[cut], held.at[cut], sems.at[0, k]) for k, cut in enumerate(cuts)]
+    store = [pltpu.make_async_copy(held.at[cut], result.at[cut], sems.at[1, k]) for k, cut in enumerate(cuts)]
+    for copy in fetch:
+        copy.start()
+    for arrived, leaving in zip(fetch, store):
+        arrived.wait()
+        leaving.start()
+    for copy in store:
         copy.wait()
+
+
+def passing_kernel(*refs):
+    for source, result in zip(refs, refs[len(refs) // 2 :]):
+        result[...] = source[...]
 
 
 def choose(held, own_map, other_map, own_rows, other_rows):
@@ -119,16 +130,17 @@
 
 
 def expert_kernel(experts, own, other, *refs):
-    own_w, other_w, own_down, other_down, own_out, other_out, rows, hidden, gates, ups, downs, sems = refs
+    weights, (own_out, other_out, rows, hidden, gates, ups, downs, sems) = refs[:6], refs[6:]
     cap, width = own_out.shape
     tiles, _, size = gates.shape
     each = tiles // 2
     queue = []
     for tile in range(tiles):
-        stack, part = (own_w, other_w)[tile // each], pl.ds(tile % each * size, size)
-        queue.append(pltpu.make_async_copy(stack.at[0, :, part], gates.at[tile], sems.at[tile, 0]))
-        queue.append(pltpu.make_async_copy(stack.at[1, :, part], ups.at[tile], sems.at[tile, 1]))
-    for half, down in enumerate((own_down, other_down)):
+        part = pl.ds(tile % each * size, size)
+        gate_w, up_w = weights[tile // each * 3 : tile // each * 3 + 2]
+        queue.append(pltpu.make_async_copy(gate_w.at[:, part], gates.at[tile], sems.at[tile, 0]))
+        queue.append(pltpu.make_async_copy(up_w.at[:, part], ups.at[tile], sems.at[tile, 1]))
+    for half, down in enumerate(weights[2::3]):
         queue.append(pltpu.make_async_copy(down, downs.at[half], sems.at[half, 2]))
     ahead = iter(queue[4:])
     for copy in queue[:4]:
@@ -183,10 +195,11 @@
     size = min(hidden, 256)
     cap = -(-(5 * count // experts) // 16) * 16
     wide = width + -(-3 * experts // 128) * 128
+    hbm = functools.partial(pltpu.HBM, dtype=jnp.bfloat16)
     in_hbm = functools.partial(pltpu.with_memory_space_constraint, memory_space=pltpu.HBM)
     bf16 = functools.partial(jax.ShapeDtypeStruct, dtype=jnp.bfloat16)
 
-    block, *picked, stack = call(
+    block, *picked = call(
         functools.partial(first_kernel, experts),
         [
             bf16((count, wide)),
@@ -194,16 +207,12 @@
             bf16((count, cap)),
             bf16((cap, wide)),
             bf16((cap, wide)),
-            bf16((2, width, hidden)),
         ],
-        [tokens, routes.T, route_scale.T, in_hbm(w_gate[0]), in_hbm(w_up[0])],
-        (),
-        [pltpu.SemaphoreType.DMA((2,))],
-        [IN_VMEM] * 3 + [ANYWHERE] * 2,
-        out_specs=[IN_VMEM] * 6,
-    )
+        [in_hbm(tokens), in_hbm(routes.T), in_hbm(route_scale.T)],
+    )
+    own = (w_gate[0], w_up[0], w_down[0])
     swap = functools.partial(lax.ppermute, axis_name="local", perm=[(0, 1), (1, 0)])
-    weights = [in_hbm(stack), swap(stack), in_hbm(w_down[0]), swap(w_down[0])]
+    others = [swap(own[0]), swap(own[1])]
 
     def along(block, pairs):
         moves = [(2 * a + y, 2 * b + y) for a, b in pairs for y in range(2)]
@@ -237,8 +246,19 @@
                 pltpu.VMEM((2, hidden, width), jnp.bfloat16),
                 pltpu.SemaphoreType.DMA((tiles, 3)),
             ],
-            [IN_VMEM] * 2 + [ANYWHERE] * 4,
+            [IN_VMEM] * 2 + [ANYWHERE] * 6,
             32,
+        )
+
+    def carry(weight, after=()):
+        return call(
+            copy_kernel,
+            [hbm(weight.shape)],
+            [in_hbm(weight)],
+            after,
+            [pltpu.VMEM(weight.shape, jnp.bfloat16), pltpu.SemaphoreType.DMA((2, 4))],
+            [ANYWHERE],
+            out_specs=[ANYWHERE],
         )
 
     def spread(maps, own_out, other_out, extras=(), after=()):
@@ -264,9 +284,6 @@
                 if 0 <= a + way < places and 0 <= a - way * (step - 1) < places
             ]
             held[way, step] = along(held.get((way, step - 1), block), pairs)
-
-    def hold(step, until):
-        held[1, step], held[-1, step] = tied([held[1, step], held[-1, step]], until)
 
     def do_pick(slot, after=()):
         keys = sorted({row[slot - 1] for row in plan})
@@ -291,23 +308,30 @@
 
     relay(1)
     picks[0] = picked[:2], picked[2], across(picked[3])
-    hold(1, [picks[0][2]])
+    (down,) = carry(own[2], [picks[0][2]])
+    held[1, 1], held[-1, 1] = tied([held[1, 1], held[-1, 1]], [down, *others])
+    others.append(swap(down))
+    weights = [*map(in_hbm, own), *others]
     relay(2)
     do_pick(1)
-    do_expert(0)
-    hold(2, [picks[1][2], outs[0][0]])
+    held[1, 2], held[-1, 2] = call(
+        passing_kernel, [bf16((count, wide))] * 2, [held[1, 2], held[-1, 2]], [*last, picks[1][2]]
+    )
     for step in range(3, places):
         relay(step)
+    do_expert(1)
     do_pick(2)
-    do_expert(1, after=[outs[0][1]])
-    total = ordered(spread, picks[0][0], *outs[0], after=[picks[2][2]])
+    do_expert(0)
+    do_spread(1)
+    do_pick(3)
     do_expert(2)
     for slot in range(3, places):
-        do_pick(slot)
-        do_spread(slot - 2)
+        do_spread(slot - 1, after=returned[slot - 3])
         do_expert(slot)
-        do_spread(slot - 1)
-    do_spread(places - 1, after=returned[0])
+        if slot + 1 < places:
+            do_pick(slot + 1)
+    total = ordered(spread, picks[0][0], *outs[0])
+    do_spread(places - 1)
     total = total.astype(jnp.float32)
     for block in sum(returned, []):
         total = total + block.astype(jnp.float32)

time: 205 us -> 228 us (1.11)
  waiting for transfers between devices: 105 us -> 141 us
  local copies, waits for them, and re-layouts: 11.2 us -> 0 us
    ppermute x11, waiting for transfers between devices: 62.9 us -> 84.7 us  [along(): return lax.ppermute(block, 'node', moves)]
    ppermute x8, waiting for transfers between devices: 42.5 us -> 56.3 us  [across(): return lax.ppermute(block, 'node', [(n, n ^ 1) for n in range(experts)])]
    unnamed x40 -> x0, local copies, waits for them, and re-layouts: 11.2 us -> none
    ppermute x11, starting transfers between devices: 25.8 us -> 23.4 us  [along(): return lax.ppermute(block, 'node', moves)]
    pallas_call x12 -> x14, Pallas kernels: 49.4 us -> 48.4 us  [call(): pl.pallas_call(body, out_shape=outs, in_specs=specs, out_specs=out_specs...]
  transfers between devices with their start and end apart: 21 -> 22, of which waited for: 12 -> 11; matrix products, arithmetic and copies ran while one was open for 0% -> 0% of each run, Pallas kernels for 21% -> 21%
where the time goes in v7:
time: 228 us; the launch traced here: 227 us
  waiting for transfers between devices  141 us (62%)
  Pallas kernels  48.4 us (21%)
  starting transfers between devices  36 us (16%)
    ppermute x11, waiting for transfers between devices, along(): return lax.ppermute(block, 'node', moves)  84.7 us
    ppermute x8, waiting for transfers between devices, across(): return lax.ppermute(block, 'node', [(n, n ^ 1) for n in range(experts)])  56.3 us
    pallas_call x14, Pallas kernels, call(): pl.pallas_call(body, out_shape=outs, in_specs=specs, out_specs=out_specs...  48.4 us
    ppermute x11, starting transfers between devices, along(): return lax.ppermute(block, 'node', moves)  23.4 us
    ppermute x8, starting transfers between devices, across(): return lax.ppermute(block, 'node', [(n, n ^ 1) for n in range(experts)])  12 us
  transfers between devices with their start and end apart: 22, of which 11 were waited for; matrix products, arithmetic and copies ran while one was open for 0% of the time, Pallas kernels for 21%

profile of v7, /device:TPU:0, one launch (start us, length us, event | category | flops | bytes accessed | tf_op | source)
XLA Modules:
  0.0 227.3 jit_solution(3703522562574002545)
XLA Ops:
  0.0 0.5 collective-permute-start.1
  0.5 0.1 collective-permute-start.2
  0.5 2.3 shard_map.64
  2.8 3.0 %collective-permute-start = (bf16[80,3712]{1,0:T(8,128)(2,1)S(1)}, bf16[80,3712]{1,0:T(8,128)(2,1)S(1)}, u32[]{:S(2)}, u32[]{:S(2)}) collective-permute-start(bf16[80,3712]{1,0:T(8,128)(2,1)S(1)} %get-tuple-element.37), channel_id=1, source_target_pairs={{0,2},{2,0},{4,6},{6,4},{8,10},{10,8},{12,14},{14,12},{1,3},{3,1},... | collective-permute-start | bytes 1781768 | tf_op jit(solution)/shard_map/ppermute | solution.py:222
  5.8 13.6 %collective-permute-done.refs_1_ = bf16[80,3712]{1,0:T(8,128)(2,1)S(1)} collective-permute-done((bf16[80,3712]{1,0:T(8,128)(2,1)S(1)}, bf16[80,3712]{1,0:T(8,128)(2,1)S(1)}, u32[]{:S(2)}, u32[]{:S(2)}) %collective-permute-start) | collective-permute-done | bytes 593952 | tf_op jit(solution)/shard_map/ppermute | solution.py:222
  19.4 3.1 %shard_map.65.refs_2_ = bf16[512,3584]{1,0:T(8,128)(2,1)} custom-call(bf16[512,3584]{1,0:T(8,128)(2,1)} %bitcast.5, bf16[80,3712]{1,0:T(8,128)(2,1)S(1)} %collective-permute-done.refs_1_), custom_call_target="tpu_custom_call" | custom-call | tf_op jit(solution)/shard_map/pallas_call | solution.py:33
  22.5 0.1 collective-permute-start.3
  22.6 3.8 %collective-permute-start.4 = (bf16[128,3712]{1,0:T(8,128)(2,1)S(1)}, bf16[128,3712]{1,0:T(8,128)(2,1)S(1)}, u32[]{:S(2)}, u32[]{:S(2)}) collective-permute-start(bf16[128,3712]{1,0:T(8,128)(2,1)S(1)} %get-tuple-element.38), channel_id=1, source_target_pairs={{0,4},{2,6},{4,8},{6,10},{8,12},{10,14},{1,5},{3,7},{5,9},{7,11},{... | collective-permute-start | bytes 2850824 | tf_op jit(solution)/shard_map/ppermute | solution.py:219
  26.4 1.3 collective-permute-start.5
  27.7 19.6 %collective-permute-done.4.refs_0_ = bf16[128,3712]{1,0:T(8,128)(2,1)S(1)} collective-permute-done((bf16[128,3712]{1,0:T(8,128)(2,1)S(1)}, bf16[128,3712]{1,0:T(8,128)(2,1)S(1)}, u32[]{:S(2)}, u32[]{:S(2)}) %collective-permute-start.4) | collective-permute-done | bytes 950304 | tf_op jit(solution)/shard_map/ppermute | solution.py:219
  47.3 4.2 %collective-permute-done.5.refs_1_ = bf16[128,3712]{1,0:T(8,128)(2,1)S(1)} collective-permute-done((bf16[128,3712]{1,0:T(8,128)(2,1)S(1)}, bf16[128,3712]{1,0:T(8,128)(2,1)S(1)}, u32[]{:S(2)}, u32[]{:S(2)}) %collective-permute-start.5) | collective-permute-done | bytes 950304 | tf_op jit(solution)/shard_map/ppermute | solution.py:219
  51.4 0.0 collective-permute-done.1.refs_3_.refs_5_
  51.4 0.0 collective-permute-done.2.refs_4_.refs_6_
  51.4 0.7 collective-permute-start.6
  52.2 1.3 collective-permute-start.7
  53.5 1.0 shard_map.67
  54.5 1.6 collective-permute-start.8
  56.1 13.2 %collective-permute-done.8.refs_3_.refs_1_ = bf16[80,3712]{1,0:T(8,128)(2,1)S(1)} collective-permute-done((bf16[80,3712]{1,0:T(8,128)(2,1)S(1)}, bf16[80,3712]{1,0:T(8,128)(2,1)S(1)}, u32[]{:S(2)}, u32[]{:S(2)}) %collective-permute-start.8) | collective-permute-done | bytes 593952 | tf_op jit(solution)/shard_map/ppermute | solution.py:222
  69.3 0.0 collective-permute-done.6.refs_0_
  69.3 9.4 %collective-permute-done.7.refs_1_ = bf16[128,3712]{1,0:T(8,128)(2,1)S(1)} collective-permute-done((bf16[128,3712]{1,0:T(8,128)(2,1)S(1)}, bf16[128,3712]{1,0:T(8,128)(2,1)S(1)}, u32[]{:S(2)}, u32[]{:S(2)}) %collective-permute-start.7) | collective-permute-done | bytes 950304 | tf_op jit(solution)/shard_map/ppermute | solution.py:219
  78.7 0.1 shard_map.68
  78.8 1.3 collective-permute-start.10
  80.1 0.7 collective-permute-start.11
  80.9 0.0 collective-permute-done.3.refs_7_
  80.9 9.2 %shard_map.69 = (bf16[80,3584]{1,0:T(8,128)(2,1)S(1)}, bf16[80,3584]{1,0:T(8,128)(2,1)S(1)}) custom-call(bf16[80,3712]{1,0:T(8,128)(2,1)S(1)} %get-tuple-element.45.refs_0_, bf16[80,3712]{1,0:T(8,128)(2,1)S(1)} %collective-permute-done.8.refs_3_.refs_1_, bf16[3584,512]{1,0:T(8,128)(2,1)} %bitcast.11, bf16[3584,512]{1,0:T(8,128)(2,1)} %bitcast.16, ...), custom_call_target="tpu_custom_call" | custom-call | tf_op jit(solution)/shard_map/pallas_call | solution.py:33
  90.1 1.6 collective-permute-start.12
  91.7 1.2 shard_map.70
  92.9 0.6 collective-permute-start.14
  93.5 9.2 %shard_map.71 = (bf16[80,3584]{1,0:T(8,128)(2,1)S(1)}, bf16[80,3584]{1,0:T(8,128)(2,1)S(1)}) custom-call(bf16[80,3712]{1,0:T(8,128)(2,1)S(1)} %get-tuple-element.36.refs_0_, bf16[80,3712]{1,0:T(8,128)(2,1)S(1)} %collective-permute-done.refs_1_, bf16[3584,512]{1,0:T(8,128)(2,1)} %bitcast.12, bf16[3584,512]{1,0:T(8,128)(2,1)} %bitcast.17, ...), custom_call_target="tpu_custom_call" | custom-call | tf_op jit(solution)/shard_map/pallas_call | solution.py:33
  102.7 3.4 %collective-permute-done.12.refs_3_ = bf16[80,3584]{1,0:T(8,128)(2,1)S(1)} collective-permute-done((bf16[80,3584]{1,0:T(8,128)(2,1)S(1)}, bf16[80,3584]{1,0:T(8,128)(2,1)S(1)}, u32[]{:S(2)}, u32[]{:S(2)}) %collective-permute-start.12) | collective-permute-done | bytes 573472 | tf_op jit(solution)/shard_map/ppermute | solution.py:222
  106.1 0.6 shard_map.72.refs_4_
  106.7 0.7 collective-permute-start.16
  107.5 5.2 %collective-permute-start.17 = (bf16[128,3584]{1,0:T(8,128)(2,1)S(1)}, bf16[128,3584]{1,0:T(8,128)(2,1)S(1)}, u32[]{:S(2)}, u32[]{:S(2)}) collective-permute-start(bf16[128,3584]{1,0:T(8,128)(2,1)S(1)} %shard_map.72.refs_4_), channel_id=1, source_target_pairs={{0,4},{2,6},{4,8},{6,10},{1,5},{3,7},{5,9},{7,11},{16,20},{18,22},... | collective-permute-start | bytes 2752520 | tf_op jit(solution)/shard_map/ppermute | solution.py:219
  112.7 0.0 collective-permute-done.10.refs_1_
  112.7 0.0 collective-permute-done.11.refs_3_
  112.7 1.3 shard_map.73
  114.0 1.6 collective-permute-start.13
  115.6 3.3 %collective-permute-done.14.refs_1_ = bf16[80,3712]{1,0:T(8,128)(2,1)S(1)} collective-permute-done((bf16[80,3712]{1,0:T(8,128)(2,1)S(1)}, bf16[80,3712]{1,0:T(8,128)(2,1)S(1)}, u32[]{:S(2)}, u32[]{:S(2)}) %collective-permute-start.14) | collective-permute-done | bytes 593952 | tf_op jit(solution)/shard_map/ppermute | solution.py:222
  118.8 9.2 %shard_map.74 = (bf16[80,3584]{1,0:T(8,128)(2,1)S(1)}, bf16[80,3584]{1,0:T(8,128)(2,1)S(1)}) custom-call(bf16[80,3712]{1,0:T(8,128)(2,1)S(1)} %get-tuple-element.55.refs_0_, bf16[80,3712]{1,0:T(8,128)(2,1)S(1)} %collective-permute-done.14.refs_1_, bf16[3584,512]{1,0:T(8,128)(2,1)} %bitcast.13, bf16[3584,512]{1,0:T(8,128)(2,1)} %bitcast.18, ...), custom_call_target="tpu_custom_call" | custom-call | tf_op jit(solution)/shard_map/pallas_call | solution.py:33
  128.1 1.6 collective-permute-start.15
  129.6 0.5 collective-permute-start.9
  130.2 0.0 collective-permute-done.16.refs_5_
  130.2 0.0 collective-permute-done.17.refs_6_
  130.2 13.9 %collective-permute-done.15.refs_3_ = bf16[80,3584]{1,0:T(8,128)(2,1)S(1)} collective-permute-done((bf16[80,3584]{1,0:T(8,128)(2,1)S(1)}, bf16[80,3584]{1,0:T(8,128)(2,1)S(1)}, u32[]{:S(2)}, u32[]{:S(2)}) %collective-permute-start.15) | collective-permute-done | bytes 573472 | tf_op jit(solution)/shard_map/ppermute | solution.py:222
  144.0 0.6 shard_map.75.refs_8_
  144.7 0.0 collective-permute-done.13.refs_1_
  144.7 9.2 %shard_map.76 = (bf16[80,3584]{1,0:T(8,128)(2,1)S(1)}, bf16[80,3584]{1,0:T(8,128)(2,1)S(1)}) custom-call(bf16[80,3712]{1,0:T(8,128)(2,1)S(1)} %get-tuple-element.52.refs_0_, bf16[80,3712]{1,0:T(8,128)(2,1)S(1)} %collective-permute-done.13.refs_1_, bf16[3584,512]{1,0:T(8,128)(2,1)} %bitcast.14, bf16[3584,512]{1,0:T(8,128)(2,1)} %bitcast.19, ...), custom_call_target="tpu_custom_call" | custom-call | tf_op jit(solution)/shard_map/pallas_call | solution.py:33
  153.9 1.6 collective-permute-start.19
  155.5 0.8 collective-permute-start.18
  156.2 0.0 collective-permute-done.9.refs_3_
  156.3 0.6 shard_map.77.refs_4_
  156.9 9.0 %collective-permute-done.19.refs_3_ = bf16[80,3584]{1,0:T(8,128)(2,1)S(1)} collective-permute-done((bf16[80,3584]{1,0:T(8,128)(2,1)S(1)}, bf16[80,3584]{1,0:T(8,128)(2,1)S(1)}, u32[]{:S(2)}, u32[]{:S(2)}) %collective-permute-start.19) | collective-permute-done | bytes 573472 | tf_op jit(solution)/shard_map/ppermute | solution.py:222
  165.9 0.6 shard_map.78
  166.5 1.3 collective-permute-start.20
  167.8 6.3 %collective-permute-start.21 = (bf16[128,3584]{1,0:T(8,128)(2,1)S(1)}, bf16[128,3584]{1,0:T(8,128)(2,1)S(1)}, u32[]{:S(2)}, u32[]{:S(2)}) collective-permute-start(bf16[128,3584]{1,0:T(8,128)(2,1)S(1)} %shard_map.78), channel_id=1, source_target_pairs={{0,12},{2,14},{4,0},{6,2},{1,13},{3,15},{5,1},{7,3},{16,28},{18,30... | collective-permute-start | bytes 2752520 | tf_op jit(solution)/shard_map/ppermute | solution.py:219
  174.1 38.2 %collective-permute-done.18 = bf16[128,3584]{1,0:T(8,128)(2,1)S(1)} collective-permute-done((bf16[128,3584]{1,0:T(8,128)(2,1)S(1)}, bf16[128,3584]{1,0:T(8,128)(2,1)S(1)}, u32[]{:S(2)}, u32[]{:S(2)}) %collective-permute-start.18) | collective-permute-done | bytes 917536 | tf_op jit(solution)/shard_map/ppermute | solution.py:219
  212.4 0.0 collective-permute-done.20
  212.4 13.3 %collective-permute-done.21 = bf16[128,3584]{1,0:T(8,128)(2,1)S(1)} collective-permute-done((bf16[128,3584]{1,0:T(8,128)(2,1)S(1)}, bf16[128,3584]{1,0:T(8,128)(2,1)S(1)}, u32[]{:S(2)}, u32[]{:S(2)}) %collective-permute-start.21) | collective-permute-done | bytes 917536 | tf_op jit(solution)/shard_map/ppermute | solution.py:219
  225.7 1.6 add_convert_fusion
  (1 shorter events, 0.0 us)
Async XLA Ops:
  0.0 51.4 %collective-permute-start.1 = (bf16[3584,512]{1,0:T(8,128)(2,1)}, bf16[3584,512]{1,0:T(8,128)(2,1)}, u32[]{:S(2)}, u32[]{:S(2)}) collective-permute-start(bf16[3584,512]{1,0:T(8,128)(2,1)} %bitcast.10), channel_id=1, source_target_pairs={{0,1},{1,0},{2,3},{3,2},{4,5},{5,4},{6,7},{7,6},{8,9},{9,8},{10,11... | collective-permute-start | bytes 11010056 | tf_op jit(solution)/shard_map/ppermute | solution.py:215
  0.5 51.0 %collective-permute-start.2 = (bf16[3584,512]{1,0:T(8,128)(2,1)}, bf16[3584,512]{1,0:T(8,128)(2,1)}, u32[]{:S(2)}, u32[]{:S(2)}) collective-permute-start(bf16[3584,512]{1,0:T(8,128)(2,1)} %bitcast.15), channel_id=1, source_target_pairs={{0,1},{1,0},{2,3},{3,2},{4,5},{5,4},{6,7},{7,6},{8,9},{9,8},{10,11... | collective-permute-start | bytes 11010056 | tf_op jit(solution)/shard_map/ppermute | solution.py:215
  2.8 16.6 %collective-permute-start = (bf16[80,3712]{1,0:T(8,128)(2,1)S(1)}, bf16[80,3712]{1,0:T(8,128)(2,1)S(1)}, u32[]{:S(2)}, u32[]{:S(2)}) collective-permute-start(bf16[80,3712]{1,0:T(8,128)(2,1)S(1)} %get-tuple-element.37), channel_id=1, source_target_pairs={{0,2},{2,0},{4,6},{6,4},{8,10},{10,8},{12,14},{14,12},{1,3},{3,1},... | collective-permute-start | bytes 1781768 | tf_op jit(solution)/shard_map/ppermute | solution.py:222
  22.5 58.4 %collective-permute-start.3 = (bf16[512,3584]{1,0:T(8,128)(2,1)}, bf16[512,3584]{1,0:T(8,128)(2,1)}, u32[]{:S(2)}, u32[]{:S(2)}) collective-permute-start(bf16[512,3584]{1,0:T(8,128)(2,1)} %shard_map.65.refs_2_), channel_id=1, source_target_pairs={{0,1},{1,0},{2,3},{3,2},{4,5},{5,4},{6,7},{7,6},{8,9},{9,8},{10,11... | collective-permute-start | bytes 11010056 | tf_op jit(solution)/shard_map/ppermute | solution.py:313
  22.6 24.6 %collective-permute-start.4 = (bf16[128,3712]{1,0:T(8,128)(2,1)S(1)}, bf16[128,3712]{1,0:T(8,128)(2,1)S(1)}, u32[]{:S(2)}, u32[]{:S(2)}) collective-permute-start(bf16[128,3712]{1,0:T(8,128)(2,1)S(1)} %get-tuple-element.38), channel_id=1, source_target_pairs={{0,4},{2,6},{4,8},{6,10},{8,12},{10,14},{1,5},{3,7},{5,9},{7,11},{... | collective-permute-start | bytes 2850824 | tf_op jit(solution)/shard_map/ppermute | solution.py:219
  26.4 25.1 %collective-permute-start.5 = (bf16[128,3712]{1,0:T(8,128)(2,1)S(1)}, bf16[128,3712]{1,0:T(8,128)(2,1)S(1)}, u32[]{:S(2)}, u32[]{:S(2)}) collective-permute-start(bf16[128,3712]{1,0:T(8,128)(2,1)S(1)} %get-tuple-element.38), channel_id=1, source_target_pairs={{4,0},{6,2},{8,4},{10,6},{12,8},{14,10},{5,1},{7,3},{9,5},{11,7},{... | collective-permute-start | bytes 2850824 | tf_op jit(solution)/shard_map/ppermute | solution.py:219
  51.4 17.8 %collective-permute-start.6 = (bf16[128,3712]{1,0:T(8,128)(2,1)S(1)}, bf16[128,3712]{1,0:T(8,128)(2,1)S(1)}, u32[]{:S(2)}, u32[]{:S(2)}) collective-permute-start(bf16[128,3712]{1,0:T(8,128)(2,1)S(1)} %get-tuple-element.39.refs_1_.refs_2_), channel_id=1, source_target_pairs={{4,8},{6,10},{8,12},{10,14},{5,9},{7,11},{9,13},{11,15},{20,24},{2... | collective-permute-start | bytes 2850824 | tf_op jit(solution)/shard_map/ppermute | solution.py:219
  52.2 26.6 %collective-permute-start.7 = (bf16[128,3712]{1,0:T(8,128)(2,1)S(1)}, bf16[128,3712]{1,0:T(8,128)(2,1)S(1)}, u32[]{:S(2)}, u32[]{:S(2)}) collective-permute-start(bf16[128,3712]{1,0:T(8,128)(2,1)S(1)} %get-tuple-element.40.refs_0_), channel_id=1, source_target_pairs={{4,0},{6,2},{8,4},{10,6},{5,1},{7,3},{9,5},{11,7},{20,16},{22,18},... | collective-permute-start | bytes 2850824 | tf_op jit(solution)/shard_map/ppermute | solution.py:219
  54.5 14.8 %collective-permute-start.8 = (bf16[80,3712]{1,0:T(8,128)(2,1)S(1)}, bf16[80,3712]{1,0:T(8,128)(2,1)S(1)}, u32[]{:S(2)}, u32[]{:S(2)}) collective-permute-start(bf16[80,3712]{1,0:T(8,128)(2,1)S(1)} %get-tuple-element.42), channel_id=1, source_target_pairs={{0,2},{2,0},{4,6},{6,4},{8,10},{10,8},{12,14},{14,12},{1,3},{3,1},... | collective-permute-start | bytes 1781768 | tf_op jit(solution)/shard_map/ppermute | solution.py:222
  78.8 33.8 %collective-permute-start.10 = (bf16[128,3712]{1,0:T(8,128)(2,1)S(1)}, bf16[128,3712]{1,0:T(8,128)(2,1)S(1)}, u32[]{:S(2)}, u32[]{:S(2)}) collective-permute-start(bf16[128,3712]{1,0:T(8,128)(2,1)S(1)} %get-tuple-element.43.refs_0_), channel_id=1, source_target_pairs={{4,0},{6,2},{5,1},{7,3},{20,16},{22,18},{21,17},{23,19}} | collective-permute-start | bytes 2850824 | tf_op jit(solution)/shard_map/ppermute | solution.py:219
  80.1 32.6 %collective-permute-start.11 = (bf16[128,3712]{1,0:T(8,128)(2,1)S(1)}, bf16[128,3712]{1,0:T(8,128)(2,1)S(1)}, u32[]{:S(2)}, u32[]{:S(2)}) collective-permute-start(bf16[128,3712]{1,0:T(8,128)(2,1)S(1)} %get-tuple-element.44.refs_1_), channel_id=1, source_target_pairs={{8,12},{10,14},{9,13},{11,15},{24,28},{26,30},{25,29},{27,31}} | collective-permute-start | bytes 2850824 | tf_op jit(solution)/shard_map/ppermute | solution.py:219
  90.1 16.0 %collective-permute-start.12 = (bf16[80,3584]{1,0:T(8,128)(2,1)S(1)}, bf16[80,3584]{1,0:T(8,128)(2,1)S(1)}, u32[]{:S(2)}, u32[]{:S(2)}) collective-permute-start(bf16[80,3584]{1,0:T(8,128)(2,1)S(1)} %get-tuple-element.51), channel_id=1, source_target_pairs={{0,2},{2,0},{4,6},{6,4},{8,10},{10,8},{12,14},{14,12},{1,3},{3,1},... | collective-permute-start | bytes 1720328 | tf_op jit(solution)/shard_map/ppermute | solution.py:222
  92.9 25.9 %collective-permute-start.14 = (bf16[80,3712]{1,0:T(8,128)(2,1)S(1)}, bf16[80,3712]{1,0:T(8,128)(2,1)S(1)}, u32[]{:S(2)}, u32[]{:S(2)}) collective-permute-start(bf16[80,3712]{1,0:T(8,128)(2,1)S(1)} %get-tuple-element.56), channel_id=1, source_target_pairs={{0,2},{2,0},{4,6},{6,4},{8,10},{10,8},{12,14},{14,12},{1,3},{3,1},... | collective-permute-start | bytes 1781768 | tf_op jit(solution)/shard_map/ppermute | solution.py:222
  106.7 23.4 %collective-permute-start.16 = (bf16[128,3584]{1,0:T(8,128)(2,1)S(1)}, bf16[128,3584]{1,0:T(8,128)(2,1)S(1)}, u32[]{:S(2)}, u32[]{:S(2)}) collective-permute-start(bf16[128,3584]{1,0:T(8,128)(2,1)S(1)} %shard_map.72.refs_4_), channel_id=1, source_target_pairs={{8,4},{10,6},{12,8},{14,10},{9,5},{11,7},{13,9},{15,11},{24,20},{2... | collective-permute-start | bytes 2752520 | tf_op jit(solution)/shard_map/ppermute | solution.py:219
  107.5 22.7 %collective-permute-start.17 = (bf16[128,3584]{1,0:T(8,128)(2,1)S(1)}, bf16[128,3584]{1,0:T(8,128)(2,1)S(1)}, u32[]{:S(2)}, u32[]{:S(2)}) collective-permute-start(bf16[128,3584]{1,0:T(8,128)(2,1)S(1)} %shard_map.72.refs_4_), channel_id=1, source_target_pairs={{0,4},{2,6},{4,8},{6,10},{1,5},{3,7},{5,9},{7,11},{16,20},{18,22},... | collective-permute-start | bytes 2752520 | tf_op jit(solution)/shard_map/ppermute | solution.py:219
  114.0 30.7 %collective-permute-start.13 = (bf16[80,3712]{1,0:T(8,128)(2,1)S(1)}, bf16[80,3712]{1,0:T(8,128)(2,1)S(1)}, u32[]{:S(2)}, u32[]{:S(2)}) collective-permute-start(bf16[80,3712]{1,0:T(8,128)(2,1)S(1)} %get-tuple-element.53), channel_id=1, source_target_pairs={{0,2},{2,0},{4,6},{6,4},{8,10},{10,8},{12,14},{14,12},{1,3},{3,1},... | collective-permute-start | bytes 1781768 | tf_op jit(solution)/shard_map/ppermute | solution.py:222
  128.1 16.0 %collective-permute-start.15 = (bf16[80,3584]{1,0:T(8,128)(2,1)S(1)}, bf16[80,3584]{1,0:T(8,128)(2,1)S(1)}, u32[]{:S(2)}, u32[]{:S(2)}) collective-permute-start(bf16[80,3584]{1,0:T(8,128)(2,1)S(1)} %get-tuple-element.59), channel_id=1, source_target_pairs={{0,2},{2,0},{4,6},{6,4},{8,10},{10,8},{12,14},{14,12},{1,3},{3,1},... | collective-permute-start | bytes 1720328 | tf_op jit(solution)/shard_map/ppermute | solution.py:222
  129.6 26.6 %collective-permute-start.9 = (bf16[80,3584]{1,0:T(8,128)(2,1)S(1)}, bf16[80,3584]{1,0:T(8,128)(2,1)S(1)}, u32[]{:S(2)}, u32[]{:S(2)}) collective-permute-start(bf16[80,3584]{1,0:T(8,128)(2,1)S(1)} %get-tuple-element.49), channel_id=1, source_target_pairs={{0,2},{2,0},{4,6},{6,4},{8,10},{10,8},{12,14},{14,12},{1,3},{3,1},... | collective-permute-start | bytes 1720328 | tf_op jit(solution)/shard_map/ppermute | solution.py:222
  153.9 11.9 %collective-permute-start.19 = (bf16[80,3584]{1,0:T(8,128)(2,1)S(1)}, bf16[80,3584]{1,0:T(8,128)(2,1)S(1)}, u32[]{:S(2)}, u32[]{:S(2)}) collective-permute-start(bf16[80,3584]{1,0:T(8,128)(2,1)S(1)} %get-tuple-element.62), channel_id=1, source_target_pairs={{0,2},{2,0},{4,6},{6,4},{8,10},{10,8},{12,14},{14,12},{1,3},{3,1},... | collective-permute-start | bytes 1720328 | tf_op jit(solution)/shard_map/ppermute | solution.py:222
  155.5 56.9 %collective-permute-start.18 = (bf16[128,3584]{1,0:T(8,128)(2,1)S(1)}, bf16[128,3584]{1,0:T(8,128)(2,1)S(1)}, u32[]{:S(2)}, u32[]{:S(2)}) collective-permute-start(bf16[128,3584]{1,0:T(8,128)(2,1)S(1)} %shard_map.75.refs_8_), channel_id=1, source_target_pairs={{0,8},{2,10},{4,12},{6,14},{8,0},{10,2},{12,4},{14,6},{1,9},{3,11}... | collective-permute-start | bytes 2752520 | tf_op jit(solution)/shard_map/ppermute | solution.py:219
  166.5 45.9 %collective-permute-start.20 = (bf16[128,3584]{1,0:T(8,128)(2,1)S(1)}, bf16[128,3584]{1,0:T(8,128)(2,1)S(1)}, u32[]{:S(2)}, u32[]{:S(2)}) collective-permute-start(bf16[128,3584]{1,0:T(8,128)(2,1)S(1)} %shard_map.78), channel_id=1, source_target_pairs={{8,12},{10,14},{12,0},{14,2},{9,13},{11,15},{13,1},{15,3},{24,28},... | collective-permute-start | bytes 2752520 | tf_op jit(solution)/shard_map/ppermute | solution.py:219
  167.8 57.9 %collective-permute-start.21 = (bf16[128,3584]{1,0:T(8,128)(2,1)S(1)}, bf16[128,3584]{1,0:T(8,128)(2,1)S(1)}, u32[]{:S(2)}, u32[]{:S(2)}) collective-permute-start(bf16[128,3584]{1,0:T(8,128)(2,1)S(1)} %shard_map.78), channel_id=1, source_target_pairs={{0,12},{2,14},{4,0},{6,2},{1,13},{3,15},{5,1},{7,3},{16,28},{18,30... | collective-permute-start | bytes 2752520 | tf_op jit(solution)/shard_map/ppermute | solution.py:219

commit v8 on v6

--- a/solution.py
+++ b/solution.py
@@ -57,12 +57,16 @@
 
 
 def first_kernel(experts, tokens, routes, scale, gate_w, up_w, block, *refs):
-    picked, (stack, sems) = refs[:4], refs[4:]
-    copies = [
-        pltpu.make_async_copy(gate_w, stack.at[0], sems.at[0]),
-        pltpu.make_async_copy(up_w, stack.at[1], sems.at[1]),
-    ]
-    for copy in copies:
+    picked, (stack, held, sems) = refs[:4], refs[4:]
+    pieces = sems.shape[2]
+    rows = gate_w.shape[0] // pieces
+    fetch, store = [], []
+    for k in range(pieces):
+        cut = pl.ds(k * rows, rows)
+        for n, source in enumerate((gate_w, up_w)):
+            fetch.append(pltpu.make_async_copy(source.at[cut], held.at[n, cut], sems.at[0, n, k]))
+            store.append(pltpu.make_async_copy(held.at[n, cut], stack.at[n, cut], sems.at[1, n, k]))
+    for copy in fetch:
         copy.start()
     count, width = tokens.shape
     lane = lax.broadcasted_iota(jnp.int32, (count, block.shape[1] - width), 1)
@@ -77,9 +81,17 @@
     marks = jnp.where(part == 0, high, jnp.where(part == 1, middle, jnp.where(part == 2, low, 0.0)))
     block[:, :width] = tokens[...]
     block[:, width:] = marks.astype(jnp.bfloat16)
+    for arrived, leaving in zip(fetch, store):
+        arrived.wait()
+        leaving.start()
     choose(block, *picked)
-    for copy in copies:
+    for copy in store:
         copy.wait()
+
+
+def passing_kernel(*refs):
+    for source, result in zip(refs, refs[len(refs) // 2 :]):
+        result[...] = source[...]
 
 
 def choose(held, own_map, other_map, own_rows, other_rows):
@@ -183,9 +195,11 @@
     size = min(hidden, 256)
     cap = -(-(5 * count // experts) // 16) * 16
     wide = width + -(-3 * experts // 128) * 128
+    hbm = functools.partial(pltpu.HBM, dtype=jnp.bfloat16)
     in_hbm = functools.partial(pltpu.with_memory_space_constraint, memory_space=pltpu.HBM)
     bf16 = functools.partial(jax.ShapeDtypeStruct, dtype=jnp.bfloat16)
 
+    own = (w_gate[0], w_up[0], w_down[0])
     block, *picked, stack = call(
         functools.partial(first_kernel, experts),
         [
@@ -194,16 +208,16 @@
             bf16((count, cap)),
             bf16((cap, wide)),
             bf16((cap, wide)),
-            bf16((2, width, hidden)),
+            hbm((2, width, hidden)),
         ],
-        [tokens, routes.T, route_scale.T, in_hbm(w_gate[0]), in_hbm(w_up[0])],
+        [*map(in_hbm, (tokens, routes.T, route_scale.T, own[0], own[1]))],
         (),
-        [pltpu.SemaphoreType.DMA((2,))],
+        [pltpu.VMEM((2, width, hidden), jnp.bfloat16), pltpu.SemaphoreType.DMA((2, 2, 4))],
         [IN_VMEM] * 3 + [ANYWHERE] * 2,
-        out_specs=[IN_VMEM] * 6,
+        out_specs=[IN_VMEM] * 5 + [ANYWHERE],
     )
     swap = functools.partial(lax.ppermute, axis_name="local", perm=[(0, 1), (1, 0)])
-    weights = [in_hbm(stack), swap(stack), in_hbm(w_down[0]), swap(w_down[0])]
+    weights = [in_hbm(stack), swap(stack), in_hbm(own[2]), swap(own[2])]
 
     def along(block, pairs):
         moves = [(2 * a + y, 2 * b + y) for a, b in pairs for y in range(2)]
@@ -265,9 +279,6 @@
             ]
             held[way, step] = along(held.get((way, step - 1), block), pairs)
 
-    def hold(step, until):
-        held[1, step], held[-1, step] = tied([held[1, step], held[-1, step]], until)
-
     def do_pick(slot, after=()):
         keys = sorted({row[slot - 1] for row in plan})
         blocks = [held[key] for key in keys]
@@ -291,23 +302,27 @@
 
     relay(1)
     picks[0] = picked[:2], picked[2], across(picked[3])
-    hold(1, [picks[0][2]])
+    held[1, 1], held[-1, 1] = tied([held[1, 1], held[-1, 1]], [picks[0][2]])
     relay(2)
     do_pick(1)
     do_expert(0)
-    hold(2, [picks[1][2], outs[0][0]])
+    held[1, 2], held[-1, 2] = call(
+        passing_kernel, [bf16((count, wide))] * 2, [held[1, 2], held[-1, 2]], [*last, picks[1][2], outs[0][1]]
+    )
     for step in range(3, places):
         relay(step)
     do_pick(2)
-    do_expert(1, after=[outs[0][1]])
-    total = ordered(spread, picks[0][0], *outs[0], after=[picks[2][2]])
+    do_expert(1)
     do_expert(2)
+    do_spread(1)
+    do_pick(3)
     for slot in range(3, places):
-        do_pick(slot)
-        do_spread(slot - 2)
         do_expert(slot)
-        do_spread(slot - 1)
-    do_spread(places - 1, after=returned[0])
+        do_spread(slot - 1, after=returned[slot - 3])
+        if slot + 1 < places:
+            do_pick(slot + 1)
+    total = ordered(spread, picks[0][0], *outs[0])
+    do_spread(places - 1)
     total = total.astype(jnp.float32)
     for block in sum(returned, []):
         total = total + block.astype(jnp.float32)

time: 205 us -> 201 us (0.980)
  local copies, waits for them, and re-layouts: 11.2 us -> 1.88 us
  starting transfers between devices: 36.9 us -> 40.9 us
    unnamed x40 -> x8, local copies, waits for them, and re-layouts: 11.2 us -> 1.88 us
    ppermute x11, waiting for transfers between devices: 62.9 us -> 70.3 us  [along(): return lax.ppermute(block, 'node', moves)]
    ppermute x8, waiting for transfers between devices: 42.5 us -> 35.9 us  [across(): return lax.ppermute(block, 'node', [(n, n ^ 1) for n in range(experts)])]
    ppermute x11, starting transfers between devices: 25.8 us -> 31.7 us  [along(): return lax.ppermute(block, 'node', moves)]
    pallas_call x12 -> x13, Pallas kernels: 49.4 us -> 50.1 us  [call(): pl.pallas_call(body, out_shape=outs, in_specs=specs, out_specs=out_specs...]
  transfers between devices with their start and end apart: 21 -> 21, of which waited for: 12 -> 13; matrix products, arithmetic and copies ran while one was open for 0% -> 0% of each run, Pallas kernels for 21% -> 21%
where the time goes in v8:
time: 201 us
  waiting for transfers between devices  106 us (53%)
  Pallas kernels  50.1 us (25%)
  starting transfers between devices  40.9 us (20%)
    ppermute x11, waiting for transfers between devices, along(): return lax.ppermute(block, 'node', moves)  70.3 us
    pallas_call x13, Pallas kernels, call(): pl.pallas_call(body, out_shape=outs, in_specs=specs, out_specs=out_specs...  50.1 us
    ppermute x8, waiting for transfers between devices, across(): return lax.ppermute(block, 'node', [(n, n ^ 1) for n in range(experts)])  35.9 us
    ppermute x11, starting transfers between devices, along(): return lax.ppermute(block, 'node', moves)  31.7 us
    ppermute x8, starting transfers between devices, across(): return lax.ppermute(block, 'node', [(n, n ^ 1) for n in range(experts)])  8.67 us
  transfers between devices with their start and end apart: 21, of which 13 were waited for; matrix products, arithmetic and copies ran while one was open for 0% of the time, Pallas kernels for 21%

profile of v8, /device:TPU:0, one launch (start us, length us, event | category | flops | bytes accessed | tf_op | source)
XLA Modules:
  0.0 200.8 jit_solution(11247206083311204767)
XLA Ops:
  0.0 7.3 %shard_map.64 = (bf16[128,3712]{1,0:T(8,128)(2,1)S(1)}, bf16[128,80]{1,0:T(8,128)(2,1)S(1)}, bf16[128,80]{1,0:T(8,128)(2,1)S(1)}, bf16[80,3712]{1,0:T(8,128)(2,1...) custom-call(bf16[128,3584]{1,0:T(8,128)(2,1)} %tokens.1, s32[2,128]{1,0:T(2,128)} %bitcast.7, ...), custom_call_target="tpu_custom_call" | custom-call | tf_op jit(solution)/shard_map/pallas_call | solution.py:33
  7.3 0.0 copy-start.2
  7.3 0.8 copy-done.2
  8.1 0.5 collective-permute-start.1
  8.6 0.1 collective-permute-start.2
  8.6 5.0 %collective-permute-start.3 = (bf16[128,3712]{1,0:T(8,128)(2,1)S(1)}, bf16[128,3712]{1,0:T(8,128)(2,1)S(1)}, u32[]{:S(2)}, u32[]{:S(2)}) collective-permute-start(bf16[128,3712]{1,0:T(8,128)(2,1)S(1)} %get-tuple-element.40), channel_id=1, source_target_pairs={{0,4},{2,6},{4,8},{6,10},{8,12},{10,14},{1,5},{3,7},{5,9},{7,11},{... | collective-permute-start | bytes 2850824 | tf_op jit(solution)/shard_map/ppermute | solution.py:224
  13.6 1.3 collective-permute-start.4
  14.9 1.6 collective-permute-start
  16.5 13.5 %collective-permute-done.refs_2_.refs_1_ = bf16[80,3712]{1,0:T(8,128)(2,1)S(1)} collective-permute-done((bf16[80,3712]{1,0:T(8,128)(2,1)S(1)}, bf16[80,3712]{1,0:T(8,128)(2,1)S(1)}, u32[]{:S(2)}, u32[]{:S(2)}) %collective-permute-start) | collective-permute-done | bytes 593952 | tf_op jit(solution)/shard_map/ppermute | solution.py:227
  30.0 0.0 copy-start
  30.0 4.0 %collective-permute-done.3.refs_0_ = bf16[128,3712]{1,0:T(8,128)(2,1)S(1)} collective-permute-done((bf16[128,3712]{1,0:T(8,128)(2,1)S(1)}, bf16[128,3712]{1,0:T(8,128)(2,1)S(1)}, u32[]{:S(2)}, u32[]{:S(2)}) %collective-permute-start.3) | collective-permute-done | bytes 950304 | tf_op jit(solution)/shard_map/ppermute | solution.py:224
  34.0 4.2 %collective-permute-done.4.refs_1_ = bf16[128,3712]{1,0:T(8,128)(2,1)S(1)} collective-permute-done((bf16[128,3712]{1,0:T(8,128)(2,1)S(1)}, bf16[128,3712]{1,0:T(8,128)(2,1)S(1)}, u32[]{:S(2)}, u32[]{:S(2)}) %collective-permute-start.4) | collective-permute-done | bytes 950304 | tf_op jit(solution)/shard_map/ppermute | solution.py:224
  38.2 0.0 copy-done
  38.2 0.0 copy-start.1
  38.2 0.8 collective-permute-start.6
  39.1 1.3 collective-permute-start.7
  40.4 1.0 shard_map.66
  41.4 1.6 collective-permute-start.8
  43.0 0.0 collective-permute-done.2.refs_5_
  43.0 0.0 collective-permute-done.1.refs_3_
  43.0 0.0 copy-done.1
  43.0 0.0 copy-start.3
  43.0 1.1 copy-done.3
  44.1 9.2 %shard_map.67 = (bf16[80,3584]{1,0:T(8,128)(2,1)S(1)}, bf16[80,3584]{1,0:T(8,128)(2,1)S(1)}) custom-call(bf16[80,3712]{1,0:T(8,128)(2,1)S(1)} %copy-done.3, bf16[80,3712]{1,0:T(8,128)(2,1)S(1)} %copy-done.1, bf16[2,3584,512]{2,1,0:T(8,128)(2,1)} %get-tuple-element.39.refs_2_, bf16[2,3584,512]{2,1,0:T(8,128)(2,1)} %collective-permute-done.1.refs_3_, ...), custom_call_target="tpu_custom_call" | custom-call | tf_op jit(solution)/shard_map/pallas_call | solution.py:33
  53.3 0.6 collective-permute-start.5
  53.9 2.8 %collective-permute-done.8.refs_3_.refs_1_ = bf16[80,3712]{1,0:T(8,128)(2,1)S(1)} collective-permute-done((bf16[80,3712]{1,0:T(8,128)(2,1)S(1)}, bf16[80,3712]{1,0:T(8,128)(2,1)S(1)}, u32[]{:S(2)}, u32[]{:S(2)}) %collective-permute-start.8) | collective-permute-done | bytes 593952 | tf_op jit(solution)/shard_map/ppermute | solution.py:227
  56.7 0.0 collective-permute-done.6.refs_0_
  56.7 8.3 %collective-permute-done.7.refs_1_ = bf16[128,3712]{1,0:T(8,128)(2,1)S(1)} collective-permute-done((bf16[128,3712]{1,0:T(8,128)(2,1)S(1)}, bf16[128,3712]{1,0:T(8,128)(2,1)S(1)}, u32[]{:S(2)}, u32[]{:S(2)}) %collective-permute-start.7) | collective-permute-done | bytes 950304 | tf_op jit(solution)/shard_map/ppermute | solution.py:224
  65.1 2.8 %collective-permute-done.5.refs_4_.refs_3_ = bf16[80,3584]{1,0:T(8,128)(2,1)S(1)} collective-permute-done((bf16[80,3584]{1,0:T(8,128)(2,1)S(1)}, bf16[80,3584]{1,0:T(8,128)(2,1)S(1)}, u32[]{:S(2)}, u32[]{:S(2)}) %collective-permute-start.5) | collective-permute-done | bytes 573472 | tf_op jit(solution)/shard_map/ppermute | solution.py:227
  67.9 0.1 shard_map.68
  68.0 1.3 collective-permute-start.11
  69.3 0.7 collective-permute-start.12
  70.1 1.2 shard_map.69
  71.3 1.6 collective-permute-start.9
  72.9 9.2 %shard_map.70 = (bf16[80,3584]{1,0:T(8,128)(2,1)S(1)}, bf16[80,3584]{1,0:T(8,128)(2,1)S(1)}) custom-call(bf16[80,3712]{1,0:T(8,128)(2,1)S(1)} %get-tuple-element.53.refs_0_, bf16[80,3712]{1,0:T(8,128)(2,1)S(1)} %collective-permute-done.8.refs_3_.refs_1_, bf16[2,3584,512]{2,1,0:T(8,128)(2,1)} %get-tuple-element.39.refs_2_, ...), custom_call_target="tpu_custom_call" | custom-call | tf_op jit(solution)/shard_map/pallas_call | solution.py:33
  82.1 0.6 collective-permute-start.13
  82.7 5.0 %collective-permute-done.9.refs_1_ = bf16[80,3712]{1,0:T(8,128)(2,1)S(1)} collective-permute-done((bf16[80,3712]{1,0:T(8,128)(2,1)S(1)}, bf16[80,3712]{1,0:T(8,128)(2,1)S(1)}, u32[]{:S(2)}, u32[]{:S(2)}) %collective-permute-start.9) | collective-permute-done | bytes 593952 | tf_op jit(solution)/shard_map/ppermute | solution.py:227
  87.7 9.2 %shard_map.71 = (bf16[80,3584]{1,0:T(8,128)(2,1)S(1)}, bf16[80,3584]{1,0:T(8,128)(2,1)S(1)}) custom-call(bf16[80,3712]{1,0:T(8,128)(2,1)S(1)} %get-tuple-element.51.refs_0_, bf16[80,3712]{1,0:T(8,128)(2,1)S(1)} %collective-permute-done.9.refs_1_, bf16[2,3584,512]{2,1,0:T(8,128)(2,1)} %get-tuple-element.39.refs_2_, ...), custom_call_target="tpu_custom_call" | custom-call | tf_op jit(solution)/shard_map/pallas_call | solution.py:33
  96.9 0.8 collective-permute-done.13.refs_3_
  97.7 0.6 shard_map.72.refs_4_
  98.3 0.0 collective-permute-done.11.refs_1_
  98.3 0.0 collective-permute-done.12.refs_3_
  98.3 1.0 shard_map.73
  99.4 0.9 collective-permute-start.14
  100.3 0.7 collective-permute-start.15
  101.0 7.5 %collective-permute-start.16 = (bf16[128,3584]{1,0:T(8,128)(2,1)S(1)}, bf16[128,3584]{1,0:T(8,128)(2,1)S(1)}, u32[]{:S(2)}, u32[]{:S(2)}) collective-permute-start(bf16[128,3584]{1,0:T(8,128)(2,1)S(1)} %shard_map.72.refs_4_), channel_id=1, source_target_pairs={{0,4},{2,6},{4,8},{6,10},{1,5},{3,7},{5,9},{7,11},{16,20},{18,22},... | collective-permute-start | bytes 2752520 | tf_op jit(solution)/shard_map/ppermute | solution.py:224
  108.5 1.0 collective-permute-start.10
  109.5 6.3 %collective-permute-done.14.refs_1_ = bf16[80,3712]{1,0:T(8,128)(2,1)S(1)} collective-permute-done((bf16[80,3712]{1,0:T(8,128)(2,1)S(1)}, bf16[80,3712]{1,0:T(8,128)(2,1)S(1)}, u32[]{:S(2)}, u32[]{:S(2)}) %collective-permute-start.14) | collective-permute-done | bytes 593952 | tf_op jit(solution)/shard_map/ppermute | solution.py:227
  115.8 9.2 %shard_map.74 = (bf16[80,3584]{1,0:T(8,128)(2,1)S(1)}, bf16[80,3584]{1,0:T(8,128)(2,1)S(1)}) custom-call(bf16[80,3712]{1,0:T(8,128)(2,1)S(1)} %get-tuple-element.59.refs_0_, bf16[80,3712]{1,0:T(8,128)(2,1)S(1)} %collective-permute-done.14.refs_1_, bf16[2,3584,512]{2,1,0:T(8,128)(2,1)} %get-tuple-element.39.refs_2_, ...), custom_call_target="tpu_custom_call" | custom-call | tf_op jit(solution)/shard_map/pallas_call | solution.py:33
  125.0 0.9 collective-permute-start.18
  125.9 2.2 %collective-permute-done.10.refs_3_ = bf16[80,3584]{1,0:T(8,128)(2,1)S(1)} collective-permute-done((bf16[80,3584]{1,0:T(8,128)(2,1)S(1)}, bf16[80,3584]{1,0:T(8,128)(2,1)S(1)}, u32[]{:S(2)}, u32[]{:S(2)}) %collective-permute-start.10) | collective-permute-done | bytes 573472 | tf_op jit(solution)/shard_map/ppermute | solution.py:227
  128.1 0.0 collective-permute-done.15.refs_5_
  128.1 0.0 collective-permute-done.16.refs_6_
  128.1 0.6 shard_map.75.refs_4_
  128.7 5.5 %collective-permute-start.17 = (bf16[128,3584]{1,0:T(8,128)(2,1)S(1)}, bf16[128,3584]{1,0:T(8,128)(2,1)S(1)}, u32[]{:S(2)}, u32[]{:S(2)}) collective-permute-start(bf16[128,3584]{1,0:T(8,128)(2,1)S(1)} %shard_map.75.refs_4_), channel_id=1, source_target_pairs={{0,8},{2,10},{4,12},{6,14},{8,0},{10,2},{12,4},{14,6},{1,9},{3,11}... | collective-permute-start | bytes 2752520 | tf_op jit(solution)/shard_map/ppermute | solution.py:224
  134.2 0.6 shard_map.76.refs_4_
  134.8 2.4 %collective-permute-done.18.refs_3_ = bf16[80,3584]{1,0:T(8,128)(2,1)S(1)} collective-permute-done((bf16[80,3584]{1,0:T(8,128)(2,1)S(1)}, bf16[80,3584]{1,0:T(8,128)(2,1)S(1)}, u32[]{:S(2)}, u32[]{:S(2)}) %collective-permute-start.18) | collective-permute-done | bytes 573472 | tf_op jit(solution)/shard_map/ppermute | solution.py:227
  137.2 0.6 shard_map.77
  137.8 1.3 collective-permute-start.19
  139.1 6.3 %collective-permute-start.20 = (bf16[128,3584]{1,0:T(8,128)(2,1)S(1)}, bf16[128,3584]{1,0:T(8,128)(2,1)S(1)}, u32[]{:S(2)}, u32[]{:S(2)}) collective-permute-start(bf16[128,3584]{1,0:T(8,128)(2,1)S(1)} %shard_map.77), channel_id=1, source_target_pairs={{0,12},{2,14},{4,0},{6,2},{1,13},{3,15},{5,1},{7,3},{16,28},{18,30... | collective-permute-start | bytes 2752520 | tf_op jit(solution)/shard_map/ppermute | solution.py:224
  145.5 42.4 %collective-permute-done.17 = bf16[128,3584]{1,0:T(8,128)(2,1)S(1)} collective-permute-done((bf16[128,3584]{1,0:T(8,128)(2,1)S(1)}, bf16[128,3584]{1,0:T(8,128)(2,1)S(1)}, u32[]{:S(2)}, u32[]{:S(2)}) %collective-permute-start.17) | collective-permute-done | bytes 917536 | tf_op jit(solution)/shard_map/ppermute | solution.py:224
  187.9 0.0 collective-permute-done.19
  187.9 11.3 %collective-permute-done.20 = bf16[128,3584]{1,0:T(8,128)(2,1)S(1)} collective-permute-done((bf16[128,3584]{1,0:T(8,128)(2,1)S(1)}, bf16[128,3584]{1,0:T(8,128)(2,1)S(1)}, u32[]{:S(2)}, u32[]{:S(2)}) %collective-permute-start.20) | collective-permute-done | bytes 917536 | tf_op jit(solution)/shard_map/ppermute | solution.py:224
  199.2 1.6 add_convert_fusion
  (1 shorter events, 0.0 us)
Async XLA Ops:
  7.3 0.8 copy-start.2
  8.1 34.9 %collective-permute-start.1 = (bf16[2,3584,512]{2,1,0:T(8,128)(2,1)}, bf16[2,3584,512]{2,1,0:T(8,128)(2,1)}, u32[]{:S(2)}, u32[]{:S(2)}) collective-permute-start(bf16[2,3584,512]{2,1,0:T(8,128)(2,1)} %get-tuple-element.39.refs_2_), channel_id=1, source_target_pairs={{0,1},{1,0},{2,3},{3,2},{4,5},{5,4},{6,7},{7,6},{8,9},{9,8},{10,11... | collective-permute-start | bytes 22020104 | tf_op jit(solution)/shard_map/ppermute | solution.py:220
  8.6 34.4 %collective-permute-start.2 = (bf16[512,3584]{1,0:T(8,128)(2,1)}, bf16[512,3584]{1,0:T(8,128)(2,1)}, u32[]{:S(2)}, u32[]{:S(2)}) collective-permute-start(bf16[512,3584]{1,0:T(8,128)(2,1)} %bitcast.4.refs_4_), channel_id=1, source_target_pairs={{0,1},{1,0},{2,3},{3,2},{4,5},{5,4},{6,7},{7,6},{8,9},{9,8},{10,11... | collective-permute-start | bytes 11010056 | tf_op jit(solution)/shard_map/ppermute | solution.py:220
  8.6 25.4 %collective-permute-start.3 = (bf16[128,3712]{1,0:T(8,128)(2,1)S(1)}, bf16[128,3712]{1,0:T(8,128)(2,1)S(1)}, u32[]{:S(2)}, u32[]{:S(2)}) collective-permute-start(bf16[128,3712]{1,0:T(8,128)(2,1)S(1)} %get-tuple-element.40), channel_id=1, source_target_pairs={{0,4},{2,6},{4,8},{6,10},{8,12},{10,14},{1,5},{3,7},{5,9},{7,11},{... | collective-permute-start | bytes 2850824 | tf_op jit(solution)/shard_map/ppermute | solution.py:224
  13.6 24.6 %collective-permute-start.4 = (bf16[128,3712]{1,0:T(8,128)(2,1)S(1)}, bf16[128,3712]{1,0:T(8,128)(2,1)S(1)}, u32[]{:S(2)}, u32[]{:S(2)}) collective-permute-start(bf16[128,3712]{1,0:T(8,128)(2,1)S(1)} %get-tuple-element.40), channel_id=1, source_target_pairs={{4,0},{6,2},{8,4},{10,6},{12,8},{14,10},{5,1},{7,3},{9,5},{11,7},{... | collective-permute-start | bytes 2850824 | tf_op jit(solution)/shard_map/ppermute | solution.py:224
  14.9 15.1 %collective-permute-start = (bf16[80,3712]{1,0:T(8,128)(2,1)S(1)}, bf16[80,3712]{1,0:T(8,128)(2,1)S(1)}, u32[]{:S(2)}, u32[]{:S(2)}) collective-permute-start(bf16[80,3712]{1,0:T(8,128)(2,1)S(1)} %get-tuple-element.38), channel_id=1, source_target_pairs={{0,2},{2,0},{4,6},{6,4},{8,10},{10,8},{12,14},{14,12},{1,3},{3,1},... | collective-permute-start | bytes 1781768 | tf_op jit(solution)/shard_map/ppermute | solution.py:227
  30.0 8.2 %copy-start = (bf16[80,3712]{1,0:T(8,128)(2,1)}, bf16[80,3712]{1,0:T(8,128)(2,1)S(1)}, u32[]{:S(2)}) copy-start(bf16[80,3712]{1,0:T(8,128)(2,1)S(1)} %collective-permute-done.refs_2_.refs_1_) | copy-start | bytes 1781764
  38.2 4.8 %copy-start.1 = (bf16[80,3712]{1,0:T(8,128)(2,1)S(1)}, bf16[80,3712]{1,0:T(8,128)(2,1)}, u32[]{:S(2)}) copy-start(bf16[80,3712]{1,0:T(8,128)(2,1)} %copy-done) | copy-start | bytes 1781764
  38.2 18.5 %collective-permute-start.6 = (bf16[128,3712]{1,0:T(8,128)(2,1)S(1)}, bf16[128,3712]{1,0:T(8,128)(2,1)S(1)}, u32[]{:S(2)}, u32[]{:S(2)}) collective-permute-start(bf16[128,3712]{1,0:T(8,128)(2,1)S(1)} %get-tuple-element.42.refs_1_.refs_2_), channel_id=1, source_target_pairs={{4,8},{6,10},{8,12},{10,14},{5,9},{7,11},{9,13},{11,15},{20,24},{2... | collective-permute-start | bytes 2850824 | tf_op jit(solution)/shard_map/ppermute | solution.py:224
  39.1 26.0 %collective-permute-start.7 = (bf16[128,3712]{1,0:T(8,128)(2,1)S(1)}, bf16[128,3712]{1,0:T(8,128)(2,1)S(1)}, u32[]{:S(2)}, u32[]{:S(2)}) collective-permute-start(bf16[128,3712]{1,0:T(8,128)(2,1)S(1)} %get-tuple-element.41.refs_0_), channel_id=1, source_target_pairs={{4,0},{6,2},{8,4},{10,6},{5,1},{7,3},{9,5},{11,7},{20,16},{22,18},... | collective-permute-start | bytes 2850824 | tf_op jit(solution)/shard_map/ppermute | solution.py:224
  41.4 15.3 %collective-permute-start.8 = (bf16[80,3712]{1,0:T(8,128)(2,1)S(1)}, bf16[80,3712]{1,0:T(8,128)(2,1)S(1)}, u32[]{:S(2)}, u32[]{:S(2)}) collective-permute-start(bf16[80,3712]{1,0:T(8,128)(2,1)S(1)} %get-tuple-element.46), channel_id=1, source_target_pairs={{0,2},{2,0},{4,6},{6,4},{8,10},{10,8},{12,14},{14,12},{1,3},{3,1},... | collective-permute-start | bytes 1781768 | tf_op jit(solution)/shard_map/ppermute | solution.py:227
  43.0 1.1 copy-start.3
  53.3 14.6 %collective-permute-start.5 = (bf16[80,3584]{1,0:T(8,128)(2,1)S(1)}, bf16[80,3584]{1,0:T(8,128)(2,1)S(1)}, u32[]{:S(2)}, u32[]{:S(2)}) collective-permute-start(bf16[80,3584]{1,0:T(8,128)(2,1)S(1)} %get-tuple-element.45), channel_id=1, source_target_pairs={{0,2},{2,0},{4,6},{6,4},{8,10},{10,8},{12,14},{14,12},{1,3},{3,1},... | collective-permute-start | bytes 1720328 | tf_op jit(solution)/shard_map/ppermute | solution.py:227
  68.0 30.3 %collective-permute-start.11 = (bf16[128,3712]{1,0:T(8,128)(2,1)S(1)}, bf16[128,3712]{1,0:T(8,128)(2,1)S(1)}, u32[]{:S(2)}, u32[]{:S(2)}) collective-permute-start(bf16[128,3712]{1,0:T(8,128)(2,1)S(1)} %get-tuple-element.47.refs_0_), channel_id=1, source_target_pairs={{4,0},{6,2},{5,1},{7,3},{20,16},{22,18},{21,17},{23,19}} | collective-permute-start | bytes 2850824 | tf_op jit(solution)/shard_map/ppermute | solution.py:224
  69.3 29.0 %collective-permute-start.12 = (bf16[128,3712]{1,0:T(8,128)(2,1)S(1)}, bf16[128,3712]{1,0:T(8,128)(2,1)S(1)}, u32[]{:S(2)}, u32[]{:S(2)}) collective-permute-start(bf16[128,3712]{1,0:T(8,128)(2,1)S(1)} %get-tuple-element.48.refs_1_), channel_id=1, source_target_pairs={{8,12},{10,14},{9,13},{11,15},{24,28},{26,30},{25,29},{27,31}} | collective-permute-start | bytes 2850824 | tf_op jit(solution)/shard_map/ppermute | solution.py:224
  71.3 16.4 %collective-permute-start.9 = (bf16[80,3712]{1,0:T(8,128)(2,1)S(1)}, bf16[80,3712]{1,0:T(8,128)(2,1)S(1)}, u32[]{:S(2)}, u32[]{:S(2)}) collective-permute-start(bf16[80,3712]{1,0:T(8,128)(2,1)S(1)} %get-tuple-element.52), channel_id=1, source_target_pairs={{0,2},{2,0},{4,6},{6,4},{8,10},{10,8},{12,14},{14,12},{1,3},{3,1},... | collective-permute-start | bytes 1781768 | tf_op jit(solution)/shard_map/ppermute | solution.py:227
  82.1 15.6 %collective-permute-start.13 = (bf16[80,3584]{1,0:T(8,128)(2,1)S(1)}, bf16[80,3584]{1,0:T(8,128)(2,1)S(1)}, u32[]{:S(2)}, u32[]{:S(2)}) collective-permute-start(bf16[80,3584]{1,0:T(8,128)(2,1)S(1)} %get-tuple-element.58), channel_id=1, source_target_pairs={{0,2},{2,0},{4,6},{6,4},{8,10},{10,8},{12,14},{14,12},{1,3},{3,1},... | collective-permute-start | bytes 1720328 | tf_op jit(solution)/shard_map/ppermute | solution.py:227
  99.4 16.4 %collective-permute-start.14 = (bf16[80,3712]{1,0:T(8,128)(2,1)S(1)}, bf16[80,3712]{1,0:T(8,128)(2,1)S(1)}, u32[]{:S(2)}, u32[]{:S(2)}) collective-permute-start(bf16[80,3712]{1,0:T(8,128)(2,1)S(1)} %get-tuple-element.60), channel_id=1, source_target_pairs={{0,2},{2,0},{4,6},{6,4},{8,10},{10,8},{12,14},{14,12},{1,3},{3,1},... | collective-permute-start | bytes 1781768 | tf_op jit(solution)/shard_map/ppermute | solution.py:227
  100.3 27.8 %collective-permute-start.15 = (bf16[128,3584]{1,0:T(8,128)(2,1)S(1)}, bf16[128,3584]{1,0:T(8,128)(2,1)S(1)}, u32[]{:S(2)}, u32[]{:S(2)}) collective-permute-start(bf16[128,3584]{1,0:T(8,128)(2,1)S(1)} %shard_map.72.refs_4_), channel_id=1, source_target_pairs={{8,4},{10,6},{12,8},{14,10},{9,5},{11,7},{13,9},{15,11},{24,20},{2... | collective-permute-start | bytes 2752520 | tf_op jit(solution)/shard_map/ppermute | solution.py:224
  101.0 27.1 %collective-permute-start.16 = (bf16[128,3584]{1,0:T(8,128)(2,1)S(1)}, bf16[128,3584]{1,0:T(8,128)(2,1)S(1)}, u32[]{:S(2)}, u32[]{:S(2)}) collective-permute-start(bf16[128,3584]{1,0:T(8,128)(2,1)S(1)} %shard_map.72.refs_4_), channel_id=1, source_target_pairs={{0,4},{2,6},{4,8},{6,10},{1,5},{3,7},{5,9},{7,11},{16,20},{18,22},... | collective-permute-start | bytes 2752520 | tf_op jit(solution)/shard_map/ppermute | solution.py:224
  108.5 19.6 %collective-permute-start.10 = (bf16[80,3584]{1,0:T(8,128)(2,1)S(1)}, bf16[80,3584]{1,0:T(8,128)(2,1)S(1)}, u32[]{:S(2)}, u32[]{:S(2)}) collective-permute-start(bf16[80,3584]{1,0:T(8,128)(2,1)S(1)} %get-tuple-element.56), channel_id=1, source_target_pairs={{0,2},{2,0},{4,6},{6,4},{8,10},{10,8},{12,14},{14,12},{1,3},{3,1},... | collective-permute-start | bytes 1720328 | tf_op jit(solution)/shard_map/ppermute | solution.py:227
  125.0 12.1 %collective-permute-start.18 = (bf16[80,3584]{1,0:T(8,128)(2,1)S(1)}, bf16[80,3584]{1,0:T(8,128)(2,1)S(1)}, u32[]{:S(2)}, u32[]{:S(2)}) collective-permute-start(bf16[80,3584]{1,0:T(8,128)(2,1)S(1)} %get-tuple-element.64), channel_id=1, source_target_pairs={{0,2},{2,0},{4,6},{6,4},{8,10},{10,8},{12,14},{14,12},{1,3},{3,1},... | collective-permute-start | bytes 1720328 | tf_op jit(solution)/shard_map/ppermute | solution.py:227
  128.7 59.2 %collective-permute-start.17 = (bf16[128,3584]{1,0:T(8,128)(2,1)S(1)}, bf16[128,3584]{1,0:T(8,128)(2,1)S(1)}, u32[]{:S(2)}, u32[]{:S(2)}) collective-permute-start(bf16[128,3584]{1,0:T(8,128)(2,1)S(1)} %shard_map.75.refs_4_), channel_id=1, source_target_pairs={{0,8},{2,10},{4,12},{6,14},{8,0},{10,2},{12,4},{14,6},{1,9},{3,11}... | collective-permute-start | bytes 2752520 | tf_op jit(solution)/shard_map/ppermute | solution.py:224
  137.8 50.1 %collective-permute-start.19 = (bf16[128,3584]{1,0:T(8,128)(2,1)S(1)}, bf16[128,3584]{1,0:T(8,128)(2,1)S(1)}, u32[]{:S(2)}, u32[]{:S(2)}) collective-permute-start(bf16[128,3584]{1,0:T(8,128)(2,1)S(1)} %shard_map.77), channel_id=1, source_target_pairs={{8,12},{10,14},{12,0},{14,2},{9,13},{11,15},{13,1},{15,3},{24,28},... | collective-permute-start | bytes 2752520 | tf_op jit(solution)/shard_map/ppermute | solution.py:224
  139.1 60.1 %collective-permute-start.20 = (bf16[128,3584]{1,0:T(8,128)(2,1)S(1)}, bf16[128,3584]{1,0:T(8,128)(2,1)S(1)}, u32[]{:S(2)}, u32[]{:S(2)}) collective-permute-start(bf16[128,3584]{1,0:T(8,128)(2,1)S(1)} %shard_map.77), channel_id=1, source_target_pairs={{0,12},{2,14},{4,0},{6,2},{1,13},{3,15},{5,1},{7,3},{16,28},{18,30... | collective-permute-start | bytes 2752520 | tf_op jit(solution)/shard_map/ppermute | solution.py:224

commit v9 on v8

--- a/solution.py
+++ b/solution.py
@@ -21,7 +21,7 @@
     return plan
 
 
-def call(kernel, outs, ins, after=(), scratch=(), specs=None, vmem=16, out_specs=None):
+def call(kernel, outs, ins, after=(), scratch=(), specs=None, vmem=16, out_specs=None, cost=0):
     body = kernel
     if after:
         first, last = len(ins), len(ins) + len(after)
@@ -37,7 +37,7 @@
         out_specs=out_specs or [IN_VMEM] * len(outs),
         scratch_shapes=scratch,
         compiler_params=pltpu.CompilerParams(vmem_limit_bytes=vmem * MIB),
-        cost_estimate=pl.CostEstimate(flops=0, bytes_accessed=0, transcendentals=0),
+        cost_estimate=pl.CostEstimate(flops=0, bytes_accessed=cost, transcendentals=0),
     )(*ins, *after)
 
 
@@ -187,6 +187,13 @@
     result[...] = total.astype(jnp.bfloat16)
 
 
+def sum_kernel(*refs):
+    total = refs[0][...].astype(jnp.float32)
+    for extra in refs[1:-1]:
+        total += extra[...].astype(jnp.float32)
+    refs[-1][...] = total.astype(jnp.bfloat16)
+
+
 def on_device(tokens, routes, route_scale, w_gate, w_up, w_down):
     count, width = tokens.shape
     experts = lax.axis_size("node")
@@ -263,8 +270,8 @@
 
     last = []
 
-    def ordered(function, *args, after=()):
-        out = function(*args, after=(*last, *after))
+    def ordered(function, *args, after=(), **options):
+        out = function(*args, after=(*last, *after), **options)
         last[:] = [out[0] if isinstance(out, (list, tuple)) else out]
         return out
 
@@ -290,9 +297,22 @@
         own_out, other_out = ordered(expert, picks[slot][1], picks[slot][2], after=after)
         outs[slot] = own_out, across(other_out)
 
+    def origin(place, slot):
+        way, step = plan[place][slot - 1]
+        return place - way * step
+
+    hops = []
+    for place in range(places):
+        target = origin(place, places - 1)
+        near = place + (1 if target > place else -1)
+        if near != target and origin(near, places - 2) == target:
+            hops.append((place, near))
+    staying = {places - 1: [a for a, _ in hops], places - 2: [b for _, b in hops]}
+    kept = {}
+
     def do_spread(slot, after=()):
-        done = ordered(spread, picks[slot][0], *outs[slot], after=after)
-        home = [(a, a - row[slot - 1][0] * row[slot - 1][1]) for a, row in enumerate(plan)]
+        kept[slot] = done = ordered(spread, picks[slot][0], *outs[slot], after=after)
+        home = [(a, origin(a, slot)) for a in range(places) if a not in staying.get(slot, ())]
         rounds = []
         while home:
             now = list({b: (a, b) for a, b in home}.values())
@@ -300,29 +320,36 @@
             rounds.append(along(done, now))
         returned.append(rounds)
 
+    def call_sum(blocks, after=(), cost=0):
+        return call(sum_kernel, [bf16((count, width))], blocks, after, cost=cost)
+
     relay(1)
     picks[0] = picked[:2], picked[2], across(picked[3])
     held[1, 1], held[-1, 1] = tied([held[1, 1], held[-1, 1]], [picks[0][2]])
     relay(2)
     do_pick(1)
-    do_expert(0)
+    do_expert(1)
     held[1, 2], held[-1, 2] = call(
-        passing_kernel, [bf16((count, wide))] * 2, [held[1, 2], held[-1, 2]], [*last, picks[1][2], outs[0][1]]
+        passing_kernel, [bf16((count, wide))] * 2, [held[1, 2], held[-1, 2]], [*last, picks[1][2]]
     )
     for step in range(3, places):
         relay(step)
     do_pick(2)
-    do_expert(1)
-    do_expert(2)
     do_spread(1)
     do_pick(3)
+    do_expert(2)
     for slot in range(3, places):
         do_expert(slot)
         do_spread(slot - 1, after=returned[slot - 3])
         if slot + 1 < places:
             do_pick(slot + 1)
+    do_expert(0)
+    do_spread(places - 1)
+    near = returned.pop(places - 3)
+    (summed,) = ordered(call_sum, [*returned.pop(0), *near] if places > 3 else near, cost=128 * MIB)
+    (joined,) = ordered(call_sum, [kept[places - 2], along(kept[places - 1], hops)])
+    returned.append([summed, along(joined, [(q, origin(q, places - 2)) for _, q in hops])])
     total = ordered(spread, picks[0][0], *outs[0])
-    do_spread(places - 1)
     total = total.astype(jnp.float32)
     for block in sum(returned, []):
         total = total + block.astype(jnp.float32)

time: 201 us -> 180 us (0.90)
  waiting for transfers between devices: 106 us -> 89.1 us
  starting transfers between devices: 40.9 us -> 37.9 us
    ppermute x11 -> x12, waiting for transfers between devices: 70.3 us -> 39.2 us  [along(): return lax.ppermute(block, 'node', moves)]
    ppermute x8, waiting for transfers between devices: 35.9 us -> 49.9 us  [across(): return lax.ppermute(block, 'node', [(n, n ^ 1) for n in range(experts)])]
    ppermute x11 -> x12, starting transfers between devices: 31.7 us -> 25.8 us  [along(): return lax.ppermute(block, 'node', moves)]
    ppermute x8, starting transfers between devices: 8.67 us -> 11.6 us  [across(): return lax.ppermute(block, 'node', [(n, n ^ 1) for n in range(experts)])]
    pallas_call x13 -> x15, Pallas kernels: 50.1 us -> 50.4 us  [call(): pl.pallas_call(body, out_shape=outs, in_specs=specs, out_specs=out_specs...]
  transfers between devices with their start and end apart: 21 -> 22, of which waited for: 13 -> 13; matrix products, arithmetic and copies ran while one was open for 0% -> 0% of each run, Pallas kernels for 21% -> 24%
where the time goes in v9:
time: 180 us
  waiting for transfers between devices  89.1 us (50%)
  Pallas kernels  50.4 us (28%)
  starting transfers between devices  37.9 us (21%)
    pallas_call x15, Pallas kernels, call(): pl.pallas_call(body, out_shape=outs, in_specs=specs, out_specs=out_specs...  50.4 us
    ppermute x8, waiting for transfers between devices, across(): return lax.ppermute(block, 'node', [(n, n ^ 1) for n in range(experts)])  49.9 us
    ppermute x12, waiting for transfers between devices, along(): return lax.ppermute(block, 'node', moves)  39.2 us
    ppermute x12, starting transfers between devices, along(): return lax.ppermute(block, 'node', moves)  25.8 us
    ppermute x8, starting transfers between devices, across(): return lax.ppermute(block, 'node', [(n, n ^ 1) for n in range(experts)])  11.6 us
  transfers between devices with their start and end apart: 22, of which 13 were waited for; matrix products, arithmetic and copies ran while one was open for 0% of the time, Pallas kernels for 24%

profile of v9, /device:TPU:0, one launch (start us, length us, event | category | flops | bytes accessed | tf_op | source)
XLA Modules:
  0.0 179.9 jit_solution(3647248727082993289)
XLA Ops:
  0.0 7.3 %shard_map.64 = (bf16[128,3712]{1,0:T(8,128)(2,1)S(1)}, bf16[128,80]{1,0:T(8,128)(2,1)S(1)}, bf16[128,80]{1,0:T(8,128)(2,1)S(1)}, bf16[80,3712]{1,0:T(8,128)(2,1...) custom-call(bf16[128,3584]{1,0:T(8,128)(2,1)} %tokens.1, s32[2,128]{1,0:T(2,128)} %bitcast.7, ...), custom_call_target="tpu_custom_call" | custom-call | tf_op jit(solution)/shard_map/pallas_call | solution.py:33
  7.3 0.0 copy-start.2
  7.3 0.8 copy-done.2
  8.1 0.5 collective-permute-start.1
  8.6 0.1 collective-permute-start.2
  8.7 5.0 %collective-permute-start.3 = (bf16[128,3712]{1,0:T(8,128)(2,1)S(1)}, bf16[128,3712]{1,0:T(8,128)(2,1)S(1)}, u32[]{:S(2)}, u32[]{:S(2)}) collective-permute-start(bf16[128,3712]{1,0:T(8,128)(2,1)S(1)} %get-tuple-element.40), channel_id=1, source_target_pairs={{0,4},{2,6},{4,8},{6,10},{8,12},{10,14},{1,5},{3,7},{5,9},{7,11},{... | collective-permute-start | bytes 2850824 | tf_op jit(solution)/shard_map/ppermute | solution.py:231
  13.6 1.3 collective-permute-start.4
  14.9 1.6 collective-permute-start
  16.5 13.5 %collective-permute-done.refs_2_.refs_1_ = bf16[80,3712]{1,0:T(8,128)(2,1)S(1)} collective-permute-done((bf16[80,3712]{1,0:T(8,128)(2,1)S(1)}, bf16[80,3712]{1,0:T(8,128)(2,1)S(1)}, u32[]{:S(2)}, u32[]{:S(2)}) %collective-permute-start) | collective-permute-done | bytes 593952 | tf_op jit(solution)/shard_map/ppermute | solution.py:234
  30.0 4.0 %collective-permute-done.3.refs_0_ = bf16[128,3712]{1,0:T(8,128)(2,1)S(1)} collective-permute-done((bf16[128,3712]{1,0:T(8,128)(2,1)S(1)}, bf16[128,3712]{1,0:T(8,128)(2,1)S(1)}, u32[]{:S(2)}, u32[]{:S(2)}) %collective-permute-start.3) | collective-permute-done | bytes 950304 | tf_op jit(solution)/shard_map/ppermute | solution.py:231
  34.0 4.2 %collective-permute-done.4.refs_1_ = bf16[128,3712]{1,0:T(8,128)(2,1)S(1)} collective-permute-done((bf16[128,3712]{1,0:T(8,128)(2,1)S(1)}, bf16[128,3712]{1,0:T(8,128)(2,1)S(1)}, u32[]{:S(2)}, u32[]{:S(2)}) %collective-permute-start.4) | collective-permute-done | bytes 950304 | tf_op jit(solution)/shard_map/ppermute | solution.py:231
  38.2 0.0 copy-done
  38.2 0.7 collective-permute-start.5
  38.9 1.3 collective-permute-start.6
  40.2 1.0 shard_map.66
  41.3 1.6 collective-permute-start.7
  42.9 12.6 %collective-permute-done.7.refs_1_.refs_3_ = bf16[80,3712]{1,0:T(8,128)(2,1)S(1)} collective-permute-done((bf16[80,3712]{1,0:T(8,128)(2,1)S(1)}, bf16[80,3712]{1,0:T(8,128)(2,1)S(1)}, u32[]{:S(2)}, u32[]{:S(2)}) %collective-permute-start.7) | collective-permute-done | bytes 593952 | tf_op jit(solution)/shard_map/ppermute | solution.py:234
  55.5 0.0 collective-permute-done.2.refs_5_
  55.5 0.0 collective-permute-done.1.refs_3_
  55.5 9.2 %shard_map.67 = (bf16[80,3584]{1,0:T(8,128)(2,1)S(1)}, bf16[80,3584]{1,0:T(8,128)(2,1)S(1)}) custom-call(bf16[80,3712]{1,0:T(8,128)(2,1)S(1)} %get-tuple-element.43.refs_0_, bf16[80,3712]{1,0:T(8,128)(2,1)S(1)} %collective-permute-done.7.refs_1_.refs_3_, bf16[2,3584,512]{2,1,0:T(8,128)(2,1)} %get-tuple-element.39.refs_2_, ...), custom_call_target="tpu_custom_call" | custom-call | tf_op jit(solution)/shard_map/pallas_call | solution.py:33
  64.7 0.0 collective-permute-done.5.refs_0_
  64.7 0.2 collective-permute-done.6.refs_1_
  64.9 0.1 shard_map.68
  65.1 0.7 collective-permute-start.10
  65.8 1.3 collective-permute-start.9
  67.1 1.6 collective-permute-start.11
  68.7 1.0 shard_map.69
  69.7 0.6 collective-permute-start.8
  70.3 12.8 %collective-permute-done.11.refs_3_ = bf16[80,3584]{1,0:T(8,128)(2,1)S(1)} collective-permute-done((bf16[80,3584]{1,0:T(8,128)(2,1)S(1)}, bf16[80,3584]{1,0:T(8,128)(2,1)S(1)}, u32[]{:S(2)}, u32[]{:S(2)}) %collective-permute-start.11) | collective-permute-done | bytes 573472 | tf_op jit(solution)/shard_map/ppermute | solution.py:234
  83.1 0.6 shard_map.70.refs_4_
  83.7 0.0 collective-permute-done.10.refs_3_
  83.7 6.7 %collective-permute-done.9.refs_1_ = bf16[128,3712]{1,0:T(8,128)(2,1)S(1)} collective-permute-done((bf16[128,3712]{1,0:T(8,128)(2,1)S(1)}, bf16[128,3712]{1,0:T(8,128)(2,1)S(1)}, u32[]{:S(2)}, u32[]{:S(2)}) %collective-permute-start.9) | collective-permute-done | bytes 950304 | tf_op jit(solution)/shard_map/ppermute | solution.py:231
  90.4 1.0 shard_map.71
  91.5 1.6 collective-permute-start.13
  93.0 0.7 collective-permute-start.14
  93.8 2.3 %collective-permute-start.15 = (bf16[128,3584]{1,0:T(8,128)(2,1)S(1)}, bf16[128,3584]{1,0:T(8,128)(2,1)S(1)}, u32[]{:S(2)}, u32[]{:S(2)}) collective-permute-start(bf16[128,3584]{1,0:T(8,128)(2,1)S(1)} %shard_map.70.refs_4_), channel_id=1, source_target_pairs={{0,4},{2,6},{4,8},{6,10},{1,5},{3,7},{5,9},{7,11},{16,20},{18,22},... | collective-permute-start | bytes 2752520 | tf_op jit(solution)/shard_map/ppermute | solution.py:231
  96.0 0.0 collective-permute-done.8.refs_1_
  96.0 9.2 %shard_map.72 = (bf16[80,3584]{1,0:T(8,128)(2,1)S(1)}, bf16[80,3584]{1,0:T(8,128)(2,1)S(1)}) custom-call(bf16[80,3712]{1,0:T(8,128)(2,1)S(1)} %get-tuple-element.51.refs_0_, bf16[80,3712]{1,0:T(8,128)(2,1)S(1)} %collective-permute-done.8.refs_1_, bf16[2,3584,512]{2,1,0:T(8,128)(2,1)} %get-tuple-element.39.refs_2_, ...), custom_call_target="tpu_custom_call" | custom-call | tf_op jit(solution)/shard_map/pallas_call | solution.py:33
  105.3 0.6 collective-permute-start.12
  105.8 0.6 collective-permute-done.13.refs_1_
  106.5 9.2 %shard_map.73 = (bf16[80,3584]{1,0:T(8,128)(2,1)S(1)}, bf16[80,3584]{1,0:T(8,128)(2,1)S(1)}) custom-call(bf16[80,3712]{1,0:T(8,128)(2,1)S(1)} %get-tuple-element.58.refs_0_, bf16[80,3712]{1,0:T(8,128)(2,1)S(1)} %collective-permute-done.13.refs_1_, bf16[2,3584,512]{2,1,0:T(8,128)(2,1)} %get-tuple-element.39.refs_2_, ...), custom_call_target="tpu_custom_call" | custom-call | tf_op jit(solution)/shard_map/pallas_call | solution.py:33
  115.7 2.5 %collective-permute-start.17 = (bf16[80,3584]{1,0:T(8,128)(2,1)S(1)}, bf16[80,3584]{1,0:T(8,128)(2,1)S(1)}, u32[]{:S(2)}, u32[]{:S(2)}) collective-permute-start(bf16[80,3584]{1,0:T(8,128)(2,1)S(1)} %get-tuple-element.64), channel_id=1, source_target_pairs={{0,2},{2,0},{4,6},{6,4},{8,10},{10,8},{12,14},{14,12},{1,3},{3,1},... | collective-permute-start | bytes 1720328 | tf_op jit(solution)/shard_map/ppermute | solution.py:234
  118.2 0.0 collective-permute-done.14.refs_5_.refs_0_
  118.2 0.0 collective-permute-done.15.refs_6_.refs_1_
  118.2 2.2 %collective-permute-done.12.refs_3_ = bf16[80,3584]{1,0:T(8,128)(2,1)S(1)} collective-permute-done((bf16[80,3584]{1,0:T(8,128)(2,1)S(1)}, bf16[80,3584]{1,0:T(8,128)(2,1)S(1)}, u32[]{:S(2)}, u32[]{:S(2)}) %collective-permute-start.12) | collective-permute-done | bytes 573472 | tf_op jit(solution)/shard_map/ppermute | solution.py:234
  120.4 0.6 shard_map.74.refs_6_.refs_0_
  121.0 8.6 %collective-permute-start.19 = (bf16[128,3584]{1,0:T(8,128)(2,1)S(1)}, bf16[128,3584]{1,0:T(8,128)(2,1)S(1)}, u32[]{:S(2)}, u32[]{:S(2)}) collective-permute-start(bf16[128,3584]{1,0:T(8,128)(2,1)S(1)} %shard_map.74.refs_6_.refs_0_), channel_id=1, source_target_pairs={{0,8},{2,10},{12,4},{14,6},{1,9},{3,11},{13,5},{15,7},{16,24},{18,... | collective-permute-start | bytes 2752520 | tf_op jit(solution)/shard_map/ppermute | solution.py:231
  129.6 0.0 copy-done.1
  129.6 9.2 %shard_map.75 = (bf16[80,3584]{1,0:T(8,128)(2,1)S(1)}, bf16[80,3584]{1,0:T(8,128)(2,1)S(1)}) custom-call(bf16[80,3712]{1,0:T(8,128)(2,1)S(1)} %copy-done.3, bf16[80,3712]{1,0:T(8,128)(2,1)S(1)} %copy-done.1, bf16[2,3584,512]{2,1,0:T(8,128)(2,1)} %get-tuple-element.39.refs_2_, bf16[2,3584,512]{2,1,0:T(8,128)(2,1)} %collective-permute-done.1.refs_3_, ...), custom_call_target="tpu_custom_call" | custom-call | tf_op jit(solution)/shard_map/pallas_call | solution.py:33
  138.9 0.0 collective-permute-done.17.refs_3_
  138.9 0.6 shard_map.76.refs_3_
  139.5 1.3 collective-permute-start.18
  140.9 1.3 collective-permute-start.20
  142.2 7.2 %collective-permute-done.19.refs_2_ = bf16[128,3584]{1,0:T(8,128)(2,1)S(1)} collective-permute-done((bf16[128,3584]{1,0:T(8,128)(2,1)S(1)}, bf16[128,3584]{1,0:T(8,128)(2,1)S(1)}, u32[]{:S(2)}, u32[]{:S(2)}) %collective-permute-start.19) | collective-permute-done | bytes 917536 | tf_op jit(solution)/shard_map/ppermute | solution.py:231
  149.4 0.3 shard_map.77.refs_2_
  149.7 11.4 %collective-permute-done.18.refs_1_ = bf16[128,3584]{1,0:T(8,128)(2,1)S(1)} collective-permute-done((bf16[128,3584]{1,0:T(8,128)(2,1)S(1)}, bf16[128,3584]{1,0:T(8,128)(2,1)S(1)}, u32[]{:S(2)}, u32[]{:S(2)}) %collective-permute-start.18) | collective-permute-done | bytes 917536 | tf_op jit(solution)/shard_map/ppermute | solution.py:231
  161.1 0.2 shard_map.78.refs_4_
  161.3 1.3 collective-permute-start.21
  162.6 1.6 collective-permute-start.16
  164.2 8.2 %collective-permute-done.16.refs_3_ = bf16[80,3584]{1,0:T(8,128)(2,1)S(1)} collective-permute-done((bf16[80,3584]{1,0:T(8,128)(2,1)S(1)}, bf16[80,3584]{1,0:T(8,128)(2,1)S(1)}, u32[]{:S(2)}, u32[]{:S(2)}) %collective-permute-start.16) | collective-permute-done | bytes 573472 | tf_op jit(solution)/shard_map/ppermute | solution.py:234
  172.4 0.6 shard_map.79
  173.0 0.0 collective-permute-done.20
  173.0 5.5 %collective-permute-done.21 = bf16[128,3584]{1,0:T(8,128)(2,1)S(1)} collective-permute-done((bf16[128,3584]{1,0:T(8,128)(2,1)S(1)}, bf16[128,3584]{1,0:T(8,128)(2,1)S(1)}, u32[]{:S(2)}, u32[]{:S(2)}) %collective-permute-start.21) | collective-permute-done | bytes 917536 | tf_op jit(solution)/shard_map/ppermute | solution.py:231
  178.5 1.4 add_convert_fusion
  (5 shorter events, 0.0 us)
Async XLA Ops:
  7.3 0.8 copy-start.2
  8.1 47.4 %collective-permute-start.1 = (bf16[2,3584,512]{2,1,0:T(8,128)(2,1)}, bf16[2,3584,512]{2,1,0:T(8,128)(2,1)}, u32[]{:S(2)}, u32[]{:S(2)}) collective-permute-start(bf16[2,3584,512]{2,1,0:T(8,128)(2,1)} %get-tuple-element.39.refs_2_), channel_id=1, source_target_pairs={{0,1},{1,0},{2,3},{3,2},{4,5},{5,4},{6,7},{7,6},{8,9},{9,8},{10,11... | collective-permute-start | bytes 22020104 | tf_op jit(solution)/shard_map/ppermute | solution.py:227
  8.6 46.9 %collective-permute-start.2 = (bf16[512,3584]{1,0:T(8,128)(2,1)}, bf16[512,3584]{1,0:T(8,128)(2,1)}, u32[]{:S(2)}, u32[]{:S(2)}) collective-permute-start(bf16[512,3584]{1,0:T(8,128)(2,1)} %bitcast.4.refs_4_), channel_id=1, source_target_pairs={{0,1},{1,0},{2,3},{3,2},{4,5},{5,4},{6,7},{7,6},{8,9},{9,8},{10,11... | collective-permute-start | bytes 11010056 | tf_op jit(solution)/shard_map/ppermute | solution.py:227
  8.7 25.4 %collective-permute-start.3 = (bf16[128,3712]{1,0:T(8,128)(2,1)S(1)}, bf16[128,3712]{1,0:T(8,128)(2,1)S(1)}, u32[]{:S(2)}, u32[]{:S(2)}) collective-permute-start(bf16[128,3712]{1,0:T(8,128)(2,1)S(1)} %get-tuple-element.40), channel_id=1, source_target_pairs={{0,4},{2,6},{4,8},{6,10},{8,12},{10,14},{1,5},{3,7},{5,9},{7,11},{... | collective-permute-start | bytes 2850824 | tf_op jit(solution)/shard_map/ppermute | solution.py:231
  13.6 24.6 %collective-permute-start.4 = (bf16[128,3712]{1,0:T(8,128)(2,1)S(1)}, bf16[128,3712]{1,0:T(8,128)(2,1)S(1)}, u32[]{:S(2)}, u32[]{:S(2)}) collective-permute-start(bf16[128,3712]{1,0:T(8,128)(2,1)S(1)} %get-tuple-element.40), channel_id=1, source_target_pairs={{4,0},{6,2},{8,4},{10,6},{12,8},{14,10},{5,1},{7,3},{9,5},{11,7},{... | collective-permute-start | bytes 2850824 | tf_op jit(solution)/shard_map/ppermute | solution.py:231
  14.9 15.1 %collective-permute-start = (bf16[80,3712]{1,0:T(8,128)(2,1)S(1)}, bf16[80,3712]{1,0:T(8,128)(2,1)S(1)}, u32[]{:S(2)}, u32[]{:S(2)}) collective-permute-start(bf16[80,3712]{1,0:T(8,128)(2,1)S(1)} %get-tuple-element.38), channel_id=1, source_target_pairs={{0,2},{2,0},{4,6},{6,4},{8,10},{10,8},{12,14},{14,12},{1,3},{3,1},... | collective-permute-start | bytes 1781768 | tf_op jit(solution)/shard_map/ppermute | solution.py:234
  30.0 8.2 %copy-start = (bf16[80,3712]{1,0:T(8,128)(2,1)}, bf16[80,3712]{1,0:T(8,128)(2,1)S(1)}, u32[]{:S(2)}) copy-start(bf16[80,3712]{1,0:T(8,128)(2,1)S(1)} %collective-permute-done.refs_2_.refs_1_) | copy-start | bytes 1781764
  38.2 26.5 %collective-permute-start.5 = (bf16[128,3712]{1,0:T(8,128)(2,1)S(1)}, bf16[128,3712]{1,0:T(8,128)(2,1)S(1)}, u32[]{:S(2)}, u32[]{:S(2)}) collective-permute-start(bf16[128,3712]{1,0:T(8,128)(2,1)S(1)} %get-tuple-element.41.refs_1_.refs_2_), channel_id=1, source_target_pairs={{4,8},{6,10},{8,12},{10,14},{5,9},{7,11},{9,13},{11,15},{20,24},{2... | collective-permute-start | bytes 2850824 | tf_op jit(solution)/shard_map/ppermute | solution.py:231
  38.9 26.0 %collective-permute-start.6 = (bf16[128,3712]{1,0:T(8,128)(2,1)S(1)}, bf16[128,3712]{1,0:T(8,128)(2,1)S(1)}, u32[]{:S(2)}, u32[]{:S(2)}) collective-permute-start(bf16[128,3712]{1,0:T(8,128)(2,1)S(1)} %get-tuple-element.42.refs_0_), channel_id=1, source_target_pairs={{4,0},{6,2},{8,4},{10,6},{5,1},{7,3},{9,5},{11,7},{20,16},{22,18},... | collective-permute-start | bytes 2850824 | tf_op jit(solution)/shard_map/ppermute | solution.py:231
  41.3 14.2 %collective-permute-start.7 = (bf16[80,3712]{1,0:T(8,128)(2,1)S(1)}, bf16[80,3712]{1,0:T(8,128)(2,1)S(1)}, u32[]{:S(2)}, u32[]{:S(2)}) collective-permute-start(bf16[80,3712]{1,0:T(8,128)(2,1)S(1)} %get-tuple-element.44), channel_id=1, source_target_pairs={{0,2},{2,0},{4,6},{6,4},{8,10},{10,8},{12,14},{14,12},{1,3},{3,1},... | collective-permute-start | bytes 1781768 | tf_op jit(solution)/shard_map/ppermute | solution.py:234
  65.1 18.6 %collective-permute-start.10 = (bf16[128,3712]{1,0:T(8,128)(2,1)S(1)}, bf16[128,3712]{1,0:T(8,128)(2,1)S(1)}, u32[]{:S(2)}, u32[]{:S(2)}) collective-permute-start(bf16[128,3712]{1,0:T(8,128)(2,1)S(1)} %get-tuple-element.48.refs_1_), channel_id=1, source_target_pairs={{8,12},{10,14},{9,13},{11,15},{24,28},{26,30},{25,29},{27,31}} | collective-permute-start | bytes 2850824 | tf_op jit(solution)/shard_map/ppermute | solution.py:231
  65.8 24.6 %collective-permute-start.9 = (bf16[128,3712]{1,0:T(8,128)(2,1)S(1)}, bf16[128,3712]{1,0:T(8,128)(2,1)S(1)}, u32[]{:S(2)}, u32[]{:S(2)}) collective-permute-start(bf16[128,3712]{1,0:T(8,128)(2,1)S(1)} %get-tuple-element.47.refs_0_), channel_id=1, source_target_pairs={{4,0},{6,2},{5,1},{7,3},{20,16},{22,18},{21,17},{23,19}} | collective-permute-start | bytes 2850824 | tf_op jit(solution)/shard_map/ppermute | solution.py:231
  67.1 16.0 %collective-permute-start.11 = (bf16[80,3584]{1,0:T(8,128)(2,1)S(1)}, bf16[80,3584]{1,0:T(8,128)(2,1)S(1)}, u32[]{:S(2)}, u32[]{:S(2)}) collective-permute-start(bf16[80,3584]{1,0:T(8,128)(2,1)S(1)} %get-tuple-element.54), channel_id=1, source_target_pairs={{0,2},{2,0},{4,6},{6,4},{8,10},{10,8},{12,14},{14,12},{1,3},{3,1},... | collective-permute-start | bytes 1720328 | tf_op jit(solution)/shard_map/ppermute | solution.py:234
  69.7 26.3 %collective-permute-start.8 = (bf16[80,3712]{1,0:T(8,128)(2,1)S(1)}, bf16[80,3712]{1,0:T(8,128)(2,1)S(1)}, u32[]{:S(2)}, u32[]{:S(2)}) collective-permute-start(bf16[80,3712]{1,0:T(8,128)(2,1)S(1)} %get-tuple-element.52), channel_id=1, source_target_pairs={{0,2},{2,0},{4,6},{6,4},{8,10},{10,8},{12,14},{14,12},{1,3},{3,1},... | collective-permute-start | bytes 1781768 | tf_op jit(solution)/shard_map/ppermute | solution.py:234
  91.5 15.0 %collective-permute-start.13 = (bf16[80,3712]{1,0:T(8,128)(2,1)S(1)}, bf16[80,3712]{1,0:T(8,128)(2,1)S(1)}, u32[]{:S(2)}, u32[]{:S(2)}) collective-permute-start(bf16[80,3712]{1,0:T(8,128)(2,1)S(1)} %get-tuple-element.59), channel_id=1, source_target_pairs={{0,2},{2,0},{4,6},{6,4},{8,10},{10,8},{12,14},{14,12},{1,3},{3,1},... | collective-permute-start | bytes 1781768 | tf_op jit(solution)/shard_map/ppermute | solution.py:234
  93.0 25.2 %collective-permute-start.14 = (bf16[128,3584]{1,0:T(8,128)(2,1)S(1)}, bf16[128,3584]{1,0:T(8,128)(2,1)S(1)}, u32[]{:S(2)}, u32[]{:S(2)}) collective-permute-start(bf16[128,3584]{1,0:T(8,128)(2,1)S(1)} %shard_map.70.refs_4_), channel_id=1, source_target_pairs={{8,4},{10,6},{12,8},{14,10},{9,5},{11,7},{13,9},{15,11},{24,20},{2... | collective-permute-start | bytes 2752520 | tf_op jit(solution)/shard_map/ppermute | solution.py:231
  93.8 24.5 %collective-permute-start.15 = (bf16[128,3584]{1,0:T(8,128)(2,1)S(1)}, bf16[128,3584]{1,0:T(8,128)(2,1)S(1)}, u32[]{:S(2)}, u32[]{:S(2)}) collective-permute-start(bf16[128,3584]{1,0:T(8,128)(2,1)S(1)} %shard_map.70.refs_4_), channel_id=1, source_target_pairs={{0,4},{2,6},{4,8},{6,10},{1,5},{3,7},{5,9},{7,11},{16,20},{18,22},... | collective-permute-start | bytes 2752520 | tf_op jit(solution)/shard_map/ppermute | solution.py:231
  105.3 15.1 %collective-permute-start.12 = (bf16[80,3584]{1,0:T(8,128)(2,1)S(1)}, bf16[80,3584]{1,0:T(8,128)(2,1)S(1)}, u32[]{:S(2)}, u32[]{:S(2)}) collective-permute-start(bf16[80,3584]{1,0:T(8,128)(2,1)S(1)} %get-tuple-element.57), channel_id=1, source_target_pairs={{0,2},{2,0},{4,6},{6,4},{8,10},{10,8},{12,14},{14,12},{1,3},{3,1},... | collective-permute-start | bytes 1720328 | tf_op jit(solution)/shard_map/ppermute | solution.py:234
  115.7 23.2 %collective-permute-start.17 = (bf16[80,3584]{1,0:T(8,128)(2,1)S(1)}, bf16[80,3584]{1,0:T(8,128)(2,1)S(1)}, u32[]{:S(2)}, u32[]{:S(2)}) collective-permute-start(bf16[80,3584]{1,0:T(8,128)(2,1)S(1)} %get-tuple-element.64), channel_id=1, source_target_pairs={{0,2},{2,0},{4,6},{6,4},{8,10},{10,8},{12,14},{14,12},{1,3},{3,1},... | collective-permute-start | bytes 1720328 | tf_op jit(solution)/shard_map/ppermute | solution.py:234
  120.4 9.2 %copy-start.1 = (bf16[80,3712]{1,0:T(8,128)(2,1)S(1)}, bf16[80,3712]{1,0:T(8,128)(2,1)}, u32[]{:S(2)}) copy-start(bf16[80,3712]{1,0:T(8,128)(2,1)} %copy-done) | copy-start | bytes 1781764
  120.4 9.2 %copy-start.3 = (bf16[80,3712]{1,0:T(8,128)(2,1)S(1)}, bf16[80,3712]{1,0:T(8,128)(2,1)}, u32[]{:S(2)}) copy-start(bf16[80,3712]{1,0:T(8,128)(2,1)} %copy-done.2) | copy-start | bytes 1781764
  121.0 28.4 %collective-permute-start.19 = (bf16[128,3584]{1,0:T(8,128)(2,1)S(1)}, bf16[128,3584]{1,0:T(8,128)(2,1)S(1)}, u32[]{:S(2)}, u32[]{:S(2)}) collective-permute-start(bf16[128,3584]{1,0:T(8,128)(2,1)S(1)} %shard_map.74.refs_6_.refs_0_), channel_id=1, source_target_pairs={{0,8},{2,10},{12,4},{14,6},{1,9},{3,11},{13,5},{15,7},{16,24},{18,... | collective-permute-start | bytes 2752520 | tf_op jit(solution)/shard_map/ppermute | solution.py:231
  139.5 21.6 %collective-permute-start.18 = (bf16[128,3584]{1,0:T(8,128)(2,1)S(1)}, bf16[128,3584]{1,0:T(8,128)(2,1)S(1)}, u32[]{:S(2)}, u32[]{:S(2)}) collective-permute-start(bf16[128,3584]{1,0:T(8,128)(2,1)S(1)} %shard_map.76.refs_3_), channel_id=1, source_target_pairs={{0,4},{2,6},{12,8},{14,10},{1,5},{3,7},{13,9},{15,11},{16,20},{18,... | collective-permute-start | bytes 2752520 | tf_op jit(solution)/shard_map/ppermute | solution.py:231
  140.9 32.2 %collective-permute-start.20 = (bf16[128,3584]{1,0:T(8,128)(2,1)S(1)}, bf16[128,3584]{1,0:T(8,128)(2,1)S(1)}, u32[]{:S(2)}, u32[]{:S(2)}) collective-permute-start(bf16[128,3584]{1,0:T(8,128)(2,1)S(1)} %shard_map.76.refs_3_), channel_id=1, source_target_pairs={{4,0},{6,2},{8,12},{10,14},{5,1},{7,3},{9,13},{11,15},{20,16},{22,... | collective-permute-start | bytes 2752520 | tf_op jit(solution)/shard_map/ppermute | solution.py:231
  161.3 17.2 %collective-permute-start.21 = (bf16[128,3584]{1,0:T(8,128)(2,1)S(1)}, bf16[128,3584]{1,0:T(8,128)(2,1)S(1)}, u32[]{:S(2)}, u32[]{:S(2)}) collective-permute-start(bf16[128,3584]{1,0:T(8,128)(2,1)S(1)} %shard_map.78.refs_4_), channel_id=1, source_target_pairs={{4,12},{6,14},{8,0},{10,2},{5,13},{7,15},{9,1},{11,3},{20,28},{22,... | collective-permute-start | bytes 2752520 | tf_op jit(solution)/shard_map/ppermute | solution.py:231
  162.6 9.8 %collective-permute-start.16 = (bf16[80,3584]{1,0:T(8,128)(2,1)S(1)}, bf16[80,3584]{1,0:T(8,128)(2,1)S(1)}, u32[]{:S(2)}, u32[]{:S(2)}) collective-permute-start(bf16[80,3584]{1,0:T(8,128)(2,1)S(1)} %get-tuple-element.62), channel_id=1, source_target_pairs={{0,2},{2,0},{4,6},{6,4},{8,10},{10,8},{12,14},{14,12},{1,3},{3,1},... | collective-permute-start | bytes 1720328 | tf_op jit(solution)/shard_map/ppermute | solution.py:234

commit v10 on v9

--- a/solution.py
+++ b/solution.py
@@ -131,20 +131,24 @@
 
 
 def expert_kernel(experts, own, other, *refs):
-    own_w, other_w, own_down, other_down, own_out, other_out, rows, hidden, gates, ups, downs, sems = refs
+    own_w, other_w, own_down, other_down, own_out, other_out, rows, hidden, total, gates, ups, downs, sems = refs
     cap, width = own_out.shape
     tiles, _, size = gates.shape
     each = tiles // 2
-    queue = []
-    for tile in range(tiles):
-        stack, part = (own_w, other_w)[tile // each], pl.ds(tile % each * size, size)
-        queue.append(pltpu.make_async_copy(stack.at[0, :, part], gates.at[tile], sems.at[tile, 0]))
-        queue.append(pltpu.make_async_copy(stack.at[1, :, part], ups.at[tile], sems.at[tile, 1]))
-    for half, down in enumerate((own_down, other_down)):
-        queue.append(pltpu.make_async_copy(down, downs.at[half], sems.at[half, 2]))
-    ahead = iter(queue[4:])
-    for copy in queue[:4]:
-        copy.start()
+    halves = []
+    for half, (stack, down) in enumerate(((own_w, own_down), (other_w, other_down))):
+        queue = []
+        for tile in range(half * each, half * each + each):
+            part = pl.ds(tile % each * size, size)
+            queue.append(pltpu.make_async_copy(stack.at[0, :, part], gates.at[tile], sems.at[tile, 0]))
+            queue.append(pltpu.make_async_copy(stack.at[1, :, part], ups.at[tile], sems.at[tile, 1]))
+        for tile in range(half * each, half * each + each):
+            part = pl.ds(tile % each * size, size)
+            queue.append(pltpu.make_async_copy(down.at[part], downs.at[tile], sems.at[tile, 2]))
+        halves.append(queue)
+    ahead = iter(halves[0] + halves[1])
+    for _ in range(4):
+        next(ahead).start()
 
     def arrived(copy):
         copy.wait()
@@ -154,14 +158,6 @@
 
     rows[:cap] = own[:, :width]
     rows[cap:] = other[:, :width]
-    for tile in range(tiles):
-        arrived(queue[2 * tile])
-        gate = jnp.dot(rows[...], gates[tile], preferred_element_type=jnp.float32)
-        arrived(queue[2 * tile + 1])
-        up = jnp.dot(rows[...], ups[tile], preferred_element_type=jnp.float32)
-        hidden[:, tile * size : (tile + 1) * size] = (gate / (1.0 + jnp.exp(-gate)) * up).astype(jnp.bfloat16)
-    arrived(queue[-2])
-    arrived(queue[-1])
     node = lax.axis_index("node")
     scales = []
     for marked in (own, other):
@@ -170,12 +166,26 @@
         mine = (lax.rem(lane, experts) == node) & (lane < 3 * experts)
         scales.append(jnp.sum(jnp.where(mine, marks, 0.0), axis=1, keepdims=True))
     step = 512 if width % 512 == 0 else width
-    for start in range(0, width, step):
-        cut = slice(start, start + step)
-        out = jnp.dot(hidden[:, : each * size], downs[0, :, cut], preferred_element_type=jnp.float32)
-        out += jnp.dot(hidden[:, each * size :], downs[1, :, cut], preferred_element_type=jnp.float32)
-        own_out[:, cut] = (out[:cap] * scales[0]).astype(jnp.bfloat16)
-        other_out[:, cut] = (out[cap:] * scales[1]).astype(jnp.bfloat16)
+    for half, queue in enumerate(halves):
+        for k in range(each):
+            tile = half * each + k
+            arrived(queue[2 * k])
+            gate = jnp.dot(rows[...], gates[tile], preferred_element_type=jnp.float32)
+            arrived(queue[2 * k + 1])
+            up = jnp.dot(rows[...], ups[tile], preferred_element_type=jnp.float32)
+            hidden[tile] = (gate / (1.0 + jnp.exp(-gate)) * up).astype(jnp.bfloat16)
+        for copy in queue[2 * each :]:
+            arrived(copy)
+        for first in range(0, width, step):
+            cut = slice(first, first + step)
+            out = jnp.zeros((2 * cap, step), jnp.float32) if half == 0 else total[:, cut]
+            for tile in range(half * each, half * each + each):
+                out += jnp.dot(hidden[tile], downs[tile, :, cut], preferred_element_type=jnp.float32)
+            if half == 0:
+                total[:, cut] = out
+            else:
+                own_out[:, cut] = (out[:cap] * scales[0]).astype(jnp.bfloat16)
+                other_out[:, cut] = (out[cap:] * scales[1]).astype(jnp.bfloat16)
 
 
 def spread_kernel(own_map, other_map, own_out, other_out, *refs):
@@ -252,10 +262,11 @@
             after,
             [
                 pltpu.VMEM((2 * cap, width), jnp.bfloat16),
-                pltpu.VMEM((2 * cap, 2 * hidden), jnp.bfloat16),
+                pltpu.VMEM((tiles, 2 * cap, size), jnp.bfloat16),
+                pltpu.VMEM((2 * cap, width), jnp.float32),
                 pltpu.VMEM((tiles, width, size), jnp.bfloat16),
                 pltpu.VMEM((tiles, width, size), jnp.bfloat16),
-                pltpu.VMEM((2, hidden, width), jnp.bfloat16),
+                pltpu.VMEM((tiles, size, width), jnp.bfloat16),
                 pltpu.SemaphoreType.DMA((tiles, 3)),
             ],
             [IN_VMEM] * 2 + [ANYWHERE] * 4,
@@ -336,15 +347,15 @@
         relay(step)
     do_pick(2)
     do_spread(1)
-    do_pick(3)
+    do_pick(3, after=[picks[2][2]])
     do_expert(2)
     for slot in range(3, places):
-        do_expert(slot)
-        do_spread(slot - 1, after=returned[slot - 3])
+        do_expert(slot, after=returned[slot - 3])
+        do_spread(slot - 1)
         if slot + 1 < places:
             do_pick(slot + 1)
+    do_spread(places - 1)
     do_expert(0)
-    do_spread(places - 1)
     near = returned.pop(places - 3)
     (summed,) = ordered(call_sum, [*returned.pop(0), *near] if places > 3 else near, cost=128 * MIB)
     (joined,) = ordered(call_sum, [kept[places - 2], along(kept[places - 1], hops)])

time: 180 us -> 184 us (1.022)
  starting transfers between devices: 37.9 us -> 45.3 us
  waiting for transfers between devices: 89.1 us -> 85.6 us
    ppermute x12, waiting for transfers between devices: 39.2 us -> 30.4 us  [along(): return lax.ppermute(block, 'node', moves)]
    ppermute x12, starting transfers between devices: 25.8 us -> 33.8 us  [along(): return lax.ppermute(block, 'node', moves)]
    ppermute x8, waiting for transfers between devices: 49.9 us -> 55.2 us  [across(): return lax.ppermute(block, 'node', [(n, n ^ 1) for n in range(experts)])]
  transfers between devices with their start and end apart: 22 -> 22, of which waited for: 13 -> 14; matrix products, arithmetic and copies ran while one was open for 0% -> 0% of each run, Pallas kernels for 24% -> 23%
where the time goes in v10:
time: 184 us
  waiting for transfers between devices  85.6 us (47%)
  Pallas kernels  50.2 us (27%)
  starting transfers between devices  45.3 us (25%)
    ppermute x8, waiting for transfers between devices, across(): return lax.ppermute(block, 'node', [(n, n ^ 1) for n in range(experts)])  55.2 us
    pallas_call x15, Pallas kernels, call(): pl.pallas_call(body, out_shape=outs, in_specs=specs, out_specs=out_specs...  50.2 us
    ppermute x12, starting transfers between devices, along(): return lax.ppermute(block, 'node', moves)  33.8 us
    ppermute x12, waiting for transfers between devices, along(): return lax.ppermute(block, 'node', moves)  30.4 us
    ppermute x8, starting transfers between devices, across(): return lax.ppermute(block, 'node', [(n, n ^ 1) for n in range(experts)])  11 us
  transfers between devices with their start and end apart: 22, of which 14 were waited for; matrix products, arithmetic and copies ran while one was open for 0% of the time, Pallas kernels for 23%

profile of v10, /device:TPU:0, one launch (start us, length us, event | category | flops | bytes accessed | tf_op | source)
XLA Modules:
  0.0 183.6 jit_solution(18054765408971305016)
XLA Ops:
  0.0 7.3 %shard_map.64 = (bf16[128,3712]{1,0:T(8,128)(2,1)S(1)}, bf16[128,80]{1,0:T(8,128)(2,1)S(1)}, bf16[128,80]{1,0:T(8,128)(2,1)S(1)}, bf16[80,3712]{1,0:T(8,128)(2,1...) custom-call(bf16[128,3584]{1,0:T(8,128)(2,1)} %tokens.1, s32[2,128]{1,0:T(2,128)} %bitcast.7, ...), custom_call_target="tpu_custom_call" | custom-call | tf_op jit(solution)/shard_map/pallas_call | solution.py:33
  7.3 0.0 copy-start.2
  7.3 0.8 copy-done.2
  8.1 0.5 collective-permute-start.1
  8.6 0.1 collective-permute-start.2
  8.7 5.0 %collective-permute-start.3 = (bf16[128,3712]{1,0:T(8,128)(2,1)S(1)}, bf16[128,3712]{1,0:T(8,128)(2,1)S(1)}, u32[]{:S(2)}, u32[]{:S(2)}) collective-permute-start(bf16[128,3712]{1,0:T(8,128)(2,1)S(1)} %get-tuple-element.40), channel_id=1, source_target_pairs={{0,4},{2,6},{4,8},{6,10},{8,12},{10,14},{1,5},{3,7},{5,9},{7,11},{... | collective-permute-start | bytes 2850824 | tf_op jit(solution)/shard_map/ppermute | solution.py:241
  13.6 1.3 collective-permute-start.4
  14.9 1.6 collective-permute-start
  16.5 13.5 %collective-permute-done.refs_2_.refs_1_ = bf16[80,3712]{1,0:T(8,128)(2,1)S(1)} collective-permute-done((bf16[80,3712]{1,0:T(8,128)(2,1)S(1)}, bf16[80,3712]{1,0:T(8,128)(2,1)S(1)}, u32[]{:S(2)}, u32[]{:S(2)}) %collective-permute-start) | collective-permute-done | bytes 593952 | tf_op jit(solution)/shard_map/ppermute | solution.py:244
  30.0 4.0 %collective-permute-done.3.refs_0_ = bf16[128,3712]{1,0:T(8,128)(2,1)S(1)} collective-permute-done((bf16[128,3712]{1,0:T(8,128)(2,1)S(1)}, bf16[128,3712]{1,0:T(8,128)(2,1)S(1)}, u32[]{:S(2)}, u32[]{:S(2)}) %collective-permute-start.3) | collective-permute-done | bytes 950304 | tf_op jit(solution)/shard_map/ppermute | solution.py:241
  34.0 4.2 %collective-permute-done.4.refs_1_ = bf16[128,3712]{1,0:T(8,128)(2,1)S(1)} collective-permute-done((bf16[128,3712]{1,0:T(8,128)(2,1)S(1)}, bf16[128,3712]{1,0:T(8,128)(2,1)S(1)}, u32[]{:S(2)}, u32[]{:S(2)}) %collective-permute-start.4) | collective-permute-done | bytes 950304 | tf_op jit(solution)/shard_map/ppermute | solution.py:241
  38.2 0.0 copy-done
  38.2 0.7 collective-permute-start.5
  38.9 1.3 collective-permute-start.6
  40.2 1.0 shard_map.66
  41.3 1.6 collective-permute-start.7
  42.9 12.6 %collective-permute-done.7.refs_1_.refs_3_ = bf16[80,3712]{1,0:T(8,128)(2,1)S(1)} collective-permute-done((bf16[80,3712]{1,0:T(8,128)(2,1)S(1)}, bf16[80,3712]{1,0:T(8,128)(2,1)S(1)}, u32[]{:S(2)}, u32[]{:S(2)}) %collective-permute-start.7) | collective-permute-done | bytes 593952 | tf_op jit(solution)/shard_map/ppermute | solution.py:244
  55.5 0.0 collective-permute-done.2.refs_5_
  55.5 0.0 collective-permute-done.1.refs_3_
  55.5 9.1 %shard_map.67 = (bf16[80,3584]{1,0:T(8,128)(2,1)S(1)}, bf16[80,3584]{1,0:T(8,128)(2,1)S(1)}) custom-call(bf16[80,3712]{1,0:T(8,128)(2,1)S(1)} %get-tuple-element.43.refs_0_, bf16[80,3712]{1,0:T(8,128)(2,1)S(1)} %collective-permute-done.7.refs_1_.refs_3_, bf16[2,3584,512]{2,1,0:T(8,128)(2,1)} %get-tuple-element.39.refs_2_, ...), custom_call_target="tpu_custom_call" | custom-call | tf_op jit(solution)/shard_map/pallas_call | solution.py:33
  64.7 0.0 collective-permute-done.5.refs_0_
  64.7 0.3 collective-permute-done.6.refs_1_
  64.9 0.1 shard_map.68
  65.1 1.3 collective-permute-start.8
  66.4 0.7 collective-permute-start.9
  67.1 1.6 collective-permute-start.10
  68.7 1.0 shard_map.69
  69.7 0.6 collective-permute-start.11
  70.3 12.8 %collective-permute-done.10.refs_3_ = bf16[80,3584]{1,0:T(8,128)(2,1)S(1)} collective-permute-done((bf16[80,3584]{1,0:T(8,128)(2,1)S(1)}, bf16[80,3584]{1,0:T(8,128)(2,1)S(1)}, u32[]{:S(2)}, u32[]{:S(2)}) %collective-permute-start.10) | collective-permute-done | bytes 573472 | tf_op jit(solution)/shard_map/ppermute | solution.py:244
  83.1 0.6 shard_map.70.refs_4_
  83.7 0.7 collective-permute-start.13
  84.4 7.0 %collective-permute-start.14 = (bf16[128,3584]{1,0:T(8,128)(2,1)S(1)}, bf16[128,3584]{1,0:T(8,128)(2,1)S(1)}, u32[]{:S(2)}, u32[]{:S(2)}) collective-permute-start(bf16[128,3584]{1,0:T(8,128)(2,1)S(1)} %shard_map.70.refs_4_), channel_id=1, source_target_pairs={{0,4},{2,6},{4,8},{6,10},{1,5},{3,7},{5,9},{7,11},{16,20},{18,22},... | collective-permute-start | bytes 2752520 | tf_op jit(solution)/shard_map/ppermute | solution.py:241
  91.5 1.2 collective-permute-done.11.refs_5_.refs_1_
  92.7 0.0 collective-permute-done.8.refs_1_
  92.7 0.0 collective-permute-done.9.refs_3_
  92.7 1.2 shard_map.71
  93.9 1.6 collective-permute-start.12
  95.5 9.1 %shard_map.72 = (bf16[80,3584]{1,0:T(8,128)(2,1)S(1)}, bf16[80,3584]{1,0:T(8,128)(2,1)S(1)}) custom-call(bf16[80,3712]{1,0:T(8,128)(2,1)S(1)} %get-tuple-element.57.refs_0_, bf16[80,3712]{1,0:T(8,128)(2,1)S(1)} %collective-permute-done.11.refs_5_.refs_1_, bf16[2,3584,512]{2,1,0:T(8,128)(2,1)} %get-tuple-element.39.refs_2_, ...), custom_call_target="tpu_custom_call" | custom-call | tf_op jit(solution)/shard_map/pallas_call | solution.py:33
  104.6 0.6 collective-permute-start.16
  105.2 0.0 collective-permute-done.13.refs_7_.refs_0_
  105.2 0.0 collective-permute-done.14.refs_8_.refs_1_
  105.2 3.3 %collective-permute-done.12.refs_1_ = bf16[80,3712]{1,0:T(8,128)(2,1)S(1)} collective-permute-done((bf16[80,3712]{1,0:T(8,128)(2,1)S(1)}, bf16[80,3712]{1,0:T(8,128)(2,1)S(1)}, u32[]{:S(2)}, u32[]{:S(2)}) %collective-permute-start.12) | collective-permute-done | bytes 593952 | tf_op jit(solution)/shard_map/ppermute | solution.py:244
  108.5 9.1 %shard_map.73 = (bf16[80,3584]{1,0:T(8,128)(2,1)S(1)}, bf16[80,3584]{1,0:T(8,128)(2,1)S(1)}) custom-call(bf16[80,3712]{1,0:T(8,128)(2,1)S(1)} %get-tuple-element.55.refs_0_, bf16[80,3712]{1,0:T(8,128)(2,1)S(1)} %collective-permute-done.12.refs_1_, bf16[2,3584,512]{2,1,0:T(8,128)(2,1)} %get-tuple-element.39.refs_2_, ...), custom_call_target="tpu_custom_call" | custom-call | tf_op jit(solution)/shard_map/pallas_call | solution.py:33
  117.7 2.5 %collective-permute-start.15 = (bf16[80,3584]{1,0:T(8,128)(2,1)S(1)}, bf16[80,3584]{1,0:T(8,128)(2,1)S(1)}, u32[]{:S(2)}, u32[]{:S(2)}) collective-permute-start(bf16[80,3584]{1,0:T(8,128)(2,1)S(1)} %get-tuple-element.60), channel_id=1, source_target_pairs={{0,2},{2,0},{4,6},{6,4},{8,10},{10,8},{12,14},{14,12},{1,3},{3,1},... | collective-permute-start | bytes 1720328 | tf_op jit(solution)/shard_map/ppermute | solution.py:244
  120.2 0.6 collective-permute-done.16.refs_3_
  120.8 0.6 shard_map.74.refs_4_.refs_0_
  121.4 0.0 copy-start.1
  121.5 7.1 %collective-permute-start.19 = (bf16[128,3584]{1,0:T(8,128)(2,1)S(1)}, bf16[128,3584]{1,0:T(8,128)(2,1)S(1)}, u32[]{:S(2)}, u32[]{:S(2)}) collective-permute-start(bf16[128,3584]{1,0:T(8,128)(2,1)S(1)} %shard_map.74.refs_4_.refs_0_), channel_id=1, source_target_pairs={{0,8},{2,10},{12,4},{14,6},{1,9},{3,11},{13,5},{15,7},{16,24},{18,... | collective-permute-start | bytes 2752520 | tf_op jit(solution)/shard_map/ppermute | solution.py:241
  128.5 2.3 %collective-permute-done.15.refs_3_ = bf16[80,3584]{1,0:T(8,128)(2,1)S(1)} collective-permute-done((bf16[80,3584]{1,0:T(8,128)(2,1)S(1)}, bf16[80,3584]{1,0:T(8,128)(2,1)S(1)}, u32[]{:S(2)}, u32[]{:S(2)}) %collective-permute-start.15) | collective-permute-done | bytes 573472 | tf_op jit(solution)/shard_map/ppermute | solution.py:244
  130.9 0.6 shard_map.75.refs_6_
  131.5 5.9 %collective-permute-start.18 = (bf16[128,3584]{1,0:T(8,128)(2,1)S(1)}, bf16[128,3584]{1,0:T(8,128)(2,1)S(1)}, u32[]{:S(2)}, u32[]{:S(2)}) collective-permute-start(bf16[128,3584]{1,0:T(8,128)(2,1)S(1)} %shard_map.75.refs_6_), channel_id=1, source_target_pairs={{0,4},{2,6},{12,8},{14,10},{1,5},{3,7},{13,9},{15,11},{16,20},{18,... | collective-permute-start | bytes 2752520 | tf_op jit(solution)/shard_map/ppermute | solution.py:241
  137.4 1.5 collective-permute-start.20
  138.9 9.1 %shard_map.76 = (bf16[80,3584]{1,0:T(8,128)(2,1)S(1)}, bf16[80,3584]{1,0:T(8,128)(2,1)S(1)}) custom-call(bf16[80,3712]{1,0:T(8,128)(2,1)S(1)} %copy-done.3, bf16[80,3712]{1,0:T(8,128)(2,1)S(1)} %copy-done.1, bf16[2,3584,512]{2,1,0:T(8,128)(2,1)} %get-tuple-element.39.refs_2_, bf16[2,3584,512]{2,1,0:T(8,128)(2,1)} %collective-permute-done.1.refs_3_, ...), custom_call_target="tpu_custom_call" | custom-call | tf_op jit(solution)/shard_map/pallas_call | solution.py:33
  148.0 1.2 collective-permute-done.19.refs_2_
  149.3 0.3 shard_map.77.refs_2_
  149.6 13.2 %collective-permute-done.18.refs_1_ = bf16[128,3584]{1,0:T(8,128)(2,1)S(1)} collective-permute-done((bf16[128,3584]{1,0:T(8,128)(2,1)S(1)}, bf16[128,3584]{1,0:T(8,128)(2,1)S(1)}, u32[]{:S(2)}, u32[]{:S(2)}) %collective-permute-start.18) | collective-permute-done | bytes 917536 | tf_op jit(solution)/shard_map/ppermute | solution.py:241
  162.7 0.2 shard_map.78.refs_4_
  163.0 1.3 collective-permute-start.21
  164.3 1.0 collective-permute-start.17
  165.2 8.8 %collective-permute-done.17.refs_3_ = bf16[80,3584]{1,0:T(8,128)(2,1)S(1)} collective-permute-done((bf16[80,3584]{1,0:T(8,128)(2,1)S(1)}, bf16[80,3584]{1,0:T(8,128)(2,1)S(1)}, u32[]{:S(2)}, u32[]{:S(2)}) %collective-permute-start.17) | collective-permute-done | bytes 573472 | tf_op jit(solution)/shard_map/ppermute | solution.py:244
  174.0 0.6 shard_map.79
  174.6 0.0 collective-permute-done.20
  174.7 7.6 %collective-permute-done.21 = bf16[128,3584]{1,0:T(8,128)(2,1)S(1)} collective-permute-done((bf16[128,3584]{1,0:T(8,128)(2,1)S(1)}, bf16[128,3584]{1,0:T(8,128)(2,1)S(1)}, u32[]{:S(2)}, u32[]{:S(2)}) %collective-permute-start.21) | collective-permute-done | bytes 917536 | tf_op jit(solution)/shard_map/ppermute | solution.py:241
  182.3 1.4 add_convert_fusion
  (5 shorter events, 0.0 us)
Async XLA Ops:
  7.3 0.8 copy-start.2
  8.1 47.4 %collective-permute-start.1 = (bf16[2,3584,512]{2,1,0:T(8,128)(2,1)}, bf16[2,3584,512]{2,1,0:T(8,128)(2,1)}, u32[]{:S(2)}, u32[]{:S(2)}) collective-permute-start(bf16[2,3584,512]{2,1,0:T(8,128)(2,1)} %get-tuple-element.39.refs_2_), channel_id=1, source_target_pairs={{0,1},{1,0},{2,3},{3,2},{4,5},{5,4},{6,7},{7,6},{8,9},{9,8},{10,11... | collective-permute-start | bytes 22020104 | tf_op jit(solution)/shard_map/ppermute | solution.py:237
  8.6 46.9 %collective-permute-start.2 = (bf16[512,3584]{1,0:T(8,128)(2,1)}, bf16[512,3584]{1,0:T(8,128)(2,1)}, u32[]{:S(2)}, u32[]{:S(2)}) collective-permute-start(bf16[512,3584]{1,0:T(8,128)(2,1)} %bitcast.4.refs_4_), channel_id=1, source_target_pairs={{0,1},{1,0},{2,3},{3,2},{4,5},{5,4},{6,7},{7,6},{8,9},{9,8},{10,11... | collective-permute-start | bytes 11010056 | tf_op jit(solution)/shard_map/ppermute | solution.py:237
  8.7 25.4 %collective-permute-start.3 = (bf16[128,3712]{1,0:T(8,128)(2,1)S(1)}, bf16[128,3712]{1,0:T(8,128)(2,1)S(1)}, u32[]{:S(2)}, u32[]{:S(2)}) collective-permute-start(bf16[128,3712]{1,0:T(8,128)(2,1)S(1)} %get-tuple-element.40), channel_id=1, source_target_pairs={{0,4},{2,6},{4,8},{6,10},{8,12},{10,14},{1,5},{3,7},{5,9},{7,11},{... | collective-permute-start | bytes 2850824 | tf_op jit(solution)/shard_map/ppermute | solution.py:241
  13.6 24.6 %collective-permute-start.4 = (bf16[128,3712]{1,0:T(8,128)(2,1)S(1)}, bf16[128,3712]{1,0:T(8,128)(2,1)S(1)}, u32[]{:S(2)}, u32[]{:S(2)}) collective-permute-start(bf16[128,3712]{1,0:T(8,128)(2,1)S(1)} %get-tuple-element.40), channel_id=1, source_target_pairs={{4,0},{6,2},{8,4},{10,6},{12,8},{14,10},{5,1},{7,3},{9,5},{11,7},{... | collective-permute-start | bytes 2850824 | tf_op jit(solution)/shard_map/ppermute | solution.py:241
  14.9 15.1 %collective-permute-start = (bf16[80,3712]{1,0:T(8,128)(2,1)S(1)}, bf16[80,3712]{1,0:T(8,128)(2,1)S(1)}, u32[]{:S(2)}, u32[]{:S(2)}) collective-permute-start(bf16[80,3712]{1,0:T(8,128)(2,1)S(1)} %get-tuple-element.38), channel_id=1, source_target_pairs={{0,2},{2,0},{4,6},{6,4},{8,10},{10,8},{12,14},{14,12},{1,3},{3,1},... | collective-permute-start | bytes 1781768 | tf_op jit(solution)/shard_map/ppermute | solution.py:244
  30.0 8.2 %copy-start = (bf16[80,3712]{1,0:T(8,128)(2,1)}, bf16[80,3712]{1,0:T(8,128)(2,1)S(1)}, u32[]{:S(2)}) copy-start(bf16[80,3712]{1,0:T(8,128)(2,1)S(1)} %collective-permute-done.refs_2_.refs_1_) | copy-start | bytes 1781764
  38.2 26.4 %collective-permute-start.5 = (bf16[128,3712]{1,0:T(8,128)(2,1)S(1)}, bf16[128,3712]{1,0:T(8,128)(2,1)S(1)}, u32[]{:S(2)}, u32[]{:S(2)}) collective-permute-start(bf16[128,3712]{1,0:T(8,128)(2,1)S(1)} %get-tuple-element.42.refs_1_.refs_2_), channel_id=1, source_target_pairs={{4,8},{6,10},{8,12},{10,14},{5,9},{7,11},{9,13},{11,15},{20,24},{2... | collective-permute-start | bytes 2850824 | tf_op jit(solution)/shard_map/ppermute | solution.py:241
  38.9 26.0 %collective-permute-start.6 = (bf16[128,3712]{1,0:T(8,128)(2,1)S(1)}, bf16[128,3712]{1,0:T(8,128)(2,1)S(1)}, u32[]{:S(2)}, u32[]{:S(2)}) collective-permute-start(bf16[128,3712]{1,0:T(8,128)(2,1)S(1)} %get-tuple-element.41.refs_0_), channel_id=1, source_target_pairs={{4,0},{6,2},{8,4},{10,6},{5,1},{7,3},{9,5},{11,7},{20,16},{22,18},... | collective-permute-start | bytes 2850824 | tf_op jit(solution)/shard_map/ppermute | solution.py:241
  41.3 14.2 %collective-permute-start.7 = (bf16[80,3712]{1,0:T(8,128)(2,1)S(1)}, bf16[80,3712]{1,0:T(8,128)(2,1)S(1)}, u32[]{:S(2)}, u32[]{:S(2)}) collective-permute-start(bf16[80,3712]{1,0:T(8,128)(2,1)S(1)} %get-tuple-element.44), channel_id=1, source_target_pairs={{0,2},{2,0},{4,6},{6,4},{8,10},{10,8},{12,14},{14,12},{1,3},{3,1},... | collective-permute-start | bytes 1781768 | tf_op jit(solution)/shard_map/ppermute | solution.py:244
  65.1 27.6 %collective-permute-start.8 = (bf16[128,3712]{1,0:T(8,128)(2,1)S(1)}, bf16[128,3712]{1,0:T(8,128)(2,1)S(1)}, u32[]{:S(2)}, u32[]{:S(2)}) collective-permute-start(bf16[128,3712]{1,0:T(8,128)(2,1)S(1)} %get-tuple-element.47.refs_0_), channel_id=1, source_target_pairs={{4,0},{6,2},{5,1},{7,3},{20,16},{22,18},{21,17},{23,19}} | collective-permute-start | bytes 2850824 | tf_op jit(solution)/shard_map/ppermute | solution.py:241
  66.4 26.3 %collective-permute-start.9 = (bf16[128,3712]{1,0:T(8,128)(2,1)S(1)}, bf16[128,3712]{1,0:T(8,128)(2,1)S(1)}, u32[]{:S(2)}, u32[]{:S(2)}) collective-permute-start(bf16[128,3712]{1,0:T(8,128)(2,1)S(1)} %get-tuple-element.48.refs_1_), channel_id=1, source_target_pairs={{8,12},{10,14},{9,13},{11,15},{24,28},{26,30},{25,29},{27,31}} | collective-permute-start | bytes 2850824 | tf_op jit(solution)/shard_map/ppermute | solution.py:241
  67.1 16.0 %collective-permute-start.10 = (bf16[80,3584]{1,0:T(8,128)(2,1)S(1)}, bf16[80,3584]{1,0:T(8,128)(2,1)S(1)}, u32[]{:S(2)}, u32[]{:S(2)}) collective-permute-start(bf16[80,3584]{1,0:T(8,128)(2,1)S(1)} %get-tuple-element.50), channel_id=1, source_target_pairs={{0,2},{2,0},{4,6},{6,4},{8,10},{10,8},{12,14},{14,12},{1,3},{3,1},... | collective-permute-start | bytes 1720328 | tf_op jit(solution)/shard_map/ppermute | solution.py:244
  69.7 23.0 %collective-permute-start.11 = (bf16[80,3712]{1,0:T(8,128)(2,1)S(1)}, bf16[80,3712]{1,0:T(8,128)(2,1)S(1)}, u32[]{:S(2)}, u32[]{:S(2)}) collective-permute-start(bf16[80,3712]{1,0:T(8,128)(2,1)S(1)} %get-tuple-element.52), channel_id=1, source_target_pairs={{0,2},{2,0},{4,6},{6,4},{8,10},{10,8},{12,14},{14,12},{1,3},{3,1},... | collective-permute-start | bytes 1781768 | tf_op jit(solution)/shard_map/ppermute | solution.py:244
  83.7 21.5 %collective-permute-start.13 = (bf16[128,3584]{1,0:T(8,128)(2,1)S(1)}, bf16[128,3584]{1,0:T(8,128)(2,1)S(1)}, u32[]{:S(2)}, u32[]{:S(2)}) collective-permute-start(bf16[128,3584]{1,0:T(8,128)(2,1)S(1)} %shard_map.70.refs_4_), channel_id=1, source_target_pairs={{8,4},{10,6},{12,8},{14,10},{9,5},{11,7},{13,9},{15,11},{24,20},{2... | collective-permute-start | bytes 2752520 | tf_op jit(solution)/shard_map/ppermute | solution.py:241
  84.4 20.8 %collective-permute-start.14 = (bf16[128,3584]{1,0:T(8,128)(2,1)S(1)}, bf16[128,3584]{1,0:T(8,128)(2,1)S(1)}, u32[]{:S(2)}, u32[]{:S(2)}) collective-permute-start(bf16[128,3584]{1,0:T(8,128)(2,1)S(1)} %shard_map.70.refs_4_), channel_id=1, source_target_pairs={{0,4},{2,6},{4,8},{6,10},{1,5},{3,7},{5,9},{7,11},{16,20},{18,22},... | collective-permute-start | bytes 2752520 | tf_op jit(solution)/shard_map/ppermute | solution.py:241
  93.9 14.6 %collective-permute-start.12 = (bf16[80,3712]{1,0:T(8,128)(2,1)S(1)}, bf16[80,3712]{1,0:T(8,128)(2,1)S(1)}, u32[]{:S(2)}, u32[]{:S(2)}) collective-permute-start(bf16[80,3712]{1,0:T(8,128)(2,1)S(1)} %get-tuple-element.56), channel_id=1, source_target_pairs={{0,2},{2,0},{4,6},{6,4},{8,10},{10,8},{12,14},{14,12},{1,3},{3,1},... | collective-permute-start | bytes 1781768 | tf_op jit(solution)/shard_map/ppermute | solution.py:244
  104.6 16.2 %collective-permute-start.16 = (bf16[80,3584]{1,0:T(8,128)(2,1)S(1)}, bf16[80,3584]{1,0:T(8,128)(2,1)S(1)}, u32[]{:S(2)}, u32[]{:S(2)}) collective-permute-start(bf16[80,3584]{1,0:T(8,128)(2,1)S(1)} %get-tuple-element.62), channel_id=1, source_target_pairs={{0,2},{2,0},{4,6},{6,4},{8,10},{10,8},{12,14},{14,12},{1,3},{3,1},... | collective-permute-start | bytes 1720328 | tf_op jit(solution)/shard_map/ppermute | solution.py:244
  117.7 13.2 %collective-permute-start.15 = (bf16[80,3584]{1,0:T(8,128)(2,1)S(1)}, bf16[80,3584]{1,0:T(8,128)(2,1)S(1)}, u32[]{:S(2)}, u32[]{:S(2)}) collective-permute-start(bf16[80,3584]{1,0:T(8,128)(2,1)S(1)} %get-tuple-element.60), channel_id=1, source_target_pairs={{0,2},{2,0},{4,6},{6,4},{8,10},{10,8},{12,14},{14,12},{1,3},{3,1},... | collective-permute-start | bytes 1720328 | tf_op jit(solution)/shard_map/ppermute | solution.py:244
  121.4 17.4 %copy-start.1 = (bf16[80,3712]{1,0:T(8,128)(2,1)S(1)}, bf16[80,3712]{1,0:T(8,128)(2,1)}, u32[]{:S(2)}) copy-start(bf16[80,3712]{1,0:T(8,128)(2,1)} %copy-done) | copy-start | bytes 1781764
  121.4 17.4 %copy-start.3 = (bf16[80,3712]{1,0:T(8,128)(2,1)S(1)}, bf16[80,3712]{1,0:T(8,128)(2,1)}, u32[]{:S(2)}) copy-start(bf16[80,3712]{1,0:T(8,128)(2,1)} %copy-done.2) | copy-start | bytes 1781764
  121.5 27.8 %collective-permute-start.19 = (bf16[128,3584]{1,0:T(8,128)(2,1)S(1)}, bf16[128,3584]{1,0:T(8,128)(2,1)S(1)}, u32[]{:S(2)}, u32[]{:S(2)}) collective-permute-start(bf16[128,3584]{1,0:T(8,128)(2,1)S(1)} %shard_map.74.refs_4_.refs_0_), channel_id=1, source_target_pairs={{0,8},{2,10},{12,4},{14,6},{1,9},{3,11},{13,5},{15,7},{16,24},{18,... | collective-permute-start | bytes 2752520 | tf_op jit(solution)/shard_map/ppermute | solution.py:241
  131.5 31.3 %collective-permute-start.18 = (bf16[128,3584]{1,0:T(8,128)(2,1)S(1)}, bf16[128,3584]{1,0:T(8,128)(2,1)S(1)}, u32[]{:S(2)}, u32[]{:S(2)}) collective-permute-start(bf16[128,3584]{1,0:T(8,128)(2,1)S(1)} %shard_map.75.refs_6_), channel_id=1, source_target_pairs={{0,4},{2,6},{12,8},{14,10},{1,5},{3,7},{13,9},{15,11},{16,20},{18,... | collective-permute-start | bytes 2752520 | tf_op jit(solution)/shard_map/ppermute | solution.py:241
  137.4 37.3 %collective-permute-start.20 = (bf16[128,3584]{1,0:T(8,128)(2,1)S(1)}, bf16[128,3584]{1,0:T(8,128)(2,1)S(1)}, u32[]{:S(2)}, u32[]{:S(2)}) collective-permute-start(bf16[128,3584]{1,0:T(8,128)(2,1)S(1)} %shard_map.75.refs_6_), channel_id=1, source_target_pairs={{4,0},{6,2},{8,12},{10,14},{5,1},{7,3},{9,13},{11,15},{20,16},{22,... | collective-permute-start | bytes 2752520 | tf_op jit(solution)/shard_map/ppermute | solution.py:241
  163.0 19.3 %collective-permute-start.21 = (bf16[128,3584]{1,0:T(8,128)(2,1)S(1)}, bf16[128,3584]{1,0:T(8,128)(2,1)S(1)}, u32[]{:S(2)}, u32[]{:S(2)}) collective-permute-start(bf16[128,3584]{1,0:T(8,128)(2,1)S(1)} %shard_map.78.refs_4_), channel_id=1, source_target_pairs={{4,12},{6,14},{8,0},{10,2},{5,13},{7,15},{9,1},{11,3},{20,28},{22,... | collective-permute-start | bytes 2752520 | tf_op jit(solution)/shard_map/ppermute | solution.py:241
  164.3 9.8 %collective-permute-start.17 = (bf16[80,3584]{1,0:T(8,128)(2,1)S(1)}, bf16[80,3584]{1,0:T(8,128)(2,1)S(1)}, u32[]{:S(2)}, u32[]{:S(2)}) collective-permute-start(bf16[80,3584]{1,0:T(8,128)(2,1)S(1)} %get-tuple-element.64), channel_id=1, source_target_pairs={{0,2},{2,0},{4,6},{6,4},{8,10},{10,8},{12,14},{14,12},{1,3},{3,1},... | collective-permute-start | bytes 1720328 | tf_op jit(solution)/shard_map/ppermute | solution.py:244

commit v11 on v9

--- a/solution.py
+++ b/solution.py
@@ -57,8 +57,16 @@
 
 
 def first_kernel(experts, tokens, routes, scale, gate_w, up_w, block, *refs):
-    picked, (stack, held, sems) = refs[:4], refs[4:]
+    picked, (stack, held, route_held, scale_held, sems, own_sems) = refs[:4], refs[4:]
     pieces = sems.shape[2]
+    count, width = tokens.shape
+    ins = [
+        pltpu.make_async_copy(routes, route_held, own_sems.at[0]),
+        pltpu.make_async_copy(scale, scale_held, own_sems.at[1]),
+        pltpu.make_async_copy(tokens, block.at[:, :width], own_sems.at[2]),
+    ]
+    for copy in ins:
+        copy.start()
     rows = gate_w.shape[0] // pieces
     fetch, store = [], []
     for k in range(pieces):
@@ -68,19 +76,20 @@
             store.append(pltpu.make_async_copy(held.at[n, cut], stack.at[n, cut], sems.at[1, n, k]))
     for copy in fetch:
         copy.start()
-    count, width = tokens.shape
+    for copy in ins[:2]:
+        copy.wait()
     lane = lax.broadcasted_iota(jnp.int32, (count, block.shape[1] - width), 1)
     expert, part = lax.rem(lane, experts), lax.div(lane, experts)
     weight = jnp.zeros(lane.shape, jnp.float32)
-    routes, scale = routes[...].T, scale[...].T
+    routes, scale = route_held[...].T, scale_held[...].T
     for r in range(routes.shape[1]):
         weight += jnp.where(routes[:, r : r + 1] == expert, scale[:, r : r + 1], 0.0)
     high = weight.astype(jnp.bfloat16).astype(jnp.float32)
     middle = (weight - high).astype(jnp.bfloat16).astype(jnp.float32)
     low = weight - high - middle
     marks = jnp.where(part == 0, high, jnp.where(part == 1, middle, jnp.where(part == 2, low, 0.0)))
-    block[:, :width] = tokens[...]
     block[:, width:] = marks.astype(jnp.bfloat16)
+    ins[2].wait()
     for arrived, leaving in zip(fetch, store):
         arrived.wait()
         leaving.start()
@@ -213,14 +222,20 @@
             bf16((count, wide)),
             bf16((count, cap)),
             bf16((count, cap)),
-            bf16((cap, wide)),
+            hbm((cap, wide)),
             bf16((cap, wide)),
             hbm((2, width, hidden)),
         ],
         [*map(in_hbm, (tokens, routes.T, route_scale.T, own[0], own[1]))],
         (),
-        [pltpu.VMEM((2, width, hidden), jnp.bfloat16), pltpu.SemaphoreType.DMA((2, 2, 4))],
-        [IN_VMEM] * 3 + [ANYWHERE] * 2,
+        [
+            pltpu.VMEM((2, width, hidden), jnp.bfloat16),
+            pltpu.VMEM(routes.shape[::-1], routes.dtype),
+            pltpu.VMEM(routes.shape[::-1], route_scale.dtype),
+            pltpu.SemaphoreType.DMA((2, 2, 8)),
+            pltpu.SemaphoreType.DMA((3,)),
+        ],
+        [ANYWHERE] * 5,
         out_specs=[IN_VMEM] * 5 + [ANYWHERE],
     )
     swap = functools.partial(lax.ppermute, axis_name="local", perm=[(0, 1), (1, 0)])
@@ -260,10 +275,12 @@
             ],
             [IN_VMEM] * 2 + [ANYWHERE] * 4,
             32,
+            cost=64 * MIB,
         )
 
-    def spread(maps, own_out, other_out, extras=(), after=()):
-        return call(spread_kernel, [bf16((count, width))], [*maps, own_out, other_out, *extras], after)[0]
+    def spread(maps, own_out, other_out, extras=(), after=(), cost=0):
+        ins = [*maps, own_out, other_out, *extras]
+        return call(spread_kernel, [bf16((count, width))], ins, after, cost=cost)[0]
 
     plan = arrivals(places)
     held = {}
@@ -346,10 +363,9 @@
     do_expert(0)
     do_spread(places - 1)
     near = returned.pop(places - 3)
-    (summed,) = ordered(call_sum, [*returned.pop(0), *near] if places > 3 else near, cost=128 * MIB)
+    total = ordered(spread, picks[0][0], *outs[0], [*returned.pop(0), *near] if places > 3 else near, cost=128 * MIB)
     (joined,) = ordered(call_sum, [kept[places - 2], along(kept[places - 1], hops)])
-    returned.append([summed, along(joined, [(q, origin(q, places - 2)) for _, q in hops])])
-    total = ordered(spread, picks[0][0], *outs[0])
+    returned.append([along(joined, [(q, origin(q, places - 2)) for _, q in hops])])
     total = total.astype(jnp.float32)
     for block in sum(returned, []):
         total = total + block.astype(jnp.float32)

time: 180 us -> 180 us (level)
    pallas_call x15 -> x14, Pallas kernels: 50.4 us -> 50.2 us  [call(): pl.pallas_call(body, out_shape=outs, in_specs=specs, out_specs=out_specs...]
  transfers between devices with their start and end apart: 22 -> 22, of which waited for: 13 -> 12; matrix products, arithmetic and copies ran while one was open for 0% -> 0% of each run, Pallas kernels for 24% -> 24%
where the time goes in v11:
time: 180 us; the launch traced here: 179 us
  waiting for transfers between devices  89.7 us (50%)
  Pallas kernels  50.2 us (28%)
  starting transfers between devices  37.9 us (21%)
    pallas_call x14, Pallas kernels, call(): pl.pallas_call(body, out_shape=outs, in_specs=specs, out_specs=out_specs...  50.2 us
    ppermute x8, waiting for transfers between devices, across(): return lax.ppermute(block, 'node', [(n, n ^ 1) for n in range(experts)])  48.7 us
    ppermute x12, waiting for transfers between devices, along(): return lax.ppermute(block, 'node', moves)  40.9 us
    ppermute x12, starting transfers between devices, along(): return lax.ppermute(block, 'node', moves)  25.7 us
    ppermute x8, starting transfers between devices, across(): return lax.ppermute(block, 'node', [(n, n ^ 1) for n in range(experts)])  11.6 us
  transfers between devices with their start and end apart: 22, of which 12 were waited for; matrix products, arithmetic and copies ran while one was open for 0% of the time, Pallas kernels for 24%

profile of v11, /device:TPU:0, one launch (start us, length us, event | category | flops | bytes accessed | tf_op | source)
XLA Modules:
  0.0 179.3 jit_solution(6538116657852588941)
XLA Ops:
  0.0 7.3 %shard_map.64 = (bf16[128,3712]{1,0:T(8,128)(2,1)S(1)}, bf16[128,80]{1,0:T(8,128)(2,1)S(1)}, bf16[128,80]{1,0:T(8,128)(2,1)S(1)}, bf16[80,3712]{1,0:T(8,128)(2,1...) custom-call(bf16[128,3584]{1,0:T(8,128)(2,1)} %tokens.1, s32[2,128]{1,0:T(2,128)} %bitcast.7, ...), custom_call_target="tpu_custom_call" | custom-call | tf_op jit(solution)/shard_map/pallas_call | solution.py:33
  7.3 0.5 collective-permute-start.1
  7.8 0.1 collective-permute-start.2
  7.9 5.0 %collective-permute-start.3 = (bf16[128,3712]{1,0:T(8,128)(2,1)S(1)}, bf16[128,3712]{1,0:T(8,128)(2,1)S(1)}, u32[]{:S(2)}, u32[]{:S(2)}) collective-permute-start(bf16[128,3712]{1,0:T(8,128)(2,1)S(1)} %get-tuple-element.40), channel_id=1, source_target_pairs={{0,4},{2,6},{4,8},{6,10},{8,12},{10,14},{1,5},{3,7},{5,9},{7,11},{... | collective-permute-start | bytes 2850824 | tf_op jit(solution)/shard_map/ppermute | solution.py:246
  12.8 1.3 collective-permute-start.4
  14.1 1.6 collective-permute-start
  15.7 13.6 %collective-permute-done.refs_2_.refs_1_ = bf16[80,3712]{1,0:T(8,128)(2,1)S(1)} collective-permute-done((bf16[80,3712]{1,0:T(8,128)(2,1)S(1)}, bf16[80,3712]{1,0:T(8,128)(2,1)S(1)}, u32[]{:S(2)}, u32[]{:S(2)}) %collective-permute-start) | collective-permute-done | bytes 593952 | tf_op jit(solution)/shard_map/ppermute | solution.py:249
  29.3 4.0 %collective-permute-done.3.refs_0_ = bf16[128,3712]{1,0:T(8,128)(2,1)S(1)} collective-permute-done((bf16[128,3712]{1,0:T(8,128)(2,1)S(1)}, bf16[128,3712]{1,0:T(8,128)(2,1)S(1)}, u32[]{:S(2)}, u32[]{:S(2)}) %collective-permute-start.3) | collective-permute-done | bytes 950304 | tf_op jit(solution)/shard_map/ppermute | solution.py:246
  33.3 4.2 %collective-permute-done.4.refs_1_ = bf16[128,3712]{1,0:T(8,128)(2,1)S(1)} collective-permute-done((bf16[128,3712]{1,0:T(8,128)(2,1)S(1)}, bf16[128,3712]{1,0:T(8,128)(2,1)S(1)}, u32[]{:S(2)}, u32[]{:S(2)}) %collective-permute-start.4) | collective-permute-done | bytes 950304 | tf_op jit(solution)/shard_map/ppermute | solution.py:246
  37.5 0.0 copy-done
  37.5 0.7 collective-permute-start.5
  38.2 1.3 collective-permute-start.6
  39.5 1.0 shard_map.66
  40.6 1.6 collective-permute-start.7
  42.1 12.7 %collective-permute-done.7.refs_1_.refs_3_ = bf16[80,3712]{1,0:T(8,128)(2,1)S(1)} collective-permute-done((bf16[80,3712]{1,0:T(8,128)(2,1)S(1)}, bf16[80,3712]{1,0:T(8,128)(2,1)S(1)}, u32[]{:S(2)}, u32[]{:S(2)}) %collective-permute-start.7) | collective-permute-done | bytes 593952 | tf_op jit(solution)/shard_map/ppermute | solution.py:249
  54.9 0.0 collective-permute-done.2.refs_5_
  54.9 0.0 collective-permute-done.1.refs_3_
  54.9 9.2 %shard_map.67 = (bf16[80,3584]{1,0:T(8,128)(2,1)S(1)}, bf16[80,3584]{1,0:T(8,128)(2,1)S(1)}) custom-call(bf16[80,3712]{1,0:T(8,128)(2,1)S(1)} %get-tuple-element.43.refs_0_, bf16[80,3712]{1,0:T(8,128)(2,1)S(1)} %collective-permute-done.7.refs_1_.refs_3_, bf16[2,3584,512]{2,1,0:T(8,128)(2,1)} %get-tuple-element.39.refs_2_, ...), custom_call_target="tpu_custom_call" | custom-call | bytes 67108864 | tf_op jit(solution)/shard_map/pallas_call | solution.py:33
  64.1 0.0 collective-permute-done.5.refs_0_
  64.1 0.2 collective-permute-done.6.refs_1_
  64.3 0.1 shard_map.68
  64.4 0.7 collective-permute-start.10
  65.2 1.3 collective-permute-start.9
  66.5 1.6 collective-permute-start.11
  68.1 1.0 shard_map.69
  69.1 0.6 collective-permute-start.8
  69.6 12.8 %collective-permute-done.11.refs_3_ = bf16[80,3584]{1,0:T(8,128)(2,1)S(1)} collective-permute-done((bf16[80,3584]{1,0:T(8,128)(2,1)S(1)}, bf16[80,3584]{1,0:T(8,128)(2,1)S(1)}, u32[]{:S(2)}, u32[]{:S(2)}) %collective-permute-start.11) | collective-permute-done | bytes 573472 | tf_op jit(solution)/shard_map/ppermute | solution.py:249
  82.4 0.6 shard_map.70.refs_4_
  83.1 0.0 collective-permute-done.10.refs_3_
  83.1 6.8 %collective-permute-done.9.refs_1_ = bf16[128,3712]{1,0:T(8,128)(2,1)S(1)} collective-permute-done((bf16[128,3712]{1,0:T(8,128)(2,1)S(1)}, bf16[128,3712]{1,0:T(8,128)(2,1)S(1)}, u32[]{:S(2)}, u32[]{:S(2)}) %collective-permute-start.9) | collective-permute-done | bytes 950304 | tf_op jit(solution)/shard_map/ppermute | solution.py:246
  89.9 1.0 shard_map.71
  90.9 1.6 collective-permute-start.13
  92.5 0.7 collective-permute-start.14
  93.2 2.3 %collective-permute-start.15 = (bf16[128,3584]{1,0:T(8,128)(2,1)S(1)}, bf16[128,3584]{1,0:T(8,128)(2,1)S(1)}, u32[]{:S(2)}, u32[]{:S(2)}) collective-permute-start(bf16[128,3584]{1,0:T(8,128)(2,1)S(1)} %shard_map.70.refs_4_), channel_id=1, source_target_pairs={{0,4},{2,6},{4,8},{6,10},{1,5},{3,7},{5,9},{7,11},{16,20},{18,22},... | collective-permute-start | bytes 2752520 | tf_op jit(solution)/shard_map/ppermute | solution.py:246
  95.5 0.0 collective-permute-done.8.refs_1_
  95.5 9.2 %shard_map.72 = (bf16[80,3584]{1,0:T(8,128)(2,1)S(1)}, bf16[80,3584]{1,0:T(8,128)(2,1)S(1)}) custom-call(bf16[80,3712]{1,0:T(8,128)(2,1)S(1)} %get-tuple-element.51.refs_0_, bf16[80,3712]{1,0:T(8,128)(2,1)S(1)} %collective-permute-done.8.refs_1_, bf16[2,3584,512]{2,1,0:T(8,128)(2,1)} %get-tuple-element.39.refs_2_, ...), custom_call_target="tpu_custom_call" | custom-call | bytes 67108864 | tf_op jit(solution)/shard_map/pallas_call | solution.py:33
  104.7 0.6 collective-permute-start.12
  105.3 0.5 collective-permute-done.13.refs_1_
  105.8 9.2 %shard_map.73 = (bf16[80,3584]{1,0:T(8,128)(2,1)S(1)}, bf16[80,3584]{1,0:T(8,128)(2,1)S(1)}) custom-call(bf16[80,3712]{1,0:T(8,128)(2,1)S(1)} %get-tuple-element.58.refs_0_, bf16[80,3712]{1,0:T(8,128)(2,1)S(1)} %collective-permute-done.13.refs_1_, bf16[2,3584,512]{2,1,0:T(8,128)(2,1)} %get-tuple-element.39.refs_2_, ...), custom_call_target="tpu_custom_call" | custom-call | bytes 67108864 | tf_op jit(solution)/shard_map/pallas_call | solution.py:33
  115.1 0.0 copy-start.1
  115.1 0.0 copy-start.2
  115.1 2.5 %collective-permute-start.18 = (bf16[80,3584]{1,0:T(8,128)(2,1)S(1)}, bf16[80,3584]{1,0:T(8,128)(2,1)S(1)}, u32[]{:S(2)}, u32[]{:S(2)}) collective-permute-start(bf16[80,3584]{1,0:T(8,128)(2,1)S(1)} %get-tuple-element.64), channel_id=1, source_target_pairs={{0,2},{2,0},{4,6},{6,4},{8,10},{10,8},{12,14},{14,12},{1,3},{3,1},... | collective-permute-start | bytes 1720328 | tf_op jit(solution)/shard_map/ppermute | solution.py:249
  117.6 0.0 collective-permute-done.14.refs_5_.refs_4_
  117.6 0.0 collective-permute-done.15.refs_6_.refs_5_
  117.6 2.2 %collective-permute-done.12.refs_3_ = bf16[80,3584]{1,0:T(8,128)(2,1)S(1)} collective-permute-done((bf16[80,3584]{1,0:T(8,128)(2,1)S(1)}, bf16[80,3584]{1,0:T(8,128)(2,1)S(1)}, u32[]{:S(2)}, u32[]{:S(2)}) %collective-permute-start.12) | collective-permute-done | bytes 573472 | tf_op jit(solution)/shard_map/ppermute | solution.py:249
  119.8 0.6 shard_map.74.refs_6_.refs_0_
  120.4 8.5 %collective-permute-start.17 = (bf16[128,3584]{1,0:T(8,128)(2,1)S(1)}, bf16[128,3584]{1,0:T(8,128)(2,1)S(1)}, u32[]{:S(2)}, u32[]{:S(2)}) collective-permute-start(bf16[128,3584]{1,0:T(8,128)(2,1)S(1)} %shard_map.74.refs_6_.refs_0_), channel_id=1, source_target_pairs={{0,8},{2,10},{12,4},{14,6},{1,9},{3,11},{13,5},{15,7},{16,24},{18,... | collective-permute-start | bytes 2752520 | tf_op jit(solution)/shard_map/ppermute | solution.py:246
  129.0 0.0 copy-done.1
  129.0 0.0 copy-done.2
  129.0 9.2 %shard_map.75 = (bf16[80,3584]{1,0:T(8,128)(2,1)S(1)}, bf16[80,3584]{1,0:T(8,128)(2,1)S(1)}) custom-call(bf16[80,3712]{1,0:T(8,128)(2,1)S(1)} %copy-done.2, bf16[80,3712]{1,0:T(8,128)(2,1)S(1)} %copy-done.1, bf16[2,3584,512]{2,1,0:T(8,128)(2,1)} %get-tuple-element.39.refs_2_, bf16[2,3584,512]{2,1,0:T(8,128)(2,1)} %collective-permute-done.1.refs_3_, ...), custom_call_target="tpu_custom_call" | custom-call | bytes 67108864 | tf_op jit(solution)/shard_map/pallas_call | solution.py:33
  138.2 0.0 collective-permute-done.18.refs_3_
  138.2 0.6 shard_map.76.refs_7_
  138.9 1.3 collective-permute-start.20
  140.2 1.6 collective-permute-start.16
  141.8 1.3 collective-permute-start.19
  143.1 6.9 %collective-permute-done.16.refs_3_ = bf16[80,3584]{1,0:T(8,128)(2,1)S(1)} collective-permute-done((bf16[80,3584]{1,0:T(8,128)(2,1)S(1)}, bf16[80,3584]{1,0:T(8,128)(2,1)S(1)}, u32[]{:S(2)}, u32[]{:S(2)}) %collective-permute-start.16) | collective-permute-done | bytes 573472 | tf_op jit(solution)/shard_map/ppermute | solution.py:249
  150.0 0.0 collective-permute-done.17.refs_6_
  150.0 0.8 shard_map.77.refs_2_
  150.8 9.8 %collective-permute-done.20.refs_1_ = bf16[128,3584]{1,0:T(8,128)(2,1)S(1)} collective-permute-done((bf16[128,3584]{1,0:T(8,128)(2,1)S(1)}, bf16[128,3584]{1,0:T(8,128)(2,1)S(1)}, u32[]{:S(2)}, u32[]{:S(2)}) %collective-permute-start.20) | collective-permute-done | bytes 917536 | tf_op jit(solution)/shard_map/ppermute | solution.py:246
  160.6 0.2 shard_map.78
  160.9 1.3 collective-permute-start.21
  162.2 0.0 collective-permute-done.19
  162.2 15.9 %collective-permute-done.21 = bf16[128,3584]{1,0:T(8,128)(2,1)S(1)} collective-permute-done((bf16[128,3584]{1,0:T(8,128)(2,1)S(1)}, bf16[128,3584]{1,0:T(8,128)(2,1)S(1)}, u32[]{:S(2)}, u32[]{:S(2)}) %collective-permute-start.21) | collective-permute-done | bytes 917536 | tf_op jit(solution)/shard_map/ppermute | solution.py:246
  178.1 1.3 add_convert_fusion
  (2 shorter events, 0.0 us)
Async XLA Ops:
  7.3 47.6 %collective-permute-start.1 = (bf16[2,3584,512]{2,1,0:T(8,128)(2,1)}, bf16[2,3584,512]{2,1,0:T(8,128)(2,1)}, u32[]{:S(2)}, u32[]{:S(2)}) collective-permute-start(bf16[2,3584,512]{2,1,0:T(8,128)(2,1)} %get-tuple-element.39.refs_2_), channel_id=1, source_target_pairs={{0,1},{1,0},{2,3},{3,2},{4,5},{5,4},{6,7},{7,6},{8,9},{9,8},{10,11... | collective-permute-start | bytes 22020104 | tf_op jit(solution)/shard_map/ppermute | solution.py:242
  7.8 47.1 %collective-permute-start.2 = (bf16[512,3584]{1,0:T(8,128)(2,1)}, bf16[512,3584]{1,0:T(8,128)(2,1)}, u32[]{:S(2)}, u32[]{:S(2)}) collective-permute-start(bf16[512,3584]{1,0:T(8,128)(2,1)} %bitcast.4.refs_4_), channel_id=1, source_target_pairs={{0,1},{1,0},{2,3},{3,2},{4,5},{5,4},{6,7},{7,6},{8,9},{9,8},{10,11... | collective-permute-start | bytes 11010056 | tf_op jit(solution)/shard_map/ppermute | solution.py:242
  7.9 25.4 %collective-permute-start.3 = (bf16[128,3712]{1,0:T(8,128)(2,1)S(1)}, bf16[128,3712]{1,0:T(8,128)(2,1)S(1)}, u32[]{:S(2)}, u32[]{:S(2)}) collective-permute-start(bf16[128,3712]{1,0:T(8,128)(2,1)S(1)} %get-tuple-element.40), channel_id=1, source_target_pairs={{0,4},{2,6},{4,8},{6,10},{8,12},{10,14},{1,5},{3,7},{5,9},{7,11},{... | collective-permute-start | bytes 2850824 | tf_op jit(solution)/shard_map/ppermute | solution.py:246
  12.8 24.7 %collective-permute-start.4 = (bf16[128,3712]{1,0:T(8,128)(2,1)S(1)}, bf16[128,3712]{1,0:T(8,128)(2,1)S(1)}, u32[]{:S(2)}, u32[]{:S(2)}) collective-permute-start(bf16[128,3712]{1,0:T(8,128)(2,1)S(1)} %get-tuple-element.40), channel_id=1, source_target_pairs={{4,0},{6,2},{8,4},{10,6},{12,8},{14,10},{5,1},{7,3},{9,5},{11,7},{... | collective-permute-start | bytes 2850824 | tf_op jit(solution)/shard_map/ppermute | solution.py:246
  14.1 15.2 %collective-permute-start = (bf16[80,3712]{1,0:T(8,128)(2,1)S(1)}, bf16[80,3712]{1,0:T(8,128)(2,1)S(1)}, u32[]{:S(2)}, u32[]{:S(2)}) collective-permute-start(bf16[80,3712]{1,0:T(8,128)(2,1)S(1)} %get-tuple-element.38), channel_id=1, source_target_pairs={{0,2},{2,0},{4,6},{6,4},{8,10},{10,8},{12,14},{14,12},{1,3},{3,1},... | collective-permute-start | bytes 1781768 | tf_op jit(solution)/shard_map/ppermute | solution.py:249
  29.3 8.2 %copy-start = (bf16[80,3712]{1,0:T(8,128)(2,1)}, bf16[80,3712]{1,0:T(8,128)(2,1)S(1)}, u32[]{:S(2)}) copy-start(bf16[80,3712]{1,0:T(8,128)(2,1)S(1)} %collective-permute-done.refs_2_.refs_1_) | copy-start | bytes 1781764
  37.5 26.6 %collective-permute-start.5 = (bf16[128,3712]{1,0:T(8,128)(2,1)S(1)}, bf16[128,3712]{1,0:T(8,128)(2,1)S(1)}, u32[]{:S(2)}, u32[]{:S(2)}) collective-permute-start(bf16[128,3712]{1,0:T(8,128)(2,1)S(1)} %get-tuple-element.41.refs_1_.refs_2_), channel_id=1, source_target_pairs={{4,8},{6,10},{8,12},{10,14},{5,9},{7,11},{9,13},{11,15},{20,24},{2... | collective-permute-start | bytes 2850824 | tf_op jit(solution)/shard_map/ppermute | solution.py:246
  38.2 26.1 %collective-permute-start.6 = (bf16[128,3712]{1,0:T(8,128)(2,1)S(1)}, bf16[128,3712]{1,0:T(8,128)(2,1)S(1)}, u32[]{:S(2)}, u32[]{:S(2)}) collective-permute-start(bf16[128,3712]{1,0:T(8,128)(2,1)S(1)} %get-tuple-element.42.refs_0_), channel_id=1, source_target_pairs={{4,0},{6,2},{8,4},{10,6},{5,1},{7,3},{9,5},{11,7},{20,16},{22,18},... | collective-permute-start | bytes 2850824 | tf_op jit(solution)/shard_map/ppermute | solution.py:246
  40.6 14.3 %collective-permute-start.7 = (bf16[80,3712]{1,0:T(8,128)(2,1)S(1)}, bf16[80,3712]{1,0:T(8,128)(2,1)S(1)}, u32[]{:S(2)}, u32[]{:S(2)}) collective-permute-start(bf16[80,3712]{1,0:T(8,128)(2,1)S(1)} %get-tuple-element.44), channel_id=1, source_target_pairs={{0,2},{2,0},{4,6},{6,4},{8,10},{10,8},{12,14},{14,12},{1,3},{3,1},... | collective-permute-start | bytes 1781768 | tf_op jit(solution)/shard_map/ppermute | solution.py:249
  64.4 18.6 %collective-permute-start.10 = (bf16[128,3712]{1,0:T(8,128)(2,1)S(1)}, bf16[128,3712]{1,0:T(8,128)(2,1)S(1)}, u32[]{:S(2)}, u32[]{:S(2)}) collective-permute-start(bf16[128,3712]{1,0:T(8,128)(2,1)S(1)} %get-tuple-element.48.refs_1_), channel_id=1, source_target_pairs={{8,12},{10,14},{9,13},{11,15},{24,28},{26,30},{25,29},{27,31}} | collective-permute-start | bytes 2850824 | tf_op jit(solution)/shard_map/ppermute | solution.py:246
  65.2 24.7 %collective-permute-start.9 = (bf16[128,3712]{1,0:T(8,128)(2,1)S(1)}, bf16[128,3712]{1,0:T(8,128)(2,1)S(1)}, u32[]{:S(2)}, u32[]{:S(2)}) collective-permute-start(bf16[128,3712]{1,0:T(8,128)(2,1)S(1)} %get-tuple-element.47.refs_0_), channel_id=1, source_target_pairs={{4,0},{6,2},{5,1},{7,3},{20,16},{22,18},{21,17},{23,19}} | collective-permute-start | bytes 2850824 | tf_op jit(solution)/shard_map/ppermute | solution.py:246
  66.5 16.0 %collective-permute-start.11 = (bf16[80,3584]{1,0:T(8,128)(2,1)S(1)}, bf16[80,3584]{1,0:T(8,128)(2,1)S(1)}, u32[]{:S(2)}, u32[]{:S(2)}) collective-permute-start(bf16[80,3584]{1,0:T(8,128)(2,1)S(1)} %get-tuple-element.54), channel_id=1, source_target_pairs={{0,2},{2,0},{4,6},{6,4},{8,10},{10,8},{12,14},{14,12},{1,3},{3,1},... | collective-permute-start | bytes 1720328 | tf_op jit(solution)/shard_map/ppermute | solution.py:249
  69.1 26.4 %collective-permute-start.8 = (bf16[80,3712]{1,0:T(8,128)(2,1)S(1)}, bf16[80,3712]{1,0:T(8,128)(2,1)S(1)}, u32[]{:S(2)}, u32[]{:S(2)}) collective-permute-start(bf16[80,3712]{1,0:T(8,128)(2,1)S(1)} %get-tuple-element.52), channel_id=1, source_target_pairs={{0,2},{2,0},{4,6},{6,4},{8,10},{10,8},{12,14},{14,12},{1,3},{3,1},... | collective-permute-start | bytes 1781768 | tf_op jit(solution)/shard_map/ppermute | solution.py:249
  90.9 14.9 %collective-permute-start.13 = (bf16[80,3712]{1,0:T(8,128)(2,1)S(1)}, bf16[80,3712]{1,0:T(8,128)(2,1)S(1)}, u32[]{:S(2)}, u32[]{:S(2)}) collective-permute-start(bf16[80,3712]{1,0:T(8,128)(2,1)S(1)} %get-tuple-element.59), channel_id=1, source_target_pairs={{0,2},{2,0},{4,6},{6,4},{8,10},{10,8},{12,14},{14,12},{1,3},{3,1},... | collective-permute-start | bytes 1781768 | tf_op jit(solution)/shard_map/ppermute | solution.py:249
  92.5 25.1 %collective-permute-start.14 = (bf16[128,3584]{1,0:T(8,128)(2,1)S(1)}, bf16[128,3584]{1,0:T(8,128)(2,1)S(1)}, u32[]{:S(2)}, u32[]{:S(2)}) collective-permute-start(bf16[128,3584]{1,0:T(8,128)(2,1)S(1)} %shard_map.70.refs_4_), channel_id=1, source_target_pairs={{8,4},{10,6},{12,8},{14,10},{9,5},{11,7},{13,9},{15,11},{24,20},{2... | collective-permute-start | bytes 2752520 | tf_op jit(solution)/shard_map/ppermute | solution.py:246
  93.2 24.4 %collective-permute-start.15 = (bf16[128,3584]{1,0:T(8,128)(2,1)S(1)}, bf16[128,3584]{1,0:T(8,128)(2,1)S(1)}, u32[]{:S(2)}, u32[]{:S(2)}) collective-permute-start(bf16[128,3584]{1,0:T(8,128)(2,1)S(1)} %shard_map.70.refs_4_), channel_id=1, source_target_pairs={{0,4},{2,6},{4,8},{6,10},{1,5},{3,7},{5,9},{7,11},{16,20},{18,22},... | collective-permute-start | bytes 2752520 | tf_op jit(solution)/shard_map/ppermute | solution.py:246
  104.7 15.1 %collective-permute-start.12 = (bf16[80,3584]{1,0:T(8,128)(2,1)S(1)}, bf16[80,3584]{1,0:T(8,128)(2,1)S(1)}, u32[]{:S(2)}, u32[]{:S(2)}) collective-permute-start(bf16[80,3584]{1,0:T(8,128)(2,1)S(1)} %get-tuple-element.57), channel_id=1, source_target_pairs={{0,2},{2,0},{4,6},{6,4},{8,10},{10,8},{12,14},{14,12},{1,3},{3,1},... | collective-permute-start | bytes 1720328 | tf_op jit(solution)/shard_map/ppermute | solution.py:249
  115.1 13.9 %copy-start.1 = (bf16[80,3712]{1,0:T(8,128)(2,1)S(1)}, bf16[80,3712]{1,0:T(8,128)(2,1)}, u32[]{:S(2)}) copy-start(bf16[80,3712]{1,0:T(8,128)(2,1)} %copy-done) | copy-start | bytes 1781764
  115.1 13.9 %copy-start.2 = (bf16[80,3712]{1,0:T(8,128)(2,1)S(1)}, bf16[80,3712]{1,0:T(8,128)(2,1)}, u32[]{:S(2)}) copy-start(bf16[80,3712]{1,0:T(8,128)(2,1)} %get-tuple-element.37.refs_0_) | copy-start | bytes 1781764
  115.1 23.1 %collective-permute-start.18 = (bf16[80,3584]{1,0:T(8,128)(2,1)S(1)}, bf16[80,3584]{1,0:T(8,128)(2,1)S(1)}, u32[]{:S(2)}, u32[]{:S(2)}) collective-permute-start(bf16[80,3584]{1,0:T(8,128)(2,1)S(1)} %get-tuple-element.64), channel_id=1, source_target_pairs={{0,2},{2,0},{4,6},{6,4},{8,10},{10,8},{12,14},{14,12},{1,3},{3,1},... | collective-permute-start | bytes 1720328 | tf_op jit(solution)/shard_map/ppermute | solution.py:249
  120.4 29.5 %collective-permute-start.17 = (bf16[128,3584]{1,0:T(8,128)(2,1)S(1)}, bf16[128,3584]{1,0:T(8,128)(2,1)S(1)}, u32[]{:S(2)}, u32[]{:S(2)}) collective-permute-start(bf16[128,3584]{1,0:T(8,128)(2,1)S(1)} %shard_map.74.refs_6_.refs_0_), channel_id=1, source_target_pairs={{0,8},{2,10},{12,4},{14,6},{1,9},{3,11},{13,5},{15,7},{16,24},{18,... | collective-permute-start | bytes 2752520 | tf_op jit(solution)/shard_map/ppermute | solution.py:246
  138.9 21.8 %collective-permute-start.20 = (bf16[128,3584]{1,0:T(8,128)(2,1)S(1)}, bf16[128,3584]{1,0:T(8,128)(2,1)S(1)}, u32[]{:S(2)}, u32[]{:S(2)}) collective-permute-start(bf16[128,3584]{1,0:T(8,128)(2,1)S(1)} %shard_map.76.refs_7_), channel_id=1, source_target_pairs={{0,4},{2,6},{12,8},{14,10},{1,5},{3,7},{13,9},{15,11},{16,20},{18,... | collective-permute-start | bytes 2752520 | tf_op jit(solution)/shard_map/ppermute | solution.py:246
  140.2 9.8 %collective-permute-start.16 = (bf16[80,3584]{1,0:T(8,128)(2,1)S(1)}, bf16[80,3584]{1,0:T(8,128)(2,1)S(1)}, u32[]{:S(2)}, u32[]{:S(2)}) collective-permute-start(bf16[80,3584]{1,0:T(8,128)(2,1)S(1)} %get-tuple-element.62), channel_id=1, source_target_pairs={{0,2},{2,0},{4,6},{6,4},{8,10},{10,8},{12,14},{14,12},{1,3},{3,1},... | collective-permute-start | bytes 1720328 | tf_op jit(solution)/shard_map/ppermute | solution.py:249
  141.8 20.3 %collective-permute-start.19 = (bf16[128,3584]{1,0:T(8,128)(2,1)S(1)}, bf16[128,3584]{1,0:T(8,128)(2,1)S(1)}, u32[]{:S(2)}, u32[]{:S(2)}) collective-permute-start(bf16[128,3584]{1,0:T(8,128)(2,1)S(1)} %shard_map.76.refs_7_), channel_id=1, source_target_pairs={{4,0},{6,2},{8,12},{10,14},{5,1},{7,3},{9,13},{11,15},{20,16},{22,... | collective-permute-start | bytes 2752520 | tf_op jit(solution)/shard_map/ppermute | solution.py:246
  160.9 17.2 %collective-permute-start.21 = (bf16[128,3584]{1,0:T(8,128)(2,1)S(1)}, bf16[128,3584]{1,0:T(8,128)(2,1)S(1)}, u32[]{:S(2)}, u32[]{:S(2)}) collective-permute-start(bf16[128,3584]{1,0:T(8,128)(2,1)S(1)} %shard_map.78), channel_id=1, source_target_pairs={{4,12},{6,14},{8,0},{10,2},{5,13},{7,15},{9,1},{11,3},{20,28},{22,... | collective-permute-start | bytes 2752520 | tf_op jit(solution)/shard_map/ppermute | solution.py:246

commit v12 on v11

--- a/solution.py
+++ b/solution.py
@@ -15,9 +15,14 @@
 def arrivals(places):
     plan = []
     for place in range(places):
-        left = [(-1, step) for step in range(1, places - place)]
-        right = [(1, step) for step in range(1, place + 1)]
-        plan.append(left + right if place < places // 2 else right + left)
+        spare, row = [], []
+        for step in range(1, places):
+            here = [way for way in (1, -1) if 0 <= place - way * step < places]
+            if len(here) == 2 and place % 2 == 0:
+                here.reverse()
+            spare += [(way, step) for way in here[1:]]
+            row.append((here[0], step) if here else spare.pop(0))
+        plan.append(row)
     return plan
 
 

time: 180 us -> 185 us (1.028)
  waiting for transfers between devices: 89.7 us -> 98.4 us
  starting transfers between devices: 37.9 us -> 34.4 us
    ppermute x12 -> x11, waiting for transfers between devices: 40.9 us -> 46.3 us  [along(): return lax.ppermute(block, 'node', moves)]
    ppermute x12 -> x11, starting transfers between devices: 25.7 us -> 22.2 us  [along(): return lax.ppermute(block, 'node', moves)]
    ppermute x8, waiting for transfers between devices: 48.7 us -> 52.1 us  [across(): return lax.ppermute(block, 'node', [(n, n ^ 1) for n in range(experts)])]
  transfers between devices with their start and end apart: 22 -> 21, of which waited for: 12 -> 13; matrix products, arithmetic and copies ran while one was open for 0% -> 0% of each run, Pallas kernels for 24% -> 23%
where the time goes in v12:
time: 185 us
  waiting for transfers between devices  98.4 us (53%)
  Pallas kernels  50.3 us (27%)
  starting transfers between devices  34.4 us (19%)
    ppermute x8, waiting for transfers between devices, across(): return lax.ppermute(block, 'node', [(n, n ^ 1) for n in range(experts)])  52.1 us
    pallas_call x14, Pallas kernels, call(): pl.pallas_call(body, out_shape=outs, in_specs=specs, out_specs=out_specs...  50.3 us
    ppermute x11, waiting for transfers between devices, along(): return lax.ppermute(block, 'node', moves)  46.3 us
    ppermute x11, starting transfers between devices, along(): return lax.ppermute(block, 'node', moves)  22.2 us
    ppermute x8, starting transfers between devices, across(): return lax.ppermute(block, 'node', [(n, n ^ 1) for n in range(experts)])  11.7 us
  transfers between devices with their start and end apart: 21, of which 13 were waited for; matrix products, arithmetic and copies ran while one was open for 0% of the time, Pallas kernels for 23%

profile of v12, /device:TPU:0, one launch (start us, length us, event | category | flops | bytes accessed | tf_op | source)
XLA Modules:
  0.0 184.6 jit_solution(336200256013042818)
XLA Ops:
  0.0 7.3 %shard_map.64 = (bf16[128,3712]{1,0:T(8,128)(2,1)S(1)}, bf16[128,80]{1,0:T(8,128)(2,1)S(1)}, bf16[128,80]{1,0:T(8,128)(2,1)S(1)}, bf16[80,3712]{1,0:T(8,128)(2,1...) custom-call(bf16[128,3584]{1,0:T(8,128)(2,1)} %tokens.1, s32[2,128]{1,0:T(2,128)} %bitcast.7, ...), custom_call_target="tpu_custom_call" | custom-call | tf_op jit(solution)/shard_map/pallas_call | solution.py:38
  7.3 0.5 collective-permute-start.1
  7.8 0.1 collective-permute-start.2
  7.9 5.0 %collective-permute-start.3 = (bf16[128,3712]{1,0:T(8,128)(2,1)S(1)}, bf16[128,3712]{1,0:T(8,128)(2,1)S(1)}, u32[]{:S(2)}, u32[]{:S(2)}) collective-permute-start(bf16[128,3712]{1,0:T(8,128)(2,1)S(1)} %get-tuple-element.40), channel_id=1, source_target_pairs={{0,4},{2,6},{4,8},{6,10},{8,12},{10,14},{1,5},{3,7},{5,9},{7,11},{... | collective-permute-start | bytes 2850824 | tf_op jit(solution)/shard_map/ppermute | solution.py:251
  12.8 1.3 collective-permute-start.4
  14.1 1.6 collective-permute-start
  15.7 13.6 %collective-permute-done.refs_2_.refs_1_ = bf16[80,3712]{1,0:T(8,128)(2,1)S(1)} collective-permute-done((bf16[80,3712]{1,0:T(8,128)(2,1)S(1)}, bf16[80,3712]{1,0:T(8,128)(2,1)S(1)}, u32[]{:S(2)}, u32[]{:S(2)}) %collective-permute-start) | collective-permute-done | bytes 593952 | tf_op jit(solution)/shard_map/ppermute | solution.py:254
  29.3 0.0 copy-start
  29.3 4.0 %collective-permute-done.3.refs_0_ = bf16[128,3712]{1,0:T(8,128)(2,1)S(1)} collective-permute-done((bf16[128,3712]{1,0:T(8,128)(2,1)S(1)}, bf16[128,3712]{1,0:T(8,128)(2,1)S(1)}, u32[]{:S(2)}, u32[]{:S(2)}) %collective-permute-start.3) | collective-permute-done | bytes 950304 | tf_op jit(solution)/shard_map/ppermute | solution.py:251
  33.3 4.2 %collective-permute-done.4.refs_1_ = bf16[128,3712]{1,0:T(8,128)(2,1)S(1)} collective-permute-done((bf16[128,3712]{1,0:T(8,128)(2,1)S(1)}, bf16[128,3712]{1,0:T(8,128)(2,1)S(1)}, u32[]{:S(2)}, u32[]{:S(2)}) %collective-permute-start.4) | collective-permute-done | bytes 950304 | tf_op jit(solution)/shard_map/ppermute | solution.py:251
  37.5 0.0 copy-done
  37.5 0.7 collective-permute-start.5
  38.2 1.3 collective-permute-start.6
  39.5 1.0 shard_map.66
  40.6 1.6 collective-permute-start.7
  42.1 12.7 %collective-permute-done.7.refs_1_.refs_3_ = bf16[80,3712]{1,0:T(8,128)(2,1)S(1)} collective-permute-done((bf16[80,3712]{1,0:T(8,128)(2,1)S(1)}, bf16[80,3712]{1,0:T(8,128)(2,1)S(1)}, u32[]{:S(2)}, u32[]{:S(2)}) %collective-permute-start.7) | collective-permute-done | bytes 593952 | tf_op jit(solution)/shard_map/ppermute | solution.py:254
  54.9 0.0 collective-permute-done.2.refs_5_
  54.9 0.0 collective-permute-done.1.refs_3_
  54.9 9.2 %shard_map.67 = (bf16[80,3584]{1,0:T(8,128)(2,1)S(1)}, bf16[80,3584]{1,0:T(8,128)(2,1)S(1)}) custom-call(bf16[80,3712]{1,0:T(8,128)(2,1)S(1)} %get-tuple-element.43.refs_0_, bf16[80,3712]{1,0:T(8,128)(2,1)S(1)} %collective-permute-done.7.refs_1_.refs_3_, bf16[2,3584,512]{2,1,0:T(8,128)(2,1)} %get-tuple-element.39.refs_2_, ...), custom_call_target="tpu_custom_call" | custom-call | bytes 67108864 | tf_op jit(solution)/shard_map/pallas_call | solution.py:38
  64.1 0.0 collective-permute-done.5.refs_0_
  64.1 0.2 collective-permute-done.6.refs_1_
  64.3 0.1 shard_map.68
  64.4 0.7 collective-permute-start.10
  65.2 1.3 collective-permute-start.9
  66.5 1.6 collective-permute-start.11
  68.1 1.0 shard_map.69
  69.1 0.6 collective-permute-start.8
  69.7 12.8 %collective-permute-done.11.refs_3_ = bf16[80,3584]{1,0:T(8,128)(2,1)S(1)} collective-permute-done((bf16[80,3584]{1,0:T(8,128)(2,1)S(1)}, bf16[80,3584]{1,0:T(8,128)(2,1)S(1)}, u32[]{:S(2)}, u32[]{:S(2)}) %collective-permute-start.11) | collective-permute-done | bytes 573472 | tf_op jit(solution)/shard_map/ppermute | solution.py:254
  82.5 0.6 shard_map.70.refs_4_
  83.1 0.0 collective-permute-done.10.refs_3_
  83.1 6.8 %collective-permute-done.9.refs_1_ = bf16[128,3712]{1,0:T(8,128)(2,1)S(1)} collective-permute-done((bf16[128,3712]{1,0:T(8,128)(2,1)S(1)}, bf16[128,3712]{1,0:T(8,128)(2,1)S(1)}, u32[]{:S(2)}, u32[]{:S(2)}) %collective-permute-start.9) | collective-permute-done | bytes 950304 | tf_op jit(solution)/shard_map/ppermute | solution.py:251
  89.9 1.2 shard_map.71
  91.1 1.6 collective-permute-start.13
  92.7 0.0 collective-permute-start.14
  92.7 0.7 collective-permute-done.8.refs_1_
  93.4 9.2 %shard_map.72 = (bf16[80,3584]{1,0:T(8,128)(2,1)S(1)}, bf16[80,3584]{1,0:T(8,128)(2,1)S(1)}) custom-call(bf16[80,3712]{1,0:T(8,128)(2,1)S(1)} %get-tuple-element.51.refs_0_, bf16[80,3712]{1,0:T(8,128)(2,1)S(1)} %collective-permute-done.8.refs_1_, bf16[2,3584,512]{2,1,0:T(8,128)(2,1)} %get-tuple-element.39.refs_2_, ...), custom_call_target="tpu_custom_call" | custom-call | bytes 67108864 | tf_op jit(solution)/shard_map/pallas_call | solution.py:38
  102.6 1.6 collective-permute-start.12
  104.2 3.3 %collective-permute-done.13.refs_1_ = bf16[80,3712]{1,0:T(8,128)(2,1)S(1)} collective-permute-done((bf16[80,3712]{1,0:T(8,128)(2,1)S(1)}, bf16[80,3712]{1,0:T(8,128)(2,1)S(1)}, u32[]{:S(2)}, u32[]{:S(2)}) %collective-permute-start.13) | collective-permute-done | bytes 593952 | tf_op jit(solution)/shard_map/ppermute | solution.py:254
  107.5 9.2 %shard_map.73 = (bf16[80,3584]{1,0:T(8,128)(2,1)S(1)}, bf16[80,3584]{1,0:T(8,128)(2,1)S(1)}) custom-call(bf16[80,3712]{1,0:T(8,128)(2,1)S(1)} %get-tuple-element.58.refs_0_, bf16[80,3712]{1,0:T(8,128)(2,1)S(1)} %collective-permute-done.13.refs_1_, bf16[2,3584,512]{2,1,0:T(8,128)(2,1)} %get-tuple-element.39.refs_2_, ...), custom_call_target="tpu_custom_call" | custom-call | bytes 67108864 | tf_op jit(solution)/shard_map/pallas_call | solution.py:38
  116.7 0.0 copy-start.1
  116.7 0.0 copy-start.2
  116.8 1.6 collective-permute-start.17
  118.3 0.0 collective-permute-done.14.refs_5_.refs_4_
  118.3 1.5 collective-permute-done.12.refs_3_
  119.8 0.6 shard_map.74.refs_6_.refs_0_
  120.4 8.6 %collective-permute-start.16 = (bf16[128,3584]{1,0:T(8,128)(2,1)S(1)}, bf16[128,3584]{1,0:T(8,128)(2,1)S(1)}, u32[]{:S(2)}, u32[]{:S(2)}) collective-permute-start(bf16[128,3584]{1,0:T(8,128)(2,1)S(1)} %shard_map.74.refs_6_.refs_0_), channel_id=1, source_target_pairs={{0,8},{2,10},{12,4},{14,6},{1,9},{3,11},{13,5},{15,7},{16,24},{18,... | collective-permute-start | bytes 2752520 | tf_op jit(solution)/shard_map/ppermute | solution.py:251
  129.0 0.0 copy-done.1
  129.0 0.0 copy-done.2
  129.0 9.2 %shard_map.75 = (bf16[80,3584]{1,0:T(8,128)(2,1)S(1)}, bf16[80,3584]{1,0:T(8,128)(2,1)S(1)}) custom-call(bf16[80,3712]{1,0:T(8,128)(2,1)S(1)} %copy-done.2, bf16[80,3712]{1,0:T(8,128)(2,1)S(1)} %copy-done.1, bf16[2,3584,512]{2,1,0:T(8,128)(2,1)} %get-tuple-element.39.refs_2_, bf16[2,3584,512]{2,1,0:T(8,128)(2,1)} %collective-permute-done.1.refs_3_, ...), custom_call_target="tpu_custom_call" | custom-call | bytes 67108864 | tf_op jit(solution)/shard_map/pallas_call | solution.py:38
  138.2 0.0 collective-permute-done.17.refs_3_
  138.2 0.6 shard_map.76.refs_6_
  138.9 1.3 collective-permute-start.19
  140.2 1.6 collective-permute-start.15
  141.8 0.7 collective-permute-start.18
  142.5 7.5 %collective-permute-done.15.refs_3_ = bf16[80,3584]{1,0:T(8,128)(2,1)S(1)} collective-permute-done((bf16[80,3584]{1,0:T(8,128)(2,1)S(1)}, bf16[80,3584]{1,0:T(8,128)(2,1)S(1)}, u32[]{:S(2)}, u32[]{:S(2)}) %collective-permute-start.15) | collective-permute-done | bytes 573472 | tf_op jit(solution)/shard_map/ppermute | solution.py:254
  150.0 0.0 collective-permute-done.16.refs_5_
  150.0 0.7 shard_map.77.refs_2_
  150.7 9.9 %collective-permute-done.19.refs_1_ = bf16[128,3584]{1,0:T(8,128)(2,1)S(1)} collective-permute-done((bf16[128,3584]{1,0:T(8,128)(2,1)S(1)}, bf16[128,3584]{1,0:T(8,128)(2,1)S(1)}, u32[]{:S(2)}, u32[]{:S(2)}) %collective-permute-start.19) | collective-permute-done | bytes 917536 | tf_op jit(solution)/shard_map/ppermute | solution.py:251
  160.7 0.2 shard_map.78
  160.9 1.3 collective-permute-start.20
  162.2 0.0 collective-permute-done.18
  162.2 21.2 %collective-permute-done.20 = bf16[128,3584]{1,0:T(8,128)(2,1)S(1)} collective-permute-done((bf16[128,3584]{1,0:T(8,128)(2,1)S(1)}, bf16[128,3584]{1,0:T(8,128)(2,1)S(1)}, u32[]{:S(2)}, u32[]{:S(2)}) %collective-permute-start.20) | collective-permute-done | bytes 917536 | tf_op jit(solution)/shard_map/ppermute | solution.py:251
  183.4 1.3 add_convert_fusion
  (1 shorter events, 0.0 us)
Async XLA Ops:
  7.3 47.6 %collective-permute-start.1 = (bf16[2,3584,512]{2,1,0:T(8,128)(2,1)}, bf16[2,3584,512]{2,1,0:T(8,128)(2,1)}, u32[]{:S(2)}, u32[]{:S(2)}) collective-permute-start(bf16[2,3584,512]{2,1,0:T(8,128)(2,1)} %get-tuple-element.39.refs_2_), channel_id=1, source_target_pairs={{0,1},{1,0},{2,3},{3,2},{4,5},{5,4},{6,7},{7,6},{8,9},{9,8},{10,11... | collective-permute-start | bytes 22020104 | tf_op jit(solution)/shard_map/ppermute | solution.py:247
  7.8 47.1 %collective-permute-start.2 = (bf16[512,3584]{1,0:T(8,128)(2,1)}, bf16[512,3584]{1,0:T(8,128)(2,1)}, u32[]{:S(2)}, u32[]{:S(2)}) collective-permute-start(bf16[512,3584]{1,0:T(8,128)(2,1)} %bitcast.4.refs_4_), channel_id=1, source_target_pairs={{0,1},{1,0},{2,3},{3,2},{4,5},{5,4},{6,7},{7,6},{8,9},{9,8},{10,11... | collective-permute-start | bytes 11010056 | tf_op jit(solution)/shard_map/ppermute | solution.py:247
  7.9 25.4 %collective-permute-start.3 = (bf16[128,3712]{1,0:T(8,128)(2,1)S(1)}, bf16[128,3712]{1,0:T(8,128)(2,1)S(1)}, u32[]{:S(2)}, u32[]{:S(2)}) collective-permute-start(bf16[128,3712]{1,0:T(8,128)(2,1)S(1)} %get-tuple-element.40), channel_id=1, source_target_pairs={{0,4},{2,6},{4,8},{6,10},{8,12},{10,14},{1,5},{3,7},{5,9},{7,11},{... | collective-permute-start | bytes 2850824 | tf_op jit(solution)/shard_map/ppermute | solution.py:251
  12.8 24.7 %collective-permute-start.4 = (bf16[128,3712]{1,0:T(8,128)(2,1)S(1)}, bf16[128,3712]{1,0:T(8,128)(2,1)S(1)}, u32[]{:S(2)}, u32[]{:S(2)}) collective-permute-start(bf16[128,3712]{1,0:T(8,128)(2,1)S(1)} %get-tuple-element.40), channel_id=1, source_target_pairs={{4,0},{6,2},{8,4},{10,6},{12,8},{14,10},{5,1},{7,3},{9,5},{11,7},{... | collective-permute-start | bytes 2850824 | tf_op jit(solution)/shard_map/ppermute | solution.py:251
  14.1 15.2 %collective-permute-start = (bf16[80,3712]{1,0:T(8,128)(2,1)S(1)}, bf16[80,3712]{1,0:T(8,128)(2,1)S(1)}, u32[]{:S(2)}, u32[]{:S(2)}) collective-permute-start(bf16[80,3712]{1,0:T(8,128)(2,1)S(1)} %get-tuple-element.38), channel_id=1, source_target_pairs={{0,2},{2,0},{4,6},{6,4},{8,10},{10,8},{12,14},{14,12},{1,3},{3,1},... | collective-permute-start | bytes 1781768 | tf_op jit(solution)/shard_map/ppermute | solution.py:254
  29.3 8.2 %copy-start = (bf16[80,3712]{1,0:T(8,128)(2,1)}, bf16[80,3712]{1,0:T(8,128)(2,1)S(1)}, u32[]{:S(2)}) copy-start(bf16[80,3712]{1,0:T(8,128)(2,1)S(1)} %collective-permute-done.refs_2_.refs_1_) | copy-start | bytes 1781764
  37.5 26.6 %collective-permute-start.5 = (bf16[128,3712]{1,0:T(8,128)(2,1)S(1)}, bf16[128,3712]{1,0:T(8,128)(2,1)S(1)}, u32[]{:S(2)}, u32[]{:S(2)}) collective-permute-start(bf16[128,3712]{1,0:T(8,128)(2,1)S(1)} %get-tuple-element.41.refs_1_.refs_2_), channel_id=1, source_target_pairs={{4,8},{6,10},{8,12},{10,14},{5,9},{7,11},{9,13},{11,15},{20,24},{2... | collective-permute-start | bytes 2850824 | tf_op jit(solution)/shard_map/ppermute | solution.py:251
  38.2 26.1 %collective-permute-start.6 = (bf16[128,3712]{1,0:T(8,128)(2,1)S(1)}, bf16[128,3712]{1,0:T(8,128)(2,1)S(1)}, u32[]{:S(2)}, u32[]{:S(2)}) collective-permute-start(bf16[128,3712]{1,0:T(8,128)(2,1)S(1)} %get-tuple-element.42.refs_0_), channel_id=1, source_target_pairs={{4,0},{6,2},{8,4},{10,6},{5,1},{7,3},{9,5},{11,7},{20,16},{22,18},... | collective-permute-start | bytes 2850824 | tf_op jit(solution)/shard_map/ppermute | solution.py:251
  40.6 14.3 %collective-permute-start.7 = (bf16[80,3712]{1,0:T(8,128)(2,1)S(1)}, bf16[80,3712]{1,0:T(8,128)(2,1)S(1)}, u32[]{:S(2)}, u32[]{:S(2)}) collective-permute-start(bf16[80,3712]{1,0:T(8,128)(2,1)S(1)} %get-tuple-element.44), channel_id=1, source_target_pairs={{0,2},{2,0},{4,6},{6,4},{8,10},{10,8},{12,14},{14,12},{1,3},{3,1},... | collective-permute-start | bytes 1781768 | tf_op jit(solution)/shard_map/ppermute | solution.py:254
  64.4 18.6 %collective-permute-start.10 = (bf16[128,3712]{1,0:T(8,128)(2,1)S(1)}, bf16[128,3712]{1,0:T(8,128)(2,1)S(1)}, u32[]{:S(2)}, u32[]{:S(2)}) collective-permute-start(bf16[128,3712]{1,0:T(8,128)(2,1)S(1)} %get-tuple-element.48.refs_1_), channel_id=1, source_target_pairs={{8,12},{10,14},{9,13},{11,15},{24,28},{26,30},{25,29},{27,31}} | collective-permute-start | bytes 2850824 | tf_op jit(solution)/shard_map/ppermute | solution.py:251
  65.2 24.7 %collective-permute-start.9 = (bf16[128,3712]{1,0:T(8,128)(2,1)S(1)}, bf16[128,3712]{1,0:T(8,128)(2,1)S(1)}, u32[]{:S(2)}, u32[]{:S(2)}) collective-permute-start(bf16[128,3712]{1,0:T(8,128)(2,1)S(1)} %get-tuple-element.47.refs_0_), channel_id=1, source_target_pairs={{4,0},{6,2},{5,1},{7,3},{20,16},{22,18},{21,17},{23,19}} | collective-permute-start | bytes 2850824 | tf_op jit(solution)/shard_map/ppermute | solution.py:251
  66.5 16.0 %collective-permute-start.11 = (bf16[80,3584]{1,0:T(8,128)(2,1)S(1)}, bf16[80,3584]{1,0:T(8,128)(2,1)S(1)}, u32[]{:S(2)}, u32[]{:S(2)}) collective-permute-start(bf16[80,3584]{1,0:T(8,128)(2,1)S(1)} %get-tuple-element.54), channel_id=1, source_target_pairs={{0,2},{2,0},{4,6},{6,4},{8,10},{10,8},{12,14},{14,12},{1,3},{3,1},... | collective-permute-start | bytes 1720328 | tf_op jit(solution)/shard_map/ppermute | solution.py:254
  69.1 24.3 %collective-permute-start.8 = (bf16[80,3712]{1,0:T(8,128)(2,1)S(1)}, bf16[80,3712]{1,0:T(8,128)(2,1)S(1)}, u32[]{:S(2)}, u32[]{:S(2)}) collective-permute-start(bf16[80,3712]{1,0:T(8,128)(2,1)S(1)} %get-tuple-element.52), channel_id=1, source_target_pairs={{0,2},{2,0},{4,6},{6,4},{8,10},{10,8},{12,14},{14,12},{1,3},{3,1},... | collective-permute-start | bytes 1781768 | tf_op jit(solution)/shard_map/ppermute | solution.py:254
  91.1 16.4 %collective-permute-start.13 = (bf16[80,3712]{1,0:T(8,128)(2,1)S(1)}, bf16[80,3712]{1,0:T(8,128)(2,1)S(1)}, u32[]{:S(2)}, u32[]{:S(2)}) collective-permute-start(bf16[80,3712]{1,0:T(8,128)(2,1)S(1)} %get-tuple-element.59), channel_id=1, source_target_pairs={{0,2},{2,0},{4,6},{6,4},{8,10},{10,8},{12,14},{14,12},{1,3},{3,1},... | collective-permute-start | bytes 1781768 | tf_op jit(solution)/shard_map/ppermute | solution.py:254
  92.7 25.7 %collective-permute-start.14 = (bf16[128,3584]{1,0:T(8,128)(2,1)S(1)}, bf16[128,3584]{1,0:T(8,128)(2,1)S(1)}, u32[]{:S(2)}, u32[]{:S(2)}) collective-permute-start(bf16[128,3584]{1,0:T(8,128)(2,1)S(1)} %shard_map.70.refs_4_), channel_id=1, source_target_pairs={{0,4},{2,6},{4,0},{6,2},{8,12},{10,14},{12,8},{14,10},{1,5},{3,7},... | collective-permute-start | bytes 2752520 | tf_op jit(solution)/shard_map/ppermute | solution.py:251
  102.6 17.2 %collective-permute-start.12 = (bf16[80,3584]{1,0:T(8,128)(2,1)S(1)}, bf16[80,3584]{1,0:T(8,128)(2,1)S(1)}, u32[]{:S(2)}, u32[]{:S(2)}) collective-permute-start(bf16[80,3584]{1,0:T(8,128)(2,1)S(1)} %get-tuple-element.57), channel_id=1, source_target_pairs={{0,2},{2,0},{4,6},{6,4},{8,10},{10,8},{12,14},{14,12},{1,3},{3,1},... | collective-permute-start | bytes 1720328 | tf_op jit(solution)/shard_map/ppermute | solution.py:254
  116.7 12.2 %copy-start.1 = (bf16[80,3712]{1,0:T(8,128)(2,1)S(1)}, bf16[80,3712]{1,0:T(8,128)(2,1)}, u32[]{:S(2)}) copy-start(bf16[80,3712]{1,0:T(8,128)(2,1)} %copy-done) | copy-start | bytes 1781764
  116.7 12.2 %copy-start.2 = (bf16[80,3712]{1,0:T(8,128)(2,1)S(1)}, bf16[80,3712]{1,0:T(8,128)(2,1)}, u32[]{:S(2)}) copy-start(bf16[80,3712]{1,0:T(8,128)(2,1)} %get-tuple-element.37.refs_0_) | copy-start | bytes 1781764
  116.8 21.5 %collective-permute-start.17 = (bf16[80,3584]{1,0:T(8,128)(2,1)S(1)}, bf16[80,3584]{1,0:T(8,128)(2,1)S(1)}, u32[]{:S(2)}, u32[]{:S(2)}) collective-permute-start(bf16[80,3584]{1,0:T(8,128)(2,1)S(1)} %get-tuple-element.64), channel_id=1, source_target_pairs={{0,2},{2,0},{4,6},{6,4},{8,10},{10,8},{12,14},{14,12},{1,3},{3,1},... | collective-permute-start | bytes 1720328 | tf_op jit(solution)/shard_map/ppermute | solution.py:254
  120.4 29.6 %collective-permute-start.16 = (bf16[128,3584]{1,0:T(8,128)(2,1)S(1)}, bf16[128,3584]{1,0:T(8,128)(2,1)S(1)}, u32[]{:S(2)}, u32[]{:S(2)}) collective-permute-start(bf16[128,3584]{1,0:T(8,128)(2,1)S(1)} %shard_map.74.refs_6_.refs_0_), channel_id=1, source_target_pairs={{0,8},{2,10},{12,4},{14,6},{1,9},{3,11},{13,5},{15,7},{16,24},{18,... | collective-permute-start | bytes 2752520 | tf_op jit(solution)/shard_map/ppermute | solution.py:251
  138.9 21.8 %collective-permute-start.19 = (bf16[128,3584]{1,0:T(8,128)(2,1)S(1)}, bf16[128,3584]{1,0:T(8,128)(2,1)S(1)}, u32[]{:S(2)}, u32[]{:S(2)}) collective-permute-start(bf16[128,3584]{1,0:T(8,128)(2,1)S(1)} %shard_map.76.refs_6_), channel_id=1, source_target_pairs={{0,4},{2,6},{12,8},{14,10},{1,5},{3,7},{13,9},{15,11},{16,20},{18,... | collective-permute-start | bytes 2752520 | tf_op jit(solution)/shard_map/ppermute | solution.py:251
  140.2 9.8 %collective-permute-start.15 = (bf16[80,3584]{1,0:T(8,128)(2,1)S(1)}, bf16[80,3584]{1,0:T(8,128)(2,1)S(1)}, u32[]{:S(2)}, u32[]{:S(2)}) collective-permute-start(bf16[80,3584]{1,0:T(8,128)(2,1)S(1)} %get-tuple-element.62), channel_id=1, source_target_pairs={{0,2},{2,0},{4,6},{6,4},{8,10},{10,8},{12,14},{14,12},{1,3},{3,1},... | collective-permute-start | bytes 1720328 | tf_op jit(solution)/shard_map/ppermute | solution.py:254
  141.8 20.4 %collective-permute-start.18 = (bf16[128,3584]{1,0:T(8,128)(2,1)S(1)}, bf16[128,3584]{1,0:T(8,128)(2,1)S(1)}, u32[]{:S(2)}, u32[]{:S(2)}) collective-permute-start(bf16[128,3584]{1,0:T(8,128)(2,1)S(1)} %shard_map.76.refs_6_), channel_id=1, source_target_pairs={{4,8},{6,10},{8,4},{10,6},{5,9},{7,11},{9,5},{11,7},{20,24},{22,26... | collective-permute-start | bytes 2752520 | tf_op jit(solution)/shard_map/ppermute | solution.py:251
  160.9 22.5 %collective-permute-start.20 = (bf16[128,3584]{1,0:T(8,128)(2,1)S(1)}, bf16[128,3584]{1,0:T(8,128)(2,1)S(1)}, u32[]{:S(2)}, u32[]{:S(2)}) collective-permute-start(bf16[128,3584]{1,0:T(8,128)(2,1)S(1)} %shard_map.78), channel_id=1, source_target_pairs={{4,12},{6,14},{8,0},{10,2},{5,13},{7,15},{9,1},{11,3},{20,28},{22,... | collective-permute-start | bytes 2752520 | tf_op jit(solution)/shard_map/ppermute | solution.py:251

commit v13 on v11

--- a/solution.py
+++ b/solution.py
@@ -56,25 +56,15 @@
     )(*[in_vmem(a) for a in arrays], *after)
 
 
-def first_kernel(experts, tokens, routes, scale, gate_w, up_w, block, *refs):
-    picked, (stack, held, route_held, scale_held, sems, own_sems) = refs[:4], refs[4:]
-    pieces = sems.shape[2]
+def first_kernel(experts, tokens, routes, scale, block, *refs):
+    picked, (route_held, scale_held, sems) = refs[:4], refs[4:]
     count, width = tokens.shape
     ins = [
-        pltpu.make_async_copy(routes, route_held, own_sems.at[0]),
-        pltpu.make_async_copy(scale, scale_held, own_sems.at[1]),
-        pltpu.make_async_copy(tokens, block.at[:, :width], own_sems.at[2]),
+        pltpu.make_async_copy(routes, route_held, sems.at[0]),
+        pltpu.make_async_copy(scale, scale_held, sems.at[1]),
+        pltpu.make_async_copy(tokens, block.at[:, :width], sems.at[2]),
     ]
     for copy in ins:
-        copy.start()
-    rows = gate_w.shape[0] // pieces
-    fetch, store = [], []
-    for k in range(pieces):
-        cut = pl.ds(k * rows, rows)
-        for n, source in enumerate((gate_w, up_w)):
-            fetch.append(pltpu.make_async_copy(source.at[cut], held.at[n, cut], sems.at[0, n, k]))
-            store.append(pltpu.make_async_copy(held.at[n, cut], stack.at[n, cut], sems.at[1, n, k]))
-    for copy in fetch:
         copy.start()
     for copy in ins[:2]:
         copy.wait()
@@ -90,12 +80,7 @@
     marks = jnp.where(part == 0, high, jnp.where(part == 1, middle, jnp.where(part == 2, low, 0.0)))
     block[:, width:] = marks.astype(jnp.bfloat16)
     ins[2].wait()
-    for arrived, leaving in zip(fetch, store):
-        arrived.wait()
-        leaving.start()
     choose(block, *picked)
-    for copy in store:
-        copy.wait()
 
 
 def passing_kernel(*refs):
@@ -140,16 +125,17 @@
 
 
 def expert_kernel(experts, own, other, *refs):
-    own_w, other_w, own_down, other_down, own_out, other_out, rows, hidden, gates, ups, downs, sems = refs
+    weights, (own_out, other_out, rows, hidden, gates, ups, downs, sems) = refs[:6], refs[6:]
     cap, width = own_out.shape
     tiles, _, size = gates.shape
     each = tiles // 2
     queue = []
     for tile in range(tiles):
-        stack, part = (own_w, other_w)[tile // each], pl.ds(tile % each * size, size)
-        queue.append(pltpu.make_async_copy(stack.at[0, :, part], gates.at[tile], sems.at[tile, 0]))
-        queue.append(pltpu.make_async_copy(stack.at[1, :, part], ups.at[tile], sems.at[tile, 1]))
-    for half, down in enumerate((own_down, other_down)):
+        part = pl.ds(tile % each * size, size)
+        gate_w, up_w = weights[tile // each * 3 : tile // each * 3 + 2]
+        queue.append(pltpu.make_async_copy(gate_w.at[:, part], gates.at[tile], sems.at[tile, 0]))
+        queue.append(pltpu.make_async_copy(up_w.at[:, part], ups.at[tile], sems.at[tile, 1]))
+    for half, down in enumerate(weights[2::3]):
         queue.append(pltpu.make_async_copy(down, downs.at[half], sems.at[half, 2]))
     ahead = iter(queue[4:])
     for copy in queue[:4]:
@@ -196,11 +182,27 @@
     result[...] = total.astype(jnp.bfloat16)
 
 
-def sum_kernel(*refs):
-    total = refs[0][...].astype(jnp.float32)
-    for extra in refs[1:-1]:
-        total += extra[...].astype(jnp.float32)
-    refs[-1][...] = total.astype(jnp.bfloat16)
+def join_kernel(index, whole, half, result):
+    size = half.shape[1]
+    total = whole[:, index * size : (index + 1) * size].astype(jnp.float32) + half[...].astype(jnp.float32)
+    result[...] = total.astype(jnp.bfloat16)
+
+
+def halves_kernel(*refs):
+    spread_kernel(*refs[:-2])
+    size = refs[-1].shape[1]
+    refs[-2][...] = refs[-3][:, :size]
+    refs[-1][...] = refs[-3][:, size:]
+
+
+def finish_kernel(*refs):
+    *whole, low, high, result = refs
+    size = low.shape[1]
+    for half, first in ((low, 0), (high, size)):
+        total = half[...].astype(jnp.float32)
+        for extra in whole:
+            total += extra[:, first : first + size].astype(jnp.float32)
+        result[:, first : first + size] = total.astype(jnp.bfloat16)
 
 
 def on_device(tokens, routes, route_scale, w_gate, w_up, w_down):
@@ -216,30 +218,20 @@
     bf16 = functools.partial(jax.ShapeDtypeStruct, dtype=jnp.bfloat16)
 
     own = (w_gate[0], w_up[0], w_down[0])
-    block, *picked, stack = call(
+    block, *picked = call(
         functools.partial(first_kernel, experts),
-        [
-            bf16((count, wide)),
-            bf16((count, cap)),
-            bf16((count, cap)),
-            hbm((cap, wide)),
-            bf16((cap, wide)),
-            hbm((2, width, hidden)),
-        ],
-        [*map(in_hbm, (tokens, routes.T, route_scale.T, own[0], own[1]))],
+        [bf16((count, wide)), bf16((count, cap)), bf16((count, cap)), hbm((cap, wide)), bf16((cap, wide))],
+        [*map(in_hbm, (tokens, routes.T, route_scale.T))],
         (),
         [
-            pltpu.VMEM((2, width, hidden), jnp.bfloat16),
             pltpu.VMEM(routes.shape[::-1], routes.dtype),
             pltpu.VMEM(routes.shape[::-1], route_scale.dtype),
-            pltpu.SemaphoreType.DMA((2, 2, 8)),
             pltpu.SemaphoreType.DMA((3,)),
         ],
-        [ANYWHERE] * 5,
-        out_specs=[IN_VMEM] * 5 + [ANYWHERE],
+        [ANYWHERE] * 3,
     )
     swap = functools.partial(lax.ppermute, axis_name="local", perm=[(0, 1), (1, 0)])
-    weights = [in_hbm(stack), swap(stack), in_hbm(own[2]), swap(own[2])]
+    weights = [in_hbm(w) for w in (*own, *map(swap, own))]
 
     def along(block, pairs):
         moves = [(2 * a + y, 2 * b + y) for a, b in pairs for y in range(2)]
@@ -248,7 +240,7 @@
     def across(block):
         return lax.ppermute(block, "node", [(n, n ^ 1) for n in range(experts)])
 
-    def pick(blocks, users, after=()):
+    def pick(blocks, users, after=(), cost=0):
         return call(
             functools.partial(pick_kernel, users),
             [bf16((count, cap)), bf16((count, cap)), bf16((cap, wide)), bf16((cap, wide))],
@@ -256,9 +248,10 @@
             after,
             [pltpu.VMEM((count, wide), jnp.bfloat16), pltpu.SemaphoreType.DMA],
             [ANYWHERE] * len(blocks),
+            cost=cost,
         )
 
-    def expert(own_rows, other_rows, after=()):
+    def expert(own_rows, other_rows, after=(), cost=0):
         tiles = 2 * hidden // size
         return call(
             functools.partial(expert_kernel, experts),
@@ -273,9 +266,9 @@
                 pltpu.VMEM((2, hidden, width), jnp.bfloat16),
                 pltpu.SemaphoreType.DMA((tiles, 3)),
             ],
-            [IN_VMEM] * 2 + [ANYWHERE] * 4,
+            [IN_VMEM] * 2 + [ANYWHERE] * 6,
             32,
-            cost=64 * MIB,
+            cost=cost,
         )
 
     def spread(maps, own_out, other_out, extras=(), after=(), cost=0):
@@ -303,15 +296,15 @@
             ]
             held[way, step] = along(held.get((way, step - 1), block), pairs)
 
-    def do_pick(slot, after=()):
+    def do_pick(slot, after=(), cost=0):
         keys = sorted({row[slot - 1] for row in plan})
         blocks = [held[key] for key in keys]
         users = [[place for place, row in enumerate(plan) if row[slot - 1] == key] for key in keys]
-        *maps, own_rows, other_rows = ordered(pick, blocks, users, after=after)
+        *maps, own_rows, other_rows = ordered(pick, blocks, users, after=after, cost=cost)
         picks[slot] = maps, own_rows, across(other_rows)
 
-    def do_expert(slot, after=()):
-        own_out, other_out = ordered(expert, picks[slot][1], picks[slot][2], after=after)
+    def do_expert(slot, after=(), cost=0):
+        own_out, other_out = ordered(expert, picks[slot][1], picks[slot][2], after=after, cost=cost)
         outs[slot] = own_out, across(other_out)
 
     def origin(place, slot):
@@ -325,10 +318,15 @@
         if near != target and origin(near, places - 2) == target:
             hops.append((place, near))
     staying = {places - 1: [a for a, _ in hops], places - 2: [b for _, b in hops]}
-    kept = {}
+    kept, halves = {}, []
+
+    def spread_halves(maps, own_out, other_out, after=()):
+        outs = [bf16((count, width)), bf16((count, width // 2)), bf16((count, width // 2))]
+        return call(halves_kernel, outs, [*maps, own_out, other_out], after)
 
     def do_spread(slot, after=()):
-        kept[slot] = done = ordered(spread, picks[slot][0], *outs[slot], after=after)
+        done, *halves[:] = ordered(spread_halves, picks[slot][0], *outs[slot], after=after)
+        kept[slot] = done
         home = [(a, origin(a, slot)) for a in range(places) if a not in staying.get(slot, ())]
         rounds = []
         while home:
@@ -337,17 +335,22 @@
             rounds.append(along(done, now))
         returned.append(rounds)
 
-    def call_sum(blocks, after=(), cost=0):
-        return call(sum_kernel, [bf16((count, width))], blocks, after, cost=cost)
+    def join(whole, half, index, after=()):
+        return call(functools.partial(join_kernel, index), [bf16(half.shape)], [whole, half], after)[0]
+
+    def finish(whole, parts):
+        while len(whole) > 8:
+            summed = sum(array.astype(jnp.float32) for array in whole[:8])
+            whole = [summed.astype(jnp.bfloat16), *whole[8:]]
+        return call(finish_kernel, [bf16((count, width))], [*whole, *parts])[0]
 
     relay(1)
+    relay(2)
+    do_pick(1, after=weights[3:])
     picks[0] = picked[:2], picked[2], across(picked[3])
-    held[1, 1], held[-1, 1] = tied([held[1, 1], held[-1, 1]], [picks[0][2]])
-    relay(2)
-    do_pick(1)
-    do_expert(1)
+    do_expert(1, cost=64 * MIB)
     held[1, 2], held[-1, 2] = call(
-        passing_kernel, [bf16((count, wide))] * 2, [held[1, 2], held[-1, 2]], [*last, picks[1][2]]
+        passing_kernel, [bf16((count, wide))] * 2, [held[1, 2], held[-1, 2]], [*last, picks[1][2], picks[0][2]]
     )
     for step in range(3, places):
         relay(step)
@@ -364,12 +367,11 @@
     do_spread(places - 1)
     near = returned.pop(places - 3)
     total = ordered(spread, picks[0][0], *outs[0], [*returned.pop(0), *near] if places > 3 else near, cost=128 * MIB)
-    (joined,) = ordered(call_sum, [kept[places - 2], along(kept[places - 1], hops)])
-    returned.append([along(joined, [(q, origin(q, places - 2)) for _, q in hops])])
-    total = total.astype(jnp.float32)
-    for block in sum(returned, []):
-        total = total + block.astype(jnp.float32)
-    return total.astype(jnp.bfloat16)
+    homes = [(q, origin(q, places - 2)) for _, q in hops]
+    parts = []
+    for arrived in [along(half, hops) for half in halves]:
+        parts.append(along(ordered(join, kept[places - 2], arrived, len(parts)), homes))
+    return finish([total, *sum(returned, [])], parts)
 
 
 def solution(mesh):

time: 180 us -> 183 us (1.017)
  starting transfers between devices: 37.9 us -> 43.1 us
  local copies, waits for them, and re-layouts: 0.01 us -> 4.79 us
  waiting for transfers between devices: 89.7 us -> 85.9 us
    ppermute x8, waiting for transfers between devices: 48.7 us -> 35.3 us  [across(): return lax.ppermute(block, 'node', [(n, n ^ 1) for n in range(experts)])]
    ppermute x12 -> x14, waiting for transfers between devices: 40.9 us -> 50.6 us  [along(): return lax.ppermute(block, 'node', moves)]
    ppermute x12 -> x14, starting transfers between devices: 25.7 us -> 31.6 us  [along(): return lax.ppermute(block, 'node', moves)]
    unnamed x6 -> x8, local copies, waits for them, and re-layouts: 0.01 us -> 4.79 us
    pallas_call x14 -> x16, Pallas kernels: 50.2 us -> 48.8 us  [call(): pl.pallas_call(body, out_shape=outs, in_specs=specs, out_specs=out_specs...]
  transfers between devices with their start and end apart: 22 -> 25, of which waited for: 12 -> 13; matrix products, arithmetic and copies ran while one was open for 0% -> 0% of each run, Pallas kernels for 24% -> 26%
where the time goes in v13:
time: 183 us
  waiting for transfers between devices  85.9 us (47%)
  Pallas kernels  48.8 us (27%)
  starting transfers between devices  43.1 us (24%)
  local copies, waits for them, and re-layouts  4.79 us (3%)
    ppermute x14, waiting for transfers between devices, along(): return lax.ppermute(block, 'node', moves)  50.6 us
    pallas_call x16, Pallas kernels, call(): pl.pallas_call(body, out_shape=outs, in_specs=specs, out_specs=out_specs...  48.8 us
    ppermute x8, waiting for transfers between devices, across(): return lax.ppermute(block, 'node', [(n, n ^ 1) for n in range(experts)])  35.3 us
    ppermute x14, starting transfers between devices, along(): return lax.ppermute(block, 'node', moves)  31.6 us
    ppermute x8, starting transfers between devices, across(): return lax.ppermute(block, 'node', [(n, n ^ 1) for n in range(experts)])  10.6 us
    unnamed x8, local copies, waits for them, and re-layouts  4.79 us
  transfers between devices with their start and end apart: 25, of which 13 were waited for; matrix products, arithmetic and copies ran while one was open for 0% of the time, Pallas kernels for 26%

profile of v13, /device:TPU:0, one launch (start us, length us, event | category | flops | bytes accessed | tf_op | source)
XLA Modules:
  0.0 182.9 jit_solution(5082675583708633771)
XLA Ops:
  0.0 0.5 collective-permute-start.1
  0.5 0.1 collective-permute-start.2
  0.5 0.5 collective-permute-start.3
  1.0 2.6 %shard_map.64 = (bf16[128,3712]{1,0:T(8,128)(2,1)S(1)}, bf16[128,80]{1,0:T(8,128)(2,1)S(1)}, bf16[128,80]{1,0:T(8,128)(2,1)S(1)}, bf16[80,3712]{1,0:T(8,128)(2,1)}, bf16[80,3712]{1,0:T(8,128)(2,1)S(1)}) custom-call(bf16[128,3584]{1,0:T(8,128)(2,1)} %tokens.1, s32[2,128]{1,0:T(2,128)} %bitcast.20, f32[2,128]{1,0:T(2,128)} %bitcast.21), custom_call_target="tpu_custom_call" | custom-call | tf_op jit(solution)/shard_map/pallas_call | solution.py:33
  3.6 4.5 %collective-permute-start.4 = (bf16[128,3712]{1,0:T(8,128)(2,1)S(1)}, bf16[128,3712]{1,0:T(8,128)(2,1)S(1)}, u32[]{:S(2)}, u32[]{:S(2)}) collective-permute-start(bf16[128,3712]{1,0:T(8,128)(2,1)S(1)} %get-tuple-element.41), channel_id=1, source_target_pairs={{0,4},{2,6},{4,8},{6,10},{8,12},{10,14},{1,5},{3,7},{5,9},{7,11},{... | collective-permute-start | bytes 2850824 | tf_op jit(solution)/shard_map/ppermute | solution.py:238
  8.2 1.3 collective-permute-start.6
  9.5 19.6 %collective-permute-done.4.refs_1_.refs_2_ = bf16[128,3712]{1,0:T(8,128)(2,1)S(1)} collective-permute-done((bf16[128,3712]{1,0:T(8,128)(2,1)S(1)}, bf16[128,3712]{1,0:T(8,128)(2,1)S(1)}, u32[]{:S(2)}, u32[]{:S(2)}) %collective-permute-start.4) | collective-permute-done | bytes 950304 | tf_op jit(solution)/shard_map/ppermute | solution.py:238
  29.1 0.7 collective-permute-start.5
  29.8 3.5 %collective-permute-done.6.refs_0_ = bf16[128,3712]{1,0:T(8,128)(2,1)S(1)} collective-permute-done((bf16[128,3712]{1,0:T(8,128)(2,1)S(1)}, bf16[128,3712]{1,0:T(8,128)(2,1)S(1)}, u32[]{:S(2)}, u32[]{:S(2)}) %collective-permute-start.6) | collective-permute-done | bytes 950304 | tf_op jit(solution)/shard_map/ppermute | solution.py:238
  33.2 1.3 collective-permute-start.7
  34.5 0.0 collective-permute-done.1.refs_2_.refs_5_
  34.5 0.0 collective-permute-done.2.refs_3_.refs_6_
  34.6 0.0 collective-permute-done.3.refs_4_.refs_7_
  34.6 1.7 copy-done.1
  36.3 1.1 copy-done.2
  37.4 1.9 %copy-done.3 = bf16[512,3584]{1,0:T(8,128)(2,1)} copy-done((bf16[512,3584]{1,0:T(8,128)(2,1)}, bf16[512,3584]{1,0:T(8,128)(2,1)S(1)}, u32[]{:S(2)}) %copy-start.3) | copy-done | bytes 3670040
  39.3 1.0 shard_map.65
  40.4 1.6 collective-permute-start.8
  42.0 0.5 collective-permute-start
  42.5 14.3 %collective-permute-done.8.refs_1_.refs_3_ = bf16[80,3712]{1,0:T(8,128)(2,1)S(1)} collective-permute-done((bf16[80,3712]{1,0:T(8,128)(2,1)S(1)}, bf16[80,3712]{1,0:T(8,128)(2,1)S(1)}, u32[]{:S(2)}, u32[]{:S(2)}) %collective-permute-start.8) | collective-permute-done | bytes 593952 | tf_op jit(solution)/shard_map/ppermute | solution.py:241
  56.8 9.2 %shard_map.66 = (bf16[80,3584]{1,0:T(8,128)(2,1)S(1)}, bf16[80,3584]{1,0:T(8,128)(2,1)S(1)}) custom-call(bf16[80,3712]{1,0:T(8,128)(2,1)S(1)} %get-tuple-element.42.refs_0_, bf16[80,3712]{1,0:T(8,128)(2,1)S(1)} %collective-permute-done.8.refs_1_.refs_3_, bf16[3584,512]{1,0:T(8,128)(2,1)} %bitcast.6, bf16[3584,512]{1,0:T(8,128)(2,1)} %bitcast.11, ...), custom_call_target="tpu_custom_call" | custom-call | bytes 67108864 | tf_op jit(solution)/shard_map/pallas_call | solution.py:33
  66.0 1.9 %collective-permute-done.refs_4_.refs_1_ = bf16[80,3712]{1,0:T(8,128)(2,1)S(1)} collective-permute-done((bf16[80,3712]{1,0:T(8,128)(2,1)S(1)}, bf16[80,3712]{1,0:T(8,128)(2,1)S(1)}, u32[]{:S(2)}, u32[]{:S(2)}) %collective-permute-start) | collective-permute-done | bytes 593952 | tf_op jit(solution)/shard_map/ppermute | solution.py:241
  67.9 0.0 collective-permute-done.5.refs_0_
  67.9 0.0 collective-permute-done.7.refs_1_
  67.9 0.1 shard_map.67
  68.0 1.3 collective-permute-start.10
  69.3 0.7 collective-permute-start.11
  70.1 1.6 collective-permute-start.12
  71.6 1.0 shard_map.68
  72.7 0.6 collective-permute-start.9
  73.2 12.8 %collective-permute-done.12.refs_3_ = bf16[80,3584]{1,0:T(8,128)(2,1)S(1)} collective-permute-done((bf16[80,3584]{1,0:T(8,128)(2,1)S(1)}, bf16[80,3584]{1,0:T(8,128)(2,1)S(1)}, u32[]{:S(2)}, u32[]{:S(2)}) %collective-permute-start.12) | collective-permute-done | bytes 573472 | tf_op jit(solution)/shard_map/ppermute | solution.py:241
  86.0 1.5 shard_map.69
  87.5 0.7 collective-permute-start.15
  88.2 5.2 %collective-permute-start.16 = (bf16[128,3584]{1,0:T(8,128)(2,1)S(1)}, bf16[128,3584]{1,0:T(8,128)(2,1)S(1)}, u32[]{:S(2)}, u32[]{:S(2)}) collective-permute-start(bf16[128,3584]{1,0:T(8,128)(2,1)S(1)} %get-tuple-element.54.refs_4_), channel_id=1, source_target_pairs={{0,4},{2,6},{4,8},{6,10},{1,5},{3,7},{5,9},{7,11},{16,20},{18,22},... | collective-permute-start | bytes 2752520 | tf_op jit(solution)/shard_map/ppermute | solution.py:238
  93.5 0.0 collective-permute-done.10.refs_1_
  93.5 1.2 shard_map.70
  94.7 1.6 collective-permute-start.14
  96.3 2.5 %collective-permute-done.9.refs_1_ = bf16[80,3712]{1,0:T(8,128)(2,1)S(1)} collective-permute-done((bf16[80,3712]{1,0:T(8,128)(2,1)S(1)}, bf16[80,3712]{1,0:T(8,128)(2,1)S(1)}, u32[]{:S(2)}, u32[]{:S(2)}) %collective-permute-start.9) | collective-permute-done | bytes 593952 | tf_op jit(solution)/shard_map/ppermute | solution.py:241
  98.8 9.2 %shard_map.71 = (bf16[80,3584]{1,0:T(8,128)(2,1)S(1)}, bf16[80,3584]{1,0:T(8,128)(2,1)S(1)}) custom-call(bf16[80,3712]{1,0:T(8,128)(2,1)S(1)} %get-tuple-element.50.refs_0_, bf16[80,3712]{1,0:T(8,128)(2,1)S(1)} %collective-permute-done.9.refs_1_, bf16[3584,512]{1,0:T(8,128)(2,1)} %bitcast.7, bf16[3584,512]{1,0:T(8,128)(2,1)} %bitcast.12, ...), custom_call_target="tpu_custom_call" | custom-call | tf_op jit(solution)/shard_map/pallas_call | solution.py:33
  108.0 1.6 collective-permute-start.13
  109.6 1.9 %collective-permute-done.14.refs_1_ = bf16[80,3712]{1,0:T(8,128)(2,1)S(1)} collective-permute-done((bf16[80,3712]{1,0:T(8,128)(2,1)S(1)}, bf16[80,3712]{1,0:T(8,128)(2,1)S(1)}, u32[]{:S(2)}, u32[]{:S(2)}) %collective-permute-start.14) | collective-permute-done | bytes 593952 | tf_op jit(solution)/shard_map/ppermute | solution.py:241
  111.5 9.2 %shard_map.72 = (bf16[80,3584]{1,0:T(8,128)(2,1)S(1)}, bf16[80,3584]{1,0:T(8,128)(2,1)S(1)}) custom-call(bf16[80,3712]{1,0:T(8,128)(2,1)S(1)} %get-tuple-element.58.refs_0_, bf16[80,3712]{1,0:T(8,128)(2,1)S(1)} %collective-permute-done.14.refs_1_, bf16[3584,512]{1,0:T(8,128)(2,1)} %bitcast.8, bf16[3584,512]{1,0:T(8,128)(2,1)} %bitcast.13, ...), custom_call_target="tpu_custom_call" | custom-call | tf_op jit(solution)/shard_map/pallas_call | solution.py:33
  120.7 0.0 copy-start
  120.7 1.6 collective-permute-start.19
  122.3 1.6 collective-permute-done.13.refs_3_
  124.0 1.5 shard_map.73
  125.4 6.0 %collective-permute-start.18 = (bf16[128,3584]{1,0:T(8,128)(2,1)S(1)}, bf16[128,3584]{1,0:T(8,128)(2,1)S(1)}, u32[]{:S(2)}, u32[]{:S(2)}) collective-permute-start(bf16[128,3584]{1,0:T(8,128)(2,1)S(1)} %get-tuple-element.61.refs_8_.refs_0_), channel_id=1, source_target_pairs={{0,8},{2,10},{12,4},{14,6},{1,9},{3,11},{13,5},{15,7},{16,24},{18,... | collective-permute-start | bytes 2752520 | tf_op jit(solution)/shard_map/ppermute | solution.py:238
  131.4 9.2 %shard_map.74 = (bf16[80,3584]{1,0:T(8,128)(2,1)S(1)}, bf16[80,3584]{1,0:T(8,128)(2,1)S(1)}) custom-call(bf16[80,3712]{1,0:T(8,128)(2,1)S(1)} %copy-done, bf16[80,3712]{1,0:T(8,128)(2,1)S(1)} %collective-permute-done.refs_4_.refs_1_, bf16[3584,512]{1,0:T(8,128)(2,1)} %bitcast.9, bf16[3584,512]{1,0:T(8,128)(2,1)} %bitcast.14, bf16[512,3584]{1,0:T(8,128)(2,1)} %bitcast.19, ...), custom_call_target="tpu_custom_call" | custom-call | tf_op jit(solution)/shard_map/pallas_call | solution.py:33
  140.7 1.6 collective-permute-start.17
  142.3 0.6 shard_map.75
  142.9 1.3 collective-permute-start.21
  144.2 1.3 collective-permute-start.20
  145.5 4.6 %collective-permute-start.23 = (bf16[128,1792]{1,0:T(8,128)(2,1)S(1)}, bf16[128,1792]{1,0:T(8,128)(2,1)S(1)}, u32[]{:S(2)}, u32[]{:S(2)}) collective-permute-start(bf16[128,1792]{1,0:T(8,128)(2,1)S(1)} %get-tuple-element.68), channel_id=1, source_target_pairs={{0,4},{2,6},{12,8},{14,10},{1,5},{3,7},{13,9},{15,11},{16,20},{18,... | collective-permute-start | bytes 1376264 | tf_op jit(solution)/shard_map/ppermute | solution.py:238
  150.1 0.3 collective-permute-done.17.refs_3_
  150.4 1.5 collective-permute-done.18.refs_6_
  151.9 0.8 shard_map.76.refs_2_.refs_0_
  152.8 7.0 %collective-permute-done.21.refs_1_ = bf16[128,1792]{1,0:T(8,128)(2,1)S(1)} collective-permute-done((bf16[128,1792]{1,0:T(8,128)(2,1)S(1)}, bf16[128,1792]{1,0:T(8,128)(2,1)S(1)}, u32[]{:S(2)}, u32[]{:S(2)}) %collective-permute-start.21) | collective-permute-done | bytes 458784 | tf_op jit(solution)/shard_map/ppermute | solution.py:238
  159.8 0.1 shard_map.77.refs_2_
  159.9 1.3 collective-permute-start.22
  161.2 3.5 %collective-permute-done.23.refs_1_ = bf16[128,1792]{1,0:T(8,128)(2,1)S(1)} collective-permute-done((bf16[128,1792]{1,0:T(8,128)(2,1)S(1)}, bf16[128,1792]{1,0:T(8,128)(2,1)S(1)}, u32[]{:S(2)}, u32[]{:S(2)}) %collective-permute-start.23) | collective-permute-done | bytes 458784 | tf_op jit(solution)/shard_map/ppermute | solution.py:238
  164.7 0.1 shard_map.78
  164.8 1.3 collective-permute-start.24
  166.1 15.5 %collective-permute-done.20.refs_1_ = bf16[128,3584]{1,0:T(8,128)(2,1)S(1)} collective-permute-done((bf16[128,3584]{1,0:T(8,128)(2,1)S(1)}, bf16[128,3584]{1,0:T(8,128)(2,1)S(1)}, u32[]{:S(2)}, u32[]{:S(2)}) %collective-permute-start.20) | collective-permute-done | bytes 917536 | tf_op jit(solution)/shard_map/ppermute | solution.py:238
  181.6 1.3 shard_map.79
  (10 shorter events, 0.0 us)
Async XLA Ops:
  0.0 34.5 %collective-permute-start.1 = (bf16[3584,512]{1,0:T(8,128)(2,1)}, bf16[3584,512]{1,0:T(8,128)(2,1)S(1)}, u32[]{:S(2)}, u32[]{:S(2)}) collective-permute-start(bf16[3584,512]{1,0:T(8,128)(2,1)} %bitcast.5), channel_id=1, source_target_pairs={{0,1},{1,0},{2,3},{3,2},{4,5},{5,4},{6,7},{7,6},{8,9},{9,8},{10,11... | collective-permute-start | bytes 11010056 | tf_op jit(solution)/shard_map/ppermute | solution.py:234
  0.5 34.1 %collective-permute-start.2 = (bf16[3584,512]{1,0:T(8,128)(2,1)}, bf16[3584,512]{1,0:T(8,128)(2,1)S(1)}, u32[]{:S(2)}, u32[]{:S(2)}) collective-permute-start(bf16[3584,512]{1,0:T(8,128)(2,1)} %bitcast.10), channel_id=1, source_target_pairs={{0,1},{1,0},{2,3},{3,2},{4,5},{5,4},{6,7},{7,6},{8,9},{9,8},{10,11... | collective-permute-start | bytes 11010056 | tf_op jit(solution)/shard_map/ppermute | solution.py:234
  0.5 34.0 %collective-permute-start.3 = (bf16[512,3584]{1,0:T(8,128)(2,1)}, bf16[512,3584]{1,0:T(8,128)(2,1)S(1)}, u32[]{:S(2)}, u32[]{:S(2)}) collective-permute-start(bf16[512,3584]{1,0:T(8,128)(2,1)} %bitcast.15), channel_id=1, source_target_pairs={{0,1},{1,0},{2,3},{3,2},{4,5},{5,4},{6,7},{7,6},{8,9},{9,8},{10,11... | collective-permute-start | bytes 11010056 | tf_op jit(solution)/shard_map/ppermute | solution.py:234
  3.6 25.5 %collective-permute-start.4 = (bf16[128,3712]{1,0:T(8,128)(2,1)S(1)}, bf16[128,3712]{1,0:T(8,128)(2,1)S(1)}, u32[]{:S(2)}, u32[]{:S(2)}) collective-permute-start(bf16[128,3712]{1,0:T(8,128)(2,1)S(1)} %get-tuple-element.41), channel_id=1, source_target_pairs={{0,4},{2,6},{4,8},{6,10},{8,12},{10,14},{1,5},{3,7},{5,9},{7,11},{... | collective-permute-start | bytes 2850824 | tf_op jit(solution)/shard_map/ppermute | solution.py:238
  8.2 25.1 %collective-permute-start.6 = (bf16[128,3712]{1,0:T(8,128)(2,1)S(1)}, bf16[128,3712]{1,0:T(8,128)(2,1)S(1)}, u32[]{:S(2)}, u32[]{:S(2)}) collective-permute-start(bf16[128,3712]{1,0:T(8,128)(2,1)S(1)} %get-tuple-element.41), channel_id=1, source_target_pairs={{4,0},{6,2},{8,4},{10,6},{12,8},{14,10},{5,1},{7,3},{9,5},{11,7},{... | collective-permute-start | bytes 2850824 | tf_op jit(solution)/shard_map/ppermute | solution.py:238
  29.1 38.8 %collective-permute-start.5 = (bf16[128,3712]{1,0:T(8,128)(2,1)S(1)}, bf16[128,3712]{1,0:T(8,128)(2,1)S(1)}, u32[]{:S(2)}, u32[]{:S(2)}) collective-permute-start(bf16[128,3712]{1,0:T(8,128)(2,1)S(1)} %collective-permute-done.4.refs_1_.refs_2_), channel_id=1, source_target_pairs={{4,8},{6,10},{8,12},{10,14},{5,9},{7,11},{9,13},{11,15},{20,24},{2... | collective-permute-start | bytes 2850824 | tf_op jit(solution)/shard_map/ppermute | solution.py:238
  33.2 34.7 %collective-permute-start.7 = (bf16[128,3712]{1,0:T(8,128)(2,1)S(1)}, bf16[128,3712]{1,0:T(8,128)(2,1)S(1)}, u32[]{:S(2)}, u32[]{:S(2)}) collective-permute-start(bf16[128,3712]{1,0:T(8,128)(2,1)S(1)} %collective-permute-done.6.refs_0_), channel_id=1, source_target_pairs={{4,0},{6,2},{8,4},{10,6},{5,1},{7,3},{9,5},{11,7},{20,16},{22,18},... | collective-permute-start | bytes 2850824 | tf_op jit(solution)/shard_map/ppermute | solution.py:238
  34.5 1.8 copy-start.1
  34.5 2.9 %copy-start.2 = (bf16[3584,512]{1,0:T(8,128)(2,1)}, bf16[3584,512]{1,0:T(8,128)(2,1)S(1)}, u32[]{:S(2)}) copy-start(bf16[3584,512]{1,0:T(8,128)(2,1)S(1)} %collective-permute-done.2.refs_3_.refs_6_) | copy-start | bytes 11010052
  37.4 1.9 %copy-start.3 = (bf16[512,3584]{1,0:T(8,128)(2,1)}, bf16[512,3584]{1,0:T(8,128)(2,1)S(1)}, u32[]{:S(2)}) copy-start(bf16[512,3584]{1,0:T(8,128)(2,1)S(1)} %collective-permute-done.3.refs_4_.refs_7_) | copy-start | bytes 11010052
  40.4 16.4 %collective-permute-start.8 = (bf16[80,3712]{1,0:T(8,128)(2,1)S(1)}, bf16[80,3712]{1,0:T(8,128)(2,1)S(1)}, u32[]{:S(2)}, u32[]{:S(2)}) collective-permute-start(bf16[80,3712]{1,0:T(8,128)(2,1)S(1)} %get-tuple-element.43), channel_id=1, source_target_pairs={{0,2},{2,0},{4,6},{6,4},{8,10},{10,8},{12,14},{14,12},{1,3},{3,1},... | collective-permute-start | bytes 1781768 | tf_op jit(solution)/shard_map/ppermute | solution.py:241
  42.0 25.9 %collective-permute-start = (bf16[80,3712]{1,0:T(8,128)(2,1)S(1)}, bf16[80,3712]{1,0:T(8,128)(2,1)S(1)}, u32[]{:S(2)}, u32[]{:S(2)}) collective-permute-start(bf16[80,3712]{1,0:T(8,128)(2,1)S(1)} %get-tuple-element.40), channel_id=1, source_target_pairs={{0,2},{2,0},{4,6},{6,4},{8,10},{10,8},{12,14},{14,12},{1,3},{3,1},... | collective-permute-start | bytes 1781768 | tf_op jit(solution)/shard_map/ppermute | solution.py:241
  68.0 25.4 %collective-permute-start.10 = (bf16[128,3712]{1,0:T(8,128)(2,1)S(1)}, bf16[128,3712]{1,0:T(8,128)(2,1)S(1)}, u32[]{:S(2)}, u32[]{:S(2)}) collective-permute-start(bf16[128,3712]{1,0:T(8,128)(2,1)S(1)} %get-tuple-element.46.refs_0_), channel_id=1, source_target_pairs={{4,0},{6,2},{5,1},{7,3},{20,16},{22,18},{21,17},{23,19}} | collective-permute-start | bytes 2850824 | tf_op jit(solution)/shard_map/ppermute | solution.py:238
  69.3 24.1 %collective-permute-start.11 = (bf16[128,3712]{1,0:T(8,128)(2,1)S(1)}, bf16[128,3712]{1,0:T(8,128)(2,1)S(1)}, u32[]{:S(2)}, u32[]{:S(2)}) collective-permute-start(bf16[128,3712]{1,0:T(8,128)(2,1)S(1)} %get-tuple-element.47.refs_1_), channel_id=1, source_target_pairs={{8,12},{10,14},{9,13},{11,15},{24,28},{26,30},{25,29},{27,31}} | collective-permute-start | bytes 2850824 | tf_op jit(solution)/shard_map/ppermute | solution.py:238
  70.1 16.0 %collective-permute-start.12 = (bf16[80,3584]{1,0:T(8,128)(2,1)S(1)}, bf16[80,3584]{1,0:T(8,128)(2,1)S(1)}, u32[]{:S(2)}, u32[]{:S(2)}) collective-permute-start(bf16[80,3584]{1,0:T(8,128)(2,1)S(1)} %get-tuple-element.53), channel_id=1, source_target_pairs={{0,2},{2,0},{4,6},{6,4},{8,10},{10,8},{12,14},{14,12},{1,3},{3,1},... | collective-permute-start | bytes 1720328 | tf_op jit(solution)/shard_map/ppermute | solution.py:241
  72.7 26.1 %collective-permute-start.9 = (bf16[80,3712]{1,0:T(8,128)(2,1)S(1)}, bf16[80,3712]{1,0:T(8,128)(2,1)S(1)}, u32[]{:S(2)}, u32[]{:S(2)}) collective-permute-start(bf16[80,3712]{1,0:T(8,128)(2,1)S(1)} %get-tuple-element.51), channel_id=1, source_target_pairs={{0,2},{2,0},{4,6},{6,4},{8,10},{10,8},{12,14},{14,12},{1,3},{3,1},... | collective-permute-start | bytes 1781768 | tf_op jit(solution)/shard_map/ppermute | solution.py:241
  87.5 34.8 %collective-permute-start.15 = (bf16[128,3584]{1,0:T(8,128)(2,1)S(1)}, bf16[128,3584]{1,0:T(8,128)(2,1)S(1)}, u32[]{:S(2)}, u32[]{:S(2)}) collective-permute-start(bf16[128,3584]{1,0:T(8,128)(2,1)S(1)} %get-tuple-element.54.refs_4_), channel_id=1, source_target_pairs={{8,4},{10,6},{12,8},{14,10},{9,5},{11,7},{13,9},{15,11},{24,20},{2... | collective-permute-start | bytes 2752520 | tf_op jit(solution)/shard_map/ppermute | solution.py:238
  88.2 34.1 %collective-permute-start.16 = (bf16[128,3584]{1,0:T(8,128)(2,1)S(1)}, bf16[128,3584]{1,0:T(8,128)(2,1)S(1)}, u32[]{:S(2)}, u32[]{:S(2)}) collective-permute-start(bf16[128,3584]{1,0:T(8,128)(2,1)S(1)} %get-tuple-element.54.refs_4_), channel_id=1, source_target_pairs={{0,4},{2,6},{4,8},{6,10},{1,5},{3,7},{5,9},{7,11},{16,20},{18,22},... | collective-permute-start | bytes 2752520 | tf_op jit(solution)/shard_map/ppermute | solution.py:238
  94.7 16.8 %collective-permute-start.14 = (bf16[80,3712]{1,0:T(8,128)(2,1)S(1)}, bf16[80,3712]{1,0:T(8,128)(2,1)S(1)}, u32[]{:S(2)}, u32[]{:S(2)}) collective-permute-start(bf16[80,3712]{1,0:T(8,128)(2,1)S(1)} %get-tuple-element.59), channel_id=1, source_target_pairs={{0,2},{2,0},{4,6},{6,4},{8,10},{10,8},{12,14},{14,12},{1,3},{3,1},... | collective-permute-start | bytes 1781768 | tf_op jit(solution)/shard_map/ppermute | solution.py:241
  108.0 16.0 %collective-permute-start.13 = (bf16[80,3584]{1,0:T(8,128)(2,1)S(1)}, bf16[80,3584]{1,0:T(8,128)(2,1)S(1)}, u32[]{:S(2)}, u32[]{:S(2)}) collective-permute-start(bf16[80,3584]{1,0:T(8,128)(2,1)S(1)} %get-tuple-element.57), channel_id=1, source_target_pairs={{0,2},{2,0},{4,6},{6,4},{8,10},{10,8},{12,14},{14,12},{1,3},{3,1},... | collective-permute-start | bytes 1720328 | tf_op jit(solution)/shard_map/ppermute | solution.py:241
  120.7 10.7 %copy-start = (bf16[80,3712]{1,0:T(8,128)(2,1)S(1)}, bf16[80,3712]{1,0:T(8,128)(2,1)}, u32[]{:S(2)}) copy-start(bf16[80,3712]{1,0:T(8,128)(2,1)} %get-tuple-element.39.refs_0_) | copy-start | bytes 1781764
  120.7 21.5 %collective-permute-start.19 = (bf16[80,3584]{1,0:T(8,128)(2,1)S(1)}, bf16[80,3584]{1,0:T(8,128)(2,1)S(1)}, u32[]{:S(2)}, u32[]{:S(2)}) collective-permute-start(bf16[80,3584]{1,0:T(8,128)(2,1)S(1)} %get-tuple-element.65), channel_id=1, source_target_pairs={{0,2},{2,0},{4,6},{6,4},{8,10},{10,8},{12,14},{14,12},{1,3},{3,1},... | collective-permute-start | bytes 1720328 | tf_op jit(solution)/shard_map/ppermute | solution.py:241
  125.4 26.5 %collective-permute-start.18 = (bf16[128,3584]{1,0:T(8,128)(2,1)S(1)}, bf16[128,3584]{1,0:T(8,128)(2,1)S(1)}, u32[]{:S(2)}, u32[]{:S(2)}) collective-permute-start(bf16[128,3584]{1,0:T(8,128)(2,1)S(1)} %get-tuple-element.61.refs_8_.refs_0_), channel_id=1, source_target_pairs={{0,8},{2,10},{12,4},{14,6},{1,9},{3,11},{13,5},{15,7},{16,24},{18,... | collective-permute-start | bytes 2752520 | tf_op jit(solution)/shard_map/ppermute | solution.py:238
  140.7 9.8 %collective-permute-start.17 = (bf16[80,3584]{1,0:T(8,128)(2,1)S(1)}, bf16[80,3584]{1,0:T(8,128)(2,1)S(1)}, u32[]{:S(2)}, u32[]{:S(2)}) collective-permute-start(bf16[80,3584]{1,0:T(8,128)(2,1)S(1)} %get-tuple-element.63), channel_id=1, source_target_pairs={{0,2},{2,0},{4,6},{6,4},{8,10},{10,8},{12,14},{14,12},{1,3},{3,1},... | collective-permute-start | bytes 1720328 | tf_op jit(solution)/shard_map/ppermute | solution.py:241
  142.9 16.9 %collective-permute-start.21 = (bf16[128,1792]{1,0:T(8,128)(2,1)S(1)}, bf16[128,1792]{1,0:T(8,128)(2,1)S(1)}, u32[]{:S(2)}, u32[]{:S(2)}) collective-permute-start(bf16[128,1792]{1,0:T(8,128)(2,1)S(1)} %get-tuple-element.67), channel_id=1, source_target_pairs={{0,4},{2,6},{12,8},{14,10},{1,5},{3,7},{13,9},{15,11},{16,20},{18,... | collective-permute-start | bytes 1376264 | tf_op jit(solution)/shard_map/ppermute | solution.py:238
  144.2 37.4 %collective-permute-start.20 = (bf16[128,3584]{1,0:T(8,128)(2,1)S(1)}, bf16[128,3584]{1,0:T(8,128)(2,1)S(1)}, u32[]{:S(2)}, u32[]{:S(2)}) collective-permute-start(bf16[128,3584]{1,0:T(8,128)(2,1)S(1)} %get-tuple-element.66.refs_7_), channel_id=1, source_target_pairs={{4,0},{6,2},{8,12},{10,14},{5,1},{7,3},{9,13},{11,15},{20,16},{22,... | collective-permute-start | bytes 2752520 | tf_op jit(solution)/shard_map/ppermute | solution.py:238
  145.5 19.2 %collective-permute-start.23 = (bf16[128,1792]{1,0:T(8,128)(2,1)S(1)}, bf16[128,1792]{1,0:T(8,128)(2,1)S(1)}, u32[]{:S(2)}, u32[]{:S(2)}) collective-permute-start(bf16[128,1792]{1,0:T(8,128)(2,1)S(1)} %get-tuple-element.68), channel_id=1, source_target_pairs={{0,4},{2,6},{12,8},{14,10},{1,5},{3,7},{13,9},{15,11},{16,20},{18,... | collective-permute-start | bytes 1376264 | tf_op jit(solution)/shard_map/ppermute | solution.py:238
  159.9 21.7 %collective-permute-start.22 = (bf16[128,1792]{1,0:T(8,128)(2,1)S(1)}, bf16[128,1792]{1,0:T(8,128)(2,1)S(1)}, u32[]{:S(2)}, u32[]{:S(2)}) collective-permute-start(bf16[128,1792]{1,0:T(8,128)(2,1)S(1)} %shard_map.77.refs_2_), channel_id=1, source_target_pairs={{4,12},{6,14},{8,0},{10,2},{5,13},{7,15},{9,1},{11,3},{20,28},{22,... | collective-permute-start | bytes 1376264 | tf_op jit(solution)/shard_map/ppermute | solution.py:238
  164.8 16.8 %collective-permute-start.24 = (bf16[128,1792]{1,0:T(8,128)(2,1)S(1)}, bf16[128,1792]{1,0:T(8,128)(2,1)S(1)}, u32[]{:S(2)}, u32[]{:S(2)}) collective-permute-start(bf16[128,1792]{1,0:T(8,128)(2,1)S(1)} %shard_map.78), channel_id=1, source_target_pairs={{4,12},{6,14},{8,0},{10,2},{5,13},{7,15},{9,1},{11,3},{20,28},{22,... | collective-permute-start | bytes 1376264 | tf_op jit(solution)/shard_map/ppermute | solution.py:238

commit v14 on v13

--- a/solution.py
+++ b/solution.py
@@ -182,6 +182,13 @@
     result[...] = total.astype(jnp.bfloat16)
 
 
+def sum_kernel(*refs):
+    total = refs[0][...].astype(jnp.float32)
+    for extra in refs[1:-1]:
+        total += extra[...].astype(jnp.float32)
+    refs[-1][...] = total.astype(jnp.bfloat16)
+
+
 def join_kernel(index, whole, half, result):
     size = half.shape[1]
     total = whole[:, index * size : (index + 1) * size].astype(jnp.float32) + half[...].astype(jnp.float32)
@@ -195,14 +202,23 @@
     refs[-1][...] = refs[-3][:, size:]
 
 
+def low_kernel(*refs):
+    *whole, low, result = refs
+    size = low.shape[1]
+    total = low[...].astype(jnp.float32)
+    for extra in whole:
+        total += extra[:, :size].astype(jnp.float32)
+    result[...] = total.astype(jnp.bfloat16)
+
+
 def finish_kernel(*refs):
     *whole, low, high, result = refs
     size = low.shape[1]
-    for half, first in ((low, 0), (high, size)):
-        total = half[...].astype(jnp.float32)
-        for extra in whole:
-            total += extra[:, first : first + size].astype(jnp.float32)
-        result[:, first : first + size] = total.astype(jnp.bfloat16)
+    total = high[...].astype(jnp.float32)
+    for extra in whole:
+        total += extra[:, size:].astype(jnp.float32)
+    result[:, :size] = low[...]
+    result[:, size:] = total.astype(jnp.bfloat16)
 
 
 def on_device(tokens, routes, route_scale, w_gate, w_up, w_down):
@@ -220,7 +236,7 @@
     own = (w_gate[0], w_up[0], w_down[0])
     block, *picked = call(
         functools.partial(first_kernel, experts),
-        [bf16((count, wide)), bf16((count, cap)), bf16((count, cap)), hbm((cap, wide)), bf16((cap, wide))],
+        [bf16((count, wide)), bf16((count, cap)), bf16((count, cap)), hbm((cap, wide)), hbm((cap, wide))],
         [*map(in_hbm, (tokens, routes.T, route_scale.T))],
         (),
         [
@@ -231,7 +247,7 @@
         [ANYWHERE] * 3,
     )
     swap = functools.partial(lax.ppermute, axis_name="local", perm=[(0, 1), (1, 0)])
-    weights = [in_hbm(w) for w in (*own, *map(swap, own))]
+    weights = [*map(in_hbm, own), *map(swap, own)]
 
     def along(block, pairs):
         moves = [(2 * a + y, 2 * b + y) for a, b in pairs for y in range(2)]
@@ -325,7 +341,10 @@
         return call(halves_kernel, outs, [*maps, own_out, other_out], after)
 
     def do_spread(slot, after=()):
-        done, *halves[:] = ordered(spread_halves, picks[slot][0], *outs[slot], after=after)
+        if slot == places - 1:
+            done, *halves[:] = ordered(spread_halves, picks[slot][0], *outs[slot], after=after)
+        else:
+            done = ordered(spread, picks[slot][0], *outs[slot], after=after)
         kept[slot] = done
         home = [(a, origin(a, slot)) for a in range(places) if a not in staying.get(slot, ())]
         rounds = []
@@ -335,6 +354,9 @@
             rounds.append(along(done, now))
         returned.append(rounds)
 
+    def call_sum(blocks, after=(), cost=0):
+        return call(sum_kernel, [bf16((count, width))], blocks, after, cost=cost)
+
     def join(whole, half, index, after=()):
         return call(functools.partial(join_kernel, index), [bf16(half.shape)], [whole, half], after)[0]
 
@@ -342,15 +364,15 @@
         while len(whole) > 8:
             summed = sum(array.astype(jnp.float32) for array in whole[:8])
             whole = [summed.astype(jnp.bfloat16), *whole[8:]]
-        return call(finish_kernel, [bf16((count, width))], [*whole, *parts])[0]
+        low = call(low_kernel, [bf16(parts[0].shape)], [*whole, parts[0]], cost=128 * MIB)[0]
+        return call(finish_kernel, [bf16((count, width))], [*whole, low, parts[1]])[0]
 
     relay(1)
     relay(2)
-    do_pick(1, after=weights[3:])
-    picks[0] = picked[:2], picked[2], across(picked[3])
+    do_pick(1, after=weights[3:4])
     do_expert(1, cost=64 * MIB)
     held[1, 2], held[-1, 2] = call(
-        passing_kernel, [bf16((count, wide))] * 2, [held[1, 2], held[-1, 2]], [*last, picks[1][2], picks[0][2]]
+        passing_kernel, [bf16((count, wide))] * 2, [held[1, 2], held[-1, 2]], [*last, picks[1][2]]
     )
     for step in range(3, places):
         relay(step)
@@ -363,14 +385,16 @@
         do_spread(slot - 1, after=returned[slot - 3])
         if slot + 1 < places:
             do_pick(slot + 1)
+    picks[0] = picked[:2], picked[2], across(picked[3])
+    do_spread(places - 1)
     do_expert(0)
-    do_spread(places - 1)
     near = returned.pop(places - 3)
-    total = ordered(spread, picks[0][0], *outs[0], [*returned.pop(0), *near] if places > 3 else near, cost=128 * MIB)
+    (summed,) = ordered(call_sum, [*returned.pop(0), *near] if places > 3 else near, cost=128 * MIB)
     homes = [(q, origin(q, places - 2)) for _, q in hops]
     parts = []
     for arrived in [along(half, hops) for half in halves]:
         parts.append(along(ordered(join, kept[places - 2], arrived, len(parts)), homes))
+    total = ordered(spread, picks[0][0], *outs[0], [summed])
     return finish([total, *sum(returned, [])], parts)
 
 

time: 183 us -> 174 us (0.951)
  waiting for transfers between devices: 85.9 us -> 79.7 us
  local copies, waits for them, and re-layouts: 4.79 us -> 0.01 us
    ppermute x14, waiting for transfers between devices: 50.6 us -> 39.1 us  [along(): return lax.ppermute(block, 'node', moves)]
    ppermute x8, waiting for transfers between devices: 35.3 us -> 40.6 us  [across(): return lax.ppermute(block, 'node', [(n, n ^ 1) for n in range(experts)])]
    unnamed x8 -> x4, local copies, waits for them, and re-layouts: 4.79 us -> 0.01 us
    pallas_call x16 -> x18, Pallas kernels: 48.8 us -> 49.1 us  [call(): pl.pallas_call(body, out_shape=outs, in_specs=specs, out_specs=out_specs...]
  transfers between devices with their start and end apart: 25 -> 25, of which waited for: 13 -> 14; matrix products, arithmetic and copies ran while one was open for 0% -> 0% of each run, Pallas kernels for 26% -> 28%
where the time goes in v14:
time: 174 us; the launch traced here: 173 us
  waiting for transfers between devices  79.7 us (46%)
  Pallas kernels  49.1 us (28%)
  starting transfers between devices  44.2 us (25%)
    pallas_call x18, Pallas kernels, call(): pl.pallas_call(body, out_shape=outs, in_specs=specs, out_specs=out_specs...  49.1 us
    ppermute x8, waiting for transfers between devices, across(): return lax.ppermute(block, 'node', [(n, n ^ 1) for n in range(experts)])  40.6 us
    ppermute x14, waiting for transfers between devices, along(): return lax.ppermute(block, 'node', moves)  39.1 us
    ppermute x14, starting transfers between devices, along(): return lax.ppermute(block, 'node', moves)  31.6 us
    ppermute x8, starting transfers between devices, across(): return lax.ppermute(block, 'node', [(n, n ^ 1) for n in range(experts)])  11.7 us
  transfers between devices with their start and end apart: 25, of which 14 were waited for; matrix products, arithmetic and copies ran while one was open for 0% of the time, Pallas kernels for 28%

profile of v14, /device:TPU:0, one launch (start us, length us, event | category | flops | bytes accessed | tf_op | source)
XLA Modules:
  0.0 173.4 jit_solution(3305833227255404871)
XLA Ops:
  0.0 0.5 collective-permute-start.1
  0.5 0.1 collective-permute-start.2
  0.5 0.5 collective-permute-start.3
  1.0 2.8 %shard_map.64 = (bf16[128,3712]{1,0:T(8,128)(2,1)S(1)}, bf16[128,80]{1,0:T(8,128)(2,1)S(1)}, bf16[128,80]{1,0:T(8,128)(2,1)S(1)}, bf16[80,3712]{1,0:T(8,128)(2,1)}, bf16[80,3712]{1,0:T(8,128)(2,1)}) custom-call(bf16[128,3584]{1,0:T(8,128)(2,1)} %tokens.1, s32[2,128]{1,0:T(2,128)} %bitcast.20, f32[2,128]{1,0:T(2,128)} %bitcast.21), custom_call_target="tpu_custom_call" | custom-call | tf_op jit(solution)/shard_map/pallas_call | solution.py:33
  3.8 4.5 %collective-permute-start.5 = (bf16[128,3712]{1,0:T(8,128)(2,1)S(1)}, bf16[128,3712]{1,0:T(8,128)(2,1)S(1)}, u32[]{:S(2)}, u32[]{:S(2)}) collective-permute-start(bf16[128,3712]{1,0:T(8,128)(2,1)S(1)} %get-tuple-element.39), channel_id=1, source_target_pairs={{0,4},{2,6},{4,8},{6,10},{8,12},{10,14},{1,5},{3,7},{5,9},{7,11},{... | collective-permute-start | bytes 2850824 | tf_op jit(solution)/shard_map/ppermute | solution.py:254
  8.3 1.3 collective-permute-start.4
  9.6 19.6 %collective-permute-done.5.refs_1_.refs_2_ = bf16[128,3712]{1,0:T(8,128)(2,1)S(1)} collective-permute-done((bf16[128,3712]{1,0:T(8,128)(2,1)S(1)}, bf16[128,3712]{1,0:T(8,128)(2,1)S(1)}, u32[]{:S(2)}, u32[]{:S(2)}) %collective-permute-start.5) | collective-permute-done | bytes 950304 | tf_op jit(solution)/shard_map/ppermute | solution.py:254
  29.3 0.7 collective-permute-start.6
  30.0 3.5 %collective-permute-done.4.refs_0_ = bf16[128,3712]{1,0:T(8,128)(2,1)S(1)} collective-permute-done((bf16[128,3712]{1,0:T(8,128)(2,1)S(1)}, bf16[128,3712]{1,0:T(8,128)(2,1)S(1)}, u32[]{:S(2)}, u32[]{:S(2)}) %collective-permute-start.4) | collective-permute-done | bytes 950304 | tf_op jit(solution)/shard_map/ppermute | solution.py:254
  33.4 1.3 collective-permute-start.7
  34.7 0.0 collective-permute-done.1.refs_2_.refs_5_
  34.7 1.0 shard_map.65
  35.8 1.6 collective-permute-start.8
  37.4 0.0 collective-permute-done.2.refs_6_
  37.4 0.0 collective-permute-done.3.refs_7_
  37.4 13.2 %collective-permute-done.8.refs_1_.refs_3_ = bf16[80,3712]{1,0:T(8,128)(2,1)S(1)} collective-permute-done((bf16[80,3712]{1,0:T(8,128)(2,1)S(1)}, bf16[80,3712]{1,0:T(8,128)(2,1)S(1)}, u32[]{:S(2)}, u32[]{:S(2)}) %collective-permute-start.8) | collective-permute-done | bytes 593952 | tf_op jit(solution)/shard_map/ppermute | solution.py:257
  50.6 9.6 %shard_map.66 = (bf16[80,3584]{1,0:T(8,128)(2,1)S(1)}, bf16[80,3584]{1,0:T(8,128)(2,1)S(1)}) custom-call(bf16[80,3712]{1,0:T(8,128)(2,1)S(1)} %get-tuple-element.40.refs_0_, bf16[80,3712]{1,0:T(8,128)(2,1)S(1)} %collective-permute-done.8.refs_1_.refs_3_, bf16[3584,512]{1,0:T(8,128)(2,1)} %bitcast.6, bf16[3584,512]{1,0:T(8,128)(2,1)} %bitcast.11, ...), custom_call_target="tpu_custom_call" | custom-call | bytes 67108864 | tf_op jit(solution)/shard_map/pallas_call | solution.py:33
  60.2 0.0 collective-permute-done.6.refs_0_
  60.2 0.1 shard_map.67
  60.4 0.7 collective-permute-start.10
  61.1 1.3 collective-permute-start.9
  62.4 1.6 collective-permute-start.11
  64.0 1.0 shard_map.68
  65.0 0.6 collective-permute-start.13
  65.6 12.8 %collective-permute-done.11.refs_3_ = bf16[80,3584]{1,0:T(8,128)(2,1)S(1)} collective-permute-done((bf16[80,3584]{1,0:T(8,128)(2,1)S(1)}, bf16[80,3584]{1,0:T(8,128)(2,1)S(1)}, u32[]{:S(2)}, u32[]{:S(2)}) %collective-permute-start.11) | collective-permute-done | bytes 573472 | tf_op jit(solution)/shard_map/ppermute | solution.py:257
  78.4 0.6 shard_map.69.refs_4_
  79.0 0.7 collective-permute-start.16
  79.7 5.2 %collective-permute-start.17 = (bf16[128,3584]{1,0:T(8,128)(2,1)S(1)}, bf16[128,3584]{1,0:T(8,128)(2,1)S(1)}, u32[]{:S(2)}, u32[]{:S(2)}) collective-permute-start(bf16[128,3584]{1,0:T(8,128)(2,1)S(1)} %shard_map.69.refs_4_), channel_id=1, source_target_pairs={{0,4},{2,6},{4,8},{6,10},{1,5},{3,7},{5,9},{7,11},{16,20},{18,22},... | collective-permute-start | bytes 2752520 | tf_op jit(solution)/shard_map/ppermute | solution.py:254
  85.0 0.0 collective-permute-done.9.refs_1_
  85.0 1.2 shard_map.70
  86.2 1.6 collective-permute-start.12
  87.8 3.3 %collective-permute-done.13.refs_1_ = bf16[80,3712]{1,0:T(8,128)(2,1)S(1)} collective-permute-done((bf16[80,3712]{1,0:T(8,128)(2,1)S(1)}, bf16[80,3712]{1,0:T(8,128)(2,1)S(1)}, u32[]{:S(2)}, u32[]{:S(2)}) %collective-permute-start.13) | collective-permute-done | bytes 593952 | tf_op jit(solution)/shard_map/ppermute | solution.py:257
  91.1 9.6 %shard_map.71 = (bf16[80,3584]{1,0:T(8,128)(2,1)S(1)}, bf16[80,3584]{1,0:T(8,128)(2,1)S(1)}) custom-call(bf16[80,3712]{1,0:T(8,128)(2,1)S(1)} %get-tuple-element.53.refs_0_, bf16[80,3712]{1,0:T(8,128)(2,1)S(1)} %collective-permute-done.13.refs_1_, bf16[3584,512]{1,0:T(8,128)(2,1)} %bitcast.7, bf16[3584,512]{1,0:T(8,128)(2,1)} %bitcast.12, ...), custom_call_target="tpu_custom_call" | custom-call | tf_op jit(solution)/shard_map/pallas_call | solution.py:33
  100.7 1.6 collective-permute-start.15
  102.3 1.5 collective-permute-done.12.refs_1_
  103.8 9.6 %shard_map.72 = (bf16[80,3584]{1,0:T(8,128)(2,1)S(1)}, bf16[80,3584]{1,0:T(8,128)(2,1)S(1)}) custom-call(bf16[80,3712]{1,0:T(8,128)(2,1)S(1)} %get-tuple-element.51.refs_0_, bf16[80,3712]{1,0:T(8,128)(2,1)S(1)} %collective-permute-done.12.refs_1_, bf16[3584,512]{1,0:T(8,128)(2,1)} %bitcast.8, bf16[3584,512]{1,0:T(8,128)(2,1)} %bitcast.13, ...), custom_call_target="tpu_custom_call" | custom-call | tf_op jit(solution)/shard_map/pallas_call | solution.py:33
  113.5 0.0 copy-start
  113.5 1.6 collective-permute-start.14
  115.1 0.8 collective-permute-done.15.refs_3_
  115.9 0.6 shard_map.73.refs_4_.refs_0_
  116.5 5.8 %collective-permute-start.19 = (bf16[128,3584]{1,0:T(8,128)(2,1)S(1)}, bf16[128,3584]{1,0:T(8,128)(2,1)S(1)}, u32[]{:S(2)}, u32[]{:S(2)}) collective-permute-start(bf16[128,3584]{1,0:T(8,128)(2,1)S(1)} %shard_map.73.refs_4_.refs_0_), channel_id=1, source_target_pairs={{0,8},{2,10},{12,4},{14,6},{1,9},{3,11},{13,5},{15,7},{16,24},{18,... | collective-permute-start | bytes 2752520 | tf_op jit(solution)/shard_map/ppermute | solution.py:254
  122.3 1.6 collective-permute-start
  123.9 5.6 %collective-permute-done.14.refs_3_ = bf16[80,3584]{1,0:T(8,128)(2,1)S(1)} collective-permute-done((bf16[80,3584]{1,0:T(8,128)(2,1)S(1)}, bf16[80,3584]{1,0:T(8,128)(2,1)S(1)}, u32[]{:S(2)}, u32[]{:S(2)}) %collective-permute-start.14) | collective-permute-done | bytes 573472 | tf_op jit(solution)/shard_map/ppermute | solution.py:257
  129.5 0.6 shard_map.74
  130.1 4.6 %collective-permute-start.21 = (bf16[128,1792]{1,0:T(8,128)(2,1)S(1)}, bf16[128,1792]{1,0:T(8,128)(2,1)S(1)}, u32[]{:S(2)}, u32[]{:S(2)}) collective-permute-start(bf16[128,1792]{1,0:T(8,128)(2,1)S(1)} %get-tuple-element.64), channel_id=1, source_target_pairs={{0,4},{2,6},{12,8},{14,10},{1,5},{3,7},{13,9},{15,11},{16,20},{18,... | collective-permute-start | bytes 1376264 | tf_op jit(solution)/shard_map/ppermute | solution.py:254
  134.7 1.3 collective-permute-start.20
  136.1 1.5 collective-permute-start.22
  137.6 1.0 collective-permute-done.refs_1_
  138.6 9.6 %shard_map.75 = (bf16[80,3584]{1,0:T(8,128)(2,1)S(1)}, bf16[80,3584]{1,0:T(8,128)(2,1)S(1)}) custom-call(bf16[80,3712]{1,0:T(8,128)(2,1)S(1)} %copy-done, bf16[80,3712]{1,0:T(8,128)(2,1)S(1)} %collective-permute-done.refs_1_, bf16[3584,512]{1,0:T(8,128)(2,1)} %bitcast.9, bf16[3584,512]{1,0:T(8,128)(2,1)} %bitcast.14, bf16[512,3584]{1,0:T(8,128)(2,1)} %bitcast.19, ...), custom_call_target="tpu_custom_call" | custom-call | tf_op jit(solution)/shard_map/pallas_call | solution.py:33
  148.2 1.6 collective-permute-start.18
  149.8 0.3 shard_map.76.refs_2_.refs_4_
  150.2 0.7 collective-permute-done.21.refs_1_
  150.9 0.1 shard_map.77.refs_2_
  151.0 1.3 collective-permute-start.23
  152.3 3.5 %collective-permute-done.20.refs_1_ = bf16[128,1792]{1,0:T(8,128)(2,1)S(1)} collective-permute-done((bf16[128,1792]{1,0:T(8,128)(2,1)S(1)}, bf16[128,1792]{1,0:T(8,128)(2,1)S(1)}, u32[]{:S(2)}, u32[]{:S(2)}) %collective-permute-start.20) | collective-permute-done | bytes 458784 | tf_op jit(solution)/shard_map/ppermute | solution.py:254
  155.8 0.1 shard_map.78.refs_5_
  155.9 1.3 collective-permute-start.24
  157.2 2.5 %collective-permute-done.18.refs_3_ = bf16[80,3584]{1,0:T(8,128)(2,1)S(1)} collective-permute-done((bf16[80,3584]{1,0:T(8,128)(2,1)S(1)}, bf16[80,3584]{1,0:T(8,128)(2,1)S(1)}, u32[]{:S(2)}, u32[]{:S(2)}) %collective-permute-start.18) | collective-permute-done | bytes 573472 | tf_op jit(solution)/shard_map/ppermute | solution.py:257
  159.7 0.6 shard_map.79.refs_0_
  160.3 6.5 %collective-permute-done.23.refs_2_ = bf16[128,1792]{1,0:T(8,128)(2,1)S(1)} collective-permute-done((bf16[128,1792]{1,0:T(8,128)(2,1)S(1)}, bf16[128,1792]{1,0:T(8,128)(2,1)S(1)}, u32[]{:S(2)}, u32[]{:S(2)}) %collective-permute-start.23) | collective-permute-done | bytes 458784 | tf_op jit(solution)/shard_map/ppermute | solution.py:254
  166.8 5.2 %collective-permute-done.22.refs_1_ = bf16[128,3584]{1,0:T(8,128)(2,1)S(1)} collective-permute-done((bf16[128,3584]{1,0:T(8,128)(2,1)S(1)}, bf16[128,3584]{1,0:T(8,128)(2,1)S(1)}, u32[]{:S(2)}, u32[]{:S(2)}) %collective-permute-start.22) | collective-permute-done | bytes 917536 | tf_op jit(solution)/shard_map/ppermute | solution.py:254
  172.0 0.2 shard_map.80.refs_2_
  172.2 0.0 collective-permute-done.24.refs_3_
  172.2 1.1 shard_map.81
  (8 shorter events, 0.0 us)
Async XLA Ops:
  0.0 34.7 %collective-permute-start.1 = (bf16[3584,512]{1,0:T(8,128)(2,1)}, bf16[3584,512]{1,0:T(8,128)(2,1)S(1)}, u32[]{:S(2)}, u32[]{:S(2)}) collective-permute-start(bf16[3584,512]{1,0:T(8,128)(2,1)} %bitcast.5), channel_id=1, source_target_pairs={{0,1},{1,0},{2,3},{3,2},{4,5},{5,4},{6,7},{7,6},{8,9},{9,8},{10,11... | collective-permute-start | bytes 11010056 | tf_op jit(solution)/shard_map/ppermute | solution.py:250
  0.5 36.9 %collective-permute-start.2 = (bf16[3584,512]{1,0:T(8,128)(2,1)}, bf16[3584,512]{1,0:T(8,128)(2,1)S(1)}, u32[]{:S(2)}, u32[]{:S(2)}) collective-permute-start(bf16[3584,512]{1,0:T(8,128)(2,1)} %bitcast.10), channel_id=1, source_target_pairs={{0,1},{1,0},{2,3},{3,2},{4,5},{5,4},{6,7},{7,6},{8,9},{9,8},{10,11... | collective-permute-start | bytes 11010056 | tf_op jit(solution)/shard_map/ppermute | solution.py:250
  0.5 36.8 %collective-permute-start.3 = (bf16[512,3584]{1,0:T(8,128)(2,1)}, bf16[512,3584]{1,0:T(8,128)(2,1)S(1)}, u32[]{:S(2)}, u32[]{:S(2)}) collective-permute-start(bf16[512,3584]{1,0:T(8,128)(2,1)} %bitcast.15), channel_id=1, source_target_pairs={{0,1},{1,0},{2,3},{3,2},{4,5},{5,4},{6,7},{7,6},{8,9},{9,8},{10,11... | collective-permute-start | bytes 11010056 | tf_op jit(solution)/shard_map/ppermute | solution.py:250
  3.8 25.5 %collective-permute-start.5 = (bf16[128,3712]{1,0:T(8,128)(2,1)S(1)}, bf16[128,3712]{1,0:T(8,128)(2,1)S(1)}, u32[]{:S(2)}, u32[]{:S(2)}) collective-permute-start(bf16[128,3712]{1,0:T(8,128)(2,1)S(1)} %get-tuple-element.39), channel_id=1, source_target_pairs={{0,4},{2,6},{4,8},{6,10},{8,12},{10,14},{1,5},{3,7},{5,9},{7,11},{... | collective-permute-start | bytes 2850824 | tf_op jit(solution)/shard_map/ppermute | solution.py:254
  8.3 25.1 %collective-permute-start.4 = (bf16[128,3712]{1,0:T(8,128)(2,1)S(1)}, bf16[128,3712]{1,0:T(8,128)(2,1)S(1)}, u32[]{:S(2)}, u32[]{:S(2)}) collective-permute-start(bf16[128,3712]{1,0:T(8,128)(2,1)S(1)} %get-tuple-element.39), channel_id=1, source_target_pairs={{4,0},{6,2},{8,4},{10,6},{12,8},{14,10},{5,1},{7,3},{9,5},{11,7},{... | collective-permute-start | bytes 2850824 | tf_op jit(solution)/shard_map/ppermute | solution.py:254
  29.3 31.0 %collective-permute-start.6 = (bf16[128,3712]{1,0:T(8,128)(2,1)S(1)}, bf16[128,3712]{1,0:T(8,128)(2,1)S(1)}, u32[]{:S(2)}, u32[]{:S(2)}) collective-permute-start(bf16[128,3712]{1,0:T(8,128)(2,1)S(1)} %collective-permute-done.5.refs_1_.refs_2_), channel_id=1, source_target_pairs={{4,8},{6,10},{8,12},{10,14},{5,9},{7,11},{9,13},{11,15},{20,24},{2... | collective-permute-start | bytes 2850824 | tf_op jit(solution)/shard_map/ppermute | solution.py:254
  33.4 26.8 %collective-permute-start.7 = (bf16[128,3712]{1,0:T(8,128)(2,1)S(1)}, bf16[128,3712]{1,0:T(8,128)(2,1)S(1)}, u32[]{:S(2)}, u32[]{:S(2)}) collective-permute-start(bf16[128,3712]{1,0:T(8,128)(2,1)S(1)} %collective-permute-done.4.refs_0_), channel_id=1, source_target_pairs={{4,0},{6,2},{8,4},{10,6},{5,1},{7,3},{9,5},{11,7},{20,16},{22,18},... | collective-permute-start | bytes 2850824 | tf_op jit(solution)/shard_map/ppermute | solution.py:254
  35.8 14.8 %collective-permute-start.8 = (bf16[80,3712]{1,0:T(8,128)(2,1)S(1)}, bf16[80,3712]{1,0:T(8,128)(2,1)S(1)}, u32[]{:S(2)}, u32[]{:S(2)}) collective-permute-start(bf16[80,3712]{1,0:T(8,128)(2,1)S(1)} %get-tuple-element.41), channel_id=1, source_target_pairs={{0,2},{2,0},{4,6},{6,4},{8,10},{10,8},{12,14},{14,12},{1,3},{3,1},... | collective-permute-start | bytes 1781768 | tf_op jit(solution)/shard_map/ppermute | solution.py:257
  60.4 24.6 %collective-permute-start.10 = (bf16[128,3712]{1,0:T(8,128)(2,1)S(1)}, bf16[128,3712]{1,0:T(8,128)(2,1)S(1)}, u32[]{:S(2)}, u32[]{:S(2)}) collective-permute-start(bf16[128,3712]{1,0:T(8,128)(2,1)S(1)} %get-tuple-element.45.refs_1_), channel_id=1, source_target_pairs={{8,12},{10,14},{9,13},{11,15},{24,28},{26,30},{25,29},{27,31}} | collective-permute-start | bytes 2850824 | tf_op jit(solution)/shard_map/ppermute | solution.py:254
  61.1 23.9 %collective-permute-start.9 = (bf16[128,3712]{1,0:T(8,128)(2,1)S(1)}, bf16[128,3712]{1,0:T(8,128)(2,1)S(1)}, u32[]{:S(2)}, u32[]{:S(2)}) collective-permute-start(bf16[128,3712]{1,0:T(8,128)(2,1)S(1)} %get-tuple-element.44.refs_0_), channel_id=1, source_target_pairs={{4,0},{6,2},{5,1},{7,3},{20,16},{22,18},{21,17},{23,19}} | collective-permute-start | bytes 2850824 | tf_op jit(solution)/shard_map/ppermute | solution.py:254
  62.4 16.0 %collective-permute-start.11 = (bf16[80,3584]{1,0:T(8,128)(2,1)S(1)}, bf16[80,3584]{1,0:T(8,128)(2,1)S(1)}, u32[]{:S(2)}, u32[]{:S(2)}) collective-permute-start(bf16[80,3584]{1,0:T(8,128)(2,1)S(1)} %get-tuple-element.47), channel_id=1, source_target_pairs={{0,2},{2,0},{4,6},{6,4},{8,10},{10,8},{12,14},{14,12},{1,3},{3,1},... | collective-permute-start | bytes 1720328 | tf_op jit(solution)/shard_map/ppermute | solution.py:257
  65.0 26.1 %collective-permute-start.13 = (bf16[80,3712]{1,0:T(8,128)(2,1)S(1)}, bf16[80,3712]{1,0:T(8,128)(2,1)S(1)}, u32[]{:S(2)}, u32[]{:S(2)}) collective-permute-start(bf16[80,3712]{1,0:T(8,128)(2,1)S(1)} %get-tuple-element.54), channel_id=1, source_target_pairs={{0,2},{2,0},{4,6},{6,4},{8,10},{10,8},{12,14},{14,12},{1,3},{3,1},... | collective-permute-start | bytes 1781768 | tf_op jit(solution)/shard_map/ppermute | solution.py:257
  79.0 36.1 %collective-permute-start.16 = (bf16[128,3584]{1,0:T(8,128)(2,1)S(1)}, bf16[128,3584]{1,0:T(8,128)(2,1)S(1)}, u32[]{:S(2)}, u32[]{:S(2)}) collective-permute-start(bf16[128,3584]{1,0:T(8,128)(2,1)S(1)} %shard_map.69.refs_4_), channel_id=1, source_target_pairs={{8,4},{10,6},{12,8},{14,10},{9,5},{11,7},{13,9},{15,11},{24,20},{2... | collective-permute-start | bytes 2752520 | tf_op jit(solution)/shard_map/ppermute | solution.py:254
  79.7 35.4 %collective-permute-start.17 = (bf16[128,3584]{1,0:T(8,128)(2,1)S(1)}, bf16[128,3584]{1,0:T(8,128)(2,1)S(1)}, u32[]{:S(2)}, u32[]{:S(2)}) collective-permute-start(bf16[128,3584]{1,0:T(8,128)(2,1)S(1)} %shard_map.69.refs_4_), channel_id=1, source_target_pairs={{0,4},{2,6},{4,8},{6,10},{1,5},{3,7},{5,9},{7,11},{16,20},{18,22},... | collective-permute-start | bytes 2752520 | tf_op jit(solution)/shard_map/ppermute | solution.py:254
  86.2 17.6 %collective-permute-start.12 = (bf16[80,3712]{1,0:T(8,128)(2,1)S(1)}, bf16[80,3712]{1,0:T(8,128)(2,1)S(1)}, u32[]{:S(2)}, u32[]{:S(2)}) collective-permute-start(bf16[80,3712]{1,0:T(8,128)(2,1)S(1)} %get-tuple-element.52), channel_id=1, source_target_pairs={{0,2},{2,0},{4,6},{6,4},{8,10},{10,8},{12,14},{14,12},{1,3},{3,1},... | collective-permute-start | bytes 1781768 | tf_op jit(solution)/shard_map/ppermute | solution.py:257
  100.7 15.2 %collective-permute-start.15 = (bf16[80,3584]{1,0:T(8,128)(2,1)S(1)}, bf16[80,3584]{1,0:T(8,128)(2,1)S(1)}, u32[]{:S(2)}, u32[]{:S(2)}) collective-permute-start(bf16[80,3584]{1,0:T(8,128)(2,1)S(1)} %get-tuple-element.59), channel_id=1, source_target_pairs={{0,2},{2,0},{4,6},{6,4},{8,10},{10,8},{12,14},{14,12},{1,3},{3,1},... | collective-permute-start | bytes 1720328 | tf_op jit(solution)/shard_map/ppermute | solution.py:257
  113.5 8.8 %copy-start.1 = (bf16[80,3712]{1,0:T(8,128)(2,1)S(1)}, bf16[80,3712]{1,0:T(8,128)(2,1)}, u32[]{:S(2)}) copy-start(bf16[80,3712]{1,0:T(8,128)(2,1)} %get-tuple-element.38) | copy-start | bytes 1781764
  113.5 25.1 %copy-start = (bf16[80,3712]{1,0:T(8,128)(2,1)S(1)}, bf16[80,3712]{1,0:T(8,128)(2,1)}, u32[]{:S(2)}) copy-start(bf16[80,3712]{1,0:T(8,128)(2,1)} %get-tuple-element.37.refs_0_) | copy-start | bytes 1781764
  113.5 16.0 %collective-permute-start.14 = (bf16[80,3584]{1,0:T(8,128)(2,1)S(1)}, bf16[80,3584]{1,0:T(8,128)(2,1)S(1)}, u32[]{:S(2)}, u32[]{:S(2)}) collective-permute-start(bf16[80,3584]{1,0:T(8,128)(2,1)S(1)} %get-tuple-element.57), channel_id=1, source_target_pairs={{0,2},{2,0},{4,6},{6,4},{8,10},{10,8},{12,14},{14,12},{1,3},{3,1},... | collective-permute-start | bytes 1720328 | tf_op jit(solution)/shard_map/ppermute | solution.py:257
  116.5 33.3 %collective-permute-start.19 = (bf16[128,3584]{1,0:T(8,128)(2,1)S(1)}, bf16[128,3584]{1,0:T(8,128)(2,1)S(1)}, u32[]{:S(2)}, u32[]{:S(2)}) collective-permute-start(bf16[128,3584]{1,0:T(8,128)(2,1)S(1)} %shard_map.73.refs_4_.refs_0_), channel_id=1, source_target_pairs={{0,8},{2,10},{12,4},{14,6},{1,9},{3,11},{13,5},{15,7},{16,24},{18,... | collective-permute-start | bytes 2752520 | tf_op jit(solution)/shard_map/ppermute | solution.py:254
  122.3 16.3 %collective-permute-start = (bf16[80,3712]{1,0:T(8,128)(2,1)S(1)}, bf16[80,3712]{1,0:T(8,128)(2,1)S(1)}, u32[]{:S(2)}, u32[]{:S(2)}) collective-permute-start(bf16[80,3712]{1,0:T(8,128)(2,1)S(1)} %copy-done.1), channel_id=1, source_target_pairs={{0,2},{2,0},{4,6},{6,4},{8,10},{10,8},{12,14},{14,12},{1,3},{3,1},... | collective-permute-start | bytes 1781768 | tf_op jit(solution)/shard_map/ppermute | solution.py:257
  130.1 20.8 %collective-permute-start.21 = (bf16[128,1792]{1,0:T(8,128)(2,1)S(1)}, bf16[128,1792]{1,0:T(8,128)(2,1)S(1)}, u32[]{:S(2)}, u32[]{:S(2)}) collective-permute-start(bf16[128,1792]{1,0:T(8,128)(2,1)S(1)} %get-tuple-element.64), channel_id=1, source_target_pairs={{0,4},{2,6},{12,8},{14,10},{1,5},{3,7},{13,9},{15,11},{16,20},{18,... | collective-permute-start | bytes 1376264 | tf_op jit(solution)/shard_map/ppermute | solution.py:254
  134.7 21.1 %collective-permute-start.20 = (bf16[128,1792]{1,0:T(8,128)(2,1)S(1)}, bf16[128,1792]{1,0:T(8,128)(2,1)S(1)}, u32[]{:S(2)}, u32[]{:S(2)}) collective-permute-start(bf16[128,1792]{1,0:T(8,128)(2,1)S(1)} %get-tuple-element.63), channel_id=1, source_target_pairs={{0,4},{2,6},{12,8},{14,10},{1,5},{3,7},{13,9},{15,11},{16,20},{18,... | collective-permute-start | bytes 1376264 | tf_op jit(solution)/shard_map/ppermute | solution.py:254
  136.1 36.0 %collective-permute-start.22 = (bf16[128,3584]{1,0:T(8,128)(2,1)S(1)}, bf16[128,3584]{1,0:T(8,128)(2,1)S(1)}, u32[]{:S(2)}, u32[]{:S(2)}) collective-permute-start(bf16[128,3584]{1,0:T(8,128)(2,1)S(1)} %get-tuple-element.60.refs_8_), channel_id=1, source_target_pairs={{4,0},{6,2},{8,12},{10,14},{5,1},{7,3},{9,13},{11,15},{20,16},{22,... | collective-permute-start | bytes 2752520 | tf_op jit(solution)/shard_map/ppermute | solution.py:254
  148.2 11.4 %collective-permute-start.18 = (bf16[80,3584]{1,0:T(8,128)(2,1)S(1)}, bf16[80,3584]{1,0:T(8,128)(2,1)S(1)}, u32[]{:S(2)}, u32[]{:S(2)}) collective-permute-start(bf16[80,3584]{1,0:T(8,128)(2,1)S(1)} %get-tuple-element.62), channel_id=1, source_target_pairs={{0,2},{2,0},{4,6},{6,4},{8,10},{10,8},{12,14},{14,12},{1,3},{3,1},... | collective-permute-start | bytes 1720328 | tf_op jit(solution)/shard_map/ppermute | solution.py:257
  151.0 15.8 %collective-permute-start.23 = (bf16[128,1792]{1,0:T(8,128)(2,1)S(1)}, bf16[128,1792]{1,0:T(8,128)(2,1)S(1)}, u32[]{:S(2)}, u32[]{:S(2)}) collective-permute-start(bf16[128,1792]{1,0:T(8,128)(2,1)S(1)} %shard_map.77.refs_2_), channel_id=1, source_target_pairs={{4,12},{6,14},{8,0},{10,2},{5,13},{7,15},{9,1},{11,3},{20,28},{22,... | collective-permute-start | bytes 1376264 | tf_op jit(solution)/shard_map/ppermute | solution.py:254
  155.9 16.3 %collective-permute-start.24 = (bf16[128,1792]{1,0:T(8,128)(2,1)S(1)}, bf16[128,1792]{1,0:T(8,128)(2,1)S(1)}, u32[]{:S(2)}, u32[]{:S(2)}) collective-permute-start(bf16[128,1792]{1,0:T(8,128)(2,1)S(1)} %shard_map.78.refs_5_), channel_id=1, source_target_pairs={{4,12},{6,14},{8,0},{10,2},{5,13},{7,15},{9,1},{11,3},{20,28},{22,... | collective-permute-start | bytes 1376264 | tf_op jit(solution)/shard_map/ppermute | solution.py:254

commit v15 on v14

--- a/solution.py
+++ b/solution.py
@@ -368,15 +368,17 @@
         return call(finish_kernel, [bf16((count, width))], [*whole, low, parts[1]])[0]
 
     relay(1)
+    do_pick(1, after=weights[3:4])
     relay(2)
-    do_pick(1, after=weights[3:4])
+    picks[0] = picked[:2], picked[2], across(picked[3])
     do_expert(1, cost=64 * MIB)
     held[1, 2], held[-1, 2] = call(
-        passing_kernel, [bf16((count, wide))] * 2, [held[1, 2], held[-1, 2]], [*last, picks[1][2]]
+        passing_kernel, [bf16((count, wide))] * 2, [held[1, 2], held[-1, 2]], [*last, picks[1][2], picks[0][2]]
     )
     for step in range(3, places):
         relay(step)
     do_pick(2)
+    do_expert(0)
     do_spread(1)
     do_pick(3)
     do_expert(2)
@@ -385,9 +387,7 @@
         do_spread(slot - 1, after=returned[slot - 3])
         if slot + 1 < places:
             do_pick(slot + 1)
-    picks[0] = picked[:2], picked[2], across(picked[3])
     do_spread(places - 1)
-    do_expert(0)
     near = returned.pop(places - 3)
     (summed,) = ordered(call_sum, [*returned.pop(0), *near] if places > 3 else near, cost=128 * MIB)
     homes = [(q, origin(q, places - 2)) for _, q in hops]

time: 174 us -> 177 us (1.017)
  waiting for transfers between devices: 79.7 us -> 84.1 us
    ppermute x14, waiting for transfers between devices: 39.1 us -> 56.2 us  [along(): return lax.ppermute(block, 'node', moves)]
    ppermute x8, waiting for transfers between devices: 40.6 us -> 27.9 us  [across(): return lax.ppermute(block, 'node', [(n, n ^ 1) for n in range(experts)])]
  transfers between devices with their start and end apart: 25 -> 25, of which waited for: 14 -> 14; matrix products, arithmetic and copies ran while one was open for 0% -> 0% of each run, Pallas kernels for 28% -> 27%
where the time goes in v15:
time: 177 us
  waiting for transfers between devices  84.1 us (48%)
  Pallas kernels  49.3 us (28%)
  starting transfers between devices  42.9 us (24%)
    ppermute x14, waiting for transfers between devices, along(): return lax.ppermute(block, 'node', moves)  56.2 us
    pallas_call x18, Pallas kernels, call(): pl.pallas_call(body, out_shape=outs, in_specs=specs, out_specs=out_specs...  49.3 us
    ppermute x14, starting transfers between devices, along(): return lax.ppermute(block, 'node', moves)  31.3 us
    ppermute x8, waiting for transfers between devices, across(): return lax.ppermute(block, 'node', [(n, n ^ 1) for n in range(experts)])  27.9 us
    ppermute x8, starting transfers between devices, across(): return lax.ppermute(block, 'node', [(n, n ^ 1) for n in range(experts)])  10.6 us
  transfers between devices with their start and end apart: 25, of which 14 were waited for; matrix products, arithmetic and copies ran while one was open for 0% of the time, Pallas kernels for 27%

profile of v15, /device:TPU:0, one launch (start us, length us, event | category | flops | bytes accessed | tf_op | source)
XLA Modules:
  0.0 176.6 jit_solution(8020777717007026765)
XLA Ops:
  0.0 0.5 collective-permute-start.1
  0.5 0.1 collective-permute-start.2
  0.5 0.5 collective-permute-start.3
  1.0 2.8 %shard_map.64 = (bf16[128,3712]{1,0:T(8,128)(2,1)S(1)}, bf16[128,80]{1,0:T(8,128)(2,1)S(1)}, bf16[128,80]{1,0:T(8,128)(2,1)S(1)}, bf16[80,3712]{1,0:T(8,128)(2,1)}, bf16[80,3712]{1,0:T(8,128)(2,1)}) custom-call(bf16[128,3584]{1,0:T(8,128)(2,1)} %tokens.1, s32[2,128]{1,0:T(2,128)} %bitcast.20, f32[2,128]{1,0:T(2,128)} %bitcast.21), custom_call_target="tpu_custom_call" | custom-call | tf_op jit(solution)/shard_map/pallas_call | solution.py:33
  3.8 4.7 %collective-permute-start.4 = (bf16[128,3712]{1,0:T(8,128)(2,1)S(1)}, bf16[128,3712]{1,0:T(8,128)(2,1)S(1)}, u32[]{:S(2)}, u32[]{:S(2)}) collective-permute-start(bf16[128,3712]{1,0:T(8,128)(2,1)S(1)} %get-tuple-element.39), channel_id=1, source_target_pairs={{0,4},{2,6},{4,8},{6,10},{8,12},{10,14},{1,5},{3,7},{5,9},{7,11},{... | collective-permute-start | bytes 2850824 | tf_op jit(solution)/shard_map/ppermute | solution.py:254
  8.5 1.3 collective-permute-start.6
  9.8 19.6 %collective-permute-done.4.refs_1_.refs_2_ = bf16[128,3712]{1,0:T(8,128)(2,1)S(1)} collective-permute-done((bf16[128,3712]{1,0:T(8,128)(2,1)S(1)}, bf16[128,3712]{1,0:T(8,128)(2,1)S(1)}, u32[]{:S(2)}, u32[]{:S(2)}) %collective-permute-start.4) | collective-permute-done | bytes 950304 | tf_op jit(solution)/shard_map/ppermute | solution.py:254
  29.4 0.7 collective-permute-start.5
  30.1 3.5 %collective-permute-done.6.refs_0_ = bf16[128,3712]{1,0:T(8,128)(2,1)S(1)} collective-permute-done((bf16[128,3712]{1,0:T(8,128)(2,1)S(1)}, bf16[128,3712]{1,0:T(8,128)(2,1)S(1)}, u32[]{:S(2)}, u32[]{:S(2)}) %collective-permute-start.6) | collective-permute-done | bytes 950304 | tf_op jit(solution)/shard_map/ppermute | solution.py:254
  33.6 1.3 collective-permute-start.7
  34.9 1.0 shard_map.65
  35.9 1.6 collective-permute-start.8
  37.5 0.5 collective-permute-start
  38.0 0.0 collective-permute-done.3.refs_7_
  38.0 14.3 %collective-permute-done.8.refs_1_.refs_3_ = bf16[80,3712]{1,0:T(8,128)(2,1)S(1)} collective-permute-done((bf16[80,3712]{1,0:T(8,128)(2,1)S(1)}, bf16[80,3712]{1,0:T(8,128)(2,1)S(1)}, u32[]{:S(2)}, u32[]{:S(2)}) %collective-permute-start.8) | collective-permute-done | bytes 593952 | tf_op jit(solution)/shard_map/ppermute | solution.py:257
  52.3 9.6 %shard_map.66 = (bf16[80,3584]{1,0:T(8,128)(2,1)S(1)}, bf16[80,3584]{1,0:T(8,128)(2,1)S(1)}) custom-call(bf16[80,3712]{1,0:T(8,128)(2,1)S(1)} %get-tuple-element.40.refs_0_, bf16[80,3712]{1,0:T(8,128)(2,1)S(1)} %collective-permute-done.8.refs_1_.refs_3_, bf16[3584,512]{1,0:T(8,128)(2,1)} %bitcast.6, bf16[3584,512]{1,0:T(8,128)(2,1)} %bitcast.11, ...), custom_call_target="tpu_custom_call" | custom-call | bytes 67108864 | tf_op jit(solution)/shard_map/pallas_call | solution.py:33
  62.0 0.0 copy-start
  62.0 1.4 collective-permute-done.refs_4_.refs_1_
  63.4 0.0 collective-permute-done.5.refs_0_
  63.4 0.0 collective-permute-done.7.refs_1_
  63.4 0.1 shard_map.67
  63.6 1.3 collective-permute-start.14
  64.9 0.7 collective-permute-start.15
  65.6 1.6 collective-permute-start.10
  67.2 1.2 shard_map.68
  68.4 0.6 collective-permute-start.13
  69.0 9.6 %shard_map.69 = (bf16[80,3584]{1,0:T(8,128)(2,1)S(1)}, bf16[80,3584]{1,0:T(8,128)(2,1)S(1)}) custom-call(bf16[80,3712]{1,0:T(8,128)(2,1)S(1)} %copy-done, bf16[80,3712]{1,0:T(8,128)(2,1)S(1)} %collective-permute-done.refs_4_.refs_1_, bf16[3584,512]{1,0:T(8,128)(2,1)} %bitcast.7, bf16[3584,512]{1,0:T(8,128)(2,1)} %bitcast.12, bf16[512,3584]{1,0:T(8,128)(2,1)} %bitcast.17, ...), custom_call_target="tpu_custom_call" | custom-call | tf_op jit(solution)/shard_map/pallas_call | solution.py:33
  78.6 3.0 %collective-permute-done.10.refs_3_ = bf16[80,3584]{1,0:T(8,128)(2,1)S(1)} collective-permute-done((bf16[80,3584]{1,0:T(8,128)(2,1)S(1)}, bf16[80,3584]{1,0:T(8,128)(2,1)S(1)}, u32[]{:S(2)}, u32[]{:S(2)}) %collective-permute-start.10) | collective-permute-done | bytes 573472 | tf_op jit(solution)/shard_map/ppermute | solution.py:257
  81.6 0.6 shard_map.70.refs_4_
  82.2 0.7 collective-permute-start.11
  82.9 5.2 %collective-permute-start.12 = (bf16[128,3584]{1,0:T(8,128)(2,1)S(1)}, bf16[128,3584]{1,0:T(8,128)(2,1)S(1)}, u32[]{:S(2)}, u32[]{:S(2)}) collective-permute-start(bf16[128,3584]{1,0:T(8,128)(2,1)S(1)} %shard_map.70.refs_4_), channel_id=1, source_target_pairs={{0,4},{2,6},{4,8},{6,10},{1,5},{3,7},{5,9},{7,11},{16,20},{18,22},... | collective-permute-start | bytes 2752520 | tf_op jit(solution)/shard_map/ppermute | solution.py:254
  88.2 0.0 collective-permute-done.14.refs_1_
  88.2 1.3 shard_map.71
  89.5 1.6 collective-permute-start.17
  91.1 3.3 %collective-permute-done.13.refs_1_ = bf16[80,3712]{1,0:T(8,128)(2,1)S(1)} collective-permute-done((bf16[80,3712]{1,0:T(8,128)(2,1)S(1)}, bf16[80,3712]{1,0:T(8,128)(2,1)S(1)}, u32[]{:S(2)}, u32[]{:S(2)}) %collective-permute-start.13) | collective-permute-done | bytes 593952 | tf_op jit(solution)/shard_map/ppermute | solution.py:257
  94.3 9.6 %shard_map.72 = (bf16[80,3584]{1,0:T(8,128)(2,1)S(1)}, bf16[80,3584]{1,0:T(8,128)(2,1)S(1)}) custom-call(bf16[80,3712]{1,0:T(8,128)(2,1)S(1)} %get-tuple-element.52.refs_0_, bf16[80,3712]{1,0:T(8,128)(2,1)S(1)} %collective-permute-done.13.refs_1_, bf16[3584,512]{1,0:T(8,128)(2,1)} %bitcast.8, bf16[3584,512]{1,0:T(8,128)(2,1)} %bitcast.13, ...), custom_call_target="tpu_custom_call" | custom-call | tf_op jit(solution)/shard_map/pallas_call | solution.py:33
  104.0 1.6 collective-permute-start.16
  105.5 1.5 collective-permute-done.17.refs_1_
  107.0 9.6 %shard_map.73 = (bf16[80,3584]{1,0:T(8,128)(2,1)S(1)}, bf16[80,3584]{1,0:T(8,128)(2,1)S(1)}) custom-call(bf16[80,3712]{1,0:T(8,128)(2,1)S(1)} %get-tuple-element.57.refs_0_, bf16[80,3712]{1,0:T(8,128)(2,1)S(1)} %collective-permute-done.17.refs_1_, bf16[3584,512]{1,0:T(8,128)(2,1)} %bitcast.9, bf16[3584,512]{1,0:T(8,128)(2,1)} %bitcast.14, ...), custom_call_target="tpu_custom_call" | custom-call | tf_op jit(solution)/shard_map/pallas_call | solution.py:33
  116.7 1.6 collective-permute-start.19
  118.3 0.0 collective-permute-done.11.refs_5_.refs_0_
  118.3 0.0 collective-permute-done.12.refs_6_.refs_1_
  118.3 0.9 collective-permute-done.16.refs_3_
  119.1 0.6 shard_map.74.refs_4_.refs_0_
  119.7 5.8 %collective-permute-start.18 = (bf16[128,3584]{1,0:T(8,128)(2,1)S(1)}, bf16[128,3584]{1,0:T(8,128)(2,1)S(1)}, u32[]{:S(2)}, u32[]{:S(2)}) collective-permute-start(bf16[128,3584]{1,0:T(8,128)(2,1)S(1)} %shard_map.74.refs_4_.refs_0_), channel_id=1, source_target_pairs={{0,8},{2,10},{12,4},{14,6},{1,9},{3,11},{13,5},{15,7},{16,24},{18,... | collective-permute-start | bytes 2752520 | tf_op jit(solution)/shard_map/ppermute | solution.py:254
  125.5 3.5 %collective-permute-done.19.refs_3_ = bf16[80,3584]{1,0:T(8,128)(2,1)S(1)} collective-permute-done((bf16[80,3584]{1,0:T(8,128)(2,1)S(1)}, bf16[80,3584]{1,0:T(8,128)(2,1)S(1)}, u32[]{:S(2)}, u32[]{:S(2)}) %collective-permute-start.19) | collective-permute-done | bytes 573472 | tf_op jit(solution)/shard_map/ppermute | solution.py:257
  129.1 0.6 shard_map.75
  129.7 4.4 %collective-permute-start.21 = (bf16[128,1792]{1,0:T(8,128)(2,1)S(1)}, bf16[128,1792]{1,0:T(8,128)(2,1)S(1)}, u32[]{:S(2)}, u32[]{:S(2)}) collective-permute-start(bf16[128,1792]{1,0:T(8,128)(2,1)S(1)} %get-tuple-element.64), channel_id=1, source_target_pairs={{0,4},{2,6},{12,8},{14,10},{1,5},{3,7},{13,9},{15,11},{16,20},{18,... | collective-permute-start | bytes 1376264 | tf_op jit(solution)/shard_map/ppermute | solution.py:254
  134.1 1.3 collective-permute-start.20
  135.4 1.3 collective-permute-start.22
  136.7 1.6 collective-permute-start.9
  138.3 7.9 %collective-permute-done.18.refs_2_ = bf16[128,3584]{1,0:T(8,128)(2,1)S(1)} collective-permute-done((bf16[128,3584]{1,0:T(8,128)(2,1)S(1)}, bf16[128,3584]{1,0:T(8,128)(2,1)S(1)}, u32[]{:S(2)}, u32[]{:S(2)}) %collective-permute-start.18) | collective-permute-done | bytes 917536 | tf_op jit(solution)/shard_map/ppermute | solution.py:254
  146.3 0.3 shard_map.76.refs_2_.refs_4_
  146.6 7.5 %collective-permute-done.21.refs_1_ = bf16[128,1792]{1,0:T(8,128)(2,1)S(1)} collective-permute-done((bf16[128,1792]{1,0:T(8,128)(2,1)S(1)}, bf16[128,1792]{1,0:T(8,128)(2,1)S(1)}, u32[]{:S(2)}, u32[]{:S(2)}) %collective-permute-start.21) | collective-permute-done | bytes 458784 | tf_op jit(solution)/shard_map/ppermute | solution.py:254
  154.1 0.1 shard_map.77.refs_2_
  154.2 1.3 collective-permute-start.23
  155.5 3.5 %collective-permute-done.20.refs_1_ = bf16[128,1792]{1,0:T(8,128)(2,1)S(1)} collective-permute-done((bf16[128,1792]{1,0:T(8,128)(2,1)S(1)}, bf16[128,1792]{1,0:T(8,128)(2,1)S(1)}, u32[]{:S(2)}, u32[]{:S(2)}) %collective-permute-start.20) | collective-permute-done | bytes 458784 | tf_op jit(solution)/shard_map/ppermute | solution.py:254
  159.0 0.1 shard_map.78.refs_5_
  159.1 1.3 collective-permute-start.24
  160.4 0.6 shard_map.79.refs_0_
  161.1 6.6 %collective-permute-done.23.refs_2_ = bf16[128,1792]{1,0:T(8,128)(2,1)S(1)} collective-permute-done((bf16[128,1792]{1,0:T(8,128)(2,1)S(1)}, bf16[128,1792]{1,0:T(8,128)(2,1)S(1)}, u32[]{:S(2)}, u32[]{:S(2)}) %collective-permute-start.23) | collective-permute-done | bytes 458784 | tf_op jit(solution)/shard_map/ppermute | solution.py:254
  167.6 7.6 %collective-permute-done.22.refs_1_ = bf16[128,3584]{1,0:T(8,128)(2,1)S(1)} collective-permute-done((bf16[128,3584]{1,0:T(8,128)(2,1)S(1)}, bf16[128,3584]{1,0:T(8,128)(2,1)S(1)}, u32[]{:S(2)}, u32[]{:S(2)}) %collective-permute-start.22) | collective-permute-done | bytes 917536 | tf_op jit(solution)/shard_map/ppermute | solution.py:254
  175.3 0.2 shard_map.80.refs_2_
  175.4 1.1 shard_map.81
  (8 shorter events, 0.0 us)
Async XLA Ops:
  0.0 34.9 %collective-permute-start.1 = (bf16[3584,512]{1,0:T(8,128)(2,1)}, bf16[3584,512]{1,0:T(8,128)(2,1)S(1)}, u32[]{:S(2)}, u32[]{:S(2)}) collective-permute-start(bf16[3584,512]{1,0:T(8,128)(2,1)} %bitcast.5), channel_id=1, source_target_pairs={{0,1},{1,0},{2,3},{3,2},{4,5},{5,4},{6,7},{7,6},{8,9},{9,8},{10,11... | collective-permute-start | bytes 11010056 | tf_op jit(solution)/shard_map/ppermute | solution.py:250
  0.5 37.0 %collective-permute-start.2 = (bf16[3584,512]{1,0:T(8,128)(2,1)}, bf16[3584,512]{1,0:T(8,128)(2,1)S(1)}, u32[]{:S(2)}, u32[]{:S(2)}) collective-permute-start(bf16[3584,512]{1,0:T(8,128)(2,1)} %bitcast.10), channel_id=1, source_target_pairs={{0,1},{1,0},{2,3},{3,2},{4,5},{5,4},{6,7},{7,6},{8,9},{9,8},{10,11... | collective-permute-start | bytes 11010056 | tf_op jit(solution)/shard_map/ppermute | solution.py:250
  0.5 37.5 %collective-permute-start.3 = (bf16[512,3584]{1,0:T(8,128)(2,1)}, bf16[512,3584]{1,0:T(8,128)(2,1)S(1)}, u32[]{:S(2)}, u32[]{:S(2)}) collective-permute-start(bf16[512,3584]{1,0:T(8,128)(2,1)} %bitcast.15), channel_id=1, source_target_pairs={{0,1},{1,0},{2,3},{3,2},{4,5},{5,4},{6,7},{7,6},{8,9},{9,8},{10,11... | collective-permute-start | bytes 11010056 | tf_op jit(solution)/shard_map/ppermute | solution.py:250
  3.8 33.7 %copy-start.1 = (bf16[80,3712]{1,0:T(8,128)(2,1)S(1)}, bf16[80,3712]{1,0:T(8,128)(2,1)}, u32[]{:S(2)}) copy-start(bf16[80,3712]{1,0:T(8,128)(2,1)} %get-tuple-element.38) | copy-start | bytes 1781764
  3.8 25.6 %collective-permute-start.4 = (bf16[128,3712]{1,0:T(8,128)(2,1)S(1)}, bf16[128,3712]{1,0:T(8,128)(2,1)S(1)}, u32[]{:S(2)}, u32[]{:S(2)}) collective-permute-start(bf16[128,3712]{1,0:T(8,128)(2,1)S(1)} %get-tuple-element.39), channel_id=1, source_target_pairs={{0,4},{2,6},{4,8},{6,10},{8,12},{10,14},{1,5},{3,7},{5,9},{7,11},{... | collective-permute-start | bytes 2850824 | tf_op jit(solution)/shard_map/ppermute | solution.py:254
  8.5 25.1 %collective-permute-start.6 = (bf16[128,3712]{1,0:T(8,128)(2,1)S(1)}, bf16[128,3712]{1,0:T(8,128)(2,1)S(1)}, u32[]{:S(2)}, u32[]{:S(2)}) collective-permute-start(bf16[128,3712]{1,0:T(8,128)(2,1)S(1)} %get-tuple-element.39), channel_id=1, source_target_pairs={{4,0},{6,2},{8,4},{10,6},{12,8},{14,10},{5,1},{7,3},{9,5},{11,7},{... | collective-permute-start | bytes 2850824 | tf_op jit(solution)/shard_map/ppermute | solution.py:254
  29.4 34.0 %collective-permute-start.5 = (bf16[128,3712]{1,0:T(8,128)(2,1)S(1)}, bf16[128,3712]{1,0:T(8,128)(2,1)S(1)}, u32[]{:S(2)}, u32[]{:S(2)}) collective-permute-start(bf16[128,3712]{1,0:T(8,128)(2,1)S(1)} %collective-permute-done.4.refs_1_.refs_2_), channel_id=1, source_target_pairs={{4,8},{6,10},{8,12},{10,14},{5,9},{7,11},{9,13},{11,15},{20,24},{2... | collective-permute-start | bytes 2850824 | tf_op jit(solution)/shard_map/ppermute | solution.py:254
  33.6 29.9 %collective-permute-start.7 = (bf16[128,3712]{1,0:T(8,128)(2,1)S(1)}, bf16[128,3712]{1,0:T(8,128)(2,1)S(1)}, u32[]{:S(2)}, u32[]{:S(2)}) collective-permute-start(bf16[128,3712]{1,0:T(8,128)(2,1)S(1)} %collective-permute-done.6.refs_0_), channel_id=1, source_target_pairs={{4,0},{6,2},{8,4},{10,6},{5,1},{7,3},{9,5},{11,7},{20,16},{22,18},... | collective-permute-start | bytes 2850824 | tf_op jit(solution)/shard_map/ppermute | solution.py:254
  35.9 16.4 %collective-permute-start.8 = (bf16[80,3712]{1,0:T(8,128)(2,1)S(1)}, bf16[80,3712]{1,0:T(8,128)(2,1)S(1)}, u32[]{:S(2)}, u32[]{:S(2)}) collective-permute-start(bf16[80,3712]{1,0:T(8,128)(2,1)S(1)} %get-tuple-element.41), channel_id=1, source_target_pairs={{0,2},{2,0},{4,6},{6,4},{8,10},{10,8},{12,14},{14,12},{1,3},{3,1},... | collective-permute-start | bytes 1781768 | tf_op jit(solution)/shard_map/ppermute | solution.py:257
  37.5 25.9 %collective-permute-start = (bf16[80,3712]{1,0:T(8,128)(2,1)S(1)}, bf16[80,3712]{1,0:T(8,128)(2,1)S(1)}, u32[]{:S(2)}, u32[]{:S(2)}) collective-permute-start(bf16[80,3712]{1,0:T(8,128)(2,1)S(1)} %copy-done.1), channel_id=1, source_target_pairs={{0,2},{2,0},{4,6},{6,4},{8,10},{10,8},{12,14},{14,12},{1,3},{3,1},... | collective-permute-start | bytes 1781768 | tf_op jit(solution)/shard_map/ppermute | solution.py:257
  62.0 7.0 %copy-start = (bf16[80,3712]{1,0:T(8,128)(2,1)S(1)}, bf16[80,3712]{1,0:T(8,128)(2,1)}, u32[]{:S(2)}) copy-start(bf16[80,3712]{1,0:T(8,128)(2,1)} %get-tuple-element.37.refs_0_) | copy-start | bytes 1781764
  63.6 24.6 %collective-permute-start.14 = (bf16[128,3712]{1,0:T(8,128)(2,1)S(1)}, bf16[128,3712]{1,0:T(8,128)(2,1)S(1)}, u32[]{:S(2)}, u32[]{:S(2)}) collective-permute-start(bf16[128,3712]{1,0:T(8,128)(2,1)S(1)} %get-tuple-element.44.refs_0_), channel_id=1, source_target_pairs={{4,0},{6,2},{5,1},{7,3},{20,16},{22,18},{21,17},{23,19}} | collective-permute-start | bytes 2850824 | tf_op jit(solution)/shard_map/ppermute | solution.py:254
  64.9 23.3 %collective-permute-start.15 = (bf16[128,3712]{1,0:T(8,128)(2,1)S(1)}, bf16[128,3712]{1,0:T(8,128)(2,1)S(1)}, u32[]{:S(2)}, u32[]{:S(2)}) collective-permute-start(bf16[128,3712]{1,0:T(8,128)(2,1)S(1)} %get-tuple-element.45.refs_1_), channel_id=1, source_target_pairs={{8,12},{10,14},{9,13},{11,15},{24,28},{26,30},{25,29},{27,31}} | collective-permute-start | bytes 2850824 | tf_op jit(solution)/shard_map/ppermute | solution.py:254
  65.6 16.0 %collective-permute-start.10 = (bf16[80,3584]{1,0:T(8,128)(2,1)S(1)}, bf16[80,3584]{1,0:T(8,128)(2,1)S(1)}, u32[]{:S(2)}, u32[]{:S(2)}) collective-permute-start(bf16[80,3584]{1,0:T(8,128)(2,1)S(1)} %get-tuple-element.50), channel_id=1, source_target_pairs={{0,2},{2,0},{4,6},{6,4},{8,10},{10,8},{12,14},{14,12},{1,3},{3,1},... | collective-permute-start | bytes 1720328 | tf_op jit(solution)/shard_map/ppermute | solution.py:257
  68.4 25.9 %collective-permute-start.13 = (bf16[80,3712]{1,0:T(8,128)(2,1)S(1)}, bf16[80,3712]{1,0:T(8,128)(2,1)S(1)}, u32[]{:S(2)}, u32[]{:S(2)}) collective-permute-start(bf16[80,3712]{1,0:T(8,128)(2,1)S(1)} %get-tuple-element.53), channel_id=1, source_target_pairs={{0,2},{2,0},{4,6},{6,4},{8,10},{10,8},{12,14},{14,12},{1,3},{3,1},... | collective-permute-start | bytes 1781768 | tf_op jit(solution)/shard_map/ppermute | solution.py:257
  82.2 36.1 %collective-permute-start.11 = (bf16[128,3584]{1,0:T(8,128)(2,1)S(1)}, bf16[128,3584]{1,0:T(8,128)(2,1)S(1)}, u32[]{:S(2)}, u32[]{:S(2)}) collective-permute-start(bf16[128,3584]{1,0:T(8,128)(2,1)S(1)} %shard_map.70.refs_4_), channel_id=1, source_target_pairs={{8,4},{10,6},{12,8},{14,10},{9,5},{11,7},{13,9},{15,11},{24,20},{2... | collective-permute-start | bytes 2752520 | tf_op jit(solution)/shard_map/ppermute | solution.py:254
  82.9 35.3 %collective-permute-start.12 = (bf16[128,3584]{1,0:T(8,128)(2,1)S(1)}, bf16[128,3584]{1,0:T(8,128)(2,1)S(1)}, u32[]{:S(2)}, u32[]{:S(2)}) collective-permute-start(bf16[128,3584]{1,0:T(8,128)(2,1)S(1)} %shard_map.70.refs_4_), channel_id=1, source_target_pairs={{0,4},{2,6},{4,8},{6,10},{1,5},{3,7},{5,9},{7,11},{16,20},{18,22},... | collective-permute-start | bytes 2752520 | tf_op jit(solution)/shard_map/ppermute | solution.py:254
  89.5 17.6 %collective-permute-start.17 = (bf16[80,3712]{1,0:T(8,128)(2,1)S(1)}, bf16[80,3712]{1,0:T(8,128)(2,1)S(1)}, u32[]{:S(2)}, u32[]{:S(2)}) collective-permute-start(bf16[80,3712]{1,0:T(8,128)(2,1)S(1)} %get-tuple-element.58), channel_id=1, source_target_pairs={{0,2},{2,0},{4,6},{6,4},{8,10},{10,8},{12,14},{14,12},{1,3},{3,1},... | collective-permute-start | bytes 1781768 | tf_op jit(solution)/shard_map/ppermute | solution.py:257
  104.0 15.2 %collective-permute-start.16 = (bf16[80,3584]{1,0:T(8,128)(2,1)S(1)}, bf16[80,3584]{1,0:T(8,128)(2,1)S(1)}, u32[]{:S(2)}, u32[]{:S(2)}) collective-permute-start(bf16[80,3584]{1,0:T(8,128)(2,1)S(1)} %get-tuple-element.56), channel_id=1, source_target_pairs={{0,2},{2,0},{4,6},{6,4},{8,10},{10,8},{12,14},{14,12},{1,3},{3,1},... | collective-permute-start | bytes 1720328 | tf_op jit(solution)/shard_map/ppermute | solution.py:257
  116.7 12.4 %collective-permute-start.19 = (bf16[80,3584]{1,0:T(8,128)(2,1)S(1)}, bf16[80,3584]{1,0:T(8,128)(2,1)S(1)}, u32[]{:S(2)}, u32[]{:S(2)}) collective-permute-start(bf16[80,3584]{1,0:T(8,128)(2,1)S(1)} %get-tuple-element.61), channel_id=1, source_target_pairs={{0,2},{2,0},{4,6},{6,4},{8,10},{10,8},{12,14},{14,12},{1,3},{3,1},... | collective-permute-start | bytes 1720328 | tf_op jit(solution)/shard_map/ppermute | solution.py:257
  119.7 26.5 %collective-permute-start.18 = (bf16[128,3584]{1,0:T(8,128)(2,1)S(1)}, bf16[128,3584]{1,0:T(8,128)(2,1)S(1)}, u32[]{:S(2)}, u32[]{:S(2)}) collective-permute-start(bf16[128,3584]{1,0:T(8,128)(2,1)S(1)} %shard_map.74.refs_4_.refs_0_), channel_id=1, source_target_pairs={{0,8},{2,10},{12,4},{14,6},{1,9},{3,11},{13,5},{15,7},{16,24},{18,... | collective-permute-start | bytes 2752520 | tf_op jit(solution)/shard_map/ppermute | solution.py:254
  129.7 24.4 %collective-permute-start.21 = (bf16[128,1792]{1,0:T(8,128)(2,1)S(1)}, bf16[128,1792]{1,0:T(8,128)(2,1)S(1)}, u32[]{:S(2)}, u32[]{:S(2)}) collective-permute-start(bf16[128,1792]{1,0:T(8,128)(2,1)S(1)} %get-tuple-element.64), channel_id=1, source_target_pairs={{0,4},{2,6},{12,8},{14,10},{1,5},{3,7},{13,9},{15,11},{16,20},{18,... | collective-permute-start | bytes 1376264 | tf_op jit(solution)/shard_map/ppermute | solution.py:254
  134.1 24.9 %collective-permute-start.20 = (bf16[128,1792]{1,0:T(8,128)(2,1)S(1)}, bf16[128,1792]{1,0:T(8,128)(2,1)S(1)}, u32[]{:S(2)}, u32[]{:S(2)}) collective-permute-start(bf16[128,1792]{1,0:T(8,128)(2,1)S(1)} %get-tuple-element.63), channel_id=1, source_target_pairs={{0,4},{2,6},{12,8},{14,10},{1,5},{3,7},{13,9},{15,11},{16,20},{18,... | collective-permute-start | bytes 1376264 | tf_op jit(solution)/shard_map/ppermute | solution.py:254
  135.4 39.8 %collective-permute-start.22 = (bf16[128,3584]{1,0:T(8,128)(2,1)S(1)}, bf16[128,3584]{1,0:T(8,128)(2,1)S(1)}, u32[]{:S(2)}, u32[]{:S(2)}) collective-permute-start(bf16[128,3584]{1,0:T(8,128)(2,1)S(1)} %get-tuple-element.62.refs_3_), channel_id=1, source_target_pairs={{4,0},{6,2},{8,12},{10,14},{5,1},{7,3},{9,13},{11,15},{20,16},{22,... | collective-permute-start | bytes 2752520 | tf_op jit(solution)/shard_map/ppermute | solution.py:254
  136.7 23.7 %collective-permute-start.9 = (bf16[80,3584]{1,0:T(8,128)(2,1)S(1)}, bf16[80,3584]{1,0:T(8,128)(2,1)S(1)}, u32[]{:S(2)}, u32[]{:S(2)}) collective-permute-start(bf16[80,3584]{1,0:T(8,128)(2,1)S(1)} %get-tuple-element.48), channel_id=1, source_target_pairs={{0,2},{2,0},{4,6},{6,4},{8,10},{10,8},{12,14},{14,12},{1,3},{3,1},... | collective-permute-start | bytes 1720328 | tf_op jit(solution)/shard_map/ppermute | solution.py:257
  154.2 13.4 %collective-permute-start.23 = (bf16[128,1792]{1,0:T(8,128)(2,1)S(1)}, bf16[128,1792]{1,0:T(8,128)(2,1)S(1)}, u32[]{:S(2)}, u32[]{:S(2)}) collective-permute-start(bf16[128,1792]{1,0:T(8,128)(2,1)S(1)} %shard_map.77.refs_2_), channel_id=1, source_target_pairs={{4,12},{6,14},{8,0},{10,2},{5,13},{7,15},{9,1},{11,3},{20,28},{22,... | collective-permute-start | bytes 1376264 | tf_op jit(solution)/shard_map/ppermute | solution.py:254
  159.1 16.3 %collective-permute-start.24 = (bf16[128,1792]{1,0:T(8,128)(2,1)S(1)}, bf16[128,1792]{1,0:T(8,128)(2,1)S(1)}, u32[]{:S(2)}, u32[]{:S(2)}) collective-permute-start(bf16[128,1792]{1,0:T(8,128)(2,1)S(1)} %shard_map.78.refs_5_), channel_id=1, source_target_pairs={{4,12},{6,14},{8,0},{10,2},{5,13},{7,15},{9,1},{11,3},{20,28},{22,... | collective-permute-start | bytes 1376264 | tf_op jit(solution)/shard_map/ppermute | solution.py:254

commit v16 on v14

--- a/solution.py
+++ b/solution.py
@@ -56,8 +56,7 @@
     )(*[in_vmem(a) for a in arrays], *after)
 
 
-def first_kernel(experts, tokens, routes, scale, block, *refs):
-    picked, (route_held, scale_held, sems) = refs[:4], refs[4:]
+def mark_kernel(experts, tokens, routes, scale, block, route_held, scale_held, sems):
     count, width = tokens.shape
     ins = [
         pltpu.make_async_copy(routes, route_held, sems.at[0]),
@@ -80,7 +79,6 @@
     marks = jnp.where(part == 0, high, jnp.where(part == 1, middle, jnp.where(part == 2, low, 0.0)))
     block[:, width:] = marks.astype(jnp.bfloat16)
     ins[2].wait()
-    choose(block, *picked)
 
 
 def passing_kernel(*refs):
@@ -234,9 +232,9 @@
     bf16 = functools.partial(jax.ShapeDtypeStruct, dtype=jnp.bfloat16)
 
     own = (w_gate[0], w_up[0], w_down[0])
-    block, *picked = call(
-        functools.partial(first_kernel, experts),
-        [bf16((count, wide)), bf16((count, cap)), bf16((count, cap)), hbm((cap, wide)), hbm((cap, wide))],
+    (block,) = call(
+        functools.partial(mark_kernel, experts),
+        [bf16((count, wide))],
         [*map(in_hbm, (tokens, routes.T, route_scale.T))],
         (),
         [
@@ -257,9 +255,10 @@
         return lax.ppermute(block, "node", [(n, n ^ 1) for n in range(experts)])
 
     def pick(blocks, users, after=(), cost=0):
+        rows = hbm if len(blocks) == 1 else bf16
         return call(
             functools.partial(pick_kernel, users),
-            [bf16((count, cap)), bf16((count, cap)), bf16((cap, wide)), bf16((cap, wide))],
+            [bf16((count, cap)), bf16((count, cap)), rows((cap, wide)), rows((cap, wide))],
             blocks,
             after,
             [pltpu.VMEM((count, wide), jnp.bfloat16), pltpu.SemaphoreType.DMA],
@@ -313,6 +312,10 @@
             held[way, step] = along(held.get((way, step - 1), block), pairs)
 
     def do_pick(slot, after=(), cost=0):
+        if slot == 0:
+            *maps, own_rows, other_rows = ordered(pick, [block], [range(places)], after=after)
+            picks[0] = maps, own_rows, across(other_rows)
+            return
         keys = sorted({row[slot - 1] for row in plan})
         blocks = [held[key] for key in keys]
         users = [[place for place, row in enumerate(plan) if row[slot - 1] == key] for key in keys]
@@ -340,11 +343,11 @@
         outs = [bf16((count, width)), bf16((count, width // 2)), bf16((count, width // 2))]
         return call(halves_kernel, outs, [*maps, own_out, other_out], after)
 
-    def do_spread(slot, after=()):
+    def do_spread(slot, after=(), cost=0):
         if slot == places - 1:
             done, *halves[:] = ordered(spread_halves, picks[slot][0], *outs[slot], after=after)
         else:
-            done = ordered(spread, picks[slot][0], *outs[slot], after=after)
+            done = ordered(spread, picks[slot][0], *outs[slot], after=after, cost=cost)
         kept[slot] = done
         home = [(a, origin(a, slot)) for a in range(places) if a not in staying.get(slot, ())]
         rounds = []
@@ -370,6 +373,7 @@
     relay(1)
     relay(2)
     do_pick(1, after=weights[3:4])
+    do_pick(0)
     do_expert(1, cost=64 * MIB)
     held[1, 2], held[-1, 2] = call(
         passing_kernel, [bf16((count, wide))] * 2, [held[1, 2], held[-1, 2]], [*last, picks[1][2]]
@@ -377,7 +381,7 @@
     for step in range(3, places):
         relay(step)
     do_pick(2)
-    do_spread(1)
+    do_spread(1, cost=64 * MIB)
     do_pick(3)
     do_expert(2)
     for slot in range(3, places):
@@ -385,7 +389,6 @@
         do_spread(slot - 1, after=returned[slot - 3])
         if slot + 1 < places:
             do_pick(slot + 1)
-    picks[0] = picked[:2], picked[2], across(picked[3])
     do_spread(places - 1)
     do_expert(0)
     near = returned.pop(places - 3)

time: 174 us -> 172 us (0.989)
  waiting for transfers between devices: 79.7 us -> 77.8 us
    ppermute x8, waiting for transfers between devices: 40.6 us -> 38.7 us  [across(): return lax.ppermute(block, 'node', [(n, n ^ 1) for n in range(experts)])]
    pallas_call x18 -> x19, Pallas kernels: 49.1 us -> 49.4 us  [call(): pl.pallas_call(body, out_shape=outs, in_specs=specs, out_specs=out_specs...]
where the time goes in v16:
time: 172 us
  waiting for transfers between devices  77.8 us (45%)
  Pallas kernels  49.4 us (29%)
  starting transfers between devices  44.2 us (26%)
    pallas_call x19, Pallas kernels, call(): pl.pallas_call(body, out_shape=outs, in_specs=specs, out_specs=out_specs...  49.4 us
    ppermute x14, waiting for transfers between devices, along(): return lax.ppermute(block, 'node', moves)  39 us
    ppermute x8, waiting for transfers between devices, across(): return lax.ppermute(block, 'node', [(n, n ^ 1) for n in range(experts)])  38.7 us
    ppermute x14, starting transfers between devices, along(): return lax.ppermute(block, 'node', moves)  31.6 us
    ppermute x8, starting transfers between devices, across(): return lax.ppermute(block, 'node', [(n, n ^ 1) for n in range(experts)])  11.7 us
  transfers between devices with their start and end apart: 25, of which 14 were waited for; matrix products, arithmetic and copies ran while one was open for 0% of the time, Pallas kernels for 28%

profile of v16, /device:TPU:0, one launch (start us, length us, event | category | flops | bytes accessed | tf_op | source)
XLA Modules:
  0.0 171.8 jit_solution(17022239557035424985)
XLA Ops:
  0.0 0.5 collective-permute-start.2
  0.5 0.1 collective-permute-start.4
  0.5 0.5 collective-permute-start.5
  1.0 1.2 shard_map.64.refs_0_
  2.2 4.5 %collective-permute-start.1 = (bf16[128,3712]{1,0:T(8,128)(2,1)S(1)}, bf16[128,3712]{1,0:T(8,128)(2,1)S(1)}, u32[]{:S(2)}, u32[]{:S(2)}) collective-permute-start(bf16[128,3712]{1,0:T(8,128)(2,1)S(1)} %shard_map.64.refs_0_), channel_id=1, source_target_pairs={{0,4},{2,6},{4,8},{6,10},{8,12},{10,14},{1,5},{3,7},{5,9},{7,11},{... | collective-permute-start | bytes 2850824 | tf_op jit(solution)/shard_map/ppermute | solution.py:252
  6.8 1.3 collective-permute-start
  8.1 19.6 %collective-permute-done.1.refs_1_.refs_2_ = bf16[128,3712]{1,0:T(8,128)(2,1)S(1)} collective-permute-done((bf16[128,3712]{1,0:T(8,128)(2,1)S(1)}, bf16[128,3712]{1,0:T(8,128)(2,1)S(1)}, u32[]{:S(2)}, u32[]{:S(2)}) %collective-permute-start.1) | collective-permute-done | bytes 950304 | tf_op jit(solution)/shard_map/ppermute | solution.py:252
  27.7 0.7 collective-permute-start.6
  28.4 3.5 %collective-permute-done.refs_0_ = bf16[128,3712]{1,0:T(8,128)(2,1)S(1)} collective-permute-done((bf16[128,3712]{1,0:T(8,128)(2,1)S(1)}, bf16[128,3712]{1,0:T(8,128)(2,1)S(1)}, u32[]{:S(2)}, u32[]{:S(2)}) %collective-permute-start) | collective-permute-done | bytes 950304 | tf_op jit(solution)/shard_map/ppermute | solution.py:252
  31.8 1.3 collective-permute-start.7
  33.1 1.0 shard_map.65
  34.2 1.6 collective-permute-start.8
  35.8 1.9 %shard_map.66 = (bf16[128,80]{1,0:T(8,128)(2,1)S(1)}, bf16[128,80]{1,0:T(8,128)(2,1)S(1)}, bf16[80,3712]{1,0:T(8,128)(2,1)}, bf16[80,3712]{1,0:T(8,128)(2,1)}) custom-call(bf16[128,3712]{1,0:T(8,128)(2,1)S(1)} %shard_map.64.refs_0_, bf16[128,80]{1,0:T(8,128)(2,1)S(1)} %get-tuple-element.34.refs_1_.refs_0_), custom_call_target="tpu_custom_call" | custom-call | tf_op jit(solution)/shard_map/pallas_call | solution.py:33
  37.7 11.3 %collective-permute-done.8.refs_1_.refs_3_ = bf16[80,3712]{1,0:T(8,128)(2,1)S(1)} collective-permute-done((bf16[80,3712]{1,0:T(8,128)(2,1)S(1)}, bf16[80,3712]{1,0:T(8,128)(2,1)S(1)}, u32[]{:S(2)}, u32[]{:S(2)}) %collective-permute-start.8) | collective-permute-done | bytes 593952 | tf_op jit(solution)/shard_map/ppermute | solution.py:255
  49.0 9.6 %shard_map.67 = (bf16[80,3584]{1,0:T(8,128)(2,1)S(1)}, bf16[80,3584]{1,0:T(8,128)(2,1)S(1)}) custom-call(bf16[80,3712]{1,0:T(8,128)(2,1)S(1)} %get-tuple-element.39.refs_0_, bf16[80,3712]{1,0:T(8,128)(2,1)S(1)} %collective-permute-done.8.refs_1_.refs_3_, bf16[3584,512]{1,0:T(8,128)(2,1)} %bitcast.6, bf16[3584,512]{1,0:T(8,128)(2,1)} %bitcast.11, ...), custom_call_target="tpu_custom_call" | custom-call | bytes 67108864 | tf_op jit(solution)/shard_map/pallas_call | solution.py:33
  58.6 0.0 collective-permute-done.6.refs_0_
  58.6 0.0 collective-permute-done.7.refs_1_
  58.6 0.1 shard_map.68
  58.8 0.7 collective-permute-start.10
  59.5 1.3 collective-permute-start.9
  60.8 1.6 collective-permute-start.11
  62.4 1.0 shard_map.69
  63.4 0.6 collective-permute-start.13
  64.0 12.8 %collective-permute-done.11.refs_3_ = bf16[80,3584]{1,0:T(8,128)(2,1)S(1)} collective-permute-done((bf16[80,3584]{1,0:T(8,128)(2,1)S(1)}, bf16[80,3584]{1,0:T(8,128)(2,1)S(1)}, u32[]{:S(2)}, u32[]{:S(2)}) %collective-permute-start.11) | collective-permute-done | bytes 573472 | tf_op jit(solution)/shard_map/ppermute | solution.py:255
  76.8 0.6 shard_map.70.refs_4_
  77.4 0.7 collective-permute-start.16
  78.1 5.2 %collective-permute-start.17 = (bf16[128,3584]{1,0:T(8,128)(2,1)S(1)}, bf16[128,3584]{1,0:T(8,128)(2,1)S(1)}, u32[]{:S(2)}, u32[]{:S(2)}) collective-permute-start(bf16[128,3584]{1,0:T(8,128)(2,1)S(1)} %shard_map.70.refs_4_), channel_id=1, source_target_pairs={{0,4},{2,6},{4,8},{6,10},{1,5},{3,7},{5,9},{7,11},{16,20},{18,22},... | collective-permute-start | bytes 2752520 | tf_op jit(solution)/shard_map/ppermute | solution.py:252
  83.4 0.0 collective-permute-done.9.refs_1_
  83.4 1.2 shard_map.71
  84.6 1.6 collective-permute-start.12
  86.2 3.3 %collective-permute-done.13.refs_1_ = bf16[80,3712]{1,0:T(8,128)(2,1)S(1)} collective-permute-done((bf16[80,3712]{1,0:T(8,128)(2,1)S(1)}, bf16[80,3712]{1,0:T(8,128)(2,1)S(1)}, u32[]{:S(2)}, u32[]{:S(2)}) %collective-permute-start.13) | collective-permute-done | bytes 593952 | tf_op jit(solution)/shard_map/ppermute | solution.py:255
  89.5 9.6 %shard_map.72 = (bf16[80,3584]{1,0:T(8,128)(2,1)S(1)}, bf16[80,3584]{1,0:T(8,128)(2,1)S(1)}) custom-call(bf16[80,3712]{1,0:T(8,128)(2,1)S(1)} %get-tuple-element.51.refs_0_, bf16[80,3712]{1,0:T(8,128)(2,1)S(1)} %collective-permute-done.13.refs_1_, bf16[3584,512]{1,0:T(8,128)(2,1)} %bitcast.7, bf16[3584,512]{1,0:T(8,128)(2,1)} %bitcast.12, ...), custom_call_target="tpu_custom_call" | custom-call | tf_op jit(solution)/shard_map/pallas_call | solution.py:33
  99.2 1.6 collective-permute-start.15
  100.7 1.5 collective-permute-done.12.refs_1_
  102.2 9.6 %shard_map.73 = (bf16[80,3584]{1,0:T(8,128)(2,1)S(1)}, bf16[80,3584]{1,0:T(8,128)(2,1)S(1)}) custom-call(bf16[80,3712]{1,0:T(8,128)(2,1)S(1)} %get-tuple-element.49.refs_0_, bf16[80,3712]{1,0:T(8,128)(2,1)S(1)} %collective-permute-done.12.refs_1_, bf16[3584,512]{1,0:T(8,128)(2,1)} %bitcast.8, bf16[3584,512]{1,0:T(8,128)(2,1)} %bitcast.13, ...), custom_call_target="tpu_custom_call" | custom-call | tf_op jit(solution)/shard_map/pallas_call | solution.py:33
  111.9 0.0 copy-start
  111.9 1.6 collective-permute-start.14
  113.5 0.0 collective-permute-done.16.refs_5_.refs_0_
  113.5 0.0 collective-permute-done.17.refs_6_.refs_1_
  113.5 0.8 collective-permute-done.15.refs_3_
  114.3 0.6 shard_map.74.refs_4_.refs_0_
  114.9 5.8 %collective-permute-start.19 = (bf16[128,3584]{1,0:T(8,128)(2,1)S(1)}, bf16[128,3584]{1,0:T(8,128)(2,1)S(1)}, u32[]{:S(2)}, u32[]{:S(2)}) collective-permute-start(bf16[128,3584]{1,0:T(8,128)(2,1)S(1)} %shard_map.74.refs_4_.refs_0_), channel_id=1, source_target_pairs={{0,8},{2,10},{12,4},{14,6},{1,9},{3,11},{13,5},{15,7},{16,24},{18,... | collective-permute-start | bytes 2752520 | tf_op jit(solution)/shard_map/ppermute | solution.py:252
  120.7 1.6 collective-permute-start.3
  122.3 5.6 %collective-permute-done.14.refs_3_ = bf16[80,3584]{1,0:T(8,128)(2,1)S(1)} collective-permute-done((bf16[80,3584]{1,0:T(8,128)(2,1)S(1)}, bf16[80,3584]{1,0:T(8,128)(2,1)S(1)}, u32[]{:S(2)}, u32[]{:S(2)}) %collective-permute-start.14) | collective-permute-done | bytes 573472 | tf_op jit(solution)/shard_map/ppermute | solution.py:255
  127.9 0.6 shard_map.75
  128.5 4.6 %collective-permute-start.21 = (bf16[128,1792]{1,0:T(8,128)(2,1)S(1)}, bf16[128,1792]{1,0:T(8,128)(2,1)S(1)}, u32[]{:S(2)}, u32[]{:S(2)}) collective-permute-start(bf16[128,1792]{1,0:T(8,128)(2,1)S(1)} %get-tuple-element.62), channel_id=1, source_target_pairs={{0,4},{2,6},{12,8},{14,10},{1,5},{3,7},{13,9},{15,11},{16,20},{18,... | collective-permute-start | bytes 1376264 | tf_op jit(solution)/shard_map/ppermute | solution.py:252
  133.1 1.3 collective-permute-start.20
  134.5 1.5 collective-permute-start.22
  136.0 1.0 collective-permute-done.3.refs_1_
  137.0 9.6 %shard_map.76 = (bf16[80,3584]{1,0:T(8,128)(2,1)S(1)}, bf16[80,3584]{1,0:T(8,128)(2,1)S(1)}) custom-call(bf16[80,3712]{1,0:T(8,128)(2,1)S(1)} %copy-done, bf16[80,3712]{1,0:T(8,128)(2,1)S(1)} %collective-permute-done.3.refs_1_, bf16[3584,512]{1,0:T(8,128)(2,1)} %bitcast.9, bf16[3584,512]{1,0:T(8,128)(2,1)} %bitcast.14, bf16[512,3584]{1,0:T(8,128)(2,1)} %bitcast.19, ...), custom_call_target="tpu_custom_call" | custom-call | tf_op jit(solution)/shard_map/pallas_call | solution.py:33
  146.6 1.6 collective-permute-start.18
  148.2 0.3 shard_map.77.refs_2_.refs_4_
  148.6 0.7 collective-permute-done.21.refs_1_
  149.3 0.1 shard_map.78.refs_2_
  149.4 1.3 collective-permute-start.23
  150.7 3.5 %collective-permute-done.20.refs_1_ = bf16[128,1792]{1,0:T(8,128)(2,1)S(1)} collective-permute-done((bf16[128,1792]{1,0:T(8,128)(2,1)S(1)}, bf16[128,1792]{1,0:T(8,128)(2,1)S(1)}, u32[]{:S(2)}, u32[]{:S(2)}) %collective-permute-start.20) | collective-permute-done | bytes 458784 | tf_op jit(solution)/shard_map/ppermute | solution.py:252
  154.2 0.1 shard_map.79.refs_5_
  154.3 1.3 collective-permute-start.24
  155.6 2.4 %collective-permute-done.18.refs_3_ = bf16[80,3584]{1,0:T(8,128)(2,1)S(1)} collective-permute-done((bf16[80,3584]{1,0:T(8,128)(2,1)S(1)}, bf16[80,3584]{1,0:T(8,128)(2,1)S(1)}, u32[]{:S(2)}, u32[]{:S(2)}) %collective-permute-start.18) | collective-permute-done | bytes 573472 | tf_op jit(solution)/shard_map/ppermute | solution.py:255
  158.1 0.6 shard_map.80.refs_0_
  158.7 6.5 %collective-permute-done.23.refs_2_ = bf16[128,1792]{1,0:T(8,128)(2,1)S(1)} collective-permute-done((bf16[128,1792]{1,0:T(8,128)(2,1)S(1)}, bf16[128,1792]{1,0:T(8,128)(2,1)S(1)}, u32[]{:S(2)}, u32[]{:S(2)}) %collective-permute-start.23) | collective-permute-done | bytes 458784 | tf_op jit(solution)/shard_map/ppermute | solution.py:252
  165.2 5.2 %collective-permute-done.22.refs_1_ = bf16[128,3584]{1,0:T(8,128)(2,1)S(1)} collective-permute-done((bf16[128,3584]{1,0:T(8,128)(2,1)S(1)}, bf16[128,3584]{1,0:T(8,128)(2,1)S(1)}, u32[]{:S(2)}, u32[]{:S(2)}) %collective-permute-start.22) | collective-permute-done | bytes 917536 | tf_op jit(solution)/shard_map/ppermute | solution.py:252
  170.4 0.2 shard_map.81.refs_2_
  170.6 1.1 shard_map.82
  (9 shorter events, 0.0 us)
Async XLA Ops:
  0.0 33.1 %collective-permute-start.2 = (bf16[3584,512]{1,0:T(8,128)(2,1)}, bf16[3584,512]{1,0:T(8,128)(2,1)S(1)}, u32[]{:S(2)}, u32[]{:S(2)}) collective-permute-start(bf16[3584,512]{1,0:T(8,128)(2,1)} %bitcast.5), channel_id=1, source_target_pairs={{0,1},{1,0},{2,3},{3,2},{4,5},{5,4},{6,7},{7,6},{8,9},{9,8},{10,11... | collective-permute-start | bytes 11010056 | tf_op jit(solution)/shard_map/ppermute | solution.py:248
  0.5 37.2 %collective-permute-start.4 = (bf16[3584,512]{1,0:T(8,128)(2,1)}, bf16[3584,512]{1,0:T(8,128)(2,1)S(1)}, u32[]{:S(2)}, u32[]{:S(2)}) collective-permute-start(bf16[3584,512]{1,0:T(8,128)(2,1)} %bitcast.10), channel_id=1, source_target_pairs={{0,1},{1,0},{2,3},{3,2},{4,5},{5,4},{6,7},{7,6},{8,9},{9,8},{10,11... | collective-permute-start | bytes 11010056 | tf_op jit(solution)/shard_map/ppermute | solution.py:248
  0.5 37.1 %collective-permute-start.5 = (bf16[512,3584]{1,0:T(8,128)(2,1)}, bf16[512,3584]{1,0:T(8,128)(2,1)S(1)}, u32[]{:S(2)}, u32[]{:S(2)}) collective-permute-start(bf16[512,3584]{1,0:T(8,128)(2,1)} %bitcast.15), channel_id=1, source_target_pairs={{0,1},{1,0},{2,3},{3,2},{4,5},{5,4},{6,7},{7,6},{8,9},{9,8},{10,11... | collective-permute-start | bytes 11010056 | tf_op jit(solution)/shard_map/ppermute | solution.py:248
  2.2 25.5 %collective-permute-start.1 = (bf16[128,3712]{1,0:T(8,128)(2,1)S(1)}, bf16[128,3712]{1,0:T(8,128)(2,1)S(1)}, u32[]{:S(2)}, u32[]{:S(2)}) collective-permute-start(bf16[128,3712]{1,0:T(8,128)(2,1)S(1)} %shard_map.64.refs_0_), channel_id=1, source_target_pairs={{0,4},{2,6},{4,8},{6,10},{8,12},{10,14},{1,5},{3,7},{5,9},{7,11},{... | collective-permute-start | bytes 2850824 | tf_op jit(solution)/shard_map/ppermute | solution.py:252
  6.8 25.1 %collective-permute-start = (bf16[128,3712]{1,0:T(8,128)(2,1)S(1)}, bf16[128,3712]{1,0:T(8,128)(2,1)S(1)}, u32[]{:S(2)}, u32[]{:S(2)}) collective-permute-start(bf16[128,3712]{1,0:T(8,128)(2,1)S(1)} %shard_map.64.refs_0_), channel_id=1, source_target_pairs={{4,0},{6,2},{8,4},{10,6},{12,8},{14,10},{5,1},{7,3},{9,5},{11,7},{... | collective-permute-start | bytes 2850824 | tf_op jit(solution)/shard_map/ppermute | solution.py:252
  27.7 31.0 %collective-permute-start.6 = (bf16[128,3712]{1,0:T(8,128)(2,1)S(1)}, bf16[128,3712]{1,0:T(8,128)(2,1)S(1)}, u32[]{:S(2)}, u32[]{:S(2)}) collective-permute-start(bf16[128,3712]{1,0:T(8,128)(2,1)S(1)} %collective-permute-done.1.refs_1_.refs_2_), channel_id=1, source_target_pairs={{4,8},{6,10},{8,12},{10,14},{5,9},{7,11},{9,13},{11,15},{20,24},{2... | collective-permute-start | bytes 2850824 | tf_op jit(solution)/shard_map/ppermute | solution.py:252
  31.8 26.8 %collective-permute-start.7 = (bf16[128,3712]{1,0:T(8,128)(2,1)S(1)}, bf16[128,3712]{1,0:T(8,128)(2,1)S(1)}, u32[]{:S(2)}, u32[]{:S(2)}) collective-permute-start(bf16[128,3712]{1,0:T(8,128)(2,1)S(1)} %collective-permute-done.refs_0_), channel_id=1, source_target_pairs={{4,0},{6,2},{8,4},{10,6},{5,1},{7,3},{9,5},{11,7},{20,16},{22,18},... | collective-permute-start | bytes 2850824 | tf_op jit(solution)/shard_map/ppermute | solution.py:252
  34.2 14.8 %collective-permute-start.8 = (bf16[80,3712]{1,0:T(8,128)(2,1)S(1)}, bf16[80,3712]{1,0:T(8,128)(2,1)S(1)}, u32[]{:S(2)}, u32[]{:S(2)}) collective-permute-start(bf16[80,3712]{1,0:T(8,128)(2,1)S(1)} %get-tuple-element.40), channel_id=1, source_target_pairs={{0,2},{2,0},{4,6},{6,4},{8,10},{10,8},{12,14},{14,12},{1,3},{3,1},... | collective-permute-start | bytes 1781768 | tf_op jit(solution)/shard_map/ppermute | solution.py:255
  58.8 24.6 %collective-permute-start.10 = (bf16[128,3712]{1,0:T(8,128)(2,1)S(1)}, bf16[128,3712]{1,0:T(8,128)(2,1)S(1)}, u32[]{:S(2)}, u32[]{:S(2)}) collective-permute-start(bf16[128,3712]{1,0:T(8,128)(2,1)S(1)} %get-tuple-element.43.refs_1_), channel_id=1, source_target_pairs={{8,12},{10,14},{9,13},{11,15},{24,28},{26,30},{25,29},{27,31}} | collective-permute-start | bytes 2850824 | tf_op jit(solution)/shard_map/ppermute | solution.py:252
  59.5 23.9 %collective-permute-start.9 = (bf16[128,3712]{1,0:T(8,128)(2,1)S(1)}, bf16[128,3712]{1,0:T(8,128)(2,1)S(1)}, u32[]{:S(2)}, u32[]{:S(2)}) collective-permute-start(bf16[128,3712]{1,0:T(8,128)(2,1)S(1)} %get-tuple-element.42.refs_0_), channel_id=1, source_target_pairs={{4,0},{6,2},{5,1},{7,3},{20,16},{22,18},{21,17},{23,19}} | collective-permute-start | bytes 2850824 | tf_op jit(solution)/shard_map/ppermute | solution.py:252
  60.8 16.0 %collective-permute-start.11 = (bf16[80,3584]{1,0:T(8,128)(2,1)S(1)}, bf16[80,3584]{1,0:T(8,128)(2,1)S(1)}, u32[]{:S(2)}, u32[]{:S(2)}) collective-permute-start(bf16[80,3584]{1,0:T(8,128)(2,1)S(1)} %get-tuple-element.45), channel_id=1, source_target_pairs={{0,2},{2,0},{4,6},{6,4},{8,10},{10,8},{12,14},{14,12},{1,3},{3,1},... | collective-permute-start | bytes 1720328 | tf_op jit(solution)/shard_map/ppermute | solution.py:255
  63.4 26.1 %collective-permute-start.13 = (bf16[80,3712]{1,0:T(8,128)(2,1)S(1)}, bf16[80,3712]{1,0:T(8,128)(2,1)S(1)}, u32[]{:S(2)}, u32[]{:S(2)}) collective-permute-start(bf16[80,3712]{1,0:T(8,128)(2,1)S(1)} %get-tuple-element.52), channel_id=1, source_target_pairs={{0,2},{2,0},{4,6},{6,4},{8,10},{10,8},{12,14},{14,12},{1,3},{3,1},... | collective-permute-start | bytes 1781768 | tf_op jit(solution)/shard_map/ppermute | solution.py:255
  77.4 36.1 %collective-permute-start.16 = (bf16[128,3584]{1,0:T(8,128)(2,1)S(1)}, bf16[128,3584]{1,0:T(8,128)(2,1)S(1)}, u32[]{:S(2)}, u32[]{:S(2)}) collective-permute-start(bf16[128,3584]{1,0:T(8,128)(2,1)S(1)} %shard_map.70.refs_4_), channel_id=1, source_target_pairs={{8,4},{10,6},{12,8},{14,10},{9,5},{11,7},{13,9},{15,11},{24,20},{2... | collective-permute-start | bytes 2752520 | tf_op jit(solution)/shard_map/ppermute | solution.py:252
  78.1 35.4 %collective-permute-start.17 = (bf16[128,3584]{1,0:T(8,128)(2,1)S(1)}, bf16[128,3584]{1,0:T(8,128)(2,1)S(1)}, u32[]{:S(2)}, u32[]{:S(2)}) collective-permute-start(bf16[128,3584]{1,0:T(8,128)(2,1)S(1)} %shard_map.70.refs_4_), channel_id=1, source_target_pairs={{0,4},{2,6},{4,8},{6,10},{1,5},{3,7},{5,9},{7,11},{16,20},{18,22},... | collective-permute-start | bytes 2752520 | tf_op jit(solution)/shard_map/ppermute | solution.py:252
  84.6 17.6 %collective-permute-start.12 = (bf16[80,3712]{1,0:T(8,128)(2,1)S(1)}, bf16[80,3712]{1,0:T(8,128)(2,1)S(1)}, u32[]{:S(2)}, u32[]{:S(2)}) collective-permute-start(bf16[80,3712]{1,0:T(8,128)(2,1)S(1)} %get-tuple-element.50), channel_id=1, source_target_pairs={{0,2},{2,0},{4,6},{6,4},{8,10},{10,8},{12,14},{14,12},{1,3},{3,1},... | collective-permute-start | bytes 1781768 | tf_op jit(solution)/shard_map/ppermute | solution.py:255
  99.2 15.2 %collective-permute-start.15 = (bf16[80,3584]{1,0:T(8,128)(2,1)S(1)}, bf16[80,3584]{1,0:T(8,128)(2,1)S(1)}, u32[]{:S(2)}, u32[]{:S(2)}) collective-permute-start(bf16[80,3584]{1,0:T(8,128)(2,1)S(1)} %get-tuple-element.57), channel_id=1, source_target_pairs={{0,2},{2,0},{4,6},{6,4},{8,10},{10,8},{12,14},{14,12},{1,3},{3,1},... | collective-permute-start | bytes 1720328 | tf_op jit(solution)/shard_map/ppermute | solution.py:255
  111.9 8.8 %copy-start.1 = (bf16[80,3712]{1,0:T(8,128)(2,1)S(1)}, bf16[80,3712]{1,0:T(8,128)(2,1)}, u32[]{:S(2)}) copy-start(bf16[80,3712]{1,0:T(8,128)(2,1)} %get-tuple-element.38) | copy-start | bytes 1781764
  111.9 25.1 %copy-start = (bf16[80,3712]{1,0:T(8,128)(2,1)S(1)}, bf16[80,3712]{1,0:T(8,128)(2,1)}, u32[]{:S(2)}) copy-start(bf16[80,3712]{1,0:T(8,128)(2,1)} %get-tuple-element.37.refs_0_) | copy-start | bytes 1781764
  111.9 16.0 %collective-permute-start.14 = (bf16[80,3584]{1,0:T(8,128)(2,1)S(1)}, bf16[80,3584]{1,0:T(8,128)(2,1)S(1)}, u32[]{:S(2)}, u32[]{:S(2)}) collective-permute-start(bf16[80,3584]{1,0:T(8,128)(2,1)S(1)} %get-tuple-element.55), channel_id=1, source_target_pairs={{0,2},{2,0},{4,6},{6,4},{8,10},{10,8},{12,14},{14,12},{1,3},{3,1},... | collective-permute-start | bytes 1720328 | tf_op jit(solution)/shard_map/ppermute | solution.py:255
  114.9 33.3 %collective-permute-start.19 = (bf16[128,3584]{1,0:T(8,128)(2,1)S(1)}, bf16[128,3584]{1,0:T(8,128)(2,1)S(1)}, u32[]{:S(2)}, u32[]{:S(2)}) collective-permute-start(bf16[128,3584]{1,0:T(8,128)(2,1)S(1)} %shard_map.74.refs_4_.refs_0_), channel_id=1, source_target_pairs={{0,8},{2,10},{12,4},{14,6},{1,9},{3,11},{13,5},{15,7},{16,24},{18,... | collective-permute-start | bytes 2752520 | tf_op jit(solution)/shard_map/ppermute | solution.py:252
  120.7 16.3 %collective-permute-start.3 = (bf16[80,3712]{1,0:T(8,128)(2,1)S(1)}, bf16[80,3712]{1,0:T(8,128)(2,1)S(1)}, u32[]{:S(2)}, u32[]{:S(2)}) collective-permute-start(bf16[80,3712]{1,0:T(8,128)(2,1)S(1)} %copy-done.1), channel_id=1, source_target_pairs={{0,2},{2,0},{4,6},{6,4},{8,10},{10,8},{12,14},{14,12},{1,3},{3,1},... | collective-permute-start | bytes 1781768 | tf_op jit(solution)/shard_map/ppermute | solution.py:255
  128.5 20.8 %collective-permute-start.21 = (bf16[128,1792]{1,0:T(8,128)(2,1)S(1)}, bf16[128,1792]{1,0:T(8,128)(2,1)S(1)}, u32[]{:S(2)}, u32[]{:S(2)}) collective-permute-start(bf16[128,1792]{1,0:T(8,128)(2,1)S(1)} %get-tuple-element.62), channel_id=1, source_target_pairs={{0,4},{2,6},{12,8},{14,10},{1,5},{3,7},{13,9},{15,11},{16,20},{18,... | collective-permute-start | bytes 1376264 | tf_op jit(solution)/shard_map/ppermute | solution.py:252
  133.1 21.1 %collective-permute-start.20 = (bf16[128,1792]{1,0:T(8,128)(2,1)S(1)}, bf16[128,1792]{1,0:T(8,128)(2,1)S(1)}, u32[]{:S(2)}, u32[]{:S(2)}) collective-permute-start(bf16[128,1792]{1,0:T(8,128)(2,1)S(1)} %get-tuple-element.61), channel_id=1, source_target_pairs={{0,4},{2,6},{12,8},{14,10},{1,5},{3,7},{13,9},{15,11},{16,20},{18,... | collective-permute-start | bytes 1376264 | tf_op jit(solution)/shard_map/ppermute | solution.py:252
  134.5 36.0 %collective-permute-start.22 = (bf16[128,3584]{1,0:T(8,128)(2,1)S(1)}, bf16[128,3584]{1,0:T(8,128)(2,1)S(1)}, u32[]{:S(2)}, u32[]{:S(2)}) collective-permute-start(bf16[128,3584]{1,0:T(8,128)(2,1)S(1)} %get-tuple-element.58.refs_8_), channel_id=1, source_target_pairs={{4,0},{6,2},{8,12},{10,14},{5,1},{7,3},{9,13},{11,15},{20,16},{22,... | collective-permute-start | bytes 2752520 | tf_op jit(solution)/shard_map/ppermute | solution.py:252
  146.6 11.4 %collective-permute-start.18 = (bf16[80,3584]{1,0:T(8,128)(2,1)S(1)}, bf16[80,3584]{1,0:T(8,128)(2,1)S(1)}, u32[]{:S(2)}, u32[]{:S(2)}) collective-permute-start(bf16[80,3584]{1,0:T(8,128)(2,1)S(1)} %get-tuple-element.60), channel_id=1, source_target_pairs={{0,2},{2,0},{4,6},{6,4},{8,10},{10,8},{12,14},{14,12},{1,3},{3,1},... | collective-permute-start | bytes 1720328 | tf_op jit(solution)/shard_map/ppermute | solution.py:255
  149.4 15.8 %collective-permute-start.23 = (bf16[128,1792]{1,0:T(8,128)(2,1)S(1)}, bf16[128,1792]{1,0:T(8,128)(2,1)S(1)}, u32[]{:S(2)}, u32[]{:S(2)}) collective-permute-start(bf16[128,1792]{1,0:T(8,128)(2,1)S(1)} %shard_map.78.refs_2_), channel_id=1, source_target_pairs={{4,12},{6,14},{8,0},{10,2},{5,13},{7,15},{9,1},{11,3},{20,28},{22,... | collective-permute-start | bytes 1376264 | tf_op jit(solution)/shard_map/ppermute | solution.py:252
  154.3 16.3 %collective-permute-start.24 = (bf16[128,1792]{1,0:T(8,128)(2,1)S(1)}, bf16[128,1792]{1,0:T(8,128)(2,1)S(1)}, u32[]{:S(2)}, u32[]{:S(2)}) collective-permute-start(bf16[128,1792]{1,0:T(8,128)(2,1)S(1)} %shard_map.79.refs_5_), channel_id=1, source_target_pairs={{4,12},{6,14},{8,0},{10,2},{5,13},{7,15},{9,1},{11,3},{20,28},{22,... | collective-permute-start | bytes 1376264 | tf_op jit(solution)/shard_map/ppermute | solution.py:252

commit v17 on v16

--- a/solution.py
+++ b/solution.py
@@ -122,9 +122,10 @@
     choose(held, *refs[len(users) : len(users) + 4])
 
 
-def expert_kernel(experts, own, other, *refs):
-    weights, (own_out, other_out, rows, hidden, gates, ups, downs, sems) = refs[:6], refs[6:]
-    cap, width = own_out.shape
+def expert_kernel(experts, count, *refs):
+    marked, weights, outs = refs[:count], refs[count : count + 6], refs[count + 6 : 2 * count + 6]
+    rows, hidden, gates, ups, downs, sems = refs[2 * count + 6 :]
+    cap, width = outs[0].shape
     tiles, _, size = gates.shape
     each = tiles // 2
     queue = []
@@ -145,8 +146,8 @@
             following.start()
             break
 
-    rows[:cap] = own[:, :width]
-    rows[cap:] = other[:, :width]
+    for k, source in enumerate(marked):
+        rows[k * cap : (k + 1) * cap] = source[:, :width]
     for tile in range(tiles):
         arrived(queue[2 * tile])
         gate = jnp.dot(rows[...], gates[tile], preferred_element_type=jnp.float32)
@@ -157,8 +158,8 @@
     arrived(queue[-1])
     node = lax.axis_index("node")
     scales = []
-    for marked in (own, other):
-        marks = marked[:, width:].astype(jnp.float32)
+    for source in marked:
+        marks = source[:, width:].astype(jnp.float32)
         lane = lax.broadcasted_iota(jnp.int32, marks.shape, 1)
         mine = (lax.rem(lane, experts) == node) & (lane < 3 * experts)
         scales.append(jnp.sum(jnp.where(mine, marks, 0.0), axis=1, keepdims=True))
@@ -167,8 +168,8 @@
         cut = slice(start, start + step)
         out = jnp.dot(hidden[:, : each * size], downs[0, :, cut], preferred_element_type=jnp.float32)
         out += jnp.dot(hidden[:, each * size :], downs[1, :, cut], preferred_element_type=jnp.float32)
-        own_out[:, cut] = (out[:cap] * scales[0]).astype(jnp.bfloat16)
-        other_out[:, cut] = (out[cap:] * scales[1]).astype(jnp.bfloat16)
+        for k, result in enumerate(outs):
+            result[:, cut] = (out[k * cap : (k + 1) * cap] * scales[k]).astype(jnp.bfloat16)
 
 
 def spread_kernel(own_map, other_map, own_out, other_out, *refs):
@@ -209,14 +210,14 @@
     result[...] = total.astype(jnp.bfloat16)
 
 
-def finish_kernel(*refs):
+def finish_kernel(total, *refs):
     *whole, low, high, result = refs
     size = low.shape[1]
-    total = high[...].astype(jnp.float32)
+    result[:, :size] = (low[...].astype(jnp.float32) + total[:, :size].astype(jnp.float32)).astype(jnp.bfloat16)
+    rest = high[...].astype(jnp.float32) + total[:, size:].astype(jnp.float32)
     for extra in whole:
-        total += extra[:, size:].astype(jnp.float32)
-    result[:, :size] = low[...]
-    result[:, size:] = total.astype(jnp.bfloat16)
+        rest += extra[:, size:].astype(jnp.float32)
+    result[:, size:] = rest.astype(jnp.bfloat16)
 
 
 def on_device(tokens, routes, route_scale, w_gate, w_up, w_down):
@@ -266,22 +267,22 @@
             cost=cost,
         )
 
-    def expert(own_rows, other_rows, after=(), cost=0):
+    def expert(rows, after=(), cost=0):
         tiles = 2 * hidden // size
         return call(
-            functools.partial(expert_kernel, experts),
-            [bf16((cap, width)), bf16((cap, width))],
-            [own_rows, other_rows, *weights],
+            functools.partial(expert_kernel, experts, len(rows)),
+            [bf16((cap, width))] * len(rows),
+            [*rows, *weights],
             after,
             [
-                pltpu.VMEM((2 * cap, width), jnp.bfloat16),
-                pltpu.VMEM((2 * cap, 2 * hidden), jnp.bfloat16),
+                pltpu.VMEM((len(rows) * cap, width), jnp.bfloat16),
+                pltpu.VMEM((len(rows) * cap, 2 * hidden), jnp.bfloat16),
                 pltpu.VMEM((tiles, width, size), jnp.bfloat16),
                 pltpu.VMEM((tiles, width, size), jnp.bfloat16),
                 pltpu.VMEM((2, hidden, width), jnp.bfloat16),
                 pltpu.SemaphoreType.DMA((tiles, 3)),
             ],
-            [IN_VMEM] * 2 + [ANYWHERE] * 6,
+            [IN_VMEM] * len(rows) + [ANYWHERE] * 6,
             32,
             cost=cost,
         )
@@ -323,7 +324,7 @@
         picks[slot] = maps, own_rows, across(other_rows)
 
     def do_expert(slot, after=(), cost=0):
-        own_out, other_out = ordered(expert, picks[slot][1], picks[slot][2], after=after, cost=cost)
+        own_out, other_out = ordered(expert, picks[slot][1:], after=after, cost=cost)
         outs[slot] = own_out, across(other_out)
 
     def origin(place, slot):
@@ -363,12 +364,16 @@
     def join(whole, half, index, after=()):
         return call(functools.partial(join_kernel, index), [bf16(half.shape)], [whole, half], after)[0]
 
-    def finish(whole, parts):
+    def finish(whole, parts, summed):
         while len(whole) > 8:
-            summed = sum(array.astype(jnp.float32) for array in whole[:8])
-            whole = [summed.astype(jnp.bfloat16), *whole[8:]]
-        low = call(low_kernel, [bf16(parts[0].shape)], [*whole, parts[0]], cost=128 * MIB)[0]
-        return call(finish_kernel, [bf16((count, width))], [*whole, low, parts[1]])[0]
+            merged = sum(array.astype(jnp.float32) for array in whole[:8])
+            whole = [merged.astype(jnp.bfloat16), *whole[8:]]
+        low = ordered(finish_low, whole, parts[0])
+        total = ordered(spread, picks[0][0], *outs[0], [summed])
+        return call(finish_kernel, [bf16((count, width))], [total, *whole, low, parts[1]])[0]
+
+    def finish_low(whole, half, after=()):
+        return call(low_kernel, [bf16(half.shape)], [*whole, half], after, cost=128 * MIB)[0]
 
     relay(1)
     relay(2)
@@ -389,16 +394,17 @@
         do_spread(slot - 1, after=returned[slot - 3])
         if slot + 1 < places:
             do_pick(slot + 1)
+    (own_out,) = ordered(expert, picks[0][1:2])
     do_spread(places - 1)
-    do_expert(0)
+    (other_out,) = ordered(expert, picks[0][2:])
+    outs[0] = own_out, across(other_out)
     near = returned.pop(places - 3)
     (summed,) = ordered(call_sum, [*returned.pop(0), *near] if places > 3 else near, cost=128 * MIB)
     homes = [(q, origin(q, places - 2)) for _, q in hops]
     parts = []
     for arrived in [along(half, hops) for half in halves]:
         parts.append(along(ordered(join, kept[places - 2], arrived, len(parts)), homes))
-    total = ordered(spread, picks[0][0], *outs[0], [summed])
-    return finish([total, *sum(returned, [])], parts)
+    return finish(sum(returned, []), parts, summed)
 
 
 def solution(mesh):

time: 172 us -> 173 us (level)
  Pallas kernels: 49.4 us -> 57.1 us
  waiting for transfers between devices: 77.8 us -> 70.8 us
    ppermute x8, waiting for transfers between devices: 38.7 us -> 29.7 us  [across(): return lax.ppermute(block, 'node', [(n, n ^ 1) for n in range(experts)])]
    pallas_call x19 -> x20, Pallas kernels: 49.4 us -> 57.1 us  [call(): pl.pallas_call(body, out_shape=outs, in_specs=specs, out_specs=out_specs...]
    ppermute x14, waiting for transfers between devices: 39 us -> 41.1 us  [along(): return lax.ppermute(block, 'node', moves)]
  transfers between devices with their start and end apart: 25 -> 25, of which waited for: 14 -> 10; matrix products, arithmetic and copies ran while one was open for 0% -> 0% of each run, Pallas kernels for 28% -> 32%
where the time goes in v17:
time: 173 us
  waiting for transfers between devices  70.8 us (41%)
  Pallas kernels  57.1 us (33%)
  starting transfers between devices  44.2 us (26%)
    pallas_call x20, Pallas kernels, call(): pl.pallas_call(body, out_shape=outs, in_specs=specs, out_specs=out_specs...  57.1 us
    ppermute x14, waiting for transfers between devices, along(): return lax.ppermute(block, 'node', moves)  41.1 us
    ppermute x14, starting transfers between devices, along(): return lax.ppermute(block, 'node', moves)  31.6 us
    ppermute x8, waiting for transfers between devices, across(): return lax.ppermute(block, 'node', [(n, n ^ 1) for n in range(experts)])  29.7 us
    ppermute x8, starting transfers between devices, across(): return lax.ppermute(block, 'node', [(n, n ^ 1) for n in range(experts)])  11.7 us
  transfers between devices with their start and end apart: 25, of which 10 were waited for; matrix products, arithmetic and copies ran while one was open for 0% of the time, Pallas kernels for 32%

profile of v17, /device:TPU:0, one launch (start us, length us, event | category | flops | bytes accessed | tf_op | source)
XLA Modules:
  0.0 172.5 jit_solution(606311378801214428)
XLA Ops:
  0.0 0.5 collective-permute-start.2
  0.5 0.1 collective-permute-start.3
  0.5 0.5 collective-permute-start.4
  1.0 1.2 shard_map.64.refs_0_
  2.2 4.5 %collective-permute-start.1 = (bf16[128,3712]{1,0:T(8,128)(2,1)S(1)}, bf16[128,3712]{1,0:T(8,128)(2,1)S(1)}, u32[]{:S(2)}, u32[]{:S(2)}) collective-permute-start(bf16[128,3712]{1,0:T(8,128)(2,1)S(1)} %shard_map.64.refs_0_), channel_id=1, source_target_pairs={{0,4},{2,6},{4,8},{6,10},{8,12},{10,14},{1,5},{3,7},{5,9},{7,11},{... | collective-permute-start | bytes 2850824 | tf_op jit(solution)/shard_map/ppermute | solution.py:253
  6.8 1.3 collective-permute-start
  8.1 19.6 %collective-permute-done.1.refs_1_.refs_2_ = bf16[128,3712]{1,0:T(8,128)(2,1)S(1)} collective-permute-done((bf16[128,3712]{1,0:T(8,128)(2,1)S(1)}, bf16[128,3712]{1,0:T(8,128)(2,1)S(1)}, u32[]{:S(2)}, u32[]{:S(2)}) %collective-permute-start.1) | collective-permute-done | bytes 950304 | tf_op jit(solution)/shard_map/ppermute | solution.py:253
  27.7 0.7 collective-permute-start.5
  28.4 3.5 %collective-permute-done.refs_0_ = bf16[128,3712]{1,0:T(8,128)(2,1)S(1)} collective-permute-done((bf16[128,3712]{1,0:T(8,128)(2,1)S(1)}, bf16[128,3712]{1,0:T(8,128)(2,1)S(1)}, u32[]{:S(2)}, u32[]{:S(2)}) %collective-permute-start) | collective-permute-done | bytes 950304 | tf_op jit(solution)/shard_map/ppermute | solution.py:253
  31.8 1.3 collective-permute-start.6
  33.1 1.0 shard_map.65
  34.2 1.6 collective-permute-start.7
  35.8 1.9 %shard_map.66 = (bf16[128,80]{1,0:T(8,128)(2,1)S(1)}, bf16[128,80]{1,0:T(8,128)(2,1)S(1)}, bf16[80,3712]{1,0:T(8,128)(2,1)}, bf16[80,3712]{1,0:T(8,128)(2,1)}) custom-call(bf16[128,3712]{1,0:T(8,128)(2,1)S(1)} %shard_map.64.refs_0_, bf16[128,80]{1,0:T(8,128)(2,1)S(1)} %get-tuple-element.32.refs_1_.refs_0_), custom_call_target="tpu_custom_call" | custom-call | tf_op jit(solution)/shard_map/pallas_call | solution.py:33
  37.6 0.0 collective-permute-done.3.refs_6_.refs_5_
  37.6 0.0 collective-permute-done.4.refs_7_.refs_6_
  37.7 11.3 %collective-permute-done.7.refs_1_.refs_3_ = bf16[80,3712]{1,0:T(8,128)(2,1)S(1)} collective-permute-done((bf16[80,3712]{1,0:T(8,128)(2,1)S(1)}, bf16[80,3712]{1,0:T(8,128)(2,1)S(1)}, u32[]{:S(2)}, u32[]{:S(2)}) %collective-permute-start.7) | collective-permute-done | bytes 593952 | tf_op jit(solution)/shard_map/ppermute | solution.py:256
  49.0 9.6 %shard_map.67 = (bf16[80,3584]{1,0:T(8,128)(2,1)S(1)}, bf16[80,3584]{1,0:T(8,128)(2,1)S(1)}) custom-call(bf16[80,3712]{1,0:T(8,128)(2,1)S(1)} %get-tuple-element.36.refs_0_, bf16[80,3712]{1,0:T(8,128)(2,1)S(1)} %collective-permute-done.7.refs_1_.refs_3_, bf16[3584,512]{1,0:T(8,128)(2,1)} %bitcast.6, bf16[3584,512]{1,0:T(8,128)(2,1)} %bitcast.12, ...), custom_call_target="tpu_custom_call" | custom-call | bytes 67108864 | tf_op jit(solution)/shard_map/pallas_call | solution.py:33
  58.6 0.0 collective-permute-done.6.refs_1_
  58.6 0.1 shard_map.68
  58.8 0.7 collective-permute-start.10
  59.5 1.3 collective-permute-start.9
  60.8 1.6 collective-permute-start.11
  62.4 1.0 shard_map.69
  63.4 0.6 collective-permute-start.8
  64.0 12.8 %collective-permute-done.11.refs_3_ = bf16[80,3584]{1,0:T(8,128)(2,1)S(1)} collective-permute-done((bf16[80,3584]{1,0:T(8,128)(2,1)S(1)}, bf16[80,3584]{1,0:T(8,128)(2,1)S(1)}, u32[]{:S(2)}, u32[]{:S(2)}) %collective-permute-start.11) | collective-permute-done | bytes 573472 | tf_op jit(solution)/shard_map/ppermute | solution.py:256
  76.8 0.6 shard_map.70.refs_4_
  77.4 0.7 collective-permute-start.14
  78.1 5.2 %collective-permute-start.15 = (bf16[128,3584]{1,0:T(8,128)(2,1)S(1)}, bf16[128,3584]{1,0:T(8,128)(2,1)S(1)}, u32[]{:S(2)}, u32[]{:S(2)}) collective-permute-start(bf16[128,3584]{1,0:T(8,128)(2,1)S(1)} %shard_map.70.refs_4_), channel_id=1, source_target_pairs={{0,4},{2,6},{4,8},{6,10},{1,5},{3,7},{5,9},{7,11},{16,20},{18,22},... | collective-permute-start | bytes 2752520 | tf_op jit(solution)/shard_map/ppermute | solution.py:253
  83.4 0.0 collective-permute-done.10.refs_3_
  83.4 0.0 collective-permute-done.9.refs_1_
  83.4 1.2 shard_map.71
  84.6 1.6 collective-permute-start.13
  86.2 3.3 %collective-permute-done.8.refs_1_ = bf16[80,3712]{1,0:T(8,128)(2,1)S(1)} collective-permute-done((bf16[80,3712]{1,0:T(8,128)(2,1)S(1)}, bf16[80,3712]{1,0:T(8,128)(2,1)S(1)}, u32[]{:S(2)}, u32[]{:S(2)}) %collective-permute-start.8) | collective-permute-done | bytes 593952 | tf_op jit(solution)/shard_map/ppermute | solution.py:256
  89.5 9.6 %shard_map.72 = (bf16[80,3584]{1,0:T(8,128)(2,1)S(1)}, bf16[80,3584]{1,0:T(8,128)(2,1)S(1)}) custom-call(bf16[80,3712]{1,0:T(8,128)(2,1)S(1)} %get-tuple-element.43.refs_0_, bf16[80,3712]{1,0:T(8,128)(2,1)S(1)} %collective-permute-done.8.refs_1_, bf16[3584,512]{1,0:T(8,128)(2,1)} %bitcast.7, bf16[3584,512]{1,0:T(8,128)(2,1)} %bitcast.13, ...), custom_call_target="tpu_custom_call" | custom-call | tf_op jit(solution)/shard_map/pallas_call | solution.py:33
  99.2 1.6 collective-permute-start.12
  100.7 1.5 collective-permute-done.13.refs_1_
  102.2 9.6 %shard_map.73 = (bf16[80,3584]{1,0:T(8,128)(2,1)S(1)}, bf16[80,3584]{1,0:T(8,128)(2,1)S(1)}) custom-call(bf16[80,3712]{1,0:T(8,128)(2,1)S(1)} %get-tuple-element.50.refs_0_, bf16[80,3712]{1,0:T(8,128)(2,1)S(1)} %collective-permute-done.13.refs_1_, bf16[3584,512]{1,0:T(8,128)(2,1)} %bitcast.8, bf16[3584,512]{1,0:T(8,128)(2,1)} %bitcast.14, ...), custom_call_target="tpu_custom_call" | custom-call | tf_op jit(solution)/shard_map/pallas_call | solution.py:33
  111.9 0.0 copy-start
  111.9 1.6 collective-permute-start.17
  113.5 0.0 collective-permute-done.14.refs_5_.refs_0_
  113.5 0.0 collective-permute-done.15.refs_6_.refs_1_
  113.5 0.8 collective-permute-done.12.refs_3_
  114.3 0.6 shard_map.74.refs_7_.refs_0_
  114.9 6.0 %collective-permute-start.19 = (bf16[128,3584]{1,0:T(8,128)(2,1)S(1)}, bf16[128,3584]{1,0:T(8,128)(2,1)S(1)}, u32[]{:S(2)}, u32[]{:S(2)}) collective-permute-start(bf16[128,3584]{1,0:T(8,128)(2,1)S(1)} %shard_map.74.refs_7_.refs_0_), channel_id=1, source_target_pairs={{0,8},{2,10},{12,4},{14,6},{1,9},{3,11},{13,5},{15,7},{16,24},{18,... | collective-permute-start | bytes 2752520 | tf_op jit(solution)/shard_map/ppermute | solution.py:253
  120.9 1.6 collective-permute-start.16
  122.5 8.7 %shard_map.75.refs_4_.refs_2_ = bf16[80,3584]{1,0:T(8,128)(2,1)S(1)} custom-call(bf16[80,3712]{1,0:T(8,128)(2,1)S(1)} %copy-done, bf16[3584,512]{1,0:T(8,128)(2,1)} %bitcast.9, bf16[3584,512]{1,0:T(8,128)(2,1)} %bitcast.15, bf16[512,3584]{1,0:T(8,128)(2,1)} %bitcast.21, bf16[3584,512]{1,0:T(8,128)(2,1)S(1)} %collective-permute-done.2.refs_2_.refs_5_.refs_4_, ...), custom_call_target="tpu_custom_call" | custom-call | tf_op jit(solution)/shard_map/pallas_call | solution.py:33
  131.2 0.6 shard_map.76
  131.9 1.3 collective-permute-start.21
  133.2 1.3 collective-permute-start.20
  134.5 4.6 %collective-permute-start.23 = (bf16[128,1792]{1,0:T(8,128)(2,1)S(1)}, bf16[128,1792]{1,0:T(8,128)(2,1)S(1)}, u32[]{:S(2)}, u32[]{:S(2)}) collective-permute-start(bf16[128,1792]{1,0:T(8,128)(2,1)S(1)} %get-tuple-element.58), channel_id=1, source_target_pairs={{0,4},{2,6},{12,8},{14,10},{1,5},{3,7},{13,9},{15,11},{16,20},{18,... | collective-permute-start | bytes 1376264 | tf_op jit(solution)/shard_map/ppermute | solution.py:253
  139.1 8.7 %shard_map.77.refs_3_ = bf16[80,3584]{1,0:T(8,128)(2,1)S(1)} custom-call(bf16[80,3712]{1,0:T(8,128)(2,1)S(1)} %collective-permute-done.16.refs_0_, bf16[3584,512]{1,0:T(8,128)(2,1)} %bitcast.10, bf16[3584,512]{1,0:T(8,128)(2,1)} %bitcast.16, bf16[512,3584]{1,0:T(8,128)(2,1)} %bitcast.22, ...), custom_call_target="tpu_custom_call" | custom-call | tf_op jit(solution)/shard_map/pallas_call | solution.py:33
  147.8 1.6 collective-permute-start.18
  149.4 0.3 shard_map.78.refs_2_.refs_4_
  149.7 0.1 shard_map.79.refs_2_
  149.8 1.3 collective-permute-start.22
  151.1 3.1 %collective-permute-done.23.refs_1_ = bf16[128,1792]{1,0:T(8,128)(2,1)S(1)} collective-permute-done((bf16[128,1792]{1,0:T(8,128)(2,1)S(1)}, bf16[128,1792]{1,0:T(8,128)(2,1)S(1)}, u32[]{:S(2)}, u32[]{:S(2)}) %collective-permute-start.23) | collective-permute-done | bytes 458784 | tf_op jit(solution)/shard_map/ppermute | solution.py:253
  154.2 0.1 shard_map.80.refs_2_
  154.3 1.3 collective-permute-start.24
  155.6 8.6 %collective-permute-done.22.refs_1_ = bf16[128,1792]{1,0:T(8,128)(2,1)S(1)} collective-permute-done((bf16[128,1792]{1,0:T(8,128)(2,1)S(1)}, bf16[128,1792]{1,0:T(8,128)(2,1)S(1)}, u32[]{:S(2)}, u32[]{:S(2)}) %collective-permute-start.22) | collective-permute-done | bytes 458784 | tf_op jit(solution)/shard_map/ppermute | solution.py:253
  164.2 6.3 %collective-permute-done.20.refs_0_ = bf16[128,3584]{1,0:T(8,128)(2,1)S(1)} collective-permute-done((bf16[128,3584]{1,0:T(8,128)(2,1)S(1)}, bf16[128,3584]{1,0:T(8,128)(2,1)S(1)}, u32[]{:S(2)}, u32[]{:S(2)}) %collective-permute-start.20) | collective-permute-done | bytes 917536 | tf_op jit(solution)/shard_map/ppermute | solution.py:253
  170.6 0.1 shard_map.81.refs_5_.refs_1_
  170.7 0.0 collective-permute-done.18.refs_3_
  170.7 0.6 shard_map.82.total
  171.3 1.2 shard_map.83
  (10 shorter events, 0.0 us)
Async XLA Ops:
  0.0 33.1 %collective-permute-start.2 = (bf16[3584,512]{1,0:T(8,128)(2,1)}, bf16[3584,512]{1,0:T(8,128)(2,1)S(1)}, u32[]{:S(2)}, u32[]{:S(2)}) collective-permute-start(bf16[3584,512]{1,0:T(8,128)(2,1)} %bitcast.5), channel_id=1, source_target_pairs={{0,1},{1,0},{2,3},{3,2},{4,5},{5,4},{6,7},{7,6},{8,9},{9,8},{10,11... | collective-permute-start | bytes 11010056 | tf_op jit(solution)/shard_map/ppermute | solution.py:249
  0.5 37.2 %collective-permute-start.3 = (bf16[3584,512]{1,0:T(8,128)(2,1)}, bf16[3584,512]{1,0:T(8,128)(2,1)S(1)}, u32[]{:S(2)}, u32[]{:S(2)}) collective-permute-start(bf16[3584,512]{1,0:T(8,128)(2,1)} %bitcast.11), channel_id=1, source_target_pairs={{0,1},{1,0},{2,3},{3,2},{4,5},{5,4},{6,7},{7,6},{8,9},{9,8},{10,11... | collective-permute-start | bytes 11010056 | tf_op jit(solution)/shard_map/ppermute | solution.py:249
  0.5 37.1 %collective-permute-start.4 = (bf16[512,3584]{1,0:T(8,128)(2,1)}, bf16[512,3584]{1,0:T(8,128)(2,1)S(1)}, u32[]{:S(2)}, u32[]{:S(2)}) collective-permute-start(bf16[512,3584]{1,0:T(8,128)(2,1)} %bitcast.17), channel_id=1, source_target_pairs={{0,1},{1,0},{2,3},{3,2},{4,5},{5,4},{6,7},{7,6},{8,9},{9,8},{10,11... | collective-permute-start | bytes 11010056 | tf_op jit(solution)/shard_map/ppermute | solution.py:249
  2.2 25.5 %collective-permute-start.1 = (bf16[128,3712]{1,0:T(8,128)(2,1)S(1)}, bf16[128,3712]{1,0:T(8,128)(2,1)S(1)}, u32[]{:S(2)}, u32[]{:S(2)}) collective-permute-start(bf16[128,3712]{1,0:T(8,128)(2,1)S(1)} %shard_map.64.refs_0_), channel_id=1, source_target_pairs={{0,4},{2,6},{4,8},{6,10},{8,12},{10,14},{1,5},{3,7},{5,9},{7,11},{... | collective-permute-start | bytes 2850824 | tf_op jit(solution)/shard_map/ppermute | solution.py:253
  6.8 25.1 %collective-permute-start = (bf16[128,3712]{1,0:T(8,128)(2,1)S(1)}, bf16[128,3712]{1,0:T(8,128)(2,1)S(1)}, u32[]{:S(2)}, u32[]{:S(2)}) collective-permute-start(bf16[128,3712]{1,0:T(8,128)(2,1)S(1)} %shard_map.64.refs_0_), channel_id=1, source_target_pairs={{4,0},{6,2},{8,4},{10,6},{12,8},{14,10},{5,1},{7,3},{9,5},{11,7},{... | collective-permute-start | bytes 2850824 | tf_op jit(solution)/shard_map/ppermute | solution.py:253
  27.7 31.0 %collective-permute-start.5 = (bf16[128,3712]{1,0:T(8,128)(2,1)S(1)}, bf16[128,3712]{1,0:T(8,128)(2,1)S(1)}, u32[]{:S(2)}, u32[]{:S(2)}) collective-permute-start(bf16[128,3712]{1,0:T(8,128)(2,1)S(1)} %collective-permute-done.1.refs_1_.refs_2_), channel_id=1, source_target_pairs={{4,8},{6,10},{8,12},{10,14},{5,9},{7,11},{9,13},{11,15},{20,24},{2... | collective-permute-start | bytes 2850824 | tf_op jit(solution)/shard_map/ppermute | solution.py:253
  31.8 26.8 %collective-permute-start.6 = (bf16[128,3712]{1,0:T(8,128)(2,1)S(1)}, bf16[128,3712]{1,0:T(8,128)(2,1)S(1)}, u32[]{:S(2)}, u32[]{:S(2)}) collective-permute-start(bf16[128,3712]{1,0:T(8,128)(2,1)S(1)} %collective-permute-done.refs_0_), channel_id=1, source_target_pairs={{4,0},{6,2},{8,4},{10,6},{5,1},{7,3},{9,5},{11,7},{20,16},{22,18},... | collective-permute-start | bytes 2850824 | tf_op jit(solution)/shard_map/ppermute | solution.py:253
  34.2 14.8 %collective-permute-start.7 = (bf16[80,3712]{1,0:T(8,128)(2,1)S(1)}, bf16[80,3712]{1,0:T(8,128)(2,1)S(1)}, u32[]{:S(2)}, u32[]{:S(2)}) collective-permute-start(bf16[80,3712]{1,0:T(8,128)(2,1)S(1)} %get-tuple-element.37), channel_id=1, source_target_pairs={{0,2},{2,0},{4,6},{6,4},{8,10},{10,8},{12,14},{14,12},{1,3},{3,1},... | collective-permute-start | bytes 1781768 | tf_op jit(solution)/shard_map/ppermute | solution.py:256
  58.8 24.6 %collective-permute-start.10 = (bf16[128,3712]{1,0:T(8,128)(2,1)S(1)}, bf16[128,3712]{1,0:T(8,128)(2,1)S(1)}, u32[]{:S(2)}, u32[]{:S(2)}) collective-permute-start(bf16[128,3712]{1,0:T(8,128)(2,1)S(1)} %get-tuple-element.40.refs_1_), channel_id=1, source_target_pairs={{8,12},{10,14},{9,13},{11,15},{24,28},{26,30},{25,29},{27,31}} | collective-permute-start | bytes 2850824 | tf_op jit(solution)/shard_map/ppermute | solution.py:253
  59.5 23.9 %collective-permute-start.9 = (bf16[128,3712]{1,0:T(8,128)(2,1)S(1)}, bf16[128,3712]{1,0:T(8,128)(2,1)S(1)}, u32[]{:S(2)}, u32[]{:S(2)}) collective-permute-start(bf16[128,3712]{1,0:T(8,128)(2,1)S(1)} %get-tuple-element.39.refs_0_), channel_id=1, source_target_pairs={{4,0},{6,2},{5,1},{7,3},{20,16},{22,18},{21,17},{23,19}} | collective-permute-start | bytes 2850824 | tf_op jit(solution)/shard_map/ppermute | solution.py:253
  60.8 16.0 %collective-permute-start.11 = (bf16[80,3584]{1,0:T(8,128)(2,1)S(1)}, bf16[80,3584]{1,0:T(8,128)(2,1)S(1)}, u32[]{:S(2)}, u32[]{:S(2)}) collective-permute-start(bf16[80,3584]{1,0:T(8,128)(2,1)S(1)} %get-tuple-element.46), channel_id=1, source_target_pairs={{0,2},{2,0},{4,6},{6,4},{8,10},{10,8},{12,14},{14,12},{1,3},{3,1},... | collective-permute-start | bytes 1720328 | tf_op jit(solution)/shard_map/ppermute | solution.py:256
  63.4 26.1 %collective-permute-start.8 = (bf16[80,3712]{1,0:T(8,128)(2,1)S(1)}, bf16[80,3712]{1,0:T(8,128)(2,1)S(1)}, u32[]{:S(2)}, u32[]{:S(2)}) collective-permute-start(bf16[80,3712]{1,0:T(8,128)(2,1)S(1)} %get-tuple-element.44), channel_id=1, source_target_pairs={{0,2},{2,0},{4,6},{6,4},{8,10},{10,8},{12,14},{14,12},{1,3},{3,1},... | collective-permute-start | bytes 1781768 | tf_op jit(solution)/shard_map/ppermute | solution.py:256
  77.4 36.1 %collective-permute-start.14 = (bf16[128,3584]{1,0:T(8,128)(2,1)S(1)}, bf16[128,3584]{1,0:T(8,128)(2,1)S(1)}, u32[]{:S(2)}, u32[]{:S(2)}) collective-permute-start(bf16[128,3584]{1,0:T(8,128)(2,1)S(1)} %shard_map.70.refs_4_), channel_id=1, source_target_pairs={{8,4},{10,6},{12,8},{14,10},{9,5},{11,7},{13,9},{15,11},{24,20},{2... | collective-permute-start | bytes 2752520 | tf_op jit(solution)/shard_map/ppermute | solution.py:253
  78.1 35.4 %collective-permute-start.15 = (bf16[128,3584]{1,0:T(8,128)(2,1)S(1)}, bf16[128,3584]{1,0:T(8,128)(2,1)S(1)}, u32[]{:S(2)}, u32[]{:S(2)}) collective-permute-start(bf16[128,3584]{1,0:T(8,128)(2,1)S(1)} %shard_map.70.refs_4_), channel_id=1, source_target_pairs={{0,4},{2,6},{4,8},{6,10},{1,5},{3,7},{5,9},{7,11},{16,20},{18,22},... | collective-permute-start | bytes 2752520 | tf_op jit(solution)/shard_map/ppermute | solution.py:253
  84.6 17.6 %collective-permute-start.13 = (bf16[80,3712]{1,0:T(8,128)(2,1)S(1)}, bf16[80,3712]{1,0:T(8,128)(2,1)S(1)}, u32[]{:S(2)}, u32[]{:S(2)}) collective-permute-start(bf16[80,3712]{1,0:T(8,128)(2,1)S(1)} %get-tuple-element.51), channel_id=1, source_target_pairs={{0,2},{2,0},{4,6},{6,4},{8,10},{10,8},{12,14},{14,12},{1,3},{3,1},... | collective-permute-start | bytes 1781768 | tf_op jit(solution)/shard_map/ppermute | solution.py:256
  99.2 15.2 %collective-permute-start.12 = (bf16[80,3584]{1,0:T(8,128)(2,1)S(1)}, bf16[80,3584]{1,0:T(8,128)(2,1)S(1)}, u32[]{:S(2)}, u32[]{:S(2)}) collective-permute-start(bf16[80,3584]{1,0:T(8,128)(2,1)S(1)} %get-tuple-element.49), channel_id=1, source_target_pairs={{0,2},{2,0},{4,6},{6,4},{8,10},{10,8},{12,14},{14,12},{1,3},{3,1},... | collective-permute-start | bytes 1720328 | tf_op jit(solution)/shard_map/ppermute | solution.py:256
  111.9 9.1 %copy-start.1 = (bf16[80,3712]{1,0:T(8,128)(2,1)S(1)}, bf16[80,3712]{1,0:T(8,128)(2,1)}, u32[]{:S(2)}) copy-start(bf16[80,3712]{1,0:T(8,128)(2,1)} %get-tuple-element.53) | copy-start | bytes 1781764
  111.9 10.6 %copy-start = (bf16[80,3712]{1,0:T(8,128)(2,1)S(1)}, bf16[80,3712]{1,0:T(8,128)(2,1)}, u32[]{:S(2)}) copy-start(bf16[80,3712]{1,0:T(8,128)(2,1)} %get-tuple-element.35.refs_0_) | copy-start | bytes 1781764
  111.9 19.3 %collective-permute-start.17 = (bf16[80,3584]{1,0:T(8,128)(2,1)S(1)}, bf16[80,3584]{1,0:T(8,128)(2,1)S(1)}, u32[]{:S(2)}, u32[]{:S(2)}) collective-permute-start(bf16[80,3584]{1,0:T(8,128)(2,1)S(1)} %get-tuple-element.55), channel_id=1, source_target_pairs={{0,2},{2,0},{4,6},{6,4},{8,10},{10,8},{12,14},{14,12},{1,3},{3,1},... | collective-permute-start | bytes 1720328 | tf_op jit(solution)/shard_map/ppermute | solution.py:256
  114.9 34.4 %collective-permute-start.19 = (bf16[128,3584]{1,0:T(8,128)(2,1)S(1)}, bf16[128,3584]{1,0:T(8,128)(2,1)S(1)}, u32[]{:S(2)}, u32[]{:S(2)}) collective-permute-start(bf16[128,3584]{1,0:T(8,128)(2,1)S(1)} %shard_map.74.refs_7_.refs_0_), channel_id=1, source_target_pairs={{0,8},{2,10},{12,4},{14,6},{1,9},{3,11},{13,5},{15,7},{16,24},{18,... | collective-permute-start | bytes 2752520 | tf_op jit(solution)/shard_map/ppermute | solution.py:253
  120.9 18.2 %collective-permute-start.16 = (bf16[80,3712]{1,0:T(8,128)(2,1)S(1)}, bf16[80,3712]{1,0:T(8,128)(2,1)S(1)}, u32[]{:S(2)}, u32[]{:S(2)}) collective-permute-start(bf16[80,3712]{1,0:T(8,128)(2,1)S(1)} %copy-done.1), channel_id=1, source_target_pairs={{0,2},{2,0},{4,6},{6,4},{8,10},{10,8},{12,14},{14,12},{1,3},{3,1},... | collective-permute-start | bytes 1781768 | tf_op jit(solution)/shard_map/ppermute | solution.py:256
  131.9 17.8 %collective-permute-start.21 = (bf16[128,1792]{1,0:T(8,128)(2,1)S(1)}, bf16[128,1792]{1,0:T(8,128)(2,1)S(1)}, u32[]{:S(2)}, u32[]{:S(2)}) collective-permute-start(bf16[128,1792]{1,0:T(8,128)(2,1)S(1)} %get-tuple-element.57), channel_id=1, source_target_pairs={{0,4},{2,6},{12,8},{14,10},{1,5},{3,7},{13,9},{15,11},{16,20},{18,... | collective-permute-start | bytes 1376264 | tf_op jit(solution)/shard_map/ppermute | solution.py:253
  133.2 37.4 %collective-permute-start.20 = (bf16[128,3584]{1,0:T(8,128)(2,1)S(1)}, bf16[128,3584]{1,0:T(8,128)(2,1)S(1)}, u32[]{:S(2)}, u32[]{:S(2)}) collective-permute-start(bf16[128,3584]{1,0:T(8,128)(2,1)S(1)} %get-tuple-element.56.refs_7_), channel_id=1, source_target_pairs={{4,0},{6,2},{8,12},{10,14},{5,1},{7,3},{9,13},{11,15},{20,16},{22,... | collective-permute-start | bytes 2752520 | tf_op jit(solution)/shard_map/ppermute | solution.py:253
  134.5 19.7 %collective-permute-start.23 = (bf16[128,1792]{1,0:T(8,128)(2,1)S(1)}, bf16[128,1792]{1,0:T(8,128)(2,1)S(1)}, u32[]{:S(2)}, u32[]{:S(2)}) collective-permute-start(bf16[128,1792]{1,0:T(8,128)(2,1)S(1)} %get-tuple-element.58), channel_id=1, source_target_pairs={{0,4},{2,6},{12,8},{14,10},{1,5},{3,7},{13,9},{15,11},{16,20},{18,... | collective-permute-start | bytes 1376264 | tf_op jit(solution)/shard_map/ppermute | solution.py:253
  147.8 22.9 %collective-permute-start.18 = (bf16[80,3584]{1,0:T(8,128)(2,1)S(1)}, bf16[80,3584]{1,0:T(8,128)(2,1)S(1)}, u32[]{:S(2)}, u32[]{:S(2)}) collective-permute-start(bf16[80,3584]{1,0:T(8,128)(2,1)S(1)} %shard_map.77.refs_3_), channel_id=1, source_target_pairs={{0,2},{2,0},{4,6},{6,4},{8,10},{10,8},{12,14},{14,12},{1,3},{3,1},... | collective-permute-start | bytes 1720328 | tf_op jit(solution)/shard_map/ppermute | solution.py:256
  149.8 14.4 %collective-permute-start.22 = (bf16[128,1792]{1,0:T(8,128)(2,1)S(1)}, bf16[128,1792]{1,0:T(8,128)(2,1)S(1)}, u32[]{:S(2)}, u32[]{:S(2)}) collective-permute-start(bf16[128,1792]{1,0:T(8,128)(2,1)S(1)} %shard_map.79.refs_2_), channel_id=1, source_target_pairs={{4,12},{6,14},{8,0},{10,2},{5,13},{7,15},{9,1},{11,3},{20,28},{22,... | collective-permute-start | bytes 1376264 | tf_op jit(solution)/shard_map/ppermute | solution.py:253
  154.3 17.0 %collective-permute-start.24 = (bf16[128,1792]{1,0:T(8,128)(2,1)S(1)}, bf16[128,1792]{1,0:T(8,128)(2,1)S(1)}, u32[]{:S(2)}, u32[]{:S(2)}) collective-permute-start(bf16[128,1792]{1,0:T(8,128)(2,1)S(1)} %shard_map.80.refs_2_), channel_id=1, source_target_pairs={{4,12},{6,14},{8,0},{10,2},{5,13},{7,15},{9,1},{11,3},{20,28},{22,... | collective-permute-start | bytes 1376264 | tf_op jit(solution)/shard_map/ppermute | solution.py:253

commit v18 on v17

--- a/solution.py
+++ b/solution.py
@@ -15,9 +15,9 @@
 def arrivals(places):
     plan = []
     for place in range(places):
-        left = [(-1, step) for step in range(1, places - place)]
-        right = [(1, step) for step in range(1, place + 1)]
-        plan.append(left + right if place < places // 2 else right + left)
+        ways = (-1, 1) if place < places // 2 else (1, -1)
+        steps = [(way, step) for step in range(1, places) for way in ways]
+        plan.append([(way, step) for way, step in steps if 0 <= place - way * step < places])
     return plan
 
 
@@ -331,13 +331,13 @@
         way, step = plan[place][slot - 1]
         return place - way * step
 
-    hops = []
-    for place in range(places):
-        target = origin(place, places - 1)
-        near = place + (1 if target > place else -1)
-        if near != target and origin(near, places - 2) == target:
-            hops.append((place, near))
-    staying = {places - 1: [a for a, _ in hops], places - 2: [b for _, b in hops]}
+    final = places - 1
+    hops = [
+        (a, b)
+        for a, b in ((0, 1), (places - 1, places - 2))
+        if origin(a, final) == origin(b, final) and origin(b, final) not in (a, b)
+    ]
+    staying = {place for hop in hops for place in hop}
     kept, halves = {}, []
 
     def spread_halves(maps, own_out, other_out, after=()):
@@ -350,7 +350,7 @@
         else:
             done = ordered(spread, picks[slot][0], *outs[slot], after=after, cost=cost)
         kept[slot] = done
-        home = [(a, origin(a, slot)) for a in range(places) if a not in staying.get(slot, ())]
+        home = [(a, origin(a, slot)) for a in range(places) if slot < final or a not in staying]
         rounds = []
         while home:
             now = list({b: (a, b) for a, b in home}.values())
@@ -400,10 +400,10 @@
     outs[0] = own_out, across(other_out)
     near = returned.pop(places - 3)
     (summed,) = ordered(call_sum, [*returned.pop(0), *near] if places > 3 else near, cost=128 * MIB)
-    homes = [(q, origin(q, places - 2)) for _, q in hops]
+    homes = [(q, origin(q, final)) for _, q in hops]
     parts = []
     for arrived in [along(half, hops) for half in halves]:
-        parts.append(along(ordered(join, kept[places - 2], arrived, len(parts)), homes))
+        parts.append(along(ordered(join, kept[final], arrived, len(parts)), homes))
     return finish(sum(returned, []), parts, summed)
 
 

time: 173 us -> 171 us (0.988)
  starting transfers between devices: 44.2 us -> 39.6 us
  waiting for transfers between devices: 70.8 us -> 73.3 us
    ppermute x14 -> x13, starting transfers between devices: 31.6 us -> 27 us  [along(): return lax.ppermute(block, 'node', moves)]
    ppermute x8, waiting for transfers between devices: 29.7 us -> 32.3 us  [across(): return lax.ppermute(block, 'node', [(n, n ^ 1) for n in range(experts)])]
    ppermute x14 -> x13, waiting for transfers between devices: 41.1 us -> 41 us  [along(): return lax.ppermute(block, 'node', moves)]
  transfers between devices with their start and end apart: 25 -> 24, of which waited for: 10 -> 12; matrix products, arithmetic and copies ran while one was open for 0% -> 0% of each run, Pallas kernels for 32% -> 33%
where the time goes in v18:
time: 171 us; the launch traced here: 170 us
  waiting for transfers between devices  73.3 us (43%)
  Pallas kernels  56.9 us (33%)
  starting transfers between devices  39.6 us (23%)
    pallas_call x20, Pallas kernels, call(): pl.pallas_call(body, out_shape=outs, in_specs=specs, out_specs=out_specs...  56.9 us
    ppermute x13, waiting for transfers between devices, along(): return lax.ppermute(block, 'node', moves)  41 us
    ppermute x8, waiting for transfers between devices, across(): return lax.ppermute(block, 'node', [(n, n ^ 1) for n in range(experts)])  32.3 us
    ppermute x13, starting transfers between devices, along(): return lax.ppermute(block, 'node', moves)  27 us
    ppermute x8, starting transfers between devices, across(): return lax.ppermute(block, 'node', [(n, n ^ 1) for n in range(experts)])  11.6 us
  transfers between devices with their start and end apart: 24, of which 12 were waited for; matrix products, arithmetic and copies ran while one was open for 0% of the time, Pallas kernels for 33%

profile of v18, /device:TPU:0, one launch (start us, length us, event | category | flops | bytes accessed | tf_op | source)
XLA Modules:
  0.0 170.2 jit_solution(7295911190148624884)
XLA Ops:
  0.0 0.5 collective-permute-start.2
  0.5 0.1 collective-permute-start.3
  0.5 0.5 collective-permute-start.4
  1.0 1.2 shard_map.64.refs_0_
  2.2 4.5 %collective-permute-start.1 = (bf16[128,3712]{1,0:T(8,128)(2,1)S(1)}, bf16[128,3712]{1,0:T(8,128)(2,1)S(1)}, u32[]{:S(2)}, u32[]{:S(2)}) collective-permute-start(bf16[128,3712]{1,0:T(8,128)(2,1)S(1)} %shard_map.64.refs_0_), channel_id=1, source_target_pairs={{0,4},{2,6},{4,8},{6,10},{8,12},{10,14},{1,5},{3,7},{5,9},{7,11},{... | collective-permute-start | bytes 2850824 | tf_op jit(solution)/shard_map/ppermute | solution.py:253
  6.8 1.3 collective-permute-start
  8.1 19.6 %collective-permute-done.1.refs_1_.refs_2_ = bf16[128,3712]{1,0:T(8,128)(2,1)S(1)} collective-permute-done((bf16[128,3712]{1,0:T(8,128)(2,1)S(1)}, bf16[128,3712]{1,0:T(8,128)(2,1)S(1)}, u32[]{:S(2)}, u32[]{:S(2)}) %collective-permute-start.1) | collective-permute-done | bytes 950304 | tf_op jit(solution)/shard_map/ppermute | solution.py:253
  27.7 0.7 collective-permute-start.5
  28.4 3.5 %collective-permute-done.refs_0_ = bf16[128,3712]{1,0:T(8,128)(2,1)S(1)} collective-permute-done((bf16[128,3712]{1,0:T(8,128)(2,1)S(1)}, bf16[128,3712]{1,0:T(8,128)(2,1)S(1)}, u32[]{:S(2)}, u32[]{:S(2)}) %collective-permute-start) | collective-permute-done | bytes 950304 | tf_op jit(solution)/shard_map/ppermute | solution.py:253
  31.8 1.3 collective-permute-start.6
  33.1 1.0 shard_map.65
  34.2 1.6 collective-permute-start.7
  35.8 1.9 %shard_map.66 = (bf16[128,80]{1,0:T(8,128)(2,1)S(1)}, bf16[128,80]{1,0:T(8,128)(2,1)S(1)}, bf16[80,3712]{1,0:T(8,128)(2,1)}, bf16[80,3712]{1,0:T(8,128)(2,1)}) custom-call(bf16[128,3712]{1,0:T(8,128)(2,1)S(1)} %shard_map.64.refs_0_, bf16[128,80]{1,0:T(8,128)(2,1)S(1)} %get-tuple-element.32.refs_1_.refs_0_), custom_call_target="tpu_custom_call" | custom-call | tf_op jit(solution)/shard_map/pallas_call | solution.py:33
  37.6 0.0 collective-permute-done.4.refs_7_.refs_6_
  37.7 11.3 %collective-permute-done.7.refs_1_.refs_3_ = bf16[80,3712]{1,0:T(8,128)(2,1)S(1)} collective-permute-done((bf16[80,3712]{1,0:T(8,128)(2,1)S(1)}, bf16[80,3712]{1,0:T(8,128)(2,1)S(1)}, u32[]{:S(2)}, u32[]{:S(2)}) %collective-permute-start.7) | collective-permute-done | bytes 593952 | tf_op jit(solution)/shard_map/ppermute | solution.py:256
  49.0 9.6 %shard_map.67 = (bf16[80,3584]{1,0:T(8,128)(2,1)S(1)}, bf16[80,3584]{1,0:T(8,128)(2,1)S(1)}) custom-call(bf16[80,3712]{1,0:T(8,128)(2,1)S(1)} %get-tuple-element.36.refs_0_, bf16[80,3712]{1,0:T(8,128)(2,1)S(1)} %collective-permute-done.7.refs_1_.refs_3_, bf16[3584,512]{1,0:T(8,128)(2,1)} %bitcast.6, bf16[3584,512]{1,0:T(8,128)(2,1)} %bitcast.12, ...), custom_call_target="tpu_custom_call" | custom-call | bytes 67108864 | tf_op jit(solution)/shard_map/pallas_call | solution.py:33
  58.6 0.0 collective-permute-done.5.refs_0_
  58.6 0.0 collective-permute-done.6.refs_1_
  58.6 0.1 shard_map.68
  58.8 0.7 collective-permute-start.10
  59.5 1.3 collective-permute-start.9
  60.8 1.6 collective-permute-start.11
  62.4 1.0 shard_map.69
  63.4 0.6 collective-permute-start.8
  64.0 12.8 %collective-permute-done.11.refs_3_ = bf16[80,3584]{1,0:T(8,128)(2,1)S(1)} collective-permute-done((bf16[80,3584]{1,0:T(8,128)(2,1)S(1)}, bf16[80,3584]{1,0:T(8,128)(2,1)S(1)}, u32[]{:S(2)}, u32[]{:S(2)}) %collective-permute-start.11) | collective-permute-done | bytes 573472 | tf_op jit(solution)/shard_map/ppermute | solution.py:256
  76.8 0.6 shard_map.70.refs_4_
  77.4 0.7 collective-permute-start.14
  78.1 5.2 %collective-permute-start.15 = (bf16[128,3584]{1,0:T(8,128)(2,1)S(1)}, bf16[128,3584]{1,0:T(8,128)(2,1)S(1)}, u32[]{:S(2)}, u32[]{:S(2)}) collective-permute-start(bf16[128,3584]{1,0:T(8,128)(2,1)S(1)} %shard_map.70.refs_4_), channel_id=1, source_target_pairs={{0,4},{2,6},{4,8},{6,10},{1,5},{3,7},{5,9},{7,11},{16,20},{18,22},... | collective-permute-start | bytes 2752520 | tf_op jit(solution)/shard_map/ppermute | solution.py:253
  83.4 0.0 collective-permute-done.9.refs_1_
  83.4 1.2 shard_map.71
  84.6 1.6 collective-permute-start.13
  86.2 3.3 %collective-permute-done.8.refs_1_ = bf16[80,3712]{1,0:T(8,128)(2,1)S(1)} collective-permute-done((bf16[80,3712]{1,0:T(8,128)(2,1)S(1)}, bf16[80,3712]{1,0:T(8,128)(2,1)S(1)}, u32[]{:S(2)}, u32[]{:S(2)}) %collective-permute-start.8) | collective-permute-done | bytes 593952 | tf_op jit(solution)/shard_map/ppermute | solution.py:256
  89.5 9.6 %shard_map.72 = (bf16[80,3584]{1,0:T(8,128)(2,1)S(1)}, bf16[80,3584]{1,0:T(8,128)(2,1)S(1)}) custom-call(bf16[80,3712]{1,0:T(8,128)(2,1)S(1)} %get-tuple-element.43.refs_0_, bf16[80,3712]{1,0:T(8,128)(2,1)S(1)} %collective-permute-done.8.refs_1_, bf16[3584,512]{1,0:T(8,128)(2,1)} %bitcast.7, bf16[3584,512]{1,0:T(8,128)(2,1)} %bitcast.13, ...), custom_call_target="tpu_custom_call" | custom-call | tf_op jit(solution)/shard_map/pallas_call | solution.py:33
  99.2 1.6 collective-permute-start.12
  100.7 1.5 collective-permute-done.13.refs_1_
  102.2 9.6 %shard_map.73 = (bf16[80,3584]{1,0:T(8,128)(2,1)S(1)}, bf16[80,3584]{1,0:T(8,128)(2,1)S(1)}) custom-call(bf16[80,3712]{1,0:T(8,128)(2,1)S(1)} %get-tuple-element.50.refs_0_, bf16[80,3712]{1,0:T(8,128)(2,1)S(1)} %collective-permute-done.13.refs_1_, bf16[3584,512]{1,0:T(8,128)(2,1)} %bitcast.8, bf16[3584,512]{1,0:T(8,128)(2,1)} %bitcast.14, ...), custom_call_target="tpu_custom_call" | custom-call | tf_op jit(solution)/shard_map/pallas_call | solution.py:33
  111.9 0.0 copy-start
  111.9 1.6 collective-permute-start.17
  113.5 0.0 collective-permute-done.14.refs_5_.refs_0_
  113.5 0.0 collective-permute-done.15.refs_6_.refs_1_
  113.5 0.8 collective-permute-done.12.refs_3_
  114.3 0.6 shard_map.74.refs_7_
  114.9 4.1 %collective-permute-start.19 = (bf16[128,3584]{1,0:T(8,128)(2,1)S(1)}, bf16[128,3584]{1,0:T(8,128)(2,1)S(1)}, u32[]{:S(2)}, u32[]{:S(2)}) collective-permute-start(bf16[128,3584]{1,0:T(8,128)(2,1)S(1)} %shard_map.74.refs_7_), channel_id=1, source_target_pairs={{0,8},{2,10},{4,0},{6,2},{8,12},{10,14},{12,4},{14,6},{1,9},{3,11}... | collective-permute-start | bytes 2752520 | tf_op jit(solution)/shard_map/ppermute | solution.py:253
  119.0 1.5 collective-permute-start.16
  120.6 8.7 %shard_map.75.refs_4_.refs_2_ = bf16[80,3584]{1,0:T(8,128)(2,1)S(1)} custom-call(bf16[80,3712]{1,0:T(8,128)(2,1)S(1)} %copy-done, bf16[3584,512]{1,0:T(8,128)(2,1)} %bitcast.9, bf16[3584,512]{1,0:T(8,128)(2,1)} %bitcast.15, bf16[512,3584]{1,0:T(8,128)(2,1)} %bitcast.21, bf16[3584,512]{1,0:T(8,128)(2,1)S(1)} %collective-permute-done.2.refs_2_.refs_5_.refs_4_, ...), custom_call_target="tpu_custom_call" | custom-call | tf_op jit(solution)/shard_map/pallas_call | solution.py:33
  129.2 0.0 collective-permute-done.17.refs_3_
  129.2 0.6 shard_map.76
  129.9 3.3 %collective-permute-start.20 = (bf16[128,1792]{1,0:T(8,128)(2,1)S(1)}, bf16[128,1792]{1,0:T(8,128)(2,1)S(1)}, u32[]{:S(2)}, u32[]{:S(2)}) collective-permute-start(bf16[128,1792]{1,0:T(8,128)(2,1)S(1)} %get-tuple-element.57), channel_id=1, source_target_pairs={{0,4},{2,6},{12,8},{14,10},{1,5},{3,7},{13,9},{15,11},{16,20},{18,... | collective-permute-start | bytes 1376264 | tf_op jit(solution)/shard_map/ppermute | solution.py:253
  133.2 1.3 collective-permute-start.22
  134.5 2.5 %collective-permute-done.16.refs_0_ = bf16[80,3712]{1,0:T(8,128)(2,1)S(1)} collective-permute-done((bf16[80,3712]{1,0:T(8,128)(2,1)S(1)}, bf16[80,3712]{1,0:T(8,128)(2,1)S(1)}, u32[]{:S(2)}, u32[]{:S(2)}) %collective-permute-start.16) | collective-permute-done | bytes 593952 | tf_op jit(solution)/shard_map/ppermute | solution.py:256
  137.0 8.7 %shard_map.77.refs_3_ = bf16[80,3584]{1,0:T(8,128)(2,1)S(1)} custom-call(bf16[80,3712]{1,0:T(8,128)(2,1)S(1)} %collective-permute-done.16.refs_0_, bf16[3584,512]{1,0:T(8,128)(2,1)} %bitcast.10, bf16[3584,512]{1,0:T(8,128)(2,1)} %bitcast.16, bf16[512,3584]{1,0:T(8,128)(2,1)} %bitcast.22, ...), custom_call_target="tpu_custom_call" | custom-call | tf_op jit(solution)/shard_map/pallas_call | solution.py:33
  145.7 1.6 collective-permute-start.18
  147.3 0.3 shard_map.78.refs_2_.refs_4_
  147.6 0.1 collective-permute-done.20.refs_1_
  147.7 0.1 shard_map.79.refs_2_
  147.8 1.3 collective-permute-start.21
  149.1 3.5 %collective-permute-done.22.refs_1_ = bf16[128,1792]{1,0:T(8,128)(2,1)S(1)} collective-permute-done((bf16[128,1792]{1,0:T(8,128)(2,1)S(1)}, bf16[128,1792]{1,0:T(8,128)(2,1)S(1)}, u32[]{:S(2)}, u32[]{:S(2)}) %collective-permute-start.22) | collective-permute-done | bytes 458784 | tf_op jit(solution)/shard_map/ppermute | solution.py:253
  152.6 0.1 shard_map.80.refs_1_
  152.7 1.3 collective-permute-start.23
  154.0 10.0 %collective-permute-done.21.refs_0_ = bf16[128,1792]{1,0:T(8,128)(2,1)S(1)} collective-permute-done((bf16[128,1792]{1,0:T(8,128)(2,1)S(1)}, bf16[128,1792]{1,0:T(8,128)(2,1)S(1)}, u32[]{:S(2)}, u32[]{:S(2)}) %collective-permute-start.21) | collective-permute-done | bytes 458784 | tf_op jit(solution)/shard_map/ppermute | solution.py:253
  164.1 0.0 collective-permute-done.18.refs_3_
  164.1 0.6 shard_map.82.total
  164.7 4.3 %collective-permute-done.23.refs_1_ = bf16[128,1792]{1,0:T(8,128)(2,1)S(1)} collective-permute-done((bf16[128,1792]{1,0:T(8,128)(2,1)S(1)}, bf16[128,1792]{1,0:T(8,128)(2,1)S(1)}, u32[]{:S(2)}, u32[]{:S(2)}) %collective-permute-start.23) | collective-permute-done | bytes 458784 | tf_op jit(solution)/shard_map/ppermute | solution.py:253
  169.1 1.1 shard_map.83
  (8 shorter events, 0.0 us)
Async XLA Ops:
  0.0 33.1 %collective-permute-start.2 = (bf16[3584,512]{1,0:T(8,128)(2,1)}, bf16[3584,512]{1,0:T(8,128)(2,1)S(1)}, u32[]{:S(2)}, u32[]{:S(2)}) collective-permute-start(bf16[3584,512]{1,0:T(8,128)(2,1)} %bitcast.5), channel_id=1, source_target_pairs={{0,1},{1,0},{2,3},{3,2},{4,5},{5,4},{6,7},{7,6},{8,9},{9,8},{10,11... | collective-permute-start | bytes 11010056 | tf_op jit(solution)/shard_map/ppermute | solution.py:249
  0.5 37.2 %collective-permute-start.3 = (bf16[3584,512]{1,0:T(8,128)(2,1)}, bf16[3584,512]{1,0:T(8,128)(2,1)S(1)}, u32[]{:S(2)}, u32[]{:S(2)}) collective-permute-start(bf16[3584,512]{1,0:T(8,128)(2,1)} %bitcast.11), channel_id=1, source_target_pairs={{0,1},{1,0},{2,3},{3,2},{4,5},{5,4},{6,7},{7,6},{8,9},{9,8},{10,11... | collective-permute-start | bytes 11010056 | tf_op jit(solution)/shard_map/ppermute | solution.py:249
  0.5 37.1 %collective-permute-start.4 = (bf16[512,3584]{1,0:T(8,128)(2,1)}, bf16[512,3584]{1,0:T(8,128)(2,1)S(1)}, u32[]{:S(2)}, u32[]{:S(2)}) collective-permute-start(bf16[512,3584]{1,0:T(8,128)(2,1)} %bitcast.17), channel_id=1, source_target_pairs={{0,1},{1,0},{2,3},{3,2},{4,5},{5,4},{6,7},{7,6},{8,9},{9,8},{10,11... | collective-permute-start | bytes 11010056 | tf_op jit(solution)/shard_map/ppermute | solution.py:249
  2.2 25.5 %collective-permute-start.1 = (bf16[128,3712]{1,0:T(8,128)(2,1)S(1)}, bf16[128,3712]{1,0:T(8,128)(2,1)S(1)}, u32[]{:S(2)}, u32[]{:S(2)}) collective-permute-start(bf16[128,3712]{1,0:T(8,128)(2,1)S(1)} %shard_map.64.refs_0_), channel_id=1, source_target_pairs={{0,4},{2,6},{4,8},{6,10},{8,12},{10,14},{1,5},{3,7},{5,9},{7,11},{... | collective-permute-start | bytes 2850824 | tf_op jit(solution)/shard_map/ppermute | solution.py:253
  6.8 25.1 %collective-permute-start = (bf16[128,3712]{1,0:T(8,128)(2,1)S(1)}, bf16[128,3712]{1,0:T(8,128)(2,1)S(1)}, u32[]{:S(2)}, u32[]{:S(2)}) collective-permute-start(bf16[128,3712]{1,0:T(8,128)(2,1)S(1)} %shard_map.64.refs_0_), channel_id=1, source_target_pairs={{4,0},{6,2},{8,4},{10,6},{12,8},{14,10},{5,1},{7,3},{9,5},{11,7},{... | collective-permute-start | bytes 2850824 | tf_op jit(solution)/shard_map/ppermute | solution.py:253
  27.7 31.0 %collective-permute-start.5 = (bf16[128,3712]{1,0:T(8,128)(2,1)S(1)}, bf16[128,3712]{1,0:T(8,128)(2,1)S(1)}, u32[]{:S(2)}, u32[]{:S(2)}) collective-permute-start(bf16[128,3712]{1,0:T(8,128)(2,1)S(1)} %collective-permute-done.1.refs_1_.refs_2_), channel_id=1, source_target_pairs={{4,8},{6,10},{8,12},{10,14},{5,9},{7,11},{9,13},{11,15},{20,24},{2... | collective-permute-start | bytes 2850824 | tf_op jit(solution)/shard_map/ppermute | solution.py:253
  31.8 26.8 %collective-permute-start.6 = (bf16[128,3712]{1,0:T(8,128)(2,1)S(1)}, bf16[128,3712]{1,0:T(8,128)(2,1)S(1)}, u32[]{:S(2)}, u32[]{:S(2)}) collective-permute-start(bf16[128,3712]{1,0:T(8,128)(2,1)S(1)} %collective-permute-done.refs_0_), channel_id=1, source_target_pairs={{4,0},{6,2},{8,4},{10,6},{5,1},{7,3},{9,5},{11,7},{20,16},{22,18},... | collective-permute-start | bytes 2850824 | tf_op jit(solution)/shard_map/ppermute | solution.py:253
  34.2 14.8 %collective-permute-start.7 = (bf16[80,3712]{1,0:T(8,128)(2,1)S(1)}, bf16[80,3712]{1,0:T(8,128)(2,1)S(1)}, u32[]{:S(2)}, u32[]{:S(2)}) collective-permute-start(bf16[80,3712]{1,0:T(8,128)(2,1)S(1)} %get-tuple-element.37), channel_id=1, source_target_pairs={{0,2},{2,0},{4,6},{6,4},{8,10},{10,8},{12,14},{14,12},{1,3},{3,1},... | collective-permute-start | bytes 1781768 | tf_op jit(solution)/shard_map/ppermute | solution.py:256
  58.8 24.6 %collective-permute-start.10 = (bf16[128,3712]{1,0:T(8,128)(2,1)S(1)}, bf16[128,3712]{1,0:T(8,128)(2,1)S(1)}, u32[]{:S(2)}, u32[]{:S(2)}) collective-permute-start(bf16[128,3712]{1,0:T(8,128)(2,1)S(1)} %get-tuple-element.40.refs_3_.refs_2_), channel_id=1, source_target_pairs={{8,12},{10,14},{9,13},{11,15},{24,28},{26,30},{25,29},{27,31}} | collective-permute-start | bytes 2850824 | tf_op jit(solution)/shard_map/ppermute | solution.py:253
  59.5 23.9 %collective-permute-start.9 = (bf16[128,3712]{1,0:T(8,128)(2,1)S(1)}, bf16[128,3712]{1,0:T(8,128)(2,1)S(1)}, u32[]{:S(2)}, u32[]{:S(2)}) collective-permute-start(bf16[128,3712]{1,0:T(8,128)(2,1)S(1)} %get-tuple-element.39.refs_1_.refs_0_), channel_id=1, source_target_pairs={{4,0},{6,2},{5,1},{7,3},{20,16},{22,18},{21,17},{23,19}} | collective-permute-start | bytes 2850824 | tf_op jit(solution)/shard_map/ppermute | solution.py:253
  60.8 16.0 %collective-permute-start.11 = (bf16[80,3584]{1,0:T(8,128)(2,1)S(1)}, bf16[80,3584]{1,0:T(8,128)(2,1)S(1)}, u32[]{:S(2)}, u32[]{:S(2)}) collective-permute-start(bf16[80,3584]{1,0:T(8,128)(2,1)S(1)} %get-tuple-element.46), channel_id=1, source_target_pairs={{0,2},{2,0},{4,6},{6,4},{8,10},{10,8},{12,14},{14,12},{1,3},{3,1},... | collective-permute-start | bytes 1720328 | tf_op jit(solution)/shard_map/ppermute | solution.py:256
  63.4 26.1 %collective-permute-start.8 = (bf16[80,3712]{1,0:T(8,128)(2,1)S(1)}, bf16[80,3712]{1,0:T(8,128)(2,1)S(1)}, u32[]{:S(2)}, u32[]{:S(2)}) collective-permute-start(bf16[80,3712]{1,0:T(8,128)(2,1)S(1)} %get-tuple-element.44), channel_id=1, source_target_pairs={{0,2},{2,0},{4,6},{6,4},{8,10},{10,8},{12,14},{14,12},{1,3},{3,1},... | collective-permute-start | bytes 1781768 | tf_op jit(solution)/shard_map/ppermute | solution.py:256
  77.4 36.1 %collective-permute-start.14 = (bf16[128,3584]{1,0:T(8,128)(2,1)S(1)}, bf16[128,3584]{1,0:T(8,128)(2,1)S(1)}, u32[]{:S(2)}, u32[]{:S(2)}) collective-permute-start(bf16[128,3584]{1,0:T(8,128)(2,1)S(1)} %shard_map.70.refs_4_), channel_id=1, source_target_pairs={{8,4},{10,6},{12,8},{14,10},{9,5},{11,7},{13,9},{15,11},{24,20},{2... | collective-permute-start | bytes 2752520 | tf_op jit(solution)/shard_map/ppermute | solution.py:253
  78.1 35.4 %collective-permute-start.15 = (bf16[128,3584]{1,0:T(8,128)(2,1)S(1)}, bf16[128,3584]{1,0:T(8,128)(2,1)S(1)}, u32[]{:S(2)}, u32[]{:S(2)}) collective-permute-start(bf16[128,3584]{1,0:T(8,128)(2,1)S(1)} %shard_map.70.refs_4_), channel_id=1, source_target_pairs={{0,4},{2,6},{4,8},{6,10},{1,5},{3,7},{5,9},{7,11},{16,20},{18,22},... | collective-permute-start | bytes 2752520 | tf_op jit(solution)/shard_map/ppermute | solution.py:253
  84.6 17.6 %collective-permute-start.13 = (bf16[80,3712]{1,0:T(8,128)(2,1)S(1)}, bf16[80,3712]{1,0:T(8,128)(2,1)S(1)}, u32[]{:S(2)}, u32[]{:S(2)}) collective-permute-start(bf16[80,3712]{1,0:T(8,128)(2,1)S(1)} %get-tuple-element.51), channel_id=1, source_target_pairs={{0,2},{2,0},{4,6},{6,4},{8,10},{10,8},{12,14},{14,12},{1,3},{3,1},... | collective-permute-start | bytes 1781768 | tf_op jit(solution)/shard_map/ppermute | solution.py:256
  99.2 15.2 %collective-permute-start.12 = (bf16[80,3584]{1,0:T(8,128)(2,1)S(1)}, bf16[80,3584]{1,0:T(8,128)(2,1)S(1)}, u32[]{:S(2)}, u32[]{:S(2)}) collective-permute-start(bf16[80,3584]{1,0:T(8,128)(2,1)S(1)} %get-tuple-element.49), channel_id=1, source_target_pairs={{0,2},{2,0},{4,6},{6,4},{8,10},{10,8},{12,14},{14,12},{1,3},{3,1},... | collective-permute-start | bytes 1720328 | tf_op jit(solution)/shard_map/ppermute | solution.py:256
  111.9 7.1 %copy-start.1 = (bf16[80,3712]{1,0:T(8,128)(2,1)S(1)}, bf16[80,3712]{1,0:T(8,128)(2,1)}, u32[]{:S(2)}) copy-start(bf16[80,3712]{1,0:T(8,128)(2,1)} %get-tuple-element.53) | copy-start | bytes 1781764
  111.9 8.7 %copy-start = (bf16[80,3712]{1,0:T(8,128)(2,1)S(1)}, bf16[80,3712]{1,0:T(8,128)(2,1)}, u32[]{:S(2)}) copy-start(bf16[80,3712]{1,0:T(8,128)(2,1)} %get-tuple-element.35.refs_0_) | copy-start | bytes 1781764
  111.9 17.3 %collective-permute-start.17 = (bf16[80,3584]{1,0:T(8,128)(2,1)S(1)}, bf16[80,3584]{1,0:T(8,128)(2,1)S(1)}, u32[]{:S(2)}, u32[]{:S(2)}) collective-permute-start(bf16[80,3584]{1,0:T(8,128)(2,1)S(1)} %get-tuple-element.55), channel_id=1, source_target_pairs={{0,2},{2,0},{4,6},{6,4},{8,10},{10,8},{12,14},{14,12},{1,3},{3,1},... | collective-permute-start | bytes 1720328 | tf_op jit(solution)/shard_map/ppermute | solution.py:256
  114.9 32.3 %collective-permute-start.19 = (bf16[128,3584]{1,0:T(8,128)(2,1)S(1)}, bf16[128,3584]{1,0:T(8,128)(2,1)S(1)}, u32[]{:S(2)}, u32[]{:S(2)}) collective-permute-start(bf16[128,3584]{1,0:T(8,128)(2,1)S(1)} %shard_map.74.refs_7_), channel_id=1, source_target_pairs={{0,8},{2,10},{4,0},{6,2},{8,12},{10,14},{12,4},{14,6},{1,9},{3,11}... | collective-permute-start | bytes 2752520 | tf_op jit(solution)/shard_map/ppermute | solution.py:253
  119.0 18.0 %collective-permute-start.16 = (bf16[80,3712]{1,0:T(8,128)(2,1)S(1)}, bf16[80,3712]{1,0:T(8,128)(2,1)S(1)}, u32[]{:S(2)}, u32[]{:S(2)}) collective-permute-start(bf16[80,3712]{1,0:T(8,128)(2,1)S(1)} %copy-done.1), channel_id=1, source_target_pairs={{0,2},{2,0},{4,6},{6,4},{8,10},{10,8},{12,14},{14,12},{1,3},{3,1},... | collective-permute-start | bytes 1781768 | tf_op jit(solution)/shard_map/ppermute | solution.py:256
  129.9 17.8 %collective-permute-start.20 = (bf16[128,1792]{1,0:T(8,128)(2,1)S(1)}, bf16[128,1792]{1,0:T(8,128)(2,1)S(1)}, u32[]{:S(2)}, u32[]{:S(2)}) collective-permute-start(bf16[128,1792]{1,0:T(8,128)(2,1)S(1)} %get-tuple-element.57), channel_id=1, source_target_pairs={{0,4},{2,6},{12,8},{14,10},{1,5},{3,7},{13,9},{15,11},{16,20},{18,... | collective-permute-start | bytes 1376264 | tf_op jit(solution)/shard_map/ppermute | solution.py:253
  133.2 19.4 %collective-permute-start.22 = (bf16[128,1792]{1,0:T(8,128)(2,1)S(1)}, bf16[128,1792]{1,0:T(8,128)(2,1)S(1)}, u32[]{:S(2)}, u32[]{:S(2)}) collective-permute-start(bf16[128,1792]{1,0:T(8,128)(2,1)S(1)} %get-tuple-element.58), channel_id=1, source_target_pairs={{0,4},{2,6},{12,8},{14,10},{1,5},{3,7},{13,9},{15,11},{16,20},{18,... | collective-permute-start | bytes 1376264 | tf_op jit(solution)/shard_map/ppermute | solution.py:253
  145.7 18.4 %collective-permute-start.18 = (bf16[80,3584]{1,0:T(8,128)(2,1)S(1)}, bf16[80,3584]{1,0:T(8,128)(2,1)S(1)}, u32[]{:S(2)}, u32[]{:S(2)}) collective-permute-start(bf16[80,3584]{1,0:T(8,128)(2,1)S(1)} %shard_map.77.refs_3_), channel_id=1, source_target_pairs={{0,2},{2,0},{4,6},{6,4},{8,10},{10,8},{12,14},{14,12},{1,3},{3,1},... | collective-permute-start | bytes 1720328 | tf_op jit(solution)/shard_map/ppermute | solution.py:256
  147.8 16.3 %collective-permute-start.21 = (bf16[128,1792]{1,0:T(8,128)(2,1)S(1)}, bf16[128,1792]{1,0:T(8,128)(2,1)S(1)}, u32[]{:S(2)}, u32[]{:S(2)}) collective-permute-start(bf16[128,1792]{1,0:T(8,128)(2,1)S(1)} %shard_map.79.refs_2_), channel_id=1, source_target_pairs={{4,12},{6,14},{8,0},{10,2},{5,13},{7,15},{9,1},{11,3},{20,28},{22,... | collective-permute-start | bytes 1376264 | tf_op jit(solution)/shard_map/ppermute | solution.py:253
  152.7 16.3 %collective-permute-start.23 = (bf16[128,1792]{1,0:T(8,128)(2,1)S(1)}, bf16[128,1792]{1,0:T(8,128)(2,1)S(1)}, u32[]{:S(2)}, u32[]{:S(2)}) collective-permute-start(bf16[128,1792]{1,0:T(8,128)(2,1)S(1)} %shard_map.80.refs_1_), channel_id=1, source_target_pairs={{4,12},{6,14},{8,0},{10,2},{5,13},{7,15},{9,1},{11,3},{20,28},{22,... | collective-permute-start | bytes 1376264 | tf_op jit(solution)/shard_map/ppermute | solution.py:253

commit v19 on v18

--- a/solution.py
+++ b/solution.py
@@ -385,7 +385,8 @@
     )
     for step in range(3, places):
         relay(step)
-    do_pick(2)
+    do_pick(2, after=[picks[0][2]])
+    do_expert(0)
     do_spread(1, cost=64 * MIB)
     do_pick(3)
     do_expert(2)
@@ -394,10 +395,7 @@
         do_spread(slot - 1, after=returned[slot - 3])
         if slot + 1 < places:
             do_pick(slot + 1)
-    (own_out,) = ordered(expert, picks[0][1:2])
     do_spread(places - 1)
-    (other_out,) = ordered(expert, picks[0][2:])
-    outs[0] = own_out, across(other_out)
     near = returned.pop(places - 3)
     (summed,) = ordered(call_sum, [*returned.pop(0), *near] if places > 3 else near, cost=128 * MIB)
     homes = [(q, origin(q, final)) for _, q in hops]

time: 171 us -> 166 us (0.971)
  Pallas kernels: 56.9 us -> 49.4 us
  waiting for transfers between devices: 73.3 us -> 75.8 us
    ppermute x13, waiting for transfers between devices: 41 us -> 51.2 us  [along(): return lax.ppermute(block, 'node', moves)]
    ppermute x8, waiting for transfers between devices: 32.3 us -> 24.5 us  [across(): return lax.ppermute(block, 'node', [(n, n ^ 1) for n in range(experts)])]
    pallas_call x20 -> x19, Pallas kernels: 56.9 us -> 49.4 us  [call(): pl.pallas_call(body, out_shape=outs, in_specs=specs, out_specs=out_specs...]
  transfers between devices with their start and end apart: 24 -> 24, of which waited for: 12 -> 13; matrix products, arithmetic and copies ran while one was open for 0% -> 0% of each run, Pallas kernels for 33% -> 29%
where the time goes in v19:
time: 166 us; the launch traced here: 165 us
  waiting for transfers between devices  75.8 us (46%)
  Pallas kernels  49.4 us (30%)
  starting transfers between devices  40 us (24%)
    ppermute x13, waiting for transfers between devices, along(): return lax.ppermute(block, 'node', moves)  51.2 us
    pallas_call x19, Pallas kernels, call(): pl.pallas_call(body, out_shape=outs, in_specs=specs, out_specs=out_specs...  49.4 us
    ppermute x13, starting transfers between devices, along(): return lax.ppermute(block, 'node', moves)  28.3 us
    ppermute x8, waiting for transfers between devices, across(): return lax.ppermute(block, 'node', [(n, n ^ 1) for n in range(experts)])  24.5 us
    ppermute x8, starting transfers between devices, across(): return lax.ppermute(block, 'node', [(n, n ^ 1) for n in range(experts)])  10.7 us
  transfers between devices with their start and end apart: 24, of which 13 were waited for; matrix products, arithmetic and copies ran while one was open for 0% of the time, Pallas kernels for 29%

profile of v19, /device:TPU:0, one launch (start us, length us, event | category | flops | bytes accessed | tf_op | source)
XLA Modules:
  0.0 165.5 jit_solution(8626718038772524798)
XLA Ops:
  0.0 0.5 collective-permute-start.2
  0.5 0.1 collective-permute-start.4
  0.5 0.5 collective-permute-start.5
  1.0 1.2 shard_map.64.refs_0_
  2.2 4.5 %collective-permute-start.1 = (bf16[128,3712]{1,0:T(8,128)(2,1)S(1)}, bf16[128,3712]{1,0:T(8,128)(2,1)S(1)}, u32[]{:S(2)}, u32[]{:S(2)}) collective-permute-start(bf16[128,3712]{1,0:T(8,128)(2,1)S(1)} %shard_map.64.refs_0_), channel_id=1, source_target_pairs={{0,4},{2,6},{4,8},{6,10},{8,12},{10,14},{1,5},{3,7},{5,9},{7,11},{... | collective-permute-start | bytes 2850824 | tf_op jit(solution)/shard_map/ppermute | solution.py:253
  6.8 1.3 collective-permute-start
  8.1 19.6 %collective-permute-done.1.refs_1_.refs_2_ = bf16[128,3712]{1,0:T(8,128)(2,1)S(1)} collective-permute-done((bf16[128,3712]{1,0:T(8,128)(2,1)S(1)}, bf16[128,3712]{1,0:T(8,128)(2,1)S(1)}, u32[]{:S(2)}, u32[]{:S(2)}) %collective-permute-start.1) | collective-permute-done | bytes 950304 | tf_op jit(solution)/shard_map/ppermute | solution.py:253
  27.7 0.7 collective-permute-start.6
  28.4 3.5 %collective-permute-done.refs_0_ = bf16[128,3712]{1,0:T(8,128)(2,1)S(1)} collective-permute-done((bf16[128,3712]{1,0:T(8,128)(2,1)S(1)}, bf16[128,3712]{1,0:T(8,128)(2,1)S(1)}, u32[]{:S(2)}, u32[]{:S(2)}) %collective-permute-start) | collective-permute-done | bytes 950304 | tf_op jit(solution)/shard_map/ppermute | solution.py:253
  31.8 1.3 collective-permute-start.7
  33.1 0.0 collective-permute-done.2.refs_2_.refs_5_
  33.1 1.0 shard_map.65
  34.2 1.6 collective-permute-start.8
  35.8 1.9 %shard_map.66 = (bf16[128,80]{1,0:T(8,128)(2,1)S(1)}, bf16[128,80]{1,0:T(8,128)(2,1)S(1)}, bf16[80,3712]{1,0:T(8,128)(2,1)}, bf16[80,3712]{1,0:T(8,128)(2,1)}) custom-call(bf16[128,3712]{1,0:T(8,128)(2,1)S(1)} %shard_map.64.refs_0_, bf16[128,80]{1,0:T(8,128)(2,1)S(1)} %get-tuple-element.34.refs_1_.refs_0_), custom_call_target="tpu_custom_call" | custom-call | tf_op jit(solution)/shard_map/pallas_call | solution.py:33
  37.6 0.6 collective-permute-start.3
  38.2 0.0 collective-permute-done.5.refs_7_
  38.2 12.4 %collective-permute-done.8.refs_1_.refs_3_ = bf16[80,3712]{1,0:T(8,128)(2,1)S(1)} collective-permute-done((bf16[80,3712]{1,0:T(8,128)(2,1)S(1)}, bf16[80,3712]{1,0:T(8,128)(2,1)S(1)}, u32[]{:S(2)}, u32[]{:S(2)}) %collective-permute-start.8) | collective-permute-done | bytes 593952 | tf_op jit(solution)/shard_map/ppermute | solution.py:256
  50.6 9.6 %shard_map.67 = (bf16[80,3584]{1,0:T(8,128)(2,1)S(1)}, bf16[80,3584]{1,0:T(8,128)(2,1)S(1)}) custom-call(bf16[80,3712]{1,0:T(8,128)(2,1)S(1)} %get-tuple-element.39.refs_0_, bf16[80,3712]{1,0:T(8,128)(2,1)S(1)} %collective-permute-done.8.refs_1_.refs_3_, bf16[3584,512]{1,0:T(8,128)(2,1)} %bitcast.6, bf16[3584,512]{1,0:T(8,128)(2,1)} %bitcast.11, ...), custom_call_target="tpu_custom_call" | custom-call | bytes 67108864 | tf_op jit(solution)/shard_map/pallas_call | solution.py:33
  60.2 0.0 collective-permute-done.6.refs_0_
  60.2 0.0 collective-permute-done.7.refs_1_
  60.3 0.0 copy-start
  60.3 0.1 shard_map.68
  60.4 1.4 collective-permute-start.14
  61.8 0.7 collective-permute-start.15
  62.6 1.6 collective-permute-start.10
  64.2 1.2 shard_map.69
  65.4 0.6 collective-permute-start.13
  65.9 9.6 %shard_map.70 = (bf16[80,3584]{1,0:T(8,128)(2,1)S(1)}, bf16[80,3584]{1,0:T(8,128)(2,1)S(1)}) custom-call(bf16[80,3712]{1,0:T(8,128)(2,1)S(1)} %copy-done, bf16[80,3712]{1,0:T(8,128)(2,1)S(1)} %collective-permute-done.3.refs_5_.refs_1_, bf16[3584,512]{1,0:T(8,128)(2,1)} %bitcast.7, bf16[3584,512]{1,0:T(8,128)(2,1)} %bitcast.12, bf16[512,3584]{1,0:T(8,128)(2,1)} %bitcast.17, ...), custom_call_target="tpu_custom_call" | custom-call | tf_op jit(solution)/shard_map/pallas_call | solution.py:33
  75.6 3.0 %collective-permute-done.10.refs_3_ = bf16[80,3584]{1,0:T(8,128)(2,1)S(1)} collective-permute-done((bf16[80,3584]{1,0:T(8,128)(2,1)S(1)}, bf16[80,3584]{1,0:T(8,128)(2,1)S(1)}, u32[]{:S(2)}, u32[]{:S(2)}) %collective-permute-start.10) | collective-permute-done | bytes 573472 | tf_op jit(solution)/shard_map/ppermute | solution.py:256
  78.5 0.6 shard_map.71.refs_4_
  79.2 0.7 collective-permute-start.11
  79.9 5.2 %collective-permute-start.12 = (bf16[128,3584]{1,0:T(8,128)(2,1)S(1)}, bf16[128,3584]{1,0:T(8,128)(2,1)S(1)}, u32[]{:S(2)}, u32[]{:S(2)}) collective-permute-start(bf16[128,3584]{1,0:T(8,128)(2,1)S(1)} %shard_map.71.refs_4_), channel_id=1, source_target_pairs={{0,4},{2,6},{4,8},{6,10},{1,5},{3,7},{5,9},{7,11},{16,20},{18,22},... | collective-permute-start | bytes 2752520 | tf_op jit(solution)/shard_map/ppermute | solution.py:253
  85.1 0.0 collective-permute-done.15.refs_3_
  85.2 1.3 shard_map.72
  86.4 1.6 collective-permute-start.17
  88.0 3.3 %collective-permute-done.13.refs_1_ = bf16[80,3712]{1,0:T(8,128)(2,1)S(1)} collective-permute-done((bf16[80,3712]{1,0:T(8,128)(2,1)S(1)}, bf16[80,3712]{1,0:T(8,128)(2,1)S(1)}, u32[]{:S(2)}, u32[]{:S(2)}) %collective-permute-start.13) | collective-permute-done | bytes 593952 | tf_op jit(solution)/shard_map/ppermute | solution.py:256
  91.3 9.6 %shard_map.73 = (bf16[80,3584]{1,0:T(8,128)(2,1)S(1)}, bf16[80,3584]{1,0:T(8,128)(2,1)S(1)}) custom-call(bf16[80,3712]{1,0:T(8,128)(2,1)S(1)} %get-tuple-element.50.refs_0_, bf16[80,3712]{1,0:T(8,128)(2,1)S(1)} %collective-permute-done.13.refs_1_, bf16[3584,512]{1,0:T(8,128)(2,1)} %bitcast.8, bf16[3584,512]{1,0:T(8,128)(2,1)} %bitcast.13, ...), custom_call_target="tpu_custom_call" | custom-call | tf_op jit(solution)/shard_map/pallas_call | solution.py:33
  100.9 1.6 collective-permute-start.16
  102.5 1.5 collective-permute-done.17.refs_1_
  104.0 9.6 %shard_map.74 = (bf16[80,3584]{1,0:T(8,128)(2,1)S(1)}, bf16[80,3584]{1,0:T(8,128)(2,1)S(1)}) custom-call(bf16[80,3712]{1,0:T(8,128)(2,1)S(1)} %get-tuple-element.55.refs_0_, bf16[80,3712]{1,0:T(8,128)(2,1)S(1)} %collective-permute-done.17.refs_1_, bf16[3584,512]{1,0:T(8,128)(2,1)} %bitcast.9, bf16[3584,512]{1,0:T(8,128)(2,1)} %bitcast.14, ...), custom_call_target="tpu_custom_call" | custom-call | tf_op jit(solution)/shard_map/pallas_call | solution.py:33
  113.6 1.6 collective-permute-start.19
  115.2 0.0 collective-permute-done.11.refs_5_.refs_0_
  115.2 0.0 collective-permute-done.12.refs_6_.refs_1_
  115.2 0.9 collective-permute-done.16.refs_3_
  116.1 0.6 shard_map.75.refs_4_
  116.7 4.1 %collective-permute-start.18 = (bf16[128,3584]{1,0:T(8,128)(2,1)S(1)}, bf16[128,3584]{1,0:T(8,128)(2,1)S(1)}, u32[]{:S(2)}, u32[]{:S(2)}) collective-permute-start(bf16[128,3584]{1,0:T(8,128)(2,1)S(1)} %shard_map.75.refs_4_), channel_id=1, source_target_pairs={{0,8},{2,10},{4,0},{6,2},{8,12},{10,14},{12,4},{14,6},{1,9},{3,11}... | collective-permute-start | bytes 2752520 | tf_op jit(solution)/shard_map/ppermute | solution.py:253
  120.8 3.6 %collective-permute-done.19.refs_3_ = bf16[80,3584]{1,0:T(8,128)(2,1)S(1)} collective-permute-done((bf16[80,3584]{1,0:T(8,128)(2,1)S(1)}, bf16[80,3584]{1,0:T(8,128)(2,1)S(1)}, u32[]{:S(2)}, u32[]{:S(2)}) %collective-permute-start.19) | collective-permute-done | bytes 573472 | tf_op jit(solution)/shard_map/ppermute | solution.py:256
  124.4 0.6 shard_map.76
  125.0 4.4 %collective-permute-start.20 = (bf16[128,1792]{1,0:T(8,128)(2,1)S(1)}, bf16[128,1792]{1,0:T(8,128)(2,1)S(1)}, u32[]{:S(2)}, u32[]{:S(2)}) collective-permute-start(bf16[128,1792]{1,0:T(8,128)(2,1)S(1)} %get-tuple-element.61), channel_id=1, source_target_pairs={{0,4},{2,6},{12,8},{14,10},{1,5},{3,7},{13,9},{15,11},{16,20},{18,... | collective-permute-start | bytes 1376264 | tf_op jit(solution)/shard_map/ppermute | solution.py:253
  129.5 1.3 collective-permute-start.22
  130.8 1.6 collective-permute-start.9
  132.4 6.9 %collective-permute-done.18.refs_2_ = bf16[128,3584]{1,0:T(8,128)(2,1)S(1)} collective-permute-done((bf16[128,3584]{1,0:T(8,128)(2,1)S(1)}, bf16[128,3584]{1,0:T(8,128)(2,1)S(1)}, u32[]{:S(2)}, u32[]{:S(2)}) %collective-permute-start.18) | collective-permute-done | bytes 917536 | tf_op jit(solution)/shard_map/ppermute | solution.py:253
  139.2 0.3 shard_map.77.refs_2_.refs_4_
  139.6 6.9 %collective-permute-done.20.refs_1_ = bf16[128,1792]{1,0:T(8,128)(2,1)S(1)} collective-permute-done((bf16[128,1792]{1,0:T(8,128)(2,1)S(1)}, bf16[128,1792]{1,0:T(8,128)(2,1)S(1)}, u32[]{:S(2)}, u32[]{:S(2)}) %collective-permute-start.20) | collective-permute-done | bytes 458784 | tf_op jit(solution)/shard_map/ppermute | solution.py:253
  146.5 0.1 shard_map.78.refs_2_
  146.6 1.3 collective-permute-start.21
  147.9 3.5 %collective-permute-done.22.refs_1_ = bf16[128,1792]{1,0:T(8,128)(2,1)S(1)} collective-permute-done((bf16[128,1792]{1,0:T(8,128)(2,1)S(1)}, bf16[128,1792]{1,0:T(8,128)(2,1)S(1)}, u32[]{:S(2)}, u32[]{:S(2)}) %collective-permute-start.22) | collective-permute-done | bytes 458784 | tf_op jit(solution)/shard_map/ppermute | solution.py:253
  151.4 0.1 shard_map.79.refs_1_
  151.5 1.3 collective-permute-start.23
  152.8 6.6 %collective-permute-done.21.refs_0_ = bf16[128,1792]{1,0:T(8,128)(2,1)S(1)} collective-permute-done((bf16[128,1792]{1,0:T(8,128)(2,1)S(1)}, bf16[128,1792]{1,0:T(8,128)(2,1)S(1)}, u32[]{:S(2)}, u32[]{:S(2)}) %collective-permute-start.21) | collective-permute-done | bytes 458784 | tf_op jit(solution)/shard_map/ppermute | solution.py:253
  159.5 0.0 collective-permute-done.9.refs_3_
  159.5 0.6 shard_map.81.total
  160.1 4.2 %collective-permute-done.23.refs_1_ = bf16[128,1792]{1,0:T(8,128)(2,1)S(1)} collective-permute-done((bf16[128,1792]{1,0:T(8,128)(2,1)S(1)}, bf16[128,1792]{1,0:T(8,128)(2,1)S(1)}, u32[]{:S(2)}, u32[]{:S(2)}) %collective-permute-start.23) | collective-permute-done | bytes 458784 | tf_op jit(solution)/shard_map/ppermute | solution.py:253
  164.3 1.1 shard_map.82
  (5 shorter events, 0.0 us)
Async XLA Ops:
  0.0 33.1 %collective-permute-start.2 = (bf16[3584,512]{1,0:T(8,128)(2,1)}, bf16[3584,512]{1,0:T(8,128)(2,1)S(1)}, u32[]{:S(2)}, u32[]{:S(2)}) collective-permute-start(bf16[3584,512]{1,0:T(8,128)(2,1)} %bitcast.5), channel_id=1, source_target_pairs={{0,1},{1,0},{2,3},{3,2},{4,5},{5,4},{6,7},{7,6},{8,9},{9,8},{10,11... | collective-permute-start | bytes 11010056 | tf_op jit(solution)/shard_map/ppermute | solution.py:249
  0.5 37.2 %collective-permute-start.4 = (bf16[3584,512]{1,0:T(8,128)(2,1)}, bf16[3584,512]{1,0:T(8,128)(2,1)S(1)}, u32[]{:S(2)}, u32[]{:S(2)}) collective-permute-start(bf16[3584,512]{1,0:T(8,128)(2,1)} %bitcast.10), channel_id=1, source_target_pairs={{0,1},{1,0},{2,3},{3,2},{4,5},{5,4},{6,7},{7,6},{8,9},{9,8},{10,11... | collective-permute-start | bytes 11010056 | tf_op jit(solution)/shard_map/ppermute | solution.py:249
  0.5 37.7 %collective-permute-start.5 = (bf16[512,3584]{1,0:T(8,128)(2,1)}, bf16[512,3584]{1,0:T(8,128)(2,1)S(1)}, u32[]{:S(2)}, u32[]{:S(2)}) collective-permute-start(bf16[512,3584]{1,0:T(8,128)(2,1)} %bitcast.15), channel_id=1, source_target_pairs={{0,1},{1,0},{2,3},{3,2},{4,5},{5,4},{6,7},{7,6},{8,9},{9,8},{10,11... | collective-permute-start | bytes 11010056 | tf_op jit(solution)/shard_map/ppermute | solution.py:249
  2.2 25.5 %collective-permute-start.1 = (bf16[128,3712]{1,0:T(8,128)(2,1)S(1)}, bf16[128,3712]{1,0:T(8,128)(2,1)S(1)}, u32[]{:S(2)}, u32[]{:S(2)}) collective-permute-start(bf16[128,3712]{1,0:T(8,128)(2,1)S(1)} %shard_map.64.refs_0_), channel_id=1, source_target_pairs={{0,4},{2,6},{4,8},{6,10},{8,12},{10,14},{1,5},{3,7},{5,9},{7,11},{... | collective-permute-start | bytes 2850824 | tf_op jit(solution)/shard_map/ppermute | solution.py:253
  6.8 25.1 %collective-permute-start = (bf16[128,3712]{1,0:T(8,128)(2,1)S(1)}, bf16[128,3712]{1,0:T(8,128)(2,1)S(1)}, u32[]{:S(2)}, u32[]{:S(2)}) collective-permute-start(bf16[128,3712]{1,0:T(8,128)(2,1)S(1)} %shard_map.64.refs_0_), channel_id=1, source_target_pairs={{4,0},{6,2},{8,4},{10,6},{12,8},{14,10},{5,1},{7,3},{9,5},{11,7},{... | collective-permute-start | bytes 2850824 | tf_op jit(solution)/shard_map/ppermute | solution.py:253
  27.7 32.6 %collective-permute-start.6 = (bf16[128,3712]{1,0:T(8,128)(2,1)S(1)}, bf16[128,3712]{1,0:T(8,128)(2,1)S(1)}, u32[]{:S(2)}, u32[]{:S(2)}) collective-permute-start(bf16[128,3712]{1,0:T(8,128)(2,1)S(1)} %collective-permute-done.1.refs_1_.refs_2_), channel_id=1, source_target_pairs={{4,8},{6,10},{8,12},{10,14},{5,9},{7,11},{9,13},{11,15},{20,24},{2... | collective-permute-start | bytes 2850824 | tf_op jit(solution)/shard_map/ppermute | solution.py:253
  31.8 28.4 %collective-permute-start.7 = (bf16[128,3712]{1,0:T(8,128)(2,1)S(1)}, bf16[128,3712]{1,0:T(8,128)(2,1)S(1)}, u32[]{:S(2)}, u32[]{:S(2)}) collective-permute-start(bf16[128,3712]{1,0:T(8,128)(2,1)S(1)} %collective-permute-done.refs_0_), channel_id=1, source_target_pairs={{4,0},{6,2},{8,4},{10,6},{5,1},{7,3},{9,5},{11,7},{20,16},{22,18},... | collective-permute-start | bytes 2850824 | tf_op jit(solution)/shard_map/ppermute | solution.py:253
  34.2 16.4 %collective-permute-start.8 = (bf16[80,3712]{1,0:T(8,128)(2,1)S(1)}, bf16[80,3712]{1,0:T(8,128)(2,1)S(1)}, u32[]{:S(2)}, u32[]{:S(2)}) collective-permute-start(bf16[80,3712]{1,0:T(8,128)(2,1)S(1)} %get-tuple-element.40), channel_id=1, source_target_pairs={{0,2},{2,0},{4,6},{6,4},{8,10},{10,8},{12,14},{14,12},{1,3},{3,1},... | collective-permute-start | bytes 1781768 | tf_op jit(solution)/shard_map/ppermute | solution.py:256
  37.6 26.5 %collective-permute-start.3 = (bf16[80,3712]{1,0:T(8,128)(2,1)}, bf16[80,3712]{1,0:T(8,128)(2,1)S(1)}, u32[]{:S(2)}, u32[]{:S(2)}) collective-permute-start(bf16[80,3712]{1,0:T(8,128)(2,1)} %get-tuple-element.38), channel_id=1, source_target_pairs={{0,2},{2,0},{4,6},{6,4},{8,10},{10,8},{12,14},{14,12},{1,3},{3,1},... | collective-permute-start | bytes 1781768 | tf_op jit(solution)/shard_map/ppermute | solution.py:256
  60.3 5.7 %copy-start = (bf16[80,3712]{1,0:T(8,128)(2,1)S(1)}, bf16[80,3712]{1,0:T(8,128)(2,1)}, u32[]{:S(2)}) copy-start(bf16[80,3712]{1,0:T(8,128)(2,1)} %get-tuple-element.37.refs_0_) | copy-start | bytes 1781764
  60.4 24.7 %collective-permute-start.14 = (bf16[128,3712]{1,0:T(8,128)(2,1)S(1)}, bf16[128,3712]{1,0:T(8,128)(2,1)S(1)}, u32[]{:S(2)}, u32[]{:S(2)}) collective-permute-start(bf16[128,3712]{1,0:T(8,128)(2,1)S(1)} %get-tuple-element.42.refs_1_.refs_0_), channel_id=1, source_target_pairs={{4,0},{6,2},{5,1},{7,3},{20,16},{22,18},{21,17},{23,19}} | collective-permute-start | bytes 2850824 | tf_op jit(solution)/shard_map/ppermute | solution.py:253
  61.8 23.3 %collective-permute-start.15 = (bf16[128,3712]{1,0:T(8,128)(2,1)S(1)}, bf16[128,3712]{1,0:T(8,128)(2,1)S(1)}, u32[]{:S(2)}, u32[]{:S(2)}) collective-permute-start(bf16[128,3712]{1,0:T(8,128)(2,1)S(1)} %get-tuple-element.43.refs_3_.refs_2_), channel_id=1, source_target_pairs={{8,12},{10,14},{9,13},{11,15},{24,28},{26,30},{25,29},{27,31}} | collective-permute-start | bytes 2850824 | tf_op jit(solution)/shard_map/ppermute | solution.py:253
  62.6 16.0 %collective-permute-start.10 = (bf16[80,3584]{1,0:T(8,128)(2,1)S(1)}, bf16[80,3584]{1,0:T(8,128)(2,1)S(1)}, u32[]{:S(2)}, u32[]{:S(2)}) collective-permute-start(bf16[80,3584]{1,0:T(8,128)(2,1)S(1)} %get-tuple-element.48), channel_id=1, source_target_pairs={{0,2},{2,0},{4,6},{6,4},{8,10},{10,8},{12,14},{14,12},{1,3},{3,1},... | collective-permute-start | bytes 1720328 | tf_op jit(solution)/shard_map/ppermute | solution.py:256
  65.4 25.9 %collective-permute-start.13 = (bf16[80,3712]{1,0:T(8,128)(2,1)S(1)}, bf16[80,3712]{1,0:T(8,128)(2,1)S(1)}, u32[]{:S(2)}, u32[]{:S(2)}) collective-permute-start(bf16[80,3712]{1,0:T(8,128)(2,1)S(1)} %get-tuple-element.51), channel_id=1, source_target_pairs={{0,2},{2,0},{4,6},{6,4},{8,10},{10,8},{12,14},{14,12},{1,3},{3,1},... | collective-permute-start | bytes 1781768 | tf_op jit(solution)/shard_map/ppermute | solution.py:256
  79.2 36.1 %collective-permute-start.11 = (bf16[128,3584]{1,0:T(8,128)(2,1)S(1)}, bf16[128,3584]{1,0:T(8,128)(2,1)S(1)}, u32[]{:S(2)}, u32[]{:S(2)}) collective-permute-start(bf16[128,3584]{1,0:T(8,128)(2,1)S(1)} %shard_map.71.refs_4_), channel_id=1, source_target_pairs={{8,4},{10,6},{12,8},{14,10},{9,5},{11,7},{13,9},{15,11},{24,20},{2... | collective-permute-start | bytes 2752520 | tf_op jit(solution)/shard_map/ppermute | solution.py:253
  79.9 35.3 %collective-permute-start.12 = (bf16[128,3584]{1,0:T(8,128)(2,1)S(1)}, bf16[128,3584]{1,0:T(8,128)(2,1)S(1)}, u32[]{:S(2)}, u32[]{:S(2)}) collective-permute-start(bf16[128,3584]{1,0:T(8,128)(2,1)S(1)} %shard_map.71.refs_4_), channel_id=1, source_target_pairs={{0,4},{2,6},{4,8},{6,10},{1,5},{3,7},{5,9},{7,11},{16,20},{18,22},... | collective-permute-start | bytes 2752520 | tf_op jit(solution)/shard_map/ppermute | solution.py:253
  86.4 17.6 %collective-permute-start.17 = (bf16[80,3712]{1,0:T(8,128)(2,1)S(1)}, bf16[80,3712]{1,0:T(8,128)(2,1)S(1)}, u32[]{:S(2)}, u32[]{:S(2)}) collective-permute-start(bf16[80,3712]{1,0:T(8,128)(2,1)S(1)} %get-tuple-element.56), channel_id=1, source_target_pairs={{0,2},{2,0},{4,6},{6,4},{8,10},{10,8},{12,14},{14,12},{1,3},{3,1},... | collective-permute-start | bytes 1781768 | tf_op jit(solution)/shard_map/ppermute | solution.py:256
  100.9 15.2 %collective-permute-start.16 = (bf16[80,3584]{1,0:T(8,128)(2,1)S(1)}, bf16[80,3584]{1,0:T(8,128)(2,1)S(1)}, u32[]{:S(2)}, u32[]{:S(2)}) collective-permute-start(bf16[80,3584]{1,0:T(8,128)(2,1)S(1)} %get-tuple-element.54), channel_id=1, source_target_pairs={{0,2},{2,0},{4,6},{6,4},{8,10},{10,8},{12,14},{14,12},{1,3},{3,1},... | collective-permute-start | bytes 1720328 | tf_op jit(solution)/shard_map/ppermute | solution.py:256
  113.6 10.8 %collective-permute-start.19 = (bf16[80,3584]{1,0:T(8,128)(2,1)S(1)}, bf16[80,3584]{1,0:T(8,128)(2,1)S(1)}, u32[]{:S(2)}, u32[]{:S(2)}) collective-permute-start(bf16[80,3584]{1,0:T(8,128)(2,1)S(1)} %get-tuple-element.59), channel_id=1, source_target_pairs={{0,2},{2,0},{4,6},{6,4},{8,10},{10,8},{12,14},{14,12},{1,3},{3,1},... | collective-permute-start | bytes 1720328 | tf_op jit(solution)/shard_map/ppermute | solution.py:256
  116.7 22.5 %collective-permute-start.18 = (bf16[128,3584]{1,0:T(8,128)(2,1)S(1)}, bf16[128,3584]{1,0:T(8,128)(2,1)S(1)}, u32[]{:S(2)}, u32[]{:S(2)}) collective-permute-start(bf16[128,3584]{1,0:T(8,128)(2,1)S(1)} %shard_map.75.refs_4_), channel_id=1, source_target_pairs={{0,8},{2,10},{4,0},{6,2},{8,12},{10,14},{12,4},{14,6},{1,9},{3,11}... | collective-permute-start | bytes 2752520 | tf_op jit(solution)/shard_map/ppermute | solution.py:253
  125.0 21.5 %collective-permute-start.20 = (bf16[128,1792]{1,0:T(8,128)(2,1)S(1)}, bf16[128,1792]{1,0:T(8,128)(2,1)S(1)}, u32[]{:S(2)}, u32[]{:S(2)}) collective-permute-start(bf16[128,1792]{1,0:T(8,128)(2,1)S(1)} %get-tuple-element.61), channel_id=1, source_target_pairs={{0,4},{2,6},{12,8},{14,10},{1,5},{3,7},{13,9},{15,11},{16,20},{18,... | collective-permute-start | bytes 1376264 | tf_op jit(solution)/shard_map/ppermute | solution.py:253
  129.5 22.0 %collective-permute-start.22 = (bf16[128,1792]{1,0:T(8,128)(2,1)S(1)}, bf16[128,1792]{1,0:T(8,128)(2,1)S(1)}, u32[]{:S(2)}, u32[]{:S(2)}) collective-permute-start(bf16[128,1792]{1,0:T(8,128)(2,1)S(1)} %get-tuple-element.62), channel_id=1, source_target_pairs={{0,4},{2,6},{12,8},{14,10},{1,5},{3,7},{13,9},{15,11},{16,20},{18,... | collective-permute-start | bytes 1376264 | tf_op jit(solution)/shard_map/ppermute | solution.py:253
  130.8 28.7 %collective-permute-start.9 = (bf16[80,3584]{1,0:T(8,128)(2,1)S(1)}, bf16[80,3584]{1,0:T(8,128)(2,1)S(1)}, u32[]{:S(2)}, u32[]{:S(2)}) collective-permute-start(bf16[80,3584]{1,0:T(8,128)(2,1)S(1)} %get-tuple-element.46), channel_id=1, source_target_pairs={{0,2},{2,0},{4,6},{6,4},{8,10},{10,8},{12,14},{14,12},{1,3},{3,1},... | collective-permute-start | bytes 1720328 | tf_op jit(solution)/shard_map/ppermute | solution.py:256
  146.6 12.8 %collective-permute-start.21 = (bf16[128,1792]{1,0:T(8,128)(2,1)S(1)}, bf16[128,1792]{1,0:T(8,128)(2,1)S(1)}, u32[]{:S(2)}, u32[]{:S(2)}) collective-permute-start(bf16[128,1792]{1,0:T(8,128)(2,1)S(1)} %shard_map.78.refs_2_), channel_id=1, source_target_pairs={{4,12},{6,14},{8,0},{10,2},{5,13},{7,15},{9,1},{11,3},{20,28},{22,... | collective-permute-start | bytes 1376264 | tf_op jit(solution)/shard_map/ppermute | solution.py:253
  151.5 12.8 %collective-permute-start.23 = (bf16[128,1792]{1,0:T(8,128)(2,1)S(1)}, bf16[128,1792]{1,0:T(8,128)(2,1)S(1)}, u32[]{:S(2)}, u32[]{:S(2)}) collective-permute-start(bf16[128,1792]{1,0:T(8,128)(2,1)S(1)} %shard_map.79.refs_1_), channel_id=1, source_target_pairs={{4,12},{6,14},{8,0},{10,2},{5,13},{7,15},{9,1},{11,3},{20,28},{22,... | collective-permute-start | bytes 1376264 | tf_op jit(solution)/shard_map/ppermute | solution.py:253

commit v20 on v19

--- a/solution.py
+++ b/solution.py
@@ -86,7 +86,7 @@
         result[...] = source[...]
 
 
-def choose(held, own_map, other_map, own_rows, other_rows):
+def choose(held, own_map, other_map, scales, own_rows, other_rows):
     node = lax.axis_index("node")
     count, cap = own_map.shape
     marks = held[:, held.shape[1] - 128 :].astype(jnp.float32)
@@ -98,17 +98,21 @@
     )
     place = jnp.where(named > 0, rank, -1.0)
     slot = lax.broadcasted_iota(jnp.int32, (count, cap), 1)
-    for expert, one_hot, rows in ((node, own_map, own_rows), (node ^ 1, other_map, other_rows)):
+    scales[...] = jnp.zeros(scales.shape, jnp.float32)
+    width, experts = own_rows.shape[1], lax.axis_size("node")
+    for k, (expert, one_hot, rows) in enumerate(((node, own_map, own_rows), (node ^ 1, other_map, other_rows))):
+        parts = (lax.rem(lane, experts) == expert) & (lane < 3 * experts)
+        scales[:, k : k + 1] = jnp.sum(jnp.where(parts, marks, 0.0), axis=1, keepdims=True)
         mine = jnp.sum(jnp.where(lane == expert, place, 0.0), axis=1, keepdims=True).astype(jnp.int32)
         chosen = jnp.where(mine == slot, 1.0, 0.0).astype(jnp.bfloat16)
         one_hot[...] = chosen
         rows[...] = lax.dot_general(
-            chosen, held[...], (((0,), (0,)), ((), ())), preferred_element_type=jnp.float32
+            chosen, held[:, :width], (((0,), (0,)), ((), ())), preferred_element_type=jnp.float32
         ).astype(jnp.bfloat16)
 
 
 def pick_kernel(users, *refs):
-    blocks, (held, sem) = refs[: len(users)], refs[len(users) + 4 :]
+    blocks, (held, sem) = refs[: len(users)], refs[len(users) + 5 :]
     node = lax.axis_index("node")
     for block, places in zip(blocks, users):
         here = functools.reduce(jnp.logical_or, [lax.div(node, 2) == place for place in places])
@@ -119,10 +123,10 @@
             copy.start()
             copy.wait()
 
-    choose(held, *refs[len(users) : len(users) + 4])
-
-
-def expert_kernel(experts, count, *refs):
+    choose(held, *refs[len(users) : len(users) + 5])
+
+
+def expert_kernel(count, *refs):
     marked, weights, outs = refs[:count], refs[count : count + 6], refs[count + 6 : 2 * count + 6]
     rows, hidden, gates, ups, downs, sems = refs[2 * count + 6 :]
     cap, width = outs[0].shape
@@ -147,7 +151,7 @@
             break
 
     for k, source in enumerate(marked):
-        rows[k * cap : (k + 1) * cap] = source[:, :width]
+        rows[k * cap : (k + 1) * cap] = source[...]
     for tile in range(tiles):
         arrived(queue[2 * tile])
         gate = jnp.dot(rows[...], gates[tile], preferred_element_type=jnp.float32)
@@ -156,26 +160,19 @@
         hidden[:, tile * size : (tile + 1) * size] = (gate / (1.0 + jnp.exp(-gate)) * up).astype(jnp.bfloat16)
     arrived(queue[-2])
     arrived(queue[-1])
-    node = lax.axis_index("node")
-    scales = []
-    for source in marked:
-        marks = source[:, width:].astype(jnp.float32)
-        lane = lax.broadcasted_iota(jnp.int32, marks.shape, 1)
-        mine = (lax.rem(lane, experts) == node) & (lane < 3 * experts)
-        scales.append(jnp.sum(jnp.where(mine, marks, 0.0), axis=1, keepdims=True))
     step = 512 if width % 512 == 0 else width
     for start in range(0, width, step):
         cut = slice(start, start + step)
         out = jnp.dot(hidden[:, : each * size], downs[0, :, cut], preferred_element_type=jnp.float32)
         out += jnp.dot(hidden[:, each * size :], downs[1, :, cut], preferred_element_type=jnp.float32)
         for k, result in enumerate(outs):
-            result[:, cut] = (out[k * cap : (k + 1) * cap] * scales[k]).astype(jnp.bfloat16)
-
-
-def spread_kernel(own_map, other_map, own_out, other_out, *refs):
+            result[:, cut] = out[k * cap : (k + 1) * cap].astype(jnp.bfloat16)
+
+
+def spread_kernel(own_map, other_map, scales, own_out, other_out, *refs):
     result = refs[-1]
-    total = jnp.dot(own_map[...], own_out[...], preferred_element_type=jnp.float32)
-    total += jnp.dot(other_map[...], other_out[...], preferred_element_type=jnp.float32)
+    total = jnp.dot(own_map[...], own_out[...], preferred_element_type=jnp.float32) * scales[:, :1]
+    total += jnp.dot(other_map[...], other_out[...], preferred_element_type=jnp.float32) * scales[:, 1:2]
     for extra in refs[:-1]:
         total += extra[...].astype(jnp.float32)
     result[...] = total.astype(jnp.bfloat16)
@@ -257,9 +254,10 @@
 
     def pick(blocks, users, after=(), cost=0):
         rows = hbm if len(blocks) == 1 else bf16
+        factors = jax.ShapeDtypeStruct((count, 128), jnp.float32)
         return call(
             functools.partial(pick_kernel, users),
-            [bf16((count, cap)), bf16((count, cap)), rows((cap, wide)), rows((cap, wide))],
+            [bf16((count, cap)), bf16((count, cap)), factors, rows((cap, width)), rows((cap, width))],
             blocks,
             after,
             [pltpu.VMEM((count, wide), jnp.bfloat16), pltpu.SemaphoreType.DMA],
@@ -270,7 +268,7 @@
     def expert(rows, after=(), cost=0):
         tiles = 2 * hidden // size
         return call(
-            functools.partial(expert_kernel, experts, len(rows)),
+            functools.partial(expert_kernel, len(rows)),
             [bf16((cap, width))] * len(rows),
             [*rows, *weights],
             after,

time: 166 us -> 165 us (level)
  no operation moved by 1% of the time
where the time goes in v20:
time: 165 us; the launch traced here: 164 us
  waiting for transfers between devices  74.5 us (45%)
  Pallas kernels  49.5 us (30%)
  starting transfers between devices  40 us (24%)
    ppermute x13, waiting for transfers between devices, along(): return lax.ppermute(block, 'node', moves)  51.3 us
    pallas_call x19, Pallas kernels, call(): pl.pallas_call(body, out_shape=outs, in_specs=specs, out_specs=out_specs...  49.5 us
    ppermute x13, starting transfers between devices, along(): return lax.ppermute(block, 'node', moves)  28.4 us
    ppermute x8, waiting for transfers between devices, across(): return lax.ppermute(block, 'node', [(n, n ^ 1) for n in range(experts)])  23.2 us
    ppermute x8, starting transfers between devices, across(): return lax.ppermute(block, 'node', [(n, n ^ 1) for n in range(experts)])  10.6 us
  transfers between devices with their start and end apart: 24, of which 13 were waited for; matrix products, arithmetic and copies ran while one was open for 0% of the time, Pallas kernels for 29%

profile of v20, /device:TPU:0, one launch (start us, length us, event | category | flops | bytes accessed | tf_op | source)
XLA Modules:
  0.0 164.3 jit_solution(11037813522078538439)
XLA Ops:
  0.0 0.5 collective-permute-start.2
  0.5 0.1 collective-permute-start.4
  0.5 0.5 collective-permute-start.5
  1.0 1.2 shard_map.64.refs_0_
  2.2 4.5 %collective-permute-start.1 = (bf16[128,3712]{1,0:T(8,128)(2,1)S(1)}, bf16[128,3712]{1,0:T(8,128)(2,1)S(1)}, u32[]{:S(2)}, u32[]{:S(2)}) collective-permute-start(bf16[128,3712]{1,0:T(8,128)(2,1)S(1)} %shard_map.64.refs_0_), channel_id=1, source_target_pairs={{0,4},{2,6},{4,8},{6,10},{8,12},{10,14},{1,5},{3,7},{5,9},{7,11},{... | collective-permute-start | bytes 2850824 | tf_op jit(solution)/shard_map/ppermute | solution.py:250
  6.8 1.3 collective-permute-start
  8.1 19.6 %collective-permute-done.1.refs_1_.refs_2_ = bf16[128,3712]{1,0:T(8,128)(2,1)S(1)} collective-permute-done((bf16[128,3712]{1,0:T(8,128)(2,1)S(1)}, bf16[128,3712]{1,0:T(8,128)(2,1)S(1)}, u32[]{:S(2)}, u32[]{:S(2)}) %collective-permute-start.1) | collective-permute-done | bytes 950304 | tf_op jit(solution)/shard_map/ppermute | solution.py:250
  27.7 0.7 collective-permute-start.6
  28.4 3.5 %collective-permute-done.refs_0_ = bf16[128,3712]{1,0:T(8,128)(2,1)S(1)} collective-permute-done((bf16[128,3712]{1,0:T(8,128)(2,1)S(1)}, bf16[128,3712]{1,0:T(8,128)(2,1)S(1)}, u32[]{:S(2)}, u32[]{:S(2)}) %collective-permute-start) | collective-permute-done | bytes 950304 | tf_op jit(solution)/shard_map/ppermute | solution.py:250
  31.8 1.3 collective-permute-start.7
  33.1 0.0 collective-permute-done.2.refs_2_.refs_5_
  33.1 1.0 shard_map.65
  34.2 1.6 collective-permute-start.8
  35.7 1.8 %shard_map.66 = (bf16[128,80]{1,0:T(8,128)(2,1)S(1)}, bf16[128,80]{1,0:T(8,128)(2,1)S(1)}, f32[128,128]{1,0:T(8,128)S(1)}, bf16[80,3584]{1,0:T(8,128)(2,1)}, bf16[80,3584]{1,0:T(8,128)(2,1)}) custom-call(bf16[128,3712]{1,0:T(8,128)(2,1)S(1)} %shard_map.64.refs_0_, bf16[128,80]{1,0:T(8,128)(2,1)S(1)} %get-tuple-element.38.refs_1_.refs_0_), custom_call_target="tpu_custom_call" | custom-call | tf_op jit(solution)/shard_map/pallas_call | solution.py:33
  37.6 0.0 collective-permute-done.4.refs_6_
  37.6 0.6 collective-permute-start.3
  38.2 0.0 collective-permute-done.5.refs_7_
  38.2 12.0 %collective-permute-done.8.refs_1_.refs_3_ = bf16[80,3584]{1,0:T(8,128)(2,1)S(1)} collective-permute-done((bf16[80,3584]{1,0:T(8,128)(2,1)S(1)}, bf16[80,3584]{1,0:T(8,128)(2,1)S(1)}, u32[]{:S(2)}, u32[]{:S(2)}) %collective-permute-start.8) | collective-permute-done | bytes 573472 | tf_op jit(solution)/shard_map/ppermute | solution.py:253
  50.1 9.6 %shard_map.67 = (bf16[80,3584]{1,0:T(8,128)(2,1)S(1)}, bf16[80,3584]{1,0:T(8,128)(2,1)S(1)}) custom-call(bf16[80,3584]{1,0:T(8,128)(2,1)S(1)} %get-tuple-element.44.refs_0_, bf16[80,3584]{1,0:T(8,128)(2,1)S(1)} %collective-permute-done.8.refs_1_.refs_3_, bf16[3584,512]{1,0:T(8,128)(2,1)} %bitcast.6, bf16[3584,512]{1,0:T(8,128)(2,1)} %bitcast.11, ...), custom_call_target="tpu_custom_call" | custom-call | bytes 67108864 | tf_op jit(solution)/shard_map/pallas_call | solution.py:33
  59.8 0.0 collective-permute-done.7.refs_1_
  59.8 0.0 copy-start
  59.8 0.1 shard_map.68
  59.9 1.4 collective-permute-start.14
  61.4 0.7 collective-permute-start.15
  62.1 1.6 collective-permute-start.10
  63.7 0.0 collective-permute-done.3.refs_5_.refs_1_
  63.7 1.2 shard_map.69
  64.9 0.6 collective-permute-start.13
  65.5 9.6 %shard_map.70 = (bf16[80,3584]{1,0:T(8,128)(2,1)S(1)}, bf16[80,3584]{1,0:T(8,128)(2,1)S(1)}) custom-call(bf16[80,3584]{1,0:T(8,128)(2,1)S(1)} %copy-done, bf16[80,3584]{1,0:T(8,128)(2,1)S(1)} %collective-permute-done.3.refs_5_.refs_1_, bf16[3584,512]{1,0:T(8,128)(2,1)} %bitcast.7, bf16[3584,512]{1,0:T(8,128)(2,1)} %bitcast.12, bf16[512,3584]{1,0:T(8,128)(2,1)} %bitcast.17, ...), custom_call_target="tpu_custom_call" | custom-call | tf_op jit(solution)/shard_map/pallas_call | solution.py:33
  75.1 3.0 %collective-permute-done.10.refs_4_ = bf16[80,3584]{1,0:T(8,128)(2,1)S(1)} collective-permute-done((bf16[80,3584]{1,0:T(8,128)(2,1)S(1)}, bf16[80,3584]{1,0:T(8,128)(2,1)S(1)}, u32[]{:S(2)}, u32[]{:S(2)}) %collective-permute-start.10) | collective-permute-done | bytes 573472 | tf_op jit(solution)/shard_map/ppermute | solution.py:253
  78.1 0.6 shard_map.71.refs_4_
  78.7 0.7 collective-permute-start.11
  79.4 5.2 %collective-permute-start.12 = (bf16[128,3584]{1,0:T(8,128)(2,1)S(1)}, bf16[128,3584]{1,0:T(8,128)(2,1)S(1)}, u32[]{:S(2)}, u32[]{:S(2)}) collective-permute-start(bf16[128,3584]{1,0:T(8,128)(2,1)S(1)} %shard_map.71.refs_4_), channel_id=1, source_target_pairs={{0,4},{2,6},{4,8},{6,10},{1,5},{3,7},{5,9},{7,11},{16,20},{18,22},... | collective-permute-start | bytes 2752520 | tf_op jit(solution)/shard_map/ppermute | solution.py:250
  84.7 0.0 collective-permute-done.15.refs_3_
  84.7 1.3 shard_map.72
  86.0 1.6 collective-permute-start.17
  87.6 2.8 %collective-permute-done.13.refs_1_ = bf16[80,3584]{1,0:T(8,128)(2,1)S(1)} collective-permute-done((bf16[80,3584]{1,0:T(8,128)(2,1)S(1)}, bf16[80,3584]{1,0:T(8,128)(2,1)S(1)}, u32[]{:S(2)}, u32[]{:S(2)}) %collective-permute-start.13) | collective-permute-done | bytes 573472 | tf_op jit(solution)/shard_map/ppermute | solution.py:253
  90.4 9.6 %shard_map.73 = (bf16[80,3584]{1,0:T(8,128)(2,1)S(1)}, bf16[80,3584]{1,0:T(8,128)(2,1)S(1)}) custom-call(bf16[80,3584]{1,0:T(8,128)(2,1)S(1)} %get-tuple-element.57.refs_0_, bf16[80,3584]{1,0:T(8,128)(2,1)S(1)} %collective-permute-done.13.refs_1_, bf16[3584,512]{1,0:T(8,128)(2,1)} %bitcast.8, bf16[3584,512]{1,0:T(8,128)(2,1)} %bitcast.13, ...), custom_call_target="tpu_custom_call" | custom-call | tf_op jit(solution)/shard_map/pallas_call | solution.py:33
  100.0 1.6 collective-permute-start.16
  101.6 0.9 collective-permute-done.17.refs_1_
  102.5 9.6 %shard_map.74 = (bf16[80,3584]{1,0:T(8,128)(2,1)S(1)}, bf16[80,3584]{1,0:T(8,128)(2,1)S(1)}) custom-call(bf16[80,3584]{1,0:T(8,128)(2,1)S(1)} %get-tuple-element.62.refs_0_, bf16[80,3584]{1,0:T(8,128)(2,1)S(1)} %collective-permute-done.17.refs_1_, bf16[3584,512]{1,0:T(8,128)(2,1)} %bitcast.9, bf16[3584,512]{1,0:T(8,128)(2,1)} %bitcast.14, ...), custom_call_target="tpu_custom_call" | custom-call | tf_op jit(solution)/shard_map/pallas_call | solution.py:33
  112.1 1.6 collective-permute-start.19
  113.7 0.0 collective-permute-done.11.refs_6_.refs_0_
  113.7 0.0 collective-permute-done.12.refs_7_.refs_1_
  113.7 1.0 collective-permute-done.16.refs_4_
  114.8 0.6 shard_map.75.refs_5_
  115.4 4.1 %collective-permute-start.18 = (bf16[128,3584]{1,0:T(8,128)(2,1)S(1)}, bf16[128,3584]{1,0:T(8,128)(2,1)S(1)}, u32[]{:S(2)}, u32[]{:S(2)}) collective-permute-start(bf16[128,3584]{1,0:T(8,128)(2,1)S(1)} %shard_map.75.refs_5_), channel_id=1, source_target_pairs={{0,8},{2,10},{4,0},{6,2},{8,12},{10,14},{12,4},{14,6},{1,9},{3,11}... | collective-permute-start | bytes 2752520 | tf_op jit(solution)/shard_map/ppermute | solution.py:250
  119.5 3.6 %collective-permute-done.19.refs_4_ = bf16[80,3584]{1,0:T(8,128)(2,1)S(1)} collective-permute-done((bf16[80,3584]{1,0:T(8,128)(2,1)S(1)}, bf16[80,3584]{1,0:T(8,128)(2,1)S(1)}, u32[]{:S(2)}, u32[]{:S(2)}) %collective-permute-start.19) | collective-permute-done | bytes 573472 | tf_op jit(solution)/shard_map/ppermute | solution.py:253
  123.1 0.6 shard_map.76
  123.7 4.4 %collective-permute-start.20 = (bf16[128,1792]{1,0:T(8,128)(2,1)S(1)}, bf16[128,1792]{1,0:T(8,128)(2,1)S(1)}, u32[]{:S(2)}, u32[]{:S(2)}) collective-permute-start(bf16[128,1792]{1,0:T(8,128)(2,1)S(1)} %get-tuple-element.69), channel_id=1, source_target_pairs={{0,4},{2,6},{12,8},{14,10},{1,5},{3,7},{13,9},{15,11},{16,20},{18,... | collective-permute-start | bytes 1376264 | tf_op jit(solution)/shard_map/ppermute | solution.py:250
  128.1 1.3 collective-permute-start.22
  129.5 1.6 collective-permute-start.9
  131.0 6.7 %collective-permute-done.18.refs_2_ = bf16[128,3584]{1,0:T(8,128)(2,1)S(1)} collective-permute-done((bf16[128,3584]{1,0:T(8,128)(2,1)S(1)}, bf16[128,3584]{1,0:T(8,128)(2,1)S(1)}, u32[]{:S(2)}, u32[]{:S(2)}) %collective-permute-start.18) | collective-permute-done | bytes 917536 | tf_op jit(solution)/shard_map/ppermute | solution.py:250
  137.7 0.3 shard_map.77.refs_2_.refs_5_
  138.1 7.1 %collective-permute-done.20.refs_1_ = bf16[128,1792]{1,0:T(8,128)(2,1)S(1)} collective-permute-done((bf16[128,1792]{1,0:T(8,128)(2,1)S(1)}, bf16[128,1792]{1,0:T(8,128)(2,1)S(1)}, u32[]{:S(2)}, u32[]{:S(2)}) %collective-permute-start.20) | collective-permute-done | bytes 458784 | tf_op jit(solution)/shard_map/ppermute | solution.py:250
  145.2 0.1 shard_map.78.refs_2_
  145.3 1.3 collective-permute-start.21
  146.6 3.5 %collective-permute-done.22.refs_1_ = bf16[128,1792]{1,0:T(8,128)(2,1)S(1)} collective-permute-done((bf16[128,1792]{1,0:T(8,128)(2,1)S(1)}, bf16[128,1792]{1,0:T(8,128)(2,1)S(1)}, u32[]{:S(2)}, u32[]{:S(2)}) %collective-permute-start.22) | collective-permute-done | bytes 458784 | tf_op jit(solution)/shard_map/ppermute | solution.py:250
  150.1 0.1 shard_map.79.refs_1_
  150.2 1.3 collective-permute-start.23
  151.5 6.8 %collective-permute-done.21.refs_0_ = bf16[128,1792]{1,0:T(8,128)(2,1)S(1)} collective-permute-done((bf16[128,1792]{1,0:T(8,128)(2,1)S(1)}, bf16[128,1792]{1,0:T(8,128)(2,1)S(1)}, u32[]{:S(2)}, u32[]{:S(2)}) %collective-permute-start.21) | collective-permute-done | bytes 458784 | tf_op jit(solution)/shard_map/ppermute | solution.py:250
  158.3 0.7 shard_map.81.total
  159.1 4.1 %collective-permute-done.23.refs_1_ = bf16[128,1792]{1,0:T(8,128)(2,1)S(1)} collective-permute-done((bf16[128,1792]{1,0:T(8,128)(2,1)S(1)}, bf16[128,1792]{1,0:T(8,128)(2,1)S(1)}, u32[]{:S(2)}, u32[]{:S(2)}) %collective-permute-start.23) | collective-permute-done | bytes 458784 | tf_op jit(solution)/shard_map/ppermute | solution.py:250
  163.2 1.1 shard_map.82
  (5 shorter events, 0.0 us)
Async XLA Ops:
  0.0 33.1 %collective-permute-start.2 = (bf16[3584,512]{1,0:T(8,128)(2,1)}, bf16[3584,512]{1,0:T(8,128)(2,1)S(1)}, u32[]{:S(2)}, u32[]{:S(2)}) collective-permute-start(bf16[3584,512]{1,0:T(8,128)(2,1)} %bitcast.5), channel_id=1, source_target_pairs={{0,1},{1,0},{2,3},{3,2},{4,5},{5,4},{6,7},{7,6},{8,9},{9,8},{10,11... | collective-permute-start | bytes 11010056 | tf_op jit(solution)/shard_map/ppermute | solution.py:246
  0.5 37.1 %collective-permute-start.4 = (bf16[3584,512]{1,0:T(8,128)(2,1)}, bf16[3584,512]{1,0:T(8,128)(2,1)S(1)}, u32[]{:S(2)}, u32[]{:S(2)}) collective-permute-start(bf16[3584,512]{1,0:T(8,128)(2,1)} %bitcast.10), channel_id=1, source_target_pairs={{0,1},{1,0},{2,3},{3,2},{4,5},{5,4},{6,7},{7,6},{8,9},{9,8},{10,11... | collective-permute-start | bytes 11010056 | tf_op jit(solution)/shard_map/ppermute | solution.py:246
  0.5 37.7 %collective-permute-start.5 = (bf16[512,3584]{1,0:T(8,128)(2,1)}, bf16[512,3584]{1,0:T(8,128)(2,1)S(1)}, u32[]{:S(2)}, u32[]{:S(2)}) collective-permute-start(bf16[512,3584]{1,0:T(8,128)(2,1)} %bitcast.15), channel_id=1, source_target_pairs={{0,1},{1,0},{2,3},{3,2},{4,5},{5,4},{6,7},{7,6},{8,9},{9,8},{10,11... | collective-permute-start | bytes 11010056 | tf_op jit(solution)/shard_map/ppermute | solution.py:246
  2.2 25.5 %collective-permute-start.1 = (bf16[128,3712]{1,0:T(8,128)(2,1)S(1)}, bf16[128,3712]{1,0:T(8,128)(2,1)S(1)}, u32[]{:S(2)}, u32[]{:S(2)}) collective-permute-start(bf16[128,3712]{1,0:T(8,128)(2,1)S(1)} %shard_map.64.refs_0_), channel_id=1, source_target_pairs={{0,4},{2,6},{4,8},{6,10},{8,12},{10,14},{1,5},{3,7},{5,9},{7,11},{... | collective-permute-start | bytes 2850824 | tf_op jit(solution)/shard_map/ppermute | solution.py:250
  6.8 25.1 %collective-permute-start = (bf16[128,3712]{1,0:T(8,128)(2,1)S(1)}, bf16[128,3712]{1,0:T(8,128)(2,1)S(1)}, u32[]{:S(2)}, u32[]{:S(2)}) collective-permute-start(bf16[128,3712]{1,0:T(8,128)(2,1)S(1)} %shard_map.64.refs_0_), channel_id=1, source_target_pairs={{4,0},{6,2},{8,4},{10,6},{12,8},{14,10},{5,1},{7,3},{9,5},{11,7},{... | collective-permute-start | bytes 2850824 | tf_op jit(solution)/shard_map/ppermute | solution.py:250
  27.7 32.1 %collective-permute-start.6 = (bf16[128,3712]{1,0:T(8,128)(2,1)S(1)}, bf16[128,3712]{1,0:T(8,128)(2,1)S(1)}, u32[]{:S(2)}, u32[]{:S(2)}) collective-permute-start(bf16[128,3712]{1,0:T(8,128)(2,1)S(1)} %collective-permute-done.1.refs_1_.refs_2_), channel_id=1, source_target_pairs={{4,8},{6,10},{8,12},{10,14},{5,9},{7,11},{9,13},{11,15},{20,24},{2... | collective-permute-start | bytes 2850824 | tf_op jit(solution)/shard_map/ppermute | solution.py:250
  31.8 28.0 %collective-permute-start.7 = (bf16[128,3712]{1,0:T(8,128)(2,1)S(1)}, bf16[128,3712]{1,0:T(8,128)(2,1)S(1)}, u32[]{:S(2)}, u32[]{:S(2)}) collective-permute-start(bf16[128,3712]{1,0:T(8,128)(2,1)S(1)} %collective-permute-done.refs_0_), channel_id=1, source_target_pairs={{4,0},{6,2},{8,4},{10,6},{5,1},{7,3},{9,5},{11,7},{20,16},{22,18},... | collective-permute-start | bytes 2850824 | tf_op jit(solution)/shard_map/ppermute | solution.py:250
  34.2 16.0 %collective-permute-start.8 = (bf16[80,3584]{1,0:T(8,128)(2,1)S(1)}, bf16[80,3584]{1,0:T(8,128)(2,1)S(1)}, u32[]{:S(2)}, u32[]{:S(2)}) collective-permute-start(bf16[80,3584]{1,0:T(8,128)(2,1)S(1)} %get-tuple-element.45), channel_id=1, source_target_pairs={{0,2},{2,0},{4,6},{6,4},{8,10},{10,8},{12,14},{14,12},{1,3},{3,1},... | collective-permute-start | bytes 1720328 | tf_op jit(solution)/shard_map/ppermute | solution.py:253
  37.6 26.1 %collective-permute-start.3 = (bf16[80,3584]{1,0:T(8,128)(2,1)}, bf16[80,3584]{1,0:T(8,128)(2,1)S(1)}, u32[]{:S(2)}, u32[]{:S(2)}) collective-permute-start(bf16[80,3584]{1,0:T(8,128)(2,1)} %get-tuple-element.43), channel_id=1, source_target_pairs={{0,2},{2,0},{4,6},{6,4},{8,10},{10,8},{12,14},{14,12},{1,3},{3,1},... | collective-permute-start | bytes 1720328 | tf_op jit(solution)/shard_map/ppermute | solution.py:253
  59.8 5.7 %copy-start = (bf16[80,3584]{1,0:T(8,128)(2,1)S(1)}, bf16[80,3584]{1,0:T(8,128)(2,1)}, u32[]{:S(2)}) copy-start(bf16[80,3584]{1,0:T(8,128)(2,1)} %get-tuple-element.42.refs_0_) | copy-start | bytes 1720324
  59.9 24.7 %collective-permute-start.14 = (bf16[128,3712]{1,0:T(8,128)(2,1)S(1)}, bf16[128,3712]{1,0:T(8,128)(2,1)S(1)}, u32[]{:S(2)}, u32[]{:S(2)}) collective-permute-start(bf16[128,3712]{1,0:T(8,128)(2,1)S(1)} %get-tuple-element.47.refs_1_.refs_0_), channel_id=1, source_target_pairs={{4,0},{6,2},{5,1},{7,3},{20,16},{22,18},{21,17},{23,19}} | collective-permute-start | bytes 2850824 | tf_op jit(solution)/shard_map/ppermute | solution.py:250
  61.4 23.3 %collective-permute-start.15 = (bf16[128,3712]{1,0:T(8,128)(2,1)S(1)}, bf16[128,3712]{1,0:T(8,128)(2,1)S(1)}, u32[]{:S(2)}, u32[]{:S(2)}) collective-permute-start(bf16[128,3712]{1,0:T(8,128)(2,1)S(1)} %get-tuple-element.48.refs_3_.refs_2_), channel_id=1, source_target_pairs={{8,12},{10,14},{9,13},{11,15},{24,28},{26,30},{25,29},{27,31}} | collective-permute-start | bytes 2850824 | tf_op jit(solution)/shard_map/ppermute | solution.py:250
  62.1 16.0 %collective-permute-start.10 = (bf16[80,3584]{1,0:T(8,128)(2,1)S(1)}, bf16[80,3584]{1,0:T(8,128)(2,1)S(1)}, u32[]{:S(2)}, u32[]{:S(2)}) collective-permute-start(bf16[80,3584]{1,0:T(8,128)(2,1)S(1)} %get-tuple-element.54), channel_id=1, source_target_pairs={{0,2},{2,0},{4,6},{6,4},{8,10},{10,8},{12,14},{14,12},{1,3},{3,1},... | collective-permute-start | bytes 1720328 | tf_op jit(solution)/shard_map/ppermute | solution.py:253
  64.9 25.5 %collective-permute-start.13 = (bf16[80,3584]{1,0:T(8,128)(2,1)S(1)}, bf16[80,3584]{1,0:T(8,128)(2,1)S(1)}, u32[]{:S(2)}, u32[]{:S(2)}) collective-permute-start(bf16[80,3584]{1,0:T(8,128)(2,1)S(1)} %get-tuple-element.58), channel_id=1, source_target_pairs={{0,2},{2,0},{4,6},{6,4},{8,10},{10,8},{12,14},{14,12},{1,3},{3,1},... | collective-permute-start | bytes 1720328 | tf_op jit(solution)/shard_map/ppermute | solution.py:253
  78.7 35.0 %collective-permute-start.11 = (bf16[128,3584]{1,0:T(8,128)(2,1)S(1)}, bf16[128,3584]{1,0:T(8,128)(2,1)S(1)}, u32[]{:S(2)}, u32[]{:S(2)}) collective-permute-start(bf16[128,3584]{1,0:T(8,128)(2,1)S(1)} %shard_map.71.refs_4_), channel_id=1, source_target_pairs={{8,4},{10,6},{12,8},{14,10},{9,5},{11,7},{13,9},{15,11},{24,20},{2... | collective-permute-start | bytes 2752520 | tf_op jit(solution)/shard_map/ppermute | solution.py:250
  79.4 34.3 %collective-permute-start.12 = (bf16[128,3584]{1,0:T(8,128)(2,1)S(1)}, bf16[128,3584]{1,0:T(8,128)(2,1)S(1)}, u32[]{:S(2)}, u32[]{:S(2)}) collective-permute-start(bf16[128,3584]{1,0:T(8,128)(2,1)S(1)} %shard_map.71.refs_4_), channel_id=1, source_target_pairs={{0,4},{2,6},{4,8},{6,10},{1,5},{3,7},{5,9},{7,11},{16,20},{18,22},... | collective-permute-start | bytes 2752520 | tf_op jit(solution)/shard_map/ppermute | solution.py:250
  86.0 16.5 %collective-permute-start.17 = (bf16[80,3584]{1,0:T(8,128)(2,1)S(1)}, bf16[80,3584]{1,0:T(8,128)(2,1)S(1)}, u32[]{:S(2)}, u32[]{:S(2)}) collective-permute-start(bf16[80,3584]{1,0:T(8,128)(2,1)S(1)} %get-tuple-element.63), channel_id=1, source_target_pairs={{0,2},{2,0},{4,6},{6,4},{8,10},{10,8},{12,14},{14,12},{1,3},{3,1},... | collective-permute-start | bytes 1720328 | tf_op jit(solution)/shard_map/ppermute | solution.py:253
  100.0 14.7 %collective-permute-start.16 = (bf16[80,3584]{1,0:T(8,128)(2,1)S(1)}, bf16[80,3584]{1,0:T(8,128)(2,1)S(1)}, u32[]{:S(2)}, u32[]{:S(2)}) collective-permute-start(bf16[80,3584]{1,0:T(8,128)(2,1)S(1)} %get-tuple-element.61), channel_id=1, source_target_pairs={{0,2},{2,0},{4,6},{6,4},{8,10},{10,8},{12,14},{14,12},{1,3},{3,1},... | collective-permute-start | bytes 1720328 | tf_op jit(solution)/shard_map/ppermute | solution.py:253
  112.1 11.0 %collective-permute-start.19 = (bf16[80,3584]{1,0:T(8,128)(2,1)S(1)}, bf16[80,3584]{1,0:T(8,128)(2,1)S(1)}, u32[]{:S(2)}, u32[]{:S(2)}) collective-permute-start(bf16[80,3584]{1,0:T(8,128)(2,1)S(1)} %get-tuple-element.67), channel_id=1, source_target_pairs={{0,2},{2,0},{4,6},{6,4},{8,10},{10,8},{12,14},{14,12},{1,3},{3,1},... | collective-permute-start | bytes 1720328 | tf_op jit(solution)/shard_map/ppermute | solution.py:253
  115.4 22.3 %collective-permute-start.18 = (bf16[128,3584]{1,0:T(8,128)(2,1)S(1)}, bf16[128,3584]{1,0:T(8,128)(2,1)S(1)}, u32[]{:S(2)}, u32[]{:S(2)}) collective-permute-start(bf16[128,3584]{1,0:T(8,128)(2,1)S(1)} %shard_map.75.refs_5_), channel_id=1, source_target_pairs={{0,8},{2,10},{4,0},{6,2},{8,12},{10,14},{12,4},{14,6},{1,9},{3,11}... | collective-permute-start | bytes 2752520 | tf_op jit(solution)/shard_map/ppermute | solution.py:250
  123.7 21.5 %collective-permute-start.20 = (bf16[128,1792]{1,0:T(8,128)(2,1)S(1)}, bf16[128,1792]{1,0:T(8,128)(2,1)S(1)}, u32[]{:S(2)}, u32[]{:S(2)}) collective-permute-start(bf16[128,1792]{1,0:T(8,128)(2,1)S(1)} %get-tuple-element.69), channel_id=1, source_target_pairs={{0,4},{2,6},{12,8},{14,10},{1,5},{3,7},{13,9},{15,11},{16,20},{18,... | collective-permute-start | bytes 1376264 | tf_op jit(solution)/shard_map/ppermute | solution.py:250
  128.1 22.0 %collective-permute-start.22 = (bf16[128,1792]{1,0:T(8,128)(2,1)S(1)}, bf16[128,1792]{1,0:T(8,128)(2,1)S(1)}, u32[]{:S(2)}, u32[]{:S(2)}) collective-permute-start(bf16[128,1792]{1,0:T(8,128)(2,1)S(1)} %get-tuple-element.70), channel_id=1, source_target_pairs={{0,4},{2,6},{12,8},{14,10},{1,5},{3,7},{13,9},{15,11},{16,20},{18,... | collective-permute-start | bytes 1376264 | tf_op jit(solution)/shard_map/ppermute | solution.py:250
  129.5 28.8 %collective-permute-start.9 = (bf16[80,3584]{1,0:T(8,128)(2,1)S(1)}, bf16[80,3584]{1,0:T(8,128)(2,1)S(1)}, u32[]{:S(2)}, u32[]{:S(2)}) collective-permute-start(bf16[80,3584]{1,0:T(8,128)(2,1)S(1)} %get-tuple-element.51), channel_id=1, source_target_pairs={{0,2},{2,0},{4,6},{6,4},{8,10},{10,8},{12,14},{14,12},{1,3},{3,1},... | collective-permute-start | bytes 1720328 | tf_op jit(solution)/shard_map/ppermute | solution.py:253
  145.3 13.0 %collective-permute-start.21 = (bf16[128,1792]{1,0:T(8,128)(2,1)S(1)}, bf16[128,1792]{1,0:T(8,128)(2,1)S(1)}, u32[]{:S(2)}, u32[]{:S(2)}) collective-permute-start(bf16[128,1792]{1,0:T(8,128)(2,1)S(1)} %shard_map.78.refs_2_), channel_id=1, source_target_pairs={{4,12},{6,14},{8,0},{10,2},{5,13},{7,15},{9,1},{11,3},{20,28},{22,... | collective-permute-start | bytes 1376264 | tf_op jit(solution)/shard_map/ppermute | solution.py:250
  150.2 13.0 %collective-permute-start.23 = (bf16[128,1792]{1,0:T(8,128)(2,1)S(1)}, bf16[128,1792]{1,0:T(8,128)(2,1)S(1)}, u32[]{:S(2)}, u32[]{:S(2)}) collective-permute-start(bf16[128,1792]{1,0:T(8,128)(2,1)S(1)} %shard_map.79.refs_1_), channel_id=1, source_target_pairs={{4,12},{6,14},{8,0},{10,2},{5,13},{7,15},{9,1},{11,3},{20,28},{22,... | collective-permute-start | bytes 1376264 | tf_op jit(solution)/shard_map/ppermute | solution.py:250

commit v21 on v20

--- a/solution.py
+++ b/solution.py
@@ -185,36 +185,33 @@
     refs[-1][...] = total.astype(jnp.bfloat16)
 
 
-def join_kernel(index, whole, half, result):
-    size = half.shape[1]
-    total = whole[:, index * size : (index + 1) * size].astype(jnp.float32) + half[...].astype(jnp.float32)
+def join_kernel(first, whole, part, result):
+    cut = slice(first, first + part.shape[1])
+    result[...] = (whole[:, cut].astype(jnp.float32) + part[...].astype(jnp.float32)).astype(jnp.bfloat16)
+
+
+def parts_kernel(count, *refs):
+    spread_kernel(*refs[:-count])
+    first = 0
+    for part in refs[-count:]:
+        part[...] = refs[-count - 1][:, first : first + part.shape[1]]
+        first += part.shape[1]
+
+
+def columns_kernel(first, *refs):
+    *whole, part, result = refs
+    total = part[...].astype(jnp.float32)
+    for extra in whole:
+        total += extra[:, first : first + part.shape[1]].astype(jnp.float32)
     result[...] = total.astype(jnp.bfloat16)
 
 
-def halves_kernel(*refs):
-    spread_kernel(*refs[:-2])
-    size = refs[-1].shape[1]
-    refs[-2][...] = refs[-3][:, :size]
-    refs[-1][...] = refs[-3][:, size:]
-
-
-def low_kernel(*refs):
-    *whole, low, result = refs
-    size = low.shape[1]
-    total = low[...].astype(jnp.float32)
-    for extra in whole:
-        total += extra[:, :size].astype(jnp.float32)
-    result[...] = total.astype(jnp.bfloat16)
-
-
 def finish_kernel(total, *refs):
-    *whole, low, high, result = refs
-    size = low.shape[1]
-    result[:, :size] = (low[...].astype(jnp.float32) + total[:, :size].astype(jnp.float32)).astype(jnp.bfloat16)
-    rest = high[...].astype(jnp.float32) + total[:, size:].astype(jnp.float32)
-    for extra in whole:
-        rest += extra[:, size:].astype(jnp.float32)
-    result[:, size:] = rest.astype(jnp.bfloat16)
+    result, first = refs[-1], 0
+    for part in refs[:-1]:
+        cut = slice(first, first + part.shape[1])
+        result[:, cut] = (total[:, cut].astype(jnp.float32) + part[...].astype(jnp.float32)).astype(jnp.bfloat16)
+        first += part.shape[1]
 
 
 def on_device(tokens, routes, route_scale, w_gate, w_up, w_down):
@@ -336,15 +333,17 @@
         if origin(a, final) == origin(b, final) and origin(b, final) not in (a, b)
     ]
     staying = {place for hop in hops for place in hop}
-    kept, halves = {}, []
-
-    def spread_halves(maps, own_out, other_out, after=()):
-        outs = [bf16((count, width)), bf16((count, width // 2)), bf16((count, width // 2))]
-        return call(halves_kernel, outs, [*maps, own_out, other_out], after)
+    kept, pieces_of_last = {}, []
+    edges = [-(-(width // 128) * k // 3) * 128 for k in range(4)]
+    sizes = [b - a for a, b in zip(edges, edges[1:])]
+
+    def spread_parts(maps, own_out, other_out, after=()):
+        outs = [bf16((count, width)), *(bf16((count, size)) for size in sizes)]
+        return call(functools.partial(parts_kernel, len(sizes)), outs, [*maps, own_out, other_out], after)
 
     def do_spread(slot, after=(), cost=0):
         if slot == places - 1:
-            done, *halves[:] = ordered(spread_halves, picks[slot][0], *outs[slot], after=after)
+            done, *pieces_of_last[:] = ordered(spread_parts, picks[slot][0], *outs[slot], after=after)
         else:
             done = ordered(spread, picks[slot][0], *outs[slot], after=after, cost=cost)
         kept[slot] = done
@@ -359,19 +358,21 @@
     def call_sum(blocks, after=(), cost=0):
         return call(sum_kernel, [bf16((count, width))], blocks, after, cost=cost)
 
-    def join(whole, half, index, after=()):
-        return call(functools.partial(join_kernel, index), [bf16(half.shape)], [whole, half], after)[0]
-
-    def finish(whole, parts, summed):
+    def join(whole, part, first, after=()):
+        return call(functools.partial(join_kernel, first), [bf16(part.shape)], [whole, part], after)[0]
+
+    def columns(whole, part, first, after=(), cost=0):
+        kernel = functools.partial(columns_kernel, first)
+        return call(kernel, [bf16(part.shape)], [*whole, part], after, cost=cost)[0]
+
+    def finish(whole, parts, total):
         while len(whole) > 8:
             merged = sum(array.astype(jnp.float32) for array in whole[:8])
             whole = [merged.astype(jnp.bfloat16), *whole[8:]]
-        low = ordered(finish_low, whole, parts[0])
-        total = ordered(spread, picks[0][0], *outs[0], [summed])
-        return call(finish_kernel, [bf16((count, width))], [total, *whole, low, parts[1]])[0]
-
-    def finish_low(whole, half, after=()):
-        return call(low_kernel, [bf16(half.shape)], [*whole, half], after, cost=128 * MIB)[0]
+        done = [ordered(columns, whole, part, first, cost=128 * MIB) for part, first in zip(parts[:-1], edges)]
+        if whole:
+            parts[-1] = ordered(columns, whole, parts[-1], edges[len(parts) - 1])
+        return call(finish_kernel, [bf16((count, width))], [total, *done, parts[-1]])[0]
 
     relay(1)
     relay(2)
@@ -398,9 +399,11 @@
     (summed,) = ordered(call_sum, [*returned.pop(0), *near] if places > 3 else near, cost=128 * MIB)
     homes = [(q, origin(q, final)) for _, q in hops]
     parts = []
-    for arrived in [along(half, hops) for half in halves]:
-        parts.append(along(ordered(join, kept[final], arrived, len(parts)), homes))
-    return finish(sum(returned, []), parts, summed)
+    for arrived, first in zip([along(part, hops) for part in pieces_of_last], edges):
+        parts.append(along(ordered(join, kept[final], arrived, first), homes))
+        if first == 0:
+            total = ordered(spread, picks[0][0], *outs[0], [summed])
+    return finish(sum(returned, []), parts, total)
 
 
 def solution(mesh):

time: 165 us -> 162 us (0.982)
  waiting for transfers between devices: 74.5 us -> 70.6 us
    ppermute x13 -> x15, waiting for transfers between devices: 51.3 us -> 41.1 us  [along(): return lax.ppermute(block, 'node', moves)]
    ppermute x8, waiting for transfers between devices: 23.2 us -> 29.6 us  [across(): return lax.ppermute(block, 'node', [(n, n ^ 1) for n in range(experts)])]
    ppermute x13 -> x15, starting transfers between devices: 28.4 us -> 30.3 us  [along(): return lax.ppermute(block, 'node', moves)]
    pallas_call x19 -> x21, Pallas kernels: 49.5 us -> 49.6 us  [call(): pl.pallas_call(body, out_shape=outs, in_specs=specs, out_specs=out_specs...]
  transfers between devices with their start and end apart: 24 -> 26, of which waited for: 13 -> 13; matrix products, arithmetic and copies ran while one was open for 0% -> 0% of each run, Pallas kernels for 29% -> 30%
where the time goes in v21:
time: 162 us; the launch traced here: 161 us
  waiting for transfers between devices  70.6 us (44%)
  Pallas kernels  49.6 us (31%)
  starting transfers between devices  40.8 us (25%)
    pallas_call x21, Pallas kernels, call(): pl.pallas_call(body, out_shape=outs, in_specs=specs, out_specs=out_specs...  49.6 us
    ppermute x15, waiting for transfers between devices, along(): return lax.ppermute(block, 'node', moves)  41.1 us
    ppermute x15, starting transfers between devices, along(): return lax.ppermute(block, 'node', moves)  30.3 us
    ppermute x8, waiting for transfers between devices, across(): return lax.ppermute(block, 'node', [(n, n ^ 1) for n in range(experts)])  29.6 us
    ppermute x8, starting transfers between devices, across(): return lax.ppermute(block, 'node', [(n, n ^ 1) for n in range(experts)])  9.51 us
  transfers between devices with their start and end apart: 26, of which 13 were waited for; matrix products, arithmetic and copies ran while one was open for 0% of the time, Pallas kernels for 30%

profile of v21, /device:TPU:0, one launch (start us, length us, event | category | flops | bytes accessed | tf_op | source)
XLA Modules:
  0.0 161.4 jit_solution(11500215836557744148)
XLA Ops:
  0.0 0.5 collective-permute-start.2
  0.5 0.1 collective-permute-start.4
  0.5 0.5 collective-permute-start.5
  1.0 1.2 shard_map.64.refs_0_
  2.2 4.5 %collective-permute-start.1 = (bf16[128,3712]{1,0:T(8,128)(2,1)S(1)}, bf16[128,3712]{1,0:T(8,128)(2,1)S(1)}, u32[]{:S(2)}, u32[]{:S(2)}) collective-permute-start(bf16[128,3712]{1,0:T(8,128)(2,1)S(1)} %shard_map.64.refs_0_), channel_id=1, source_target_pairs={{0,4},{2,6},{4,8},{6,10},{8,12},{10,14},{1,5},{3,7},{5,9},{7,11},{... | collective-permute-start | bytes 2850824 | tf_op jit(solution)/shard_map/ppermute | solution.py:247
  6.8 1.3 collective-permute-start
  8.1 19.6 %collective-permute-done.1.refs_1_.refs_2_ = bf16[128,3712]{1,0:T(8,128)(2,1)S(1)} collective-permute-done((bf16[128,3712]{1,0:T(8,128)(2,1)S(1)}, bf16[128,3712]{1,0:T(8,128)(2,1)S(1)}, u32[]{:S(2)}, u32[]{:S(2)}) %collective-permute-start.1) | collective-permute-done | bytes 950304 | tf_op jit(solution)/shard_map/ppermute | solution.py:247
  27.7 0.7 collective-permute-start.6
  28.4 3.5 %collective-permute-done.refs_0_ = bf16[128,3712]{1,0:T(8,128)(2,1)S(1)} collective-permute-done((bf16[128,3712]{1,0:T(8,128)(2,1)S(1)}, bf16[128,3712]{1,0:T(8,128)(2,1)S(1)}, u32[]{:S(2)}, u32[]{:S(2)}) %collective-permute-start) | collective-permute-done | bytes 950304 | tf_op jit(solution)/shard_map/ppermute | solution.py:247
  31.8 1.3 collective-permute-start.7
  33.1 1.0 shard_map.65
  34.2 1.6 collective-permute-start.8
  35.7 1.8 %shard_map.66 = (bf16[128,80]{1,0:T(8,128)(2,1)S(1)}, bf16[128,80]{1,0:T(8,128)(2,1)S(1)}, f32[128,128]{1,0:T(8,128)S(1)}, bf16[80,3584]{1,0:T(8,128)(2,1)}, bf16[80,3584]{1,0:T(8,128)(2,1)}) custom-call(bf16[128,3712]{1,0:T(8,128)(2,1)S(1)} %shard_map.64.refs_0_, bf16[128,80]{1,0:T(8,128)(2,1)S(1)} %get-tuple-element.39.refs_1_.refs_0_), custom_call_target="tpu_custom_call" | custom-call | tf_op jit(solution)/shard_map/pallas_call | solution.py:33
  37.6 0.6 collective-permute-start.3
  38.2 0.0 collective-permute-done.5.refs_7_
  38.2 12.0 %collective-permute-done.8.refs_1_.refs_3_ = bf16[80,3584]{1,0:T(8,128)(2,1)S(1)} collective-permute-done((bf16[80,3584]{1,0:T(8,128)(2,1)S(1)}, bf16[80,3584]{1,0:T(8,128)(2,1)S(1)}, u32[]{:S(2)}, u32[]{:S(2)}) %collective-permute-start.8) | collective-permute-done | bytes 573472 | tf_op jit(solution)/shard_map/ppermute | solution.py:250
  50.1 9.6 %shard_map.67 = (bf16[80,3584]{1,0:T(8,128)(2,1)S(1)}, bf16[80,3584]{1,0:T(8,128)(2,1)S(1)}) custom-call(bf16[80,3584]{1,0:T(8,128)(2,1)S(1)} %get-tuple-element.45.refs_0_, bf16[80,3584]{1,0:T(8,128)(2,1)S(1)} %collective-permute-done.8.refs_1_.refs_3_, bf16[3584,512]{1,0:T(8,128)(2,1)} %bitcast.6, bf16[3584,512]{1,0:T(8,128)(2,1)} %bitcast.11, ...), custom_call_target="tpu_custom_call" | custom-call | bytes 67108864 | tf_op jit(solution)/shard_map/pallas_call | solution.py:33
  59.8 0.0 collective-permute-done.6.refs_0_
  59.8 0.0 collective-permute-done.7.refs_1_
  59.8 0.0 copy-start
  59.8 0.1 shard_map.68
  59.9 1.4 collective-permute-start.14
  61.4 0.7 collective-permute-start.15
  62.1 1.6 collective-permute-start.10
  63.7 0.0 collective-permute-done.3.refs_5_.refs_1_
  63.7 1.2 shard_map.69
  64.9 0.6 collective-permute-start.13
  65.5 9.6 %shard_map.70 = (bf16[80,3584]{1,0:T(8,128)(2,1)S(1)}, bf16[80,3584]{1,0:T(8,128)(2,1)S(1)}) custom-call(bf16[80,3584]{1,0:T(8,128)(2,1)S(1)} %copy-done, bf16[80,3584]{1,0:T(8,128)(2,1)S(1)} %collective-permute-done.3.refs_5_.refs_1_, bf16[3584,512]{1,0:T(8,128)(2,1)} %bitcast.7, bf16[3584,512]{1,0:T(8,128)(2,1)} %bitcast.12, bf16[512,3584]{1,0:T(8,128)(2,1)} %bitcast.17, ...), custom_call_target="tpu_custom_call" | custom-call | tf_op jit(solution)/shard_map/pallas_call | solution.py:33
  75.1 3.0 %collective-permute-done.10.refs_4_ = bf16[80,3584]{1,0:T(8,128)(2,1)S(1)} collective-permute-done((bf16[80,3584]{1,0:T(8,128)(2,1)S(1)}, bf16[80,3584]{1,0:T(8,128)(2,1)S(1)}, u32[]{:S(2)}, u32[]{:S(2)}) %collective-permute-start.10) | collective-permute-done | bytes 573472 | tf_op jit(solution)/shard_map/ppermute | solution.py:250
  78.1 0.6 shard_map.71.refs_4_
  78.7 0.7 collective-permute-start.11
  79.4 5.2 %collective-permute-start.12 = (bf16[128,3584]{1,0:T(8,128)(2,1)S(1)}, bf16[128,3584]{1,0:T(8,128)(2,1)S(1)}, u32[]{:S(2)}, u32[]{:S(2)}) collective-permute-start(bf16[128,3584]{1,0:T(8,128)(2,1)S(1)} %shard_map.71.refs_4_), channel_id=1, source_target_pairs={{0,4},{2,6},{4,8},{6,10},{1,5},{3,7},{5,9},{7,11},{16,20},{18,22},... | collective-permute-start | bytes 2752520 | tf_op jit(solution)/shard_map/ppermute | solution.py:247
  84.7 0.0 collective-permute-done.14.refs_1_
  84.7 1.3 shard_map.72
  86.0 1.6 collective-permute-start.17
  87.6 2.8 %collective-permute-done.13.refs_1_ = bf16[80,3584]{1,0:T(8,128)(2,1)S(1)} collective-permute-done((bf16[80,3584]{1,0:T(8,128)(2,1)S(1)}, bf16[80,3584]{1,0:T(8,128)(2,1)S(1)}, u32[]{:S(2)}, u32[]{:S(2)}) %collective-permute-start.13) | collective-permute-done | bytes 573472 | tf_op jit(solution)/shard_map/ppermute | solution.py:250
  90.4 9.6 %shard_map.73 = (bf16[80,3584]{1,0:T(8,128)(2,1)S(1)}, bf16[80,3584]{1,0:T(8,128)(2,1)S(1)}) custom-call(bf16[80,3584]{1,0:T(8,128)(2,1)S(1)} %get-tuple-element.58.refs_0_, bf16[80,3584]{1,0:T(8,128)(2,1)S(1)} %collective-permute-done.13.refs_1_, bf16[3584,512]{1,0:T(8,128)(2,1)} %bitcast.8, bf16[3584,512]{1,0:T(8,128)(2,1)} %bitcast.13, ...), custom_call_target="tpu_custom_call" | custom-call | tf_op jit(solution)/shard_map/pallas_call | solution.py:33
  100.0 1.6 collective-permute-start.16
  101.6 0.9 collective-permute-done.17.refs_1_
  102.5 9.6 %shard_map.74 = (bf16[80,3584]{1,0:T(8,128)(2,1)S(1)}, bf16[80,3584]{1,0:T(8,128)(2,1)S(1)}) custom-call(bf16[80,3584]{1,0:T(8,128)(2,1)S(1)} %get-tuple-element.63.refs_0_, bf16[80,3584]{1,0:T(8,128)(2,1)S(1)} %collective-permute-done.17.refs_1_, bf16[3584,512]{1,0:T(8,128)(2,1)} %bitcast.9, bf16[3584,512]{1,0:T(8,128)(2,1)} %bitcast.14, ...), custom_call_target="tpu_custom_call" | custom-call | tf_op jit(solution)/shard_map/pallas_call | solution.py:33
  112.2 0.6 shard_map.75.refs_5_
  112.8 4.4 %collective-permute-start.18 = (bf16[128,3584]{1,0:T(8,128)(2,1)S(1)}, bf16[128,3584]{1,0:T(8,128)(2,1)S(1)}, u32[]{:S(2)}, u32[]{:S(2)}) collective-permute-start(bf16[128,3584]{1,0:T(8,128)(2,1)S(1)} %shard_map.75.refs_5_), channel_id=1, source_target_pairs={{0,8},{2,10},{4,0},{6,2},{8,12},{10,14},{12,4},{14,6},{1,9},{3,11}... | collective-permute-start | bytes 2752520 | tf_op jit(solution)/shard_map/ppermute | solution.py:247
  117.2 1.5 collective-permute-start.19
  118.7 0.5 collective-permute-start.9
  119.2 10.9 %collective-permute-done.19.refs_4_ = bf16[80,3584]{1,0:T(8,128)(2,1)S(1)} collective-permute-done((bf16[80,3584]{1,0:T(8,128)(2,1)S(1)}, bf16[80,3584]{1,0:T(8,128)(2,1)S(1)}, u32[]{:S(2)}, u32[]{:S(2)}) %collective-permute-start.19) | collective-permute-done | bytes 573472 | tf_op jit(solution)/shard_map/ppermute | solution.py:250
  130.2 0.7 shard_map.76
  130.9 3.4 %collective-permute-start.20 = (bf16[128,1280]{1,0:T(8,128)(2,1)S(1)}, bf16[128,1280]{1,0:T(8,128)(2,1)S(1)}, u32[]{:S(2)}, u32[]{:S(2)}) collective-permute-start(bf16[128,1280]{1,0:T(8,128)(2,1)S(1)} %get-tuple-element.70), channel_id=1, source_target_pairs={{0,4},{2,6},{12,8},{14,10},{1,5},{3,7},{13,9},{15,11},{16,20},{18,... | collective-permute-start | bytes 983048 | tf_op jit(solution)/shard_map/ppermute | solution.py:247
  134.3 1.3 collective-permute-start.23
  135.6 1.3 collective-permute-start.22
  137.0 0.3 shard_map.77.refs_2_.refs_5_
  137.3 5.3 %collective-permute-done.20.refs_1_ = bf16[128,1280]{1,0:T(8,128)(2,1)S(1)} collective-permute-done((bf16[128,1280]{1,0:T(8,128)(2,1)S(1)}, bf16[128,1280]{1,0:T(8,128)(2,1)S(1)}, u32[]{:S(2)}, u32[]{:S(2)}) %collective-permute-start.20) | collective-permute-done | bytes 327712 | tf_op jit(solution)/shard_map/ppermute | solution.py:247
  142.6 0.1 shard_map.78.refs_6_
  142.6 1.3 collective-permute-start.21
  143.9 0.7 shard_map.79.refs_2_.total
  144.7 1.0 collective-permute-done.23.refs_1_
  145.7 0.1 shard_map.80.refs_2_
  145.8 1.3 collective-permute-start.24
  147.1 1.8 %collective-permute-done.22.refs_1_ = bf16[128,1152]{1,0:T(8,128)(2,1)S(1)} collective-permute-done((bf16[128,1152]{1,0:T(8,128)(2,1)S(1)}, bf16[128,1152]{1,0:T(8,128)(2,1)S(1)}, u32[]{:S(2)}, u32[]{:S(2)}) %collective-permute-start.22) | collective-permute-done | bytes 294944 | tf_op jit(solution)/shard_map/ppermute | solution.py:247
  148.9 0.1 shard_map.81.refs_1_
  149.0 1.3 collective-permute-start.25
  150.3 3.6 %collective-permute-done.21.refs_0_ = bf16[128,1280]{1,0:T(8,128)(2,1)S(1)} collective-permute-done((bf16[128,1280]{1,0:T(8,128)(2,1)S(1)}, bf16[128,1280]{1,0:T(8,128)(2,1)S(1)}, u32[]{:S(2)}, u32[]{:S(2)}) %collective-permute-start.21) | collective-permute-done | bytes 327712 | tf_op jit(solution)/shard_map/ppermute | solution.py:247
  153.9 3.1 %collective-permute-done.24.refs_0_ = bf16[128,1152]{1,0:T(8,128)(2,1)S(1)} collective-permute-done((bf16[128,1152]{1,0:T(8,128)(2,1)S(1)}, bf16[128,1152]{1,0:T(8,128)(2,1)S(1)}, u32[]{:S(2)}, u32[]{:S(2)}) %collective-permute-start.24) | collective-permute-done | bytes 294944 | tf_op jit(solution)/shard_map/ppermute | solution.py:247
  157.1 3.1 %collective-permute-done.25.refs_2_ = bf16[128,1152]{1,0:T(8,128)(2,1)S(1)} collective-permute-done((bf16[128,1152]{1,0:T(8,128)(2,1)S(1)}, bf16[128,1152]{1,0:T(8,128)(2,1)S(1)}, u32[]{:S(2)}, u32[]{:S(2)}) %collective-permute-start.25) | collective-permute-done | bytes 294944 | tf_op jit(solution)/shard_map/ppermute | solution.py:247
  160.2 1.1 shard_map.84
  (11 shorter events, 0.1 us)
Async XLA Ops:
  0.0 33.1 %collective-permute-start.2 = (bf16[3584,512]{1,0:T(8,128)(2,1)}, bf16[3584,512]{1,0:T(8,128)(2,1)S(1)}, u32[]{:S(2)}, u32[]{:S(2)}) collective-permute-start(bf16[3584,512]{1,0:T(8,128)(2,1)} %bitcast.5), channel_id=1, source_target_pairs={{0,1},{1,0},{2,3},{3,2},{4,5},{5,4},{6,7},{7,6},{8,9},{9,8},{10,11... | collective-permute-start | bytes 11010056 | tf_op jit(solution)/shard_map/ppermute | solution.py:243
  0.5 37.1 %collective-permute-start.4 = (bf16[3584,512]{1,0:T(8,128)(2,1)}, bf16[3584,512]{1,0:T(8,128)(2,1)S(1)}, u32[]{:S(2)}, u32[]{:S(2)}) collective-permute-start(bf16[3584,512]{1,0:T(8,128)(2,1)} %bitcast.10), channel_id=1, source_target_pairs={{0,1},{1,0},{2,3},{3,2},{4,5},{5,4},{6,7},{7,6},{8,9},{9,8},{10,11... | collective-permute-start | bytes 11010056 | tf_op jit(solution)/shard_map/ppermute | solution.py:243
  0.5 37.7 %collective-permute-start.5 = (bf16[512,3584]{1,0:T(8,128)(2,1)}, bf16[512,3584]{1,0:T(8,128)(2,1)S(1)}, u32[]{:S(2)}, u32[]{:S(2)}) collective-permute-start(bf16[512,3584]{1,0:T(8,128)(2,1)} %bitcast.15), channel_id=1, source_target_pairs={{0,1},{1,0},{2,3},{3,2},{4,5},{5,4},{6,7},{7,6},{8,9},{9,8},{10,11... | collective-permute-start | bytes 11010056 | tf_op jit(solution)/shard_map/ppermute | solution.py:243
  2.2 25.5 %collective-permute-start.1 = (bf16[128,3712]{1,0:T(8,128)(2,1)S(1)}, bf16[128,3712]{1,0:T(8,128)(2,1)S(1)}, u32[]{:S(2)}, u32[]{:S(2)}) collective-permute-start(bf16[128,3712]{1,0:T(8,128)(2,1)S(1)} %shard_map.64.refs_0_), channel_id=1, source_target_pairs={{0,4},{2,6},{4,8},{6,10},{8,12},{10,14},{1,5},{3,7},{5,9},{7,11},{... | collective-permute-start | bytes 2850824 | tf_op jit(solution)/shard_map/ppermute | solution.py:247
  6.8 25.1 %collective-permute-start = (bf16[128,3712]{1,0:T(8,128)(2,1)S(1)}, bf16[128,3712]{1,0:T(8,128)(2,1)S(1)}, u32[]{:S(2)}, u32[]{:S(2)}) collective-permute-start(bf16[128,3712]{1,0:T(8,128)(2,1)S(1)} %shard_map.64.refs_0_), channel_id=1, source_target_pairs={{4,0},{6,2},{8,4},{10,6},{12,8},{14,10},{5,1},{7,3},{9,5},{11,7},{... | collective-permute-start | bytes 2850824 | tf_op jit(solution)/shard_map/ppermute | solution.py:247
  27.7 32.1 %collective-permute-start.6 = (bf16[128,3712]{1,0:T(8,128)(2,1)S(1)}, bf16[128,3712]{1,0:T(8,128)(2,1)S(1)}, u32[]{:S(2)}, u32[]{:S(2)}) collective-permute-start(bf16[128,3712]{1,0:T(8,128)(2,1)S(1)} %collective-permute-done.1.refs_1_.refs_2_), channel_id=1, source_target_pairs={{4,8},{6,10},{8,12},{10,14},{5,9},{7,11},{9,13},{11,15},{20,24},{2... | collective-permute-start | bytes 2850824 | tf_op jit(solution)/shard_map/ppermute | solution.py:247
  31.8 28.0 %collective-permute-start.7 = (bf16[128,3712]{1,0:T(8,128)(2,1)S(1)}, bf16[128,3712]{1,0:T(8,128)(2,1)S(1)}, u32[]{:S(2)}, u32[]{:S(2)}) collective-permute-start(bf16[128,3712]{1,0:T(8,128)(2,1)S(1)} %collective-permute-done.refs_0_), channel_id=1, source_target_pairs={{4,0},{6,2},{8,4},{10,6},{5,1},{7,3},{9,5},{11,7},{20,16},{22,18},... | collective-permute-start | bytes 2850824 | tf_op jit(solution)/shard_map/ppermute | solution.py:247
  34.2 16.0 %collective-permute-start.8 = (bf16[80,3584]{1,0:T(8,128)(2,1)S(1)}, bf16[80,3584]{1,0:T(8,128)(2,1)S(1)}, u32[]{:S(2)}, u32[]{:S(2)}) collective-permute-start(bf16[80,3584]{1,0:T(8,128)(2,1)S(1)} %get-tuple-element.46), channel_id=1, source_target_pairs={{0,2},{2,0},{4,6},{6,4},{8,10},{10,8},{12,14},{14,12},{1,3},{3,1},... | collective-permute-start | bytes 1720328 | tf_op jit(solution)/shard_map/ppermute | solution.py:250
  37.6 26.1 %collective-permute-start.3 = (bf16[80,3584]{1,0:T(8,128)(2,1)}, bf16[80,3584]{1,0:T(8,128)(2,1)S(1)}, u32[]{:S(2)}, u32[]{:S(2)}) collective-permute-start(bf16[80,3584]{1,0:T(8,128)(2,1)} %get-tuple-element.44), channel_id=1, source_target_pairs={{0,2},{2,0},{4,6},{6,4},{8,10},{10,8},{12,14},{14,12},{1,3},{3,1},... | collective-permute-start | bytes 1720328 | tf_op jit(solution)/shard_map/ppermute | solution.py:250
  59.8 5.7 %copy-start = (bf16[80,3584]{1,0:T(8,128)(2,1)S(1)}, bf16[80,3584]{1,0:T(8,128)(2,1)}, u32[]{:S(2)}) copy-start(bf16[80,3584]{1,0:T(8,128)(2,1)} %get-tuple-element.43.refs_0_) | copy-start | bytes 1720324
  59.9 24.7 %collective-permute-start.14 = (bf16[128,3712]{1,0:T(8,128)(2,1)S(1)}, bf16[128,3712]{1,0:T(8,128)(2,1)S(1)}, u32[]{:S(2)}, u32[]{:S(2)}) collective-permute-start(bf16[128,3712]{1,0:T(8,128)(2,1)S(1)} %get-tuple-element.48.refs_1_.refs_0_), channel_id=1, source_target_pairs={{4,0},{6,2},{5,1},{7,3},{20,16},{22,18},{21,17},{23,19}} | collective-permute-start | bytes 2850824 | tf_op jit(solution)/shard_map/ppermute | solution.py:247
  61.4 23.3 %collective-permute-start.15 = (bf16[128,3712]{1,0:T(8,128)(2,1)S(1)}, bf16[128,3712]{1,0:T(8,128)(2,1)S(1)}, u32[]{:S(2)}, u32[]{:S(2)}) collective-permute-start(bf16[128,3712]{1,0:T(8,128)(2,1)S(1)} %get-tuple-element.49.refs_3_.refs_2_), channel_id=1, source_target_pairs={{8,12},{10,14},{9,13},{11,15},{24,28},{26,30},{25,29},{27,31}} | collective-permute-start | bytes 2850824 | tf_op jit(solution)/shard_map/ppermute | solution.py:247
  62.1 16.0 %collective-permute-start.10 = (bf16[80,3584]{1,0:T(8,128)(2,1)S(1)}, bf16[80,3584]{1,0:T(8,128)(2,1)S(1)}, u32[]{:S(2)}, u32[]{:S(2)}) collective-permute-start(bf16[80,3584]{1,0:T(8,128)(2,1)S(1)} %get-tuple-element.55), channel_id=1, source_target_pairs={{0,2},{2,0},{4,6},{6,4},{8,10},{10,8},{12,14},{14,12},{1,3},{3,1},... | collective-permute-start | bytes 1720328 | tf_op jit(solution)/shard_map/ppermute | solution.py:250
  64.9 25.5 %collective-permute-start.13 = (bf16[80,3584]{1,0:T(8,128)(2,1)S(1)}, bf16[80,3584]{1,0:T(8,128)(2,1)S(1)}, u32[]{:S(2)}, u32[]{:S(2)}) collective-permute-start(bf16[80,3584]{1,0:T(8,128)(2,1)S(1)} %get-tuple-element.59), channel_id=1, source_target_pairs={{0,2},{2,0},{4,6},{6,4},{8,10},{10,8},{12,14},{14,12},{1,3},{3,1},... | collective-permute-start | bytes 1720328 | tf_op jit(solution)/shard_map/ppermute | solution.py:250
  78.7 33.4 %collective-permute-start.11 = (bf16[128,3584]{1,0:T(8,128)(2,1)S(1)}, bf16[128,3584]{1,0:T(8,128)(2,1)S(1)}, u32[]{:S(2)}, u32[]{:S(2)}) collective-permute-start(bf16[128,3584]{1,0:T(8,128)(2,1)S(1)} %shard_map.71.refs_4_), channel_id=1, source_target_pairs={{8,4},{10,6},{12,8},{14,10},{9,5},{11,7},{13,9},{15,11},{24,20},{2... | collective-permute-start | bytes 2752520 | tf_op jit(solution)/shard_map/ppermute | solution.py:247
  79.4 32.7 %collective-permute-start.12 = (bf16[128,3584]{1,0:T(8,128)(2,1)S(1)}, bf16[128,3584]{1,0:T(8,128)(2,1)S(1)}, u32[]{:S(2)}, u32[]{:S(2)}) collective-permute-start(bf16[128,3584]{1,0:T(8,128)(2,1)S(1)} %shard_map.71.refs_4_), channel_id=1, source_target_pairs={{0,4},{2,6},{4,8},{6,10},{1,5},{3,7},{5,9},{7,11},{16,20},{18,22},... | collective-permute-start | bytes 2752520 | tf_op jit(solution)/shard_map/ppermute | solution.py:247
  86.0 16.5 %collective-permute-start.17 = (bf16[80,3584]{1,0:T(8,128)(2,1)S(1)}, bf16[80,3584]{1,0:T(8,128)(2,1)S(1)}, u32[]{:S(2)}, u32[]{:S(2)}) collective-permute-start(bf16[80,3584]{1,0:T(8,128)(2,1)S(1)} %get-tuple-element.64), channel_id=1, source_target_pairs={{0,2},{2,0},{4,6},{6,4},{8,10},{10,8},{12,14},{14,12},{1,3},{3,1},... | collective-permute-start | bytes 1720328 | tf_op jit(solution)/shard_map/ppermute | solution.py:250
  100.0 12.1 %collective-permute-start.16 = (bf16[80,3584]{1,0:T(8,128)(2,1)S(1)}, bf16[80,3584]{1,0:T(8,128)(2,1)S(1)}, u32[]{:S(2)}, u32[]{:S(2)}) collective-permute-start(bf16[80,3584]{1,0:T(8,128)(2,1)S(1)} %get-tuple-element.62), channel_id=1, source_target_pairs={{0,2},{2,0},{4,6},{6,4},{8,10},{10,8},{12,14},{14,12},{1,3},{3,1},... | collective-permute-start | bytes 1720328 | tf_op jit(solution)/shard_map/ppermute | solution.py:250
  112.8 24.2 %collective-permute-start.18 = (bf16[128,3584]{1,0:T(8,128)(2,1)S(1)}, bf16[128,3584]{1,0:T(8,128)(2,1)S(1)}, u32[]{:S(2)}, u32[]{:S(2)}) collective-permute-start(bf16[128,3584]{1,0:T(8,128)(2,1)S(1)} %shard_map.75.refs_5_), channel_id=1, source_target_pairs={{0,8},{2,10},{4,0},{6,2},{8,12},{10,14},{12,4},{14,6},{1,9},{3,11}... | collective-permute-start | bytes 2752520 | tf_op jit(solution)/shard_map/ppermute | solution.py:247
  117.2 13.0 %collective-permute-start.19 = (bf16[80,3584]{1,0:T(8,128)(2,1)S(1)}, bf16[80,3584]{1,0:T(8,128)(2,1)S(1)}, u32[]{:S(2)}, u32[]{:S(2)}) collective-permute-start(bf16[80,3584]{1,0:T(8,128)(2,1)S(1)} %get-tuple-element.68), channel_id=1, source_target_pairs={{0,2},{2,0},{4,6},{6,4},{8,10},{10,8},{12,14},{14,12},{1,3},{3,1},... | collective-permute-start | bytes 1720328 | tf_op jit(solution)/shard_map/ppermute | solution.py:250
  118.7 25.2 %collective-permute-start.9 = (bf16[80,3584]{1,0:T(8,128)(2,1)S(1)}, bf16[80,3584]{1,0:T(8,128)(2,1)S(1)}, u32[]{:S(2)}, u32[]{:S(2)}) collective-permute-start(bf16[80,3584]{1,0:T(8,128)(2,1)S(1)} %get-tuple-element.52), channel_id=1, source_target_pairs={{0,2},{2,0},{4,6},{6,4},{8,10},{10,8},{12,14},{14,12},{1,3},{3,1},... | collective-permute-start | bytes 1720328 | tf_op jit(solution)/shard_map/ppermute | solution.py:250
  130.9 11.7 %collective-permute-start.20 = (bf16[128,1280]{1,0:T(8,128)(2,1)S(1)}, bf16[128,1280]{1,0:T(8,128)(2,1)S(1)}, u32[]{:S(2)}, u32[]{:S(2)}) collective-permute-start(bf16[128,1280]{1,0:T(8,128)(2,1)S(1)} %get-tuple-element.70), channel_id=1, source_target_pairs={{0,4},{2,6},{12,8},{14,10},{1,5},{3,7},{13,9},{15,11},{16,20},{18,... | collective-permute-start | bytes 983048 | tf_op jit(solution)/shard_map/ppermute | solution.py:247
  134.3 11.4 %collective-permute-start.23 = (bf16[128,1152]{1,0:T(8,128)(2,1)S(1)}, bf16[128,1152]{1,0:T(8,128)(2,1)S(1)}, u32[]{:S(2)}, u32[]{:S(2)}) collective-permute-start(bf16[128,1152]{1,0:T(8,128)(2,1)S(1)} %get-tuple-element.72), channel_id=1, source_target_pairs={{0,4},{2,6},{12,8},{14,10},{1,5},{3,7},{13,9},{15,11},{16,20},{18,... | collective-permute-start | bytes 884744 | tf_op jit(solution)/shard_map/ppermute | solution.py:247
  135.6 13.2 %collective-permute-start.22 = (bf16[128,1152]{1,0:T(8,128)(2,1)S(1)}, bf16[128,1152]{1,0:T(8,128)(2,1)S(1)}, u32[]{:S(2)}, u32[]{:S(2)}) collective-permute-start(bf16[128,1152]{1,0:T(8,128)(2,1)S(1)} %get-tuple-element.71), channel_id=1, source_target_pairs={{0,4},{2,6},{12,8},{14,10},{1,5},{3,7},{13,9},{15,11},{16,20},{18,... | collective-permute-start | bytes 884744 | tf_op jit(solution)/shard_map/ppermute | solution.py:247
  142.6 11.3 %collective-permute-start.21 = (bf16[128,1280]{1,0:T(8,128)(2,1)S(1)}, bf16[128,1280]{1,0:T(8,128)(2,1)S(1)}, u32[]{:S(2)}, u32[]{:S(2)}) collective-permute-start(bf16[128,1280]{1,0:T(8,128)(2,1)S(1)} %shard_map.78.refs_6_), channel_id=1, source_target_pairs={{4,12},{6,14},{8,0},{10,2},{5,13},{7,15},{9,1},{11,3},{20,28},{22,... | collective-permute-start | bytes 983048 | tf_op jit(solution)/shard_map/ppermute | solution.py:247
  145.8 11.3 %collective-permute-start.24 = (bf16[128,1152]{1,0:T(8,128)(2,1)S(1)}, bf16[128,1152]{1,0:T(8,128)(2,1)S(1)}, u32[]{:S(2)}, u32[]{:S(2)}) collective-permute-start(bf16[128,1152]{1,0:T(8,128)(2,1)S(1)} %shard_map.80.refs_2_), channel_id=1, source_target_pairs={{4,12},{6,14},{8,0},{10,2},{5,13},{7,15},{9,1},{11,3},{20,28},{22,... | collective-permute-start | bytes 884744 | tf_op jit(solution)/shard_map/ppermute | solution.py:247
  149.0 11.3 %collective-permute-start.25 = (bf16[128,1152]{1,0:T(8,128)(2,1)S(1)}, bf16[128,1152]{1,0:T(8,128)(2,1)S(1)}, u32[]{:S(2)}, u32[]{:S(2)}) collective-permute-start(bf16[128,1152]{1,0:T(8,128)(2,1)S(1)} %shard_map.81.refs_1_), channel_id=1, source_target_pairs={{4,12},{6,14},{8,0},{10,2},{5,13},{7,15},{9,1},{11,3},{20,28},{22,... | collective-permute-start | bytes 884744 | tf_op jit(solution)/shard_map/ppermute | solution.py:247

commit v22 on v21

--- a/solution.py
+++ b/solution.py
@@ -334,7 +334,7 @@
     ]
     staying = {place for hop in hops for place in hop}
     kept, pieces_of_last = {}, []
-    edges = [-(-(width // 128) * k // 3) * 128 for k in range(4)]
+    edges = [-(-(width // 128) * k // 4) * 128 for k in range(5)]
     sizes = [b - a for a, b in zip(edges, edges[1:])]
 
     def spread_parts(maps, own_out, other_out, after=()):

time: 162 us -> 161 us (level)
  waiting for transfers between devices: 70.6 us -> 65.7 us
  starting transfers between devices: 40.8 us -> 45 us
    ppermute x15 -> x17, waiting for transfers between devices: 41.1 us -> 36.1 us  [along(): return lax.ppermute(block, 'node', moves)]
    ppermute x15 -> x17, starting transfers between devices: 30.3 us -> 34.5 us  [along(): return lax.ppermute(block, 'node', moves)]
    pallas_call x21 -> x23, Pallas kernels: 49.6 us -> 49.6 us  [call(): pl.pallas_call(body, out_shape=outs, in_specs=specs, out_specs=out_specs...]
  transfers between devices with their start and end apart: 26 -> 28, of which waited for: 13 -> 15; matrix products, arithmetic and copies ran while one was open for 0% -> 0% of each run, Pallas kernels for 30% -> 30%
where the time goes in v22:
time: 161 us
  waiting for transfers between devices  65.7 us (41%)
  Pallas kernels  49.6 us (31%)
  starting transfers between devices  45 us (28%)
    pallas_call x23, Pallas kernels, call(): pl.pallas_call(body, out_shape=outs, in_specs=specs, out_specs=out_specs...  49.6 us
    ppermute x17, waiting for transfers between devices, along(): return lax.ppermute(block, 'node', moves)  36.1 us
    ppermute x17, starting transfers between devices, along(): return lax.ppermute(block, 'node', moves)  34.5 us
    ppermute x8, waiting for transfers between devices, across(): return lax.ppermute(block, 'node', [(n, n ^ 1) for n in range(experts)])  29.6 us
    ppermute x8, starting transfers between devices, across(): return lax.ppermute(block, 'node', [(n, n ^ 1) for n in range(experts)])  9.51 us
  transfers between devices with their start and end apart: 28, of which 15 were waited for; matrix products, arithmetic and copies ran while one was open for 0% of the time, Pallas kernels for 30%

profile of v22, /device:TPU:0, one launch (start us, length us, event | category | flops | bytes accessed | tf_op | source)
XLA Modules:
  0.0 160.7 jit_solution(5984775339027178771)
XLA Ops:
  0.0 0.5 collective-permute-start.2
  0.5 0.1 collective-permute-start.4
  0.5 0.5 collective-permute-start.5
  1.0 1.2 shard_map.64.refs_0_
  2.2 4.5 %collective-permute-start.1 = (bf16[128,3712]{1,0:T(8,128)(2,1)S(1)}, bf16[128,3712]{1,0:T(8,128)(2,1)S(1)}, u32[]{:S(2)}, u32[]{:S(2)}) collective-permute-start(bf16[128,3712]{1,0:T(8,128)(2,1)S(1)} %shard_map.64.refs_0_), channel_id=1, source_target_pairs={{0,4},{2,6},{4,8},{6,10},{8,12},{10,14},{1,5},{3,7},{5,9},{7,11},{... | collective-permute-start | bytes 2850824 | tf_op jit(solution)/shard_map/ppermute | solution.py:247
  6.8 1.3 collective-permute-start
  8.1 19.6 %collective-permute-done.1.refs_1_.refs_2_ = bf16[128,3712]{1,0:T(8,128)(2,1)S(1)} collective-permute-done((bf16[128,3712]{1,0:T(8,128)(2,1)S(1)}, bf16[128,3712]{1,0:T(8,128)(2,1)S(1)}, u32[]{:S(2)}, u32[]{:S(2)}) %collective-permute-start.1) | collective-permute-done | bytes 950304 | tf_op jit(solution)/shard_map/ppermute | solution.py:247
  27.7 0.7 collective-permute-start.6
  28.4 3.5 %collective-permute-done.refs_0_ = bf16[128,3712]{1,0:T(8,128)(2,1)S(1)} collective-permute-done((bf16[128,3712]{1,0:T(8,128)(2,1)S(1)}, bf16[128,3712]{1,0:T(8,128)(2,1)S(1)}, u32[]{:S(2)}, u32[]{:S(2)}) %collective-permute-start) | collective-permute-done | bytes 950304 | tf_op jit(solution)/shard_map/ppermute | solution.py:247
  31.8 1.3 collective-permute-start.7
  33.1 1.0 shard_map.65
  34.2 1.6 collective-permute-start.8
  35.7 1.8 %shard_map.66 = (bf16[128,80]{1,0:T(8,128)(2,1)S(1)}, bf16[128,80]{1,0:T(8,128)(2,1)S(1)}, f32[128,128]{1,0:T(8,128)S(1)}, bf16[80,3584]{1,0:T(8,128)(2,1)}, bf16[80,3584]{1,0:T(8,128)(2,1)}) custom-call(bf16[128,3712]{1,0:T(8,128)(2,1)S(1)} %shard_map.64.refs_0_, bf16[128,80]{1,0:T(8,128)(2,1)S(1)} %get-tuple-element.40.refs_1_.refs_0_), custom_call_target="tpu_custom_call" | custom-call | tf_op jit(solution)/shard_map/pallas_call | solution.py:33
  37.6 0.6 collective-permute-start.3
  38.2 12.0 %collective-permute-done.8.refs_1_.refs_3_ = bf16[80,3584]{1,0:T(8,128)(2,1)S(1)} collective-permute-done((bf16[80,3584]{1,0:T(8,128)(2,1)S(1)}, bf16[80,3584]{1,0:T(8,128)(2,1)S(1)}, u32[]{:S(2)}, u32[]{:S(2)}) %collective-permute-start.8) | collective-permute-done | bytes 573472 | tf_op jit(solution)/shard_map/ppermute | solution.py:250
  50.1 9.6 %shard_map.67 = (bf16[80,3584]{1,0:T(8,128)(2,1)S(1)}, bf16[80,3584]{1,0:T(8,128)(2,1)S(1)}) custom-call(bf16[80,3584]{1,0:T(8,128)(2,1)S(1)} %get-tuple-element.46.refs_0_, bf16[80,3584]{1,0:T(8,128)(2,1)S(1)} %collective-permute-done.8.refs_1_.refs_3_, bf16[3584,512]{1,0:T(8,128)(2,1)} %bitcast.6, bf16[3584,512]{1,0:T(8,128)(2,1)} %bitcast.11, ...), custom_call_target="tpu_custom_call" | custom-call | bytes 67108864 | tf_op jit(solution)/shard_map/pallas_call | solution.py:33
  59.8 0.0 copy-start
  59.8 0.1 shard_map.68
  59.9 1.4 collective-permute-start.14
  61.4 0.7 collective-permute-start.15
  62.1 1.6 collective-permute-start.10
  63.7 1.2 shard_map.69
  64.9 0.6 collective-permute-start.13
  65.5 9.6 %shard_map.70 = (bf16[80,3584]{1,0:T(8,128)(2,1)S(1)}, bf16[80,3584]{1,0:T(8,128)(2,1)S(1)}) custom-call(bf16[80,3584]{1,0:T(8,128)(2,1)S(1)} %copy-done, bf16[80,3584]{1,0:T(8,128)(2,1)S(1)} %collective-permute-done.3.refs_5_.refs_1_, bf16[3584,512]{1,0:T(8,128)(2,1)} %bitcast.7, bf16[3584,512]{1,0:T(8,128)(2,1)} %bitcast.12, bf16[512,3584]{1,0:T(8,128)(2,1)} %bitcast.17, ...), custom_call_target="tpu_custom_call" | custom-call | tf_op jit(solution)/shard_map/pallas_call | solution.py:33
  75.1 3.0 %collective-permute-done.10.refs_4_ = bf16[80,3584]{1,0:T(8,128)(2,1)S(1)} collective-permute-done((bf16[80,3584]{1,0:T(8,128)(2,1)S(1)}, bf16[80,3584]{1,0:T(8,128)(2,1)S(1)}, u32[]{:S(2)}, u32[]{:S(2)}) %collective-permute-start.10) | collective-permute-done | bytes 573472 | tf_op jit(solution)/shard_map/ppermute | solution.py:250
  78.1 0.6 shard_map.71.refs_4_
  78.7 0.7 collective-permute-start.11
  79.4 5.2 %collective-permute-start.12 = (bf16[128,3584]{1,0:T(8,128)(2,1)S(1)}, bf16[128,3584]{1,0:T(8,128)(2,1)S(1)}, u32[]{:S(2)}, u32[]{:S(2)}) collective-permute-start(bf16[128,3584]{1,0:T(8,128)(2,1)S(1)} %shard_map.71.refs_4_), channel_id=1, source_target_pairs={{0,4},{2,6},{4,8},{6,10},{1,5},{3,7},{5,9},{7,11},{16,20},{18,22},... | collective-permute-start | bytes 2752520 | tf_op jit(solution)/shard_map/ppermute | solution.py:247
  84.7 1.3 shard_map.72
  86.0 1.6 collective-permute-start.17
  87.6 2.8 %collective-permute-done.13.refs_1_ = bf16[80,3584]{1,0:T(8,128)(2,1)S(1)} collective-permute-done((bf16[80,3584]{1,0:T(8,128)(2,1)S(1)}, bf16[80,3584]{1,0:T(8,128)(2,1)S(1)}, u32[]{:S(2)}, u32[]{:S(2)}) %collective-permute-start.13) | collective-permute-done | bytes 573472 | tf_op jit(solution)/shard_map/ppermute | solution.py:250
  90.4 9.6 %shard_map.73 = (bf16[80,3584]{1,0:T(8,128)(2,1)S(1)}, bf16[80,3584]{1,0:T(8,128)(2,1)S(1)}) custom-call(bf16[80,3584]{1,0:T(8,128)(2,1)S(1)} %get-tuple-element.59.refs_0_, bf16[80,3584]{1,0:T(8,128)(2,1)S(1)} %collective-permute-done.13.refs_1_, bf16[3584,512]{1,0:T(8,128)(2,1)} %bitcast.8, bf16[3584,512]{1,0:T(8,128)(2,1)} %bitcast.13, ...), custom_call_target="tpu_custom_call" | custom-call | tf_op jit(solution)/shard_map/pallas_call | solution.py:33
  100.0 1.6 collective-permute-start.16
  101.6 0.9 collective-permute-done.17.refs_1_
  102.5 9.6 %shard_map.74 = (bf16[80,3584]{1,0:T(8,128)(2,1)S(1)}, bf16[80,3584]{1,0:T(8,128)(2,1)S(1)}) custom-call(bf16[80,3584]{1,0:T(8,128)(2,1)S(1)} %get-tuple-element.64.refs_0_, bf16[80,3584]{1,0:T(8,128)(2,1)S(1)} %collective-permute-done.17.refs_1_, bf16[3584,512]{1,0:T(8,128)(2,1)} %bitcast.9, bf16[3584,512]{1,0:T(8,128)(2,1)} %bitcast.14, ...), custom_call_target="tpu_custom_call" | custom-call | tf_op jit(solution)/shard_map/pallas_call | solution.py:33
  112.2 0.6 shard_map.75.refs_5_
  112.8 4.4 %collective-permute-start.18 = (bf16[128,3584]{1,0:T(8,128)(2,1)S(1)}, bf16[128,3584]{1,0:T(8,128)(2,1)S(1)}, u32[]{:S(2)}, u32[]{:S(2)}) collective-permute-start(bf16[128,3584]{1,0:T(8,128)(2,1)S(1)} %shard_map.75.refs_5_), channel_id=1, source_target_pairs={{0,8},{2,10},{4,0},{6,2},{8,12},{10,14},{12,4},{14,6},{1,9},{3,11}... | collective-permute-start | bytes 2752520 | tf_op jit(solution)/shard_map/ppermute | solution.py:247
  117.2 1.5 collective-permute-start.19
  118.7 0.5 collective-permute-start.9
  119.2 10.9 %collective-permute-done.19.refs_4_ = bf16[80,3584]{1,0:T(8,128)(2,1)S(1)} collective-permute-done((bf16[80,3584]{1,0:T(8,128)(2,1)S(1)}, bf16[80,3584]{1,0:T(8,128)(2,1)S(1)}, u32[]{:S(2)}, u32[]{:S(2)}) %collective-permute-start.19) | collective-permute-done | bytes 573472 | tf_op jit(solution)/shard_map/ppermute | solution.py:250
  130.2 0.7 shard_map.76
  130.9 3.4 %collective-permute-start.20 = (bf16[128,896]{1,0:T(8,128)(2,1)S(1)}, bf16[128,896]{1,0:T(8,128)(2,1)S(1)}, u32[]{:S(2)}, u32[]{:S(2)}) collective-permute-start(bf16[128,896]{1,0:T(8,128)(2,1)S(1)} %get-tuple-element.71), channel_id=1, source_target_pairs={{0,4},{2,6},{12,8},{14,10},{1,5},{3,7},{13,9},{15,11},{16,20},{18,... | collective-permute-start | bytes 688136 | tf_op jit(solution)/shard_map/ppermute | solution.py:247
  134.3 1.3 collective-permute-start.24
  135.6 1.3 collective-permute-start.23
  137.0 2.9 %collective-permute-start.22 = (bf16[128,896]{1,0:T(8,128)(2,1)S(1)}, bf16[128,896]{1,0:T(8,128)(2,1)S(1)}, u32[]{:S(2)}, u32[]{:S(2)}) collective-permute-start(bf16[128,896]{1,0:T(8,128)(2,1)S(1)} %get-tuple-element.72), channel_id=1, source_target_pairs={{0,4},{2,6},{12,8},{14,10},{1,5},{3,7},{13,9},{15,11},{16,20},{18,... | collective-permute-start | bytes 688136 | tf_op jit(solution)/shard_map/ppermute | solution.py:247
  139.9 0.3 shard_map.77.refs_2_.refs_5_
  140.3 1.1 collective-permute-done.20.refs_1_
  141.3 0.1 shard_map.78.refs_6_
  141.4 1.3 collective-permute-start.21
  142.7 0.7 shard_map.79.refs_2_.total
  143.5 0.5 collective-permute-done.24.refs_1_
  144.0 0.1 shard_map.80.refs_2_
  144.0 1.3 collective-permute-start.25
  145.3 1.1 collective-permute-done.23.refs_1_
  146.4 0.1 shard_map.81.refs_2_
  146.5 1.3 collective-permute-start.26
  147.8 1.1 collective-permute-done.22.refs_1_
  148.9 0.1 shard_map.82.refs_1_
  148.9 1.3 collective-permute-start.27
  150.2 1.9 %collective-permute-done.21.refs_0_ = bf16[128,896]{1,0:T(8,128)(2,1)S(1)} collective-permute-done((bf16[128,896]{1,0:T(8,128)(2,1)S(1)}, bf16[128,896]{1,0:T(8,128)(2,1)S(1)}, u32[]{:S(2)}, u32[]{:S(2)}) %collective-permute-start.21) | collective-permute-done | bytes 229408 | tf_op jit(solution)/shard_map/ppermute | solution.py:247
  152.2 2.4 %collective-permute-done.25.refs_0_ = bf16[128,896]{1,0:T(8,128)(2,1)S(1)} collective-permute-done((bf16[128,896]{1,0:T(8,128)(2,1)S(1)}, bf16[128,896]{1,0:T(8,128)(2,1)S(1)}, u32[]{:S(2)}, u32[]{:S(2)}) %collective-permute-start.25) | collective-permute-done | bytes 229408 | tf_op jit(solution)/shard_map/ppermute | solution.py:247
  154.6 2.4 %collective-permute-done.26.refs_0_ = bf16[128,896]{1,0:T(8,128)(2,1)S(1)} collective-permute-done((bf16[128,896]{1,0:T(8,128)(2,1)S(1)}, bf16[128,896]{1,0:T(8,128)(2,1)S(1)}, u32[]{:S(2)}, u32[]{:S(2)}) %collective-permute-start.26) | collective-permute-done | bytes 229408 | tf_op jit(solution)/shard_map/ppermute | solution.py:247
  157.1 2.4 %collective-permute-done.27.refs_3_ = bf16[128,896]{1,0:T(8,128)(2,1)S(1)} collective-permute-done((bf16[128,896]{1,0:T(8,128)(2,1)S(1)}, bf16[128,896]{1,0:T(8,128)(2,1)S(1)}, u32[]{:S(2)}, u32[]{:S(2)}) %collective-permute-start.27) | collective-permute-done | bytes 229408 | tf_op jit(solution)/shard_map/ppermute | solution.py:247
  159.5 1.1 shard_map.86
  (17 shorter events, 0.1 us)
Async XLA Ops:
  0.0 33.1 %collective-permute-start.2 = (bf16[3584,512]{1,0:T(8,128)(2,1)}, bf16[3584,512]{1,0:T(8,128)(2,1)S(1)}, u32[]{:S(2)}, u32[]{:S(2)}) collective-permute-start(bf16[3584,512]{1,0:T(8,128)(2,1)} %bitcast.5), channel_id=1, source_target_pairs={{0,1},{1,0},{2,3},{3,2},{4,5},{5,4},{6,7},{7,6},{8,9},{9,8},{10,11... | collective-permute-start | bytes 11010056 | tf_op jit(solution)/shard_map/ppermute | solution.py:243
  0.5 37.1 %collective-permute-start.4 = (bf16[3584,512]{1,0:T(8,128)(2,1)}, bf16[3584,512]{1,0:T(8,128)(2,1)S(1)}, u32[]{:S(2)}, u32[]{:S(2)}) collective-permute-start(bf16[3584,512]{1,0:T(8,128)(2,1)} %bitcast.10), channel_id=1, source_target_pairs={{0,1},{1,0},{2,3},{3,2},{4,5},{5,4},{6,7},{7,6},{8,9},{9,8},{10,11... | collective-permute-start | bytes 11010056 | tf_op jit(solution)/shard_map/ppermute | solution.py:243
  0.5 37.7 %collective-permute-start.5 = (bf16[512,3584]{1,0:T(8,128)(2,1)}, bf16[512,3584]{1,0:T(8,128)(2,1)S(1)}, u32[]{:S(2)}, u32[]{:S(2)}) collective-permute-start(bf16[512,3584]{1,0:T(8,128)(2,1)} %bitcast.15), channel_id=1, source_target_pairs={{0,1},{1,0},{2,3},{3,2},{4,5},{5,4},{6,7},{7,6},{8,9},{9,8},{10,11... | collective-permute-start | bytes 11010056 | tf_op jit(solution)/shard_map/ppermute | solution.py:243
  2.2 25.5 %collective-permute-start.1 = (bf16[128,3712]{1,0:T(8,128)(2,1)S(1)}, bf16[128,3712]{1,0:T(8,128)(2,1)S(1)}, u32[]{:S(2)}, u32[]{:S(2)}) collective-permute-start(bf16[128,3712]{1,0:T(8,128)(2,1)S(1)} %shard_map.64.refs_0_), channel_id=1, source_target_pairs={{0,4},{2,6},{4,8},{6,10},{8,12},{10,14},{1,5},{3,7},{5,9},{7,11},{... | collective-permute-start | bytes 2850824 | tf_op jit(solution)/shard_map/ppermute | solution.py:247
  6.8 25.1 %collective-permute-start = (bf16[128,3712]{1,0:T(8,128)(2,1)S(1)}, bf16[128,3712]{1,0:T(8,128)(2,1)S(1)}, u32[]{:S(2)}, u32[]{:S(2)}) collective-permute-start(bf16[128,3712]{1,0:T(8,128)(2,1)S(1)} %shard_map.64.refs_0_), channel_id=1, source_target_pairs={{4,0},{6,2},{8,4},{10,6},{12,8},{14,10},{5,1},{7,3},{9,5},{11,7},{... | collective-permute-start | bytes 2850824 | tf_op jit(solution)/shard_map/ppermute | solution.py:247
  27.7 32.1 %collective-permute-start.6 = (bf16[128,3712]{1,0:T(8,128)(2,1)S(1)}, bf16[128,3712]{1,0:T(8,128)(2,1)S(1)}, u32[]{:S(2)}, u32[]{:S(2)}) collective-permute-start(bf16[128,3712]{1,0:T(8,128)(2,1)S(1)} %collective-permute-done.1.refs_1_.refs_2_), channel_id=1, source_target_pairs={{4,8},{6,10},{8,12},{10,14},{5,9},{7,11},{9,13},{11,15},{20,24},{2... | collective-permute-start | bytes 2850824 | tf_op jit(solution)/shard_map/ppermute | solution.py:247
  31.8 28.0 %collective-permute-start.7 = (bf16[128,3712]{1,0:T(8,128)(2,1)S(1)}, bf16[128,3712]{1,0:T(8,128)(2,1)S(1)}, u32[]{:S(2)}, u32[]{:S(2)}) collective-permute-start(bf16[128,3712]{1,0:T(8,128)(2,1)S(1)} %collective-permute-done.refs_0_), channel_id=1, source_target_pairs={{4,0},{6,2},{8,4},{10,6},{5,1},{7,3},{9,5},{11,7},{20,16},{22,18},... | collective-permute-start | bytes 2850824 | tf_op jit(solution)/shard_map/ppermute | solution.py:247
  34.2 16.0 %collective-permute-start.8 = (bf16[80,3584]{1,0:T(8,128)(2,1)S(1)}, bf16[80,3584]{1,0:T(8,128)(2,1)S(1)}, u32[]{:S(2)}, u32[]{:S(2)}) collective-permute-start(bf16[80,3584]{1,0:T(8,128)(2,1)S(1)} %get-tuple-element.47), channel_id=1, source_target_pairs={{0,2},{2,0},{4,6},{6,4},{8,10},{10,8},{12,14},{14,12},{1,3},{3,1},... | collective-permute-start | bytes 1720328 | tf_op jit(solution)/shard_map/ppermute | solution.py:250
  37.6 26.1 %collective-permute-start.3 = (bf16[80,3584]{1,0:T(8,128)(2,1)}, bf16[80,3584]{1,0:T(8,128)(2,1)S(1)}, u32[]{:S(2)}, u32[]{:S(2)}) collective-permute-start(bf16[80,3584]{1,0:T(8,128)(2,1)} %get-tuple-element.45), channel_id=1, source_target_pairs={{0,2},{2,0},{4,6},{6,4},{8,10},{10,8},{12,14},{14,12},{1,3},{3,1},... | collective-permute-start | bytes 1720328 | tf_op jit(solution)/shard_map/ppermute | solution.py:250
  59.8 5.7 %copy-start = (bf16[80,3584]{1,0:T(8,128)(2,1)S(1)}, bf16[80,3584]{1,0:T(8,128)(2,1)}, u32[]{:S(2)}) copy-start(bf16[80,3584]{1,0:T(8,128)(2,1)} %get-tuple-element.44.refs_0_) | copy-start | bytes 1720324
  59.9 24.7 %collective-permute-start.14 = (bf16[128,3712]{1,0:T(8,128)(2,1)S(1)}, bf16[128,3712]{1,0:T(8,128)(2,1)S(1)}, u32[]{:S(2)}, u32[]{:S(2)}) collective-permute-start(bf16[128,3712]{1,0:T(8,128)(2,1)S(1)} %get-tuple-element.49.refs_1_.refs_0_), channel_id=1, source_target_pairs={{4,0},{6,2},{5,1},{7,3},{20,16},{22,18},{21,17},{23,19}} | collective-permute-start | bytes 2850824 | tf_op jit(solution)/shard_map/ppermute | solution.py:247
  61.4 23.3 %collective-permute-start.15 = (bf16[128,3712]{1,0:T(8,128)(2,1)S(1)}, bf16[128,3712]{1,0:T(8,128)(2,1)S(1)}, u32[]{:S(2)}, u32[]{:S(2)}) collective-permute-start(bf16[128,3712]{1,0:T(8,128)(2,1)S(1)} %get-tuple-element.50.refs_3_.refs_2_), channel_id=1, source_target_pairs={{8,12},{10,14},{9,13},{11,15},{24,28},{26,30},{25,29},{27,31}} | collective-permute-start | bytes 2850824 | tf_op jit(solution)/shard_map/ppermute | solution.py:247
  62.1 16.0 %collective-permute-start.10 = (bf16[80,3584]{1,0:T(8,128)(2,1)S(1)}, bf16[80,3584]{1,0:T(8,128)(2,1)S(1)}, u32[]{:S(2)}, u32[]{:S(2)}) collective-permute-start(bf16[80,3584]{1,0:T(8,128)(2,1)S(1)} %get-tuple-element.56), channel_id=1, source_target_pairs={{0,2},{2,0},{4,6},{6,4},{8,10},{10,8},{12,14},{14,12},{1,3},{3,1},... | collective-permute-start | bytes 1720328 | tf_op jit(solution)/shard_map/ppermute | solution.py:250
  64.9 25.5 %collective-permute-start.13 = (bf16[80,3584]{1,0:T(8,128)(2,1)S(1)}, bf16[80,3584]{1,0:T(8,128)(2,1)S(1)}, u32[]{:S(2)}, u32[]{:S(2)}) collective-permute-start(bf16[80,3584]{1,0:T(8,128)(2,1)S(1)} %get-tuple-element.60), channel_id=1, source_target_pairs={{0,2},{2,0},{4,6},{6,4},{8,10},{10,8},{12,14},{14,12},{1,3},{3,1},... | collective-permute-start | bytes 1720328 | tf_op jit(solution)/shard_map/ppermute | solution.py:250
  78.7 33.4 %collective-permute-start.11 = (bf16[128,3584]{1,0:T(8,128)(2,1)S(1)}, bf16[128,3584]{1,0:T(8,128)(2,1)S(1)}, u32[]{:S(2)}, u32[]{:S(2)}) collective-permute-start(bf16[128,3584]{1,0:T(8,128)(2,1)S(1)} %shard_map.71.refs_4_), channel_id=1, source_target_pairs={{8,4},{10,6},{12,8},{14,10},{9,5},{11,7},{13,9},{15,11},{24,20},{2... | collective-permute-start | bytes 2752520 | tf_op jit(solution)/shard_map/ppermute | solution.py:247
  79.4 32.7 %collective-permute-start.12 = (bf16[128,3584]{1,0:T(8,128)(2,1)S(1)}, bf16[128,3584]{1,0:T(8,128)(2,1)S(1)}, u32[]{:S(2)}, u32[]{:S(2)}) collective-permute-start(bf16[128,3584]{1,0:T(8,128)(2,1)S(1)} %shard_map.71.refs_4_), channel_id=1, source_target_pairs={{0,4},{2,6},{4,8},{6,10},{1,5},{3,7},{5,9},{7,11},{16,20},{18,22},... | collective-permute-start | bytes 2752520 | tf_op jit(solution)/shard_map/ppermute | solution.py:247
  86.0 16.5 %collective-permute-start.17 = (bf16[80,3584]{1,0:T(8,128)(2,1)S(1)}, bf16[80,3584]{1,0:T(8,128)(2,1)S(1)}, u32[]{:S(2)}, u32[]{:S(2)}) collective-permute-start(bf16[80,3584]{1,0:T(8,128)(2,1)S(1)} %get-tuple-element.65), channel_id=1, source_target_pairs={{0,2},{2,0},{4,6},{6,4},{8,10},{10,8},{12,14},{14,12},{1,3},{3,1},... | collective-permute-start | bytes 1720328 | tf_op jit(solution)/shard_map/ppermute | solution.py:250
  100.0 12.1 %collective-permute-start.16 = (bf16[80,3584]{1,0:T(8,128)(2,1)S(1)}, bf16[80,3584]{1,0:T(8,128)(2,1)S(1)}, u32[]{:S(2)}, u32[]{:S(2)}) collective-permute-start(bf16[80,3584]{1,0:T(8,128)(2,1)S(1)} %get-tuple-element.63), channel_id=1, source_target_pairs={{0,2},{2,0},{4,6},{6,4},{8,10},{10,8},{12,14},{14,12},{1,3},{3,1},... | collective-permute-start | bytes 1720328 | tf_op jit(solution)/shard_map/ppermute | solution.py:250
  112.8 24.2 %collective-permute-start.18 = (bf16[128,3584]{1,0:T(8,128)(2,1)S(1)}, bf16[128,3584]{1,0:T(8,128)(2,1)S(1)}, u32[]{:S(2)}, u32[]{:S(2)}) collective-permute-start(bf16[128,3584]{1,0:T(8,128)(2,1)S(1)} %shard_map.75.refs_5_), channel_id=1, source_target_pairs={{0,8},{2,10},{4,0},{6,2},{8,12},{10,14},{12,4},{14,6},{1,9},{3,11}... | collective-permute-start | bytes 2752520 | tf_op jit(solution)/shard_map/ppermute | solution.py:247
  117.2 13.0 %collective-permute-start.19 = (bf16[80,3584]{1,0:T(8,128)(2,1)S(1)}, bf16[80,3584]{1,0:T(8,128)(2,1)S(1)}, u32[]{:S(2)}, u32[]{:S(2)}) collective-permute-start(bf16[80,3584]{1,0:T(8,128)(2,1)S(1)} %get-tuple-element.69), channel_id=1, source_target_pairs={{0,2},{2,0},{4,6},{6,4},{8,10},{10,8},{12,14},{14,12},{1,3},{3,1},... | collective-permute-start | bytes 1720328 | tf_op jit(solution)/shard_map/ppermute | solution.py:250
  118.7 24.0 %collective-permute-start.9 = (bf16[80,3584]{1,0:T(8,128)(2,1)S(1)}, bf16[80,3584]{1,0:T(8,128)(2,1)S(1)}, u32[]{:S(2)}, u32[]{:S(2)}) collective-permute-start(bf16[80,3584]{1,0:T(8,128)(2,1)S(1)} %get-tuple-element.53), channel_id=1, source_target_pairs={{0,2},{2,0},{4,6},{6,4},{8,10},{10,8},{12,14},{14,12},{1,3},{3,1},... | collective-permute-start | bytes 1720328 | tf_op jit(solution)/shard_map/ppermute | solution.py:250
  130.9 10.4 %collective-permute-start.20 = (bf16[128,896]{1,0:T(8,128)(2,1)S(1)}, bf16[128,896]{1,0:T(8,128)(2,1)S(1)}, u32[]{:S(2)}, u32[]{:S(2)}) collective-permute-start(bf16[128,896]{1,0:T(8,128)(2,1)S(1)} %get-tuple-element.71), channel_id=1, source_target_pairs={{0,4},{2,6},{12,8},{14,10},{1,5},{3,7},{13,9},{15,11},{16,20},{18,... | collective-permute-start | bytes 688136 | tf_op jit(solution)/shard_map/ppermute | solution.py:247
  134.3 9.6 %collective-permute-start.24 = (bf16[128,896]{1,0:T(8,128)(2,1)S(1)}, bf16[128,896]{1,0:T(8,128)(2,1)S(1)}, u32[]{:S(2)}, u32[]{:S(2)}) collective-permute-start(bf16[128,896]{1,0:T(8,128)(2,1)S(1)} %get-tuple-element.74), channel_id=1, source_target_pairs={{0,4},{2,6},{12,8},{14,10},{1,5},{3,7},{13,9},{15,11},{16,20},{18,... | collective-permute-start | bytes 688136 | tf_op jit(solution)/shard_map/ppermute | solution.py:247
  135.6 10.8 %collective-permute-start.23 = (bf16[128,896]{1,0:T(8,128)(2,1)S(1)}, bf16[128,896]{1,0:T(8,128)(2,1)S(1)}, u32[]{:S(2)}, u32[]{:S(2)}) collective-permute-start(bf16[128,896]{1,0:T(8,128)(2,1)S(1)} %get-tuple-element.73), channel_id=1, source_target_pairs={{0,4},{2,6},{12,8},{14,10},{1,5},{3,7},{13,9},{15,11},{16,20},{18,... | collective-permute-start | bytes 688136 | tf_op jit(solution)/shard_map/ppermute | solution.py:247
  137.0 11.9 %collective-permute-start.22 = (bf16[128,896]{1,0:T(8,128)(2,1)S(1)}, bf16[128,896]{1,0:T(8,128)(2,1)S(1)}, u32[]{:S(2)}, u32[]{:S(2)}) collective-permute-start(bf16[128,896]{1,0:T(8,128)(2,1)S(1)} %get-tuple-element.72), channel_id=1, source_target_pairs={{0,4},{2,6},{12,8},{14,10},{1,5},{3,7},{13,9},{15,11},{16,20},{18,... | collective-permute-start | bytes 688136 | tf_op jit(solution)/shard_map/ppermute | solution.py:247
  141.4 10.8 %collective-permute-start.21 = (bf16[128,896]{1,0:T(8,128)(2,1)S(1)}, bf16[128,896]{1,0:T(8,128)(2,1)S(1)}, u32[]{:S(2)}, u32[]{:S(2)}) collective-permute-start(bf16[128,896]{1,0:T(8,128)(2,1)S(1)} %shard_map.78.refs_6_), channel_id=1, source_target_pairs={{4,12},{6,14},{8,0},{10,2},{5,13},{7,15},{9,1},{11,3},{20,28},{22,... | collective-permute-start | bytes 688136 | tf_op jit(solution)/shard_map/ppermute | solution.py:247
  144.0 10.6 %collective-permute-start.25 = (bf16[128,896]{1,0:T(8,128)(2,1)S(1)}, bf16[128,896]{1,0:T(8,128)(2,1)S(1)}, u32[]{:S(2)}, u32[]{:S(2)}) collective-permute-start(bf16[128,896]{1,0:T(8,128)(2,1)S(1)} %shard_map.80.refs_2_), channel_id=1, source_target_pairs={{4,12},{6,14},{8,0},{10,2},{5,13},{7,15},{9,1},{11,3},{20,28},{22,... | collective-permute-start | bytes 688136 | tf_op jit(solution)/shard_map/ppermute | solution.py:247
  146.5 10.6 %collective-permute-start.26 = (bf16[128,896]{1,0:T(8,128)(2,1)S(1)}, bf16[128,896]{1,0:T(8,128)(2,1)S(1)}, u32[]{:S(2)}, u32[]{:S(2)}) collective-permute-start(bf16[128,896]{1,0:T(8,128)(2,1)S(1)} %shard_map.81.refs_2_), channel_id=1, source_target_pairs={{4,12},{6,14},{8,0},{10,2},{5,13},{7,15},{9,1},{11,3},{20,28},{22,... | collective-permute-start | bytes 688136 | tf_op jit(solution)/shard_map/ppermute | solution.py:247
  148.9 10.6 %collective-permute-start.27 = (bf16[128,896]{1,0:T(8,128)(2,1)S(1)}, bf16[128,896]{1,0:T(8,128)(2,1)S(1)}, u32[]{:S(2)}, u32[]{:S(2)}) collective-permute-start(bf16[128,896]{1,0:T(8,128)(2,1)S(1)} %shard_map.82.refs_1_), channel_id=1, source_target_pairs={{4,12},{6,14},{8,0},{10,2},{5,13},{7,15},{9,1},{11,3},{20,28},{22,... | collective-permute-start | bytes 688136 | tf_op jit(solution)/shard_map/ppermute | solution.py:247

commit v23 on v22

--- a/solution.py
+++ b/solution.py
@@ -334,7 +334,7 @@
     ]
     staying = {place for hop in hops for place in hop}
     kept, pieces_of_last = {}, []
-    edges = [-(-(width // 128) * k // 4) * 128 for k in range(5)]
+    edges = [-(-(width // 128) * k // 5) * 128 for k in range(6)]
     sizes = [b - a for a, b in zip(edges, edges[1:])]
 
     def spread_parts(maps, own_out, other_out, after=()):

time: 161 us -> 165 us (1.025)
  starting transfers between devices: 45 us -> 49 us
    ppermute x17 -> x19, starting transfers between devices: 34.5 us -> 38.5 us  [along(): return lax.ppermute(block, 'node', moves)]
    ppermute x17 -> x19, waiting for transfers between devices: 36.1 us -> 35.4 us  [along(): return lax.ppermute(block, 'node', moves)]
    pallas_call x23 -> x25, Pallas kernels: 49.6 us -> 49.6 us  [call(): pl.pallas_call(body, out_shape=outs, in_specs=specs, out_specs=out_specs...]
  transfers between devices with their start and end apart: 28 -> 30, of which waited for: 15 -> 12; matrix products, arithmetic and copies ran while one was open for 0% -> 0% of each run, Pallas kernels for 30% -> 29%
where the time goes in v23:
time: 165 us; the launch traced here: 164 us
  waiting for transfers between devices  65 us (39%)
  Pallas kernels  49.6 us (30%)
  starting transfers between devices  49 us (30%)
    pallas_call x25, Pallas kernels, call(): pl.pallas_call(body, out_shape=outs, in_specs=specs, out_specs=out_specs...  49.6 us
    ppermute x19, starting transfers between devices, along(): return lax.ppermute(block, 'node', moves)  38.5 us
    ppermute x19, waiting for transfers between devices, along(): return lax.ppermute(block, 'node', moves)  35.4 us
    ppermute x8, waiting for transfers between devices, across(): return lax.ppermute(block, 'node', [(n, n ^ 1) for n in range(experts)])  29.6 us
    ppermute x8, starting transfers between devices, across(): return lax.ppermute(block, 'node', [(n, n ^ 1) for n in range(experts)])  9.51 us
  transfers between devices with their start and end apart: 30, of which 12 were waited for; matrix products, arithmetic and copies ran while one was open for 0% of the time, Pallas kernels for 29%

profile of v23, /device:TPU:0, one launch (start us, length us, event | category | flops | bytes accessed | tf_op | source)
XLA Modules:
  0.0 164.1 jit_solution(12000359254715737859)
XLA Ops:
  0.0 0.5 collective-permute-start.2
  0.5 0.1 collective-permute-start.4
  0.5 0.5 collective-permute-start.5
  1.0 1.2 shard_map.64.refs_0_
  2.2 4.5 %collective-permute-start.1 = (bf16[128,3712]{1,0:T(8,128)(2,1)S(1)}, bf16[128,3712]{1,0:T(8,128)(2,1)S(1)}, u32[]{:S(2)}, u32[]{:S(2)}) collective-permute-start(bf16[128,3712]{1,0:T(8,128)(2,1)S(1)} %shard_map.64.refs_0_), channel_id=1, source_target_pairs={{0,4},{2,6},{4,8},{6,10},{8,12},{10,14},{1,5},{3,7},{5,9},{7,11},{... | collective-permute-start | bytes 2850824 | tf_op jit(solution)/shard_map/ppermute | solution.py:247
  6.8 1.3 collective-permute-start
  8.1 19.6 %collective-permute-done.1.refs_1_.refs_2_ = bf16[128,3712]{1,0:T(8,128)(2,1)S(1)} collective-permute-done((bf16[128,3712]{1,0:T(8,128)(2,1)S(1)}, bf16[128,3712]{1,0:T(8,128)(2,1)S(1)}, u32[]{:S(2)}, u32[]{:S(2)}) %collective-permute-start.1) | collective-permute-done | bytes 950304 | tf_op jit(solution)/shard_map/ppermute | solution.py:247
  27.7 0.7 collective-permute-start.6
  28.4 3.5 %collective-permute-done.refs_0_ = bf16[128,3712]{1,0:T(8,128)(2,1)S(1)} collective-permute-done((bf16[128,3712]{1,0:T(8,128)(2,1)S(1)}, bf16[128,3712]{1,0:T(8,128)(2,1)S(1)}, u32[]{:S(2)}, u32[]{:S(2)}) %collective-permute-start) | collective-permute-done | bytes 950304 | tf_op jit(solution)/shard_map/ppermute | solution.py:247
  31.8 1.3 collective-permute-start.7
  33.1 1.0 shard_map.65
  34.2 1.6 collective-permute-start.8
  35.7 1.8 %shard_map.66 = (bf16[128,80]{1,0:T(8,128)(2,1)S(1)}, bf16[128,80]{1,0:T(8,128)(2,1)S(1)}, f32[128,128]{1,0:T(8,128)S(1)}, bf16[80,3584]{1,0:T(8,128)(2,1)}, bf16[80,3584]{1,0:T(8,128)(2,1)}) custom-call(bf16[128,3712]{1,0:T(8,128)(2,1)S(1)} %shard_map.64.refs_0_, bf16[128,80]{1,0:T(8,128)(2,1)S(1)} %get-tuple-element.41.refs_1_.refs_0_), custom_call_target="tpu_custom_call" | custom-call | tf_op jit(solution)/shard_map/pallas_call | solution.py:33
  37.6 0.0 collective-permute-done.4.refs_6_
  37.6 0.6 collective-permute-start.3
  38.2 0.0 collective-permute-done.5.refs_7_
  38.2 12.0 %collective-permute-done.8.refs_1_.refs_3_ = bf16[80,3584]{1,0:T(8,128)(2,1)S(1)} collective-permute-done((bf16[80,3584]{1,0:T(8,128)(2,1)S(1)}, bf16[80,3584]{1,0:T(8,128)(2,1)S(1)}, u32[]{:S(2)}, u32[]{:S(2)}) %collective-permute-start.8) | collective-permute-done | bytes 573472 | tf_op jit(solution)/shard_map/ppermute | solution.py:250
  50.1 9.6 %shard_map.67 = (bf16[80,3584]{1,0:T(8,128)(2,1)S(1)}, bf16[80,3584]{1,0:T(8,128)(2,1)S(1)}) custom-call(bf16[80,3584]{1,0:T(8,128)(2,1)S(1)} %get-tuple-element.47.refs_0_, bf16[80,3584]{1,0:T(8,128)(2,1)S(1)} %collective-permute-done.8.refs_1_.refs_3_, bf16[3584,512]{1,0:T(8,128)(2,1)} %bitcast.6, bf16[3584,512]{1,0:T(8,128)(2,1)} %bitcast.11, ...), custom_call_target="tpu_custom_call" | custom-call | bytes 67108864 | tf_op jit(solution)/shard_map/pallas_call | solution.py:33
  59.8 0.0 collective-permute-done.6.refs_0_
  59.8 0.0 copy-start
  59.8 0.1 shard_map.68
  59.9 1.4 collective-permute-start.14
  61.4 0.7 collective-permute-start.15
  62.1 1.6 collective-permute-start.10
  63.7 0.0 collective-permute-done.3.refs_5_.refs_1_
  63.7 1.2 shard_map.69
  64.9 0.6 collective-permute-start.13
  65.5 9.6 %shard_map.70 = (bf16[80,3584]{1,0:T(8,128)(2,1)S(1)}, bf16[80,3584]{1,0:T(8,128)(2,1)S(1)}) custom-call(bf16[80,3584]{1,0:T(8,128)(2,1)S(1)} %copy-done, bf16[80,3584]{1,0:T(8,128)(2,1)S(1)} %collective-permute-done.3.refs_5_.refs_1_, bf16[3584,512]{1,0:T(8,128)(2,1)} %bitcast.7, bf16[3584,512]{1,0:T(8,128)(2,1)} %bitcast.12, bf16[512,3584]{1,0:T(8,128)(2,1)} %bitcast.17, ...), custom_call_target="tpu_custom_call" | custom-call | tf_op jit(solution)/shard_map/pallas_call | solution.py:33
  75.1 3.0 %collective-permute-done.10.refs_4_ = bf16[80,3584]{1,0:T(8,128)(2,1)S(1)} collective-permute-done((bf16[80,3584]{1,0:T(8,128)(2,1)S(1)}, bf16[80,3584]{1,0:T(8,128)(2,1)S(1)}, u32[]{:S(2)}, u32[]{:S(2)}) %collective-permute-start.10) | collective-permute-done | bytes 573472 | tf_op jit(solution)/shard_map/ppermute | solution.py:250
  78.1 0.6 shard_map.71.refs_4_
  78.7 0.7 collective-permute-start.11
  79.4 5.2 %collective-permute-start.12 = (bf16[128,3584]{1,0:T(8,128)(2,1)S(1)}, bf16[128,3584]{1,0:T(8,128)(2,1)S(1)}, u32[]{:S(2)}, u32[]{:S(2)}) collective-permute-start(bf16[128,3584]{1,0:T(8,128)(2,1)S(1)} %shard_map.71.refs_4_), channel_id=1, source_target_pairs={{0,4},{2,6},{4,8},{6,10},{1,5},{3,7},{5,9},{7,11},{16,20},{18,22},... | collective-permute-start | bytes 2752520 | tf_op jit(solution)/shard_map/ppermute | solution.py:247
  84.7 0.0 collective-permute-done.14.refs_1_
  84.7 1.3 shard_map.72
  86.0 1.6 collective-permute-start.17
  87.6 2.8 %collective-permute-done.13.refs_1_ = bf16[80,3584]{1,0:T(8,128)(2,1)S(1)} collective-permute-done((bf16[80,3584]{1,0:T(8,128)(2,1)S(1)}, bf16[80,3584]{1,0:T(8,128)(2,1)S(1)}, u32[]{:S(2)}, u32[]{:S(2)}) %collective-permute-start.13) | collective-permute-done | bytes 573472 | tf_op jit(solution)/shard_map/ppermute | solution.py:250
  90.4 9.6 %shard_map.73 = (bf16[80,3584]{1,0:T(8,128)(2,1)S(1)}, bf16[80,3584]{1,0:T(8,128)(2,1)S(1)}) custom-call(bf16[80,3584]{1,0:T(8,128)(2,1)S(1)} %get-tuple-element.60.refs_0_, bf16[80,3584]{1,0:T(8,128)(2,1)S(1)} %collective-permute-done.13.refs_1_, bf16[3584,512]{1,0:T(8,128)(2,1)} %bitcast.8, bf16[3584,512]{1,0:T(8,128)(2,1)} %bitcast.13, ...), custom_call_target="tpu_custom_call" | custom-call | tf_op jit(solution)/shard_map/pallas_call | solution.py:33
  100.0 1.6 collective-permute-start.16
  101.6 0.9 collective-permute-done.17.refs_1_
  102.5 9.6 %shard_map.74 = (bf16[80,3584]{1,0:T(8,128)(2,1)S(1)}, bf16[80,3584]{1,0:T(8,128)(2,1)S(1)}) custom-call(bf16[80,3584]{1,0:T(8,128)(2,1)S(1)} %get-tuple-element.65.refs_0_, bf16[80,3584]{1,0:T(8,128)(2,1)S(1)} %collective-permute-done.17.refs_1_, bf16[3584,512]{1,0:T(8,128)(2,1)} %bitcast.9, bf16[3584,512]{1,0:T(8,128)(2,1)} %bitcast.14, ...), custom_call_target="tpu_custom_call" | custom-call | tf_op jit(solution)/shard_map/pallas_call | solution.py:33
  112.2 0.6 shard_map.75.refs_5_
  112.8 4.4 %collective-permute-start.18 = (bf16[128,3584]{1,0:T(8,128)(2,1)S(1)}, bf16[128,3584]{1,0:T(8,128)(2,1)S(1)}, u32[]{:S(2)}, u32[]{:S(2)}) collective-permute-start(bf16[128,3584]{1,0:T(8,128)(2,1)S(1)} %shard_map.75.refs_5_), channel_id=1, source_target_pairs={{0,8},{2,10},{4,0},{6,2},{8,12},{10,14},{12,4},{14,6},{1,9},{3,11}... | collective-permute-start | bytes 2752520 | tf_op jit(solution)/shard_map/ppermute | solution.py:247
  117.2 1.5 collective-permute-start.19
  118.7 0.5 collective-permute-start.9
  119.2 10.9 %collective-permute-done.19.refs_4_ = bf16[80,3584]{1,0:T(8,128)(2,1)S(1)} collective-permute-done((bf16[80,3584]{1,0:T(8,128)(2,1)S(1)}, bf16[80,3584]{1,0:T(8,128)(2,1)S(1)}, u32[]{:S(2)}, u32[]{:S(2)}) %collective-permute-start.19) | collective-permute-done | bytes 573472 | tf_op jit(solution)/shard_map/ppermute | solution.py:250
  130.2 0.7 shard_map.76
  130.9 3.4 %collective-permute-start.20 = (bf16[128,768]{1,0:T(8,128)(2,1)S(1)}, bf16[128,768]{1,0:T(8,128)(2,1)S(1)}, u32[]{:S(2)}, u32[]{:S(2)}) collective-permute-start(bf16[128,768]{1,0:T(8,128)(2,1)S(1)} %get-tuple-element.72), channel_id=1, source_target_pairs={{0,4},{2,6},{12,8},{14,10},{1,5},{3,7},{13,9},{15,11},{16,20},{18,... | collective-permute-start | bytes 589832 | tf_op jit(solution)/shard_map/ppermute | solution.py:247
  134.3 1.3 collective-permute-start.25
  135.6 1.3 collective-permute-start.23
  136.9 3.7 %collective-permute-done.20.refs_1_ = bf16[128,768]{1,0:T(8,128)(2,1)S(1)} collective-permute-done((bf16[128,768]{1,0:T(8,128)(2,1)S(1)}, bf16[128,768]{1,0:T(8,128)(2,1)S(1)}, u32[]{:S(2)}, u32[]{:S(2)}) %collective-permute-start.20) | collective-permute-done | bytes 196640 | tf_op jit(solution)/shard_map/ppermute | solution.py:247
  140.7 4.4 %collective-permute-start.24 = (bf16[128,640]{1,0:T(8,128)(2,1)S(1)}, bf16[128,640]{1,0:T(8,128)(2,1)S(1)}, u32[]{:S(2)}, u32[]{:S(2)}) collective-permute-start(bf16[128,640]{1,0:T(8,128)(2,1)S(1)} %get-tuple-element.75), channel_id=1, source_target_pairs={{0,4},{2,6},{12,8},{14,10},{1,5},{3,7},{13,9},{15,11},{16,20},{18,... | collective-permute-start | bytes 491528 | tf_op jit(solution)/shard_map/ppermute | solution.py:247
  145.1 1.3 collective-permute-start.22
  146.4 0.3 shard_map.77.refs_2_.refs_5_
  146.8 1.3 collective-permute-start.21
  148.1 0.7 shard_map.79.refs_2_.total
  148.9 1.3 collective-permute-start.26
  150.3 1.3 collective-permute-start.28
  151.6 1.3 collective-permute-start.27
  153.0 1.3 collective-permute-start.29
  154.3 1.0 collective-permute-done.21.refs_0_
  155.3 2.1 %collective-permute-done.26.refs_0_ = bf16[128,768]{1,0:T(8,128)(2,1)S(1)} collective-permute-done((bf16[128,768]{1,0:T(8,128)(2,1)S(1)}, bf16[128,768]{1,0:T(8,128)(2,1)S(1)}, u32[]{:S(2)}, u32[]{:S(2)}) %collective-permute-start.26) | collective-permute-done | bytes 196640 | tf_op jit(solution)/shard_map/ppermute | solution.py:247
  157.4 3.8 %collective-permute-done.27.refs_0_ = bf16[128,640]{1,0:T(8,128)(2,1)S(1)} collective-permute-done((bf16[128,640]{1,0:T(8,128)(2,1)S(1)}, bf16[128,640]{1,0:T(8,128)(2,1)S(1)}, u32[]{:S(2)}, u32[]{:S(2)}) %collective-permute-start.27) | collective-permute-done | bytes 163872 | tf_op jit(solution)/shard_map/ppermute | solution.py:247
  161.3 1.7 %collective-permute-done.29.refs_4_ = bf16[128,640]{1,0:T(8,128)(2,1)S(1)} collective-permute-done((bf16[128,640]{1,0:T(8,128)(2,1)S(1)}, bf16[128,640]{1,0:T(8,128)(2,1)S(1)}, u32[]{:S(2)}, u32[]{:S(2)}) %collective-permute-start.29) | collective-permute-done | bytes 163872 | tf_op jit(solution)/shard_map/ppermute | solution.py:247
  163.0 1.1 shard_map.88
  (23 shorter events, 0.3 us)
Async XLA Ops:
  0.0 33.1 %collective-permute-start.2 = (bf16[3584,512]{1,0:T(8,128)(2,1)}, bf16[3584,512]{1,0:T(8,128)(2,1)S(1)}, u32[]{:S(2)}, u32[]{:S(2)}) collective-permute-start(bf16[3584,512]{1,0:T(8,128)(2,1)} %bitcast.5), channel_id=1, source_target_pairs={{0,1},{1,0},{2,3},{3,2},{4,5},{5,4},{6,7},{7,6},{8,9},{9,8},{10,11... | collective-permute-start | bytes 11010056 | tf_op jit(solution)/shard_map/ppermute | solution.py:243
  0.5 37.2 %collective-permute-start.4 = (bf16[3584,512]{1,0:T(8,128)(2,1)}, bf16[3584,512]{1,0:T(8,128)(2,1)S(1)}, u32[]{:S(2)}, u32[]{:S(2)}) collective-permute-start(bf16[3584,512]{1,0:T(8,128)(2,1)} %bitcast.10), channel_id=1, source_target_pairs={{0,1},{1,0},{2,3},{3,2},{4,5},{5,4},{6,7},{7,6},{8,9},{9,8},{10,11... | collective-permute-start | bytes 11010056 | tf_op jit(solution)/shard_map/ppermute | solution.py:243
  0.5 37.7 %collective-permute-start.5 = (bf16[512,3584]{1,0:T(8,128)(2,1)}, bf16[512,3584]{1,0:T(8,128)(2,1)S(1)}, u32[]{:S(2)}, u32[]{:S(2)}) collective-permute-start(bf16[512,3584]{1,0:T(8,128)(2,1)} %bitcast.15), channel_id=1, source_target_pairs={{0,1},{1,0},{2,3},{3,2},{4,5},{5,4},{6,7},{7,6},{8,9},{9,8},{10,11... | collective-permute-start | bytes 11010056 | tf_op jit(solution)/shard_map/ppermute | solution.py:243
  2.2 25.5 %collective-permute-start.1 = (bf16[128,3712]{1,0:T(8,128)(2,1)S(1)}, bf16[128,3712]{1,0:T(8,128)(2,1)S(1)}, u32[]{:S(2)}, u32[]{:S(2)}) collective-permute-start(bf16[128,3712]{1,0:T(8,128)(2,1)S(1)} %shard_map.64.refs_0_), channel_id=1, source_target_pairs={{0,4},{2,6},{4,8},{6,10},{8,12},{10,14},{1,5},{3,7},{5,9},{7,11},{... | collective-permute-start | bytes 2850824 | tf_op jit(solution)/shard_map/ppermute | solution.py:247
  6.8 25.1 %collective-permute-start = (bf16[128,3712]{1,0:T(8,128)(2,1)S(1)}, bf16[128,3712]{1,0:T(8,128)(2,1)S(1)}, u32[]{:S(2)}, u32[]{:S(2)}) collective-permute-start(bf16[128,3712]{1,0:T(8,128)(2,1)S(1)} %shard_map.64.refs_0_), channel_id=1, source_target_pairs={{4,0},{6,2},{8,4},{10,6},{12,8},{14,10},{5,1},{7,3},{9,5},{11,7},{... | collective-permute-start | bytes 2850824 | tf_op jit(solution)/shard_map/ppermute | solution.py:247
  27.7 32.1 %collective-permute-start.6 = (bf16[128,3712]{1,0:T(8,128)(2,1)S(1)}, bf16[128,3712]{1,0:T(8,128)(2,1)S(1)}, u32[]{:S(2)}, u32[]{:S(2)}) collective-permute-start(bf16[128,3712]{1,0:T(8,128)(2,1)S(1)} %collective-permute-done.1.refs_1_.refs_2_), channel_id=1, source_target_pairs={{4,8},{6,10},{8,12},{10,14},{5,9},{7,11},{9,13},{11,15},{20,24},{2... | collective-permute-start | bytes 2850824 | tf_op jit(solution)/shard_map/ppermute | solution.py:247
  31.8 28.0 %collective-permute-start.7 = (bf16[128,3712]{1,0:T(8,128)(2,1)S(1)}, bf16[128,3712]{1,0:T(8,128)(2,1)S(1)}, u32[]{:S(2)}, u32[]{:S(2)}) collective-permute-start(bf16[128,3712]{1,0:T(8,128)(2,1)S(1)} %collective-permute-done.refs_0_), channel_id=1, source_target_pairs={{4,0},{6,2},{8,4},{10,6},{5,1},{7,3},{9,5},{11,7},{20,16},{22,18},... | collective-permute-start | bytes 2850824 | tf_op jit(solution)/shard_map/ppermute | solution.py:247
  34.2 16.0 %collective-permute-start.8 = (bf16[80,3584]{1,0:T(8,128)(2,1)S(1)}, bf16[80,3584]{1,0:T(8,128)(2,1)S(1)}, u32[]{:S(2)}, u32[]{:S(2)}) collective-permute-start(bf16[80,3584]{1,0:T(8,128)(2,1)S(1)} %get-tuple-element.48), channel_id=1, source_target_pairs={{0,2},{2,0},{4,6},{6,4},{8,10},{10,8},{12,14},{14,12},{1,3},{3,1},... | collective-permute-start | bytes 1720328 | tf_op jit(solution)/shard_map/ppermute | solution.py:250
  37.6 26.1 %collective-permute-start.3 = (bf16[80,3584]{1,0:T(8,128)(2,1)}, bf16[80,3584]{1,0:T(8,128)(2,1)S(1)}, u32[]{:S(2)}, u32[]{:S(2)}) collective-permute-start(bf16[80,3584]{1,0:T(8,128)(2,1)} %get-tuple-element.46), channel_id=1, source_target_pairs={{0,2},{2,0},{4,6},{6,4},{8,10},{10,8},{12,14},{14,12},{1,3},{3,1},... | collective-permute-start | bytes 1720328 | tf_op jit(solution)/shard_map/ppermute | solution.py:250
  59.8 5.7 %copy-start = (bf16[80,3584]{1,0:T(8,128)(2,1)S(1)}, bf16[80,3584]{1,0:T(8,128)(2,1)}, u32[]{:S(2)}) copy-start(bf16[80,3584]{1,0:T(8,128)(2,1)} %get-tuple-element.45.refs_0_) | copy-start | bytes 1720324
  59.9 24.7 %collective-permute-start.14 = (bf16[128,3712]{1,0:T(8,128)(2,1)S(1)}, bf16[128,3712]{1,0:T(8,128)(2,1)S(1)}, u32[]{:S(2)}, u32[]{:S(2)}) collective-permute-start(bf16[128,3712]{1,0:T(8,128)(2,1)S(1)} %get-tuple-element.50.refs_1_.refs_0_), channel_id=1, source_target_pairs={{4,0},{6,2},{5,1},{7,3},{20,16},{22,18},{21,17},{23,19}} | collective-permute-start | bytes 2850824 | tf_op jit(solution)/shard_map/ppermute | solution.py:247
  61.4 23.3 %collective-permute-start.15 = (bf16[128,3712]{1,0:T(8,128)(2,1)S(1)}, bf16[128,3712]{1,0:T(8,128)(2,1)S(1)}, u32[]{:S(2)}, u32[]{:S(2)}) collective-permute-start(bf16[128,3712]{1,0:T(8,128)(2,1)S(1)} %get-tuple-element.51.refs_3_.refs_2_), channel_id=1, source_target_pairs={{8,12},{10,14},{9,13},{11,15},{24,28},{26,30},{25,29},{27,31}} | collective-permute-start | bytes 2850824 | tf_op jit(solution)/shard_map/ppermute | solution.py:247
  62.1 16.0 %collective-permute-start.10 = (bf16[80,3584]{1,0:T(8,128)(2,1)S(1)}, bf16[80,3584]{1,0:T(8,128)(2,1)S(1)}, u32[]{:S(2)}, u32[]{:S(2)}) collective-permute-start(bf16[80,3584]{1,0:T(8,128)(2,1)S(1)} %get-tuple-element.57), channel_id=1, source_target_pairs={{0,2},{2,0},{4,6},{6,4},{8,10},{10,8},{12,14},{14,12},{1,3},{3,1},... | collective-permute-start | bytes 1720328 | tf_op jit(solution)/shard_map/ppermute | solution.py:250
  64.9 25.5 %collective-permute-start.13 = (bf16[80,3584]{1,0:T(8,128)(2,1)S(1)}, bf16[80,3584]{1,0:T(8,128)(2,1)S(1)}, u32[]{:S(2)}, u32[]{:S(2)}) collective-permute-start(bf16[80,3584]{1,0:T(8,128)(2,1)S(1)} %get-tuple-element.61), channel_id=1, source_target_pairs={{0,2},{2,0},{4,6},{6,4},{8,10},{10,8},{12,14},{14,12},{1,3},{3,1},... | collective-permute-start | bytes 1720328 | tf_op jit(solution)/shard_map/ppermute | solution.py:250
  78.7 33.4 %collective-permute-start.11 = (bf16[128,3584]{1,0:T(8,128)(2,1)S(1)}, bf16[128,3584]{1,0:T(8,128)(2,1)S(1)}, u32[]{:S(2)}, u32[]{:S(2)}) collective-permute-start(bf16[128,3584]{1,0:T(8,128)(2,1)S(1)} %shard_map.71.refs_4_), channel_id=1, source_target_pairs={{8,4},{10,6},{12,8},{14,10},{9,5},{11,7},{13,9},{15,11},{24,20},{2... | collective-permute-start | bytes 2752520 | tf_op jit(solution)/shard_map/ppermute | solution.py:247
  79.4 32.7 %collective-permute-start.12 = (bf16[128,3584]{1,0:T(8,128)(2,1)S(1)}, bf16[128,3584]{1,0:T(8,128)(2,1)S(1)}, u32[]{:S(2)}, u32[]{:S(2)}) collective-permute-start(bf16[128,3584]{1,0:T(8,128)(2,1)S(1)} %shard_map.71.refs_4_), channel_id=1, source_target_pairs={{0,4},{2,6},{4,8},{6,10},{1,5},{3,7},{5,9},{7,11},{16,20},{18,22},... | collective-permute-start | bytes 2752520 | tf_op jit(solution)/shard_map/ppermute | solution.py:247
  86.0 16.5 %collective-permute-start.17 = (bf16[80,3584]{1,0:T(8,128)(2,1)S(1)}, bf16[80,3584]{1,0:T(8,128)(2,1)S(1)}, u32[]{:S(2)}, u32[]{:S(2)}) collective-permute-start(bf16[80,3584]{1,0:T(8,128)(2,1)S(1)} %get-tuple-element.66), channel_id=1, source_target_pairs={{0,2},{2,0},{4,6},{6,4},{8,10},{10,8},{12,14},{14,12},{1,3},{3,1},... | collective-permute-start | bytes 1720328 | tf_op jit(solution)/shard_map/ppermute | solution.py:250
  100.0 12.1 %collective-permute-start.16 = (bf16[80,3584]{1,0:T(8,128)(2,1)S(1)}, bf16[80,3584]{1,0:T(8,128)(2,1)S(1)}, u32[]{:S(2)}, u32[]{:S(2)}) collective-permute-start(bf16[80,3584]{1,0:T(8,128)(2,1)S(1)} %get-tuple-element.64), channel_id=1, source_target_pairs={{0,2},{2,0},{4,6},{6,4},{8,10},{10,8},{12,14},{14,12},{1,3},{3,1},... | collective-permute-start | bytes 1720328 | tf_op jit(solution)/shard_map/ppermute | solution.py:250
  112.8 32.3 %collective-permute-start.18 = (bf16[128,3584]{1,0:T(8,128)(2,1)S(1)}, bf16[128,3584]{1,0:T(8,128)(2,1)S(1)}, u32[]{:S(2)}, u32[]{:S(2)}) collective-permute-start(bf16[128,3584]{1,0:T(8,128)(2,1)S(1)} %shard_map.75.refs_5_), channel_id=1, source_target_pairs={{0,8},{2,10},{4,0},{6,2},{8,12},{10,14},{12,4},{14,6},{1,9},{3,11}... | collective-permute-start | bytes 2752520 | tf_op jit(solution)/shard_map/ppermute | solution.py:247
  117.2 13.0 %collective-permute-start.19 = (bf16[80,3584]{1,0:T(8,128)(2,1)S(1)}, bf16[80,3584]{1,0:T(8,128)(2,1)S(1)}, u32[]{:S(2)}, u32[]{:S(2)}) collective-permute-start(bf16[80,3584]{1,0:T(8,128)(2,1)S(1)} %get-tuple-element.70), channel_id=1, source_target_pairs={{0,2},{2,0},{4,6},{6,4},{8,10},{10,8},{12,14},{14,12},{1,3},{3,1},... | collective-permute-start | bytes 1720328 | tf_op jit(solution)/shard_map/ppermute | solution.py:250
  118.7 28.0 %collective-permute-start.9 = (bf16[80,3584]{1,0:T(8,128)(2,1)S(1)}, bf16[80,3584]{1,0:T(8,128)(2,1)S(1)}, u32[]{:S(2)}, u32[]{:S(2)}) collective-permute-start(bf16[80,3584]{1,0:T(8,128)(2,1)S(1)} %get-tuple-element.54), channel_id=1, source_target_pairs={{0,2},{2,0},{4,6},{6,4},{8,10},{10,8},{12,14},{14,12},{1,3},{3,1},... | collective-permute-start | bytes 1720328 | tf_op jit(solution)/shard_map/ppermute | solution.py:250
  130.9 9.8 %collective-permute-start.20 = (bf16[128,768]{1,0:T(8,128)(2,1)S(1)}, bf16[128,768]{1,0:T(8,128)(2,1)S(1)}, u32[]{:S(2)}, u32[]{:S(2)}) collective-permute-start(bf16[128,768]{1,0:T(8,128)(2,1)S(1)} %get-tuple-element.72), channel_id=1, source_target_pairs={{0,4},{2,6},{12,8},{14,10},{1,5},{3,7},{13,9},{15,11},{16,20},{18,... | collective-permute-start | bytes 589832 | tf_op jit(solution)/shard_map/ppermute | solution.py:247
  134.3 14.5 %collective-permute-start.25 = (bf16[128,768]{1,0:T(8,128)(2,1)S(1)}, bf16[128,768]{1,0:T(8,128)(2,1)S(1)}, u32[]{:S(2)}, u32[]{:S(2)}) collective-permute-start(bf16[128,768]{1,0:T(8,128)(2,1)S(1)} %get-tuple-element.76), channel_id=1, source_target_pairs={{0,4},{2,6},{12,8},{14,10},{1,5},{3,7},{13,9},{15,11},{16,20},{18,... | collective-permute-start | bytes 589832 | tf_op jit(solution)/shard_map/ppermute | solution.py:247
  135.6 14.6 %collective-permute-start.23 = (bf16[128,768]{1,0:T(8,128)(2,1)S(1)}, bf16[128,768]{1,0:T(8,128)(2,1)S(1)}, u32[]{:S(2)}, u32[]{:S(2)}) collective-permute-start(bf16[128,768]{1,0:T(8,128)(2,1)S(1)} %get-tuple-element.74), channel_id=1, source_target_pairs={{0,4},{2,6},{12,8},{14,10},{1,5},{3,7},{13,9},{15,11},{16,20},{18,... | collective-permute-start | bytes 589832 | tf_op jit(solution)/shard_map/ppermute | solution.py:247
  140.7 9.5 %collective-permute-start.24 = (bf16[128,640]{1,0:T(8,128)(2,1)S(1)}, bf16[128,640]{1,0:T(8,128)(2,1)S(1)}, u32[]{:S(2)}, u32[]{:S(2)}) collective-permute-start(bf16[128,640]{1,0:T(8,128)(2,1)S(1)} %get-tuple-element.75), channel_id=1, source_target_pairs={{0,4},{2,6},{12,8},{14,10},{1,5},{3,7},{13,9},{15,11},{16,20},{18,... | collective-permute-start | bytes 491528 | tf_op jit(solution)/shard_map/ppermute | solution.py:247
  145.1 7.9 %collective-permute-start.22 = (bf16[128,640]{1,0:T(8,128)(2,1)S(1)}, bf16[128,640]{1,0:T(8,128)(2,1)S(1)}, u32[]{:S(2)}, u32[]{:S(2)}) collective-permute-start(bf16[128,640]{1,0:T(8,128)(2,1)S(1)} %get-tuple-element.73), channel_id=1, source_target_pairs={{0,4},{2,6},{12,8},{14,10},{1,5},{3,7},{13,9},{15,11},{16,20},{18,... | collective-permute-start | bytes 491528 | tf_op jit(solution)/shard_map/ppermute | solution.py:247
  146.8 8.5 %collective-permute-start.21 = (bf16[128,768]{1,0:T(8,128)(2,1)S(1)}, bf16[128,768]{1,0:T(8,128)(2,1)S(1)}, u32[]{:S(2)}, u32[]{:S(2)}) collective-permute-start(bf16[128,768]{1,0:T(8,128)(2,1)S(1)} %shard_map.78.refs_6_), channel_id=1, source_target_pairs={{4,12},{6,14},{8,0},{10,2},{5,13},{7,15},{9,1},{11,3},{20,28},{22,... | collective-permute-start | bytes 589832 | tf_op jit(solution)/shard_map/ppermute | solution.py:247
  148.9 8.5 %collective-permute-start.26 = (bf16[128,768]{1,0:T(8,128)(2,1)S(1)}, bf16[128,768]{1,0:T(8,128)(2,1)S(1)}, u32[]{:S(2)}, u32[]{:S(2)}) collective-permute-start(bf16[128,768]{1,0:T(8,128)(2,1)S(1)} %shard_map.80.refs_2_), channel_id=1, source_target_pairs={{4,12},{6,14},{8,0},{10,2},{5,13},{7,15},{9,1},{11,3},{20,28},{22,... | collective-permute-start | bytes 589832 | tf_op jit(solution)/shard_map/ppermute | solution.py:247
  150.3 10.9 %collective-permute-start.28 = (bf16[128,768]{1,0:T(8,128)(2,1)S(1)}, bf16[128,768]{1,0:T(8,128)(2,1)S(1)}, u32[]{:S(2)}, u32[]{:S(2)}) collective-permute-start(bf16[128,768]{1,0:T(8,128)(2,1)S(1)} %shard_map.82.refs_2_), channel_id=1, source_target_pairs={{4,12},{6,14},{8,0},{10,2},{5,13},{7,15},{9,1},{11,3},{20,28},{22,... | collective-permute-start | bytes 589832 | tf_op jit(solution)/shard_map/ppermute | solution.py:247
  151.6 9.6 %collective-permute-start.27 = (bf16[128,640]{1,0:T(8,128)(2,1)S(1)}, bf16[128,640]{1,0:T(8,128)(2,1)S(1)}, u32[]{:S(2)}, u32[]{:S(2)}) collective-permute-start(bf16[128,640]{1,0:T(8,128)(2,1)S(1)} %shard_map.81.refs_2_), channel_id=1, source_target_pairs={{4,12},{6,14},{8,0},{10,2},{5,13},{7,15},{9,1},{11,3},{20,28},{22,... | collective-permute-start | bytes 491528 | tf_op jit(solution)/shard_map/ppermute | solution.py:247
  153.0 10.0 %collective-permute-start.29 = (bf16[128,640]{1,0:T(8,128)(2,1)S(1)}, bf16[128,640]{1,0:T(8,128)(2,1)S(1)}, u32[]{:S(2)}, u32[]{:S(2)}) collective-permute-start(bf16[128,640]{1,0:T(8,128)(2,1)S(1)} %shard_map.83.refs_1_), channel_id=1, source_target_pairs={{4,12},{6,14},{8,0},{10,2},{5,13},{7,15},{9,1},{11,3},{20,28},{22,... | collective-permute-start | bytes 491528 | tf_op jit(solution)/shard_map/ppermute | solution.py:247
